TPU v7x, 32 devices: a whole 2x2x4 slice. The times are simulated.
32 devices in a mesh: groups: 2 (over y), tensor: 4 (over z), expert: 4 (over x, core).
Axes of the slice: x: 2, y: 2, z: 4, core: 2. Of those that a mesh axis runs over, the one named last changes fastest.
Arguments:
- tokens: bfloat16 [1024, 3072], P(('groups', 'expert'), 'tensor'), parts along dimension 0, may hold values from -6 to 6
- expert_ids: int32 [1024, 2], P(('groups', 'expert')), parts along dimension 0, may hold values from 0 to 3, all different within a row; in each aligned block of 128 rows (0 to 127, 128 to 255, ...) at most 64 rows name the same one
- route_logits: float32 [1024, 2], P(('groups', 'expert')), parts along dimension 0, may hold values from -6 to 6
- gate_weight: bfloat16 [4, 3072, 8192], P('expert', None, 'tensor'), may hold values from -0.109375 to 0.109375
- up_weight: bfloat16 [4, 3072, 8192], P('expert', None, 'tensor'), may hold values from -0.109375 to 0.109375
- down_weight: bfloat16 [4, 8192, 3072], P('expert', 'tensor'), may hold values from -0.09375 to 0.09375
Outputs:
- mixed: bfloat16 [1024, 3072], P(('groups', 'expert'), 'tensor'), parts along dimension 0
There are 2 independent parts, one for each index of `groups`. A program takes and returns all parts, laid end to end along the dimension named above; an argument that names none is the same for every part. Nothing has to cross between parts.
Inputs may be any that keep to these rules, and one draw needn't show every extreme that they name: `expert_ids`: each row names two different experts. In each aligned block of 128 rows (the rows of one device) no expert is named by more than 64 rows, a bound that some block reaches.
All inputs are finite; a program needn't handle non-finite values.
Results may differ from a plain program's by a relative error of at most 0.012.
Values may be sent and summed in bfloat16 or wider, within the bound.
No kernel may reach another device: no remote copies, remote signals or barrier semaphores. Data moves between devices by JAX's collectives and lax.ppermute only.
A program may use at most 128 MiB of HBM per device.

v0:
```python
import jax
import jax.numpy as jnp
from jax import lax
from jax.sharding import PartitionSpec as P


def routing(expert_ids, route_logits, experts, capacity):
    flat = expert_ids.reshape(-1)
    onehot = (flat[:, None] == jnp.arange(experts, dtype=jnp.int32)[None, :]).astype(jnp.int32)
    before = jnp.cumsum(onehot, axis=0) - onehot
    position = jnp.sum(before * onehot, axis=1)
    slots = (flat * capacity + position).reshape(-1, 2)
    share = jax.nn.sigmoid(route_logits[:, 0] - route_logits[:, 1])
    mixing = jnp.stack([share, 1.0 - share], axis=1)
    return (slots, mixing)


def per_device(tokens, expert_ids, route_logits, gate_weight, up_weight, down_weight):
    tok_rows = tokens.shape[0]
    experts = lax.axis_size("expert")
    capacity = tok_rows // 2
    slot_count = experts * capacity
    slots, mixing = routing(expert_ids, route_logits, experts, capacity)
    target = jnp.arange(slot_count, dtype=jnp.int32)[:, None]
    placed = ((slots[:, 0][None, :] == target) | (slots[:, 1][None, :] == target)).astype(
        jnp.bfloat16
    )
    gate_local = gate_weight[0]
    up_local = up_weight[0]
    down_local = down_weight[0]
    outgoing = jnp.dot(placed, tokens, preferred_element_type=jnp.float32).astype(jnp.bfloat16)
    arrived = lax.all_to_all(outgoing, "expert", split_axis=0, concat_axis=0, tiled=True)
    piece = lax.all_gather(arrived, "tensor", axis=1, tiled=True)
    gate = jnp.dot(piece, gate_local, preferred_element_type=jnp.float32)
    up = jnp.dot(piece, up_local, preferred_element_type=jnp.float32)
    hidden = (jax.nn.silu(gate) * up).astype(jnp.bfloat16)
    terms = jnp.dot(hidden, down_local, preferred_element_type=jnp.float32)
    summed = lax.psum_scatter(
        terms.astype(jnp.bfloat16), "tensor", scatter_dimension=1, tiled=True
    ).astype(jnp.float32)
    returned = lax.all_to_all(
        summed.astype(jnp.bfloat16), "expert", split_axis=0, concat_axis=0, tiled=True
    ).astype(summed.dtype)
    picked = returned[slots]
    return jnp.sum(picked * mixing[:, :, None], axis=1).astype(jnp.bfloat16)


def solution(mesh):
    in_specs = (
        P(("groups", "expert"), "tensor"),
        P(("groups", "expert"), None),
        P(("groups", "expert"), None),
        P("expert", None, "tensor"),
        P("expert", None, "tensor"),
        P("expert", "tensor", None),
    )
    out_specs = P(("groups", "expert"), "tensor")
    return jax.shard_map(
        per_device, mesh=mesh, in_specs=in_specs, out_specs=out_specs, check_vma=False
    )
```

profile of v0, /device:TPU:0, one launch (start us, length us, event | category | flops | bytes accessed | tf_op | source)
XLA Modules:
  0.0 142.2 jit_solution(8939996114927215260)
XLA Ops:
  6.5 0.0 copy-start
  6.5 0.0 all-gather.2.cloned.1.call-start
  6.5 0.8 copy.24
  7.4 0.1 eq.59
  7.5 0.1 eq.55
  7.7 1.2 reduce-window.6
  8.9 0.1 slice.26
  9.0 0.1 copy.26
  9.1 0.1 copy.27
  9.2 0.1 add_bitcast_fusion
  9.3 0.1 reduce_sum.21
  9.4 0.1 copy.28
  9.5 0.7 compare_select_fusion
  10.2 0.0 copy-done
  10.2 0.2 convolution_convert_fusion
  10.5 11.6 %all_to_all.21 = bf16[4,64,768]{2,1,0:T(8,128)(2,1)} all-to-all(bf16[4,64,768]{2,1,0:T(8,128)(2,1)S(1)} %bitcast.50), channel_id=1, replica_groups=mesh['groups'=2,'tensor'=4,'expert'=4] {'expert'}, dimensions={0} | all-to-all | bytes 786432 | tf_op jit(solution)/shard_map/all_to_all | solution.py:32
  22.0 0.0 all-gather.2.cloned.1.call-update
  22.1 0.0 reduce-scatter.2.cloned.1.call-start
  22.1 37.9 %all-gather.2.cloned.1.call-done = bf16[256,3072]{1,0:T(8,128)(2,1)} async-done(((bf16[256,768]{1,0:T(8,128)(2,1)}), bf16[256,3072]{1,0:T(8,128)(2,1)}) %all-gather.2.cloned.1.call-update) | async-done | bytes 1572880 | tf_op jit(solution)/shard_map/all_gather | solution.py:33
  60.0 0.0 copy-start.2
  60.0 9.9 %fusion.4 = f32[256,2048]{1,0:T(8,128)} fusion(bf16[256,3072]{1,0:T(8,128)(2,1)} %all-gather.2.cloned.1.call-done, bf16[1,3072,2048]{2,1,0:T(8,128)(2,1)} %param.9), kind=kOutput, calls=%fused_computation.5 | convolution fusion | flops 3221225472 | bytes 16252928 | tf_op jit(solution)/shard_map/dot_general | solution.py:34
  70.0 0.0 copy-done.2
  70.0 16.9 %fusion.6 = bf16[256,3072]{1,0:T(8,128)(2,1)} fusion(bf16[1,2048,3072]{2,1,0:T(8,128)(2,1)} %param.11, bf16[256,3072]{1,0:T(8,128)(2,1)S(1)} %copy-done.2, bf16[1,3072,2048]{2,1,0:T(8,128)(2,1)} %param.10, f32[256,2048]{1,0:T(8,128)} %fusion.4), kind=kOutput, calls=%fused_computation.7 | convolution fusion | flops 6446383104 | bytes 30408704 | tf_op jit(solution)/shard_map/dot_general | solution.py:37
  86.9 0.0 copy-start.1
  86.9 0.0 reduce-scatter.2.cloned.1.call-update
  86.9 34.3 %reduce-scatter.2.cloned.1.call-done = bf16[256,768]{1,0:T(8,128)(2,1)} async-done(((bf16[256,3072]{1,0:T(8,128)(2,1)}), bf16[256,768]{1,0:T(8,128)(2,1)}) %reduce-scatter.2.cloned.1.call-update) | async-done | bytes 393232 | tf_op jit(solution)/shard_map/reduce_scatter | solution.py:38
  121.2 3.5 %all-to-all-start.1 = ((bf16[4,64,768]{2,1,0:T(8,128)(2,1)}), bf16[4,64,768]{2,1,0:T(8,128)(2,1)S(1)}, u32[]{:S(2)}, u32[]{:S(2)}) async-start(bf16[4,64,768]{2,1,0:T(8,128)(2,1)} %bitcast.51), calls=%async_computation.2 | async-start | bytes 786432 | tf_op jit(solution)/shard_map/all_to_all | solution.py:41
  124.7 0.0 copy-done.1
  124.7 0.1 copy.29
  124.8 0.1 reshape.33
  125.0 0.1 copy.30
  125.1 7.0 %all-to-all-done.1 = bf16[4,64,768]{2,1,0:T(8,128)(2,1)S(1)} async-done(((bf16[4,64,768]{2,1,0:T(8,128)(2,1)}), bf16[4,64,768]{2,1,0:T(8,128)(2,1)S(1)}, u32[]{:S(2)}, u32[]{:S(2)}) %all-to-all-start.1) | async-done | bytes 393248 | tf_op jit(solution)/shard_map/all_to_all | solution.py:41
  132.1 0.1 bitcast_convert_fusion
  132.1 1.1 gather_fusion
  133.2 0.5 reshape.32
  133.7 1.7 %multiply_reduce_fusion = bf16[128,768]{1,0:T(8,128)(2,1)} fusion(f32[128,2,768]{2,1,0:T(2,128)S(1)} %reshape.32, f32[128,2]{1,0:T(8,128)S(1)} %copy.30), kind=kLoop, calls=%fused_computation.11 | loop fusion | flops 294912 | bytes 984064 | tf_op jit(solution)/shard_map/reduce_sum | solution.py:45
  (8 shorter events, 0.1 us)
Async XLA Ops:
  6.5 3.7 %copy-start = (bf16[128,768]{1,0:T(8,128)(2,1)S(1)}, bf16[128,768]{1,0:T(8,128)(2,1)}, u32[]{:S(2)}) copy-start(bf16[128,768]{1,0:T(8,128)(2,1)} %param.6) | copy-start | bytes 589828
  6.5 53.5 %all-gather.2.cloned.1.call-start = ((), (), s32[]{:S(2)}) async-start(), calls=%async_computation.3 | async-start | bytes 1966080 | tf_op jit(solution)/shard_map/all_gather | solution.py:33
  22.1 99.1 %reduce-scatter.2.cloned.1.call-start = ((), (), s32[]{:S(2)}) async-start(), calls=%async_computation.4 | async-start | bytes 1966080 | tf_op jit(solution)/shard_map/reduce_scatter | solution.py:38
  60.0 9.9 %copy-start.2 = (bf16[256,3072]{1,0:T(8,128)(2,1)S(1)}, bf16[256,3072]{1,0:T(8,128)(2,1)}, u32[]{:S(2)}) copy-start(bf16[256,3072]{1,0:T(8,128)(2,1)} %all-gather.2.cloned.1.call-done) | copy-start | bytes 4718596
  86.9 37.8 %copy-start.1 = (f32[128,2]{0,1:T(2,128)S(1)}, f32[128,2]{0,1:T(2,128)}, u32[]{:S(2)}) copy-start(f32[128,2]{0,1:T(2,128)} %param.8) | copy-start | bytes 3076
  121.2 10.9 %all-to-all-start.1 = ((bf16[4,64,768]{2,1,0:T(8,128)(2,1)}), bf16[4,64,768]{2,1,0:T(8,128)(2,1)S(1)}, u32[]{:S(2)}, u32[]{:S(2)}) async-start(bf16[4,64,768]{2,1,0:T(8,128)(2,1)} %bitcast.51), calls=%async_computation.2 | async-start | bytes 786432 | tf_op jit(solution)/shard_map/all_to_all | solution.py:41
Sparse Core Ops, SparseCore 0:
  22.2 37.8 all-gather.1
  87.0 34.1 reduce-scatter.1
where the time goes:
time: 142 us
  waiting for transfers between devices  79.2 us (56%)
  matrix products  27.1 us (19%)
  between operations  13.5 us (10%)
  blocking collectives  11.6 us (8%)
  other arithmetic  3.87 us (3%)
  local copies, waits for them, and re-layouts  3.52 us (2%)
  starting transfers between devices  3.5 us (2%)
    all_gather x1, waiting for transfers between devices, per_device(): piece = lax.all_gather(arrived, 'tensor', axis=1, tiled=True)  37.9 us
    reduce_scatter x1, waiting for transfers between devices, per_device(): lax.psum_scatter(terms.astype(jnp.bfloat16), 'tensor', scatter_dimension=...  34.3 us
    dot_general x1, matrix products, per_device(): terms = jnp.dot(hidden, down_local, preferred_element_type=jnp.float32)  16.9 us
    all_to_all x1, blocking collectives, per_device(): lax.all_to_all(outgoing, 'expert', split_axis=0, concat_axis=0, tiled=True)  11.6 us
    dot_general x1, matrix products, per_device(): gate = jnp.dot(piece, gate_local, preferred_element_type=jnp.float32)  9.93 us
    all_to_all x1, waiting for transfers between devices, per_device(): lax.all_to_all(summed.astype(jnp.bfloat16), 'expert', split_axis=0, conca...  6.99 us
    all_to_all x1, starting transfers between devices, per_device(): lax.all_to_all(summed.astype(jnp.bfloat16), 'expert', split_axis=0, conca...  3.46 us
  transfers between devices with their start and end apart: 3, of which 3 were waited for; matrix products, arithmetic and copies ran while one was open for 0% of the time, Pallas kernels for 0%

commit v1 on v0

v1 whole, which is shorter than its diff:
```python
import functools

import jax
import jax.numpy as jnp
from jax import lax
from jax.experimental import pallas as pl
from jax.experimental.pallas import tpu as pltpu
from jax.sharding import PartitionSpec as P

F32 = jnp.float32
BF16 = jnp.bfloat16
VMEM_LIMIT = 24 * 1024 * 1024


def params():
    return pltpu.CompilerParams(vmem_limit_bytes=VMEM_LIMIT)


def cost(flops, moved):
    return pl.CostEstimate(flops=flops, bytes_accessed=moved, transcendentals=0)


def whole(shape):
    return pl.BlockSpec(shape, lambda *_: (0,) * len(shape))


def routing_kernel(me_ref, ids_ref, placed_ref, *, experts, capacity):
    rows = ids_ref.shape[1]
    relative = lax.bitwise_xor(ids_ref[...], me_ref[0])
    lane = lax.broadcasted_iota(jnp.int32, (experts, rows), 0)
    names = (lane == relative[0:1]) | (lane == relative[1:2])
    earlier = lax.broadcasted_iota(jnp.int32, (rows, rows), 0) < lax.broadcasted_iota(
        jnp.int32, (rows, rows), 1
    )
    before = jnp.dot(
        names.astype(BF16), earlier.astype(BF16), preferred_element_type=F32
    ).astype(jnp.int32)
    position = jnp.where(names, before, -1)
    slot = lax.broadcasted_iota(jnp.int32, (capacity, rows), 0)
    for d in range(experts):
        hit = position[d : d + 1] == slot
        placed_ref[d * capacity : (d + 1) * capacity, :] = jnp.where(hit, 1.0, 0.0).astype(BF16)


def place(me, expert_ids, experts, capacity):
    rows = expert_ids.shape[0]
    return pl.pallas_call(
        functools.partial(routing_kernel, experts=experts, capacity=capacity),
        out_shape=jax.ShapeDtypeStruct((experts * capacity, rows), BF16),
        in_specs=[
            pl.BlockSpec(memory_space=pltpu.SMEM),
            pl.BlockSpec(memory_space=pltpu.VMEM),
        ],
        out_specs=pl.BlockSpec(memory_space=pltpu.VMEM),
        compiler_params=params(),
        name="routing",
    )(me.reshape(1), expert_ids.T)


def dispatch_kernel(placed_ref, block_ref, *out_refs):
    capacity = out_refs[0].shape[0]
    for d, out in enumerate(out_refs):
        out[...] = jnp.dot(
            placed_ref[d * capacity : (d + 1) * capacity, :],
            block_ref[...],
            preferred_element_type=F32,
        ).astype(BF16)


def dispatch(placed, block, experts, capacity):
    rows, width = block.shape
    return pl.pallas_call(
        dispatch_kernel,
        out_shape=[jax.ShapeDtypeStruct((capacity, width), BF16)] * experts,
        in_specs=[pl.BlockSpec(memory_space=pltpu.VMEM)] * 2,
        out_specs=[pl.BlockSpec(memory_space=pltpu.VMEM)] * experts,
        cost_estimate=cost(2 * experts * capacity * rows * width, 4 * rows * width),
        compiler_params=params(),
        name="dispatch",
    )(placed, block)


def gate_up_kernel(*refs, experts, first, last):
    x_refs = refs[1 : 1 + experts]
    gate_w, up_w = refs[1 + experts : 3 + experts]
    rest = refs[3 + experts :]
    if not first:
        old_gate, old_up = rest[:2]
        rest = rest[2:]
    x = jnp.concatenate([r[...] for r in x_refs], axis=0)
    gate = jnp.dot(x, gate_w[0], preferred_element_type=F32)
    up = jnp.dot(x, up_w[0], preferred_element_type=F32)
    if not first:
        gate = gate + old_gate[...]
        up = up + old_up[...]
    if last:
        rest[0][...] = (gate / (1.0 + jnp.exp(-gate)) * up).astype(BF16)
    else:
        rest[0][...] = gate
        rest[1][...] = up


def gate_up(part, x_blocks, gate_w, up_w, sums, last):
    experts = len(x_blocks)
    capacity, width = x_blocks[0].shape
    rows = experts * capacity
    hidden = gate_w.shape[2]
    tile = min(512, hidden)
    first = sums is None
    weight = pl.BlockSpec((1, width, tile), lambda n, part: (0, part[0], n))
    column = pl.BlockSpec((rows, tile), lambda n, part: (0, n))
    if last:
        out_shape = jax.ShapeDtypeStruct((rows, hidden), BF16)
        out_specs = column
    else:
        out_shape = [jax.ShapeDtypeStruct((rows, hidden), F32)] * 2
        out_specs = [column] * 2
    return pl.pallas_call(
        functools.partial(gate_up_kernel, experts=experts, first=first, last=last),
        out_shape=out_shape,
        grid_spec=pltpu.PrefetchScalarGridSpec(
            num_scalar_prefetch=1,
            grid=(hidden // tile,),
            in_specs=[whole((capacity, width))] * experts
            + [weight] * 2
            + ([] if first else [column] * 2),
            out_specs=out_specs,
        ),
        cost_estimate=cost(4 * rows * width * hidden, 4 * width * hidden + 16 * rows * hidden),
        compiler_params=params(),
        name="gate_up",
    )(part.reshape(1), *x_blocks, gate_w, up_w, *(() if first else sums))


def down_kernel(part_ref, h_ref, w_ref, *out_refs):
    capacity = out_refs[0].shape[0]
    y = jnp.dot(h_ref[...], w_ref[0], preferred_element_type=F32).astype(BF16)
    for d, out in enumerate(out_refs):
        out[...] = y[d * capacity : (d + 1) * capacity]


def down(part, hidden, down_w, width, experts):
    rows, depth = hidden.shape
    capacity = rows // experts
    tile = min(256, width)
    steps = width // tile
    return pl.pallas_call(
        down_kernel,
        out_shape=[jax.ShapeDtypeStruct((capacity, width), BF16)] * experts,
        grid_spec=pltpu.PrefetchScalarGridSpec(
            num_scalar_prefetch=1,
            grid=(steps,),
            in_specs=[
                whole((rows, depth)),
                pl.BlockSpec((1, depth, tile), lambda n, part: (0, 0, part[0] * steps + n)),
            ],
            out_specs=[pl.BlockSpec((capacity, tile), lambda n, part: (0, n))] * experts,
        ),
        cost_estimate=cost(2 * rows * depth * width, 2 * depth * width + 2 * rows * width),
        compiler_params=params(),
        name="down",
    )(part.reshape(1), hidden, down_w)


def combine_kernel(pick_ref, mix_ref, *refs):
    out = refs[-1]
    rows = out.shape[0]
    y = jnp.concatenate([r[...] for r in refs[:-1]], axis=0)
    picked = jnp.dot(pick_ref[...], y, preferred_element_type=F32)
    out[...] = (
        picked[:rows] * mix_ref[:, 0:1] + picked[rows:] * mix_ref[:, 1:2]
    ).astype(BF16)


def combine(pick, mixing, blocks):
    rows = mixing.shape[0]
    width = blocks[0].shape[1]
    return pl.pallas_call(
        combine_kernel,
        out_shape=jax.ShapeDtypeStruct((rows, width), BF16),
        in_specs=[pl.BlockSpec(memory_space=pltpu.VMEM)] * (2 + len(blocks)),
        out_specs=pl.BlockSpec(memory_space=pltpu.VMEM),
        cost_estimate=cost(4 * rows * pick.shape[1] * width, 6 * rows * width),
        compiler_params=params(),
        name="combine",
    )(pick, mixing, *blocks)


def swap(value, axis, distance):
    if distance == 0:
        return value
    count = lax.axis_size(axis)
    return lax.ppermute(value, axis, [(i, i ^ distance) for i in range(count)])


def per_device(tokens, expert_ids, route_logits, gate_weight, up_weight, down_weight):
    rows, own_width = tokens.shape
    experts = lax.axis_size("expert")
    shards = lax.axis_size("tensor")
    capacity = rows // 2
    me = lax.axis_index("expert").astype(jnp.int32)
    column = lax.axis_index("tensor").astype(jnp.int32)
    direct = shards <= 8
    distances = list(range(shards)) if direct else [0]
    width = own_width if direct else own_width * shards

    def part_of(distance):
        return lax.bitwise_xor(column, jnp.int32(distance)) if direct else jnp.int32(0)

    if direct:
        blocks = [swap(tokens, "tensor", d) for d in distances]
    else:
        blocks = [lax.all_gather(tokens, "tensor", axis=1, tiled=True)]
    placed = place(me, expert_ids, experts, capacity)

    sums = None
    for d in distances:
        outgoing = dispatch(placed, blocks[d], experts, capacity)
        arrived = [swap(block, "expert", e) for e, block in enumerate(outgoing)]
        sums = gate_up(part_of(d), arrived, gate_weight, up_weight, sums, d == distances[-1])
    hidden = sums

    names = expert_ids[:, :, None] == jnp.arange(experts, dtype=jnp.int32)[None, None, :]
    named = jnp.sum(names.astype(F32), axis=1)
    earlier = (jnp.arange(rows)[:, None] > jnp.arange(rows)[None, :]).astype(F32)
    before = jnp.dot(earlier, named).astype(jnp.int32)
    position = jnp.sum(jnp.where(names, before[:, None, :], 0), axis=2)
    slots = lax.bitwise_xor(expert_ids, me) * capacity + position
    pick = (
        slots.T[:, :, None] == jnp.arange(experts * capacity, dtype=jnp.int32)[None, None, :]
    ).astype(BF16).reshape(2 * rows, experts * capacity)
    share = jax.nn.sigmoid(route_logits[:, 0] - route_logits[:, 1])
    mixing = jnp.stack([share, 1.0 - share], axis=1)

    total = []
    for d in reversed(distances):
        terms = down(part_of(d), hidden, down_weight, width, experts)
        returned = [swap(block, "expert", e) for e, block in enumerate(terms)]
        mixed = combine(pick, mixing, returned)
        if not direct:
            return lax.psum_scatter(mixed, "tensor", scatter_dimension=1, tiled=True)
        total.append(swap(mixed, "tensor", d))
    out = total[0].astype(F32)
    for term in total[1:]:
        out = out + term.astype(F32)
    return out.astype(BF16)


def solution(mesh):
    in_specs = (
        P(("groups", "expert"), "tensor"),
        P(("groups", "expert"), None),
        P(("groups", "expert"), None),
        P("expert", None, "tensor"),
        P("expert", None, "tensor"),
        P("expert", "tensor", None),
    )
    out_specs = P(("groups", "expert"), "tensor")
    return jax.shard_map(
        per_device, mesh=mesh, in_specs=in_specs, out_specs=out_specs, check_vma=False
    )
```

time: 142 us -> 102 us (0.72)
  waiting for transfers between devices: 79.2 us -> 14.9 us
  matrix products: 27.1 us -> 0.14 us
  local copies, waits for them, and re-layouts: 3.52 us -> 29.2 us
  Pallas kernels: 0 us -> 25.1 us
  starting transfers between devices: 3.5 us -> 28.4 us
  between operations: 13.5 us -> 0.36 us
  blocking collectives: 11.6 us -> 0 us
    all_gather x1 -> x0, waiting for transfers between devices: 37.9 us -> none  [per_device(): piece = lax.all_gather(arrived, 'tensor', axis=1, tiled=True)]
    reduce_scatter x1 -> x0, waiting for transfers between devices: 34.3 us -> none  [per_device(): lax.psum_scatter(terms.astype(jnp.bfloat16), 'tensor', scatter_dimension=...]
    ppermute x0 -> x30, starting transfers between devices: none -> 28.4 us  [swap(): return lax.ppermute(value, axis, [(i, i ^ distance) for i in range(count)])]
    unnamed x7 -> x18, local copies, waits for them, and re-layouts: 0.84 us -> 29 us
    dot_general x3 -> x1, matrix products: 27.1 us -> 0.14 us  [per_device(): before = jnp.dot(earlier, named).astype(jnp.int32)]
    pallas_call x0 -> x17, Pallas kernels: none -> 25.1 us  [the longest x4 15.5 us: gate_up(): pl.pallas_call(functools.partial(gate_up_kernel, experts=experts, first=f...]
    ppermute x0 -> x30, waiting for transfers between devices: none -> 14.9 us  [swap(): return lax.ppermute(value, axis, [(i, i ^ distance) for i in range(count)])]
    all_to_all x1 -> x0, blocking collectives: 11.6 us -> none  [per_device(): lax.all_to_all(outgoing, 'expert', split_axis=0, concat_axis=0, tiled=True)]
  transfers between devices with their start and end apart: 3 -> 30, of which waited for: 3 -> 5; matrix products, arithmetic and copies ran while one was open for 0% -> 2% of each run, Pallas kernels for 0% -> 18%
where the time goes in v1:
time: 102 us; the launch traced here: 101 us
  local copies, waits for them, and re-layouts  29.2 us (29%)
  starting transfers between devices  28.4 us (28%)
  Pallas kernels  25.1 us (25%)
  waiting for transfers between devices  14.9 us (15%)
  other arithmetic  2.98 us (3%)
    unnamed x18, local copies, waits for them, and re-layouts  29 us
    ppermute x30, starting transfers between devices, swap(): return lax.ppermute(value, axis, [(i, i ^ distance) for i in range(count)])  28.4 us
    pallas_call x4, Pallas kernels, gate_up(): pl.pallas_call(functools.partial(gate_up_kernel, experts=experts, first=f...  15.5 us
    ppermute x30, waiting for transfers between devices, swap(): return lax.ppermute(value, axis, [(i, i ^ distance) for i in range(count)])  14.9 us
    pallas_call x4, Pallas kernels, down(): pl.pallas_call(down_kernel, out_shape=[jax.ShapeDtypeStruct((capacity, wi...  7.41 us
  transfers between devices with their start and end apart: 30, of which 5 were waited for; matrix products, arithmetic and copies ran while one was open for 2% of the time, Pallas kernels for 18%

profile of v1, /device:TPU:0, one launch (start us, length us, event | category | flops | bytes accessed | tf_op | source)
XLA Modules:
  0.0 101.1 jit_solution(8175210597723408098)
XLA Ops:
  0.0 3.0 %collective-permute-start.8 = (bf16[128,768]{1,0:T(8,128)(2,1)}, bf16[128,768]{1,0:T(8,128)(2,1)S(1)}, u32[]{:S(2)}, u32[]{:S(2)}) collective-permute-start(bf16[128,768]{1,0:T(8,128)(2,1)} %block_ref.1), channel_id=1, source_target_pairs={{0,4},{4,0},{8,12},{12,8},{1,5},{5,1},{9,13},{13,9},{2,6},{6,2},{1... | collective-permute-start | bytes 589832 | tf_op jit(solution)/shard_map/ppermute | solution.py:193
  3.0 2.6 %collective-permute-start.4 = (bf16[128,768]{1,0:T(8,128)(2,1)}, bf16[128,768]{1,0:T(8,128)(2,1)S(1)}, u32[]{:S(2)}, u32[]{:S(2)}) collective-permute-start(bf16[128,768]{1,0:T(8,128)(2,1)} %block_ref.1), channel_id=1, source_target_pairs={{0,8},{4,12},{8,0},{12,4},{1,9},{5,13},{9,1},{13,5},{2,10},{6,14},... | collective-permute-start | bytes 589832 | tf_op jit(solution)/shard_map/ppermute | solution.py:193
  5.6 0.7 copy-done.7
  6.5 0.9 copy-done.6
  7.7 1.8 %collective-permute-start.13 = (bf16[64,768]{1,0:T(8,128)(2,1)S(1)}, bf16[64,768]{1,0:T(8,128)(2,1)S(1)}, u32[]{:S(2)}, u32[]{:S(2)}) collective-permute-start(bf16[64,768]{1,0:T(8,128)(2,1)S(1)} %get-tuple-element.57), channel_id=1, source_target_pairs={{0,2},{1,3},{2,0},{3,1},{4,6},{5,7},{6,4},{7,5},{8,10},{9,11},{10,... | collective-permute-start | bytes 294920 | tf_op jit(solution)/shard_map/ppermute | solution.py:193
  9.5 0.7 convert_reduce_fusion
  10.3 0.7 select_reduce_fusion
  11.0 0.7 add_bitcast_fusion
  12.2 1.8 %collective-permute-start.10 = (bf16[64,768]{1,0:T(8,128)(2,1)S(1)}, bf16[64,768]{1,0:T(8,128)(2,1)S(1)}, u32[]{:S(2)}, u32[]{:S(2)}) collective-permute-start(bf16[64,768]{1,0:T(8,128)(2,1)S(1)} %get-tuple-element.53), channel_id=1, source_target_pairs={{0,2},{1,3},{2,0},{3,1},{4,6},{5,7},{6,4},{7,5},{8,10},{9,11},{10,... | collective-permute-start | bytes 294920 | tf_op jit(solution)/shard_map/ppermute | solution.py:193
  14.0 1.2 %collective-permute-start.11 = (bf16[64,768]{1,0:T(8,128)(2,1)S(1)}, bf16[64,768]{1,0:T(8,128)(2,1)S(1)}, u32[]{:S(2)}, u32[]{:S(2)}) collective-permute-start(bf16[64,768]{1,0:T(8,128)(2,1)S(1)} %get-tuple-element.54), channel_id=1, source_target_pairs={{0,3},{1,2},{2,1},{3,0},{4,7},{5,6},{6,5},{7,4},{8,11},{9,10},{10,... | collective-permute-start | bytes 294920 | tf_op jit(solution)/shard_map/ppermute | solution.py:193
  15.2 1.3 %collective-permute-done.14.refs_4_ = bf16[64,768]{1,0:T(8,128)(2,1)S(1)} collective-permute-done((bf16[64,768]{1,0:T(8,128)(2,1)S(1)}, bf16[64,768]{1,0:T(8,128)(2,1)S(1)}, u32[]{:S(2)}, u32[]{:S(2)}) %collective-permute-start.14) | collective-permute-done | bytes 98336 | tf_op jit(solution)/shard_map/ppermute | solution.py:193
  16.5 0.8 collective-permute-start.9
  17.3 4.6 %copy-done.2 = bf16[1,3072,2048]{2,1,0:T(8,128)(2,1)S(1)} copy-done((bf16[1,3072,2048]{2,1,0:T(8,128)(2,1)S(1)}, bf16[1,3072,2048]{2,1,0:T(8,128)(2,1)}, u32[]{:S(2)}) %copy-start.2) | copy-done | bytes 12582936
  21.9 4.6 %copy-done.4 = bf16[1,3072,2048]{2,1,0:T(8,128)(2,1)S(1)} copy-done((bf16[1,3072,2048]{2,1,0:T(8,128)(2,1)S(1)}, bf16[1,3072,2048]{2,1,0:T(8,128)(2,1)}, u32[]{:S(2)}) %copy-start.4) | copy-done | bytes 12582936
  26.4 3.1 %gate_up.4 = (f32[256,2048]{1,0:T(8,128)S(1)}, f32[256,2048]{1,0:T(8,128)S(1)}) custom-call(s32[1]{0:T(128)} %bitcast.7.refs_0_.part_ref, bf16[64,768]{1,0:T(8,128)(2,1)S(1)} %get-tuple-element.55.refs_1_, bf16[64,768]{1,0:T(8,128)(2,1)S(1)} %collective-permute-done.12.refs_2_, bf16[64,768]{1,0:T(8,128)(2,1)S(1)} %collective-permute-done.13.refs_3_, ...), custom_call_target="tpu_custom_call" | custom-call | flops 1610612736 | bytes 14680064 | tf_op jit(solution)/shard_map/gate_up/pallas_call | solution.py:118
  29.9 0.7 collective-permute-start.6
  30.9 1.2 %collective-permute-start.7 = (bf16[64,768]{1,0:T(8,128)(2,1)S(1)}, bf16[64,768]{1,0:T(8,128)(2,1)S(1)}, u32[]{:S(2)}, u32[]{:S(2)}) collective-permute-start(bf16[64,768]{1,0:T(8,128)(2,1)S(1)} %get-tuple-element.50), channel_id=1, source_target_pairs={{0,3},{1,2},{2,1},{3,0},{4,7},{5,6},{6,5},{7,4},{8,11},{9,10},{10,... | collective-permute-start | bytes 294920 | tf_op jit(solution)/shard_map/ppermute | solution.py:193
  32.1 0.4 collective-permute-start.1
  32.5 0.6 collective-permute-start.2
  33.1 4.6 %copy-done.3 = bf16[1,3072,2048]{2,1,0:T(8,128)(2,1)S(1)} copy-done((bf16[1,3072,2048]{2,1,0:T(8,128)(2,1)S(1)}, bf16[1,3072,2048]{2,1,0:T(8,128)(2,1)}, u32[]{:S(2)}) %copy-start.3) | copy-done | bytes 12582936
  37.7 4.6 %gate_up.5 = (f32[256,2048]{1,0:T(8,128)S(1)}, f32[256,2048]{1,0:T(8,128)S(1)}) custom-call(s32[1]{0:T(128)} %bitcast.6.refs_0_.part_ref, bf16[64,768]{1,0:T(8,128)(2,1)S(1)} %get-tuple-element.51.refs_1_, bf16[64,768]{1,0:T(8,128)(2,1)S(1)} %collective-permute-done.9.refs_2_, bf16[64,768]{1,0:T(8,128)(2,1)S(1)} %collective-permute-done.10.refs_3_, ...), custom_call_target="tpu_custom_call" | custom-call | flops 1610612736 | bytes 14680064 | tf_op jit(solution)/shard_map/gate_up/pallas_call | solution.py:118
  42.3 0.9 collective-permute-start.3
  43.2 4.6 %gate_up.6 = (f32[256,2048]{1,0:T(8,128)S(1)}, f32[256,2048]{1,0:T(8,128)S(1)}) custom-call(s32[1]{0:T(128)} %bitcast.5.refs_0_.part_ref, bf16[64,768]{1,0:T(8,128)(2,1)S(1)} %get-tuple-element.47.refs_1_, bf16[64,768]{1,0:T(8,128)(2,1)S(1)} %collective-permute-done.5.refs_2_, bf16[64,768]{1,0:T(8,128)(2,1)S(1)} %collective-permute-done.6.refs_3_, ...), custom_call_target="tpu_custom_call" | custom-call | flops 1610612736 | bytes 14680064 | tf_op jit(solution)/shard_map/gate_up/pallas_call | solution.py:118
  47.8 4.6 %copy-done.5 = bf16[1,3072,2048]{2,1,0:T(8,128)(2,1)S(1)} copy-done((bf16[1,3072,2048]{2,1,0:T(8,128)(2,1)S(1)}, bf16[1,3072,2048]{2,1,0:T(8,128)(2,1)}, u32[]{:S(2)}) %copy-start.5) | copy-done | bytes 12582936
  52.4 3.2 %gate_up.7.h_ref = bf16[256,2048]{1,0:T(8,128)(2,1)S(1)} custom-call(s32[1]{0:T(128)} %bitcast.2.refs_0_.part_ref, bf16[64,768]{1,0:T(8,128)(2,1)S(1)} %get-tuple-element.43.refs_1_, bf16[64,768]{1,0:T(8,128)(2,1)S(1)} %collective-permute-done.1.refs_2_, bf16[64,768]{1,0:T(8,128)(2,1)S(1)} %collective-permute-done.2.refs_3_, ...), custom_call_target="tpu_custom_call" | custom-call | flops 1610612736 | bytes 14680064 | tf_op jit(solution)/shard_map/gate_up/pallas_call | solution.py:118
  55.7 4.6 %copy-done = bf16[1,2048,3072]{2,1,0:T(8,128)(2,1)S(1)} copy-done((bf16[1,2048,3072]{2,1,0:T(8,128)(2,1)S(1)}, bf16[1,2048,3072]{2,1,0:T(8,128)(2,1)}, u32[]{:S(2)}) %copy-start) | copy-done | bytes 12582936
  60.2 1.9 %down.4 = (bf16[64,768]{1,0:T(8,128)(2,1)S(1)}, bf16[64,768]{1,0:T(8,128)(2,1)S(1)}, bf16[64,768]{1,0:T(8,128)(2,1)S(1)}, bf16[64,768]{1,0:T(8,128)(2,1)S(1)}) custom-call(s32[1]{0:T(128)} %bitcast.2.refs_0_.part_ref, bf16[256,2048]{1,0:T(8,128)(2,1)S(1)} %gate_up.7.h_ref, bf16[1,2048,3072]{2,1,0:T(8,128)(2,1)S(1)} %copy-done), custom_call_target="tpu_custom_call" | custom-call | flops 805306368 | bytes 3538944 | tf_op jit(solution)/shard_map/down/pallas_call | solution.py:147
  62.1 1.9 %down.5 = (bf16[64,768]{1,0:T(8,128)(2,1)S(1)}, bf16[64,768]{1,0:T(8,128)(2,1)S(1)}, bf16[64,768]{1,0:T(8,128)(2,1)S(1)}, bf16[64,768]{1,0:T(8,128)(2,1)S(1)}) custom-call(s32[1]{0:T(128)} %bitcast.5.refs_0_.part_ref, bf16[256,2048]{1,0:T(8,128)(2,1)S(1)} %gate_up.7.h_ref, bf16[1,2048,3072]{2,1,0:T(8,128)(2,1)S(1)} %copy-done), custom_call_target="tpu_custom_call" | custom-call | flops 805306368 | bytes 3538944 | tf_op jit(solution)/shard_map/down/pallas_call | solution.py:147
  64.0 0.7 collective-permute-start.15
  64.7 0.7 collective-permute-start.16
  65.3 0.8 collective-permute-start.17
  66.1 0.7 collective-permute-start.19
  66.8 0.7 collective-permute-start.20
  67.5 1.8 %down.6 = (bf16[64,768]{1,0:T(8,128)(2,1)S(1)}, bf16[64,768]{1,0:T(8,128)(2,1)S(1)}, bf16[64,768]{1,0:T(8,128)(2,1)S(1)}, bf16[64,768]{1,0:T(8,128)(2,1)S(1)}) custom-call(s32[1]{0:T(128)} %bitcast.6.refs_0_.part_ref, bf16[256,2048]{1,0:T(8,128)(2,1)S(1)} %gate_up.7.h_ref, bf16[1,2048,3072]{2,1,0:T(8,128)(2,1)S(1)} %copy-done), custom_call_target="tpu_custom_call" | custom-call | flops 805306368 | bytes 3538944 | tf_op jit(solution)/shard_map/down/pallas_call | solution.py:147
  69.4 0.8 collective-permute-start.21
  70.3 0.7 collective-permute-start.23
  71.0 1.0 collective-permute-start.24
  72.0 1.6 %collective-permute-start.25 = (bf16[64,768]{1,0:T(8,128)(2,1)S(1)}, bf16[64,768]{1,0:T(8,128)(2,1)S(1)}, u32[]{:S(2)}, u32[]{:S(2)}) collective-permute-start(bf16[64,768]{1,0:T(8,128)(2,1)S(1)} %get-tuple-element.76), channel_id=1, source_target_pairs={{0,3},{1,2},{2,1},{3,0},{4,7},{5,6},{6,5},{7,4},{8,11},{9,10},{10,... | collective-permute-start | bytes 294920 | tf_op jit(solution)/shard_map/ppermute | solution.py:193
  73.7 4.6 %copy-done.1 = bf16[1,2048,3072]{2,1,0:T(8,128)(2,1)S(1)} copy-done((bf16[1,2048,3072]{2,1,0:T(8,128)(2,1)S(1)}, bf16[1,2048,3072]{2,1,0:T(8,128)(2,1)}, u32[]{:S(2)}) %copy-start.1) | copy-done | bytes 12582936
  78.3 1.8 %down.7 = (bf16[64,768]{1,0:T(8,128)(2,1)S(1)}, bf16[64,768]{1,0:T(8,128)(2,1)S(1)}, bf16[64,768]{1,0:T(8,128)(2,1)S(1)}, bf16[64,768]{1,0:T(8,128)(2,1)S(1)}) custom-call(s32[1]{0:T(128)} %bitcast.7.refs_0_.part_ref, bf16[256,2048]{1,0:T(8,128)(2,1)S(1)} %gate_up.7.h_ref, bf16[1,2048,3072]{2,1,0:T(8,128)(2,1)S(1)} %copy-done.1), custom_call_target="tpu_custom_call" | custom-call | flops 805306368 | bytes 3538944 | tf_op jit(solution)/shard_map/down/pallas_call | solution.py:147
  80.1 0.3 combine.4
  80.5 3.7 %collective-permute-start.18 = (bf16[128,768]{1,0:T(8,128)(2,1)S(1)}, bf16[128,768]{1,0:T(8,128)(2,1)S(1)}, u32[]{:S(2)}, u32[]{:S(2)}) collective-permute-start(bf16[128,768]{1,0:T(8,128)(2,1)S(1)} %combine.4), channel_id=1, source_target_pairs={{0,12},{4,8},{8,4},{12,0},{1,13},{5,9},{9,5},{13,1},{2,14},{6,10},... | collective-permute-start | bytes 589832 | tf_op jit(solution)/shard_map/ppermute | solution.py:193
  84.9 0.8 collective-permute-start.26
  85.7 0.6 collective-permute-start.28
  86.3 0.4 collective-permute-start.29
  86.7 4.6 %collective-permute-done.28.refs_2_ = bf16[64,768]{1,0:T(8,128)(2,1)S(1)} collective-permute-done((bf16[64,768]{1,0:T(8,128)(2,1)S(1)}, bf16[64,768]{1,0:T(8,128)(2,1)S(1)}, u32[]{:S(2)}, u32[]{:S(2)}) %collective-permute-start.28) | collective-permute-done | bytes 98336 | tf_op jit(solution)/shard_map/ppermute | solution.py:193
  91.7 8.6 %collective-permute-done.22 = bf16[128,768]{1,0:T(8,128)(2,1)S(1)} collective-permute-done((bf16[128,768]{1,0:T(8,128)(2,1)S(1)}, bf16[128,768]{1,0:T(8,128)(2,1)S(1)}, u32[]{:S(2)}, u32[]{:S(2)}) %collective-permute-start.22) | collective-permute-done | bytes 196640 | tf_op jit(solution)/shard_map/ppermute | solution.py:193
  100.3 0.8 add_convert_fusion
  (56 shorter events, 3.0 us)
Async XLA Ops:
  0.0 11.7 %collective-permute-start.8 = (bf16[128,768]{1,0:T(8,128)(2,1)}, bf16[128,768]{1,0:T(8,128)(2,1)S(1)}, u32[]{:S(2)}, u32[]{:S(2)}) collective-permute-start(bf16[128,768]{1,0:T(8,128)(2,1)} %block_ref.1), channel_id=1, source_target_pairs={{0,4},{4,0},{8,12},{12,8},{1,5},{5,1},{9,13},{13,9},{2,6},{6,2},{1... | collective-permute-start | bytes 589832 | tf_op jit(solution)/shard_map/ppermute | solution.py:193
  3.0 26.5 %collective-permute-start.4 = (bf16[128,768]{1,0:T(8,128)(2,1)}, bf16[128,768]{1,0:T(8,128)(2,1)S(1)}, u32[]{:S(2)}, u32[]{:S(2)}) collective-permute-start(bf16[128,768]{1,0:T(8,128)(2,1)} %block_ref.1), channel_id=1, source_target_pairs={{0,8},{4,12},{8,0},{12,4},{1,9},{5,13},{9,1},{13,5},{2,10},{6,14},... | collective-permute-start | bytes 589832 | tf_op jit(solution)/shard_map/ppermute | solution.py:193
  5.6 24.3 %collective-permute-start = (bf16[128,768]{1,0:T(8,128)(2,1)}, bf16[128,768]{1,0:T(8,128)(2,1)S(1)}, u32[]{:S(2)}, u32[]{:S(2)}) collective-permute-start(bf16[128,768]{1,0:T(8,128)(2,1)} %block_ref.1), channel_id=1, source_target_pairs={{0,12},{4,8},{8,4},{12,0},{1,13},{5,9},{9,5},{13,1},{2,14},{6,10},... | collective-permute-start | bytes 589832 | tf_op jit(solution)/shard_map/ppermute | solution.py:193
  5.6 0.7 copy-start.7
  6.5 0.9 copy-start.6
  7.6 4.6 %collective-permute-start.12 = (bf16[64,768]{1,0:T(8,128)(2,1)S(1)}, bf16[64,768]{1,0:T(8,128)(2,1)S(1)}, u32[]{:S(2)}, u32[]{:S(2)}) collective-permute-start(bf16[64,768]{1,0:T(8,128)(2,1)S(1)} %get-tuple-element.56), channel_id=1, source_target_pairs={{0,1},{1,0},{2,3},{3,2},{4,5},{5,4},{6,7},{7,6},{8,9},{9,8},{10,11... | collective-permute-start | bytes 294920 | tf_op jit(solution)/shard_map/ppermute | solution.py:193
  7.7 6.3 %collective-permute-start.13 = (bf16[64,768]{1,0:T(8,128)(2,1)S(1)}, bf16[64,768]{1,0:T(8,128)(2,1)S(1)}, u32[]{:S(2)}, u32[]{:S(2)}) collective-permute-start(bf16[64,768]{1,0:T(8,128)(2,1)S(1)} %get-tuple-element.57), channel_id=1, source_target_pairs={{0,2},{1,3},{2,0},{3,1},{4,6},{5,7},{6,4},{7,5},{8,10},{9,11},{10,... | collective-permute-start | bytes 294920 | tf_op jit(solution)/shard_map/ppermute | solution.py:193
  11.7 4.8 %collective-permute-start.14 = (bf16[64,768]{1,0:T(8,128)(2,1)S(1)}, bf16[64,768]{1,0:T(8,128)(2,1)S(1)}, u32[]{:S(2)}, u32[]{:S(2)}) collective-permute-start(bf16[64,768]{1,0:T(8,128)(2,1)S(1)} %get-tuple-element.58), channel_id=1, source_target_pairs={{0,3},{1,2},{2,1},{3,0},{4,7},{5,6},{6,5},{7,4},{8,11},{9,10},{10,... | collective-permute-start | bytes 294920 | tf_op jit(solution)/shard_map/ppermute | solution.py:193
  12.2 18.7 %collective-permute-start.10 = (bf16[64,768]{1,0:T(8,128)(2,1)S(1)}, bf16[64,768]{1,0:T(8,128)(2,1)S(1)}, u32[]{:S(2)}, u32[]{:S(2)}) collective-permute-start(bf16[64,768]{1,0:T(8,128)(2,1)S(1)} %get-tuple-element.53), channel_id=1, source_target_pairs={{0,2},{1,3},{2,0},{3,1},{4,6},{5,7},{6,4},{7,5},{8,10},{9,11},{10,... | collective-permute-start | bytes 294920 | tf_op jit(solution)/shard_map/ppermute | solution.py:193
  14.0 18.1 %collective-permute-start.11 = (bf16[64,768]{1,0:T(8,128)(2,1)S(1)}, bf16[64,768]{1,0:T(8,128)(2,1)S(1)}, u32[]{:S(2)}, u32[]{:S(2)}) collective-permute-start(bf16[64,768]{1,0:T(8,128)(2,1)S(1)} %get-tuple-element.54), channel_id=1, source_target_pairs={{0,3},{1,2},{2,1},{3,0},{4,7},{5,6},{6,5},{7,4},{8,11},{9,10},{10,... | collective-permute-start | bytes 294920 | tf_op jit(solution)/shard_map/ppermute | solution.py:193
  16.5 16.0 %collective-permute-start.9 = (bf16[64,768]{1,0:T(8,128)(2,1)S(1)}, bf16[64,768]{1,0:T(8,128)(2,1)S(1)}, u32[]{:S(2)}, u32[]{:S(2)}) collective-permute-start(bf16[64,768]{1,0:T(8,128)(2,1)S(1)} %get-tuple-element.52), channel_id=1, source_target_pairs={{0,1},{1,0},{2,3},{3,2},{4,5},{5,4},{6,7},{7,6},{8,9},{9,8},{10,11... | collective-permute-start | bytes 294920 | tf_op jit(solution)/shard_map/ppermute | solution.py:193
  17.3 4.6 %copy-start.2 = (bf16[1,3072,2048]{2,1,0:T(8,128)(2,1)S(1)}, bf16[1,3072,2048]{2,1,0:T(8,128)(2,1)}, u32[]{:S(2)}) copy-start(bf16[1,3072,2048]{2,1,0:T(8,128)(2,1)} %refs_5_.7) | copy-start | bytes 37748740
  21.9 4.6 %copy-start.4 = (bf16[1,3072,2048]{2,1,0:T(8,128)(2,1)S(1)}, bf16[1,3072,2048]{2,1,0:T(8,128)(2,1)}, u32[]{:S(2)}) copy-start(bf16[1,3072,2048]{2,1,0:T(8,128)(2,1)} %refs_6_.7) | copy-start | bytes 37748740
  29.8 12.4 %collective-permute-start.5 = (bf16[64,768]{1,0:T(8,128)(2,1)S(1)}, bf16[64,768]{1,0:T(8,128)(2,1)S(1)}, u32[]{:S(2)}, u32[]{:S(2)}) collective-permute-start(bf16[64,768]{1,0:T(8,128)(2,1)S(1)} %get-tuple-element.48), channel_id=1, source_target_pairs={{0,1},{1,0},{2,3},{3,2},{4,5},{5,4},{6,7},{7,6},{8,9},{9,8},{10,11... | collective-permute-start | bytes 294920 | tf_op jit(solution)/shard_map/ppermute | solution.py:193
  29.9 13.3 %collective-permute-start.6 = (bf16[64,768]{1,0:T(8,128)(2,1)S(1)}, bf16[64,768]{1,0:T(8,128)(2,1)S(1)}, u32[]{:S(2)}, u32[]{:S(2)}) collective-permute-start(bf16[64,768]{1,0:T(8,128)(2,1)S(1)} %get-tuple-element.49), channel_id=1, source_target_pairs={{0,2},{1,3},{2,0},{3,1},{4,6},{5,7},{6,4},{7,5},{8,10},{9,11},{10,... | collective-permute-start | bytes 294920 | tf_op jit(solution)/shard_map/ppermute | solution.py:193
  30.9 12.3 %collective-permute-start.7 = (bf16[64,768]{1,0:T(8,128)(2,1)S(1)}, bf16[64,768]{1,0:T(8,128)(2,1)S(1)}, u32[]{:S(2)}, u32[]{:S(2)}) collective-permute-start(bf16[64,768]{1,0:T(8,128)(2,1)S(1)} %get-tuple-element.50), channel_id=1, source_target_pairs={{0,3},{1,2},{2,1},{3,0},{4,7},{5,6},{6,5},{7,4},{8,11},{9,10},{10,... | collective-permute-start | bytes 294920 | tf_op jit(solution)/shard_map/ppermute | solution.py:193
  32.1 15.7 %collective-permute-start.1 = (bf16[64,768]{1,0:T(8,128)(2,1)S(1)}, bf16[64,768]{1,0:T(8,128)(2,1)S(1)}, u32[]{:S(2)}, u32[]{:S(2)}) collective-permute-start(bf16[64,768]{1,0:T(8,128)(2,1)S(1)} %get-tuple-element.44), channel_id=1, source_target_pairs={{0,1},{1,0},{2,3},{3,2},{4,5},{5,4},{6,7},{7,6},{8,9},{9,8},{10,11... | collective-permute-start | bytes 294920 | tf_op jit(solution)/shard_map/ppermute | solution.py:193
  32.5 15.4 %collective-permute-start.2 = (bf16[64,768]{1,0:T(8,128)(2,1)S(1)}, bf16[64,768]{1,0:T(8,128)(2,1)S(1)}, u32[]{:S(2)}, u32[]{:S(2)}) collective-permute-start(bf16[64,768]{1,0:T(8,128)(2,1)S(1)} %get-tuple-element.45), channel_id=1, source_target_pairs={{0,2},{1,3},{2,0},{3,1},{4,6},{5,7},{6,4},{7,5},{8,10},{9,11},{10,... | collective-permute-start | bytes 294920 | tf_op jit(solution)/shard_map/ppermute | solution.py:193
  33.1 4.6 %copy-start.3 = (bf16[1,3072,2048]{2,1,0:T(8,128)(2,1)S(1)}, bf16[1,3072,2048]{2,1,0:T(8,128)(2,1)}, u32[]{:S(2)}) copy-start(bf16[1,3072,2048]{2,1,0:T(8,128)(2,1)} %refs_5_.7) | copy-start | bytes 37748740
  42.3 5.6 %collective-permute-start.3 = (bf16[64,768]{1,0:T(8,128)(2,1)S(1)}, bf16[64,768]{1,0:T(8,128)(2,1)S(1)}, u32[]{:S(2)}, u32[]{:S(2)}) collective-permute-start(bf16[64,768]{1,0:T(8,128)(2,1)S(1)} %get-tuple-element.46), channel_id=1, source_target_pairs={{0,3},{1,2},{2,1},{3,0},{4,7},{5,6},{6,5},{7,4},{8,11},{9,10},{10,... | collective-permute-start | bytes 294920 | tf_op jit(solution)/shard_map/ppermute | solution.py:193
  47.8 4.6 %copy-start.5 = (bf16[1,3072,2048]{2,1,0:T(8,128)(2,1)S(1)}, bf16[1,3072,2048]{2,1,0:T(8,128)(2,1)}, u32[]{:S(2)}) copy-start(bf16[1,3072,2048]{2,1,0:T(8,128)(2,1)} %refs_6_.7) | copy-start | bytes 37748740
  55.6 4.6 %copy-start = (bf16[1,2048,3072]{2,1,0:T(8,128)(2,1)S(1)}, bf16[1,2048,3072]{2,1,0:T(8,128)(2,1)}, u32[]{:S(2)}) copy-start(bf16[1,2048,3072]{2,1,0:T(8,128)(2,1)} %w_ref.7) | copy-start | bytes 37748740
  62.1 4.7 %copy-start.8 = (f32[128,2]{0,1:T(2,128)S(1)}, f32[128,2]{0,1:T(2,128)}, u32[]{:S(2)}) copy-start(f32[128,2]{0,1:T(2,128)} %param.8) | copy-start | bytes 3076
  64.0 5.4 %collective-permute-start.15 = (bf16[64,768]{1,0:T(8,128)(2,1)S(1)}, bf16[64,768]{1,0:T(8,128)(2,1)S(1)}, u32[]{:S(2)}, u32[]{:S(2)}) collective-permute-start(bf16[64,768]{1,0:T(8,128)(2,1)S(1)} %get-tuple-element.66), channel_id=1, source_target_pairs={{0,1},{1,0},{2,3},{3,2},{4,5},{5,4},{6,7},{7,6},{8,9},{9,8},{10,11... | collective-permute-start | bytes 294920 | tf_op jit(solution)/shard_map/ppermute | solution.py:193
  64.7 5.7 %collective-permute-start.16 = (bf16[64,768]{1,0:T(8,128)(2,1)S(1)}, bf16[64,768]{1,0:T(8,128)(2,1)S(1)}, u32[]{:S(2)}, u32[]{:S(2)}) collective-permute-start(bf16[64,768]{1,0:T(8,128)(2,1)S(1)} %get-tuple-element.67), channel_id=1, source_target_pairs={{0,2},{1,3},{2,0},{3,1},{4,6},{5,7},{6,4},{7,5},{8,10},{9,11},{10,... | collective-permute-start | bytes 294920 | tf_op jit(solution)/shard_map/ppermute | solution.py:193
  65.3 5.7 %collective-permute-start.17 = (bf16[64,768]{1,0:T(8,128)(2,1)S(1)}, bf16[64,768]{1,0:T(8,128)(2,1)S(1)}, u32[]{:S(2)}, u32[]{:S(2)}) collective-permute-start(bf16[64,768]{1,0:T(8,128)(2,1)S(1)} %get-tuple-element.68), channel_id=1, source_target_pairs={{0,3},{1,2},{2,1},{3,0},{4,7},{5,6},{6,5},{7,4},{8,11},{9,10},{10,... | collective-permute-start | bytes 294920 | tf_op jit(solution)/shard_map/ppermute | solution.py:193
  66.1 5.9 %collective-permute-start.19 = (bf16[64,768]{1,0:T(8,128)(2,1)S(1)}, bf16[64,768]{1,0:T(8,128)(2,1)S(1)}, u32[]{:S(2)}, u32[]{:S(2)}) collective-permute-start(bf16[64,768]{1,0:T(8,128)(2,1)S(1)} %get-tuple-element.70), channel_id=1, source_target_pairs={{0,1},{1,0},{2,3},{3,2},{4,5},{5,4},{6,7},{7,6},{8,9},{9,8},{10,11... | collective-permute-start | bytes 294920 | tf_op jit(solution)/shard_map/ppermute | solution.py:193
  66.8 13.6 %collective-permute-start.20 = (bf16[64,768]{1,0:T(8,128)(2,1)S(1)}, bf16[64,768]{1,0:T(8,128)(2,1)S(1)}, u32[]{:S(2)}, u32[]{:S(2)}) collective-permute-start(bf16[64,768]{1,0:T(8,128)(2,1)S(1)} %get-tuple-element.71), channel_id=1, source_target_pairs={{0,2},{1,3},{2,0},{3,1},{4,6},{5,7},{6,4},{7,5},{8,10},{9,11},{10,... | collective-permute-start | bytes 294920 | tf_op jit(solution)/shard_map/ppermute | solution.py:193
  69.4 11.1 %collective-permute-start.21 = (bf16[64,768]{1,0:T(8,128)(2,1)S(1)}, bf16[64,768]{1,0:T(8,128)(2,1)S(1)}, u32[]{:S(2)}, u32[]{:S(2)}) collective-permute-start(bf16[64,768]{1,0:T(8,128)(2,1)S(1)} %get-tuple-element.72), channel_id=1, source_target_pairs={{0,3},{1,2},{2,1},{3,0},{4,7},{5,6},{6,5},{7,4},{8,11},{9,10},{10,... | collective-permute-start | bytes 294920 | tf_op jit(solution)/shard_map/ppermute | solution.py:193
  70.3 14.2 %collective-permute-start.23 = (bf16[64,768]{1,0:T(8,128)(2,1)S(1)}, bf16[64,768]{1,0:T(8,128)(2,1)S(1)}, u32[]{:S(2)}, u32[]{:S(2)}) collective-permute-start(bf16[64,768]{1,0:T(8,128)(2,1)S(1)} %get-tuple-element.74), channel_id=1, source_target_pairs={{0,1},{1,0},{2,3},{3,2},{4,5},{5,4},{6,7},{7,6},{8,9},{9,8},{10,11... | collective-permute-start | bytes 294920 | tf_op jit(solution)/shard_map/ppermute | solution.py:193
  71.0 13.6 %collective-permute-start.24 = (bf16[64,768]{1,0:T(8,128)(2,1)S(1)}, bf16[64,768]{1,0:T(8,128)(2,1)S(1)}, u32[]{:S(2)}, u32[]{:S(2)}) collective-permute-start(bf16[64,768]{1,0:T(8,128)(2,1)S(1)} %get-tuple-element.75), channel_id=1, source_target_pairs={{0,2},{1,3},{2,0},{3,1},{4,6},{5,7},{6,4},{7,5},{8,10},{9,11},{10,... | collective-permute-start | bytes 294920 | tf_op jit(solution)/shard_map/ppermute | solution.py:193
  72.0 12.6 %collective-permute-start.25 = (bf16[64,768]{1,0:T(8,128)(2,1)S(1)}, bf16[64,768]{1,0:T(8,128)(2,1)S(1)}, u32[]{:S(2)}, u32[]{:S(2)}) collective-permute-start(bf16[64,768]{1,0:T(8,128)(2,1)S(1)} %get-tuple-element.76), channel_id=1, source_target_pairs={{0,3},{1,2},{2,1},{3,0},{4,7},{5,6},{6,5},{7,4},{8,11},{9,10},{10,... | collective-permute-start | bytes 294920 | tf_op jit(solution)/shard_map/ppermute | solution.py:193
  73.7 4.6 %copy-start.1 = (bf16[1,2048,3072]{2,1,0:T(8,128)(2,1)S(1)}, bf16[1,2048,3072]{2,1,0:T(8,128)(2,1)}, u32[]{:S(2)}) copy-start(bf16[1,2048,3072]{2,1,0:T(8,128)(2,1)} %w_ref.7) | copy-start | bytes 37748740
  80.4 5.9 %collective-permute-start.27 = (bf16[64,768]{1,0:T(8,128)(2,1)S(1)}, bf16[64,768]{1,0:T(8,128)(2,1)S(1)}, u32[]{:S(2)}, u32[]{:S(2)}) collective-permute-start(bf16[64,768]{1,0:T(8,128)(2,1)S(1)} %get-tuple-element.78), channel_id=1, source_target_pairs={{0,1},{1,0},{2,3},{3,2},{4,5},{5,4},{6,7},{7,6},{8,9},{9,8},{10,11... | collective-permute-start | bytes 294920 | tf_op jit(solution)/shard_map/ppermute | solution.py:193
  80.5 11.1 %collective-permute-start.18 = (bf16[128,768]{1,0:T(8,128)(2,1)S(1)}, bf16[128,768]{1,0:T(8,128)(2,1)S(1)}, u32[]{:S(2)}, u32[]{:S(2)}) collective-permute-start(bf16[128,768]{1,0:T(8,128)(2,1)S(1)} %combine.4), channel_id=1, source_target_pairs={{0,12},{4,8},{8,4},{12,0},{1,13},{5,9},{9,5},{13,1},{2,14},{6,10},... | collective-permute-start | bytes 589832 | tf_op jit(solution)/shard_map/ppermute | solution.py:193
  84.5 15.8 %collective-permute-start.22 = (bf16[128,768]{1,0:T(8,128)(2,1)S(1)}, bf16[128,768]{1,0:T(8,128)(2,1)S(1)}, u32[]{:S(2)}, u32[]{:S(2)}) collective-permute-start(bf16[128,768]{1,0:T(8,128)(2,1)S(1)} %combine.5), channel_id=1, source_target_pairs={{0,8},{4,12},{8,0},{12,4},{1,9},{5,13},{9,1},{13,5},{2,10},{6,14},... | collective-permute-start | bytes 589832 | tf_op jit(solution)/shard_map/ppermute | solution.py:193
  84.9 15.4 %collective-permute-start.26 = (bf16[128,768]{1,0:T(8,128)(2,1)S(1)}, bf16[128,768]{1,0:T(8,128)(2,1)S(1)}, u32[]{:S(2)}, u32[]{:S(2)}) collective-permute-start(bf16[128,768]{1,0:T(8,128)(2,1)S(1)} %combine.6), channel_id=1, source_target_pairs={{0,4},{4,0},{8,12},{12,8},{1,5},{5,1},{9,13},{13,9},{2,6},{6,2},{1... | collective-permute-start | bytes 589832 | tf_op jit(solution)/shard_map/ppermute | solution.py:193
  85.7 5.6 %collective-permute-start.28 = (bf16[64,768]{1,0:T(8,128)(2,1)S(1)}, bf16[64,768]{1,0:T(8,128)(2,1)S(1)}, u32[]{:S(2)}, u32[]{:S(2)}) collective-permute-start(bf16[64,768]{1,0:T(8,128)(2,1)S(1)} %get-tuple-element.79), channel_id=1, source_target_pairs={{0,2},{1,3},{2,0},{3,1},{4,6},{5,7},{6,4},{7,5},{8,10},{9,11},{10,... | collective-permute-start | bytes 294920 | tf_op jit(solution)/shard_map/ppermute | solution.py:193
  86.3 5.1 %collective-permute-start.29 = (bf16[64,768]{1,0:T(8,128)(2,1)S(1)}, bf16[64,768]{1,0:T(8,128)(2,1)S(1)}, u32[]{:S(2)}, u32[]{:S(2)}) collective-permute-start(bf16[64,768]{1,0:T(8,128)(2,1)S(1)} %get-tuple-element.80), channel_id=1, source_target_pairs={{0,3},{1,2},{2,1},{3,0},{4,7},{5,6},{6,5},{7,4},{8,11},{9,10},{10,... | collective-permute-start | bytes 294920 | tf_op jit(solution)/shard_map/ppermute | solution.py:193

commit v2 on v1

--- a/solution.py
+++ b/solution.py
@@ -9,11 +9,11 @@
 
 F32 = jnp.float32
 BF16 = jnp.bfloat16
-VMEM_LIMIT = 24 * 1024 * 1024
-
-
-def params():
-    return pltpu.CompilerParams(vmem_limit_bytes=VMEM_LIMIT)
+MIB = 1024 * 1024
+
+
+def params(mib=16):
+    return pltpu.CompilerParams(vmem_limit_bytes=mib * MIB)
 
 
 def cost(flops, moved):
@@ -24,34 +24,45 @@
     return pl.BlockSpec(shape, lambda *_: (0,) * len(shape))
 
 
-def routing_kernel(me_ref, ids_ref, placed_ref, *, experts, capacity):
+def routing_kernel(me_ref, ids_ref, placed_ref, pick_ref, *, experts, capacity):
     rows = ids_ref.shape[1]
     relative = lax.bitwise_xor(ids_ref[...], me_ref[0])
     lane = lax.broadcasted_iota(jnp.int32, (experts, rows), 0)
-    names = (lane == relative[0:1]) | (lane == relative[1:2])
+    names = [lane == relative[k : k + 1] for k in range(2)]
+    named = names[0] | names[1]
     earlier = lax.broadcasted_iota(jnp.int32, (rows, rows), 0) < lax.broadcasted_iota(
         jnp.int32, (rows, rows), 1
     )
     before = jnp.dot(
-        names.astype(BF16), earlier.astype(BF16), preferred_element_type=F32
+        jnp.where(named, 1.0, 0.0).astype(BF16),
+        jnp.where(earlier, 1.0, 0.0).astype(BF16),
+        preferred_element_type=F32,
     ).astype(jnp.int32)
-    position = jnp.where(names, before, -1)
     slot = lax.broadcasted_iota(jnp.int32, (capacity, rows), 0)
     for d in range(experts):
-        hit = position[d : d + 1] == slot
-        placed_ref[d * capacity : (d + 1) * capacity, :] = jnp.where(hit, 1.0, 0.0).astype(BF16)
+        here = slice(d * capacity, (d + 1) * capacity)
+        both = None
+        for k in range(2):
+            position = jnp.where(names[k], before, -1)
+            hit = jnp.where(position[d : d + 1] == slot, 1.0, 0.0)
+            pick_ref[here, k * rows : (k + 1) * rows] = hit.astype(BF16)
+            both = hit if k == 0 else both + hit
+        placed_ref[here, :] = both.astype(BF16)
 
 
 def place(me, expert_ids, experts, capacity):
     rows = expert_ids.shape[0]
     return pl.pallas_call(
         functools.partial(routing_kernel, experts=experts, capacity=capacity),
-        out_shape=jax.ShapeDtypeStruct((experts * capacity, rows), BF16),
+        out_shape=[
+            jax.ShapeDtypeStruct((experts * capacity, rows), BF16),
+            jax.ShapeDtypeStruct((experts * capacity, 2 * rows), BF16),
+        ],
         in_specs=[
             pl.BlockSpec(memory_space=pltpu.SMEM),
             pl.BlockSpec(memory_space=pltpu.VMEM),
         ],
-        out_specs=pl.BlockSpec(memory_space=pltpu.VMEM),
+        out_specs=[pl.BlockSpec(memory_space=pltpu.VMEM)] * 2,
         compiler_params=params(),
         name="routing",
     )(me.reshape(1), expert_ids.T)
@@ -127,7 +138,7 @@
             out_specs=out_specs,
         ),
         cost_estimate=cost(4 * rows * width * hidden, 4 * width * hidden + 16 * rows * hidden),
-        compiler_params=params(),
+        compiler_params=params(53),
         name="gate_up",
     )(part.reshape(1), *x_blocks, gate_w, up_w, *(() if first else sums))
 
@@ -157,33 +168,34 @@
             out_specs=[pl.BlockSpec((capacity, tile), lambda n, part: (0, n))] * experts,
         ),
         cost_estimate=cost(2 * rows * depth * width, 2 * depth * width + 2 * rows * width),
-        compiler_params=params(),
+        compiler_params=params(53),
         name="down",
     )(part.reshape(1), hidden, down_w)
 
 
-def combine_kernel(pick_ref, mix_ref, *refs):
+def combine_kernel(pick_ref, logits_ref, *refs):
     out = refs[-1]
     rows = out.shape[0]
     y = jnp.concatenate([r[...] for r in refs[:-1]], axis=0)
-    picked = jnp.dot(pick_ref[...], y, preferred_element_type=F32)
-    out[...] = (
-        picked[:rows] * mix_ref[:, 0:1] + picked[rows:] * mix_ref[:, 1:2]
-    ).astype(BF16)
-
-
-def combine(pick, mixing, blocks):
-    rows = mixing.shape[0]
+    picked = lax.dot_general(
+        pick_ref[...], y, (((0,), (0,)), ((), ())), preferred_element_type=F32
+    )
+    share = 1.0 / (1.0 + jnp.exp(logits_ref[:, 1:2] - logits_ref[:, 0:1]))
+    out[...] = (picked[:rows] * share + picked[rows:] * (1.0 - share)).astype(BF16)
+
+
+def combine(pick, logits, blocks):
+    rows = logits.shape[0]
     width = blocks[0].shape[1]
     return pl.pallas_call(
         combine_kernel,
         out_shape=jax.ShapeDtypeStruct((rows, width), BF16),
         in_specs=[pl.BlockSpec(memory_space=pltpu.VMEM)] * (2 + len(blocks)),
         out_specs=pl.BlockSpec(memory_space=pltpu.VMEM),
-        cost_estimate=cost(4 * rows * pick.shape[1] * width, 6 * rows * width),
+        cost_estimate=cost(4 * rows * pick.shape[0] * width, 6 * rows * width),
         compiler_params=params(),
         name="combine",
-    )(pick, mixing, *blocks)
+    )(pick, logits, *blocks)
 
 
 def swap(value, axis, distance):
@@ -211,7 +223,7 @@
         blocks = [swap(tokens, "tensor", d) for d in distances]
     else:
         blocks = [lax.all_gather(tokens, "tensor", axis=1, tiled=True)]
-    placed = place(me, expert_ids, experts, capacity)
+    placed, pick = place(me, expert_ids, experts, capacity)
 
     sums = None
     for d in distances:
@@ -220,23 +232,11 @@
         sums = gate_up(part_of(d), arrived, gate_weight, up_weight, sums, d == distances[-1])
     hidden = sums
 
-    names = expert_ids[:, :, None] == jnp.arange(experts, dtype=jnp.int32)[None, None, :]
-    named = jnp.sum(names.astype(F32), axis=1)
-    earlier = (jnp.arange(rows)[:, None] > jnp.arange(rows)[None, :]).astype(F32)
-    before = jnp.dot(earlier, named).astype(jnp.int32)
-    position = jnp.sum(jnp.where(names, before[:, None, :], 0), axis=2)
-    slots = lax.bitwise_xor(expert_ids, me) * capacity + position
-    pick = (
-        slots.T[:, :, None] == jnp.arange(experts * capacity, dtype=jnp.int32)[None, None, :]
-    ).astype(BF16).reshape(2 * rows, experts * capacity)
-    share = jax.nn.sigmoid(route_logits[:, 0] - route_logits[:, 1])
-    mixing = jnp.stack([share, 1.0 - share], axis=1)
-
     total = []
     for d in reversed(distances):
         terms = down(part_of(d), hidden, down_weight, width, experts)
         returned = [swap(block, "expert", e) for e, block in enumerate(terms)]
-        mixed = combine(pick, mixing, returned)
+        mixed = combine(pick, route_logits, returned)
         if not direct:
             return lax.psum_scatter(mixed, "tensor", scatter_dimension=1, tiled=True)
         total.append(swap(mixed, "tensor", d))

time: 102 us -> 93.7 us (0.919)
  local copies, waits for them, and re-layouts: 29.2 us -> 0.8 us
  Pallas kernels: 25.1 us -> 44.6 us
  starting transfers between devices: 28.4 us -> 30.9 us
  other arithmetic: 2.98 us -> 0.78 us
    unnamed x18 -> x5, local copies, waits for them, and re-layouts: 29 us -> 0.8 us
    pallas_call x4, Pallas kernels: 15.5 us -> 26.3 us  [gate_up(): pl.pallas_call(functools.partial(gate_up_kernel, experts=experts, first=f...]
    pallas_call x4, Pallas kernels: 7.41 us -> 15 us  [down(): pl.pallas_call(down_kernel, out_shape=[jax.ShapeDtypeStruct((capacity, wi...]
    ppermute x30, starting transfers between devices: 28.4 us -> 30.9 us  [swap(): return lax.ppermute(value, axis, [(i, i ^ distance) for i in range(count)])]
    reduce_sum x2 -> x0, other arithmetic: 1.41 us -> none  [the longest x1 0.72 us: per_device(): position = jnp.sum(jnp.where(names, before[:, None, :], 0), axis=2)]
    ppermute x30, waiting for transfers between devices: 14.9 us -> 15.9 us  [swap(): return lax.ppermute(value, axis, [(i, i ^ distance) for i in range(count)])]
  transfers between devices with their start and end apart: 30 -> 30, of which waited for: 5 -> 4; matrix products, arithmetic and copies ran while one was open for 2% -> 0% of each run, Pallas kernels for 18% -> 37%
where the time goes in v2:
time: 93.7 us; the launch traced here: 93.3 us
  Pallas kernels  44.6 us (48%)
  starting transfers between devices  30.9 us (33%)
  waiting for transfers between devices  15.9 us (17%)
    ppermute x30, starting transfers between devices, swap(): return lax.ppermute(value, axis, [(i, i ^ distance) for i in range(count)])  30.9 us
    pallas_call x4, Pallas kernels, gate_up(): pl.pallas_call(functools.partial(gate_up_kernel, experts=experts, first=f...  26.3 us
    ppermute x30, waiting for transfers between devices, swap(): return lax.ppermute(value, axis, [(i, i ^ distance) for i in range(count)])  15.9 us
    pallas_call x4, Pallas kernels, down(): pl.pallas_call(down_kernel, out_shape=[jax.ShapeDtypeStruct((capacity, wi...  15 us
    pallas_call x4, Pallas kernels, dispatch(): pl.pallas_call(dispatch_kernel, out_shape=[jax.ShapeDtypeStruct((capacity...  1.95 us
  transfers between devices with their start and end apart: 30, of which 4 were waited for; matrix products, arithmetic and copies ran while one was open for 0% of the time, Pallas kernels for 37%

profile of v2, /device:TPU:0, one launch (start us, length us, event | category | flops | bytes accessed | tf_op | source)
XLA Modules:
  0.0 93.3 jit_solution(13626273165778961211)
XLA Ops:
  0.0 3.0 %collective-permute-start.8 = (bf16[128,768]{1,0:T(8,128)(2,1)}, bf16[128,768]{1,0:T(8,128)(2,1)S(1)}, u32[]{:S(2)}, u32[]{:S(2)}) collective-permute-start(bf16[128,768]{1,0:T(8,128)(2,1)} %block_ref.1), channel_id=1, source_target_pairs={{0,4},{4,0},{8,12},{12,8},{1,5},{5,1},{9,13},{13,9},{2,6},{6,2},{1... | collective-permute-start | bytes 589832 | tf_op jit(solution)/shard_map/ppermute | solution.py:205
  3.0 0.7 copy-done
  3.7 0.2 routing.1
  3.9 1.2 %dispatch.7 = (bf16[64,768]{1,0:T(8,128)(2,1)S(1)}, bf16[64,768]{1,0:T(8,128)(2,1)S(1)}, bf16[64,768]{1,0:T(8,128)(2,1)S(1)}, bf16[64,768]{1,0:T(8,128)(2,1)S(1)}) custom-call(bf16[256,128]{1,0:T(8,128)(2,1)S(1)} %get-tuple-element.46.placed_ref, bf16[128,768]{1,0:T(8,128)(2,1)} %block_ref.1), custom_call_target="tpu_custom_call" | custom-call | flops 50331648 | bytes 393216 | tf_op jit(solution)/shard_map/dispatch/pallas_call | solution.py:83
  5.1 0.1 collective-permute-start.12
  5.1 1.6 %collective-permute-start.13 = (bf16[64,768]{1,0:T(8,128)(2,1)S(1)}, bf16[64,768]{1,0:T(8,128)(2,1)S(1)}, u32[]{:S(2)}, u32[]{:S(2)}) collective-permute-start(bf16[64,768]{1,0:T(8,128)(2,1)S(1)} %get-tuple-element.61), channel_id=1, source_target_pairs={{0,2},{1,3},{2,0},{3,1},{4,6},{5,7},{6,4},{7,5},{8,10},{9,11},{10,... | collective-permute-start | bytes 294920 | tf_op jit(solution)/shard_map/ppermute | solution.py:205
  6.7 0.3 collective-permute-start.14
  7.0 2.6 %collective-permute-start.4 = (bf16[128,768]{1,0:T(8,128)(2,1)}, bf16[128,768]{1,0:T(8,128)(2,1)S(1)}, u32[]{:S(2)}, u32[]{:S(2)}) collective-permute-start(bf16[128,768]{1,0:T(8,128)(2,1)} %block_ref.1), channel_id=1, source_target_pairs={{0,8},{4,12},{8,0},{12,4},{1,9},{5,13},{9,1},{13,5},{2,10},{6,14},... | collective-permute-start | bytes 589832 | tf_op jit(solution)/shard_map/ppermute | solution.py:205
  9.6 2.3 %collective-permute-start = (bf16[128,768]{1,0:T(8,128)(2,1)}, bf16[128,768]{1,0:T(8,128)(2,1)S(1)}, u32[]{:S(2)}, u32[]{:S(2)}) collective-permute-start(bf16[128,768]{1,0:T(8,128)(2,1)} %block_ref.1), channel_id=1, source_target_pairs={{0,12},{4,8},{8,4},{12,0},{1,13},{5,9},{9,5},{13,1},{2,14},{6,10},... | collective-permute-start | bytes 589832 | tf_op jit(solution)/shard_map/ppermute | solution.py:205
  11.9 0.3 dispatch.6
  12.2 1.6 %collective-permute-start.10 = (bf16[64,768]{1,0:T(8,128)(2,1)S(1)}, bf16[64,768]{1,0:T(8,128)(2,1)S(1)}, u32[]{:S(2)}, u32[]{:S(2)}) collective-permute-start(bf16[64,768]{1,0:T(8,128)(2,1)S(1)} %get-tuple-element.57), channel_id=1, source_target_pairs={{0,2},{1,3},{2,0},{3,1},{4,6},{5,7},{6,4},{7,5},{8,10},{9,11},{10,... | collective-permute-start | bytes 294920 | tf_op jit(solution)/shard_map/ppermute | solution.py:205
  13.7 0.6 collective-permute-start.9
  14.4 6.0 %gate_up.4 = (f32[256,2048]{1,0:T(8,128)}, f32[256,2048]{1,0:T(8,128)}) custom-call(s32[1]{0:T(128)} %bitcast.5.refs_0_.part_ref, bf16[64,768]{1,0:T(8,128)(2,1)S(1)} %get-tuple-element.59.refs_1_, bf16[64,768]{1,0:T(8,128)(2,1)S(1)} %collective-permute-done.12.refs_2_, bf16[64,768]{1,0:T(8,128)(2,1)S(1)} %collective-permute-done.13.refs_3_, ...), custom_call_target="tpu_custom_call" | custom-call | flops 1610612736 | bytes 14680064 | tf_op jit(solution)/shard_map/gate_up/pallas_call | solution.py:129
  20.4 3.2 %collective-permute-done.4.block_ref = bf16[128,768]{1,0:T(8,128)(2,1)S(1)} collective-permute-done((bf16[128,768]{1,0:T(8,128)(2,1)}, bf16[128,768]{1,0:T(8,128)(2,1)S(1)}, u32[]{:S(2)}, u32[]{:S(2)}) %collective-permute-start.4) | collective-permute-done | bytes 196640 | tf_op jit(solution)/shard_map/ppermute | solution.py:205
  23.6 0.3 dispatch.5
  23.9 0.1 collective-permute-start.5
  23.9 1.6 %collective-permute-start.6 = (bf16[64,768]{1,0:T(8,128)(2,1)S(1)}, bf16[64,768]{1,0:T(8,128)(2,1)S(1)}, u32[]{:S(2)}, u32[]{:S(2)}) collective-permute-start(bf16[64,768]{1,0:T(8,128)(2,1)S(1)} %get-tuple-element.53), channel_id=1, source_target_pairs={{0,2},{1,3},{2,0},{3,1},{4,6},{5,7},{6,4},{7,5},{8,10},{9,11},{10,... | collective-permute-start | bytes 294920 | tf_op jit(solution)/shard_map/ppermute | solution.py:205
  25.5 0.3 dispatch.4
  25.8 0.3 collective-permute-start.7
  26.1 0.4 collective-permute-start.1
  26.5 1.5 %collective-permute-start.2 = (bf16[64,768]{1,0:T(8,128)(2,1)S(1)}, bf16[64,768]{1,0:T(8,128)(2,1)S(1)}, u32[]{:S(2)}, u32[]{:S(2)}) collective-permute-start(bf16[64,768]{1,0:T(8,128)(2,1)S(1)} %get-tuple-element.49), channel_id=1, source_target_pairs={{0,2},{1,3},{2,0},{3,1},{4,6},{5,7},{6,4},{7,5},{8,10},{9,11},{10,... | collective-permute-start | bytes 294920 | tf_op jit(solution)/shard_map/ppermute | solution.py:205
  28.0 6.9 %gate_up.5 = (f32[256,2048]{1,0:T(8,128)}, f32[256,2048]{1,0:T(8,128)}) custom-call(s32[1]{0:T(128)} %bitcast.4.refs_0_.part_ref, bf16[64,768]{1,0:T(8,128)(2,1)S(1)} %get-tuple-element.55.refs_1_, bf16[64,768]{1,0:T(8,128)(2,1)S(1)} %collective-permute-done.9.refs_2_, bf16[64,768]{1,0:T(8,128)(2,1)S(1)} %collective-permute-done.10.refs_3_, ...), custom_call_target="tpu_custom_call" | custom-call | flops 1610612736 | bytes 14680064 | tf_op jit(solution)/shard_map/gate_up/pallas_call | solution.py:129
  35.0 7.0 %gate_up.6 = (f32[256,2048]{1,0:T(8,128)}, f32[256,2048]{1,0:T(8,128)}) custom-call(s32[1]{0:T(128)} %bitcast.3.refs_0_.part_ref, bf16[64,768]{1,0:T(8,128)(2,1)S(1)} %get-tuple-element.51.refs_1_, bf16[64,768]{1,0:T(8,128)(2,1)S(1)} %collective-permute-done.5.refs_2_, bf16[64,768]{1,0:T(8,128)(2,1)S(1)} %collective-permute-done.6.refs_3_, ...), custom_call_target="tpu_custom_call" | custom-call | flops 1610612736 | bytes 14680064 | tf_op jit(solution)/shard_map/gate_up/pallas_call | solution.py:129
  42.0 6.5 %gate_up.7.h_ref = bf16[256,2048]{1,0:T(8,128)(2,1)} custom-call(s32[1]{0:T(128)} %bitcast.2.refs_0_.part_ref, bf16[64,768]{1,0:T(8,128)(2,1)S(1)} %get-tuple-element.47.refs_1_, bf16[64,768]{1,0:T(8,128)(2,1)S(1)} %collective-permute-done.1.refs_2_, bf16[64,768]{1,0:T(8,128)(2,1)S(1)} %collective-permute-done.2.refs_3_, ...), custom_call_target="tpu_custom_call" | custom-call | flops 1610612736 | bytes 14680064 | tf_op jit(solution)/shard_map/gate_up/pallas_call | solution.py:129
  48.4 3.7 %down.4 = (bf16[64,768]{1,0:T(8,128)(2,1)S(1)}, bf16[64,768]{1,0:T(8,128)(2,1)S(1)}, bf16[64,768]{1,0:T(8,128)(2,1)S(1)}, bf16[64,768]{1,0:T(8,128)(2,1)S(1)}) custom-call(s32[1]{0:T(128)} %bitcast.2.refs_0_.part_ref, bf16[256,2048]{1,0:T(8,128)(2,1)} %gate_up.7.h_ref, bf16[1,2048,3072]{2,1,0:T(8,128)(2,1)} %w_ref.7), custom_call_target="tpu_custom_call" | custom-call | flops 805306368 | bytes 3538944 | tf_op jit(solution)/shard_map/down/pallas_call | solution.py:158
  52.2 0.6 collective-permute-start.15
  52.8 1.5 %collective-permute-start.16 = (bf16[64,768]{1,0:T(8,128)(2,1)S(1)}, bf16[64,768]{1,0:T(8,128)(2,1)S(1)}, u32[]{:S(2)}, u32[]{:S(2)}) collective-permute-start(bf16[64,768]{1,0:T(8,128)(2,1)S(1)} %get-tuple-element.71), channel_id=1, source_target_pairs={{0,2},{1,3},{2,0},{3,1},{4,6},{5,7},{6,4},{7,5},{8,10},{9,11},{10,... | collective-permute-start | bytes 294920 | tf_op jit(solution)/shard_map/ppermute | solution.py:205
  54.4 3.7 %down.5 = (bf16[64,768]{1,0:T(8,128)(2,1)S(1)}, bf16[64,768]{1,0:T(8,128)(2,1)S(1)}, bf16[64,768]{1,0:T(8,128)(2,1)S(1)}, bf16[64,768]{1,0:T(8,128)(2,1)S(1)}) custom-call(s32[1]{0:T(128)} %bitcast.3.refs_0_.part_ref, bf16[256,2048]{1,0:T(8,128)(2,1)} %gate_up.7.h_ref, bf16[1,2048,3072]{2,1,0:T(8,128)(2,1)} %w_ref.7), custom_call_target="tpu_custom_call" | custom-call | flops 805306368 | bytes 3538944 | tf_op jit(solution)/shard_map/down/pallas_call | solution.py:158
  58.1 0.7 collective-permute-start.19
  58.8 1.5 %collective-permute-start.20 = (bf16[64,768]{1,0:T(8,128)(2,1)S(1)}, bf16[64,768]{1,0:T(8,128)(2,1)S(1)}, u32[]{:S(2)}, u32[]{:S(2)}) collective-permute-start(bf16[64,768]{1,0:T(8,128)(2,1)S(1)} %get-tuple-element.75), channel_id=1, source_target_pairs={{0,2},{1,3},{2,0},{3,1},{4,6},{5,7},{6,4},{7,5},{8,10},{9,11},{10,... | collective-permute-start | bytes 294920 | tf_op jit(solution)/shard_map/ppermute | solution.py:205
  60.3 3.8 %down.6 = (bf16[64,768]{1,0:T(8,128)(2,1)S(1)}, bf16[64,768]{1,0:T(8,128)(2,1)S(1)}, bf16[64,768]{1,0:T(8,128)(2,1)S(1)}, bf16[64,768]{1,0:T(8,128)(2,1)S(1)}) custom-call(s32[1]{0:T(128)} %bitcast.4.refs_0_.part_ref, bf16[256,2048]{1,0:T(8,128)(2,1)} %gate_up.7.h_ref, bf16[1,2048,3072]{2,1,0:T(8,128)(2,1)} %w_ref.7), custom_call_target="tpu_custom_call" | custom-call | flops 805306368 | bytes 3538944 | tf_op jit(solution)/shard_map/down/pallas_call | solution.py:158
  64.1 0.6 collective-permute-start.23
  64.7 1.5 %collective-permute-start.24 = (bf16[64,768]{1,0:T(8,128)(2,1)S(1)}, bf16[64,768]{1,0:T(8,128)(2,1)S(1)}, u32[]{:S(2)}, u32[]{:S(2)}) collective-permute-start(bf16[64,768]{1,0:T(8,128)(2,1)S(1)} %get-tuple-element.79), channel_id=1, source_target_pairs={{0,2},{1,3},{2,0},{3,1},{4,6},{5,7},{6,4},{7,5},{8,10},{9,11},{10,... | collective-permute-start | bytes 294920 | tf_op jit(solution)/shard_map/ppermute | solution.py:205
  66.3 0.1 copy.7.logits_ref
  66.4 3.8 %down.7 = (bf16[64,768]{1,0:T(8,128)(2,1)S(1)}, bf16[64,768]{1,0:T(8,128)(2,1)S(1)}, bf16[64,768]{1,0:T(8,128)(2,1)S(1)}, bf16[64,768]{1,0:T(8,128)(2,1)S(1)}) custom-call(s32[1]{0:T(128)} %bitcast.5.refs_0_.part_ref, bf16[256,2048]{1,0:T(8,128)(2,1)} %gate_up.7.h_ref, bf16[1,2048,3072]{2,1,0:T(8,128)(2,1)} %w_ref.7), custom_call_target="tpu_custom_call" | custom-call | flops 805306368 | bytes 3538944 | tf_op jit(solution)/shard_map/down/pallas_call | solution.py:158
  70.2 0.3 combine.4
  70.5 0.7 collective-permute-start.27
  71.1 3.1 %collective-permute-start.18 = (bf16[128,768]{1,0:T(8,128)(2,1)S(1)}, bf16[128,768]{1,0:T(8,128)(2,1)S(1)}, u32[]{:S(2)}, u32[]{:S(2)}) collective-permute-start(bf16[128,768]{1,0:T(8,128)(2,1)S(1)} %combine.4), channel_id=1, source_target_pairs={{0,12},{4,8},{8,4},{12,0},{1,13},{5,9},{9,5},{13,1},{2,14},{6,10},... | collective-permute-start | bytes 589832 | tf_op jit(solution)/shard_map/ppermute | solution.py:205
  74.3 0.3 combine.5
  74.6 2.7 %collective-permute-start.22 = (bf16[128,768]{1,0:T(8,128)(2,1)S(1)}, bf16[128,768]{1,0:T(8,128)(2,1)S(1)}, u32[]{:S(2)}, u32[]{:S(2)}) collective-permute-start(bf16[128,768]{1,0:T(8,128)(2,1)S(1)} %combine.5), channel_id=1, source_target_pairs={{0,8},{4,12},{8,0},{12,4},{1,9},{5,13},{9,1},{13,5},{2,10},{6,14},... | collective-permute-start | bytes 589832 | tf_op jit(solution)/shard_map/ppermute | solution.py:205
  77.3 0.3 combine.6
  77.6 0.4 collective-permute-start.26
  78.0 1.5 %collective-permute-start.28 = (bf16[64,768]{1,0:T(8,128)(2,1)S(1)}, bf16[64,768]{1,0:T(8,128)(2,1)S(1)}, u32[]{:S(2)}, u32[]{:S(2)}) collective-permute-start(bf16[64,768]{1,0:T(8,128)(2,1)S(1)} %get-tuple-element.83), channel_id=1, source_target_pairs={{0,2},{1,3},{2,0},{3,1},{4,6},{5,7},{6,4},{7,5},{8,10},{9,11},{10,... | collective-permute-start | bytes 294920 | tf_op jit(solution)/shard_map/ppermute | solution.py:205
  79.5 3.3 %collective-permute-done.28.refs_2_ = bf16[64,768]{1,0:T(8,128)(2,1)S(1)} collective-permute-done((bf16[64,768]{1,0:T(8,128)(2,1)S(1)}, bf16[64,768]{1,0:T(8,128)(2,1)S(1)}, u32[]{:S(2)}, u32[]{:S(2)}) %collective-permute-start.28) | collective-permute-done | bytes 98336 | tf_op jit(solution)/shard_map/ppermute | solution.py:205
  82.8 1.8 %collective-permute-done.29.refs_3_ = bf16[64,768]{1,0:T(8,128)(2,1)S(1)} collective-permute-done((bf16[64,768]{1,0:T(8,128)(2,1)S(1)}, bf16[64,768]{1,0:T(8,128)(2,1)S(1)}, u32[]{:S(2)}, u32[]{:S(2)}) %collective-permute-start.29) | collective-permute-done | bytes 98336 | tf_op jit(solution)/shard_map/ppermute | solution.py:205
  84.6 0.3 combine.7
  84.9 7.5 %collective-permute-done.22 = bf16[128,768]{1,0:T(8,128)(2,1)S(1)} collective-permute-done((bf16[128,768]{1,0:T(8,128)(2,1)S(1)}, bf16[128,768]{1,0:T(8,128)(2,1)S(1)}, u32[]{:S(2)}, u32[]{:S(2)}) %collective-permute-start.22) | collective-permute-done | bytes 196640 | tf_op jit(solution)/shard_map/ppermute | solution.py:205
  92.5 0.8 add_convert_fusion
  (35 shorter events, 0.2 us)
Async XLA Ops:
  0.0 9.6 %collective-permute-start.8 = (bf16[128,768]{1,0:T(8,128)(2,1)}, bf16[128,768]{1,0:T(8,128)(2,1)S(1)}, u32[]{:S(2)}, u32[]{:S(2)}) collective-permute-start(bf16[128,768]{1,0:T(8,128)(2,1)} %block_ref.1), channel_id=1, source_target_pairs={{0,4},{4,0},{8,12},{12,8},{1,5},{5,1},{9,13},{13,9},{2,6},{6,2},{1... | collective-permute-start | bytes 589832 | tf_op jit(solution)/shard_map/ppermute | solution.py:205
  3.0 0.7 copy-start
  5.1 7.1 %collective-permute-start.12 = (bf16[64,768]{1,0:T(8,128)(2,1)S(1)}, bf16[64,768]{1,0:T(8,128)(2,1)S(1)}, u32[]{:S(2)}, u32[]{:S(2)}) collective-permute-start(bf16[64,768]{1,0:T(8,128)(2,1)S(1)} %get-tuple-element.60), channel_id=1, source_target_pairs={{0,1},{1,0},{2,3},{3,2},{4,5},{5,4},{6,7},{7,6},{8,9},{9,8},{10,11... | collective-permute-start | bytes 294920 | tf_op jit(solution)/shard_map/ppermute | solution.py:205
  5.1 8.6 %collective-permute-start.13 = (bf16[64,768]{1,0:T(8,128)(2,1)S(1)}, bf16[64,768]{1,0:T(8,128)(2,1)S(1)}, u32[]{:S(2)}, u32[]{:S(2)}) collective-permute-start(bf16[64,768]{1,0:T(8,128)(2,1)S(1)} %get-tuple-element.61), channel_id=1, source_target_pairs={{0,2},{1,3},{2,0},{3,1},{4,6},{5,7},{6,4},{7,5},{8,10},{9,11},{10,... | collective-permute-start | bytes 294920 | tf_op jit(solution)/shard_map/ppermute | solution.py:205
  6.7 7.0 %collective-permute-start.14 = (bf16[64,768]{1,0:T(8,128)(2,1)S(1)}, bf16[64,768]{1,0:T(8,128)(2,1)S(1)}, u32[]{:S(2)}, u32[]{:S(2)}) collective-permute-start(bf16[64,768]{1,0:T(8,128)(2,1)S(1)} %get-tuple-element.62), channel_id=1, source_target_pairs={{0,3},{1,2},{2,1},{3,0},{4,7},{5,6},{6,5},{7,4},{8,11},{9,10},{10,... | collective-permute-start | bytes 294920 | tf_op jit(solution)/shard_map/ppermute | solution.py:205
  7.0 16.6 %collective-permute-start.4 = (bf16[128,768]{1,0:T(8,128)(2,1)}, bf16[128,768]{1,0:T(8,128)(2,1)S(1)}, u32[]{:S(2)}, u32[]{:S(2)}) collective-permute-start(bf16[128,768]{1,0:T(8,128)(2,1)} %block_ref.1), channel_id=1, source_target_pairs={{0,8},{4,12},{8,0},{12,4},{1,9},{5,13},{9,1},{13,5},{2,10},{6,14},... | collective-permute-start | bytes 589832 | tf_op jit(solution)/shard_map/ppermute | solution.py:205
  9.6 14.3 %collective-permute-start = (bf16[128,768]{1,0:T(8,128)(2,1)}, bf16[128,768]{1,0:T(8,128)(2,1)S(1)}, u32[]{:S(2)}, u32[]{:S(2)}) collective-permute-start(bf16[128,768]{1,0:T(8,128)(2,1)} %block_ref.1), channel_id=1, source_target_pairs={{0,12},{4,8},{8,4},{12,0},{1,13},{5,9},{9,5},{13,1},{2,14},{6,10},... | collective-permute-start | bytes 589832 | tf_op jit(solution)/shard_map/ppermute | solution.py:205
  12.2 13.6 %collective-permute-start.10 = (bf16[64,768]{1,0:T(8,128)(2,1)S(1)}, bf16[64,768]{1,0:T(8,128)(2,1)S(1)}, u32[]{:S(2)}, u32[]{:S(2)}) collective-permute-start(bf16[64,768]{1,0:T(8,128)(2,1)S(1)} %get-tuple-element.57), channel_id=1, source_target_pairs={{0,2},{1,3},{2,0},{3,1},{4,6},{5,7},{6,4},{7,5},{8,10},{9,11},{10,... | collective-permute-start | bytes 294920 | tf_op jit(solution)/shard_map/ppermute | solution.py:205
  13.7 12.4 %collective-permute-start.11 = (bf16[64,768]{1,0:T(8,128)(2,1)S(1)}, bf16[64,768]{1,0:T(8,128)(2,1)S(1)}, u32[]{:S(2)}, u32[]{:S(2)}) collective-permute-start(bf16[64,768]{1,0:T(8,128)(2,1)S(1)} %get-tuple-element.58), channel_id=1, source_target_pairs={{0,3},{1,2},{2,1},{3,0},{4,7},{5,6},{6,5},{7,4},{8,11},{9,10},{10,... | collective-permute-start | bytes 294920 | tf_op jit(solution)/shard_map/ppermute | solution.py:205
  13.7 12.8 %collective-permute-start.9 = (bf16[64,768]{1,0:T(8,128)(2,1)S(1)}, bf16[64,768]{1,0:T(8,128)(2,1)S(1)}, u32[]{:S(2)}, u32[]{:S(2)}) collective-permute-start(bf16[64,768]{1,0:T(8,128)(2,1)S(1)} %get-tuple-element.56), channel_id=1, source_target_pairs={{0,1},{1,0},{2,3},{3,2},{4,5},{5,4},{6,7},{7,6},{8,9},{9,8},{10,11... | collective-permute-start | bytes 294920 | tf_op jit(solution)/shard_map/ppermute | solution.py:205
  23.9 11.0 %collective-permute-start.5 = (bf16[64,768]{1,0:T(8,128)(2,1)S(1)}, bf16[64,768]{1,0:T(8,128)(2,1)S(1)}, u32[]{:S(2)}, u32[]{:S(2)}) collective-permute-start(bf16[64,768]{1,0:T(8,128)(2,1)S(1)} %get-tuple-element.52), channel_id=1, source_target_pairs={{0,1},{1,0},{2,3},{3,2},{4,5},{5,4},{6,7},{7,6},{8,9},{9,8},{10,11... | collective-permute-start | bytes 294920 | tf_op jit(solution)/shard_map/ppermute | solution.py:205
  23.9 11.0 %collective-permute-start.6 = (bf16[64,768]{1,0:T(8,128)(2,1)S(1)}, bf16[64,768]{1,0:T(8,128)(2,1)S(1)}, u32[]{:S(2)}, u32[]{:S(2)}) collective-permute-start(bf16[64,768]{1,0:T(8,128)(2,1)S(1)} %get-tuple-element.53), channel_id=1, source_target_pairs={{0,2},{1,3},{2,0},{3,1},{4,6},{5,7},{6,4},{7,5},{8,10},{9,11},{10,... | collective-permute-start | bytes 294920 | tf_op jit(solution)/shard_map/ppermute | solution.py:205
  25.8 9.2 %collective-permute-start.7 = (bf16[64,768]{1,0:T(8,128)(2,1)S(1)}, bf16[64,768]{1,0:T(8,128)(2,1)S(1)}, u32[]{:S(2)}, u32[]{:S(2)}) collective-permute-start(bf16[64,768]{1,0:T(8,128)(2,1)S(1)} %get-tuple-element.54), channel_id=1, source_target_pairs={{0,3},{1,2},{2,1},{3,0},{4,7},{5,6},{6,5},{7,4},{8,11},{9,10},{10,... | collective-permute-start | bytes 294920 | tf_op jit(solution)/shard_map/ppermute | solution.py:205
  26.1 15.8 %collective-permute-start.1 = (bf16[64,768]{1,0:T(8,128)(2,1)S(1)}, bf16[64,768]{1,0:T(8,128)(2,1)S(1)}, u32[]{:S(2)}, u32[]{:S(2)}) collective-permute-start(bf16[64,768]{1,0:T(8,128)(2,1)S(1)} %get-tuple-element.48), channel_id=1, source_target_pairs={{0,1},{1,0},{2,3},{3,2},{4,5},{5,4},{6,7},{7,6},{8,9},{9,8},{10,11... | collective-permute-start | bytes 294920 | tf_op jit(solution)/shard_map/ppermute | solution.py:205
  26.5 15.5 %collective-permute-start.2 = (bf16[64,768]{1,0:T(8,128)(2,1)S(1)}, bf16[64,768]{1,0:T(8,128)(2,1)S(1)}, u32[]{:S(2)}, u32[]{:S(2)}) collective-permute-start(bf16[64,768]{1,0:T(8,128)(2,1)S(1)} %get-tuple-element.49), channel_id=1, source_target_pairs={{0,2},{1,3},{2,0},{3,1},{4,6},{5,7},{6,4},{7,5},{8,10},{9,11},{10,... | collective-permute-start | bytes 294920 | tf_op jit(solution)/shard_map/ppermute | solution.py:205
  34.9 7.1 %collective-permute-start.3 = (bf16[64,768]{1,0:T(8,128)(2,1)S(1)}, bf16[64,768]{1,0:T(8,128)(2,1)S(1)}, u32[]{:S(2)}, u32[]{:S(2)}) collective-permute-start(bf16[64,768]{1,0:T(8,128)(2,1)S(1)} %get-tuple-element.50), channel_id=1, source_target_pairs={{0,3},{1,2},{2,1},{3,0},{4,7},{5,6},{6,5},{7,4},{8,11},{9,10},{10,... | collective-permute-start | bytes 294920 | tf_op jit(solution)/shard_map/ppermute | solution.py:205
  52.2 8.1 %collective-permute-start.15 = (bf16[64,768]{1,0:T(8,128)(2,1)S(1)}, bf16[64,768]{1,0:T(8,128)(2,1)S(1)}, u32[]{:S(2)}, u32[]{:S(2)}) collective-permute-start(bf16[64,768]{1,0:T(8,128)(2,1)S(1)} %get-tuple-element.70), channel_id=1, source_target_pairs={{0,1},{1,0},{2,3},{3,2},{4,5},{5,4},{6,7},{7,6},{8,9},{9,8},{10,11... | collective-permute-start | bytes 294920 | tf_op jit(solution)/shard_map/ppermute | solution.py:205
  52.8 11.3 %collective-permute-start.16 = (bf16[64,768]{1,0:T(8,128)(2,1)S(1)}, bf16[64,768]{1,0:T(8,128)(2,1)S(1)}, u32[]{:S(2)}, u32[]{:S(2)}) collective-permute-start(bf16[64,768]{1,0:T(8,128)(2,1)S(1)} %get-tuple-element.71), channel_id=1, source_target_pairs={{0,2},{1,3},{2,0},{3,1},{4,6},{5,7},{6,4},{7,5},{8,10},{9,11},{10,... | collective-permute-start | bytes 294920 | tf_op jit(solution)/shard_map/ppermute | solution.py:205
  54.4 10.4 %collective-permute-start.17 = (bf16[64,768]{1,0:T(8,128)(2,1)S(1)}, bf16[64,768]{1,0:T(8,128)(2,1)S(1)}, u32[]{:S(2)}, u32[]{:S(2)}) collective-permute-start(bf16[64,768]{1,0:T(8,128)(2,1)S(1)} %get-tuple-element.72), channel_id=1, source_target_pairs={{0,3},{1,2},{2,1},{3,0},{4,7},{5,6},{6,5},{7,4},{8,11},{9,10},{10,... | collective-permute-start | bytes 294920 | tf_op jit(solution)/shard_map/ppermute | solution.py:205
  58.1 8.2 %collective-permute-start.19 = (bf16[64,768]{1,0:T(8,128)(2,1)S(1)}, bf16[64,768]{1,0:T(8,128)(2,1)S(1)}, u32[]{:S(2)}, u32[]{:S(2)}) collective-permute-start(bf16[64,768]{1,0:T(8,128)(2,1)S(1)} %get-tuple-element.74), channel_id=1, source_target_pairs={{0,1},{1,0},{2,3},{3,2},{4,5},{5,4},{6,7},{7,6},{8,9},{9,8},{10,11... | collective-permute-start | bytes 294920 | tf_op jit(solution)/shard_map/ppermute | solution.py:205
  58.8 11.7 %collective-permute-start.20 = (bf16[64,768]{1,0:T(8,128)(2,1)S(1)}, bf16[64,768]{1,0:T(8,128)(2,1)S(1)}, u32[]{:S(2)}, u32[]{:S(2)}) collective-permute-start(bf16[64,768]{1,0:T(8,128)(2,1)S(1)} %get-tuple-element.75), channel_id=1, source_target_pairs={{0,2},{1,3},{2,0},{3,1},{4,6},{5,7},{6,4},{7,5},{8,10},{9,11},{10,... | collective-permute-start | bytes 294920 | tf_op jit(solution)/shard_map/ppermute | solution.py:205
  60.3 6.0 %copy-start.1 = (f32[128,2]{0,1:T(2,128)S(1)}, f32[128,2]{0,1:T(2,128)}, u32[]{:S(2)}) copy-start(f32[128,2]{0,1:T(2,128)} %param.8) | copy-start | bytes 3076
  60.3 10.8 %collective-permute-start.21 = (bf16[64,768]{1,0:T(8,128)(2,1)S(1)}, bf16[64,768]{1,0:T(8,128)(2,1)S(1)}, u32[]{:S(2)}, u32[]{:S(2)}) collective-permute-start(bf16[64,768]{1,0:T(8,128)(2,1)S(1)} %get-tuple-element.76), channel_id=1, source_target_pairs={{0,3},{1,2},{2,1},{3,0},{4,7},{5,6},{6,5},{7,4},{8,11},{9,10},{10,... | collective-permute-start | bytes 294920 | tf_op jit(solution)/shard_map/ppermute | solution.py:205
  64.1 10.5 %collective-permute-start.23 = (bf16[64,768]{1,0:T(8,128)(2,1)S(1)}, bf16[64,768]{1,0:T(8,128)(2,1)S(1)}, u32[]{:S(2)}, u32[]{:S(2)}) collective-permute-start(bf16[64,768]{1,0:T(8,128)(2,1)S(1)} %get-tuple-element.78), channel_id=1, source_target_pairs={{0,1},{1,0},{2,3},{3,2},{4,5},{5,4},{6,7},{7,6},{8,9},{9,8},{10,11... | collective-permute-start | bytes 294920 | tf_op jit(solution)/shard_map/ppermute | solution.py:205
  64.7 12.6 %collective-permute-start.24 = (bf16[64,768]{1,0:T(8,128)(2,1)S(1)}, bf16[64,768]{1,0:T(8,128)(2,1)S(1)}, u32[]{:S(2)}, u32[]{:S(2)}) collective-permute-start(bf16[64,768]{1,0:T(8,128)(2,1)S(1)} %get-tuple-element.79), channel_id=1, source_target_pairs={{0,2},{1,3},{2,0},{3,1},{4,6},{5,7},{6,4},{7,5},{8,10},{9,11},{10,... | collective-permute-start | bytes 294920 | tf_op jit(solution)/shard_map/ppermute | solution.py:205
  66.3 11.0 %collective-permute-start.25 = (bf16[64,768]{1,0:T(8,128)(2,1)S(1)}, bf16[64,768]{1,0:T(8,128)(2,1)S(1)}, u32[]{:S(2)}, u32[]{:S(2)}) collective-permute-start(bf16[64,768]{1,0:T(8,128)(2,1)S(1)} %get-tuple-element.80), channel_id=1, source_target_pairs={{0,3},{1,2},{2,1},{3,0},{4,7},{5,6},{6,5},{7,4},{8,11},{9,10},{10,... | collective-permute-start | bytes 294920 | tf_op jit(solution)/shard_map/ppermute | solution.py:205
  70.5 9.0 %collective-permute-start.27 = (bf16[64,768]{1,0:T(8,128)(2,1)S(1)}, bf16[64,768]{1,0:T(8,128)(2,1)S(1)}, u32[]{:S(2)}, u32[]{:S(2)}) collective-permute-start(bf16[64,768]{1,0:T(8,128)(2,1)S(1)} %get-tuple-element.82), channel_id=1, source_target_pairs={{0,1},{1,0},{2,3},{3,2},{4,5},{5,4},{6,7},{7,6},{8,9},{9,8},{10,11... | collective-permute-start | bytes 294920 | tf_op jit(solution)/shard_map/ppermute | solution.py:205
  71.1 13.8 %collective-permute-start.18 = (bf16[128,768]{1,0:T(8,128)(2,1)S(1)}, bf16[128,768]{1,0:T(8,128)(2,1)S(1)}, u32[]{:S(2)}, u32[]{:S(2)}) collective-permute-start(bf16[128,768]{1,0:T(8,128)(2,1)S(1)} %combine.4), channel_id=1, source_target_pairs={{0,12},{4,8},{8,4},{12,0},{1,13},{5,9},{9,5},{13,1},{2,14},{6,10},... | collective-permute-start | bytes 589832 | tf_op jit(solution)/shard_map/ppermute | solution.py:205
  74.6 17.9 %collective-permute-start.22 = (bf16[128,768]{1,0:T(8,128)(2,1)S(1)}, bf16[128,768]{1,0:T(8,128)(2,1)S(1)}, u32[]{:S(2)}, u32[]{:S(2)}) collective-permute-start(bf16[128,768]{1,0:T(8,128)(2,1)S(1)} %combine.5), channel_id=1, source_target_pairs={{0,8},{4,12},{8,0},{12,4},{1,9},{5,13},{9,1},{13,5},{2,10},{6,14},... | collective-permute-start | bytes 589832 | tf_op jit(solution)/shard_map/ppermute | solution.py:205
  77.6 14.9 %collective-permute-start.26 = (bf16[128,768]{1,0:T(8,128)(2,1)S(1)}, bf16[128,768]{1,0:T(8,128)(2,1)S(1)}, u32[]{:S(2)}, u32[]{:S(2)}) collective-permute-start(bf16[128,768]{1,0:T(8,128)(2,1)S(1)} %combine.6), channel_id=1, source_target_pairs={{0,4},{4,0},{8,12},{12,8},{1,5},{5,1},{9,13},{13,9},{2,6},{6,2},{1... | collective-permute-start | bytes 589832 | tf_op jit(solution)/shard_map/ppermute | solution.py:205
  78.0 4.8 %collective-permute-start.28 = (bf16[64,768]{1,0:T(8,128)(2,1)S(1)}, bf16[64,768]{1,0:T(8,128)(2,1)S(1)}, u32[]{:S(2)}, u32[]{:S(2)}) collective-permute-start(bf16[64,768]{1,0:T(8,128)(2,1)S(1)} %get-tuple-element.83), channel_id=1, source_target_pairs={{0,2},{1,3},{2,0},{3,1},{4,6},{5,7},{6,4},{7,5},{8,10},{9,11},{10,... | collective-permute-start | bytes 294920 | tf_op jit(solution)/shard_map/ppermute | solution.py:205
  79.5 5.1 %collective-permute-start.29 = (bf16[64,768]{1,0:T(8,128)(2,1)S(1)}, bf16[64,768]{1,0:T(8,128)(2,1)S(1)}, u32[]{:S(2)}, u32[]{:S(2)}) collective-permute-start(bf16[64,768]{1,0:T(8,128)(2,1)S(1)} %get-tuple-element.84), channel_id=1, source_target_pairs={{0,3},{1,2},{2,1},{3,0},{4,7},{5,6},{6,5},{7,4},{8,11},{9,10},{10,... | collective-permute-start | bytes 294920 | tf_op jit(solution)/shard_map/ppermute | solution.py:205

commit v3 on v2

--- a/solution.py
+++ b/solution.py
@@ -12,16 +12,12 @@
 MIB = 1024 * 1024
 
 
-def params(mib=16):
+def params(mib=6):
     return pltpu.CompilerParams(vmem_limit_bytes=mib * MIB)
 
 
 def cost(flops, moved):
     return pl.CostEstimate(flops=flops, bytes_accessed=moved, transcendentals=0)
-
-
-def whole(shape):
-    return pl.BlockSpec(shape, lambda *_: (0,) * len(shape))
 
 
 def routing_kernel(me_ref, ids_ref, placed_ref, pick_ref, *, experts, capacity):
@@ -91,84 +87,132 @@
     )(placed, block)
 
 
-def gate_up_kernel(*refs, experts, first, last):
+def fetch_copies(parts_ref, sources, targets, sems):
+    copies = []
+    for i, (source, target) in enumerate(zip(sources, targets)):
+        count = target.shape[0]
+        start = pl.multiple_of(parts_ref[i] * count, count)
+        copies.append(
+            pltpu.make_async_copy(source.at[0, pl.ds(start, count)], target, sems.at[i])
+        )
+    return copies
+
+
+def prefetch_kernel(parts_ref, after_ref, *refs):
+    half = len(refs) // 2
+    copies = fetch_copies(parts_ref, refs[:half], refs[half:-1], refs[-1])
+    for copy in copies:
+        copy.start()
+    for copy in copies:
+        copy.wait()
+
+
+def fetch_specs(fetches):
+    sources = [pltpu.with_memory_space_constraint(w, pltpu.HBM) for w, _, _ in fetches]
+    parts = jnp.stack([jnp.asarray(part, jnp.int32) for _, part, _ in fetches] + [jnp.int32(0)])
+    shapes = [pltpu.VMEM((count, w.shape[2]), w.dtype) for w, _, count in fetches]
+    return parts, sources, shapes
+
+
+def prefetch(fetches, after):
+    parts, sources, shapes = fetch_specs(fetches)
+    return pl.pallas_call(
+        prefetch_kernel,
+        out_shape=shapes,
+        in_specs=[pl.BlockSpec(memory_space=pltpu.SMEM)]
+        + [pl.BlockSpec(memory_space=pl.ANY)] * (1 + len(sources)),
+        out_specs=[pl.BlockSpec(memory_space=pltpu.VMEM)] * len(shapes),
+        scratch_shapes=[pltpu.SemaphoreType.DMA((len(shapes),))],
+        cost_estimate=cost(0, sum(2 * count * w.shape[2] for w, _, count in fetches)),
+        compiler_params=params(),
+        name="prefetch",
+    )(parts, after, *sources)
+
+
+def gate_up_kernel(*refs, experts, first, last, fetched):
+    parts_ref = refs[0]
     x_refs = refs[1 : 1 + experts]
     gate_w, up_w = refs[1 + experts : 3 + experts]
-    rest = refs[3 + experts :]
+    rest = list(refs[3 + experts :])
     if not first:
         old_gate, old_up = rest[:2]
         rest = rest[2:]
+    copies = []
+    if fetched:
+        sources, rest = rest[:fetched], rest[fetched:]
+        copies = fetch_copies(parts_ref, sources, rest[-1 - fetched : -1], rest[-1])
+    for copy in copies:
+        copy.start()
     x = jnp.concatenate([r[...] for r in x_refs], axis=0)
-    gate = jnp.dot(x, gate_w[0], preferred_element_type=F32)
-    up = jnp.dot(x, up_w[0], preferred_element_type=F32)
-    if not first:
-        gate = gate + old_gate[...]
-        up = up + old_up[...]
-    if last:
-        rest[0][...] = (gate / (1.0 + jnp.exp(-gate)) * up).astype(BF16)
-    else:
-        rest[0][...] = gate
-        rest[1][...] = up
-
-
-def gate_up(part, x_blocks, gate_w, up_w, sums, last):
+    hidden = gate_w.shape[1]
+    tile = min(512, hidden)
+    for n in range(hidden // tile):
+        columns = slice(n * tile, (n + 1) * tile)
+        gate = jnp.dot(x, gate_w[:, columns], preferred_element_type=F32)
+        up = jnp.dot(x, up_w[:, columns], preferred_element_type=F32)
+        if not first:
+            gate = gate + old_gate[:, columns]
+            up = up + old_up[:, columns]
+        if last:
+            rest[0][:, columns] = (gate / (1.0 + jnp.exp(-gate)) * up).astype(BF16)
+        else:
+            rest[0][:, columns] = gate
+            rest[1][:, columns] = up
+    for copy in copies:
+        copy.wait()
+
+
+def gate_up(x_blocks, gate_w, up_w, sums, last, fetches):
     experts = len(x_blocks)
     capacity, width = x_blocks[0].shape
     rows = experts * capacity
-    hidden = gate_w.shape[2]
-    tile = min(512, hidden)
+    hidden = gate_w.shape[1]
     first = sums is None
-    weight = pl.BlockSpec((1, width, tile), lambda n, part: (0, part[0], n))
-    column = pl.BlockSpec((rows, tile), lambda n, part: (0, n))
+    parts, sources, shapes = fetch_specs(fetches)
+    operands = 2 + experts + (0 if first else 2)
     if last:
-        out_shape = jax.ShapeDtypeStruct((rows, hidden), BF16)
-        out_specs = column
+        out_shape = [pltpu.VMEM((rows, hidden), BF16)]
     else:
-        out_shape = [jax.ShapeDtypeStruct((rows, hidden), F32)] * 2
-        out_specs = [column] * 2
-    return pl.pallas_call(
-        functools.partial(gate_up_kernel, experts=experts, first=first, last=last),
-        out_shape=out_shape,
-        grid_spec=pltpu.PrefetchScalarGridSpec(
-            num_scalar_prefetch=1,
-            grid=(hidden // tile,),
-            in_specs=[whole((capacity, width))] * experts
-            + [weight] * 2
-            + ([] if first else [column] * 2),
-            out_specs=out_specs,
+        out_shape = [pltpu.VMEM((rows, hidden), F32)] * 2
+    results = pl.pallas_call(
+        functools.partial(
+            gate_up_kernel, experts=experts, first=first, last=last, fetched=len(fetches)
         ),
-        cost_estimate=cost(4 * rows * width * hidden, 4 * width * hidden + 16 * rows * hidden),
-        compiler_params=params(53),
+        out_shape=out_shape + shapes,
+        in_specs=[pl.BlockSpec(memory_space=pltpu.SMEM)]
+        + [pl.BlockSpec(memory_space=pltpu.VMEM)] * operands
+        + [pl.BlockSpec(memory_space=pl.ANY)] * len(sources),
+        out_specs=[pl.BlockSpec(memory_space=pltpu.VMEM)] * len(out_shape + shapes),
+        scratch_shapes=[pltpu.SemaphoreType.DMA((len(fetches),))] if fetches else [],
+        input_output_aliases={} if first or last else {3 + experts: 0, 4 + experts: 1},
+        cost_estimate=cost(4 * rows * width * hidden, 4 * width * hidden),
+        compiler_params=params(),
         name="gate_up",
-    )(part.reshape(1), *x_blocks, gate_w, up_w, *(() if first else sums))
+    )(parts, *x_blocks, gate_w, up_w, *(() if first else sums), *sources)
+    return results[: len(out_shape)], results[len(out_shape) :]
 
 
 def down_kernel(part_ref, h_ref, w_ref, *out_refs):
-    capacity = out_refs[0].shape[0]
-    y = jnp.dot(h_ref[...], w_ref[0], preferred_element_type=F32).astype(BF16)
-    for d, out in enumerate(out_refs):
-        out[...] = y[d * capacity : (d + 1) * capacity]
+    capacity, width = out_refs[0].shape
+    tile = min(256, width)
+    for n in range(width // tile):
+        start = pl.multiple_of(part_ref[0] * width + n * tile, tile)
+        y = jnp.dot(h_ref[...], w_ref[:, pl.ds(start, tile)], preferred_element_type=F32)
+        for d, out in enumerate(out_refs):
+            out[:, n * tile : (n + 1) * tile] = y[d * capacity : (d + 1) * capacity].astype(BF16)
 
 
 def down(part, hidden, down_w, width, experts):
     rows, depth = hidden.shape
     capacity = rows // experts
-    tile = min(256, width)
-    steps = width // tile
     return pl.pallas_call(
         down_kernel,
         out_shape=[jax.ShapeDtypeStruct((capacity, width), BF16)] * experts,
-        grid_spec=pltpu.PrefetchScalarGridSpec(
-            num_scalar_prefetch=1,
-            grid=(steps,),
-            in_specs=[
-                whole((rows, depth)),
-                pl.BlockSpec((1, depth, tile), lambda n, part: (0, 0, part[0] * steps + n)),
-            ],
-            out_specs=[pl.BlockSpec((capacity, tile), lambda n, part: (0, n))] * experts,
-        ),
+        in_specs=[pl.BlockSpec(memory_space=pltpu.SMEM)]
+        + [pl.BlockSpec(memory_space=pltpu.VMEM)] * 2,
+        out_specs=[pl.BlockSpec(memory_space=pltpu.VMEM)] * experts,
         cost_estimate=cost(2 * rows * depth * width, 2 * depth * width + 2 * rows * width),
-        compiler_params=params(53),
+        compiler_params=params(),
         name="down",
     )(part.reshape(1), hidden, down_w)
 
@@ -225,16 +269,35 @@
         blocks = [lax.all_gather(tokens, "tensor", axis=1, tiled=True)]
     placed, pick = place(me, expert_ids, experts, capacity)
 
+    arrived = []
+    for d in distances:
+        outgoing = dispatch(placed, blocks[d], experts, capacity)
+        arrived.append([swap(block, "expert", e) for e, block in enumerate(outgoing)])
+        if d == 0:
+            started = outgoing[0]
+
+    def slices(chosen):
+        return [(w, part_of(d), width) for d in chosen for w in (gate_weight, up_weight)]
+
+    weights = list(prefetch(slices(distances[:2]), started))
     sums = None
     for d in distances:
-        outgoing = dispatch(placed, blocks[d], experts, capacity)
-        arrived = [swap(block, "expert", e) for e, block in enumerate(outgoing)]
-        sums = gate_up(part_of(d), arrived, gate_weight, up_weight, sums, d == distances[-1])
-    hidden = sums
+        fetches = slices(distances[2:]) if d == 0 else []
+        with_down = d == min(1, distances[-1])
+        if with_down:
+            fetches = fetches + [(down_weight, 0, down_weight.shape[1])]
+        sums, fetched = gate_up(
+            arrived[d], *weights[2 * d : 2 * d + 2], sums, d == distances[-1], fetches
+        )
+        if with_down:
+            down_w = fetched[-1]
+            fetched = fetched[:-1]
+        weights.extend(fetched)
+    hidden = sums[0]
 
     total = []
     for d in reversed(distances):
-        terms = down(part_of(d), hidden, down_weight, width, experts)
+        terms = down(part_of(d), hidden, down_w, width, experts)
         returned = [swap(block, "expert", e) for e, block in enumerate(terms)]
         mixed = combine(pick, route_logits, returned)
         if not direct:

time: 93.7 us -> 81.7 us (0.87)
  Pallas kernels: 44.6 us -> 30.8 us
  local copies, waits for them, and re-layouts: 0.8 us -> 5.54 us
  starting transfers between devices: 30.9 us -> 28.5 us
    pallas_call x4, Pallas kernels: 15 us -> 4.08 us  [down(): pl.pallas_call(down_kernel, out_shape=[jax.ShapeDtypeStruct((capacity, wi...]
    pallas_call x4, Pallas kernels: 26.3 us -> 18.1 us  [gate_up(): pl.pallas_call(functools.partial(gate_up_kernel, experts=experts, first=f...]
    pallas_call x0 -> x1, Pallas kernels: none -> 5.23 us  [prefetch(): pl.pallas_call(prefetch_kernel, out_shape=shapes, in_specs=[pl.BlockSpec(...]
    unnamed x5 -> x9, local copies, waits for them, and re-layouts: 0.8 us -> 5.37 us
    ppermute x30, starting transfers between devices: 30.9 us -> 28.5 us  [swap(): return lax.ppermute(value, axis, [(i, i ^ distance) for i in range(count)])]
  transfers between devices with their start and end apart: 30 -> 30, of which waited for: 4 -> 4; matrix products, arithmetic and copies ran while one was open for 0% -> 0% of each run, Pallas kernels for 37% -> 34%
where the time goes in v3:
time: 81.7 us; the launch traced here: 81.5 us
  Pallas kernels  30.8 us (38%)
  starting transfers between devices  28.5 us (35%)
  waiting for transfers between devices  15.5 us (19%)
  local copies, waits for them, and re-layouts  5.54 us (7%)
    ppermute x30, starting transfers between devices, swap(): return lax.ppermute(value, axis, [(i, i ^ distance) for i in range(count)])  28.5 us
    pallas_call x4, Pallas kernels, gate_up(): pl.pallas_call(functools.partial(gate_up_kernel, experts=experts, first=f...  18.1 us
    ppermute x30, waiting for transfers between devices, swap(): return lax.ppermute(value, axis, [(i, i ^ distance) for i in range(count)])  15.5 us
    unnamed x9, local copies, waits for them, and re-layouts  5.37 us
    pallas_call x1, Pallas kernels, prefetch(): pl.pallas_call(prefetch_kernel, out_shape=shapes, in_specs=[pl.BlockSpec(...  5.23 us
    pallas_call x4, Pallas kernels, down(): pl.pallas_call(down_kernel, out_shape=[jax.ShapeDtypeStruct((capacity, wi...  4.08 us
    pallas_call x4, Pallas kernels, dispatch(): pl.pallas_call(dispatch_kernel, out_shape=[jax.ShapeDtypeStruct((capacity...  1.95 us
  transfers between devices with their start and end apart: 30, of which 4 were waited for; matrix products, arithmetic and copies ran while one was open for 0% of the time, Pallas kernels for 34%

profile of v3, /device:TPU:0, one launch (start us, length us, event | category | flops | bytes accessed | tf_op | source)
XLA Modules:
  0.0 81.5 jit_solution(8109984728529723188)
XLA Ops:
  0.0 3.0 %collective-permute-start.11 = (bf16[128,768]{1,0:T(8,128)(2,1)}, bf16[128,768]{1,0:T(8,128)(2,1)S(1)}, u32[]{:S(2)}, u32[]{:S(2)}) collective-permute-start(bf16[128,768]{1,0:T(8,128)(2,1)} %block_ref.1), channel_id=1, source_target_pairs={{0,4},{4,0},{8,12},{12,8},{1,5},{5,1},{9,13},{13,9},{2,6},{6,2},{1... | collective-permute-start | bytes 589832 | tf_op jit(solution)/shard_map/ppermute | solution.py:249
  3.0 0.7 copy-done.2
  3.7 0.2 routing.1
  3.9 1.2 %dispatch.5 = (bf16[64,768]{1,0:T(8,128)(2,1)S(1)}, bf16[64,768]{1,0:T(8,128)(2,1)S(1)}, bf16[64,768]{1,0:T(8,128)(2,1)S(1)}, bf16[64,768]{1,0:T(8,128)(2,1)S(1)}) custom-call(bf16[256,128]{1,0:T(8,128)(2,1)S(1)} %get-tuple-element.55.placed_ref, bf16[128,768]{1,0:T(8,128)(2,1)} %block_ref.1), custom_call_target="tpu_custom_call" | custom-call | flops 50331648 | bytes 393216 | tf_op jit(solution)/shard_map/dispatch/pallas_call | solution.py:79
  5.1 1.6 %collective-permute-start.5 = (bf16[64,768]{1,0:T(8,128)(2,1)S(1)}, bf16[64,768]{1,0:T(8,128)(2,1)S(1)}, u32[]{:S(2)}, u32[]{:S(2)}) collective-permute-start(bf16[64,768]{1,0:T(8,128)(2,1)S(1)} %get-tuple-element.62), channel_id=1, source_target_pairs={{0,2},{1,3},{2,0},{3,1},{4,6},{5,7},{6,4},{7,5},{8,10},{9,11},{10,... | collective-permute-start | bytes 294920 | tf_op jit(solution)/shard_map/ppermute | solution.py:249
  6.7 0.3 collective-permute-start.6
  7.0 2.6 %collective-permute-start.7 = (bf16[128,768]{1,0:T(8,128)(2,1)}, bf16[128,768]{1,0:T(8,128)(2,1)S(1)}, u32[]{:S(2)}, u32[]{:S(2)}) collective-permute-start(bf16[128,768]{1,0:T(8,128)(2,1)} %block_ref.1), channel_id=1, source_target_pairs={{0,8},{4,12},{8,0},{12,4},{1,9},{5,13},{9,1},{13,5},{2,10},{6,14},... | collective-permute-start | bytes 589832 | tf_op jit(solution)/shard_map/ppermute | solution.py:249
  9.6 2.3 %collective-permute-start = (bf16[128,768]{1,0:T(8,128)(2,1)}, bf16[128,768]{1,0:T(8,128)(2,1)S(1)}, u32[]{:S(2)}, u32[]{:S(2)}) collective-permute-start(bf16[128,768]{1,0:T(8,128)(2,1)} %block_ref.1), channel_id=1, source_target_pairs={{0,12},{4,8},{8,4},{12,0},{1,13},{5,9},{9,5},{13,1},{2,14},{6,10},... | collective-permute-start | bytes 589832 | tf_op jit(solution)/shard_map/ppermute | solution.py:249
  12.1 5.2 %prefetch.1 = (bf16[768,2048]{1,0:T(8,128)(2,1)S(1)}, bf16[768,2048]{1,0:T(8,128)(2,1)S(1)}, bf16[768,2048]{1,0:T(8,128)(2,1)S(1)}, bf16[768,2048]{1,0:T(8,128)(2,1)S(1)}) custom-call(s32[5]{0:T(128)S(1)} %stack.24.parts_ref, bf16[64,768]{1,0:T(8,128)(2,1)S(1)} %get-tuple-element.60.after_ref.refs_1_, bf16[1,3072,2048]{2,1,0:T(8,128)(2,1)} %refs_9_.2, ...), custom_call_target="tpu_custom_call" | custom-call | bytes 12582912 | tf_op jit(solution)/shard_map/prefetch/pallas_call | solution.py:119
  17.3 0.3 dispatch.7
  17.7 1.6 %collective-permute-start.13 = (bf16[64,768]{1,0:T(8,128)(2,1)S(1)}, bf16[64,768]{1,0:T(8,128)(2,1)S(1)}, u32[]{:S(2)}, u32[]{:S(2)}) collective-permute-start(bf16[64,768]{1,0:T(8,128)(2,1)S(1)} %get-tuple-element.76), channel_id=1, source_target_pairs={{0,2},{1,3},{2,0},{3,1},{4,6},{5,7},{6,4},{7,5},{8,10},{9,11},{10,... | collective-permute-start | bytes 294920 | tf_op jit(solution)/shard_map/ppermute | solution.py:249
  19.2 0.3 collective-permute-start.14
  19.5 6.8 %gate_up.4 = (f32[256,2048]{1,0:T(8,128)S(1)}, f32[256,2048]{1,0:T(8,128)S(1)}, bf16[768,2048]{1,0:T(8,128)(2,1)S(1)}, bf16[768,2048]{1,0:T(8,128)(2,1)S(1)}, bf...) custom-call(s32[5]{0:T(128)S(1)} %stack.21.refs_0_, bf16[64,768]{1,0:T(8,128)(2,1)S(1)} %get-tuple-element.60.after_ref.refs_1_, ...), custom_call_target="tpu_custom_call" | custom-call | flops 1610612736 | bytes 6291456 | tf_op jit(solution)/shard_map/gate_up/pallas_call | solution.py:177
  26.4 0.3 dispatch.6
  26.7 1.5 %collective-permute-start.10 = (bf16[64,768]{1,0:T(8,128)(2,1)S(1)}, bf16[64,768]{1,0:T(8,128)(2,1)S(1)}, u32[]{:S(2)}, u32[]{:S(2)}) collective-permute-start(bf16[64,768]{1,0:T(8,128)(2,1)S(1)} %get-tuple-element.71), channel_id=1, source_target_pairs={{0,3},{1,2},{2,1},{3,0},{4,7},{5,6},{6,5},{7,4},{8,11},{9,10},{10,... | collective-permute-start | bytes 294920 | tf_op jit(solution)/shard_map/ppermute | solution.py:249
  28.3 0.3 dispatch.4
  28.6 0.6 collective-permute-start.9
  29.3 1.5 %collective-permute-start.2 = (bf16[64,768]{1,0:T(8,128)(2,1)S(1)}, bf16[64,768]{1,0:T(8,128)(2,1)S(1)}, u32[]{:S(2)}, u32[]{:S(2)}) collective-permute-start(bf16[64,768]{1,0:T(8,128)(2,1)S(1)} %get-tuple-element.58), channel_id=1, source_target_pairs={{0,2},{1,3},{2,0},{3,1},{4,6},{5,7},{6,4},{7,5},{8,10},{9,11},{10,... | collective-permute-start | bytes 294920 | tf_op jit(solution)/shard_map/ppermute | solution.py:249
  30.8 7.1 %gate_up.5 = (f32[256,2048]{1,0:T(8,128)S(1)}, f32[256,2048]{1,0:T(8,128)S(1)}, bf16[2048,3072]{1,0:T(8,128)(2,1)S(1)}) custom-call(s32[2]{0:T(128)S(1)} %broadcast_1_refs_0_.2.refs_0_, bf16[64,768]{1,0:T(8,128)(2,1)S(1)} %get-tuple-element.74.refs_1_, ...), custom_call_target="tpu_custom_call", output_to_operand_aliasing={{0}: (7, {}), {1}: (8, {})} | custom-call | flops 1610612736 | bytes 6291456 | tf_op jit(solution)/shard_map/gate_up/pallas_call | solution.py:177
  37.9 0.4 collective-permute-start.3
  38.2 2.1 %gate_up.6 = (f32[256,2048]{1,0:T(8,128)S(1)}, f32[256,2048]{1,0:T(8,128)S(1)}) custom-call(s32[1]{0:T(128)} %constant.6.clone.1.refs_0_, bf16[64,768]{1,0:T(8,128)(2,1)S(1)} %get-tuple-element.68.refs_1_, bf16[64,768]{1,0:T(8,128)(2,1)S(1)} %collective-permute-done.8.refs_2_, ...), custom_call_target="tpu_custom_call", output_to_operand_aliasing={{0}: (7, {}), {1}: (8, {})} | custom-call | flops 1610612736 | bytes 6291456 | tf_op jit(solution)/shard_map/gate_up/pallas_call | solution.py:177
  40.4 2.3 %collective-permute-done.3.refs_4_ = bf16[64,768]{1,0:T(8,128)(2,1)S(1)} collective-permute-done((bf16[64,768]{1,0:T(8,128)(2,1)S(1)}, bf16[64,768]{1,0:T(8,128)(2,1)S(1)}, u32[]{:S(2)}, u32[]{:S(2)}) %collective-permute-start.3) | collective-permute-done | bytes 98336 | tf_op jit(solution)/shard_map/ppermute | solution.py:249
  42.7 2.1 %gate_up.7.h_ref = bf16[256,2048]{1,0:T(8,128)(2,1)S(1)} custom-call(s32[1]{0:T(128)} %constant.6.clone.1.refs_0_, bf16[64,768]{1,0:T(8,128)(2,1)S(1)} %get-tuple-element.56.refs_1_, bf16[64,768]{1,0:T(8,128)(2,1)S(1)} %collective-permute-done.1.refs_2_, bf16[64,768]{1,0:T(8,128)(2,1)S(1)} %collective-permute-done.2.refs_3_, ...), custom_call_target="tpu_custom_call" | custom-call | flops 1610612736 | bytes 6291456 | tf_op jit(solution)/shard_map/gate_up/pallas_call | solution.py:177
  44.8 1.0 %down.4 = (bf16[64,768]{1,0:T(8,128)(2,1)S(1)}, bf16[64,768]{1,0:T(8,128)(2,1)S(1)}, bf16[64,768]{1,0:T(8,128)(2,1)S(1)}, bf16[64,768]{1,0:T(8,128)(2,1)S(1)}) custom-call(s32[1]{0:T(128)} %bitcast.2.part_ref, bf16[256,2048]{1,0:T(8,128)(2,1)S(1)} %gate_up.7.h_ref, bf16[2048,3072]{1,0:T(8,128)(2,1)S(1)} %get-tuple-element.86.w_ref), custom_call_target="tpu_custom_call" | custom-call | flops 805306368 | bytes 3538944 | tf_op jit(solution)/shard_map/down/pallas_call | solution.py:208
  45.8 0.2 collective-permute-start.15
  46.1 0.6 collective-permute-start.16
  46.6 1.1 %collective-permute-start.17 = (bf16[64,768]{1,0:T(8,128)(2,1)S(1)}, bf16[64,768]{1,0:T(8,128)(2,1)S(1)}, u32[]{:S(2)}, u32[]{:S(2)}) collective-permute-start(bf16[64,768]{1,0:T(8,128)(2,1)S(1)} %get-tuple-element.90), channel_id=1, source_target_pairs={{0,3},{1,2},{2,1},{3,0},{4,7},{5,6},{6,5},{7,4},{8,11},{9,10},{10,... | collective-permute-start | bytes 294920 | tf_op jit(solution)/shard_map/ppermute | solution.py:249
  47.8 1.0 %down.5 = (bf16[64,768]{1,0:T(8,128)(2,1)S(1)}, bf16[64,768]{1,0:T(8,128)(2,1)S(1)}, bf16[64,768]{1,0:T(8,128)(2,1)S(1)}, bf16[64,768]{1,0:T(8,128)(2,1)S(1)}) custom-call(s32[1]{0:T(128)} %bitcast.3.part_ref, bf16[256,2048]{1,0:T(8,128)(2,1)S(1)} %gate_up.7.h_ref, bf16[2048,3072]{1,0:T(8,128)(2,1)S(1)} %get-tuple-element.86.w_ref), custom_call_target="tpu_custom_call" | custom-call | flops 805306368 | bytes 3538944 | tf_op jit(solution)/shard_map/down/pallas_call | solution.py:208
  48.8 0.5 collective-permute-start.19
  49.3 0.6 collective-permute-start.20
  49.9 0.9 %collective-permute-start.21 = (bf16[64,768]{1,0:T(8,128)(2,1)S(1)}, bf16[64,768]{1,0:T(8,128)(2,1)S(1)}, u32[]{:S(2)}, u32[]{:S(2)}) collective-permute-start(bf16[64,768]{1,0:T(8,128)(2,1)S(1)} %get-tuple-element.94), channel_id=1, source_target_pairs={{0,3},{1,2},{2,1},{3,0},{4,7},{5,6},{6,5},{7,4},{8,11},{9,10},{10,... | collective-permute-start | bytes 294920 | tf_op jit(solution)/shard_map/ppermute | solution.py:249
  50.7 1.0 %down.6 = (bf16[64,768]{1,0:T(8,128)(2,1)S(1)}, bf16[64,768]{1,0:T(8,128)(2,1)S(1)}, bf16[64,768]{1,0:T(8,128)(2,1)S(1)}, bf16[64,768]{1,0:T(8,128)(2,1)S(1)}) custom-call(s32[1]{0:T(128)} %bitcast.5.part_ref, bf16[256,2048]{1,0:T(8,128)(2,1)S(1)} %gate_up.7.h_ref, bf16[2048,3072]{1,0:T(8,128)(2,1)S(1)} %get-tuple-element.86.w_ref), custom_call_target="tpu_custom_call" | custom-call | flops 805306368 | bytes 3538944 | tf_op jit(solution)/shard_map/down/pallas_call | solution.py:208
  51.8 0.8 collective-permute-start.23
  52.7 0.7 collective-permute-start.24
  53.3 1.6 %collective-permute-start.25 = (bf16[64,768]{1,0:T(8,128)(2,1)S(1)}, bf16[64,768]{1,0:T(8,128)(2,1)S(1)}, u32[]{:S(2)}, u32[]{:S(2)}) collective-permute-start(bf16[64,768]{1,0:T(8,128)(2,1)S(1)} %get-tuple-element.98), channel_id=1, source_target_pairs={{0,3},{1,2},{2,1},{3,0},{4,7},{5,6},{6,5},{7,4},{8,11},{9,10},{10,... | collective-permute-start | bytes 294920 | tf_op jit(solution)/shard_map/ppermute | solution.py:249
  55.1 4.6 %copy-done.1 = bf16[2048,3072]{1,0:T(8,128)(2,1)S(1)} copy-done((bf16[2048,3072]{1,0:T(8,128)(2,1)S(1)}, bf16[2048,3072]{1,0:T(8,128)(2,1)}, u32[]{:S(2)}) %copy-start.1) | copy-done | bytes 12582936
  59.7 1.0 %down.7 = (bf16[64,768]{1,0:T(8,128)(2,1)S(1)}, bf16[64,768]{1,0:T(8,128)(2,1)S(1)}, bf16[64,768]{1,0:T(8,128)(2,1)S(1)}, bf16[64,768]{1,0:T(8,128)(2,1)S(1)}) custom-call(s32[1]{0:T(128)} %bitcast.4.part_ref, bf16[256,2048]{1,0:T(8,128)(2,1)S(1)} %gate_up.7.h_ref, bf16[2048,3072]{1,0:T(8,128)(2,1)S(1)} %copy-done.1), custom_call_target="tpu_custom_call" | custom-call | flops 805306368 | bytes 3538944 | tf_op jit(solution)/shard_map/down/pallas_call | solution.py:208
  60.7 0.3 combine.4
  61.1 1.6 %collective-permute-start.18 = (bf16[128,768]{1,0:T(8,128)(2,1)S(1)}, bf16[128,768]{1,0:T(8,128)(2,1)S(1)}, u32[]{:S(2)}, u32[]{:S(2)}) collective-permute-start(bf16[128,768]{1,0:T(8,128)(2,1)S(1)} %combine.4), channel_id=1, source_target_pairs={{0,12},{4,8},{8,4},{12,0},{1,13},{5,9},{9,5},{13,1},{2,14},{6,10},... | collective-permute-start | bytes 589832 | tf_op jit(solution)/shard_map/ppermute | solution.py:249
  62.7 0.3 combine.5
  63.2 0.3 combine.6
  63.5 2.8 %collective-permute-start.26 = (bf16[128,768]{1,0:T(8,128)(2,1)S(1)}, bf16[128,768]{1,0:T(8,128)(2,1)S(1)}, u32[]{:S(2)}, u32[]{:S(2)}) collective-permute-start(bf16[128,768]{1,0:T(8,128)(2,1)S(1)} %combine.6), channel_id=1, source_target_pairs={{0,4},{4,0},{8,12},{12,8},{1,5},{5,1},{9,13},{13,9},{2,6},{6,2},{1... | collective-permute-start | bytes 589832 | tf_op jit(solution)/shard_map/ppermute | solution.py:249
  66.3 0.5 collective-permute-start.28
  66.9 0.4 collective-permute-start.29
  67.3 4.7 %collective-permute-done.28.refs_2_ = bf16[64,768]{1,0:T(8,128)(2,1)S(1)} collective-permute-done((bf16[64,768]{1,0:T(8,128)(2,1)S(1)}, bf16[64,768]{1,0:T(8,128)(2,1)S(1)}, u32[]{:S(2)}, u32[]{:S(2)}) %collective-permute-start.28) | collective-permute-done | bytes 98336 | tf_op jit(solution)/shard_map/ppermute | solution.py:249
  72.0 0.3 combine.7
  72.3 8.4 %collective-permute-done.22 = bf16[128,768]{1,0:T(8,128)(2,1)S(1)} collective-permute-done((bf16[128,768]{1,0:T(8,128)(2,1)S(1)}, bf16[128,768]{1,0:T(8,128)(2,1)S(1)}, u32[]{:S(2)}, u32[]{:S(2)}) %collective-permute-start.22) | collective-permute-done | bytes 196640 | tf_op jit(solution)/shard_map/ppermute | solution.py:249
  80.7 0.8 add_convert_fusion
  (43 shorter events, 1.0 us)
Async XLA Ops:
  0.0 9.6 %collective-permute-start.11 = (bf16[128,768]{1,0:T(8,128)(2,1)}, bf16[128,768]{1,0:T(8,128)(2,1)S(1)}, u32[]{:S(2)}, u32[]{:S(2)}) collective-permute-start(bf16[128,768]{1,0:T(8,128)(2,1)} %block_ref.1), channel_id=1, source_target_pairs={{0,4},{4,0},{8,12},{12,8},{1,5},{5,1},{9,13},{13,9},{2,6},{6,2},{1... | collective-permute-start | bytes 589832 | tf_op jit(solution)/shard_map/ppermute | solution.py:249
  3.0 0.7 copy-start.2
  5.1 12.5 %collective-permute-start.4 = (bf16[64,768]{1,0:T(8,128)(2,1)S(1)}, bf16[64,768]{1,0:T(8,128)(2,1)S(1)}, u32[]{:S(2)}, u32[]{:S(2)}) collective-permute-start(bf16[64,768]{1,0:T(8,128)(2,1)S(1)} %get-tuple-element.61), channel_id=1, source_target_pairs={{0,1},{1,0},{2,3},{3,2},{4,5},{5,4},{6,7},{7,6},{8,9},{9,8},{10,11... | collective-permute-start | bytes 294920 | tf_op jit(solution)/shard_map/ppermute | solution.py:249
  5.1 12.5 %collective-permute-start.5 = (bf16[64,768]{1,0:T(8,128)(2,1)S(1)}, bf16[64,768]{1,0:T(8,128)(2,1)S(1)}, u32[]{:S(2)}, u32[]{:S(2)}) collective-permute-start(bf16[64,768]{1,0:T(8,128)(2,1)S(1)} %get-tuple-element.62), channel_id=1, source_target_pairs={{0,2},{1,3},{2,0},{3,1},{4,6},{5,7},{6,4},{7,5},{8,10},{9,11},{10,... | collective-permute-start | bytes 294920 | tf_op jit(solution)/shard_map/ppermute | solution.py:249
  6.7 12.5 %collective-permute-start.6 = (bf16[64,768]{1,0:T(8,128)(2,1)S(1)}, bf16[64,768]{1,0:T(8,128)(2,1)S(1)}, u32[]{:S(2)}, u32[]{:S(2)}) collective-permute-start(bf16[64,768]{1,0:T(8,128)(2,1)S(1)} %get-tuple-element.63), channel_id=1, source_target_pairs={{0,3},{1,2},{2,1},{3,0},{4,7},{5,6},{6,5},{7,4},{8,11},{9,10},{10,... | collective-permute-start | bytes 294920 | tf_op jit(solution)/shard_map/ppermute | solution.py:249
  7.0 19.4 %collective-permute-start.7 = (bf16[128,768]{1,0:T(8,128)(2,1)}, bf16[128,768]{1,0:T(8,128)(2,1)S(1)}, u32[]{:S(2)}, u32[]{:S(2)}) collective-permute-start(bf16[128,768]{1,0:T(8,128)(2,1)} %block_ref.1), channel_id=1, source_target_pairs={{0,8},{4,12},{8,0},{12,4},{1,9},{5,13},{9,1},{13,5},{2,10},{6,14},... | collective-permute-start | bytes 589832 | tf_op jit(solution)/shard_map/ppermute | solution.py:249
  9.6 18.6 %collective-permute-start = (bf16[128,768]{1,0:T(8,128)(2,1)}, bf16[128,768]{1,0:T(8,128)(2,1)S(1)}, u32[]{:S(2)}, u32[]{:S(2)}) collective-permute-start(bf16[128,768]{1,0:T(8,128)(2,1)} %block_ref.1), channel_id=1, source_target_pairs={{0,12},{4,8},{8,4},{12,0},{1,13},{5,9},{9,5},{13,1},{2,14},{6,10},... | collective-permute-start | bytes 589832 | tf_op jit(solution)/shard_map/ppermute | solution.py:249
  17.6 11.0 %collective-permute-start.12 = (bf16[64,768]{1,0:T(8,128)(2,1)S(1)}, bf16[64,768]{1,0:T(8,128)(2,1)S(1)}, u32[]{:S(2)}, u32[]{:S(2)}) collective-permute-start(bf16[64,768]{1,0:T(8,128)(2,1)S(1)} %get-tuple-element.75), channel_id=1, source_target_pairs={{0,1},{1,0},{2,3},{3,2},{4,5},{5,4},{6,7},{7,6},{8,9},{9,8},{10,11... | collective-permute-start | bytes 294920 | tf_op jit(solution)/shard_map/ppermute | solution.py:249
  17.7 11.5 %collective-permute-start.13 = (bf16[64,768]{1,0:T(8,128)(2,1)S(1)}, bf16[64,768]{1,0:T(8,128)(2,1)S(1)}, u32[]{:S(2)}, u32[]{:S(2)}) collective-permute-start(bf16[64,768]{1,0:T(8,128)(2,1)S(1)} %get-tuple-element.76), channel_id=1, source_target_pairs={{0,2},{1,3},{2,0},{3,1},{4,6},{5,7},{6,4},{7,5},{8,10},{9,11},{10,... | collective-permute-start | bytes 294920 | tf_op jit(solution)/shard_map/ppermute | solution.py:249
  19.2 10.0 %collective-permute-start.14 = (bf16[64,768]{1,0:T(8,128)(2,1)S(1)}, bf16[64,768]{1,0:T(8,128)(2,1)S(1)}, u32[]{:S(2)}, u32[]{:S(2)}) collective-permute-start(bf16[64,768]{1,0:T(8,128)(2,1)S(1)} %get-tuple-element.77), channel_id=1, source_target_pairs={{0,3},{1,2},{2,1},{3,0},{4,7},{5,6},{6,5},{7,4},{8,11},{9,10},{10,... | collective-permute-start | bytes 294920 | tf_op jit(solution)/shard_map/ppermute | solution.py:249
  26.7 11.2 %collective-permute-start.10 = (bf16[64,768]{1,0:T(8,128)(2,1)S(1)}, bf16[64,768]{1,0:T(8,128)(2,1)S(1)}, u32[]{:S(2)}, u32[]{:S(2)}) collective-permute-start(bf16[64,768]{1,0:T(8,128)(2,1)S(1)} %get-tuple-element.71), channel_id=1, source_target_pairs={{0,3},{1,2},{2,1},{3,0},{4,7},{5,6},{6,5},{7,4},{8,11},{9,10},{10,... | collective-permute-start | bytes 294920 | tf_op jit(solution)/shard_map/ppermute | solution.py:249
  28.2 10.1 %collective-permute-start.8 = (bf16[64,768]{1,0:T(8,128)(2,1)S(1)}, bf16[64,768]{1,0:T(8,128)(2,1)S(1)}, u32[]{:S(2)}, u32[]{:S(2)}) collective-permute-start(bf16[64,768]{1,0:T(8,128)(2,1)S(1)} %get-tuple-element.69), channel_id=1, source_target_pairs={{0,1},{1,0},{2,3},{3,2},{4,5},{5,4},{6,7},{7,6},{8,9},{9,8},{10,11... | collective-permute-start | bytes 294920 | tf_op jit(solution)/shard_map/ppermute | solution.py:249
  28.6 9.6 %collective-permute-start.9 = (bf16[64,768]{1,0:T(8,128)(2,1)S(1)}, bf16[64,768]{1,0:T(8,128)(2,1)S(1)}, u32[]{:S(2)}, u32[]{:S(2)}) collective-permute-start(bf16[64,768]{1,0:T(8,128)(2,1)S(1)} %get-tuple-element.70), channel_id=1, source_target_pairs={{0,2},{1,3},{2,0},{3,1},{4,6},{5,7},{6,4},{7,5},{8,10},{9,11},{10,... | collective-permute-start | bytes 294920 | tf_op jit(solution)/shard_map/ppermute | solution.py:249
  29.2 11.2 %collective-permute-start.1 = (bf16[64,768]{1,0:T(8,128)(2,1)S(1)}, bf16[64,768]{1,0:T(8,128)(2,1)S(1)}, u32[]{:S(2)}, u32[]{:S(2)}) collective-permute-start(bf16[64,768]{1,0:T(8,128)(2,1)S(1)} %get-tuple-element.57), channel_id=1, source_target_pairs={{0,1},{1,0},{2,3},{3,2},{4,5},{5,4},{6,7},{7,6},{8,9},{9,8},{10,11... | collective-permute-start | bytes 294920 | tf_op jit(solution)/shard_map/ppermute | solution.py:249
  29.3 11.1 %collective-permute-start.2 = (bf16[64,768]{1,0:T(8,128)(2,1)S(1)}, bf16[64,768]{1,0:T(8,128)(2,1)S(1)}, u32[]{:S(2)}, u32[]{:S(2)}) collective-permute-start(bf16[64,768]{1,0:T(8,128)(2,1)S(1)} %get-tuple-element.58), channel_id=1, source_target_pairs={{0,2},{1,3},{2,0},{3,1},{4,6},{5,7},{6,4},{7,5},{8,10},{9,11},{10,... | collective-permute-start | bytes 294920 | tf_op jit(solution)/shard_map/ppermute | solution.py:249
  37.9 12.9 %copy-start = (bf16[2048,3072]{1,0:T(8,128)(2,1)}, bf16[2048,3072]{1,0:T(8,128)(2,1)S(1)}, u32[]{:S(2)}) copy-start(bf16[2048,3072]{1,0:T(8,128)(2,1)S(1)} %get-tuple-element.86.w_ref) | copy-start | bytes 37748740
  37.9 4.8 %collective-permute-start.3 = (bf16[64,768]{1,0:T(8,128)(2,1)S(1)}, bf16[64,768]{1,0:T(8,128)(2,1)S(1)}, u32[]{:S(2)}, u32[]{:S(2)}) collective-permute-start(bf16[64,768]{1,0:T(8,128)(2,1)S(1)} %get-tuple-element.59), channel_id=1, source_target_pairs={{0,3},{1,2},{2,1},{3,0},{4,7},{5,6},{6,5},{7,4},{8,11},{9,10},{10,... | collective-permute-start | bytes 294920 | tf_op jit(solution)/shard_map/ppermute | solution.py:249
  45.8 4.0 %collective-permute-start.15 = (bf16[64,768]{1,0:T(8,128)(2,1)S(1)}, bf16[64,768]{1,0:T(8,128)(2,1)S(1)}, u32[]{:S(2)}, u32[]{:S(2)}) collective-permute-start(bf16[64,768]{1,0:T(8,128)(2,1)S(1)} %get-tuple-element.88), channel_id=1, source_target_pairs={{0,1},{1,0},{2,3},{3,2},{4,5},{5,4},{6,7},{7,6},{8,9},{9,8},{10,11... | collective-permute-start | bytes 294920 | tf_op jit(solution)/shard_map/ppermute | solution.py:249
  46.1 5.7 %collective-permute-start.16 = (bf16[64,768]{1,0:T(8,128)(2,1)S(1)}, bf16[64,768]{1,0:T(8,128)(2,1)S(1)}, u32[]{:S(2)}, u32[]{:S(2)}) collective-permute-start(bf16[64,768]{1,0:T(8,128)(2,1)S(1)} %get-tuple-element.89), channel_id=1, source_target_pairs={{0,2},{1,3},{2,0},{3,1},{4,6},{5,7},{6,4},{7,5},{8,10},{9,11},{10,... | collective-permute-start | bytes 294920 | tf_op jit(solution)/shard_map/ppermute | solution.py:249
  46.6 6.0 %collective-permute-start.17 = (bf16[64,768]{1,0:T(8,128)(2,1)S(1)}, bf16[64,768]{1,0:T(8,128)(2,1)S(1)}, u32[]{:S(2)}, u32[]{:S(2)}) collective-permute-start(bf16[64,768]{1,0:T(8,128)(2,1)S(1)} %get-tuple-element.90), channel_id=1, source_target_pairs={{0,3},{1,2},{2,1},{3,0},{4,7},{5,6},{6,5},{7,4},{8,11},{9,10},{10,... | collective-permute-start | bytes 294920 | tf_op jit(solution)/shard_map/ppermute | solution.py:249
  48.8 4.6 %collective-permute-start.19 = (bf16[64,768]{1,0:T(8,128)(2,1)S(1)}, bf16[64,768]{1,0:T(8,128)(2,1)S(1)}, u32[]{:S(2)}, u32[]{:S(2)}) collective-permute-start(bf16[64,768]{1,0:T(8,128)(2,1)S(1)} %get-tuple-element.92), channel_id=1, source_target_pairs={{0,1},{1,0},{2,3},{3,2},{4,5},{5,4},{6,7},{7,6},{8,9},{9,8},{10,11... | collective-permute-start | bytes 294920 | tf_op jit(solution)/shard_map/ppermute | solution.py:249
  49.3 11.7 %collective-permute-start.20 = (bf16[64,768]{1,0:T(8,128)(2,1)S(1)}, bf16[64,768]{1,0:T(8,128)(2,1)S(1)}, u32[]{:S(2)}, u32[]{:S(2)}) collective-permute-start(bf16[64,768]{1,0:T(8,128)(2,1)S(1)} %get-tuple-element.93), channel_id=1, source_target_pairs={{0,2},{1,3},{2,0},{3,1},{4,6},{5,7},{6,4},{7,5},{8,10},{9,11},{10,... | collective-permute-start | bytes 294920 | tf_op jit(solution)/shard_map/ppermute | solution.py:249
  49.9 5.1 %copy-start.3 = (f32[128,2]{0,1:T(2,128)S(1)}, f32[128,2]{0,1:T(2,128)}, u32[]{:S(2)}) copy-start(f32[128,2]{0,1:T(2,128)} %param.8) | copy-start | bytes 3076
  49.9 11.2 %collective-permute-start.21 = (bf16[64,768]{1,0:T(8,128)(2,1)S(1)}, bf16[64,768]{1,0:T(8,128)(2,1)S(1)}, u32[]{:S(2)}, u32[]{:S(2)}) collective-permute-start(bf16[64,768]{1,0:T(8,128)(2,1)S(1)} %get-tuple-element.94), channel_id=1, source_target_pairs={{0,3},{1,2},{2,1},{3,0},{4,7},{5,6},{6,5},{7,4},{8,11},{9,10},{10,... | collective-permute-start | bytes 294920 | tf_op jit(solution)/shard_map/ppermute | solution.py:249
  51.8 11.3 %collective-permute-start.23 = (bf16[64,768]{1,0:T(8,128)(2,1)S(1)}, bf16[64,768]{1,0:T(8,128)(2,1)S(1)}, u32[]{:S(2)}, u32[]{:S(2)}) collective-permute-start(bf16[64,768]{1,0:T(8,128)(2,1)S(1)} %get-tuple-element.96), channel_id=1, source_target_pairs={{0,1},{1,0},{2,3},{3,2},{4,5},{5,4},{6,7},{7,6},{8,9},{9,8},{10,11... | collective-permute-start | bytes 294920 | tf_op jit(solution)/shard_map/ppermute | solution.py:249
  52.7 10.5 %collective-permute-start.24 = (bf16[64,768]{1,0:T(8,128)(2,1)S(1)}, bf16[64,768]{1,0:T(8,128)(2,1)S(1)}, u32[]{:S(2)}, u32[]{:S(2)}) collective-permute-start(bf16[64,768]{1,0:T(8,128)(2,1)S(1)} %get-tuple-element.97), channel_id=1, source_target_pairs={{0,2},{1,3},{2,0},{3,1},{4,6},{5,7},{6,4},{7,5},{8,10},{9,11},{10,... | collective-permute-start | bytes 294920 | tf_op jit(solution)/shard_map/ppermute | solution.py:249
  53.3 9.9 %collective-permute-start.25 = (bf16[64,768]{1,0:T(8,128)(2,1)S(1)}, bf16[64,768]{1,0:T(8,128)(2,1)S(1)}, u32[]{:S(2)}, u32[]{:S(2)}) collective-permute-start(bf16[64,768]{1,0:T(8,128)(2,1)S(1)} %get-tuple-element.98), channel_id=1, source_target_pairs={{0,3},{1,2},{2,1},{3,0},{4,7},{5,6},{6,5},{7,4},{8,11},{9,10},{10,... | collective-permute-start | bytes 294920 | tf_op jit(solution)/shard_map/ppermute | solution.py:249
  55.1 4.6 %copy-start.1 = (bf16[2048,3072]{1,0:T(8,128)(2,1)S(1)}, bf16[2048,3072]{1,0:T(8,128)(2,1)}, u32[]{:S(2)}) copy-start(bf16[2048,3072]{1,0:T(8,128)(2,1)} %copy-done) | copy-start | bytes 37748740
  61.0 5.9 %collective-permute-start.27 = (bf16[64,768]{1,0:T(8,128)(2,1)S(1)}, bf16[64,768]{1,0:T(8,128)(2,1)S(1)}, u32[]{:S(2)}, u32[]{:S(2)}) collective-permute-start(bf16[64,768]{1,0:T(8,128)(2,1)S(1)} %get-tuple-element.100), channel_id=1, source_target_pairs={{0,1},{1,0},{2,3},{3,2},{4,5},{5,4},{6,7},{7,6},{8,9},{9,8},{10,11... | collective-permute-start | bytes 294920 | tf_op jit(solution)/shard_map/ppermute | solution.py:249
  61.1 11.2 %collective-permute-start.18 = (bf16[128,768]{1,0:T(8,128)(2,1)S(1)}, bf16[128,768]{1,0:T(8,128)(2,1)S(1)}, u32[]{:S(2)}, u32[]{:S(2)}) collective-permute-start(bf16[128,768]{1,0:T(8,128)(2,1)S(1)} %combine.4), channel_id=1, source_target_pairs={{0,12},{4,8},{8,4},{12,0},{1,13},{5,9},{9,5},{13,1},{2,14},{6,10},... | collective-permute-start | bytes 589832 | tf_op jit(solution)/shard_map/ppermute | solution.py:249
  63.1 17.7 %collective-permute-start.22 = (bf16[128,768]{1,0:T(8,128)(2,1)S(1)}, bf16[128,768]{1,0:T(8,128)(2,1)S(1)}, u32[]{:S(2)}, u32[]{:S(2)}) collective-permute-start(bf16[128,768]{1,0:T(8,128)(2,1)S(1)} %combine.5), channel_id=1, source_target_pairs={{0,8},{4,12},{8,0},{12,4},{1,9},{5,13},{9,1},{13,5},{2,10},{6,14},... | collective-permute-start | bytes 589832 | tf_op jit(solution)/shard_map/ppermute | solution.py:249
  63.5 17.2 %collective-permute-start.26 = (bf16[128,768]{1,0:T(8,128)(2,1)S(1)}, bf16[128,768]{1,0:T(8,128)(2,1)S(1)}, u32[]{:S(2)}, u32[]{:S(2)}) collective-permute-start(bf16[128,768]{1,0:T(8,128)(2,1)S(1)} %combine.6), channel_id=1, source_target_pairs={{0,4},{4,0},{8,12},{12,8},{1,5},{5,1},{9,13},{13,9},{2,6},{6,2},{1... | collective-permute-start | bytes 589832 | tf_op jit(solution)/shard_map/ppermute | solution.py:249
  66.3 5.6 %collective-permute-start.28 = (bf16[64,768]{1,0:T(8,128)(2,1)S(1)}, bf16[64,768]{1,0:T(8,128)(2,1)S(1)}, u32[]{:S(2)}, u32[]{:S(2)}) collective-permute-start(bf16[64,768]{1,0:T(8,128)(2,1)S(1)} %get-tuple-element.101), channel_id=1, source_target_pairs={{0,2},{1,3},{2,0},{3,1},{4,6},{5,7},{6,4},{7,5},{8,10},{9,11},{10,... | collective-permute-start | bytes 294920 | tf_op jit(solution)/shard_map/ppermute | solution.py:249
  66.9 5.1 %collective-permute-start.29 = (bf16[64,768]{1,0:T(8,128)(2,1)S(1)}, bf16[64,768]{1,0:T(8,128)(2,1)S(1)}, u32[]{:S(2)}, u32[]{:S(2)}) collective-permute-start(bf16[64,768]{1,0:T(8,128)(2,1)S(1)} %get-tuple-element.102), channel_id=1, source_target_pairs={{0,3},{1,2},{2,1},{3,0},{4,7},{5,6},{6,5},{7,4},{8,11},{9,10},{10,... | collective-permute-start | bytes 294920 | tf_op jit(solution)/shard_map/ppermute | solution.py:249

commit v4 on v3

--- a/solution.py
+++ b/solution.py
@@ -18,6 +18,10 @@
 
 def cost(flops, moved):
     return pl.CostEstimate(flops=flops, bytes_accessed=moved, transcendentals=0)
+
+
+def pinned(arrays):
+    return [pltpu.with_memory_space_constraint(array, pltpu.VMEM) for array in arrays]
 
 
 def routing_kernel(me_ref, ids_ref, placed_ref, pick_ref, *, experts, capacity):
@@ -64,27 +68,33 @@
     )(me.reshape(1), expert_ids.T)
 
 
-def dispatch_kernel(placed_ref, block_ref, *out_refs):
-    capacity = out_refs[0].shape[0]
-    for d, out in enumerate(out_refs):
-        out[...] = jnp.dot(
-            placed_ref[d * capacity : (d + 1) * capacity, :],
-            block_ref[...],
-            preferred_element_type=F32,
-        ).astype(BF16)
-
-
-def dispatch(placed, block, experts, capacity):
-    rows, width = block.shape
-    return pl.pallas_call(
-        dispatch_kernel,
-        out_shape=[jax.ShapeDtypeStruct((capacity, width), BF16)] * experts,
-        in_specs=[pl.BlockSpec(memory_space=pltpu.VMEM)] * 2,
+def dispatch_kernel(placed_ref, *refs, count, waits):
+    refs = refs[:count] + refs[count + waits :]
+    capacity, wide = refs[count].shape
+    width = wide // count
+    for i in range(count):
+        block = refs[i][...]
+        for d, out in enumerate(refs[count:]):
+            out[:, i * width : (i + 1) * width] = jnp.dot(
+                placed_ref[d * capacity : (d + 1) * capacity, :],
+                block,
+                preferred_element_type=F32,
+            ).astype(BF16)
+
+
+def dispatch(placed, blocks, experts, capacity, after):
+    rows, width = blocks[0].shape
+    wide = width * len(blocks)
+    return pl.pallas_call(
+        functools.partial(dispatch_kernel, count=len(blocks), waits=len(after)),
+        out_shape=[jax.ShapeDtypeStruct((capacity, wide), BF16)] * experts,
+        in_specs=[pl.BlockSpec(memory_space=pltpu.VMEM)] * (1 + len(blocks))
+        + [pl.BlockSpec(memory_space=pltpu.VMEM)] * len(after),
         out_specs=[pl.BlockSpec(memory_space=pltpu.VMEM)] * experts,
-        cost_estimate=cost(2 * experts * capacity * rows * width, 4 * rows * width),
+        cost_estimate=cost(2 * experts * capacity * rows * wide, 6 * rows * wide),
         compiler_params=params(),
         name="dispatch",
-    )(placed, block)
+    )(placed, *blocks, *pinned(after))
 
 
 def fetch_copies(parts_ref, sources, targets, sems):
@@ -129,11 +139,11 @@
     )(parts, after, *sources)
 
 
-def gate_up_kernel(*refs, experts, first, last, fetched):
+def gate_up_kernel(*refs, experts, slices, first, last, fetched):
     parts_ref = refs[0]
     x_refs = refs[1 : 1 + experts]
-    gate_w, up_w = refs[1 + experts : 3 + experts]
-    rest = list(refs[3 + experts :])
+    weights = refs[1 + experts : 1 + experts + 2 * slices]
+    rest = list(refs[1 + experts + 2 * slices :])
     if not first:
         old_gate, old_up = rest[:2]
         rest = rest[2:]
@@ -144,15 +154,22 @@
     for copy in copies:
         copy.start()
     x = jnp.concatenate([r[...] for r in x_refs], axis=0)
-    hidden = gate_w.shape[1]
+    width, hidden = weights[0].shape
     tile = min(512, hidden)
     for n in range(hidden // tile):
         columns = slice(n * tile, (n + 1) * tile)
-        gate = jnp.dot(x, gate_w[:, columns], preferred_element_type=F32)
-        up = jnp.dot(x, up_w[:, columns], preferred_element_type=F32)
-        if not first:
-            gate = gate + old_gate[:, columns]
-            up = up + old_up[:, columns]
+        sums = []
+        for kind in range(2):
+            total = None if first else (old_gate, old_up)[kind][:, columns]
+            for i in range(slices):
+                term = jnp.dot(
+                    x[:, i * width : (i + 1) * width],
+                    weights[2 * i + kind][:, columns],
+                    preferred_element_type=F32,
+                )
+                total = term if total is None else total + term
+            sums.append(total)
+        gate, up = sums
         if last:
             rest[0][:, columns] = (gate / (1.0 + jnp.exp(-gate)) * up).astype(BF16)
         else:
@@ -162,81 +179,98 @@
         copy.wait()
 
 
-def gate_up(x_blocks, gate_w, up_w, sums, last, fetches):
+def gate_up(x_blocks, weights, sums, last, fetches):
     experts = len(x_blocks)
-    capacity, width = x_blocks[0].shape
-    rows = experts * capacity
-    hidden = gate_w.shape[1]
+    rows = experts * x_blocks[0].shape[0]
+    hidden = weights[0].shape[1]
+    slices = len(weights) // 2
     first = sums is None
     parts, sources, shapes = fetch_specs(fetches)
-    operands = 2 + experts + (0 if first else 2)
+    old = [] if first else pinned(sums)
+    before = 1 + experts + len(weights)
     if last:
         out_shape = [pltpu.VMEM((rows, hidden), BF16)]
     else:
         out_shape = [pltpu.VMEM((rows, hidden), F32)] * 2
     results = pl.pallas_call(
         functools.partial(
-            gate_up_kernel, experts=experts, first=first, last=last, fetched=len(fetches)
+            gate_up_kernel,
+            experts=experts,
+            slices=slices,
+            first=first,
+            last=last,
+            fetched=len(fetches),
         ),
         out_shape=out_shape + shapes,
         in_specs=[pl.BlockSpec(memory_space=pltpu.SMEM)]
-        + [pl.BlockSpec(memory_space=pltpu.VMEM)] * operands
+        + [pl.BlockSpec(memory_space=pltpu.VMEM)] * (before - 1 + len(old))
         + [pl.BlockSpec(memory_space=pl.ANY)] * len(sources),
         out_specs=[pl.BlockSpec(memory_space=pltpu.VMEM)] * len(out_shape + shapes),
         scratch_shapes=[pltpu.SemaphoreType.DMA((len(fetches),))] if fetches else [],
-        input_output_aliases={} if first or last else {3 + experts: 0, 4 + experts: 1},
-        cost_estimate=cost(4 * rows * width * hidden, 4 * width * hidden),
+        input_output_aliases={} if first or last else {before: 0, before + 1: 1},
+        cost_estimate=cost(
+            2 * rows * hidden * sum(w.shape[0] for w in weights),
+            sum(2 * w.size for w in weights),
+        ),
         compiler_params=params(),
         name="gate_up",
-    )(parts, *x_blocks, gate_w, up_w, *(() if first else sums), *sources)
+    )(parts, *x_blocks, *pinned(weights), *old, *sources)
     return results[: len(out_shape)], results[len(out_shape) :]
 
 
-def down_kernel(part_ref, h_ref, w_ref, *out_refs):
-    capacity, width = out_refs[0].shape
+def down_kernel(parts_ref, h_ref, w_ref, *refs, slices, waits):
+    out_refs = refs[waits:]
+    capacity, wide = out_refs[0].shape
+    width = wide // slices
     tile = min(256, width)
-    for n in range(width // tile):
-        start = pl.multiple_of(part_ref[0] * width + n * tile, tile)
-        y = jnp.dot(h_ref[...], w_ref[:, pl.ds(start, tile)], preferred_element_type=F32)
-        for d, out in enumerate(out_refs):
-            out[:, n * tile : (n + 1) * tile] = y[d * capacity : (d + 1) * capacity].astype(BF16)
-
-
-def down(part, hidden, down_w, width, experts):
+    for i in range(slices):
+        for n in range(width // tile):
+            start = pl.multiple_of(parts_ref[i] * width + n * tile, tile)
+            y = jnp.dot(h_ref[...], w_ref[:, pl.ds(start, tile)], preferred_element_type=F32)
+            columns = pl.ds(i * width + n * tile, tile)
+            for d, out in enumerate(out_refs):
+                out[:, columns] = y[d * capacity : (d + 1) * capacity].astype(BF16)
+
+
+def down(parts, hidden, down_w, width, experts, after):
     rows, depth = hidden.shape
     capacity = rows // experts
-    return pl.pallas_call(
-        down_kernel,
-        out_shape=[jax.ShapeDtypeStruct((capacity, width), BF16)] * experts,
+    wide = width * len(parts)
+    return pl.pallas_call(
+        functools.partial(down_kernel, slices=len(parts), waits=len(after)),
+        out_shape=[jax.ShapeDtypeStruct((capacity, wide), BF16)] * experts,
         in_specs=[pl.BlockSpec(memory_space=pltpu.SMEM)]
-        + [pl.BlockSpec(memory_space=pltpu.VMEM)] * 2,
+        + [pl.BlockSpec(memory_space=pltpu.VMEM)] * 2
+        + [pl.BlockSpec(memory_space=pl.ANY)] * len(after),
         out_specs=[pl.BlockSpec(memory_space=pltpu.VMEM)] * experts,
-        cost_estimate=cost(2 * rows * depth * width, 2 * depth * width + 2 * rows * width),
+        cost_estimate=cost(2 * rows * depth * wide, 2 * depth * wide + 2 * rows * wide),
         compiler_params=params(),
         name="down",
-    )(part.reshape(1), hidden, down_w)
-
-
-def combine_kernel(pick_ref, logits_ref, *refs):
-    out = refs[-1]
-    rows = out.shape[0]
-    y = jnp.concatenate([r[...] for r in refs[:-1]], axis=0)
+    )(jnp.stack(parts), *pinned([hidden, down_w]), *after)
+
+
+def combine_kernel(pick_ref, logits_ref, *refs, experts):
+    y_refs, out_refs = refs[:experts], refs[experts:]
+    rows, width = out_refs[0].shape
+    y = jnp.concatenate([r[...] for r in y_refs], axis=0)
     picked = lax.dot_general(
         pick_ref[...], y, (((0,), (0,)), ((), ())), preferred_element_type=F32
     )
     share = 1.0 / (1.0 + jnp.exp(logits_ref[:, 1:2] - logits_ref[:, 0:1]))
-    out[...] = (picked[:rows] * share + picked[rows:] * (1.0 - share)).astype(BF16)
-
-
-def combine(pick, logits, blocks):
+    mixed = (picked[:rows] * share + picked[rows:] * (1.0 - share)).astype(BF16)
+    for i, out in enumerate(out_refs):
+        out[...] = mixed[:, i * width : (i + 1) * width]
+
+
+def combine(pick, logits, blocks, slices):
     rows = logits.shape[0]
-    width = blocks[0].shape[1]
-    return pl.pallas_call(
-        combine_kernel,
-        out_shape=jax.ShapeDtypeStruct((rows, width), BF16),
+    wide = blocks[0].shape[1]
+    return pl.pallas_call(
+        functools.partial(combine_kernel, experts=len(blocks)),
+        out_shape=[jax.ShapeDtypeStruct((rows, wide // slices), BF16)] * slices,
         in_specs=[pl.BlockSpec(memory_space=pltpu.VMEM)] * (2 + len(blocks)),
-        out_specs=pl.BlockSpec(memory_space=pltpu.VMEM),
-        cost_estimate=cost(4 * rows * pick.shape[0] * width, 6 * rows * width),
+        out_specs=[pl.BlockSpec(memory_space=pltpu.VMEM)] * slices,
+        cost_estimate=cost(4 * rows * pick.shape[0] * wide, 6 * rows * wide),
         compiler_params=params(),
         name="combine",
     )(pick, logits, *blocks)
@@ -269,40 +303,35 @@
         blocks = [lax.all_gather(tokens, "tensor", axis=1, tiled=True)]
     placed, pick = place(me, expert_ids, experts, capacity)
 
-    arrived = []
-    for d in distances:
-        outgoing = dispatch(placed, blocks[d], experts, capacity)
+    fetches = [(w, part_of(d), width) for d in distances for w in (gate_weight, up_weight)]
+    fetches.append((down_weight, 0, down_weight.shape[1]))
+    early = min(6, len(fetches) - 1)
+    groups = [distances[i : i + 2] for i in range(0, len(distances), 2)]
+    arrived, weights = [], []
+    for group in groups:
+        block = [blocks[d] for d in group]
+        outgoing = dispatch(placed, block, experts, capacity, weights[:1])
         arrived.append([swap(block, "expert", e) for e, block in enumerate(outgoing)])
-        if d == 0:
-            started = outgoing[0]
-
-    def slices(chosen):
-        return [(w, part_of(d), width) for d in chosen for w in (gate_weight, up_weight)]
-
-    weights = list(prefetch(slices(distances[:2]), started))
+        if not weights:
+            weights = list(prefetch(fetches[:early], outgoing[0]))
     sums = None
-    for d in distances:
-        fetches = slices(distances[2:]) if d == 0 else []
-        with_down = d == min(1, distances[-1])
-        if with_down:
-            fetches = fetches + [(down_weight, 0, down_weight.shape[1])]
-        sums, fetched = gate_up(
-            arrived[d], *weights[2 * d : 2 * d + 2], sums, d == distances[-1], fetches
-        )
-        if with_down:
-            down_w = fetched[-1]
-            fetched = fetched[:-1]
+    for group, x_blocks in zip(groups, arrived):
+        chosen = weights[2 * group[0] : 2 * group[-1] + 2]
+        later = fetches[early:] if group is groups[0] else []
+        sums, fetched = gate_up(x_blocks, chosen, sums, group is groups[-1], later)
         weights.extend(fetched)
-    hidden = sums[0]
-
+    hidden, down_w = sums[0], weights[-1]
+
+    groups = [[d] for d in reversed(distances)]
     total = []
-    for d in reversed(distances):
-        terms = down(part_of(d), hidden, down_w, width, experts)
+    for group in groups:
+        after = total[:1] if group is groups[-1] else []
+        terms = down([part_of(d) for d in group], hidden, down_w, width, experts, after)
         returned = [swap(block, "expert", e) for e, block in enumerate(terms)]
-        mixed = combine(pick, route_logits, returned)
+        mixtures = combine(pick, route_logits, returned, len(group))
         if not direct:
-            return lax.psum_scatter(mixed, "tensor", scatter_dimension=1, tiled=True)
-        total.append(swap(mixed, "tensor", d))
+            return lax.psum_scatter(mixtures[0], "tensor", scatter_dimension=1, tiled=True)
+        total.extend(swap(mixed, "tensor", d) for d, mixed in zip(group, mixtures))
     out = total[0].astype(F32)
     for term in total[1:]:
         out = out + term.astype(F32)

time: 81.7 us -> 75.3 us (0.922)
  starting transfers between devices: 28.5 us -> 22.1 us
  Pallas kernels: 30.8 us -> 27.4 us
  waiting for transfers between devices: 15.5 us -> 18.2 us
  local copies, waits for them, and re-layouts: 5.54 us -> 6.39 us
    ppermute x30 -> x24, starting transfers between devices: 28.5 us -> 22.1 us  [swap(): return lax.ppermute(value, axis, [(i, i ^ distance) for i in range(count)])]
    pallas_call x16 -> x12, Pallas kernels: 25.4 us -> 20.2 us  [the longest x2 14.1 us: gate_up(): pl.pallas_call(functools.partial(gate_up_kernel, experts=experts, slices=...]
    ppermute x30 -> x24, waiting for transfers between devices: 15.5 us -> 18.2 us  [swap(): return lax.ppermute(value, axis, [(i, i ^ distance) for i in range(count)])]
    pallas_call x1, Pallas kernels: 5.23 us -> 7.04 us  [prefetch(): pl.pallas_call(prefetch_kernel, out_shape=shapes, in_specs=[pl.BlockSpec(...]
    unnamed x9 -> x13, local copies, waits for them, and re-layouts: 5.37 us -> 6.3 us
  transfers between devices with their start and end apart: 30 -> 24, of which waited for: 4 -> 8; matrix products, arithmetic and copies ran while one was open for 0% -> 0% of each run, Pallas kernels for 34% -> 30%
where the time goes in v4:
time: 75.3 us; the launch traced here: 75.1 us
  Pallas kernels  27.4 us (36%)
  starting transfers between devices  22.1 us (29%)
  waiting for transfers between devices  18.2 us (24%)
  local copies, waits for them, and re-layouts  6.39 us (8%)
  other arithmetic  0.86 us (1%)
    ppermute x24, starting transfers between devices, swap(): return lax.ppermute(value, axis, [(i, i ^ distance) for i in range(count)])  22.1 us
    ppermute x24, waiting for transfers between devices, swap(): return lax.ppermute(value, axis, [(i, i ^ distance) for i in range(count)])  18.2 us
    pallas_call x2, Pallas kernels, gate_up(): pl.pallas_call(functools.partial(gate_up_kernel, experts=experts, slices=...  14.1 us
    pallas_call x1, Pallas kernels, prefetch(): pl.pallas_call(prefetch_kernel, out_shape=shapes, in_specs=[pl.BlockSpec(...  7.04 us
    unnamed x13, local copies, waits for them, and re-layouts  6.3 us
    pallas_call x4, Pallas kernels, down(): pl.pallas_call(functools.partial(down_kernel, slices=len(parts), waits=le...  4.09 us
  transfers between devices with their start and end apart: 24, of which 8 were waited for; matrix products, arithmetic and copies ran while one was open for 0% of the time, Pallas kernels for 30%

profile of v4, /device:TPU:0, one launch (start us, length us, event | category | flops | bytes accessed | tf_op | source)
XLA Modules:
  0.0 75.1 jit_solution(10360620888899196311)
XLA Ops:
  0.0 3.0 %collective-permute-start.2 = (bf16[128,768]{1,0:T(8,128)(2,1)}, bf16[128,768]{1,0:T(8,128)(2,1)S(1)}, u32[]{:S(2)}, u32[]{:S(2)}) collective-permute-start(bf16[128,768]{1,0:T(8,128)(2,1)} %refs_0_.2), channel_id=1, source_target_pairs={{0,4},{4,0},{8,12},{12,8},{1,5},{5,1},{9,13},{13,9},{2,6},{6,2},{1... | collective-permute-start | bytes 589832 | tf_op jit(solution)/shard_map/ppermute | solution.py:283
  3.0 2.6 %collective-permute-start = (bf16[128,768]{1,0:T(8,128)(2,1)}, bf16[128,768]{1,0:T(8,128)(2,1)S(1)}, u32[]{:S(2)}, u32[]{:S(2)}) collective-permute-start(bf16[128,768]{1,0:T(8,128)(2,1)} %refs_0_.2), channel_id=1, source_target_pairs={{0,8},{4,12},{8,0},{12,4},{1,9},{5,13},{9,1},{13,5},{2,10},{6,14},... | collective-permute-start | bytes 589832 | tf_op jit(solution)/shard_map/ppermute | solution.py:283
  5.6 0.7 copy-done.4
  6.3 0.2 routing.1
  6.5 5.1 %collective-permute-done.2.refs_1_ = bf16[128,768]{1,0:T(8,128)(2,1)S(1)} collective-permute-done((bf16[128,768]{1,0:T(8,128)(2,1)}, bf16[128,768]{1,0:T(8,128)(2,1)S(1)}, u32[]{:S(2)}, u32[]{:S(2)}) %collective-permute-start.2) | collective-permute-done | bytes 196640 | tf_op jit(solution)/shard_map/ppermute | solution.py:283
  11.6 0.9 %copy-done.3 = bf16[128,768]{1,0:T(8,128)(2,1)S(1)} copy-done((bf16[128,768]{1,0:T(8,128)(2,1)S(1)}, bf16[128,768]{1,0:T(8,128)(2,1)}, u32[]{:S(2)}) %copy-start.3) | copy-done | bytes 196632
  12.5 0.4 dispatch.2
  12.9 1.7 %collective-permute-start.7 = (bf16[64,1536]{1,0:T(8,128)(2,1)S(1)}, bf16[64,1536]{1,0:T(8,128)(2,1)S(1)}, u32[]{:S(2)}, u32[]{:S(2)}) collective-permute-start(bf16[64,1536]{1,0:T(8,128)(2,1)S(1)} %get-tuple-element.53), channel_id=1, source_target_pairs={{0,2},{1,3},{2,0},{3,1},{4,6},{5,7},{6,4},{7,5},{8,10},{9,11},{10,... | collective-permute-start | bytes 589832 | tf_op jit(solution)/shard_map/ppermute | solution.py:283
  14.7 0.1 collective-permute-start.8
  14.8 0.1 stack.30.parts_ref
  14.9 0.1 pad_add_fusion.refs_0_
  15.0 7.0 %prefetch.1 = (bf16[768,2048]{1,0:T(8,128)(2,1)S(1)}, bf16[768,2048]{1,0:T(8,128)(2,1)S(1)}, bf16[768,2048]{1,0:T(8,128)(2,1)S(1)}, bf16[768,2048]{1,0:T(8,128)(...) custom-call(s32[7]{0:T(128)S(1)} %stack.30.parts_ref, ...), custom_call_target="tpu_custom_call" | custom-call | bytes 18874368 | tf_op jit(solution)/shard_map/prefetch/pallas_call | solution.py:129
  22.0 0.4 dispatch.3
  22.4 0.4 collective-permute-start.3
  22.8 1.7 %collective-permute-start.4 = (bf16[64,1536]{1,0:T(8,128)(2,1)S(1)}, bf16[64,1536]{1,0:T(8,128)(2,1)S(1)}, u32[]{:S(2)}, u32[]{:S(2)}) collective-permute-start(bf16[64,1536]{1,0:T(8,128)(2,1)S(1)} %get-tuple-element.48), channel_id=1, source_target_pairs={{0,2},{1,3},{2,0},{3,1},{4,6},{5,7},{6,4},{7,5},{8,10},{9,11},{10,... | collective-permute-start | bytes 589832 | tf_op jit(solution)/shard_map/ppermute | solution.py:283
  24.5 10.3 %gate_up.2 = (f32[256,2048]{1,0:T(8,128)S(1)}, f32[256,2048]{1,0:T(8,128)S(1)}, bf16[768,2048]{1,0:T(8,128)(2,1)S(1)}, bf16[768,2048]{1,0:T(8,128)(2,1)S(1)}, bf16[2048,3072]{1,0:T(8,128)(2,1)S(1)}) custom-call(s32[4]{0:T(128)S(1)} %pad_add_fusion.refs_0_, bf16[64,1536]{1,0:T(8,128)(2,1)S(1)} %get-tuple-element.44.after_ref.refs_1_, ...), custom_call_target="tpu_custom_call" | custom-call | flops 3221225472 | bytes 12582912 | tf_op jit(solution)/shard_map/gate_up/pallas_call | solution.py:195
  34.9 3.8 %gate_up.3.h_ref = bf16[256,2048]{1,0:T(8,128)(2,1)S(1)} custom-call(s32[1]{0:T(128)} %constant.6.clone.1.refs_0_, bf16[64,1536]{1,0:T(8,128)(2,1)S(1)} %get-tuple-element.46.refs_1_, bf16[64,1536]{1,0:T(8,128)(2,1)S(1)} %collective-permute-done.3.refs_2_, bf16[64,1536]{1,0:T(8,128)(2,1)S(1)} %collective-permute-done.4.refs_3_, ...), custom_call_target="tpu_custom_call" | custom-call | flops 3221225472 | bytes 12582912 | tf_op jit(solution)/shard_map/gate_up/pallas_call | solution.py:195
  38.7 1.0 %down.4 = (bf16[64,768]{1,0:T(8,128)(2,1)S(1)}, bf16[64,768]{1,0:T(8,128)(2,1)S(1)}, bf16[64,768]{1,0:T(8,128)(2,1)S(1)}, bf16[64,768]{1,0:T(8,128)(2,1)S(1)}) custom-call(s32[1]{0:T(128)} %bitcast.2.parts_ref, bf16[256,2048]{1,0:T(8,128)(2,1)S(1)} %gate_up.3.h_ref, bf16[2048,3072]{1,0:T(8,128)(2,1)S(1)} %get-tuple-element.62.w_ref), custom_call_target="tpu_custom_call" | custom-call | flops 805306368 | bytes 3538944 | tf_op jit(solution)/shard_map/down/pallas_call | solution.py:239
  39.7 1.6 %collective-permute-start.10 = (bf16[64,768]{1,0:T(8,128)(2,1)S(1)}, bf16[64,768]{1,0:T(8,128)(2,1)S(1)}, u32[]{:S(2)}, u32[]{:S(2)}) collective-permute-start(bf16[64,768]{1,0:T(8,128)(2,1)S(1)} %get-tuple-element.65), channel_id=1, source_target_pairs={{0,2},{1,3},{2,0},{3,1},{4,6},{5,7},{6,4},{7,5},{8,10},{9,11},{10,... | collective-permute-start | bytes 294920 | tf_op jit(solution)/shard_map/ppermute | solution.py:283
  41.3 0.3 collective-permute-start.11
  41.6 0.3 collective-permute-start.9
  41.9 1.0 %down.5 = (bf16[64,768]{1,0:T(8,128)(2,1)S(1)}, bf16[64,768]{1,0:T(8,128)(2,1)S(1)}, bf16[64,768]{1,0:T(8,128)(2,1)S(1)}, bf16[64,768]{1,0:T(8,128)(2,1)S(1)}) custom-call(s32[1]{0:T(128)} %bitcast.5.parts_ref, bf16[256,2048]{1,0:T(8,128)(2,1)S(1)} %gate_up.3.h_ref, bf16[2048,3072]{1,0:T(8,128)(2,1)S(1)} %get-tuple-element.62.w_ref), custom_call_target="tpu_custom_call" | custom-call | flops 805306368 | bytes 3538944 | tf_op jit(solution)/shard_map/down/pallas_call | solution.py:239
  42.9 0.3 collective-permute-start.13
  43.2 1.7 %collective-permute-start.14 = (bf16[64,768]{1,0:T(8,128)(2,1)S(1)}, bf16[64,768]{1,0:T(8,128)(2,1)S(1)}, u32[]{:S(2)}, u32[]{:S(2)}) collective-permute-start(bf16[64,768]{1,0:T(8,128)(2,1)S(1)} %get-tuple-element.69), channel_id=1, source_target_pairs={{0,2},{1,3},{2,0},{3,1},{4,6},{5,7},{6,4},{7,5},{8,10},{9,11},{10,... | collective-permute-start | bytes 294920 | tf_op jit(solution)/shard_map/ppermute | solution.py:283
  44.9 0.1 copy.7.logits_ref
  45.0 0.4 collective-permute-done.10.refs_2_
  45.4 0.6 collective-permute-start.15
  46.0 0.6 collective-permute-done.11.refs_3_
  46.6 0.3 combine.4
  46.9 3.4 %collective-permute-start.12 = (bf16[128,768]{1,0:T(8,128)(2,1)S(1)}, bf16[128,768]{1,0:T(8,128)(2,1)S(1)}, u32[]{:S(2)}, u32[]{:S(2)}) collective-permute-start(bf16[128,768]{1,0:T(8,128)(2,1)S(1)} %combine.4), channel_id=1, source_target_pairs={{0,12},{4,8},{8,4},{12,0},{1,13},{5,9},{9,5},{13,1},{2,14},{6,10},... | collective-permute-start | bytes 589832 | tf_op jit(solution)/shard_map/ppermute | solution.py:283
  50.3 4.6 %copy-done.1 = bf16[2048,3072]{1,0:T(8,128)(2,1)S(1)} copy-done((bf16[2048,3072]{1,0:T(8,128)(2,1)S(1)}, bf16[2048,3072]{1,0:T(8,128)(2,1)}, u32[]{:S(2)}) %copy-start.1) | copy-done | bytes 12582936
  54.9 1.0 %down.6 = (bf16[64,768]{1,0:T(8,128)(2,1)S(1)}, bf16[64,768]{1,0:T(8,128)(2,1)S(1)}, bf16[64,768]{1,0:T(8,128)(2,1)S(1)}, bf16[64,768]{1,0:T(8,128)(2,1)S(1)}) custom-call(s32[1]{0:T(128)} %bitcast.4.parts_ref, bf16[256,2048]{1,0:T(8,128)(2,1)S(1)} %gate_up.3.h_ref, bf16[2048,3072]{1,0:T(8,128)(2,1)S(1)} %copy-done.1), custom_call_target="tpu_custom_call" | custom-call | flops 805306368 | bytes 3538944 | tf_op jit(solution)/shard_map/down/pallas_call | solution.py:239
  55.9 0.3 collective-permute-start.17
  56.2 1.5 %collective-permute-start.18 = (bf16[64,768]{1,0:T(8,128)(2,1)S(1)}, bf16[64,768]{1,0:T(8,128)(2,1)S(1)}, u32[]{:S(2)}, u32[]{:S(2)}) collective-permute-start(bf16[64,768]{1,0:T(8,128)(2,1)S(1)} %get-tuple-element.73), channel_id=1, source_target_pairs={{0,2},{1,3},{2,0},{3,1},{4,6},{5,7},{6,4},{7,5},{8,10},{9,11},{10,... | collective-permute-start | bytes 294920 | tf_op jit(solution)/shard_map/ppermute | solution.py:283
  57.7 0.2 collective-permute-start.19
  57.8 0.3 combine.5
  58.3 3.5 %collective-permute-done.18.refs_2_ = bf16[64,768]{1,0:T(8,128)(2,1)S(1)} collective-permute-done((bf16[64,768]{1,0:T(8,128)(2,1)S(1)}, bf16[64,768]{1,0:T(8,128)(2,1)S(1)}, u32[]{:S(2)}, u32[]{:S(2)}) %collective-permute-start.18) | collective-permute-done | bytes 98336 | tf_op jit(solution)/shard_map/ppermute | solution.py:283
  61.7 1.0 %collective-permute-done.19.refs_3_ = bf16[64,768]{1,0:T(8,128)(2,1)S(1)} collective-permute-done((bf16[64,768]{1,0:T(8,128)(2,1)S(1)}, bf16[64,768]{1,0:T(8,128)(2,1)S(1)}, u32[]{:S(2)}, u32[]{:S(2)}) %collective-permute-start.19) | collective-permute-done | bytes 98336 | tf_op jit(solution)/shard_map/ppermute | solution.py:283
  62.8 0.3 combine.6
  63.1 0.1 collective-permute-start.20
  63.2 1.0 %down.7 = (bf16[64,768]{1,0:T(8,128)(2,1)S(1)}, bf16[64,768]{1,0:T(8,128)(2,1)S(1)}, bf16[64,768]{1,0:T(8,128)(2,1)S(1)}, bf16[64,768]{1,0:T(8,128)(2,1)S(1)}) custom-call(s32[1]{0:T(128)} %bitcast.3.parts_ref, bf16[256,2048]{1,0:T(8,128)(2,1)S(1)} %gate_up.3.h_ref, bf16[2048,3072]{1,0:T(8,128)(2,1)S(1)} %copy-done.2, ...), custom_call_target="tpu_custom_call" | custom-call | flops 805306368 | bytes 3538944 | tf_op jit(solution)/shard_map/down/pallas_call | solution.py:239
  64.2 0.7 collective-permute-start.21
  65.0 1.5 %collective-permute-start.22 = (bf16[64,768]{1,0:T(8,128)(2,1)S(1)}, bf16[64,768]{1,0:T(8,128)(2,1)S(1)}, u32[]{:S(2)}, u32[]{:S(2)}) collective-permute-start(bf16[64,768]{1,0:T(8,128)(2,1)S(1)} %get-tuple-element.77), channel_id=1, source_target_pairs={{0,2},{1,3},{2,0},{3,1},{4,6},{5,7},{6,4},{7,5},{8,10},{9,11},{10,... | collective-permute-start | bytes 294920 | tf_op jit(solution)/shard_map/ppermute | solution.py:283
  66.5 3.6 %collective-permute-done.22.refs_2_ = bf16[64,768]{1,0:T(8,128)(2,1)S(1)} collective-permute-done((bf16[64,768]{1,0:T(8,128)(2,1)S(1)}, bf16[64,768]{1,0:T(8,128)(2,1)S(1)}, u32[]{:S(2)}, u32[]{:S(2)}) %collective-permute-start.22) | collective-permute-done | bytes 98336 | tf_op jit(solution)/shard_map/ppermute | solution.py:283
  70.0 1.5 %collective-permute-done.23.refs_3_ = bf16[64,768]{1,0:T(8,128)(2,1)S(1)} collective-permute-done((bf16[64,768]{1,0:T(8,128)(2,1)S(1)}, bf16[64,768]{1,0:T(8,128)(2,1)S(1)}, u32[]{:S(2)}, u32[]{:S(2)}) %collective-permute-start.23) | collective-permute-done | bytes 98336 | tf_op jit(solution)/shard_map/ppermute | solution.py:283
  71.5 0.3 combine.7
  71.9 2.5 %collective-permute-done.20 = bf16[128,768]{1,0:T(8,128)(2,1)S(1)} collective-permute-done((bf16[128,768]{1,0:T(8,128)(2,1)S(1)}, bf16[128,768]{1,0:T(8,128)(2,1)S(1)}, u32[]{:S(2)}, u32[]{:S(2)}) %collective-permute-start.20) | collective-permute-done | bytes 196640 | tf_op jit(solution)/shard_map/ppermute | solution.py:283
  74.3 0.8 %add_convert_fusion = bf16[128,768]{1,0:T(8,128)(2,1)} fusion(bf16[128,768]{1,0:T(8,128)(2,1)S(1)} %combine.7, bf16[128,768]{1,0:T(8,128)(2,1)S(1)} %collective-permute-done.20, bf16[128,768]{1,0:T(8,128)(2,1)S(1)} %collective-permute-done.16, bf16[128,768]{1,0:T(8,128)(2,1)S(1)} %collective-permute-done.12.refs_0_), kind=kLoop, calls=%fused_computation | loop fusion | flops 786432 | bytes 983040 | tf_op jit(solution)/shard_map/convert_element_type | solution.py:338
  (31 shorter events, 0.2 us)
Async XLA Ops:
  0.0 11.6 %collective-permute-start.2 = (bf16[128,768]{1,0:T(8,128)(2,1)}, bf16[128,768]{1,0:T(8,128)(2,1)S(1)}, u32[]{:S(2)}, u32[]{:S(2)}) collective-permute-start(bf16[128,768]{1,0:T(8,128)(2,1)} %refs_0_.2), channel_id=1, source_target_pairs={{0,4},{4,0},{8,12},{12,8},{1,5},{5,1},{9,13},{13,9},{2,6},{6,2},{1... | collective-permute-start | bytes 589832 | tf_op jit(solution)/shard_map/ppermute | solution.py:283
  3.0 19.0 %collective-permute-start = (bf16[128,768]{1,0:T(8,128)(2,1)}, bf16[128,768]{1,0:T(8,128)(2,1)S(1)}, u32[]{:S(2)}, u32[]{:S(2)}) collective-permute-start(bf16[128,768]{1,0:T(8,128)(2,1)} %refs_0_.2), channel_id=1, source_target_pairs={{0,8},{4,12},{8,0},{12,4},{1,9},{5,13},{9,1},{13,5},{2,10},{6,14},... | collective-permute-start | bytes 589832 | tf_op jit(solution)/shard_map/ppermute | solution.py:283
  5.6 16.4 %collective-permute-start.1 = (bf16[128,768]{1,0:T(8,128)(2,1)}, bf16[128,768]{1,0:T(8,128)(2,1)S(1)}, u32[]{:S(2)}, u32[]{:S(2)}) collective-permute-start(bf16[128,768]{1,0:T(8,128)(2,1)} %refs_0_.2), channel_id=1, source_target_pairs={{0,12},{4,8},{8,4},{12,0},{1,13},{5,9},{9,5},{13,1},{2,14},{6,10},... | collective-permute-start | bytes 589832 | tf_op jit(solution)/shard_map/ppermute | solution.py:283
  5.6 0.7 copy-start.4
  11.6 0.9 %copy-start.3 = (bf16[128,768]{1,0:T(8,128)(2,1)S(1)}, bf16[128,768]{1,0:T(8,128)(2,1)}, u32[]{:S(2)}) copy-start(bf16[128,768]{1,0:T(8,128)(2,1)} %refs_0_.2) | copy-start | bytes 589828
  12.9 11.6 %collective-permute-start.6 = (bf16[64,1536]{1,0:T(8,128)(2,1)S(1)}, bf16[64,1536]{1,0:T(8,128)(2,1)S(1)}, u32[]{:S(2)}, u32[]{:S(2)}) collective-permute-start(bf16[64,1536]{1,0:T(8,128)(2,1)S(1)} %get-tuple-element.52), channel_id=1, source_target_pairs={{0,1},{1,0},{2,3},{3,2},{4,5},{5,4},{6,7},{7,6},{8,9},{9,8},{10,11... | collective-permute-start | bytes 589832 | tf_op jit(solution)/shard_map/ppermute | solution.py:283
  12.9 11.6 %collective-permute-start.7 = (bf16[64,1536]{1,0:T(8,128)(2,1)S(1)}, bf16[64,1536]{1,0:T(8,128)(2,1)S(1)}, u32[]{:S(2)}, u32[]{:S(2)}) collective-permute-start(bf16[64,1536]{1,0:T(8,128)(2,1)S(1)} %get-tuple-element.53), channel_id=1, source_target_pairs={{0,2},{1,3},{2,0},{3,1},{4,6},{5,7},{6,4},{7,5},{8,10},{9,11},{10,... | collective-permute-start | bytes 589832 | tf_op jit(solution)/shard_map/ppermute | solution.py:283
  14.7 9.8 %collective-permute-start.8 = (bf16[64,1536]{1,0:T(8,128)(2,1)S(1)}, bf16[64,1536]{1,0:T(8,128)(2,1)S(1)}, u32[]{:S(2)}, u32[]{:S(2)}) collective-permute-start(bf16[64,1536]{1,0:T(8,128)(2,1)S(1)} %get-tuple-element.54), channel_id=1, source_target_pairs={{0,3},{1,2},{2,1},{3,0},{4,7},{5,6},{6,5},{7,4},{8,11},{9,10},{10,... | collective-permute-start | bytes 589832 | tf_op jit(solution)/shard_map/ppermute | solution.py:283
  22.4 12.4 %collective-permute-start.3 = (bf16[64,1536]{1,0:T(8,128)(2,1)S(1)}, bf16[64,1536]{1,0:T(8,128)(2,1)S(1)}, u32[]{:S(2)}, u32[]{:S(2)}) collective-permute-start(bf16[64,1536]{1,0:T(8,128)(2,1)S(1)} %get-tuple-element.47), channel_id=1, source_target_pairs={{0,1},{1,0},{2,3},{3,2},{4,5},{5,4},{6,7},{7,6},{8,9},{9,8},{10,11... | collective-permute-start | bytes 589832 | tf_op jit(solution)/shard_map/ppermute | solution.py:283
  22.8 12.0 %collective-permute-start.4 = (bf16[64,1536]{1,0:T(8,128)(2,1)S(1)}, bf16[64,1536]{1,0:T(8,128)(2,1)S(1)}, u32[]{:S(2)}, u32[]{:S(2)}) collective-permute-start(bf16[64,1536]{1,0:T(8,128)(2,1)S(1)} %get-tuple-element.48), channel_id=1, source_target_pairs={{0,2},{1,3},{2,0},{3,1},{4,6},{5,7},{6,4},{7,5},{8,10},{9,11},{10,... | collective-permute-start | bytes 589832 | tf_op jit(solution)/shard_map/ppermute | solution.py:283
  24.5 10.4 %collective-permute-start.5 = (bf16[64,1536]{1,0:T(8,128)(2,1)S(1)}, bf16[64,1536]{1,0:T(8,128)(2,1)S(1)}, u32[]{:S(2)}, u32[]{:S(2)}) collective-permute-start(bf16[64,1536]{1,0:T(8,128)(2,1)S(1)} %get-tuple-element.49), channel_id=1, source_target_pairs={{0,3},{1,2},{2,1},{3,0},{4,7},{5,6},{6,5},{7,4},{8,11},{9,10},{10,... | collective-permute-start | bytes 589832 | tf_op jit(solution)/shard_map/ppermute | solution.py:283
  34.8 7.1 %copy-start = (bf16[2048,3072]{1,0:T(8,128)(2,1)}, bf16[2048,3072]{1,0:T(8,128)(2,1)S(1)}, u32[]{:S(2)}) copy-start(bf16[2048,3072]{1,0:T(8,128)(2,1)S(1)} %get-tuple-element.62.w_ref) | copy-start | bytes 37748740
  39.7 5.7 %collective-permute-start.10 = (bf16[64,768]{1,0:T(8,128)(2,1)S(1)}, bf16[64,768]{1,0:T(8,128)(2,1)S(1)}, u32[]{:S(2)}, u32[]{:S(2)}) collective-permute-start(bf16[64,768]{1,0:T(8,128)(2,1)S(1)} %get-tuple-element.65), channel_id=1, source_target_pairs={{0,2},{1,3},{2,0},{3,1},{4,6},{5,7},{6,4},{7,5},{8,10},{9,11},{10,... | collective-permute-start | bytes 294920 | tf_op jit(solution)/shard_map/ppermute | solution.py:283
  41.3 5.3 %collective-permute-start.11 = (bf16[64,768]{1,0:T(8,128)(2,1)S(1)}, bf16[64,768]{1,0:T(8,128)(2,1)S(1)}, u32[]{:S(2)}, u32[]{:S(2)}) collective-permute-start(bf16[64,768]{1,0:T(8,128)(2,1)S(1)} %get-tuple-element.66), channel_id=1, source_target_pairs={{0,3},{1,2},{2,1},{3,0},{4,7},{5,6},{6,5},{7,4},{8,11},{9,10},{10,... | collective-permute-start | bytes 294920 | tf_op jit(solution)/shard_map/ppermute | solution.py:283
  41.6 3.3 %copy-start.5 = (f32[128,2]{0,1:T(2,128)S(1)}, f32[128,2]{0,1:T(2,128)}, u32[]{:S(2)}) copy-start(f32[128,2]{0,1:T(2,128)} %param.8) | copy-start | bytes 3076
  41.6 5.0 %collective-permute-start.9 = (bf16[64,768]{1,0:T(8,128)(2,1)S(1)}, bf16[64,768]{1,0:T(8,128)(2,1)S(1)}, u32[]{:S(2)}, u32[]{:S(2)}) collective-permute-start(bf16[64,768]{1,0:T(8,128)(2,1)S(1)} %get-tuple-element.64), channel_id=1, source_target_pairs={{0,1},{1,0},{2,3},{3,2},{4,5},{5,4},{6,7},{7,6},{8,9},{9,8},{10,11... | collective-permute-start | bytes 294920 | tf_op jit(solution)/shard_map/ppermute | solution.py:283
  42.9 13.3 %collective-permute-start.13 = (bf16[64,768]{1,0:T(8,128)(2,1)S(1)}, bf16[64,768]{1,0:T(8,128)(2,1)S(1)}, u32[]{:S(2)}, u32[]{:S(2)}) collective-permute-start(bf16[64,768]{1,0:T(8,128)(2,1)S(1)} %get-tuple-element.68), channel_id=1, source_target_pairs={{0,1},{1,0},{2,3},{3,2},{4,5},{5,4},{6,7},{7,6},{8,9},{9,8},{10,11... | collective-permute-start | bytes 294920 | tf_op jit(solution)/shard_map/ppermute | solution.py:283
  43.2 14.5 %collective-permute-start.14 = (bf16[64,768]{1,0:T(8,128)(2,1)S(1)}, bf16[64,768]{1,0:T(8,128)(2,1)S(1)}, u32[]{:S(2)}, u32[]{:S(2)}) collective-permute-start(bf16[64,768]{1,0:T(8,128)(2,1)S(1)} %get-tuple-element.69), channel_id=1, source_target_pairs={{0,2},{1,3},{2,0},{3,1},{4,6},{5,7},{6,4},{7,5},{8,10},{9,11},{10,... | collective-permute-start | bytes 294920 | tf_op jit(solution)/shard_map/ppermute | solution.py:283
  45.4 12.5 %collective-permute-start.15 = (bf16[64,768]{1,0:T(8,128)(2,1)S(1)}, bf16[64,768]{1,0:T(8,128)(2,1)S(1)}, u32[]{:S(2)}, u32[]{:S(2)}) collective-permute-start(bf16[64,768]{1,0:T(8,128)(2,1)S(1)} %get-tuple-element.70), channel_id=1, source_target_pairs={{0,3},{1,2},{2,1},{3,0},{4,7},{5,6},{6,5},{7,4},{8,11},{9,10},{10,... | collective-permute-start | bytes 294920 | tf_op jit(solution)/shard_map/ppermute | solution.py:283
  46.9 16.3 %collective-permute-start.12 = (bf16[128,768]{1,0:T(8,128)(2,1)S(1)}, bf16[128,768]{1,0:T(8,128)(2,1)S(1)}, u32[]{:S(2)}, u32[]{:S(2)}) collective-permute-start(bf16[128,768]{1,0:T(8,128)(2,1)S(1)} %combine.4), channel_id=1, source_target_pairs={{0,12},{4,8},{8,4},{12,0},{1,13},{5,9},{9,5},{13,1},{2,14},{6,10},... | collective-permute-start | bytes 589832 | tf_op jit(solution)/shard_map/ppermute | solution.py:283
  50.3 4.6 %copy-start.1 = (bf16[2048,3072]{1,0:T(8,128)(2,1)S(1)}, bf16[2048,3072]{1,0:T(8,128)(2,1)}, u32[]{:S(2)}) copy-start(bf16[2048,3072]{1,0:T(8,128)(2,1)} %copy-done) | copy-start | bytes 37748740
  54.9 8.3 %copy-start.2 = (bf16[2048,3072]{1,0:T(8,128)(2,1)S(1)}, bf16[2048,3072]{1,0:T(8,128)(2,1)}, u32[]{:S(2)}) copy-start(bf16[2048,3072]{1,0:T(8,128)(2,1)} %copy-done) | copy-start | bytes 37748740
  55.9 2.3 %collective-permute-start.17 = (bf16[64,768]{1,0:T(8,128)(2,1)S(1)}, bf16[64,768]{1,0:T(8,128)(2,1)S(1)}, u32[]{:S(2)}, u32[]{:S(2)}) collective-permute-start(bf16[64,768]{1,0:T(8,128)(2,1)S(1)} %get-tuple-element.72), channel_id=1, source_target_pairs={{0,1},{1,0},{2,3},{3,2},{4,5},{5,4},{6,7},{7,6},{8,9},{9,8},{10,11... | collective-permute-start | bytes 294920 | tf_op jit(solution)/shard_map/ppermute | solution.py:283
  56.2 5.5 %collective-permute-start.18 = (bf16[64,768]{1,0:T(8,128)(2,1)S(1)}, bf16[64,768]{1,0:T(8,128)(2,1)S(1)}, u32[]{:S(2)}, u32[]{:S(2)}) collective-permute-start(bf16[64,768]{1,0:T(8,128)(2,1)S(1)} %get-tuple-element.73), channel_id=1, source_target_pairs={{0,2},{1,3},{2,0},{3,1},{4,6},{5,7},{6,4},{7,5},{8,10},{9,11},{10,... | collective-permute-start | bytes 294920 | tf_op jit(solution)/shard_map/ppermute | solution.py:283
  57.7 5.1 %collective-permute-start.19 = (bf16[64,768]{1,0:T(8,128)(2,1)S(1)}, bf16[64,768]{1,0:T(8,128)(2,1)S(1)}, u32[]{:S(2)}, u32[]{:S(2)}) collective-permute-start(bf16[64,768]{1,0:T(8,128)(2,1)S(1)} %get-tuple-element.74), channel_id=1, source_target_pairs={{0,3},{1,2},{2,1},{3,0},{4,7},{5,6},{6,5},{7,4},{8,11},{9,10},{10,... | collective-permute-start | bytes 294920 | tf_op jit(solution)/shard_map/ppermute | solution.py:283
  58.2 13.7 %collective-permute-start.16 = (bf16[128,768]{1,0:T(8,128)(2,1)S(1)}, bf16[128,768]{1,0:T(8,128)(2,1)S(1)}, u32[]{:S(2)}, u32[]{:S(2)}) collective-permute-start(bf16[128,768]{1,0:T(8,128)(2,1)S(1)} %combine.5), channel_id=1, source_target_pairs={{0,8},{4,12},{8,0},{12,4},{1,9},{5,13},{9,1},{13,5},{2,10},{6,14},... | collective-permute-start | bytes 589832 | tf_op jit(solution)/shard_map/ppermute | solution.py:283
  63.1 11.2 %collective-permute-start.20 = (bf16[128,768]{1,0:T(8,128)(2,1)S(1)}, bf16[128,768]{1,0:T(8,128)(2,1)S(1)}, u32[]{:S(2)}, u32[]{:S(2)}) collective-permute-start(bf16[128,768]{1,0:T(8,128)(2,1)S(1)} %combine.6), channel_id=1, source_target_pairs={{0,4},{4,0},{8,12},{12,8},{1,5},{5,1},{9,13},{13,9},{2,6},{6,2},{1... | collective-permute-start | bytes 589832 | tf_op jit(solution)/shard_map/ppermute | solution.py:283
  64.2 2.2 %collective-permute-start.21 = (bf16[64,768]{1,0:T(8,128)(2,1)S(1)}, bf16[64,768]{1,0:T(8,128)(2,1)S(1)}, u32[]{:S(2)}, u32[]{:S(2)}) collective-permute-start(bf16[64,768]{1,0:T(8,128)(2,1)S(1)} %get-tuple-element.76), channel_id=1, source_target_pairs={{0,1},{1,0},{2,3},{3,2},{4,5},{5,4},{6,7},{7,6},{8,9},{9,8},{10,11... | collective-permute-start | bytes 294920 | tf_op jit(solution)/shard_map/ppermute | solution.py:283
  65.0 5.1 %collective-permute-start.22 = (bf16[64,768]{1,0:T(8,128)(2,1)S(1)}, bf16[64,768]{1,0:T(8,128)(2,1)S(1)}, u32[]{:S(2)}, u32[]{:S(2)}) collective-permute-start(bf16[64,768]{1,0:T(8,128)(2,1)S(1)} %get-tuple-element.77), channel_id=1, source_target_pairs={{0,2},{1,3},{2,0},{3,1},{4,6},{5,7},{6,4},{7,5},{8,10},{9,11},{10,... | collective-permute-start | bytes 294920 | tf_op jit(solution)/shard_map/ppermute | solution.py:283
  66.4 5.1 %collective-permute-start.23 = (bf16[64,768]{1,0:T(8,128)(2,1)S(1)}, bf16[64,768]{1,0:T(8,128)(2,1)S(1)}, u32[]{:S(2)}, u32[]{:S(2)}) collective-permute-start(bf16[64,768]{1,0:T(8,128)(2,1)S(1)} %get-tuple-element.78), channel_id=1, source_target_pairs={{0,3},{1,2},{2,1},{3,0},{4,7},{5,6},{6,5},{7,4},{8,11},{9,10},{10,... | collective-permute-start | bytes 294920 | tf_op jit(solution)/shard_map/ppermute | solution.py:283

commit v5 on v4

--- a/solution.py
+++ b/solution.py
@@ -156,8 +156,10 @@
     x = jnp.concatenate([r[...] for r in x_refs], axis=0)
     width, hidden = weights[0].shape
     tile = min(512, hidden)
-    for n in range(hidden // tile):
-        columns = slice(n * tile, (n + 1) * tile)
+
+    @pl.loop(0, hidden // tile)
+    def _(n):
+        columns = pl.ds(pl.multiple_of(n * tile, tile), tile)
         sums = []
         for kind in range(2):
             total = None if first else (old_gate, old_up)[kind][:, columns]
@@ -175,6 +177,7 @@
         else:
             rest[0][:, columns] = gate
             rest[1][:, columns] = up
+
     for copy in copies:
         copy.wait()
 
@@ -218,62 +221,94 @@
     return results[: len(out_shape)], results[len(out_shape) :]
 
 
-def down_kernel(parts_ref, h_ref, w_ref, *refs, slices, waits):
+def down_kernel(parts_ref, h_ref, w_ref, *refs, width, experts, waits):
     out_refs = refs[waits:]
-    capacity, wide = out_refs[0].shape
-    width = wide // slices
+    capacity = out_refs[0].shape[0]
     tile = min(256, width)
-    for i in range(slices):
-        for n in range(width // tile):
-            start = pl.multiple_of(parts_ref[i] * width + n * tile, tile)
-            y = jnp.dot(h_ref[...], w_ref[:, pl.ds(start, tile)], preferred_element_type=F32)
-            columns = pl.ds(i * width + n * tile, tile)
-            for d, out in enumerate(out_refs):
-                out[:, columns] = y[d * capacity : (d + 1) * capacity].astype(BF16)
-
-
-def down(parts, hidden, down_w, width, experts, after):
+    part = 0
+    for g in range(len(out_refs) // experts):
+        outs = out_refs[g * experts : (g + 1) * experts]
+        for i in range(outs[0].shape[1] // width):
+            for n in range(width // tile):
+                start = pl.multiple_of(parts_ref[part] * width + n * tile, tile)
+                y = jnp.dot(h_ref[...], w_ref[:, pl.ds(start, tile)], preferred_element_type=F32)
+                columns = pl.ds(i * width + n * tile, tile)
+                for d, out in enumerate(outs):
+                    out[:, columns] = y[d * capacity : (d + 1) * capacity].astype(BF16)
+            part += 1
+
+
+def down(groups, hidden, down_w, width, experts, after):
     rows, depth = hidden.shape
     capacity = rows // experts
+    parts = [part for group in groups for part in group]
     wide = width * len(parts)
-    return pl.pallas_call(
-        functools.partial(down_kernel, slices=len(parts), waits=len(after)),
-        out_shape=[jax.ShapeDtypeStruct((capacity, wide), BF16)] * experts,
+    blocks = pl.pallas_call(
+        functools.partial(down_kernel, width=width, experts=experts, waits=len(after)),
+        out_shape=[
+            jax.ShapeDtypeStruct((capacity, width * len(group)), BF16)
+            for group in groups
+            for _ in range(experts)
+        ],
         in_specs=[pl.BlockSpec(memory_space=pltpu.SMEM)]
         + [pl.BlockSpec(memory_space=pltpu.VMEM)] * 2
         + [pl.BlockSpec(memory_space=pl.ANY)] * len(after),
-        out_specs=[pl.BlockSpec(memory_space=pltpu.VMEM)] * experts,
+        out_specs=[pl.BlockSpec(memory_space=pltpu.VMEM)] * (experts * len(groups)),
         cost_estimate=cost(2 * rows * depth * wide, 2 * depth * wide + 2 * rows * wide),
         compiler_params=params(),
         name="down",
     )(jnp.stack(parts), *pinned([hidden, down_w]), *after)
-
-
-def combine_kernel(pick_ref, logits_ref, *refs, experts):
-    y_refs, out_refs = refs[:experts], refs[experts:]
-    rows, width = out_refs[0].shape
-    y = jnp.concatenate([r[...] for r in y_refs], axis=0)
+    return [blocks[i * experts : (i + 1) * experts] for i in range(len(groups))]
+
+
+def hold_kernel(*refs):
+    count = len(refs) // 2
+    for i in range(count):
+        refs[count + 1 + i][...] = refs[i][...]
+
+
+def hold(blocks, after):
+    return pl.pallas_call(
+        hold_kernel,
+        out_shape=[jax.ShapeDtypeStruct(block.shape, block.dtype) for block in blocks],
+        in_specs=[pl.BlockSpec(memory_space=pltpu.VMEM)] * len(blocks)
+        + [pl.BlockSpec(memory_space=pl.ANY)],
+        out_specs=[pl.BlockSpec(memory_space=pltpu.VMEM)] * len(blocks),
+        cost_estimate=cost(0, sum(4 * block.size for block in blocks)),
+        compiler_params=params(),
+        name="hold",
+    )(*blocks, after)
+
+
+def combine_kernel(pick_ref, logits_ref, *refs, experts, sums, index):
+    y_refs, added, out = refs[:experts], refs[experts : experts + sums], refs[-1]
+    rows, width = out.shape
+    columns = pl.ds(index * width, width)
+    y = jnp.concatenate([r[:, columns] for r in y_refs], axis=0)
     picked = lax.dot_general(
         pick_ref[...], y, (((0,), (0,)), ((), ())), preferred_element_type=F32
     )
     share = 1.0 / (1.0 + jnp.exp(logits_ref[:, 1:2] - logits_ref[:, 0:1]))
-    mixed = (picked[:rows] * share + picked[rows:] * (1.0 - share)).astype(BF16)
-    for i, out in enumerate(out_refs):
-        out[...] = mixed[:, i * width : (i + 1) * width]
-
-
-def combine(pick, logits, blocks, slices):
+    mixed = picked[:rows] * share + picked[rows:] * (1.0 - share)
+    for other in added:
+        mixed = mixed + other[...].astype(F32)
+    out[...] = mixed.astype(BF16)
+
+
+def combine(pick, logits, blocks, width, index, added):
     rows = logits.shape[0]
-    wide = blocks[0].shape[1]
-    return pl.pallas_call(
-        functools.partial(combine_kernel, experts=len(blocks)),
-        out_shape=[jax.ShapeDtypeStruct((rows, wide // slices), BF16)] * slices,
-        in_specs=[pl.BlockSpec(memory_space=pltpu.VMEM)] * (2 + len(blocks)),
-        out_specs=[pl.BlockSpec(memory_space=pltpu.VMEM)] * slices,
-        cost_estimate=cost(4 * rows * pick.shape[0] * wide, 6 * rows * wide),
+    operands = 2 + len(blocks) + len(added)
+    return pl.pallas_call(
+        functools.partial(
+            combine_kernel, experts=len(blocks), sums=len(added), index=index
+        ),
+        out_shape=jax.ShapeDtypeStruct((rows, width), BF16),
+        in_specs=[pl.BlockSpec(memory_space=pltpu.VMEM)] * operands,
+        out_specs=pl.BlockSpec(memory_space=pltpu.VMEM),
+        cost_estimate=cost(4 * rows * pick.shape[0] * width, 6 * rows * width),
         compiler_params=params(),
         name="combine",
-    )(pick, logits, *blocks)
+    )(pick, logits, *blocks, *added)
 
 
 def swap(value, axis, distance):
@@ -303,39 +338,43 @@
         blocks = [lax.all_gather(tokens, "tensor", axis=1, tiled=True)]
     placed, pick = place(me, expert_ids, experts, capacity)
 
-    fetches = [(w, part_of(d), width) for d in distances for w in (gate_weight, up_weight)]
-    fetches.append((down_weight, 0, down_weight.shape[1]))
-    early = min(6, len(fetches) - 1)
     groups = [distances[i : i + 2] for i in range(0, len(distances), 2)]
-    arrived, weights = [], []
+    ready, arrived, weights = placed, [], []
     for group in groups:
+        fetches = [(w, part_of(d), width) for d in group for w in (gate_weight, up_weight)]
+        weights.append(list(prefetch(fetches, ready)))
         block = [blocks[d] for d in group]
-        outgoing = dispatch(placed, block, experts, capacity, weights[:1])
+        outgoing = dispatch(placed, block, experts, capacity, weights[-1][:1])
         arrived.append([swap(block, "expert", e) for e, block in enumerate(outgoing)])
-        if not weights:
-            weights = list(prefetch(fetches[:early], outgoing[0]))
-    sums = None
-    for group, x_blocks in zip(groups, arrived):
-        chosen = weights[2 * group[0] : 2 * group[-1] + 2]
-        later = fetches[early:] if group is groups[0] else []
-        sums, fetched = gate_up(x_blocks, chosen, sums, group is groups[-1], later)
-        weights.extend(fetched)
-    hidden, down_w = sums[0], weights[-1]
+        ready = outgoing[0]
+
+    sums, fetched = None, []
+    for group, x_blocks, chosen in zip(groups, arrived, weights):
+        later = [(down_weight, 0, down_weight.shape[1])] if sums is None else []
+        sums, brought = gate_up(x_blocks, chosen, sums, group is groups[-1], later)
+        fetched.extend(brought)
+    hidden, down_w = sums[0], fetched[0]
 
     groups = [[d] for d in reversed(distances)]
-    total = []
+    parts = [[part_of(d) for d in group] for group in groups]
+    terms = down(parts[:1], hidden, down_w, width, experts, [])
+    sums = []
     for group in groups:
-        after = total[:1] if group is groups[-1] else []
-        terms = down([part_of(d) for d in group], hidden, down_w, width, experts, after)
-        returned = [swap(block, "expert", e) for e, block in enumerate(terms)]
-        mixtures = combine(pick, route_logits, returned, len(group))
-        if not direct:
-            return lax.psum_scatter(mixtures[0], "tensor", scatter_dimension=1, tiled=True)
-        total.extend(swap(mixed, "tensor", d) for d, mixed in zip(group, mixtures))
-    out = total[0].astype(F32)
-    for term in total[1:]:
-        out = out + term.astype(F32)
-    return out.astype(BF16)
+        blocks = terms[groups.index(group)]
+        if group is groups[-1] and sums:
+            blocks = hold(blocks, sums[0])
+        returned = [swap(block, "expert", e) for e, block in enumerate(blocks)]
+        if group is groups[0] and len(parts) > 1:
+            terms += down(parts[1:], hidden, down_w, width, experts, returned[1:2])
+        for index, d in enumerate(group):
+            last = d == distances[0]
+            added = sums if last else []
+            mixed = combine(pick, route_logits, returned, width, index, added)
+            if not last:
+                sums.append(swap(mixed, "tensor", d))
+    if direct:
+        return mixed
+    return lax.psum_scatter(mixed, "tensor", scatter_dimension=1, tiled=True)
 
 
 def solution(mesh):

time: 75.3 us -> 76.7 us (1.019)
  waiting for transfers between devices: 18.2 us -> 15 us
  Pallas kernels: 27.4 us -> 29.7 us
  starting transfers between devices: 22.1 us -> 24 us
  local copies, waits for them, and re-layouts: 6.39 us -> 7.61 us
  other arithmetic: 0.86 us -> 0.08 us
    pallas_call x2, Pallas kernels: 14.1 us -> 9.9 us  [gate_up(): pl.pallas_call(functools.partial(gate_up_kernel, experts=experts, slices=...]
    pallas_call x1 -> x2, Pallas kernels: 7.04 us -> 10.7 us  [prefetch(): pl.pallas_call(prefetch_kernel, out_shape=shapes, in_specs=[pl.BlockSpec(...]
    ppermute x24, waiting for transfers between devices: 18.2 us -> 15 us  [swap(): return lax.ppermute(value, axis, [(i, i ^ distance) for i in range(count)])]
    pallas_call x2, Pallas kernels: 0.72 us -> 2.64 us  [dispatch(): pl.pallas_call(functools.partial(dispatch_kernel, count=len(blocks), wait...]
    ppermute x24, starting transfers between devices: 22.1 us -> 24 us  [swap(): return lax.ppermute(value, axis, [(i, i ^ distance) for i in range(count)])]
    unnamed x13 -> x23, local copies, waits for them, and re-layouts: 6.3 us -> 7.43 us
    pallas_call x8 -> x7, Pallas kernels: 5.34 us -> 6.3 us  [the longest x2 4.29 us: down(): pl.pallas_call(functools.partial(down_kernel, width=width, experts=expert...]
    convert_element_type x1 -> x0, other arithmetic: 0.78 us -> none  [per_device(): return out.astype(BF16)]
  transfers between devices with their start and end apart: 24 -> 24, of which waited for: 8 -> 7; matrix products, arithmetic and copies ran while one was open for 0% -> 0% of each run, Pallas kernels for 30% -> 31%
where the time goes in v5:
time: 76.7 us; the launch traced here: 76.5 us
  Pallas kernels  29.7 us (39%)
  starting transfers between devices  24 us (31%)
  waiting for transfers between devices  15 us (20%)
  local copies, waits for them, and re-layouts  7.61 us (10%)
    ppermute x24, starting transfers between devices, swap(): return lax.ppermute(value, axis, [(i, i ^ distance) for i in range(count)])  24 us
    ppermute x24, waiting for transfers between devices, swap(): return lax.ppermute(value, axis, [(i, i ^ distance) for i in range(count)])  15 us
    pallas_call x2, Pallas kernels, prefetch(): pl.pallas_call(prefetch_kernel, out_shape=shapes, in_specs=[pl.BlockSpec(...  10.7 us
    pallas_call x2, Pallas kernels, gate_up(): pl.pallas_call(functools.partial(gate_up_kernel, experts=experts, slices=...  9.9 us
    unnamed x23, local copies, waits for them, and re-layouts  7.43 us
    pallas_call x2, Pallas kernels, down(): pl.pallas_call(functools.partial(down_kernel, width=width, experts=expert...  4.29 us
    pallas_call x2, Pallas kernels, dispatch(): pl.pallas_call(functools.partial(dispatch_kernel, count=len(blocks), wait...  2.64 us
    pallas_call x4, Pallas kernels, combine(): pl.pallas_call(functools.partial(combine_kernel, experts=len(blocks), sum...  1.99 us
  transfers between devices with their start and end apart: 24, of which 7 were waited for; matrix products, arithmetic and copies ran while one was open for 0% of the time, Pallas kernels for 31%

profile of v5, /device:TPU:0, one launch (start us, length us, event | category | flops | bytes accessed | tf_op | source)
XLA Modules:
  0.0 76.5 jit_solution(3412112979744345426)
XLA Ops:
  0.0 3.0 %collective-permute-start.2 = (bf16[128,768]{1,0:T(8,128)(2,1)}, bf16[128,768]{1,0:T(8,128)(2,1)S(1)}, u32[]{:S(2)}, u32[]{:S(2)}) collective-permute-start(bf16[128,768]{1,0:T(8,128)(2,1)} %refs_0_.4), channel_id=1, source_target_pairs={{0,4},{4,0},{8,12},{12,8},{1,5},{5,1},{9,13},{13,9},{2,6},{6,2},{1... | collective-permute-start | bytes 589832 | tf_op jit(solution)/shard_map/ppermute | solution.py:318
  3.0 2.6 %collective-permute-start = (bf16[128,768]{1,0:T(8,128)(2,1)}, bf16[128,768]{1,0:T(8,128)(2,1)}, u32[]{:S(2)}, u32[]{:S(2)}) collective-permute-start(bf16[128,768]{1,0:T(8,128)(2,1)} %refs_0_.4), channel_id=1, source_target_pairs={{0,8},{4,12},{8,0},{12,4},{1,9},{5,13},{9,1},{13,5},{2,10},{6,14},... | collective-permute-start | bytes 589832 | tf_op jit(solution)/shard_map/ppermute | solution.py:318
  5.6 0.7 copy-done.9
  6.3 0.2 routing.1
  6.5 0.1 stack.35.parts_ref
  6.6 5.2 %prefetch.2 = (bf16[768,2048]{1,0:T(8,128)(2,1)S(1)}, bf16[768,2048]{1,0:T(8,128)(2,1)S(1)}, bf16[768,2048]{1,0:T(8,128)(2,1)S(1)}, bf16[768,2048]{1,0:T(8,128)(2,1)S(1)}) custom-call(s32[5]{0:T(128)S(1)} %stack.35.parts_ref, bf16[256,128]{1,0:T(8,128)(2,1)S(1)} %get-tuple-element.47.after_ref.placed_ref, bf16[1,3072,2048]{2,1,0:T(8,128)(2,1)} %refs_2_.3, ...), custom_call_target="tpu_custom_call" | custom-call | bytes 12582912 | tf_op jit(solution)/shard_map/prefetch/pallas_call | solution.py:129
  11.8 1.6 %copy-done = bf16[768,2048]{1,0:T(8,128)(2,1)} copy-done((bf16[768,2048]{1,0:T(8,128)(2,1)}, bf16[768,2048]{1,0:T(8,128)(2,1)S(1)}, u32[]{:S(2)}) %copy-start) | copy-done | bytes 3145752
  13.4 1.7 %copy-done.2 = bf16[768,2048]{1,0:T(8,128)(2,1)} copy-done((bf16[768,2048]{1,0:T(8,128)(2,1)}, bf16[768,2048]{1,0:T(8,128)(2,1)S(1)}, u32[]{:S(2)}) %copy-start.2) | copy-done | bytes 3145752
  15.2 1.7 %copy-done.4 = bf16[768,2048]{1,0:T(8,128)(2,1)} copy-done((bf16[768,2048]{1,0:T(8,128)(2,1)}, bf16[768,2048]{1,0:T(8,128)(2,1)S(1)}, u32[]{:S(2)}) %copy-start.4) | copy-done | bytes 3145752
  16.8 0.7 copy-done.7
  17.5 0.9 %copy-done.8 = bf16[128,768]{1,0:T(8,128)(2,1)S(1)} copy-done((bf16[128,768]{1,0:T(8,128)(2,1)S(1)}, bf16[128,768]{1,0:T(8,128)(2,1)}, u32[]{:S(2)}) %copy-start.8) | copy-done | bytes 196632
  18.4 1.1 %dispatch.2 = (bf16[64,1536]{1,0:T(8,128)(2,1)S(1)}, bf16[64,1536]{1,0:T(8,128)(2,1)}, bf16[64,1536]{1,0:T(8,128)(2,1)}, bf16[64,1536]{1,0:T(8,128)(2,1)}) custom-call(bf16[256,128]{1,0:T(8,128)(2,1)S(1)} %get-tuple-element.47.after_ref.placed_ref, bf16[128,768]{1,0:T(8,128)(2,1)S(1)} %copy-done.6, bf16[128,768]{1,0:T(8,128)(2,1)S(1)} %copy-done.8, ...), custom_call_target="tpu_custom_call" | custom-call | flops 100663296 | bytes 1179648 | tf_op jit(solution)/shard_map/dispatch/pallas_call | solution.py:88
  19.6 1.7 %collective-permute-start.7 = (bf16[64,1536]{1,0:T(8,128)(2,1)}, bf16[64,1536]{1,0:T(8,128)(2,1)}, u32[]{:S(2)}, u32[]{:S(2)}) collective-permute-start(bf16[64,1536]{1,0:T(8,128)(2,1)} %get-tuple-element.59), channel_id=1, source_target_pairs={{0,2},{1,3},{2,0},{3,1},{4,6},{5,7},{6,4},{7,5},{8,10},{9,11},{10,... | collective-permute-start | bytes 589832 | tf_op jit(solution)/shard_map/ppermute | solution.py:318
  21.3 0.2 collective-permute-start.8
  21.4 0.1 stack.34.parts_ref
  21.5 5.5 %prefetch.3 = (bf16[768,2048]{1,0:T(8,128)(2,1)S(1)}, bf16[768,2048]{1,0:T(8,128)(2,1)S(1)}, bf16[768,2048]{1,0:T(8,128)(2,1)S(1)}, bf16[768,2048]{1,0:T(8,128)(2,1)S(1)}) custom-call(s32[5]{0:T(128)S(1)} %stack.34.parts_ref, bf16[64,1536]{1,0:T(8,128)(2,1)S(1)} %get-tuple-element.49.after_ref.refs_1_, bf16[1,3072,2048]{2,1,0:T(8,128)(2,1)} %refs_2_.3, ...), custom_call_target="tpu_custom_call" | custom-call | bytes 12582912 | tf_op jit(solution)/shard_map/prefetch/pallas_call | solution.py:129
  27.0 1.5 %dispatch.3 = (bf16[64,1536]{1,0:T(8,128)(2,1)S(1)}, bf16[64,1536]{1,0:T(8,128)(2,1)S(1)}, bf16[64,1536]{1,0:T(8,128)(2,1)S(1)}, bf16[64,1536]{1,0:T(8,128)(2,1)S(1)}) custom-call(bf16[256,128]{1,0:T(8,128)(2,1)S(1)} %get-tuple-element.47.after_ref.placed_ref, bf16[128,768]{1,0:T(8,128)(2,1)} %collective-permute-done.refs_0_, ...), custom_call_target="tpu_custom_call" | custom-call | flops 100663296 | bytes 1179648 | tf_op jit(solution)/shard_map/dispatch/pallas_call | solution.py:88
  28.6 0.3 collective-permute-start.3
  28.9 1.7 %collective-permute-start.4 = (bf16[64,1536]{1,0:T(8,128)(2,1)S(1)}, bf16[64,1536]{1,0:T(8,128)(2,1)S(1)}, u32[]{:S(2)}, u32[]{:S(2)}) collective-permute-start(bf16[64,1536]{1,0:T(8,128)(2,1)S(1)} %get-tuple-element.53), channel_id=1, source_target_pairs={{0,2},{1,3},{2,0},{3,1},{4,6},{5,7},{6,4},{7,5},{8,10},{9,11},{10,... | collective-permute-start | bytes 589832 | tf_op jit(solution)/shard_map/ppermute | solution.py:318
  30.6 0.4 collective-permute-done.8.refs_4_
  31.0 5.7 %gate_up.2 = (f32[256,2048]{1,0:T(8,128)S(1)}, f32[256,2048]{1,0:T(8,128)S(1)}, bf16[2048,3072]{1,0:T(8,128)(2,1)S(1)}) custom-call(s32[2]{0:T(128)S(1)} %broadcast_1_refs_0_.2.refs_0_, bf16[64,1536]{1,0:T(8,128)(2,1)S(1)} %get-tuple-element.49.after_ref.refs_1_, bf16[64,1536]{1,0:T(8,128)(2,1)} %collective-permute-done.6.refs_2_, ...), custom_call_target="tpu_custom_call" | custom-call | flops 3221225472 | bytes 12582912 | tf_op jit(solution)/shard_map/gate_up/pallas_call | solution.py:198
  36.8 2.7 %collective-permute-done.5.refs_4_ = bf16[64,1536]{1,0:T(8,128)(2,1)S(1)} collective-permute-done((bf16[64,1536]{1,0:T(8,128)(2,1)S(1)}, bf16[64,1536]{1,0:T(8,128)(2,1)S(1)}, u32[]{:S(2)}, u32[]{:S(2)}) %collective-permute-start.5) | collective-permute-done | bytes 196640 | tf_op jit(solution)/shard_map/ppermute | solution.py:318
  39.4 4.2 %gate_up.3.h_ref = bf16[256,2048]{1,0:T(8,128)(2,1)S(1)} custom-call(s32[1]{0:T(128)} %constant.14.clone.1.refs_0_, bf16[64,1536]{1,0:T(8,128)(2,1)S(1)} %get-tuple-element.51.refs_1_, bf16[64,1536]{1,0:T(8,128)(2,1)S(1)} %collective-permute-done.3.refs_2_, bf16[64,1536]{1,0:T(8,128)(2,1)S(1)} %collective-permute-done.4.refs_3_, ...), custom_call_target="tpu_custom_call" | custom-call | flops 3221225472 | bytes 12582912 | tf_op jit(solution)/shard_map/gate_up/pallas_call | solution.py:198
  43.6 1.0 %down.2 = (bf16[64,768]{1,0:T(8,128)(2,1)S(1)}, bf16[64,768]{1,0:T(8,128)(2,1)S(1)}, bf16[64,768]{1,0:T(8,128)(2,1)S(1)}, bf16[64,768]{1,0:T(8,128)(2,1)S(1)}) custom-call(s32[1]{0:T(128)} %bitcast.5.parts_ref, bf16[256,2048]{1,0:T(8,128)(2,1)S(1)} %gate_up.3.h_ref, bf16[2048,3072]{1,0:T(8,128)(2,1)S(1)} %get-tuple-element.66.w_ref), custom_call_target="tpu_custom_call" | custom-call | flops 805306368 | bytes 3538944 | tf_op jit(solution)/shard_map/down/pallas_call | solution.py:246
  44.7 0.6 collective-permute-start.9
  45.3 0.1 pad_add_fusion.parts_ref
  45.4 1.7 %collective-permute-start.10 = (bf16[64,768]{1,0:T(8,128)(2,1)S(1)}, bf16[64,768]{1,0:T(8,128)(2,1)S(1)}, u32[]{:S(2)}, u32[]{:S(2)}) collective-permute-start(bf16[64,768]{1,0:T(8,128)(2,1)S(1)} %get-tuple-element.73), channel_id=1, source_target_pairs={{0,2},{1,3},{2,0},{3,1},{4,6},{5,7},{6,4},{7,5},{8,10},{9,11},{10,... | collective-permute-start | bytes 294920 | tf_op jit(solution)/shard_map/ppermute | solution.py:318
  47.1 3.2 %down.3 = (bf16[64,768]{1,0:T(8,128)(2,1)S(1)}, bf16[64,768]{1,0:T(8,128)(2,1)S(1)}, bf16[64,768]{1,0:T(8,128)(2,1)S(1)}, bf16[64,768]{1,0:T(8,128)(2,1)S(1)}, b...) custom-call(s32[3]{0:T(128)S(1)} %pad_add_fusion.parts_ref, ...), custom_call_target="tpu_custom_call" | custom-call | flops 2415919104 | bytes 10616832 | tf_op jit(solution)/shard_map/down/pallas_call | solution.py:246
  50.3 0.5 collective-permute-start.20
  50.8 1.7 %collective-permute-start.21 = (bf16[64,768]{1,0:T(8,128)(2,1)S(1)}, bf16[64,768]{1,0:T(8,128)(2,1)S(1)}, u32[]{:S(2)}, u32[]{:S(2)}) collective-permute-start(bf16[64,768]{1,0:T(8,128)(2,1)S(1)} %get-tuple-element.85), channel_id=1, source_target_pairs={{0,2},{1,3},{2,0},{3,1},{4,6},{5,7},{6,4},{7,5},{8,10},{9,11},{10,... | collective-permute-start | bytes 294920 | tf_op jit(solution)/shard_map/ppermute | solution.py:318
  52.5 0.1 copy.10.logits_ref
  52.6 0.5 collective-permute-start.16
  53.1 1.7 %collective-permute-start.17 = (bf16[64,768]{1,0:T(8,128)(2,1)S(1)}, bf16[64,768]{1,0:T(8,128)(2,1)S(1)}, u32[]{:S(2)}, u32[]{:S(2)}) collective-permute-start(bf16[64,768]{1,0:T(8,128)(2,1)S(1)} %get-tuple-element.81), channel_id=1, source_target_pairs={{0,2},{1,3},{2,0},{3,1},{4,6},{5,7},{6,4},{7,5},{8,10},{9,11},{10,... | collective-permute-start | bytes 294920 | tf_op jit(solution)/shard_map/ppermute | solution.py:318
  54.9 0.3 combine.4
  55.2 0.5 collective-permute-done.21.refs_2_
  55.7 4.0 %collective-permute-start.12 = (bf16[128,768]{1,0:T(8,128)(2,1)S(1)}, bf16[128,768]{1,0:T(8,128)(2,1)S(1)}, u32[]{:S(2)}, u32[]{:S(2)}) collective-permute-start(bf16[128,768]{1,0:T(8,128)(2,1)S(1)} %combine.4), channel_id=1, source_target_pairs={{0,12},{4,8},{8,4},{12,0},{1,13},{5,9},{9,5},{13,1},{2,14},{6,10},... | collective-permute-start | bytes 589832 | tf_op jit(solution)/shard_map/ppermute | solution.py:318
  59.7 0.3 combine.6
  60.0 0.1 collective-permute-start.23
  60.1 1.7 %collective-permute-done.18.refs_3_ = bf16[64,768]{1,0:T(8,128)(2,1)S(1)} collective-permute-done((bf16[64,768]{1,0:T(8,128)(2,1)S(1)}, bf16[64,768]{1,0:T(8,128)(2,1)S(1)}, u32[]{:S(2)}, u32[]{:S(2)}) %collective-permute-start.18) | collective-permute-done | bytes 98336 | tf_op jit(solution)/shard_map/ppermute | solution.py:318
  61.8 0.3 combine.5
  62.2 1.7 %collective-permute-start.19 = (bf16[128,768]{1,0:T(8,128)(2,1)S(1)}, bf16[128,768]{1,0:T(8,128)(2,1)S(1)}, u32[]{:S(2)}, u32[]{:S(2)}) collective-permute-start(bf16[128,768]{1,0:T(8,128)(2,1)S(1)} %combine.5), channel_id=1, source_target_pairs={{0,8},{4,12},{8,0},{12,4},{1,9},{5,13},{9,1},{13,5},{2,10},{6,14},... | collective-permute-start | bytes 589832 | tf_op jit(solution)/shard_map/ppermute | solution.py:318
  63.9 1.6 %collective-permute-done.12.refs_4_ = bf16[128,768]{1,0:T(8,128)(2,1)S(1)} collective-permute-done((bf16[128,768]{1,0:T(8,128)(2,1)S(1)}, bf16[128,768]{1,0:T(8,128)(2,1)S(1)}, u32[]{:S(2)}, u32[]{:S(2)}) %collective-permute-start.12) | collective-permute-done | bytes 196640 | tf_op jit(solution)/shard_map/ppermute | solution.py:318
  65.5 0.1 collective-permute-start.13
  65.6 1.8 %collective-permute-start.14 = (bf16[64,768]{1,0:T(8,128)(2,1)S(1)}, bf16[64,768]{1,0:T(8,128)(2,1)S(1)}, u32[]{:S(2)}, u32[]{:S(2)}) collective-permute-start(bf16[64,768]{1,0:T(8,128)(2,1)S(1)} %get-tuple-element.77), channel_id=1, source_target_pairs={{0,2},{1,3},{2,0},{3,1},{4,6},{5,7},{6,4},{7,5},{8,10},{9,11},{10,... | collective-permute-start | bytes 294920 | tf_op jit(solution)/shard_map/ppermute | solution.py:318
  67.4 0.1 collective-permute-start.15
  67.4 3.3 %collective-permute-done.23.refs_6_ = bf16[128,768]{1,0:T(8,128)(2,1)S(1)} collective-permute-done((bf16[128,768]{1,0:T(8,128)(2,1)S(1)}, bf16[128,768]{1,0:T(8,128)(2,1)S(1)}, u32[]{:S(2)}, u32[]{:S(2)}) %collective-permute-start.23) | collective-permute-done | bytes 196640 | tf_op jit(solution)/shard_map/ppermute | solution.py:318
  70.7 4.7 %collective-permute-done.19.refs_5_ = bf16[128,768]{1,0:T(8,128)(2,1)S(1)} collective-permute-done((bf16[128,768]{1,0:T(8,128)(2,1)S(1)}, bf16[128,768]{1,0:T(8,128)(2,1)S(1)}, u32[]{:S(2)}, u32[]{:S(2)}) %collective-permute-start.19) | collective-permute-done | bytes 196640 | tf_op jit(solution)/shard_map/ppermute | solution.py:318
  75.5 1.0 %combine.7 = bf16[128,768]{1,0:T(8,128)(2,1)} custom-call(bf16[256,256]{1,0:T(8,128)(2,1)S(1)} %get-tuple-element.46.pick_ref, f32[128,2]{1,0:T(8,128)S(1)} %copy.10.logits_ref, bf16[64,768]{1,0:T(8,128)(2,1)S(1)} %get-tuple-element.75.refs_0_, bf16[64,768]{1,0:T(8,128)(2,1)S(1)} %collective-permute-done.13.refs_1_, ...), custom_call_target="tpu_custom_call" | custom-call | flops 100663296 | bytes 589824 | tf_op jit(solution)/shard_map/combine/pallas_call | solution.py:301
  (41 shorter events, 0.1 us)
Async XLA Ops:
  0.0 16.8 %collective-permute-start.2 = (bf16[128,768]{1,0:T(8,128)(2,1)}, bf16[128,768]{1,0:T(8,128)(2,1)S(1)}, u32[]{:S(2)}, u32[]{:S(2)}) collective-permute-start(bf16[128,768]{1,0:T(8,128)(2,1)} %refs_0_.4), channel_id=1, source_target_pairs={{0,4},{4,0},{8,12},{12,8},{1,5},{5,1},{9,13},{13,9},{2,6},{6,2},{1... | collective-permute-start | bytes 589832 | tf_op jit(solution)/shard_map/ppermute | solution.py:318
  3.0 24.0 %collective-permute-start = (bf16[128,768]{1,0:T(8,128)(2,1)}, bf16[128,768]{1,0:T(8,128)(2,1)}, u32[]{:S(2)}, u32[]{:S(2)}) collective-permute-start(bf16[128,768]{1,0:T(8,128)(2,1)} %refs_0_.4), channel_id=1, source_target_pairs={{0,8},{4,12},{8,0},{12,4},{1,9},{5,13},{9,1},{13,5},{2,10},{6,14},... | collective-permute-start | bytes 589832 | tf_op jit(solution)/shard_map/ppermute | solution.py:318
  5.6 21.4 %collective-permute-start.1 = (bf16[128,768]{1,0:T(8,128)(2,1)}, bf16[128,768]{1,0:T(8,128)(2,1)}, u32[]{:S(2)}, u32[]{:S(2)}) collective-permute-start(bf16[128,768]{1,0:T(8,128)(2,1)} %refs_0_.4), channel_id=1, source_target_pairs={{0,12},{4,8},{8,4},{12,0},{1,13},{5,9},{9,5},{13,1},{2,14},{6,10},... | collective-permute-start | bytes 589832 | tf_op jit(solution)/shard_map/ppermute | solution.py:318
  5.6 0.7 copy-start.9
  6.6 11.0 %copy-start.6 = (bf16[128,768]{1,0:T(8,128)(2,1)S(1)}, bf16[128,768]{1,0:T(8,128)(2,1)}, u32[]{:S(2)}) copy-start(bf16[128,768]{1,0:T(8,128)(2,1)} %refs_0_.4) | copy-start | bytes 589828
  11.8 1.6 %copy-start = (bf16[768,2048]{1,0:T(8,128)(2,1)}, bf16[768,2048]{1,0:T(8,128)(2,1)S(1)}, u32[]{:S(2)}) copy-start(bf16[768,2048]{1,0:T(8,128)(2,1)S(1)} %get-tuple-element.61.refs_6_) | copy-start | bytes 9437188
  13.4 1.7 %copy-start.2 = (bf16[768,2048]{1,0:T(8,128)(2,1)}, bf16[768,2048]{1,0:T(8,128)(2,1)S(1)}, u32[]{:S(2)}) copy-start(bf16[768,2048]{1,0:T(8,128)(2,1)S(1)} %get-tuple-element.62.refs_7_) | copy-start | bytes 9437188
  15.1 1.7 %copy-start.4 = (bf16[768,2048]{1,0:T(8,128)(2,1)}, bf16[768,2048]{1,0:T(8,128)(2,1)S(1)}, u32[]{:S(2)}) copy-start(bf16[768,2048]{1,0:T(8,128)(2,1)S(1)} %get-tuple-element.63.refs_8_) | copy-start | bytes 9437188
  16.8 0.7 copy-start.7
  17.5 0.9 %copy-start.8 = (bf16[128,768]{1,0:T(8,128)(2,1)S(1)}, bf16[128,768]{1,0:T(8,128)(2,1)}, u32[]{:S(2)}) copy-start(bf16[128,768]{1,0:T(8,128)(2,1)} %copy-done.7) | copy-start | bytes 589828
  19.6 11.1 %collective-permute-start.6 = (bf16[64,1536]{1,0:T(8,128)(2,1)}, bf16[64,1536]{1,0:T(8,128)(2,1)}, u32[]{:S(2)}, u32[]{:S(2)}) collective-permute-start(bf16[64,1536]{1,0:T(8,128)(2,1)} %get-tuple-element.58), channel_id=1, source_target_pairs={{0,1},{1,0},{2,3},{3,2},{4,5},{5,4},{6,7},{7,6},{8,9},{9,8},{10,11... | collective-permute-start | bytes 589832 | tf_op jit(solution)/shard_map/ppermute | solution.py:318
  19.6 11.1 %collective-permute-start.7 = (bf16[64,1536]{1,0:T(8,128)(2,1)}, bf16[64,1536]{1,0:T(8,128)(2,1)}, u32[]{:S(2)}, u32[]{:S(2)}) collective-permute-start(bf16[64,1536]{1,0:T(8,128)(2,1)} %get-tuple-element.59), channel_id=1, source_target_pairs={{0,2},{1,3},{2,0},{3,1},{4,6},{5,7},{6,4},{7,5},{8,10},{9,11},{10,... | collective-permute-start | bytes 589832 | tf_op jit(solution)/shard_map/ppermute | solution.py:318
  21.3 9.7 %collective-permute-start.8 = (bf16[64,1536]{1,0:T(8,128)(2,1)}, bf16[64,1536]{1,0:T(8,128)(2,1)}, u32[]{:S(2)}, u32[]{:S(2)}) collective-permute-start(bf16[64,1536]{1,0:T(8,128)(2,1)} %get-tuple-element.60), channel_id=1, source_target_pairs={{0,3},{1,2},{2,1},{3,0},{4,7},{5,6},{6,5},{7,4},{8,11},{9,10},{10,... | collective-permute-start | bytes 589832 | tf_op jit(solution)/shard_map/ppermute | solution.py:318
  21.5 9.5 %copy-start.3 = (bf16[768,2048]{1,0:T(8,128)(2,1)S(1)}, bf16[768,2048]{1,0:T(8,128)(2,1)}, u32[]{:S(2)}) copy-start(bf16[768,2048]{1,0:T(8,128)(2,1)} %copy-done.2) | copy-start | bytes 9437188
  21.5 9.5 %copy-start.5 = (bf16[768,2048]{1,0:T(8,128)(2,1)S(1)}, bf16[768,2048]{1,0:T(8,128)(2,1)}, u32[]{:S(2)}) copy-start(bf16[768,2048]{1,0:T(8,128)(2,1)} %copy-done.4) | copy-start | bytes 9437188
  27.0 4.0 %copy-start.1 = (bf16[768,2048]{1,0:T(8,128)(2,1)S(1)}, bf16[768,2048]{1,0:T(8,128)(2,1)}, u32[]{:S(2)}) copy-start(bf16[768,2048]{1,0:T(8,128)(2,1)} %copy-done) | copy-start | bytes 9437188
  28.6 8.2 %collective-permute-start.3 = (bf16[64,1536]{1,0:T(8,128)(2,1)S(1)}, bf16[64,1536]{1,0:T(8,128)(2,1)S(1)}, u32[]{:S(2)}, u32[]{:S(2)}) collective-permute-start(bf16[64,1536]{1,0:T(8,128)(2,1)S(1)} %get-tuple-element.52), channel_id=1, source_target_pairs={{0,1},{1,0},{2,3},{3,2},{4,5},{5,4},{6,7},{7,6},{8,9},{9,8},{10,11... | collective-permute-start | bytes 589832 | tf_op jit(solution)/shard_map/ppermute | solution.py:318
  28.9 7.9 %collective-permute-start.4 = (bf16[64,1536]{1,0:T(8,128)(2,1)S(1)}, bf16[64,1536]{1,0:T(8,128)(2,1)S(1)}, u32[]{:S(2)}, u32[]{:S(2)}) collective-permute-start(bf16[64,1536]{1,0:T(8,128)(2,1)S(1)} %get-tuple-element.53), channel_id=1, source_target_pairs={{0,2},{1,3},{2,0},{3,1},{4,6},{5,7},{6,4},{7,5},{8,10},{9,11},{10,... | collective-permute-start | bytes 589832 | tf_op jit(solution)/shard_map/ppermute | solution.py:318
  30.6 8.8 %collective-permute-start.5 = (bf16[64,1536]{1,0:T(8,128)(2,1)S(1)}, bf16[64,1536]{1,0:T(8,128)(2,1)S(1)}, u32[]{:S(2)}, u32[]{:S(2)}) collective-permute-start(bf16[64,1536]{1,0:T(8,128)(2,1)S(1)} %get-tuple-element.54), channel_id=1, source_target_pairs={{0,3},{1,2},{2,1},{3,0},{4,7},{5,6},{6,5},{7,4},{8,11},{9,10},{10,... | collective-permute-start | bytes 589832 | tf_op jit(solution)/shard_map/ppermute | solution.py:318
  44.7 2.4 %collective-permute-start.9 = (bf16[64,768]{1,0:T(8,128)(2,1)S(1)}, bf16[64,768]{1,0:T(8,128)(2,1)S(1)}, u32[]{:S(2)}, u32[]{:S(2)}) collective-permute-start(bf16[64,768]{1,0:T(8,128)(2,1)S(1)} %get-tuple-element.67), channel_id=1, source_target_pairs={{0,1},{1,0},{2,3},{3,2},{4,5},{5,4},{6,7},{7,6},{8,9},{9,8},{10,11... | collective-permute-start | bytes 294920 | tf_op jit(solution)/shard_map/ppermute | solution.py:318
  45.4 7.3 %collective-permute-start.10 = (bf16[64,768]{1,0:T(8,128)(2,1)S(1)}, bf16[64,768]{1,0:T(8,128)(2,1)S(1)}, u32[]{:S(2)}, u32[]{:S(2)}) collective-permute-start(bf16[64,768]{1,0:T(8,128)(2,1)S(1)} %get-tuple-element.73), channel_id=1, source_target_pairs={{0,2},{1,3},{2,0},{3,1},{4,6},{5,7},{6,4},{7,5},{8,10},{9,11},{10,... | collective-permute-start | bytes 294920 | tf_op jit(solution)/shard_map/ppermute | solution.py:318
  47.1 5.5 %copy-start.10 = (f32[128,2]{0,1:T(2,128)S(1)}, f32[128,2]{0,1:T(2,128)}, u32[]{:S(2)}) copy-start(f32[128,2]{0,1:T(2,128)} %param.8) | copy-start | bytes 3076
  47.1 6.1 %collective-permute-start.11 = (bf16[64,768]{1,0:T(8,128)(2,1)S(1)}, bf16[64,768]{1,0:T(8,128)(2,1)S(1)}, u32[]{:S(2)}, u32[]{:S(2)}) collective-permute-start(bf16[64,768]{1,0:T(8,128)(2,1)S(1)} %get-tuple-element.74), channel_id=1, source_target_pairs={{0,3},{1,2},{2,1},{3,0},{4,7},{5,6},{6,5},{7,4},{8,11},{9,10},{10,... | collective-permute-start | bytes 294920 | tf_op jit(solution)/shard_map/ppermute | solution.py:318
  50.3 4.5 %collective-permute-start.20 = (bf16[64,768]{1,0:T(8,128)(2,1)S(1)}, bf16[64,768]{1,0:T(8,128)(2,1)S(1)}, u32[]{:S(2)}, u32[]{:S(2)}) collective-permute-start(bf16[64,768]{1,0:T(8,128)(2,1)S(1)} %get-tuple-element.84), channel_id=1, source_target_pairs={{0,1},{1,0},{2,3},{3,2},{4,5},{5,4},{6,7},{7,6},{8,9},{9,8},{10,11... | collective-permute-start | bytes 294920 | tf_op jit(solution)/shard_map/ppermute | solution.py:318
  50.8 4.9 %collective-permute-start.21 = (bf16[64,768]{1,0:T(8,128)(2,1)S(1)}, bf16[64,768]{1,0:T(8,128)(2,1)S(1)}, u32[]{:S(2)}, u32[]{:S(2)}) collective-permute-start(bf16[64,768]{1,0:T(8,128)(2,1)S(1)} %get-tuple-element.85), channel_id=1, source_target_pairs={{0,2},{1,3},{2,0},{3,1},{4,6},{5,7},{6,4},{7,5},{8,10},{9,11},{10,... | collective-permute-start | bytes 294920 | tf_op jit(solution)/shard_map/ppermute | solution.py:318
  52.5 7.2 %collective-permute-start.22 = (bf16[64,768]{1,0:T(8,128)(2,1)S(1)}, bf16[64,768]{1,0:T(8,128)(2,1)S(1)}, u32[]{:S(2)}, u32[]{:S(2)}) collective-permute-start(bf16[64,768]{1,0:T(8,128)(2,1)S(1)} %get-tuple-element.86), channel_id=1, source_target_pairs={{0,3},{1,2},{2,1},{3,0},{4,7},{5,6},{6,5},{7,4},{8,11},{9,10},{10,... | collective-permute-start | bytes 294920 | tf_op jit(solution)/shard_map/ppermute | solution.py:318
  52.6 7.5 %collective-permute-start.16 = (bf16[64,768]{1,0:T(8,128)(2,1)S(1)}, bf16[64,768]{1,0:T(8,128)(2,1)S(1)}, u32[]{:S(2)}, u32[]{:S(2)}) collective-permute-start(bf16[64,768]{1,0:T(8,128)(2,1)S(1)} %get-tuple-element.80), channel_id=1, source_target_pairs={{0,1},{1,0},{2,3},{3,2},{4,5},{5,4},{6,7},{7,6},{8,9},{9,8},{10,11... | collective-permute-start | bytes 294920 | tf_op jit(solution)/shard_map/ppermute | solution.py:318
  53.1 7.0 %collective-permute-start.17 = (bf16[64,768]{1,0:T(8,128)(2,1)S(1)}, bf16[64,768]{1,0:T(8,128)(2,1)S(1)}, u32[]{:S(2)}, u32[]{:S(2)}) collective-permute-start(bf16[64,768]{1,0:T(8,128)(2,1)S(1)} %get-tuple-element.81), channel_id=1, source_target_pairs={{0,2},{1,3},{2,0},{3,1},{4,6},{5,7},{6,4},{7,5},{8,10},{9,11},{10,... | collective-permute-start | bytes 294920 | tf_op jit(solution)/shard_map/ppermute | solution.py:318
  54.9 7.0 %collective-permute-start.18 = (bf16[64,768]{1,0:T(8,128)(2,1)S(1)}, bf16[64,768]{1,0:T(8,128)(2,1)S(1)}, u32[]{:S(2)}, u32[]{:S(2)}) collective-permute-start(bf16[64,768]{1,0:T(8,128)(2,1)S(1)} %get-tuple-element.82), channel_id=1, source_target_pairs={{0,3},{1,2},{2,1},{3,0},{4,7},{5,6},{6,5},{7,4},{8,11},{9,10},{10,... | collective-permute-start | bytes 294920 | tf_op jit(solution)/shard_map/ppermute | solution.py:318
  55.7 9.8 %collective-permute-start.12 = (bf16[128,768]{1,0:T(8,128)(2,1)S(1)}, bf16[128,768]{1,0:T(8,128)(2,1)S(1)}, u32[]{:S(2)}, u32[]{:S(2)}) collective-permute-start(bf16[128,768]{1,0:T(8,128)(2,1)S(1)} %combine.4), channel_id=1, source_target_pairs={{0,12},{4,8},{8,4},{12,0},{1,13},{5,9},{9,5},{13,1},{2,14},{6,10},... | collective-permute-start | bytes 589832 | tf_op jit(solution)/shard_map/ppermute | solution.py:318
  60.0 10.7 %collective-permute-start.23 = (bf16[128,768]{1,0:T(8,128)(2,1)S(1)}, bf16[128,768]{1,0:T(8,128)(2,1)S(1)}, u32[]{:S(2)}, u32[]{:S(2)}) collective-permute-start(bf16[128,768]{1,0:T(8,128)(2,1)S(1)} %combine.6), channel_id=1, source_target_pairs={{0,4},{4,0},{8,12},{12,8},{1,5},{5,1},{9,13},{13,9},{2,6},{6,2},{1... | collective-permute-start | bytes 589832 | tf_op jit(solution)/shard_map/ppermute | solution.py:318
  62.2 13.3 %collective-permute-start.19 = (bf16[128,768]{1,0:T(8,128)(2,1)S(1)}, bf16[128,768]{1,0:T(8,128)(2,1)S(1)}, u32[]{:S(2)}, u32[]{:S(2)}) collective-permute-start(bf16[128,768]{1,0:T(8,128)(2,1)S(1)} %combine.5), channel_id=1, source_target_pairs={{0,8},{4,12},{8,0},{12,4},{1,9},{5,13},{9,1},{13,5},{2,10},{6,14},... | collective-permute-start | bytes 589832 | tf_op jit(solution)/shard_map/ppermute | solution.py:318
  65.5 10.0 %collective-permute-start.13 = (bf16[64,768]{1,0:T(8,128)(2,1)S(1)}, bf16[64,768]{1,0:T(8,128)(2,1)S(1)}, u32[]{:S(2)}, u32[]{:S(2)}) collective-permute-start(bf16[64,768]{1,0:T(8,128)(2,1)S(1)} %get-tuple-element.76), channel_id=1, source_target_pairs={{0,1},{1,0},{2,3},{3,2},{4,5},{5,4},{6,7},{7,6},{8,9},{9,8},{10,11... | collective-permute-start | bytes 294920 | tf_op jit(solution)/shard_map/ppermute | solution.py:318
  65.6 9.9 %collective-permute-start.14 = (bf16[64,768]{1,0:T(8,128)(2,1)S(1)}, bf16[64,768]{1,0:T(8,128)(2,1)S(1)}, u32[]{:S(2)}, u32[]{:S(2)}) collective-permute-start(bf16[64,768]{1,0:T(8,128)(2,1)S(1)} %get-tuple-element.77), channel_id=1, source_target_pairs={{0,2},{1,3},{2,0},{3,1},{4,6},{5,7},{6,4},{7,5},{8,10},{9,11},{10,... | collective-permute-start | bytes 294920 | tf_op jit(solution)/shard_map/ppermute | solution.py:318
  67.4 8.1 %collective-permute-start.15 = (bf16[64,768]{1,0:T(8,128)(2,1)S(1)}, bf16[64,768]{1,0:T(8,128)(2,1)S(1)}, u32[]{:S(2)}, u32[]{:S(2)}) collective-permute-start(bf16[64,768]{1,0:T(8,128)(2,1)S(1)} %get-tuple-element.78), channel_id=1, source_target_pairs={{0,3},{1,2},{2,1},{3,0},{4,7},{5,6},{6,5},{7,4},{8,11},{9,10},{10,... | collective-permute-start | bytes 294920 | tf_op jit(solution)/shard_map/ppermute | solution.py:318

commit v6 on v4

v6 whole, which is shorter than its diff:
```python
import functools

import jax
import jax.numpy as jnp
from jax import lax
from jax.experimental import pallas as pl
from jax.experimental.pallas import tpu as pltpu
from jax.sharding import PartitionSpec as P

F32 = jnp.float32
BF16 = jnp.bfloat16
MIB = 1024 * 1024


def params(mib=6):
    return pltpu.CompilerParams(vmem_limit_bytes=mib * MIB)


def cost(flops, moved):
    return pl.CostEstimate(flops=flops, bytes_accessed=moved, transcendentals=0)


def pinned(arrays):
    return [pltpu.with_memory_space_constraint(array, pltpu.VMEM) for array in arrays]


def routing_kernel(where_ref, ids_ref, logits_ref, placed_ref, pick_ref, mix_ref, *, experts):
    rows = ids_ref.shape[1]
    capacity = placed_ref.shape[0] // experts
    relative = lax.bitwise_xor(ids_ref[...], where_ref[0])
    lane = lax.broadcasted_iota(jnp.int32, (experts, rows), 0)
    names = [lane == relative[k : k + 1] for k in range(2)]
    named = names[0] | names[1]
    row = lax.broadcasted_iota(jnp.int32, (rows, rows), 0)
    column = lax.broadcasted_iota(jnp.int32, (rows, rows), 1)
    before = jnp.dot(
        jnp.where(named, 1.0, 0.0).astype(BF16),
        jnp.where(row < column, 1.0, 0.0).astype(BF16),
        preferred_element_type=F32,
    ).astype(jnp.int32)
    slot = lax.broadcasted_iota(jnp.int32, (capacity, rows), 0)
    for d in range(experts):
        here = slice(d * capacity, (d + 1) * capacity)
        both = None
        for k in range(2):
            position = jnp.where(names[k], before, -1)
            hit = jnp.where(position[d : d + 1] == slot, 1.0, 0.0)
            pick_ref[here, k * rows : (k + 1) * rows] = hit.astype(BF16)
            both = hit if k == 0 else both + hit
        placed_ref[here, :] = both.astype(BF16)
    share = 1.0 / (1.0 + jnp.exp(logits_ref[1:2] - logits_ref[0:1]))
    share = jnp.sum(jnp.where(row == column, share, 0.0), axis=1, keepdims=True)
    mix_ref[:, 0:1] = share
    mix_ref[:, 1:2] = 1.0 - share


def place(where, expert_ids, route_logits, experts, capacity):
    rows = expert_ids.shape[0]
    return pl.pallas_call(
        functools.partial(routing_kernel, experts=experts),
        out_shape=[
            jax.ShapeDtypeStruct((experts * capacity, rows), BF16),
            jax.ShapeDtypeStruct((experts * capacity, 2 * rows), BF16),
            jax.ShapeDtypeStruct((rows, 2), F32),
        ],
        in_specs=[pl.BlockSpec(memory_space=pltpu.SMEM)]
        + [pl.BlockSpec(memory_space=pltpu.VMEM)] * 2,
        out_specs=[pl.BlockSpec(memory_space=pltpu.VMEM)] * 3,
        compiler_params=params(),
        name="routing",
    )(where, expert_ids.T, route_logits.T)


def dispatch_kernel(placed_ref, *refs, count, waits):
    refs = refs[:count] + refs[count + waits :]
    capacity, wide = refs[count].shape
    width = wide // count
    for i in range(count):
        block = refs[i][...]
        for d, out in enumerate(refs[count:]):
            out[:, i * width : (i + 1) * width] = jnp.dot(
                placed_ref[d * capacity : (d + 1) * capacity, :],
                block,
                preferred_element_type=F32,
            ).astype(BF16)


def dispatch(placed, blocks, experts, capacity, after):
    rows, width = blocks[0].shape
    wide = width * len(blocks)
    return pl.pallas_call(
        functools.partial(dispatch_kernel, count=len(blocks), waits=len(after)),
        out_shape=[jax.ShapeDtypeStruct((capacity, wide), BF16)] * experts,
        in_specs=[pl.BlockSpec(memory_space=pltpu.VMEM)] * (1 + len(blocks))
        + [pl.BlockSpec(memory_space=pl.ANY)] * len(after),
        out_specs=[pl.BlockSpec(memory_space=pltpu.VMEM)] * experts,
        cost_estimate=cost(2 * experts * capacity * rows * wide, 6 * rows * wide),
        compiler_params=params(),
        name="dispatch",
    )(placed, *blocks, *pinned(after))


def part_of(where_ref, distance):
    return 0 if distance is None else lax.bitwise_xor(where_ref[1], distance)


def prefetch_kernel(where_ref, after_ref, *refs, distances):
    half = len(refs) // 2
    copies = []
    for i, distance in enumerate(distances):
        source, target, sem = refs[i], refs[half + i], refs[-1].at[i]
        count = target.shape[0]
        start = pl.multiple_of(part_of(where_ref, distance) * count, count)
        copies.append(pltpu.make_async_copy(source.at[0, pl.ds(start, count)], target, sem))
    for copy in copies:
        copy.start()
    for copy in copies:
        copy.wait()


def prefetch(where, fetches, after):
    sources = [pltpu.with_memory_space_constraint(w, pltpu.HBM) for w, _, _ in fetches]
    shapes = [pltpu.VMEM((count, w.shape[2]), w.dtype) for w, _, count in fetches]
    return pl.pallas_call(
        functools.partial(prefetch_kernel, distances=[d for _, d, _ in fetches]),
        out_shape=shapes,
        in_specs=[pl.BlockSpec(memory_space=pltpu.SMEM)]
        + [pl.BlockSpec(memory_space=pl.ANY)] * (1 + len(sources)),
        out_specs=[pl.BlockSpec(memory_space=pltpu.VMEM)] * len(shapes),
        scratch_shapes=[pltpu.SemaphoreType.DMA((len(shapes),))],
        cost_estimate=cost(0, sum(2 * count * w.shape[2] for w, _, count in fetches)),
        compiler_params=params(),
        name="prefetch",
    )(where, after, *sources)


def gate_up_kernel(*refs, experts, slices, first, last):
    x_refs = refs[:experts]
    weights = refs[experts : experts + 2 * slices]
    rest = refs[experts + 2 * slices :]
    if not first:
        old_gate, old_up = rest[:2]
        rest = rest[2:]
    x = jnp.concatenate([r[...] for r in x_refs], axis=0)
    width, hidden = weights[0].shape
    tile = min(512, hidden)
    for n in range(hidden // tile):
        columns = slice(n * tile, (n + 1) * tile)
        sums = []
        for kind in range(2):
            total = None if first else (old_gate, old_up)[kind][:, columns]
            for i in range(slices):
                term = jnp.dot(
                    x[:, i * width : (i + 1) * width],
                    weights[2 * i + kind][:, columns],
                    preferred_element_type=F32,
                )
                total = term if total is None else total + term
            sums.append(total)
        gate, up = sums
        if last:
            rest[0][:, columns] = (gate / (1.0 + jnp.exp(-gate)) * up).astype(BF16)
        else:
            rest[0][:, columns] = gate
            rest[1][:, columns] = up


def gate_up(x_blocks, weights, sums, last):
    experts = len(x_blocks)
    rows = experts * x_blocks[0].shape[0]
    hidden = weights[0].shape[1]
    first = sums is None
    old = [] if first else pinned(sums)
    before = experts + len(weights)
    if last:
        out_shape = [pltpu.VMEM((rows, hidden), BF16)]
    else:
        out_shape = [pltpu.VMEM((rows, hidden), F32)] * 2
    return pl.pallas_call(
        functools.partial(
            gate_up_kernel, experts=experts, slices=len(weights) // 2, first=first, last=last
        ),
        out_shape=out_shape,
        in_specs=[pl.BlockSpec(memory_space=pltpu.VMEM)] * (before + len(old)),
        out_specs=[pl.BlockSpec(memory_space=pltpu.VMEM)] * len(out_shape),
        input_output_aliases={} if first or last else {before: 0, before + 1: 1},
        cost_estimate=cost(
            2 * rows * hidden * sum(w.shape[0] for w in weights),
            sum(2 * w.size for w in weights),
        ),
        compiler_params=params(),
        name="gate_up",
    )(*x_blocks, *pinned(weights), *old)


def down_kernel(where_ref, h_ref, w_ref, *refs, distance, waits):
    out_refs = refs[waits:]
    capacity, width = out_refs[0].shape
    tile = min(256, width)
    for n in range(width // tile):
        start = pl.multiple_of(part_of(where_ref, distance) * width + n * tile, tile)
        y = jnp.dot(h_ref[...], w_ref[:, pl.ds(start, tile)], preferred_element_type=F32)
        columns = slice(n * tile, (n + 1) * tile)
        for d, out in enumerate(out_refs):
            out[:, columns] = y[d * capacity : (d + 1) * capacity].astype(BF16)


def down(where, distance, hidden, down_w, width, experts, after):
    rows, depth = hidden.shape
    capacity = rows // experts
    return pl.pallas_call(
        functools.partial(down_kernel, distance=distance, waits=len(after)),
        out_shape=[jax.ShapeDtypeStruct((capacity, width), BF16)] * experts,
        in_specs=[pl.BlockSpec(memory_space=pltpu.SMEM)]
        + [pl.BlockSpec(memory_space=pltpu.VMEM)] * 2
        + [pl.BlockSpec(memory_space=pl.ANY)] * len(after),
        out_specs=[pl.BlockSpec(memory_space=pltpu.VMEM)] * experts,
        cost_estimate=cost(2 * rows * depth * width, 2 * depth * width + 2 * rows * width),
        compiler_params=params(),
        name="down",
    )(where, *pinned([hidden, down_w]), *after)


def combine_kernel(pick_ref, mix_ref, *refs, experts):
    y_refs, added, out = refs[:experts], refs[experts:-1], refs[-1]
    rows = out.shape[0]
    y = jnp.concatenate([r[...] for r in y_refs], axis=0)
    picked = lax.dot_general(
        pick_ref[...], y, (((0,), (0,)), ((), ())), preferred_element_type=F32
    )
    mixed = picked[:rows] * mix_ref[:, 0:1] + picked[rows:] * mix_ref[:, 1:2]
    for other in added:
        mixed = mixed + other[...].astype(F32)
    out[...] = mixed.astype(BF16)


def combine(pick, mix, blocks, added):
    rows = mix.shape[0]
    width = blocks[0].shape[1]
    operands = 2 + len(blocks) + len(added)
    return pl.pallas_call(
        functools.partial(combine_kernel, experts=len(blocks)),
        out_shape=jax.ShapeDtypeStruct((rows, width), BF16),
        in_specs=[pl.BlockSpec(memory_space=pltpu.VMEM)] * operands,
        out_specs=pl.BlockSpec(memory_space=pltpu.VMEM),
        cost_estimate=cost(4 * rows * pick.shape[0] * width, 6 * rows * width),
        compiler_params=params(),
        name="combine",
    )(pick, mix, *blocks, *added)


def swap(value, axis, distance):
    if not distance:
        return value
    count = lax.axis_size(axis)
    return lax.ppermute(value, axis, [(i, i ^ distance) for i in range(count)])


def per_device(tokens, expert_ids, route_logits, gate_weight, up_weight, down_weight):
    rows, own_width = tokens.shape
    experts = lax.axis_size("expert")
    shards = lax.axis_size("tensor")
    capacity = rows // 2
    where = jnp.stack([lax.axis_index("expert"), lax.axis_index("tensor")]).astype(jnp.int32)
    direct = shards <= 8
    distances = list(range(shards)) if direct else [None]
    width = own_width if direct else own_width * shards

    if direct:
        blocks = [swap(tokens, "tensor", d) for d in distances]
    else:
        blocks = [lax.all_gather(tokens, "tensor", axis=1, tiled=True)]
    placed, pick, mix = place(where, expert_ids, route_logits, experts, capacity)

    def rows_of(chosen):
        return [(w, d, width) for d in chosen for w in (gate_weight, up_weight)]

    whole = [(down_weight, None, down_weight.shape[1])]
    weights = list(prefetch(where, rows_of(distances[:2]), placed))
    groups = [list(range(len(distances)))[:2]] + [[i] for i in range(2, len(distances))]
    arrived = []
    for group in groups:
        after = weights[:1] if group is groups[0] else weights[-1:]
        outgoing = dispatch(placed, [blocks[i] for i in group], experts, capacity, after)
        arrived.append([swap(block, "expert", e) for e, block in enumerate(outgoing)])
        if group is groups[0]:
            weights += prefetch(where, rows_of(distances[2:]) + whole, outgoing[0])
    sums = None
    for group, x_blocks in zip(groups, arrived):
        chosen = weights[2 * group[0] : 2 * group[-1] + 2]
        sums = gate_up(x_blocks, chosen, sums, group is groups[-1])
    hidden, down_w = sums[0], weights[-1]

    sums, mixtures = [], []
    for d in reversed(distances):
        last = d == distances[0]
        after = sums[:1] if last else mixtures[-2:-1]
        terms = down(where, d, hidden, down_w, width, experts, after)
        returned = [swap(block, "expert", e) for e, block in enumerate(terms)]
        mixed = combine(pick, mix, returned, sums[::-1] if last else [])
        if not last:
            mixtures.append(mixed)
            sums.append(swap(mixed, "tensor", d))
    if direct:
        return mixed
    return lax.psum_scatter(mixed, "tensor", scatter_dimension=1, tiled=True)


def solution(mesh):
    in_specs = (
        P(("groups", "expert"), "tensor"),
        P(("groups", "expert"), None),
        P(("groups", "expert"), None),
        P("expert", None, "tensor"),
        P("expert", None, "tensor"),
        P("expert", "tensor", None),
    )
    out_specs = P(("groups", "expert"), "tensor")
    return jax.shard_map(
        per_device, mesh=mesh, in_specs=in_specs, out_specs=out_specs, check_vma=False
    )
```

time: 75.3 us -> 73.6 us (0.977)
  local copies, waits for them, and re-layouts: 6.39 us -> 1.36 us
  Pallas kernels: 27.4 us -> 31.3 us
  starting transfers between devices: 22.1 us -> 23.8 us
  waiting for transfers between devices: 18.2 us -> 16.5 us
  other arithmetic: 0.86 us -> 0.07 us
    pallas_call x6 -> x7, Pallas kernels: 11.3 us -> 21 us  [the longest x2 14.1 us: prefetch(): pl.pallas_call(functools.partial(prefetch_kernel, distances=[d for _, d,...]
    pallas_call x2 -> x3, Pallas kernels: 14.1 us -> 7.48 us  [gate_up(): pl.pallas_call(functools.partial(gate_up_kernel, experts=experts, slices=...]
    unnamed x13 -> x6, local copies, waits for them, and re-layouts: 6.3 us -> 1.36 us
    ppermute x24 -> x27, starting transfers between devices: 22.1 us -> 23.8 us  [swap(): return lax.ppermute(value, axis, [(i, i ^ distance) for i in range(count)])]
    ppermute x24 -> x27, waiting for transfers between devices: 18.2 us -> 16.5 us  [swap(): return lax.ppermute(value, axis, [(i, i ^ distance) for i in range(count)])]
    convert_element_type x1 -> x0, other arithmetic: 0.78 us -> none  [per_device(): return out.astype(BF16)]
  transfers between devices with their start and end apart: 24 -> 27, of which waited for: 8 -> 7; matrix products, arithmetic and copies ran while one was open for 0% -> 0% of each run, Pallas kernels for 30% -> 36%
where the time goes in v6:
time: 73.6 us; the launch traced here: 73.4 us
  Pallas kernels  31.3 us (43%)
  starting transfers between devices  23.8 us (32%)
  waiting for transfers between devices  16.5 us (22%)
  local copies, waits for them, and re-layouts  1.36 us (2%)
    ppermute x27, starting transfers between devices, swap(): return lax.ppermute(value, axis, [(i, i ^ distance) for i in range(count)])  23.8 us
    ppermute x27, waiting for transfers between devices, swap(): return lax.ppermute(value, axis, [(i, i ^ distance) for i in range(count)])  16.5 us
    pallas_call x2, Pallas kernels, prefetch(): pl.pallas_call(functools.partial(prefetch_kernel, distances=[d for _, d,...  14.1 us
    pallas_call x3, Pallas kernels, gate_up(): pl.pallas_call(functools.partial(gate_up_kernel, experts=experts, slices=...  7.48 us
    pallas_call x4, Pallas kernels, down(): pl.pallas_call(functools.partial(down_kernel, distance=distance, waits=le...  6.27 us
    pallas_call x4, Pallas kernels, combine(): pl.pallas_call(functools.partial(combine_kernel, experts=len(blocks)), ou...  1.95 us
  transfers between devices with their start and end apart: 27, of which 7 were waited for; matrix products, arithmetic and copies ran while one was open for 0% of the time, Pallas kernels for 36%

profile of v6, /device:TPU:0, one launch (start us, length us, event | category | flops | bytes accessed | tf_op | source)
XLA Modules:
  0.0 73.4 jit_solution(4900960141540947582)
XLA Ops:
  0.0 3.0 %collective-permute-start.1 = (bf16[128,768]{1,0:T(8,128)(2,1)}, bf16[128,768]{1,0:T(8,128)(2,1)S(1)}, u32[]{:S(2)}, u32[]{:S(2)}) collective-permute-start(bf16[128,768]{1,0:T(8,128)(2,1)} %refs_0_.4), channel_id=1, source_target_pairs={{0,4},{4,0},{8,12},{12,8},{1,5},{5,1},{9,13},{13,9},{2,6},{6,2},{1... | collective-permute-start | bytes 589832 | tf_op jit(solution)/shard_map/ppermute | solution.py:256
  3.0 2.6 %collective-permute-start.5 = (bf16[128,768]{1,0:T(8,128)(2,1)}, bf16[128,768]{1,0:T(8,128)(2,1)S(1)}, u32[]{:S(2)}, u32[]{:S(2)}) collective-permute-start(bf16[128,768]{1,0:T(8,128)(2,1)} %refs_0_.4), channel_id=1, source_target_pairs={{0,8},{4,12},{8,0},{12,4},{1,9},{5,13},{9,1},{13,5},{2,10},{6,14},... | collective-permute-start | bytes 589832 | tf_op jit(solution)/shard_map/ppermute | solution.py:256
  5.7 0.7 copy-done.1
  6.4 0.7 copy-done.2
  7.1 0.7 routing.1
  7.8 5.2 %prefetch.2 = (bf16[768,2048]{1,0:T(8,128)(2,1)S(1)}, bf16[768,2048]{1,0:T(8,128)(2,1)S(1)}, bf16[768,2048]{1,0:T(8,128)(2,1)S(1)}, bf16[768,2048]{1,0:T(8,128)(2,1)S(1)}) custom-call(s32[2]{0:T(128)S(1)} %pad_add_fusion.where_ref, bf16[256,128]{1,0:T(8,128)(2,1)S(1)} %get-tuple-element.51.after_ref.placed_ref, bf16[1,3072,2048]{2,1,0:T(8,128)(2,1)} %refs_2_.3, ...), custom_call_target="tpu_custom_call" | custom-call | bytes 12582912 | tf_op jit(solution)/shard_map/prefetch/pallas_call | solution.py:124
  13.0 0.4 dispatch.3
  13.4 1.8 %collective-permute-start.10 = (bf16[64,1536]{1,0:T(8,128)(2,1)S(1)}, bf16[64,1536]{1,0:T(8,128)(2,1)S(1)}, u32[]{:S(2)}, u32[]{:S(2)}) collective-permute-start(bf16[64,1536]{1,0:T(8,128)(2,1)S(1)} %get-tuple-element.68), channel_id=1, source_target_pairs={{0,2},{1,3},{2,0},{3,1},{4,6},{5,7},{6,4},{7,5},{8,10},{9,11},{10,... | collective-permute-start | bytes 589832 | tf_op jit(solution)/shard_map/ppermute | solution.py:256
  15.2 0.4 collective-permute-start.9
  15.6 8.8 %prefetch.3 = (bf16[768,2048]{1,0:T(8,128)(2,1)S(1)}, bf16[768,2048]{1,0:T(8,128)(2,1)S(1)}, bf16[768,2048]{1,0:T(8,128)(2,1)S(1)}, bf16[768,2048]{1,0:T(8,128)(2,1)S(1)}, bf16[2048,3072]{1,0:T(8,128)(2,1)S(1)}) custom-call(s32[2]{0:T(128)S(1)} %pad_add_fusion.where_ref, bf16[64,1536]{1,0:T(8,128)(2,1)S(1)} %get-tuple-element.53.after_ref.refs_0_, ...), custom_call_target="tpu_custom_call" | custom-call | bytes 25165824 | tf_op jit(solution)/shard_map/prefetch/pallas_call | solution.py:124
  24.5 0.3 dispatch.5
  24.7 0.1 collective-permute-start.6
  24.9 1.7 %collective-permute-start.7 = (bf16[64,768]{1,0:T(8,128)(2,1)S(1)}, bf16[64,768]{1,0:T(8,128)(2,1)S(1)}, u32[]{:S(2)}, u32[]{:S(2)}) collective-permute-start(bf16[64,768]{1,0:T(8,128)(2,1)S(1)} %get-tuple-element.63), channel_id=1, source_target_pairs={{0,2},{1,3},{2,0},{3,1},{4,6},{5,7},{6,4},{7,5},{8,10},{9,11},{10,... | collective-permute-start | bytes 294920 | tf_op jit(solution)/shard_map/ppermute | solution.py:256
  26.6 0.3 dispatch.4
  26.9 0.1 collective-permute-start.8
  27.0 0.4 collective-permute-start.2
  27.4 1.7 %collective-permute-start.3 = (bf16[64,768]{1,0:T(8,128)(2,1)S(1)}, bf16[64,768]{1,0:T(8,128)(2,1)S(1)}, u32[]{:S(2)}, u32[]{:S(2)}) collective-permute-start(bf16[64,768]{1,0:T(8,128)(2,1)S(1)} %get-tuple-element.57), channel_id=1, source_target_pairs={{0,2},{1,3},{2,0},{3,1},{4,6},{5,7},{6,4},{7,5},{8,10},{9,11},{10,... | collective-permute-start | bytes 294920 | tf_op jit(solution)/shard_map/ppermute | solution.py:256
  29.1 3.4 %gate_up.3 = (f32[256,2048]{1,0:T(8,128)S(1)}, f32[256,2048]{1,0:T(8,128)S(1)}) custom-call(bf16[64,1536]{1,0:T(8,128)(2,1)S(1)} %get-tuple-element.53.after_ref.refs_0_, bf16[64,1536]{1,0:T(8,128)(2,1)S(1)} %collective-permute-done.9.refs_1_, bf16[64,1536]{1,0:T(8,128)(2,1)S(1)} %collective-permute-done.10.refs_2_, ...), custom_call_target="tpu_custom_call" | custom-call | flops 3221225472 | bytes 12582912 | tf_op jit(solution)/shard_map/gate_up/pallas_call | solution.py:179
  32.6 2.1 %gate_up.4 = (f32[256,2048]{1,0:T(8,128)S(1)}, f32[256,2048]{1,0:T(8,128)S(1)}) custom-call(bf16[64,768]{1,0:T(8,128)(2,1)S(1)} %get-tuple-element.61.refs_0_, bf16[64,768]{1,0:T(8,128)(2,1)S(1)} %collective-permute-done.6.refs_1_, bf16[64,768]{1,0:T(8,128)(2,1)S(1)} %collective-permute-done.7.refs_2_, ...), custom_call_target="tpu_custom_call", output_to_operand_aliasing={{0}: (6, {}), {1}: (7, {})} | custom-call | flops 1610612736 | bytes 6291456 | tf_op jit(solution)/shard_map/gate_up/pallas_call | solution.py:179
  34.7 2.9 %collective-permute-done.4.refs_3_ = bf16[64,768]{1,0:T(8,128)(2,1)S(1)} collective-permute-done((bf16[64,768]{1,0:T(8,128)(2,1)S(1)}, bf16[64,768]{1,0:T(8,128)(2,1)S(1)}, u32[]{:S(2)}, u32[]{:S(2)}) %collective-permute-start.4) | collective-permute-done | bytes 98336 | tf_op jit(solution)/shard_map/ppermute | solution.py:256
  37.6 2.0 %gate_up.5.h_ref = bf16[256,2048]{1,0:T(8,128)(2,1)S(1)} custom-call(bf16[64,768]{1,0:T(8,128)(2,1)S(1)} %get-tuple-element.55.refs_0_, bf16[64,768]{1,0:T(8,128)(2,1)S(1)} %collective-permute-done.2.refs_1_, bf16[64,768]{1,0:T(8,128)(2,1)S(1)} %collective-permute-done.3.refs_2_, bf16[64,768]{1,0:T(8,128)(2,1)S(1)} %collective-permute-done.4.refs_3_, ...), custom_call_target="tpu_custom_call" | custom-call | flops 1610612736 | bytes 6291456 | tf_op jit(solution)/shard_map/gate_up/pallas_call | solution.py:179
  39.6 1.6 %down.4 = (bf16[64,768]{1,0:T(8,128)(2,1)S(1)}, bf16[64,768]{1,0:T(8,128)(2,1)S(1)}, bf16[64,768]{1,0:T(8,128)(2,1)S(1)}, bf16[64,768]{1,0:T(8,128)(2,1)S(1)}) custom-call(s32[2]{0:T(128)S(1)} %pad_add_fusion.where_ref, bf16[256,2048]{1,0:T(8,128)(2,1)S(1)} %gate_up.5.h_ref, bf16[2048,3072]{1,0:T(8,128)(2,1)S(1)} %get-tuple-element.54.refs_1_.w_ref), custom_call_target="tpu_custom_call" | custom-call | flops 805306368 | bytes 3538944 | tf_op jit(solution)/shard_map/down/pallas_call | solution.py:211
  41.2 0.2 collective-permute-start.12
  41.4 0.3 collective-permute-start.13
  41.6 1.5 %collective-permute-start.14 = (bf16[64,768]{1,0:T(8,128)(2,1)S(1)}, bf16[64,768]{1,0:T(8,128)(2,1)S(1)}, u32[]{:S(2)}, u32[]{:S(2)}) collective-permute-start(bf16[64,768]{1,0:T(8,128)(2,1)S(1)} %get-tuple-element.80), channel_id=1, source_target_pairs={{0,3},{1,2},{2,1},{3,0},{4,7},{5,6},{6,5},{7,4},{8,11},{9,10},{10,... | collective-permute-start | bytes 294920 | tf_op jit(solution)/shard_map/ppermute | solution.py:256
  43.2 1.6 %down.7 = (bf16[64,768]{1,0:T(8,128)(2,1)S(1)}, bf16[64,768]{1,0:T(8,128)(2,1)S(1)}, bf16[64,768]{1,0:T(8,128)(2,1)S(1)}, bf16[64,768]{1,0:T(8,128)(2,1)S(1)}) custom-call(s32[2]{0:T(128)S(1)} %pad_add_fusion.where_ref, bf16[256,2048]{1,0:T(8,128)(2,1)S(1)} %gate_up.5.h_ref, bf16[2048,3072]{1,0:T(8,128)(2,1)S(1)} %get-tuple-element.54.refs_1_.w_ref), custom_call_target="tpu_custom_call" | custom-call | flops 805306368 | bytes 3538944 | tf_op jit(solution)/shard_map/down/pallas_call | solution.py:211
  44.7 0.4 collective-permute-start.23
  45.2 0.3 collective-permute-start.24
  45.4 1.2 %collective-permute-start.25 = (bf16[64,768]{1,0:T(8,128)(2,1)S(1)}, bf16[64,768]{1,0:T(8,128)(2,1)S(1)}, u32[]{:S(2)}, u32[]{:S(2)}) collective-permute-start(bf16[64,768]{1,0:T(8,128)(2,1)S(1)} %get-tuple-element.92), channel_id=1, source_target_pairs={{0,3},{1,2},{2,1},{3,0},{4,7},{5,6},{6,5},{7,4},{8,11},{9,10},{10,... | collective-permute-start | bytes 294920 | tf_op jit(solution)/shard_map/ppermute | solution.py:256
  46.7 0.3 collective-permute-done.13.refs_2_
  47.0 1.2 %collective-permute-done.14.refs_3_ = bf16[64,768]{1,0:T(8,128)(2,1)S(1)} collective-permute-done((bf16[64,768]{1,0:T(8,128)(2,1)S(1)}, bf16[64,768]{1,0:T(8,128)(2,1)S(1)}, u32[]{:S(2)}, u32[]{:S(2)}) %collective-permute-start.14) | collective-permute-done | bytes 98336 | tf_op jit(solution)/shard_map/ppermute | solution.py:256
  48.1 0.3 combine.4.refs_0_
  48.4 3.5 %collective-permute-start.15 = (bf16[128,768]{1,0:T(8,128)(2,1)S(1)}, bf16[128,768]{1,0:T(8,128)(2,1)S(1)}, u32[]{:S(2)}, u32[]{:S(2)}) collective-permute-start(bf16[128,768]{1,0:T(8,128)(2,1)S(1)} %combine.4.refs_0_), channel_id=1, source_target_pairs={{0,12},{4,8},{8,4},{12,0},{1,13},{5,9},{9,5},{13,1},{2,14},{6,10},... | collective-permute-start | bytes 589832 | tf_op jit(solution)/shard_map/ppermute | solution.py:256
  52.0 1.5 %down.6 = (bf16[64,768]{1,0:T(8,128)(2,1)S(1)}, bf16[64,768]{1,0:T(8,128)(2,1)S(1)}, bf16[64,768]{1,0:T(8,128)(2,1)S(1)}, bf16[64,768]{1,0:T(8,128)(2,1)S(1)}) custom-call(s32[2]{0:T(128)S(1)} %pad_add_fusion.where_ref, bf16[256,2048]{1,0:T(8,128)(2,1)S(1)} %gate_up.5.h_ref, bf16[2048,3072]{1,0:T(8,128)(2,1)S(1)} %get-tuple-element.54.refs_1_.w_ref, ...), custom_call_target="tpu_custom_call" | custom-call | flops 805306368 | bytes 3538944 | tf_op jit(solution)/shard_map/down/pallas_call | solution.py:211
  53.5 0.7 collective-permute-start.19
  54.2 0.5 collective-permute-start.20
  54.8 0.9 %collective-permute-start.21 = (bf16[64,768]{1,0:T(8,128)(2,1)S(1)}, bf16[64,768]{1,0:T(8,128)(2,1)S(1)}, u32[]{:S(2)}, u32[]{:S(2)}) collective-permute-start(bf16[64,768]{1,0:T(8,128)(2,1)S(1)} %get-tuple-element.88), channel_id=1, source_target_pairs={{0,3},{1,2},{2,1},{3,0},{4,7},{5,6},{6,5},{7,4},{8,11},{9,10},{10,... | collective-permute-start | bytes 294920 | tf_op jit(solution)/shard_map/ppermute | solution.py:256
  55.7 0.3 combine.6
  56.1 3.8 %collective-permute-done.20.refs_2_ = bf16[64,768]{1,0:T(8,128)(2,1)S(1)} collective-permute-done((bf16[64,768]{1,0:T(8,128)(2,1)S(1)}, bf16[64,768]{1,0:T(8,128)(2,1)S(1)}, u32[]{:S(2)}, u32[]{:S(2)}) %collective-permute-start.20) | collective-permute-done | bytes 98336 | tf_op jit(solution)/shard_map/ppermute | solution.py:256
  59.9 0.4 collective-permute-done.21.refs_3_
  60.3 0.3 combine.5
  60.7 1.6 %down.5 = (bf16[64,768]{1,0:T(8,128)(2,1)S(1)}, bf16[64,768]{1,0:T(8,128)(2,1)S(1)}, bf16[64,768]{1,0:T(8,128)(2,1)S(1)}, bf16[64,768]{1,0:T(8,128)(2,1)S(1)}) custom-call(s32[2]{0:T(128)S(1)} %pad_add_fusion.where_ref, bf16[256,2048]{1,0:T(8,128)(2,1)S(1)} %gate_up.5.h_ref, bf16[2048,3072]{1,0:T(8,128)(2,1)S(1)} %get-tuple-element.54.refs_1_.w_ref, ...), custom_call_target="tpu_custom_call" | custom-call | flops 805306368 | bytes 3538944 | tf_op jit(solution)/shard_map/down/pallas_call | solution.py:211
  62.2 0.8 %collective-permute-start.16 = (bf16[64,768]{1,0:T(8,128)(2,1)S(1)}, bf16[64,768]{1,0:T(8,128)(2,1)S(1)}, u32[]{:S(2)}, u32[]{:S(2)}) collective-permute-start(bf16[64,768]{1,0:T(8,128)(2,1)S(1)} %get-tuple-element.82), channel_id=1, source_target_pairs={{0,1},{1,0},{2,3},{3,2},{4,5},{5,4},{6,7},{7,6},{8,9},{9,8},{10,11... | collective-permute-start | bytes 294920 | tf_op jit(solution)/shard_map/ppermute | solution.py:256
  63.0 0.6 collective-permute-start.17
  63.5 0.9 %collective-permute-start.18 = (bf16[64,768]{1,0:T(8,128)(2,1)S(1)}, bf16[64,768]{1,0:T(8,128)(2,1)S(1)}, u32[]{:S(2)}, u32[]{:S(2)}) collective-permute-start(bf16[64,768]{1,0:T(8,128)(2,1)S(1)} %get-tuple-element.84), channel_id=1, source_target_pairs={{0,3},{1,2},{2,1},{3,0},{4,7},{5,6},{6,5},{7,4},{8,11},{9,10},{10,... | collective-permute-start | bytes 294920 | tf_op jit(solution)/shard_map/ppermute | solution.py:256
  64.4 4.5 %collective-permute-done.26.refs_5_ = bf16[128,768]{1,0:T(8,128)(2,1)S(1)} collective-permute-done((bf16[128,768]{1,0:T(8,128)(2,1)S(1)}, bf16[128,768]{1,0:T(8,128)(2,1)S(1)}, u32[]{:S(2)}, u32[]{:S(2)}) %collective-permute-start.26) | collective-permute-done | bytes 196640 | tf_op jit(solution)/shard_map/ppermute | solution.py:256
  68.9 3.4 %collective-permute-done.22.refs_4_ = bf16[128,768]{1,0:T(8,128)(2,1)S(1)} collective-permute-done((bf16[128,768]{1,0:T(8,128)(2,1)S(1)}, bf16[128,768]{1,0:T(8,128)(2,1)S(1)}, u32[]{:S(2)}, u32[]{:S(2)}) %collective-permute-start.22) | collective-permute-done | bytes 196640 | tf_op jit(solution)/shard_map/ppermute | solution.py:256
  72.4 1.0 %combine.7 = bf16[128,768]{1,0:T(8,128)(2,1)} custom-call(bf16[256,256]{1,0:T(8,128)(2,1)S(1)} %get-tuple-element.49.pick_ref, f32[128,2]{1,0:T(8,128)S(1)} %get-tuple-element.50.mix_ref, bf16[64,768]{1,0:T(8,128)(2,1)S(1)} %get-tuple-element.81.refs_0_, bf16[64,768]{1,0:T(8,128)(2,1)S(1)} %collective-permute-done.16.refs_1_, ...), custom_call_target="tpu_custom_call" | custom-call | flops 100663296 | bytes 589824 | tf_op jit(solution)/shard_map/combine/pallas_call | solution.py:241
  (30 shorter events, 0.4 us)
Async XLA Ops:
  0.0 13.0 %collective-permute-start.1 = (bf16[128,768]{1,0:T(8,128)(2,1)}, bf16[128,768]{1,0:T(8,128)(2,1)S(1)}, u32[]{:S(2)}, u32[]{:S(2)}) collective-permute-start(bf16[128,768]{1,0:T(8,128)(2,1)} %refs_0_.4), channel_id=1, source_target_pairs={{0,4},{4,0},{8,12},{12,8},{1,5},{5,1},{9,13},{13,9},{2,6},{6,2},{1... | collective-permute-start | bytes 589832 | tf_op jit(solution)/shard_map/ppermute | solution.py:256
  3.0 21.4 %collective-permute-start.5 = (bf16[128,768]{1,0:T(8,128)(2,1)}, bf16[128,768]{1,0:T(8,128)(2,1)S(1)}, u32[]{:S(2)}, u32[]{:S(2)}) collective-permute-start(bf16[128,768]{1,0:T(8,128)(2,1)} %refs_0_.4), channel_id=1, source_target_pairs={{0,8},{4,12},{8,0},{12,4},{1,9},{5,13},{9,1},{13,5},{2,10},{6,14},... | collective-permute-start | bytes 589832 | tf_op jit(solution)/shard_map/ppermute | solution.py:256
  5.6 19.3 %collective-permute-start = (bf16[128,768]{1,0:T(8,128)(2,1)}, bf16[128,768]{1,0:T(8,128)(2,1)S(1)}, u32[]{:S(2)}, u32[]{:S(2)}) collective-permute-start(bf16[128,768]{1,0:T(8,128)(2,1)} %refs_0_.4), channel_id=1, source_target_pairs={{0,12},{4,8},{8,4},{12,0},{1,13},{5,9},{9,5},{13,1},{2,14},{6,10},... | collective-permute-start | bytes 589832 | tf_op jit(solution)/shard_map/ppermute | solution.py:256
  5.7 0.7 copy-start.1
  6.4 0.7 copy-start.2
  7.8 5.3 %copy-start = (bf16[128,768]{1,0:T(8,128)(2,1)S(1)}, bf16[128,768]{1,0:T(8,128)(2,1)}, u32[]{:S(2)}) copy-start(bf16[128,768]{1,0:T(8,128)(2,1)} %refs_0_.4) | copy-start | bytes 589828
  13.4 13.4 %collective-permute-start.10 = (bf16[64,1536]{1,0:T(8,128)(2,1)S(1)}, bf16[64,1536]{1,0:T(8,128)(2,1)S(1)}, u32[]{:S(2)}, u32[]{:S(2)}) collective-permute-start(bf16[64,1536]{1,0:T(8,128)(2,1)S(1)} %get-tuple-element.68), channel_id=1, source_target_pairs={{0,2},{1,3},{2,0},{3,1},{4,6},{5,7},{6,4},{7,5},{8,10},{9,11},{10,... | collective-permute-start | bytes 589832 | tf_op jit(solution)/shard_map/ppermute | solution.py:256
  15.2 11.8 %collective-permute-start.11 = (bf16[64,1536]{1,0:T(8,128)(2,1)S(1)}, bf16[64,1536]{1,0:T(8,128)(2,1)S(1)}, u32[]{:S(2)}, u32[]{:S(2)}) collective-permute-start(bf16[64,1536]{1,0:T(8,128)(2,1)S(1)} %get-tuple-element.69), channel_id=1, source_target_pairs={{0,3},{1,2},{2,1},{3,0},{4,7},{5,6},{6,5},{7,4},{8,11},{9,10},{10,... | collective-permute-start | bytes 589832 | tf_op jit(solution)/shard_map/ppermute | solution.py:256
  15.2 12.2 %collective-permute-start.9 = (bf16[64,1536]{1,0:T(8,128)(2,1)S(1)}, bf16[64,1536]{1,0:T(8,128)(2,1)S(1)}, u32[]{:S(2)}, u32[]{:S(2)}) collective-permute-start(bf16[64,1536]{1,0:T(8,128)(2,1)S(1)} %get-tuple-element.67), channel_id=1, source_target_pairs={{0,1},{1,0},{2,3},{3,2},{4,5},{5,4},{6,7},{7,6},{8,9},{9,8},{10,11... | collective-permute-start | bytes 589832 | tf_op jit(solution)/shard_map/ppermute | solution.py:256
  24.7 7.8 %collective-permute-start.6 = (bf16[64,768]{1,0:T(8,128)(2,1)S(1)}, bf16[64,768]{1,0:T(8,128)(2,1)S(1)}, u32[]{:S(2)}, u32[]{:S(2)}) collective-permute-start(bf16[64,768]{1,0:T(8,128)(2,1)S(1)} %get-tuple-element.62), channel_id=1, source_target_pairs={{0,1},{1,0},{2,3},{3,2},{4,5},{5,4},{6,7},{7,6},{8,9},{9,8},{10,11... | collective-permute-start | bytes 294920 | tf_op jit(solution)/shard_map/ppermute | solution.py:256
  24.9 7.7 %collective-permute-start.7 = (bf16[64,768]{1,0:T(8,128)(2,1)S(1)}, bf16[64,768]{1,0:T(8,128)(2,1)S(1)}, u32[]{:S(2)}, u32[]{:S(2)}) collective-permute-start(bf16[64,768]{1,0:T(8,128)(2,1)S(1)} %get-tuple-element.63), channel_id=1, source_target_pairs={{0,2},{1,3},{2,0},{3,1},{4,6},{5,7},{6,4},{7,5},{8,10},{9,11},{10,... | collective-permute-start | bytes 294920 | tf_op jit(solution)/shard_map/ppermute | solution.py:256
  26.9 5.7 %collective-permute-start.8 = (bf16[64,768]{1,0:T(8,128)(2,1)S(1)}, bf16[64,768]{1,0:T(8,128)(2,1)S(1)}, u32[]{:S(2)}, u32[]{:S(2)}) collective-permute-start(bf16[64,768]{1,0:T(8,128)(2,1)S(1)} %get-tuple-element.64), channel_id=1, source_target_pairs={{0,3},{1,2},{2,1},{3,0},{4,7},{5,6},{6,5},{7,4},{8,11},{9,10},{10,... | collective-permute-start | bytes 294920 | tf_op jit(solution)/shard_map/ppermute | solution.py:256
  27.0 7.7 %collective-permute-start.2 = (bf16[64,768]{1,0:T(8,128)(2,1)S(1)}, bf16[64,768]{1,0:T(8,128)(2,1)S(1)}, u32[]{:S(2)}, u32[]{:S(2)}) collective-permute-start(bf16[64,768]{1,0:T(8,128)(2,1)S(1)} %get-tuple-element.56), channel_id=1, source_target_pairs={{0,1},{1,0},{2,3},{3,2},{4,5},{5,4},{6,7},{7,6},{8,9},{9,8},{10,11... | collective-permute-start | bytes 294920 | tf_op jit(solution)/shard_map/ppermute | solution.py:256
  27.4 7.4 %collective-permute-start.3 = (bf16[64,768]{1,0:T(8,128)(2,1)S(1)}, bf16[64,768]{1,0:T(8,128)(2,1)S(1)}, u32[]{:S(2)}, u32[]{:S(2)}) collective-permute-start(bf16[64,768]{1,0:T(8,128)(2,1)S(1)} %get-tuple-element.57), channel_id=1, source_target_pairs={{0,2},{1,3},{2,0},{3,1},{4,6},{5,7},{6,4},{7,5},{8,10},{9,11},{10,... | collective-permute-start | bytes 294920 | tf_op jit(solution)/shard_map/ppermute | solution.py:256
  32.5 5.1 %collective-permute-start.4 = (bf16[64,768]{1,0:T(8,128)(2,1)S(1)}, bf16[64,768]{1,0:T(8,128)(2,1)S(1)}, u32[]{:S(2)}, u32[]{:S(2)}) collective-permute-start(bf16[64,768]{1,0:T(8,128)(2,1)S(1)} %get-tuple-element.58), channel_id=1, source_target_pairs={{0,3},{1,2},{2,1},{3,0},{4,7},{5,6},{6,5},{7,4},{8,11},{9,10},{10,... | collective-permute-start | bytes 294920 | tf_op jit(solution)/shard_map/ppermute | solution.py:256
  41.2 4.2 %collective-permute-start.12 = (bf16[64,768]{1,0:T(8,128)(2,1)S(1)}, bf16[64,768]{1,0:T(8,128)(2,1)S(1)}, u32[]{:S(2)}, u32[]{:S(2)}) collective-permute-start(bf16[64,768]{1,0:T(8,128)(2,1)S(1)} %get-tuple-element.78), channel_id=1, source_target_pairs={{0,1},{1,0},{2,3},{3,2},{4,5},{5,4},{6,7},{7,6},{8,9},{9,8},{10,11... | collective-permute-start | bytes 294920 | tf_op jit(solution)/shard_map/ppermute | solution.py:256
  41.4 5.6 %collective-permute-start.13 = (bf16[64,768]{1,0:T(8,128)(2,1)S(1)}, bf16[64,768]{1,0:T(8,128)(2,1)S(1)}, u32[]{:S(2)}, u32[]{:S(2)}) collective-permute-start(bf16[64,768]{1,0:T(8,128)(2,1)S(1)} %get-tuple-element.79), channel_id=1, source_target_pairs={{0,2},{1,3},{2,0},{3,1},{4,6},{5,7},{6,4},{7,5},{8,10},{9,11},{10,... | collective-permute-start | bytes 294920 | tf_op jit(solution)/shard_map/ppermute | solution.py:256
  41.6 6.5 %collective-permute-start.14 = (bf16[64,768]{1,0:T(8,128)(2,1)S(1)}, bf16[64,768]{1,0:T(8,128)(2,1)S(1)}, u32[]{:S(2)}, u32[]{:S(2)}) collective-permute-start(bf16[64,768]{1,0:T(8,128)(2,1)S(1)} %get-tuple-element.80), channel_id=1, source_target_pairs={{0,3},{1,2},{2,1},{3,0},{4,7},{5,6},{6,5},{7,4},{8,11},{9,10},{10,... | collective-permute-start | bytes 294920 | tf_op jit(solution)/shard_map/ppermute | solution.py:256
  44.7 9.5 %collective-permute-start.23 = (bf16[64,768]{1,0:T(8,128)(2,1)S(1)}, bf16[64,768]{1,0:T(8,128)(2,1)S(1)}, u32[]{:S(2)}, u32[]{:S(2)}) collective-permute-start(bf16[64,768]{1,0:T(8,128)(2,1)S(1)} %get-tuple-element.90), channel_id=1, source_target_pairs={{0,1},{1,0},{2,3},{3,2},{4,5},{5,4},{6,7},{7,6},{8,9},{9,8},{10,11... | collective-permute-start | bytes 294920 | tf_op jit(solution)/shard_map/ppermute | solution.py:256
  45.2 9.6 %collective-permute-start.24 = (bf16[64,768]{1,0:T(8,128)(2,1)S(1)}, bf16[64,768]{1,0:T(8,128)(2,1)S(1)}, u32[]{:S(2)}, u32[]{:S(2)}) collective-permute-start(bf16[64,768]{1,0:T(8,128)(2,1)S(1)} %get-tuple-element.91), channel_id=1, source_target_pairs={{0,2},{1,3},{2,0},{3,1},{4,6},{5,7},{6,4},{7,5},{8,10},{9,11},{10,... | collective-permute-start | bytes 294920 | tf_op jit(solution)/shard_map/ppermute | solution.py:256
  45.4 10.3 %collective-permute-start.25 = (bf16[64,768]{1,0:T(8,128)(2,1)S(1)}, bf16[64,768]{1,0:T(8,128)(2,1)S(1)}, u32[]{:S(2)}, u32[]{:S(2)}) collective-permute-start(bf16[64,768]{1,0:T(8,128)(2,1)S(1)} %get-tuple-element.92), channel_id=1, source_target_pairs={{0,3},{1,2},{2,1},{3,0},{4,7},{5,6},{6,5},{7,4},{8,11},{9,10},{10,... | collective-permute-start | bytes 294920 | tf_op jit(solution)/shard_map/ppermute | solution.py:256
  48.4 12.2 %collective-permute-start.15 = (bf16[128,768]{1,0:T(8,128)(2,1)S(1)}, bf16[128,768]{1,0:T(8,128)(2,1)S(1)}, u32[]{:S(2)}, u32[]{:S(2)}) collective-permute-start(bf16[128,768]{1,0:T(8,128)(2,1)S(1)} %combine.4.refs_0_), channel_id=1, source_target_pairs={{0,12},{4,8},{8,4},{12,0},{1,13},{5,9},{9,5},{13,1},{2,14},{6,10},... | collective-permute-start | bytes 589832 | tf_op jit(solution)/shard_map/ppermute | solution.py:256
  53.5 2.6 %collective-permute-start.19 = (bf16[64,768]{1,0:T(8,128)(2,1)S(1)}, bf16[64,768]{1,0:T(8,128)(2,1)S(1)}, u32[]{:S(2)}, u32[]{:S(2)}) collective-permute-start(bf16[64,768]{1,0:T(8,128)(2,1)S(1)} %get-tuple-element.86), channel_id=1, source_target_pairs={{0,1},{1,0},{2,3},{3,2},{4,5},{5,4},{6,7},{7,6},{8,9},{9,8},{10,11... | collective-permute-start | bytes 294920 | tf_op jit(solution)/shard_map/ppermute | solution.py:256
  54.2 5.7 %collective-permute-start.20 = (bf16[64,768]{1,0:T(8,128)(2,1)S(1)}, bf16[64,768]{1,0:T(8,128)(2,1)S(1)}, u32[]{:S(2)}, u32[]{:S(2)}) collective-permute-start(bf16[64,768]{1,0:T(8,128)(2,1)S(1)} %get-tuple-element.87), channel_id=1, source_target_pairs={{0,2},{1,3},{2,0},{3,1},{4,6},{5,7},{6,4},{7,5},{8,10},{9,11},{10,... | collective-permute-start | bytes 294920 | tf_op jit(solution)/shard_map/ppermute | solution.py:256
  54.8 5.5 %collective-permute-start.21 = (bf16[64,768]{1,0:T(8,128)(2,1)S(1)}, bf16[64,768]{1,0:T(8,128)(2,1)S(1)}, u32[]{:S(2)}, u32[]{:S(2)}) collective-permute-start(bf16[64,768]{1,0:T(8,128)(2,1)S(1)} %get-tuple-element.88), channel_id=1, source_target_pairs={{0,3},{1,2},{2,1},{3,0},{4,7},{5,6},{6,5},{7,4},{8,11},{9,10},{10,... | collective-permute-start | bytes 294920 | tf_op jit(solution)/shard_map/ppermute | solution.py:256
  56.0 12.9 %collective-permute-start.26 = (bf16[128,768]{1,0:T(8,128)(2,1)S(1)}, bf16[128,768]{1,0:T(8,128)(2,1)S(1)}, u32[]{:S(2)}, u32[]{:S(2)}) collective-permute-start(bf16[128,768]{1,0:T(8,128)(2,1)S(1)} %combine.6), channel_id=1, source_target_pairs={{0,8},{4,12},{8,0},{12,4},{1,9},{5,13},{9,1},{13,5},{2,10},{6,14},... | collective-permute-start | bytes 589832 | tf_op jit(solution)/shard_map/ppermute | solution.py:256
  60.6 11.8 %collective-permute-start.22 = (bf16[128,768]{1,0:T(8,128)(2,1)S(1)}, bf16[128,768]{1,0:T(8,128)(2,1)S(1)}, u32[]{:S(2)}, u32[]{:S(2)}) collective-permute-start(bf16[128,768]{1,0:T(8,128)(2,1)S(1)} %combine.5), channel_id=1, source_target_pairs={{0,4},{4,0},{8,12},{12,8},{1,5},{5,1},{9,13},{13,9},{2,6},{6,2},{1... | collective-permute-start | bytes 589832 | tf_op jit(solution)/shard_map/ppermute | solution.py:256
  62.2 10.1 %collective-permute-start.16 = (bf16[64,768]{1,0:T(8,128)(2,1)S(1)}, bf16[64,768]{1,0:T(8,128)(2,1)S(1)}, u32[]{:S(2)}, u32[]{:S(2)}) collective-permute-start(bf16[64,768]{1,0:T(8,128)(2,1)S(1)} %get-tuple-element.82), channel_id=1, source_target_pairs={{0,1},{1,0},{2,3},{3,2},{4,5},{5,4},{6,7},{7,6},{8,9},{9,8},{10,11... | collective-permute-start | bytes 294920 | tf_op jit(solution)/shard_map/ppermute | solution.py:256
  63.0 9.4 %collective-permute-start.17 = (bf16[64,768]{1,0:T(8,128)(2,1)S(1)}, bf16[64,768]{1,0:T(8,128)(2,1)S(1)}, u32[]{:S(2)}, u32[]{:S(2)}) collective-permute-start(bf16[64,768]{1,0:T(8,128)(2,1)S(1)} %get-tuple-element.83), channel_id=1, source_target_pairs={{0,2},{1,3},{2,0},{3,1},{4,6},{5,7},{6,4},{7,5},{8,10},{9,11},{10,... | collective-permute-start | bytes 294920 | tf_op jit(solution)/shard_map/ppermute | solution.py:256
  63.5 8.8 %collective-permute-start.18 = (bf16[64,768]{1,0:T(8,128)(2,1)S(1)}, bf16[64,768]{1,0:T(8,128)(2,1)S(1)}, u32[]{:S(2)}, u32[]{:S(2)}) collective-permute-start(bf16[64,768]{1,0:T(8,128)(2,1)S(1)} %get-tuple-element.84), channel_id=1, source_target_pairs={{0,3},{1,2},{2,1},{3,0},{4,7},{5,6},{6,5},{7,4},{8,11},{9,10},{10,... | collective-permute-start | bytes 294920 | tf_op jit(solution)/shard_map/ppermute | solution.py:256

commit v7 on v6

v7 whole, which is shorter than its diff:
```python
import functools

import jax
import jax.numpy as jnp
from jax import lax
from jax.experimental import pallas as pl
from jax.experimental.pallas import tpu as pltpu
from jax.sharding import PartitionSpec as P

F32 = jnp.float32
BF16 = jnp.bfloat16
MIB = 1024 * 1024


def params(mib=6):
    return pltpu.CompilerParams(vmem_limit_bytes=mib * MIB)


def cost(flops, moved):
    return pl.CostEstimate(flops=flops, bytes_accessed=moved, transcendentals=0)


def pinned(arrays):
    return [pltpu.with_memory_space_constraint(array, pltpu.VMEM) for array in arrays]


def routing_kernel(me_ref, ids_ref, logits_ref, placed_ref, pick_ref, mix_ref, *, experts):
    rows = ids_ref.shape[1]
    capacity = placed_ref.shape[0] // experts
    relative = lax.bitwise_xor(ids_ref[...], me_ref[0])
    lane = lax.broadcasted_iota(jnp.int32, (experts, rows), 0)
    names = [lane == relative[k : k + 1] for k in range(2)]
    named = names[0] | names[1]
    row = lax.broadcasted_iota(jnp.int32, (rows, rows), 0)
    column = lax.broadcasted_iota(jnp.int32, (rows, rows), 1)
    before = jnp.dot(
        jnp.where(named, 1.0, 0.0).astype(BF16),
        jnp.where(row < column, 1.0, 0.0).astype(BF16),
        preferred_element_type=F32,
    ).astype(jnp.int32)
    slot = lax.broadcasted_iota(jnp.int32, (capacity, rows), 0)
    for d in range(experts):
        here = slice(d * capacity, (d + 1) * capacity)
        both = None
        for k in range(2):
            position = jnp.where(names[k], before, -1)
            hit = jnp.where(position[d : d + 1] == slot, 1.0, 0.0)
            pick_ref[here, k * rows : (k + 1) * rows] = hit.astype(BF16)
            both = hit if k == 0 else both + hit
        placed_ref[here, :] = both.astype(BF16)
    share = 1.0 / (1.0 + jnp.exp(logits_ref[1:2] - logits_ref[0:1]))
    share = jnp.sum(jnp.where(row == column, share, 0.0), axis=1, keepdims=True)
    mix_ref[:, 0:1] = share
    mix_ref[:, 1:2] = 1.0 - share


def place(me, expert_ids, route_logits, experts, capacity):
    rows = expert_ids.shape[0]
    return pl.pallas_call(
        functools.partial(routing_kernel, experts=experts),
        out_shape=[
            jax.ShapeDtypeStruct((experts * capacity, rows), BF16),
            jax.ShapeDtypeStruct((experts * capacity, 2 * rows), BF16),
            jax.ShapeDtypeStruct((rows, 2), F32),
        ],
        in_specs=[pl.BlockSpec(memory_space=pltpu.SMEM)]
        + [pl.BlockSpec(memory_space=pltpu.VMEM)] * 2,
        out_specs=[pl.BlockSpec(memory_space=pltpu.VMEM)] * 3,
        compiler_params=params(),
        name="routing",
    )(me.reshape(1), expert_ids.T, route_logits.T)


def dispatch_kernel(placed_ref, *refs, counts, waits):
    inputs, outputs = refs[: sum(counts)], refs[sum(counts) + waits :]
    capacity, wide = outputs[0].shape
    width = wide // len(counts)
    for i, count in enumerate(counts):
        block = inputs[sum(counts[:i])][...]
        for j in range(1, count):
            block = block + inputs[sum(counts[:i]) + j][...]
        for d, out in enumerate(outputs):
            out[:, i * width : (i + 1) * width] = jnp.dot(
                placed_ref[d * capacity : (d + 1) * capacity, :],
                block,
                preferred_element_type=F32,
            ).astype(BF16)


def dispatch(placed, slices, experts, capacity, after):
    rows, width = slices[0][0].shape
    wide = width * len(slices)
    arrays = [array for arrays in slices for array in arrays]
    return pl.pallas_call(
        functools.partial(
            dispatch_kernel, counts=[len(arrays) for arrays in slices], waits=len(after)
        ),
        out_shape=[jax.ShapeDtypeStruct((capacity, wide), BF16)] * experts,
        in_specs=[pl.BlockSpec(memory_space=pltpu.VMEM)] * (1 + len(arrays))
        + [pl.BlockSpec(memory_space=pl.ANY)] * len(after),
        out_specs=[pl.BlockSpec(memory_space=pltpu.VMEM)] * experts,
        cost_estimate=cost(2 * experts * capacity * rows * wide, 6 * rows * wide),
        compiler_params=params(),
        name="dispatch",
    )(placed, *arrays, *pinned(after))


def across(distance):
    return lambda column: lax.bitwise_xor(column, distance)


def second(column):
    return jnp.where(column < 2, 2, 1)


def third(column):
    return jnp.where(column < 2, 3, 0)


def everything(column):
    return 0


def prefetch_kernel(column_ref, after_ref, *refs, parts):
    half = len(refs) // 2
    copies = []
    for i, part in enumerate(parts):
        source, target, sem = refs[i], refs[half + i], refs[-1].at[i]
        count = target.shape[0]
        start = pl.multiple_of(part(column_ref[0]) * count, count)
        copies.append(pltpu.make_async_copy(source.at[0, pl.ds(start, count)], target, sem))
    for copy in copies:
        copy.start()
    for copy in copies:
        copy.wait()


def prefetch(column, fetches, after):
    sources = [pltpu.with_memory_space_constraint(w, pltpu.HBM) for w, _, _ in fetches]
    shapes = [pltpu.VMEM((count, w.shape[2]), w.dtype) for w, _, count in fetches]
    return pl.pallas_call(
        functools.partial(prefetch_kernel, parts=[part for _, part, _ in fetches]),
        out_shape=shapes,
        in_specs=[pl.BlockSpec(memory_space=pltpu.SMEM)]
        + [pl.BlockSpec(memory_space=pl.ANY)] * (1 + len(sources)),
        out_specs=[pl.BlockSpec(memory_space=pltpu.VMEM)] * len(shapes),
        scratch_shapes=[pltpu.SemaphoreType.DMA((len(shapes),))],
        cost_estimate=cost(0, sum(2 * count * w.shape[2] for w, _, count in fetches)),
        compiler_params=params(),
        name="prefetch",
    )(column.reshape(1), after, *sources)


def gate_up_kernel(*refs, experts, slices, first, last):
    x_refs = refs[:experts]
    weights = refs[experts : experts + 2 * slices]
    rest = refs[experts + 2 * slices :]
    if not first:
        old_gate, old_up = rest[:2]
        rest = rest[2:]
    x = jnp.concatenate([r[...] for r in x_refs], axis=0)
    width, hidden = weights[0].shape
    tile = min(512, hidden)
    for n in range(hidden // tile):
        columns = slice(n * tile, (n + 1) * tile)
        sums = []
        for kind in range(2):
            total = None if first else (old_gate, old_up)[kind][:, columns]
            for i in range(slices):
                term = jnp.dot(
                    x[:, i * width : (i + 1) * width],
                    weights[2 * i + kind][:, columns],
                    preferred_element_type=F32,
                )
                total = term if total is None else total + term
            sums.append(total)
        gate, up = sums
        if last:
            rest[0][:, columns] = (gate / (1.0 + jnp.exp(-gate)) * up).astype(BF16)
        else:
            rest[0][:, columns] = gate
            rest[1][:, columns] = up


def gate_up(x_blocks, weights, sums, last):
    experts = len(x_blocks)
    rows = experts * x_blocks[0].shape[0]
    hidden = weights[0].shape[1]
    first = sums is None
    old = [] if first else pinned(sums)
    before = experts + len(weights)
    if last:
        out_shape = [pltpu.VMEM((rows, hidden), BF16)]
    else:
        out_shape = [pltpu.VMEM((rows, hidden), F32)] * 2
    return pl.pallas_call(
        functools.partial(
            gate_up_kernel, experts=experts, slices=len(weights) // 2, first=first, last=last
        ),
        out_shape=out_shape,
        in_specs=[pl.BlockSpec(memory_space=pltpu.VMEM)] * (before + len(old)),
        out_specs=[pl.BlockSpec(memory_space=pltpu.VMEM)] * len(out_shape),
        input_output_aliases={} if first or last else {before: 0, before + 1: 1},
        cost_estimate=cost(
            2 * rows * hidden * sum(w.shape[0] for w in weights),
            sum(2 * w.size for w in weights),
        ),
        compiler_params=params(),
        name="gate_up",
    )(*x_blocks, *pinned(weights), *old)


def down_kernel(column_ref, h_ref, w_ref, *out_refs, part):
    capacity, width = out_refs[0].shape
    tile = min(256, width)
    for n in range(width // tile):
        start = pl.multiple_of(part(column_ref[0]) * width + n * tile, tile)
        y = jnp.dot(h_ref[...], w_ref[0, :, pl.ds(start, tile)], preferred_element_type=F32)
        columns = slice(n * tile, (n + 1) * tile)
        for d, out in enumerate(out_refs):
            out[:, columns] = y[d * capacity : (d + 1) * capacity].astype(BF16)


def down(column, part, hidden, down_w, width, experts):
    rows, depth = hidden.shape
    capacity = rows // experts
    return pl.pallas_call(
        functools.partial(down_kernel, part=part),
        out_shape=[jax.ShapeDtypeStruct((capacity, width), BF16)] * experts,
        in_specs=[pl.BlockSpec(memory_space=pltpu.SMEM)]
        + [pl.BlockSpec(memory_space=pltpu.VMEM)] * 2,
        out_specs=[pl.BlockSpec(memory_space=pltpu.VMEM)] * experts,
        cost_estimate=cost(2 * rows * depth * width, 2 * depth * width + 2 * rows * width),
        compiler_params=params(),
        name="down",
    )(column.reshape(1), *pinned([hidden, down_w]))


def combine_kernel(pick_ref, mix_ref, *refs, experts, sums, plain):
    outs = refs[len(refs) - 1 - plain :]
    y_refs, added = refs[:experts], refs[experts : experts + sums]
    rows = outs[0].shape[0]
    y = jnp.concatenate([r[...] for r in y_refs], axis=0)
    picked = lax.dot_general(
        pick_ref[...], y, (((0,), (0,)), ((), ())), preferred_element_type=F32
    )
    mixed = picked[:rows] * mix_ref[:, 0:1] + picked[rows:] * mix_ref[:, 1:2]
    if plain:
        outs[1][...] = mixed.astype(BF16)
    for other in added:
        mixed = mixed + other[...].astype(F32)
    outs[0][...] = mixed.astype(BF16)


def combine(pick, mix, blocks, added, after=(), plain=False):
    rows = mix.shape[0]
    width = blocks[0].shape[1]
    operands = 2 + len(blocks) + len(added)
    return pl.pallas_call(
        functools.partial(
            combine_kernel, experts=len(blocks), sums=len(added), plain=plain
        ),
        out_shape=[jax.ShapeDtypeStruct((rows, width), BF16)] * (1 + plain),
        in_specs=[pl.BlockSpec(memory_space=pltpu.VMEM)] * operands
        + [pl.BlockSpec(memory_space=pl.ANY)] * len(after),
        out_specs=[pl.BlockSpec(memory_space=pltpu.VMEM)] * (1 + plain),
        cost_estimate=cost(4 * rows * pick.shape[0] * width, 6 * rows * width),
        compiler_params=params(),
        name="combine",
    )(pick, mix, *blocks, *added, *after)


def add_kernel(a_ref, b_ref, out_ref):
    out_ref[...] = (a_ref[...].astype(F32) + b_ref[...].astype(F32)).astype(BF16)


def add(a, b):
    return pl.pallas_call(
        add_kernel,
        out_shape=jax.ShapeDtypeStruct(a.shape, BF16),
        in_specs=[pl.BlockSpec(memory_space=pltpu.VMEM)] * 2,
        out_specs=pl.BlockSpec(memory_space=pltpu.VMEM),
        cost_estimate=cost(a.size, 6 * a.size),
        compiler_params=params(),
        name="add",
    )(a, b)


def swap(value, axis, distance):
    if not distance:
        return value
    count = lax.axis_size(axis)
    return lax.ppermute(value, axis, [(i, i ^ distance) for i in range(count)])


def middle(value):
    return lax.ppermute(value, "tensor", [(1, 2), (2, 1)])


def outwards(value):
    return lax.ppermute(value, "tensor", [(1, 0), (2, 3)])


def inwards(value):
    return lax.ppermute(value, "tensor", [(0, 1), (3, 2)])


def per_device(tokens, expert_ids, route_logits, gate_weight, up_weight, down_weight):
    rows, own_width = tokens.shape
    experts = lax.axis_size("expert")
    shards = lax.axis_size("tensor")
    capacity = rows // 2
    me = lax.axis_index("expert").astype(jnp.int32)
    column = lax.axis_index("tensor").astype(jnp.int32)
    line = shards == 4
    width = own_width if line else own_width * shards

    if line:
        beside = swap(tokens, "tensor", 1)
        near = middle(tokens)
        far = middle(beside)
        parts = [across(0), across(1), second, third]
        slices = [[tokens], [beside], [near, outwards(near)], [far, outwards(far)]]
        groups = [[0, 1], [2], [3]]
    else:
        parts = [everything]
        slices = [[lax.all_gather(tokens, "tensor", axis=1, tiled=True)]]
        groups = [[0]]
    placed, pick, mix = place(me, expert_ids, route_logits, experts, capacity)

    weights, arrived, ready = [], [], placed
    for i, part in enumerate(parts):
        fetches = [(w, part, width) for w in (gate_weight, up_weight)]
        weights.append(list(prefetch(column, fetches, ready)))
        if i < len(groups):
            chosen = [slices[j] for j in groups[i]]
            outgoing = dispatch(placed, chosen, experts, capacity, weights[-1][:1])
            arrived.append([swap(block, "expert", e) for e, block in enumerate(outgoing)])
            ready = outgoing[0]

    sums = None
    for group, x_blocks in zip(groups, arrived):
        chosen = [w for j in group for w in weights[j]]
        sums = gate_up(x_blocks, chosen, sums, group is groups[-1])
    hidden = sums[0]

    def returned(part):
        terms = down(column, part, hidden, down_weight, width, experts)
        return [swap(block, "expert", e) for e, block in enumerate(terms)]

    if not line:
        mixed = combine(pick, mix, returned(everything), [])[0]
        return lax.psum_scatter(mixed, "tensor", scatter_dimension=1, tiled=True)
    blocks = [returned(across(distance)) for distance in range(4)]
    last = combine(pick, mix, blocks[3], [], after=blocks[2][2:3])[0]
    from_end = inwards(last)
    onwards, alone = combine(pick, mix, blocks[2], [from_end], after=blocks[1][2:3], plain=True)
    over = middle(onwards)
    crossing = middle(add(last, inwards(alone)))
    next_to = combine(pick, mix, blocks[1], [over], after=blocks[0][2:3])[0]
    beside = swap(next_to, "tensor", 1)
    return combine(pick, mix, blocks[0], [beside, crossing])[0]


def solution(mesh):
    in_specs = (
        P(("groups", "expert"), "tensor"),
        P(("groups", "expert"), None),
        P(("groups", "expert"), None),
        P("expert", None, "tensor"),
        P("expert", None, "tensor"),
        P("expert", "tensor", None),
    )
    out_specs = P(("groups", "expert"), "tensor")
    return jax.shard_map(
        per_device, mesh=mesh, in_specs=in_specs, out_specs=out_specs, check_vma=False
    )
```

time: 73.6 us -> 83.1 us (1.13)
  starting transfers between devices: 23.8 us -> 34.2 us
  Pallas kernels: 31.3 us -> 26.4 us
  waiting for transfers between devices: 16.5 us -> 20.4 us
    ppermute x0 -> x8, starting transfers between devices: none -> 10.9 us  [the longest x2 5.65 us: inwards(): return lax.ppermute(value, 'tensor', [(0, 1), (3, 2)])]
    pallas_call x13 -> x16, Pallas kernels: 23.2 us -> 18.6 us  [the longest x4 11.6 us: prefetch(): pl.pallas_call(functools.partial(prefetch_kernel, parts=[part for _, part...]
    ppermute x0 -> x8, waiting for transfers between devices: none -> 2.86 us  [the longest x2 2.11 us: outwards(): return lax.ppermute(value, 'tensor', [(1, 0), (2, 3)])]
    ppermute x27 -> x23, waiting for transfers between devices: 16.5 us -> 17.6 us  [swap(): return lax.ppermute(value, axis, [(i, i ^ distance) for i in range(count)])]
    ppermute x27 -> x23, starting transfers between devices: 23.8 us -> 23.3 us  [swap(): return lax.ppermute(value, axis, [(i, i ^ distance) for i in range(count)])]
  transfers between devices with their start and end apart: 27 -> 31, of which waited for: 7 -> 13; matrix products, arithmetic and copies ran while one was open for 0% -> 0% of each run, Pallas kernels for 36% -> 25%
where the time goes in v7:
time: 83.1 us; the launch traced here: 82.8 us
  starting transfers between devices  34.2 us (41%)
  Pallas kernels  26.4 us (32%)
  waiting for transfers between devices  20.4 us (25%)
  local copies, waits for them, and re-layouts  1.42 us (2%)
    ppermute x23, starting transfers between devices, swap(): return lax.ppermute(value, axis, [(i, i ^ distance) for i in range(count)])  23.3 us
    ppermute x23, waiting for transfers between devices, swap(): return lax.ppermute(value, axis, [(i, i ^ distance) for i in range(count)])  17.6 us
    pallas_call x4, Pallas kernels, prefetch(): pl.pallas_call(functools.partial(prefetch_kernel, parts=[part for _, part...  11.6 us
    pallas_call x3, Pallas kernels, gate_up(): pl.pallas_call(functools.partial(gate_up_kernel, experts=experts, slices=...  7.62 us
    ppermute x2, starting transfers between devices, inwards(): return lax.ppermute(value, 'tensor', [(0, 1), (3, 2)])  5.65 us
    pallas_call x4, Pallas kernels, down(): pl.pallas_call(functools.partial(down_kernel, part=part), out_shape=[jax....  4.1 us
    ppermute x4, starting transfers between devices, middle(): return lax.ppermute(value, 'tensor', [(1, 2), (2, 1)])  2.67 us
    ppermute x2, starting transfers between devices, outwards(): return lax.ppermute(value, 'tensor', [(1, 0), (2, 3)])  2.57 us
  transfers between devices with their start and end apart: 31, of which 13 were waited for; matrix products, arithmetic and copies ran while one was open for 0% of the time, Pallas kernels for 25%

profile of v7, /device:TPU:0, one launch (start us, length us, event | category | flops | bytes accessed | tf_op | source)
XLA Modules:
  0.0 82.8 jit_solution(17587625703378675981)
XLA Ops:
  0.0 0.7 collective-permute-start.3
  0.7 5.9 %collective-permute-start = (bf16[128,768]{1,0:T(8,128)(2,1)}, bf16[128,768]{1,0:T(8,128)(2,1)S(1)}, u32[]{:S(2)}, u32[]{:S(2)}) collective-permute-start(bf16[128,768]{1,0:T(8,128)(2,1)} %refs_0_.6), channel_id=1, source_target_pairs={{0,4},{4,0},{8,12},{12,8},{1,5},{5,1},{9,13},{13,9},{2,6},{6,2},{1... | collective-permute-start | bytes 589832 | tf_op jit(solution)/shard_map/ppermute | solution.py:293
  6.6 0.7 copy-done.1
  7.3 0.7 copy-done.2
  8.1 2.9 %prefetch.4 = (bf16[768,2048]{1,0:T(8,128)(2,1)S(1)}, bf16[768,2048]{1,0:T(8,128)(2,1)S(1)}) custom-call(s32[1]{0:T(128)} %bitcast.3.column_ref, bf16[256,128]{1,0:T(8,128)(2,1)S(1)} %get-tuple-element.52.after_ref.placed_ref, bf16[1,3072,2048]{2,1,0:T(8,128)(2,1)} %refs_0_.9, bf16[1,3072,2048]{2,1,0:T(8,128)(2,1)} %refs_1_.7), custom_call_target="tpu_custom_call" | custom-call | bytes 6291456 | tf_op jit(solution)/shard_map/prefetch/pallas_call | solution.py:141
  11.0 1.3 %collective-permute-start.4 = (bf16[128,768]{1,0:T(8,128)(2,1)S(1)}, bf16[128,768]{1,0:T(8,128)(2,1)S(1)}, u32[]{:S(2)}, u32[]{:S(2)}) collective-permute-start(bf16[128,768]{1,0:T(8,128)(2,1)S(1)} %collective-permute-done.3.refs_0_), channel_id=1, source_target_pairs={{4,0},{8,12},{5,1},{9,13},{6,2},{10,14},{7,3},{11,15},{20,16},{24,... | collective-permute-start | bytes 589832 | tf_op jit(solution)/shard_map/ppermute | solution.py:301
  12.8 1.6 %collective-permute-start.12 = (bf16[64,1536]{1,0:T(8,128)(2,1)S(1)}, bf16[64,1536]{1,0:T(8,128)(2,1)S(1)}, u32[]{:S(2)}, u32[]{:S(2)}) collective-permute-start(bf16[64,1536]{1,0:T(8,128)(2,1)S(1)} %get-tuple-element.69), channel_id=1, source_target_pairs={{0,2},{1,3},{2,0},{3,1},{4,6},{5,7},{6,4},{7,5},{8,10},{9,11},{10,... | collective-permute-start | bytes 589832 | tf_op jit(solution)/shard_map/ppermute | solution.py:293
  14.4 0.7 collective-permute-start.1
  15.4 2.9 %prefetch.5 = (bf16[768,2048]{1,0:T(8,128)(2,1)S(1)}, bf16[768,2048]{1,0:T(8,128)(2,1)S(1)}) custom-call(s32[1]{0:T(128)} %bitcast.3.column_ref, bf16[64,1536]{1,0:T(8,128)(2,1)S(1)} %get-tuple-element.54.after_ref.refs_0_, bf16[1,3072,2048]{2,1,0:T(8,128)(2,1)} %refs_0_.9, bf16[1,3072,2048]{2,1,0:T(8,128)(2,1)} %refs_1_.7), custom_call_target="tpu_custom_call" | custom-call | bytes 6291456 | tf_op jit(solution)/shard_map/prefetch/pallas_call | solution.py:141
  18.3 0.7 collective-permute-done.4.refs_1_
  19.3 0.8 collective-permute-start.10
  20.1 0.9 %collective-permute-start.8 = (bf16[64,768]{1,0:T(8,128)(2,1)S(1)}, bf16[64,768]{1,0:T(8,128)(2,1)S(1)}, u32[]{:S(2)}, u32[]{:S(2)}) collective-permute-start(bf16[64,768]{1,0:T(8,128)(2,1)S(1)} %get-tuple-element.64), channel_id=1, source_target_pairs={{0,1},{1,0},{2,3},{3,2},{4,5},{5,4},{6,7},{7,6},{8,9},{9,8},{10,11... | collective-permute-start | bytes 294920 | tf_op jit(solution)/shard_map/ppermute | solution.py:293
  21.0 1.1 %collective-permute-start.9 = (bf16[64,768]{1,0:T(8,128)(2,1)S(1)}, bf16[64,768]{1,0:T(8,128)(2,1)S(1)}, u32[]{:S(2)}, u32[]{:S(2)}) collective-permute-start(bf16[64,768]{1,0:T(8,128)(2,1)S(1)} %get-tuple-element.65), channel_id=1, source_target_pairs={{0,2},{1,3},{2,0},{3,1},{4,6},{5,7},{6,4},{7,5},{8,10},{9,11},{10,... | collective-permute-start | bytes 294920 | tf_op jit(solution)/shard_map/ppermute | solution.py:293
  22.1 1.3 %collective-permute-start.2 = (bf16[128,768]{1,0:T(8,128)(2,1)S(1)}, bf16[128,768]{1,0:T(8,128)(2,1)S(1)}, u32[]{:S(2)}, u32[]{:S(2)}) collective-permute-start(bf16[128,768]{1,0:T(8,128)(2,1)S(1)} %collective-permute-done.1.refs_0_), channel_id=1, source_target_pairs={{4,0},{8,12},{5,1},{9,13},{6,2},{10,14},{7,3},{11,15},{20,16},{24,... | collective-permute-start | bytes 589832 | tf_op jit(solution)/shard_map/ppermute | solution.py:301
  23.4 0.5 collective-permute-done.13.refs_3_
  23.9 3.4 %gate_up.3 = (f32[256,2048]{1,0:T(8,128)S(1)}, f32[256,2048]{1,0:T(8,128)S(1)}) custom-call(bf16[64,1536]{1,0:T(8,128)(2,1)S(1)} %get-tuple-element.54.after_ref.refs_0_, bf16[64,1536]{1,0:T(8,128)(2,1)S(1)} %collective-permute-done.11.refs_1_, bf16[64,1536]{1,0:T(8,128)(2,1)S(1)} %collective-permute-done.12.refs_2_, ...), custom_call_target="tpu_custom_call" | custom-call | flops 3221225472 | bytes 12582912 | tf_op jit(solution)/shard_map/gate_up/pallas_call | solution.py:196
  27.3 2.9 %prefetch.6 = (bf16[768,2048]{1,0:T(8,128)(2,1)S(1)}, bf16[768,2048]{1,0:T(8,128)(2,1)S(1)}) custom-call(s32[1]{0:T(128)} %bitcast.3.column_ref, bf16[64,768]{1,0:T(8,128)(2,1)S(1)} %get-tuple-element.56.after_ref.refs_0_, bf16[1,3072,2048]{2,1,0:T(8,128)(2,1)} %refs_0_.9, bf16[1,3072,2048]{2,1,0:T(8,128)(2,1)} %refs_1_.7), custom_call_target="tpu_custom_call" | custom-call | bytes 6291456 | tf_op jit(solution)/shard_map/prefetch/pallas_call | solution.py:141
  30.2 1.4 %collective-permute-done.2.refs_1_ = bf16[128,768]{1,0:T(8,128)(2,1)S(1)} collective-permute-done((bf16[128,768]{1,0:T(8,128)(2,1)S(1)}, bf16[128,768]{1,0:T(8,128)(2,1)S(1)}, u32[]{:S(2)}, u32[]{:S(2)}) %collective-permute-start.2) | collective-permute-done | bytes 196640 | tf_op jit(solution)/shard_map/ppermute | solution.py:301
  31.9 1.5 %collective-permute-start.6 = (bf16[64,768]{1,0:T(8,128)(2,1)S(1)}, bf16[64,768]{1,0:T(8,128)(2,1)S(1)}, u32[]{:S(2)}, u32[]{:S(2)}) collective-permute-start(bf16[64,768]{1,0:T(8,128)(2,1)S(1)} %get-tuple-element.60), channel_id=1, source_target_pairs={{0,2},{1,3},{2,0},{3,1},{4,6},{5,7},{6,4},{7,5},{8,10},{9,11},{10,... | collective-permute-start | bytes 294920 | tf_op jit(solution)/shard_map/ppermute | solution.py:293
  33.8 2.1 %gate_up.4 = (f32[256,2048]{1,0:T(8,128)S(1)}, f32[256,2048]{1,0:T(8,128)S(1)}) custom-call(bf16[64,768]{1,0:T(8,128)(2,1)S(1)} %get-tuple-element.56.after_ref.refs_0_, bf16[64,768]{1,0:T(8,128)(2,1)S(1)} %collective-permute-done.8.refs_1_, bf16[64,768]{1,0:T(8,128)(2,1)S(1)} %collective-permute-done.9.refs_2_, ...), custom_call_target="tpu_custom_call", output_to_operand_aliasing={{0}: (6, {}), {1}: (7, {})} | custom-call | flops 1610612736 | bytes 6291456 | tf_op jit(solution)/shard_map/gate_up/pallas_call | solution.py:196
  35.9 3.0 %prefetch.7 = (bf16[768,2048]{1,0:T(8,128)(2,1)S(1)}, bf16[768,2048]{1,0:T(8,128)(2,1)S(1)}) custom-call(s32[1]{0:T(128)} %bitcast.3.column_ref, bf16[64,768]{1,0:T(8,128)(2,1)S(1)} %get-tuple-element.58.after_ref.refs_0_, bf16[1,3072,2048]{2,1,0:T(8,128)(2,1)} %refs_0_.9, bf16[1,3072,2048]{2,1,0:T(8,128)(2,1)} %refs_1_.7), custom_call_target="tpu_custom_call" | custom-call | bytes 6291456 | tf_op jit(solution)/shard_map/prefetch/pallas_call | solution.py:141
  39.0 2.1 %gate_up.5.h_ref = bf16[256,2048]{1,0:T(8,128)(2,1)S(1)} custom-call(bf16[64,768]{1,0:T(8,128)(2,1)S(1)} %get-tuple-element.58.after_ref.refs_0_, bf16[64,768]{1,0:T(8,128)(2,1)S(1)} %collective-permute-done.5.refs_1_, bf16[64,768]{1,0:T(8,128)(2,1)S(1)} %collective-permute-done.6.refs_2_, bf16[64,768]{1,0:T(8,128)(2,1)S(1)} %collective-permute-done.7.refs_3_, ...), custom_call_target="tpu_custom_call" | custom-call | flops 1610612736 | bytes 6291456 | tf_op jit(solution)/shard_map/gate_up/pallas_call | solution.py:196
  41.1 1.0 %down.6 = (bf16[64,768]{1,0:T(8,128)(2,1)S(1)}, bf16[64,768]{1,0:T(8,128)(2,1)S(1)}, bf16[64,768]{1,0:T(8,128)(2,1)S(1)}, bf16[64,768]{1,0:T(8,128)(2,1)S(1)}) custom-call(s32[1]{0:T(128)} %bitcast.3.column_ref, bf16[256,2048]{1,0:T(8,128)(2,1)S(1)} %gate_up.5.h_ref, bf16[1,2048,3072]{2,1,0:T(8,128)(2,1)S(1)} %bitcast.5), custom_call_target="tpu_custom_call" | custom-call | flops 805306368 | bytes 3538944 | tf_op jit(solution)/shard_map/down/pallas_call | solution.py:227
  42.1 1.0 %down.7 = (bf16[64,768]{1,0:T(8,128)(2,1)S(1)}, bf16[64,768]{1,0:T(8,128)(2,1)S(1)}, bf16[64,768]{1,0:T(8,128)(2,1)S(1)}, bf16[64,768]{1,0:T(8,128)(2,1)S(1)}) custom-call(s32[1]{0:T(128)} %bitcast.3.column_ref, bf16[256,2048]{1,0:T(8,128)(2,1)S(1)} %gate_up.5.h_ref, bf16[1,2048,3072]{2,1,0:T(8,128)(2,1)S(1)} %bitcast.5), custom_call_target="tpu_custom_call" | custom-call | flops 805306368 | bytes 3538944 | tf_op jit(solution)/shard_map/down/pallas_call | solution.py:227
  43.2 1.5 %collective-permute-start.21 = (bf16[64,768]{1,0:T(8,128)(2,1)S(1)}, bf16[64,768]{1,0:T(8,128)(2,1)S(1)}, u32[]{:S(2)}, u32[]{:S(2)}) collective-permute-start(bf16[64,768]{1,0:T(8,128)(2,1)S(1)} %get-tuple-element.87), channel_id=1, source_target_pairs={{0,2},{1,3},{2,0},{3,1},{4,6},{5,7},{6,4},{7,5},{8,10},{9,11},{10,... | collective-permute-start | bytes 294920 | tf_op jit(solution)/shard_map/ppermute | solution.py:293
  44.8 0.6 collective-permute-start.24
  45.4 1.2 %collective-permute-start.25 = (bf16[64,768]{1,0:T(8,128)(2,1)S(1)}, bf16[64,768]{1,0:T(8,128)(2,1)S(1)}, u32[]{:S(2)}, u32[]{:S(2)}) collective-permute-start(bf16[64,768]{1,0:T(8,128)(2,1)S(1)} %get-tuple-element.92), channel_id=1, source_target_pairs={{0,3},{1,2},{2,1},{3,0},{4,7},{5,6},{6,5},{7,4},{8,11},{9,10},{10,... | collective-permute-start | bytes 294920 | tf_op jit(solution)/shard_map/ppermute | solution.py:293
  46.6 2.2 %collective-permute-done.21.refs_4_.refs_2_ = bf16[64,768]{1,0:T(8,128)(2,1)S(1)} collective-permute-done((bf16[64,768]{1,0:T(8,128)(2,1)S(1)}, bf16[64,768]{1,0:T(8,128)(2,1)S(1)}, u32[]{:S(2)}, u32[]{:S(2)}) %collective-permute-start.21) | collective-permute-done | bytes 98336 | tf_op jit(solution)/shard_map/ppermute | solution.py:293
  48.8 2.1 %collective-permute-done.24.refs_2_ = bf16[64,768]{1,0:T(8,128)(2,1)S(1)} collective-permute-done((bf16[64,768]{1,0:T(8,128)(2,1)S(1)}, bf16[64,768]{1,0:T(8,128)(2,1)S(1)}, u32[]{:S(2)}, u32[]{:S(2)}) %collective-permute-start.24) | collective-permute-done | bytes 98336 | tf_op jit(solution)/shard_map/ppermute | solution.py:293
  50.9 1.1 %collective-permute-done.25.refs_3_ = bf16[64,768]{1,0:T(8,128)(2,1)S(1)} collective-permute-done((bf16[64,768]{1,0:T(8,128)(2,1)S(1)}, bf16[64,768]{1,0:T(8,128)(2,1)S(1)}, u32[]{:S(2)}, u32[]{:S(2)}) %collective-permute-start.25) | collective-permute-done | bytes 98336 | tf_op jit(solution)/shard_map/ppermute | solution.py:293
  52.3 4.0 %collective-permute-start.26 = (bf16[128,768]{1,0:T(8,128)(2,1)S(1)}, bf16[128,768]{1,0:T(8,128)(2,1)S(1)}, u32[]{:S(2)}, u32[]{:S(2)}) collective-permute-start(bf16[128,768]{1,0:T(8,128)(2,1)S(1)} %combine.4.a_ref), channel_id=1, source_target_pairs={{0,4},{12,8},{1,5},{13,9},{2,6},{14,10},{3,7},{15,11},{16,20},{28,... | collective-permute-start | bytes 589832 | tf_op jit(solution)/shard_map/ppermute | solution.py:305
  56.4 1.0 %down.5 = (bf16[64,768]{1,0:T(8,128)(2,1)S(1)}, bf16[64,768]{1,0:T(8,128)(2,1)S(1)}, bf16[64,768]{1,0:T(8,128)(2,1)S(1)}, bf16[64,768]{1,0:T(8,128)(2,1)S(1)}) custom-call(s32[1]{0:T(128)} %bitcast.3.column_ref, bf16[256,2048]{1,0:T(8,128)(2,1)S(1)} %gate_up.5.h_ref, bf16[1,2048,3072]{2,1,0:T(8,128)(2,1)S(1)} %bitcast.5), custom_call_target="tpu_custom_call" | custom-call | flops 805306368 | bytes 3538944 | tf_op jit(solution)/shard_map/down/pallas_call | solution.py:227
  57.4 1.9 %collective-permute-start.18 = (bf16[64,768]{1,0:T(8,128)(2,1)S(1)}, bf16[64,768]{1,0:T(8,128)(2,1)S(1)}, u32[]{:S(2)}, u32[]{:S(2)}) collective-permute-start(bf16[64,768]{1,0:T(8,128)(2,1)S(1)} %get-tuple-element.83), channel_id=1, source_target_pairs={{0,2},{1,3},{2,0},{3,1},{4,6},{5,7},{6,4},{7,5},{8,10},{9,11},{10,... | collective-permute-start | bytes 294920 | tf_op jit(solution)/shard_map/ppermute | solution.py:293
  59.6 2.8 %collective-permute-done.18.refs_5_.refs_2_ = bf16[64,768]{1,0:T(8,128)(2,1)S(1)} collective-permute-done((bf16[64,768]{1,0:T(8,128)(2,1)S(1)}, bf16[64,768]{1,0:T(8,128)(2,1)S(1)}, u32[]{:S(2)}, u32[]{:S(2)}) %collective-permute-start.18) | collective-permute-done | bytes 98336 | tf_op jit(solution)/shard_map/ppermute | solution.py:293
  62.4 1.3 %collective-permute-done.22.refs_3_ = bf16[64,768]{1,0:T(8,128)(2,1)S(1)} collective-permute-done((bf16[64,768]{1,0:T(8,128)(2,1)S(1)}, bf16[64,768]{1,0:T(8,128)(2,1)S(1)}, u32[]{:S(2)}, u32[]{:S(2)}) %collective-permute-start.22) | collective-permute-done | bytes 98336 | tf_op jit(solution)/shard_map/ppermute | solution.py:293
  64.1 1.6 %collective-permute-start.29 = (bf16[128,768]{1,0:T(8,128)(2,1)S(1)}, bf16[128,768]{1,0:T(8,128)(2,1)S(1)}, u32[]{:S(2)}, u32[]{:S(2)}) collective-permute-start(bf16[128,768]{1,0:T(8,128)(2,1)S(1)} %get-tuple-element.94), channel_id=1, source_target_pairs={{0,4},{12,8},{1,5},{13,9},{2,6},{14,10},{3,7},{15,11},{16,20},{28,... | collective-permute-start | bytes 589832 | tf_op jit(solution)/shard_map/ppermute | solution.py:305
  65.7 0.7 collective-permute-start.27
  66.6 1.0 %down.4 = (bf16[64,768]{1,0:T(8,128)(2,1)S(1)}, bf16[64,768]{1,0:T(8,128)(2,1)S(1)}, bf16[64,768]{1,0:T(8,128)(2,1)S(1)}, bf16[64,768]{1,0:T(8,128)(2,1)S(1)}) custom-call(s32[1]{0:T(128)} %bitcast.3.column_ref, bf16[256,2048]{1,0:T(8,128)(2,1)S(1)} %gate_up.5.h_ref, bf16[1,2048,3072]{2,1,0:T(8,128)(2,1)S(1)} %bitcast.5), custom_call_target="tpu_custom_call" | custom-call | flops 805306368 | bytes 3538944 | tf_op jit(solution)/shard_map/down/pallas_call | solution.py:227
  67.7 1.7 %collective-permute-start.19 = (bf16[64,768]{1,0:T(8,128)(2,1)S(1)}, bf16[64,768]{1,0:T(8,128)(2,1)S(1)}, u32[]{:S(2)}, u32[]{:S(2)}) collective-permute-start(bf16[64,768]{1,0:T(8,128)(2,1)S(1)} %get-tuple-element.84), channel_id=1, source_target_pairs={{0,3},{1,2},{2,1},{3,0},{4,7},{5,6},{6,5},{7,4},{8,11},{9,10},{10,... | collective-permute-start | bytes 294920 | tf_op jit(solution)/shard_map/ppermute | solution.py:293
  69.7 0.7 collective-permute-done.29.b_ref
  70.5 0.7 collective-permute-start.30
  71.2 1.3 %collective-permute-done.19.refs_3_ = bf16[64,768]{1,0:T(8,128)(2,1)S(1)} collective-permute-done((bf16[64,768]{1,0:T(8,128)(2,1)S(1)}, bf16[64,768]{1,0:T(8,128)(2,1)S(1)}, u32[]{:S(2)}, u32[]{:S(2)}) %collective-permute-start.19) | collective-permute-done | bytes 98336 | tf_op jit(solution)/shard_map/ppermute | solution.py:293
  72.5 2.4 %collective-permute-done.15.refs_5_.refs_2_ = bf16[64,768]{1,0:T(8,128)(2,1)S(1)} collective-permute-done((bf16[64,768]{1,0:T(8,128)(2,1)S(1)}, bf16[64,768]{1,0:T(8,128)(2,1)S(1)}, u32[]{:S(2)}, u32[]{:S(2)}) %collective-permute-start.15) | collective-permute-done | bytes 98336 | tf_op jit(solution)/shard_map/ppermute | solution.py:293
  75.3 1.5 %collective-permute-start.28 = (bf16[128,768]{1,0:T(8,128)(2,1)S(1)}, bf16[128,768]{1,0:T(8,128)(2,1)S(1)}, u32[]{:S(2)}, u32[]{:S(2)}) collective-permute-start(bf16[128,768]{1,0:T(8,128)(2,1)S(1)} %combine.6), channel_id=1, source_target_pairs={{0,4},{4,0},{8,12},{12,8},{1,5},{5,1},{9,13},{13,9},{2,6},{6,2},{1... | collective-permute-start | bytes 589832 | tf_op jit(solution)/shard_map/ppermute | solution.py:293
  76.8 1.3 %collective-permute-start.16 = (bf16[64,768]{1,0:T(8,128)(2,1)S(1)}, bf16[64,768]{1,0:T(8,128)(2,1)S(1)}, u32[]{:S(2)}, u32[]{:S(2)}) collective-permute-start(bf16[64,768]{1,0:T(8,128)(2,1)S(1)} %get-tuple-element.80), channel_id=1, source_target_pairs={{0,3},{1,2},{2,1},{3,0},{4,7},{5,6},{6,5},{7,4},{8,11},{9,10},{10,... | collective-permute-start | bytes 294920 | tf_op jit(solution)/shard_map/ppermute | solution.py:293
  78.1 3.1 %collective-permute-done.16.refs_3_ = bf16[64,768]{1,0:T(8,128)(2,1)S(1)} collective-permute-done((bf16[64,768]{1,0:T(8,128)(2,1)S(1)}, bf16[64,768]{1,0:T(8,128)(2,1)S(1)}, u32[]{:S(2)}, u32[]{:S(2)}) %collective-permute-start.16) | collective-permute-done | bytes 98336 | tf_op jit(solution)/shard_map/ppermute | solution.py:293
  81.2 0.5 collective-permute-done.28.refs_4_
  81.8 1.0 %combine.7 = bf16[128,768]{1,0:T(8,128)(2,1)} custom-call(bf16[256,256]{1,0:T(8,128)(2,1)S(1)} %get-tuple-element.50.pick_ref, f32[128,2]{1,0:T(8,128)S(1)} %get-tuple-element.51.mix_ref, bf16[64,768]{1,0:T(8,128)(2,1)S(1)} %get-tuple-element.77.refs_0_, bf16[64,768]{1,0:T(8,128)(2,1)S(1)} %collective-permute-done.14.refs_1_, ...), custom_call_target="tpu_custom_call" | custom-call | flops 100663296 | bytes 589824 | tf_op jit(solution)/shard_map/combine/pallas_call | solution.py:259
  (47 shorter events, 4.0 us)
Async XLA Ops:
  0.0 11.0 %collective-permute-start.3 = (bf16[128,768]{1,0:T(8,128)(2,1)}, bf16[128,768]{1,0:T(8,128)(2,1)S(1)}, u32[]{:S(2)}, u32[]{:S(2)}) collective-permute-start(bf16[128,768]{1,0:T(8,128)(2,1)} %refs_0_.6), channel_id=1, source_target_pairs={{4,8},{8,4},{5,9},{9,5},{6,10},{10,6},{7,11},{11,7},{20,24},{24,20... | collective-permute-start | bytes 589832 | tf_op jit(solution)/shard_map/ppermute | solution.py:297
  0.7 11.7 %collective-permute-start = (bf16[128,768]{1,0:T(8,128)(2,1)}, bf16[128,768]{1,0:T(8,128)(2,1)S(1)}, u32[]{:S(2)}, u32[]{:S(2)}) collective-permute-start(bf16[128,768]{1,0:T(8,128)(2,1)} %refs_0_.6), channel_id=1, source_target_pairs={{0,4},{4,0},{8,12},{12,8},{1,5},{5,1},{9,13},{13,9},{2,6},{6,2},{1... | collective-permute-start | bytes 589832 | tf_op jit(solution)/shard_map/ppermute | solution.py:293
  6.6 0.7 copy-start.1
  7.3 0.7 copy-start.2
  8.1 4.2 %copy-start = (bf16[128,768]{1,0:T(8,128)(2,1)S(1)}, bf16[128,768]{1,0:T(8,128)(2,1)}, u32[]{:S(2)}) copy-start(bf16[128,768]{1,0:T(8,128)(2,1)} %refs_0_.6) | copy-start | bytes 589828
  11.0 8.0 %collective-permute-start.4 = (bf16[128,768]{1,0:T(8,128)(2,1)S(1)}, bf16[128,768]{1,0:T(8,128)(2,1)S(1)}, u32[]{:S(2)}, u32[]{:S(2)}) collective-permute-start(bf16[128,768]{1,0:T(8,128)(2,1)S(1)} %collective-permute-done.3.refs_0_), channel_id=1, source_target_pairs={{4,0},{8,12},{5,1},{9,13},{6,2},{10,14},{7,3},{11,15},{20,16},{24,... | collective-permute-start | bytes 589832 | tf_op jit(solution)/shard_map/ppermute | solution.py:301
  12.7 7.3 %collective-permute-start.11 = (bf16[64,1536]{1,0:T(8,128)(2,1)S(1)}, bf16[64,1536]{1,0:T(8,128)(2,1)S(1)}, u32[]{:S(2)}, u32[]{:S(2)}) collective-permute-start(bf16[64,1536]{1,0:T(8,128)(2,1)S(1)} %get-tuple-element.68), channel_id=1, source_target_pairs={{0,1},{1,0},{2,3},{3,2},{4,5},{5,4},{6,7},{7,6},{8,9},{9,8},{10,11... | collective-permute-start | bytes 589832 | tf_op jit(solution)/shard_map/ppermute | solution.py:293
  12.8 8.2 %collective-permute-start.12 = (bf16[64,1536]{1,0:T(8,128)(2,1)S(1)}, bf16[64,1536]{1,0:T(8,128)(2,1)S(1)}, u32[]{:S(2)}, u32[]{:S(2)}) collective-permute-start(bf16[64,1536]{1,0:T(8,128)(2,1)S(1)} %get-tuple-element.69), channel_id=1, source_target_pairs={{0,2},{1,3},{2,0},{3,1},{4,6},{5,7},{6,4},{7,5},{8,10},{9,11},{10,... | collective-permute-start | bytes 589832 | tf_op jit(solution)/shard_map/ppermute | solution.py:293
  14.4 7.7 %collective-permute-start.1 = (bf16[128,768]{1,0:T(8,128)(2,1)S(1)}, bf16[128,768]{1,0:T(8,128)(2,1)S(1)}, u32[]{:S(2)}, u32[]{:S(2)}) collective-permute-start(bf16[128,768]{1,0:T(8,128)(2,1)S(1)} %collective-permute-done.refs_1_), channel_id=1, source_target_pairs={{4,8},{8,4},{5,9},{9,5},{6,10},{10,6},{7,11},{11,7},{20,24},{24,20... | collective-permute-start | bytes 589832 | tf_op jit(solution)/shard_map/ppermute | solution.py:297
  15.0 8.8 %collective-permute-start.13 = (bf16[64,1536]{1,0:T(8,128)(2,1)S(1)}, bf16[64,1536]{1,0:T(8,128)(2,1)S(1)}, u32[]{:S(2)}, u32[]{:S(2)}) collective-permute-start(bf16[64,1536]{1,0:T(8,128)(2,1)S(1)} %get-tuple-element.70), channel_id=1, source_target_pairs={{0,3},{1,2},{2,1},{3,0},{4,7},{5,6},{6,5},{7,4},{8,11},{9,10},{10,... | collective-permute-start | bytes 589832 | tf_op jit(solution)/shard_map/ppermute | solution.py:293
  19.3 14.1 %collective-permute-start.10 = (bf16[64,768]{1,0:T(8,128)(2,1)S(1)}, bf16[64,768]{1,0:T(8,128)(2,1)S(1)}, u32[]{:S(2)}, u32[]{:S(2)}) collective-permute-start(bf16[64,768]{1,0:T(8,128)(2,1)S(1)} %get-tuple-element.66), channel_id=1, source_target_pairs={{0,3},{1,2},{2,1},{3,0},{4,7},{5,6},{6,5},{7,4},{8,11},{9,10},{10,... | collective-permute-start | bytes 294920 | tf_op jit(solution)/shard_map/ppermute | solution.py:293
  20.1 13.7 %collective-permute-start.8 = (bf16[64,768]{1,0:T(8,128)(2,1)S(1)}, bf16[64,768]{1,0:T(8,128)(2,1)S(1)}, u32[]{:S(2)}, u32[]{:S(2)}) collective-permute-start(bf16[64,768]{1,0:T(8,128)(2,1)S(1)} %get-tuple-element.64), channel_id=1, source_target_pairs={{0,1},{1,0},{2,3},{3,2},{4,5},{5,4},{6,7},{7,6},{8,9},{9,8},{10,11... | collective-permute-start | bytes 294920 | tf_op jit(solution)/shard_map/ppermute | solution.py:293
  21.0 12.8 %collective-permute-start.9 = (bf16[64,768]{1,0:T(8,128)(2,1)S(1)}, bf16[64,768]{1,0:T(8,128)(2,1)S(1)}, u32[]{:S(2)}, u32[]{:S(2)}) collective-permute-start(bf16[64,768]{1,0:T(8,128)(2,1)S(1)} %get-tuple-element.65), channel_id=1, source_target_pairs={{0,2},{1,3},{2,0},{3,1},{4,6},{5,7},{6,4},{7,5},{8,10},{9,11},{10,... | collective-permute-start | bytes 294920 | tf_op jit(solution)/shard_map/ppermute | solution.py:293
  22.1 9.5 %collective-permute-start.2 = (bf16[128,768]{1,0:T(8,128)(2,1)S(1)}, bf16[128,768]{1,0:T(8,128)(2,1)S(1)}, u32[]{:S(2)}, u32[]{:S(2)}) collective-permute-start(bf16[128,768]{1,0:T(8,128)(2,1)S(1)} %collective-permute-done.1.refs_0_), channel_id=1, source_target_pairs={{4,0},{8,12},{5,1},{9,13},{6,2},{10,14},{7,3},{11,15},{20,16},{24,... | collective-permute-start | bytes 589832 | tf_op jit(solution)/shard_map/ppermute | solution.py:301
  31.8 7.1 %collective-permute-start.5 = (bf16[64,768]{1,0:T(8,128)(2,1)S(1)}, bf16[64,768]{1,0:T(8,128)(2,1)S(1)}, u32[]{:S(2)}, u32[]{:S(2)}) collective-permute-start(bf16[64,768]{1,0:T(8,128)(2,1)S(1)} %get-tuple-element.59), channel_id=1, source_target_pairs={{0,1},{1,0},{2,3},{3,2},{4,5},{5,4},{6,7},{7,6},{8,9},{9,8},{10,11... | collective-permute-start | bytes 294920 | tf_op jit(solution)/shard_map/ppermute | solution.py:293
  31.9 7.1 %collective-permute-start.6 = (bf16[64,768]{1,0:T(8,128)(2,1)S(1)}, bf16[64,768]{1,0:T(8,128)(2,1)S(1)}, u32[]{:S(2)}, u32[]{:S(2)}) collective-permute-start(bf16[64,768]{1,0:T(8,128)(2,1)S(1)} %get-tuple-element.60), channel_id=1, source_target_pairs={{0,2},{1,3},{2,0},{3,1},{4,6},{5,7},{6,4},{7,5},{8,10},{9,11},{10,... | collective-permute-start | bytes 294920 | tf_op jit(solution)/shard_map/ppermute | solution.py:293
  33.4 5.5 %collective-permute-start.7 = (bf16[64,768]{1,0:T(8,128)(2,1)S(1)}, bf16[64,768]{1,0:T(8,128)(2,1)S(1)}, u32[]{:S(2)}, u32[]{:S(2)}) collective-permute-start(bf16[64,768]{1,0:T(8,128)(2,1)S(1)} %get-tuple-element.61), channel_id=1, source_target_pairs={{0,3},{1,2},{2,1},{3,0},{4,7},{5,6},{6,5},{7,4},{8,11},{9,10},{10,... | collective-permute-start | bytes 294920 | tf_op jit(solution)/shard_map/ppermute | solution.py:293
  33.8 7.3 %slice-start = ((s8[12582912]{0:T(1024)(128)(4,1)}), s8[4194304]{0:T(1024)(128)(4,1)S(1)}, s32[]{:S(2)}) async-start(s8[12582912]{0:T(1024)(128)(4,1)} %bitcast.4), calls=%async_computation | async-start | bytes 8388608
  35.9 5.2 %slice-start.1 = ((s8[12582912]{0:T(1024)(128)(4,1)}), s8[4194304]{0:T(1024)(128)(4,1)S(1)}, s32[]{:S(2)}) async-start(s8[12582912]{0:T(1024)(128)(4,1)} %bitcast.4), calls=%async_computation.1 | async-start | bytes 8388608
  35.9 5.2 %slice-start.2 = ((s8[12582912]{0:T(1024)(128)(4,1)}), s8[4194304]{0:T(1024)(128)(4,1)S(1)}, s32[]{:S(2)}) async-start(s8[12582912]{0:T(1024)(128)(4,1)} %bitcast.4), calls=%async_computation.2 | async-start | bytes 8388608
  43.2 5.6 %collective-permute-start.21 = (bf16[64,768]{1,0:T(8,128)(2,1)S(1)}, bf16[64,768]{1,0:T(8,128)(2,1)S(1)}, u32[]{:S(2)}, u32[]{:S(2)}) collective-permute-start(bf16[64,768]{1,0:T(8,128)(2,1)S(1)} %get-tuple-element.87), channel_id=1, source_target_pairs={{0,2},{1,3},{2,0},{3,1},{4,6},{5,7},{6,4},{7,5},{8,10},{9,11},{10,... | collective-permute-start | bytes 294920 | tf_op jit(solution)/shard_map/ppermute | solution.py:293
  44.7 4.1 %collective-permute-start.23 = (bf16[64,768]{1,0:T(8,128)(2,1)S(1)}, bf16[64,768]{1,0:T(8,128)(2,1)S(1)}, u32[]{:S(2)}, u32[]{:S(2)}) collective-permute-start(bf16[64,768]{1,0:T(8,128)(2,1)S(1)} %get-tuple-element.90), channel_id=1, source_target_pairs={{0,1},{1,0},{2,3},{3,2},{4,5},{5,4},{6,7},{7,6},{8,9},{9,8},{10,11... | collective-permute-start | bytes 294920 | tf_op jit(solution)/shard_map/ppermute | solution.py:293
  44.8 6.1 %collective-permute-start.24 = (bf16[64,768]{1,0:T(8,128)(2,1)S(1)}, bf16[64,768]{1,0:T(8,128)(2,1)S(1)}, u32[]{:S(2)}, u32[]{:S(2)}) collective-permute-start(bf16[64,768]{1,0:T(8,128)(2,1)S(1)} %get-tuple-element.91), channel_id=1, source_target_pairs={{0,2},{1,3},{2,0},{3,1},{4,6},{5,7},{6,4},{7,5},{8,10},{9,11},{10,... | collective-permute-start | bytes 294920 | tf_op jit(solution)/shard_map/ppermute | solution.py:293
  45.4 6.7 %collective-permute-start.25 = (bf16[64,768]{1,0:T(8,128)(2,1)S(1)}, bf16[64,768]{1,0:T(8,128)(2,1)S(1)}, u32[]{:S(2)}, u32[]{:S(2)}) collective-permute-start(bf16[64,768]{1,0:T(8,128)(2,1)S(1)} %get-tuple-element.92), channel_id=1, source_target_pairs={{0,3},{1,2},{2,1},{3,0},{4,7},{5,6},{6,5},{7,4},{8,11},{9,10},{10,... | collective-permute-start | bytes 294920 | tf_op jit(solution)/shard_map/ppermute | solution.py:293
  52.3 11.4 %collective-permute-start.26 = (bf16[128,768]{1,0:T(8,128)(2,1)S(1)}, bf16[128,768]{1,0:T(8,128)(2,1)S(1)}, u32[]{:S(2)}, u32[]{:S(2)}) collective-permute-start(bf16[128,768]{1,0:T(8,128)(2,1)S(1)} %combine.4.a_ref), channel_id=1, source_target_pairs={{0,4},{12,8},{1,5},{13,9},{2,6},{14,10},{3,7},{15,11},{16,20},{28,... | collective-permute-start | bytes 589832 | tf_op jit(solution)/shard_map/ppermute | solution.py:305
  57.4 5.0 %collective-permute-start.18 = (bf16[64,768]{1,0:T(8,128)(2,1)S(1)}, bf16[64,768]{1,0:T(8,128)(2,1)S(1)}, u32[]{:S(2)}, u32[]{:S(2)}) collective-permute-start(bf16[64,768]{1,0:T(8,128)(2,1)S(1)} %get-tuple-element.83), channel_id=1, source_target_pairs={{0,2},{1,3},{2,0},{3,1},{4,6},{5,7},{6,4},{7,5},{8,10},{9,11},{10,... | collective-permute-start | bytes 294920 | tf_op jit(solution)/shard_map/ppermute | solution.py:293
  59.3 3.1 %collective-permute-start.20 = (bf16[64,768]{1,0:T(8,128)(2,1)S(1)}, bf16[64,768]{1,0:T(8,128)(2,1)S(1)}, u32[]{:S(2)}, u32[]{:S(2)}) collective-permute-start(bf16[64,768]{1,0:T(8,128)(2,1)S(1)} %get-tuple-element.86), channel_id=1, source_target_pairs={{0,1},{1,0},{2,3},{3,2},{4,5},{5,4},{6,7},{7,6},{8,9},{9,8},{10,11... | collective-permute-start | bytes 294920 | tf_op jit(solution)/shard_map/ppermute | solution.py:293
  59.3 4.4 %collective-permute-start.22 = (bf16[64,768]{1,0:T(8,128)(2,1)S(1)}, bf16[64,768]{1,0:T(8,128)(2,1)S(1)}, u32[]{:S(2)}, u32[]{:S(2)}) collective-permute-start(bf16[64,768]{1,0:T(8,128)(2,1)S(1)} %get-tuple-element.88), channel_id=1, source_target_pairs={{0,3},{1,2},{2,1},{3,0},{4,7},{5,6},{6,5},{7,4},{8,11},{9,10},{10,... | collective-permute-start | bytes 294920 | tf_op jit(solution)/shard_map/ppermute | solution.py:293
  64.1 6.4 %collective-permute-start.29 = (bf16[128,768]{1,0:T(8,128)(2,1)S(1)}, bf16[128,768]{1,0:T(8,128)(2,1)S(1)}, u32[]{:S(2)}, u32[]{:S(2)}) collective-permute-start(bf16[128,768]{1,0:T(8,128)(2,1)S(1)} %get-tuple-element.94), channel_id=1, source_target_pairs={{0,4},{12,8},{1,5},{13,9},{2,6},{14,10},{3,7},{15,11},{16,20},{28,... | collective-permute-start | bytes 589832 | tf_op jit(solution)/shard_map/ppermute | solution.py:305
  65.7 9.2 %collective-permute-start.27 = (bf16[128,768]{1,0:T(8,128)(2,1)S(1)}, bf16[128,768]{1,0:T(8,128)(2,1)S(1)}, u32[]{:S(2)}, u32[]{:S(2)}) collective-permute-start(bf16[128,768]{1,0:T(8,128)(2,1)S(1)} %get-tuple-element.93), channel_id=1, source_target_pairs={{4,8},{8,4},{5,9},{9,5},{6,10},{10,6},{7,11},{11,7},{20,24},{24,20... | collective-permute-start | bytes 589832 | tf_op jit(solution)/shard_map/ppermute | solution.py:297
  66.4 4.8 %collective-permute-start.17 = (bf16[64,768]{1,0:T(8,128)(2,1)S(1)}, bf16[64,768]{1,0:T(8,128)(2,1)S(1)}, u32[]{:S(2)}, u32[]{:S(2)}) collective-permute-start(bf16[64,768]{1,0:T(8,128)(2,1)S(1)} %get-tuple-element.82), channel_id=1, source_target_pairs={{0,1},{1,0},{2,3},{3,2},{4,5},{5,4},{6,7},{7,6},{8,9},{9,8},{10,11... | collective-permute-start | bytes 294920 | tf_op jit(solution)/shard_map/ppermute | solution.py:293
  67.7 4.8 %collective-permute-start.19 = (bf16[64,768]{1,0:T(8,128)(2,1)S(1)}, bf16[64,768]{1,0:T(8,128)(2,1)S(1)}, u32[]{:S(2)}, u32[]{:S(2)}) collective-permute-start(bf16[64,768]{1,0:T(8,128)(2,1)S(1)} %get-tuple-element.84), channel_id=1, source_target_pairs={{0,3},{1,2},{2,1},{3,0},{4,7},{5,6},{6,5},{7,4},{8,11},{9,10},{10,... | collective-permute-start | bytes 294920 | tf_op jit(solution)/shard_map/ppermute | solution.py:293
  69.4 5.6 %collective-permute-start.15 = (bf16[64,768]{1,0:T(8,128)(2,1)S(1)}, bf16[64,768]{1,0:T(8,128)(2,1)S(1)}, u32[]{:S(2)}, u32[]{:S(2)}) collective-permute-start(bf16[64,768]{1,0:T(8,128)(2,1)S(1)} %get-tuple-element.79), channel_id=1, source_target_pairs={{0,2},{1,3},{2,0},{3,1},{4,6},{5,7},{6,4},{7,5},{8,10},{9,11},{10,... | collective-permute-start | bytes 294920 | tf_op jit(solution)/shard_map/ppermute | solution.py:293
  70.5 10.7 %collective-permute-start.30 = (bf16[128,768]{1,0:T(8,128)(2,1)S(1)}, bf16[128,768]{1,0:T(8,128)(2,1)S(1)}, u32[]{:S(2)}, u32[]{:S(2)}) collective-permute-start(bf16[128,768]{1,0:T(8,128)(2,1)S(1)} %add.1), channel_id=1, source_target_pairs={{4,8},{8,4},{5,9},{9,5},{6,10},{10,6},{7,11},{11,7},{20,24},{24,20... | collective-permute-start | bytes 589832 | tf_op jit(solution)/shard_map/ppermute | solution.py:297
  75.3 6.5 %collective-permute-start.28 = (bf16[128,768]{1,0:T(8,128)(2,1)S(1)}, bf16[128,768]{1,0:T(8,128)(2,1)S(1)}, u32[]{:S(2)}, u32[]{:S(2)}) collective-permute-start(bf16[128,768]{1,0:T(8,128)(2,1)S(1)} %combine.6), channel_id=1, source_target_pairs={{0,4},{4,0},{8,12},{12,8},{1,5},{5,1},{9,13},{13,9},{2,6},{6,2},{1... | collective-permute-start | bytes 589832 | tf_op jit(solution)/shard_map/ppermute | solution.py:293
  76.8 1.3 %collective-permute-start.14 = (bf16[64,768]{1,0:T(8,128)(2,1)S(1)}, bf16[64,768]{1,0:T(8,128)(2,1)S(1)}, u32[]{:S(2)}, u32[]{:S(2)}) collective-permute-start(bf16[64,768]{1,0:T(8,128)(2,1)S(1)} %get-tuple-element.78), channel_id=1, source_target_pairs={{0,1},{1,0},{2,3},{3,2},{4,5},{5,4},{6,7},{7,6},{8,9},{9,8},{10,11... | collective-permute-start | bytes 294920 | tf_op jit(solution)/shard_map/ppermute | solution.py:293
  76.8 4.4 %collective-permute-start.16 = (bf16[64,768]{1,0:T(8,128)(2,1)S(1)}, bf16[64,768]{1,0:T(8,128)(2,1)S(1)}, u32[]{:S(2)}, u32[]{:S(2)}) collective-permute-start(bf16[64,768]{1,0:T(8,128)(2,1)S(1)} %get-tuple-element.80), channel_id=1, source_target_pairs={{0,3},{1,2},{2,1},{3,0},{4,7},{5,6},{6,5},{7,4},{8,11},{9,10},{10,... | collective-permute-start | bytes 294920 | tf_op jit(solution)/shard_map/ppermute | solution.py:293

commit v8 on v7

--- a/solution.py
+++ b/solution.py
@@ -71,50 +71,36 @@
     )(me.reshape(1), expert_ids.T, route_logits.T)
 
 
-def dispatch_kernel(placed_ref, *refs, counts, waits):
-    inputs, outputs = refs[: sum(counts)], refs[sum(counts) + waits :]
+def dispatch_kernel(placed_ref, *refs, count, waits):
+    inputs, outputs = refs[:count], refs[count + waits :]
     capacity, wide = outputs[0].shape
-    width = wide // len(counts)
-    for i, count in enumerate(counts):
-        block = inputs[sum(counts[:i])][...]
-        for j in range(1, count):
-            block = block + inputs[sum(counts[:i]) + j][...]
+    width = wide // count
+    for i, block in enumerate(inputs):
         for d, out in enumerate(outputs):
             out[:, i * width : (i + 1) * width] = jnp.dot(
                 placed_ref[d * capacity : (d + 1) * capacity, :],
-                block,
+                block[...],
                 preferred_element_type=F32,
             ).astype(BF16)
 
 
 def dispatch(placed, slices, experts, capacity, after):
-    rows, width = slices[0][0].shape
+    rows, width = slices[0].shape
     wide = width * len(slices)
-    arrays = [array for arrays in slices for array in arrays]
-    return pl.pallas_call(
-        functools.partial(
-            dispatch_kernel, counts=[len(arrays) for arrays in slices], waits=len(after)
-        ),
+    return pl.pallas_call(
+        functools.partial(dispatch_kernel, count=len(slices), waits=len(after)),
         out_shape=[jax.ShapeDtypeStruct((capacity, wide), BF16)] * experts,
-        in_specs=[pl.BlockSpec(memory_space=pltpu.VMEM)] * (1 + len(arrays))
+        in_specs=[pl.BlockSpec(memory_space=pltpu.VMEM)] * (1 + len(slices))
         + [pl.BlockSpec(memory_space=pl.ANY)] * len(after),
         out_specs=[pl.BlockSpec(memory_space=pltpu.VMEM)] * experts,
         cost_estimate=cost(2 * experts * capacity * rows * wide, 6 * rows * wide),
         compiler_params=params(),
         name="dispatch",
-    )(placed, *arrays, *pinned(after))
+    )(placed, *slices, *pinned(after))
 
 
 def across(distance):
     return lambda column: lax.bitwise_xor(column, distance)
-
-
-def second(column):
-    return jnp.where(column < 2, 2, 1)
-
-
-def third(column):
-    return jnp.where(column < 2, 3, 0)
 
 
 def everything(column):
@@ -151,13 +137,14 @@
     )(column.reshape(1), after, *sources)
 
 
-def gate_up_kernel(*refs, experts, slices, first, last):
+def gate_up_kernel(*refs, experts, slices, first, last, waits):
     x_refs = refs[:experts]
     weights = refs[experts : experts + 2 * slices]
     rest = refs[experts + 2 * slices :]
     if not first:
         old_gate, old_up = rest[:2]
         rest = rest[2:]
+    rest = rest[waits:]
     x = jnp.concatenate([r[...] for r in x_refs], axis=0)
     width, hidden = weights[0].shape
     tile = min(512, hidden)
@@ -182,7 +169,7 @@
             rest[1][:, columns] = up
 
 
-def gate_up(x_blocks, weights, sums, last):
+def gate_up(x_blocks, weights, sums, last, after):
     experts = len(x_blocks)
     rows = experts * x_blocks[0].shape[0]
     hidden = weights[0].shape[1]
@@ -195,10 +182,16 @@
         out_shape = [pltpu.VMEM((rows, hidden), F32)] * 2
     return pl.pallas_call(
         functools.partial(
-            gate_up_kernel, experts=experts, slices=len(weights) // 2, first=first, last=last
+            gate_up_kernel,
+            experts=experts,
+            slices=len(weights) // 2,
+            first=first,
+            last=last,
+            waits=len(after),
         ),
         out_shape=out_shape,
-        in_specs=[pl.BlockSpec(memory_space=pltpu.VMEM)] * (before + len(old)),
+        in_specs=[pl.BlockSpec(memory_space=pltpu.VMEM)] * (before + len(old))
+        + [pl.BlockSpec(memory_space=pl.ANY)] * len(after),
         out_specs=[pl.BlockSpec(memory_space=pltpu.VMEM)] * len(out_shape),
         input_output_aliases={} if first or last else {before: 0, before + 1: 1},
         cost_estimate=cost(
@@ -207,10 +200,11 @@
         ),
         compiler_params=params(),
         name="gate_up",
-    )(*x_blocks, *pinned(weights), *old)
-
-
-def down_kernel(column_ref, h_ref, w_ref, *out_refs, part):
+    )(*x_blocks, *pinned(weights), *old, *after)
+
+
+def down_kernel(column_ref, h_ref, w_ref, *refs, part, waits):
+    out_refs = refs[waits:]
     capacity, width = out_refs[0].shape
     tile = min(256, width)
     for n in range(width // tile):
@@ -221,69 +215,49 @@
             out[:, columns] = y[d * capacity : (d + 1) * capacity].astype(BF16)
 
 
-def down(column, part, hidden, down_w, width, experts):
+def down(column, part, hidden, down_w, width, experts, after):
     rows, depth = hidden.shape
     capacity = rows // experts
     return pl.pallas_call(
-        functools.partial(down_kernel, part=part),
+        functools.partial(down_kernel, part=part, waits=len(after)),
         out_shape=[jax.ShapeDtypeStruct((capacity, width), BF16)] * experts,
         in_specs=[pl.BlockSpec(memory_space=pltpu.SMEM)]
-        + [pl.BlockSpec(memory_space=pltpu.VMEM)] * 2,
+        + [pl.BlockSpec(memory_space=pltpu.VMEM)] * 2
+        + [pl.BlockSpec(memory_space=pl.ANY)] * len(after),
         out_specs=[pl.BlockSpec(memory_space=pltpu.VMEM)] * experts,
         cost_estimate=cost(2 * rows * depth * width, 2 * depth * width + 2 * rows * width),
         compiler_params=params(),
         name="down",
-    )(column.reshape(1), *pinned([hidden, down_w]))
-
-
-def combine_kernel(pick_ref, mix_ref, *refs, experts, sums, plain):
-    outs = refs[len(refs) - 1 - plain :]
-    y_refs, added = refs[:experts], refs[experts : experts + sums]
-    rows = outs[0].shape[0]
+    )(column.reshape(1), *pinned([hidden, down_w]), *after)
+
+
+def combine_kernel(pick_ref, mix_ref, *refs, experts, sums):
+    y_refs, added, out = refs[:experts], refs[experts : experts + sums], refs[-1]
+    rows = out.shape[0]
     y = jnp.concatenate([r[...] for r in y_refs], axis=0)
     picked = lax.dot_general(
         pick_ref[...], y, (((0,), (0,)), ((), ())), preferred_element_type=F32
     )
     mixed = picked[:rows] * mix_ref[:, 0:1] + picked[rows:] * mix_ref[:, 1:2]
-    if plain:
-        outs[1][...] = mixed.astype(BF16)
     for other in added:
         mixed = mixed + other[...].astype(F32)
-    outs[0][...] = mixed.astype(BF16)
-
-
-def combine(pick, mix, blocks, added, after=(), plain=False):
+    out[...] = mixed.astype(BF16)
+
+
+def combine(pick, mix, blocks, added, after=()):
     rows = mix.shape[0]
     width = blocks[0].shape[1]
     operands = 2 + len(blocks) + len(added)
     return pl.pallas_call(
-        functools.partial(
-            combine_kernel, experts=len(blocks), sums=len(added), plain=plain
-        ),
-        out_shape=[jax.ShapeDtypeStruct((rows, width), BF16)] * (1 + plain),
+        functools.partial(combine_kernel, experts=len(blocks), sums=len(added)),
+        out_shape=jax.ShapeDtypeStruct((rows, width), BF16),
         in_specs=[pl.BlockSpec(memory_space=pltpu.VMEM)] * operands
         + [pl.BlockSpec(memory_space=pl.ANY)] * len(after),
-        out_specs=[pl.BlockSpec(memory_space=pltpu.VMEM)] * (1 + plain),
+        out_specs=pl.BlockSpec(memory_space=pltpu.VMEM),
         cost_estimate=cost(4 * rows * pick.shape[0] * width, 6 * rows * width),
         compiler_params=params(),
         name="combine",
     )(pick, mix, *blocks, *added, *after)
-
-
-def add_kernel(a_ref, b_ref, out_ref):
-    out_ref[...] = (a_ref[...].astype(F32) + b_ref[...].astype(F32)).astype(BF16)
-
-
-def add(a, b):
-    return pl.pallas_call(
-        add_kernel,
-        out_shape=jax.ShapeDtypeStruct(a.shape, BF16),
-        in_specs=[pl.BlockSpec(memory_space=pltpu.VMEM)] * 2,
-        out_specs=pl.BlockSpec(memory_space=pltpu.VMEM),
-        cost_estimate=cost(a.size, 6 * a.size),
-        compiler_params=params(),
-        name="add",
-    )(a, b)
 
 
 def swap(value, axis, distance):
@@ -291,18 +265,6 @@
         return value
     count = lax.axis_size(axis)
     return lax.ppermute(value, axis, [(i, i ^ distance) for i in range(count)])
-
-
-def middle(value):
-    return lax.ppermute(value, "tensor", [(1, 2), (2, 1)])
-
-
-def outwards(value):
-    return lax.ppermute(value, "tensor", [(1, 0), (2, 3)])
-
-
-def inwards(value):
-    return lax.ppermute(value, "tensor", [(0, 1), (3, 2)])
 
 
 def per_device(tokens, expert_ids, route_logits, gate_weight, up_weight, down_weight):
@@ -312,54 +274,51 @@
     capacity = rows // 2
     me = lax.axis_index("expert").astype(jnp.int32)
     column = lax.axis_index("tensor").astype(jnp.int32)
-    line = shards == 4
-    width = own_width if line else own_width * shards
-
-    if line:
-        beside = swap(tokens, "tensor", 1)
-        near = middle(tokens)
-        far = middle(beside)
-        parts = [across(0), across(1), second, third]
-        slices = [[tokens], [beside], [near, outwards(near)], [far, outwards(far)]]
+    doubling = shards == 4
+    width = own_width if doubling else own_width * shards
+
+    if doubling:
+        across_two = swap(tokens, "tensor", 2)
+        slices = [tokens, swap(tokens, "tensor", 1), across_two, swap(across_two, "tensor", 1)]
+        parts = [across(distance) for distance in range(4)]
         groups = [[0, 1], [2], [3]]
     else:
+        slices = [lax.all_gather(tokens, "tensor", axis=1, tiled=True)]
         parts = [everything]
-        slices = [[lax.all_gather(tokens, "tensor", axis=1, tiled=True)]]
         groups = [[0]]
     placed, pick, mix = place(me, expert_ids, route_logits, experts, capacity)
 
-    weights, arrived, ready = [], [], placed
-    for i, part in enumerate(parts):
-        fetches = [(w, part, width) for w in (gate_weight, up_weight)]
-        weights.append(list(prefetch(column, fetches, ready)))
-        if i < len(groups):
-            chosen = [slices[j] for j in groups[i]]
-            outgoing = dispatch(placed, chosen, experts, capacity, weights[-1][:1])
-            arrived.append([swap(block, "expert", e) for e, block in enumerate(outgoing)])
-            ready = outgoing[0]
-
+    def fetch(chosen, after):
+        fetches = [(w, parts[i], width) for i in chosen for w in (gate_weight, up_weight)]
+        return list(prefetch(column, fetches, after))
+
+    weights, arrived = fetch(groups[0], placed), []
+    for group in groups:
+        after = weights[-1:] if len(arrived) < 2 else []
+        outgoing = dispatch(placed, [slices[i] for i in group], experts, capacity, after)
+        arrived.append([swap(block, "expert", e) for e, block in enumerate(outgoing)])
+        if len(arrived) == 1 and len(groups) > 1:
+            weights += fetch([2, 3], outgoing[0])
     sums = None
     for group, x_blocks in zip(groups, arrived):
-        chosen = [w for j in group for w in weights[j]]
-        sums = gate_up(x_blocks, chosen, sums, group is groups[-1])
+        chosen = weights[2 * group[0] : 2 * group[-1] + 2]
+        after = arrived[1][1:2] if sums is None and len(groups) > 1 else []
+        sums = gate_up(x_blocks, chosen, sums, group is groups[-1], after)
     hidden = sums[0]
 
-    def returned(part):
-        terms = down(column, part, hidden, down_weight, width, experts)
+    def returned(part, after=()):
+        terms = down(column, part, hidden, down_weight, width, experts, after)
         return [swap(block, "expert", e) for e, block in enumerate(terms)]
 
-    if not line:
-        mixed = combine(pick, mix, returned(everything), [])[0]
+    if not doubling:
+        mixed = combine(pick, mix, returned(everything), [])
         return lax.psum_scatter(mixed, "tensor", scatter_dimension=1, tiled=True)
-    blocks = [returned(across(distance)) for distance in range(4)]
-    last = combine(pick, mix, blocks[3], [], after=blocks[2][2:3])[0]
-    from_end = inwards(last)
-    onwards, alone = combine(pick, mix, blocks[2], [from_end], after=blocks[1][2:3], plain=True)
-    over = middle(onwards)
-    crossing = middle(add(last, inwards(alone)))
-    next_to = combine(pick, mix, blocks[1], [over], after=blocks[0][2:3])[0]
-    beside = swap(next_to, "tensor", 1)
-    return combine(pick, mix, blocks[0], [beside, crossing])[0]
+    blocks = [returned(across(3)), returned(across(2))]
+    passed = swap(combine(pick, mix, blocks[0], [], blocks[1][2:3]), "tensor", 1)
+    onwards = combine(pick, mix, blocks[1], [passed])
+    over = swap(onwards, "tensor", 2)
+    beside = swap(combine(pick, mix, returned(across(1), [onwards]), []), "tensor", 1)
+    return combine(pick, mix, returned(across(0), [onwards]), [beside, over])
 
 
 def solution(mesh):

time: 83.1 us -> 75.3 us (0.906)
  starting transfers between devices: 34.2 us -> 27.3 us
  Pallas kernels: 26.4 us -> 24.2 us
  waiting for transfers between devices: 20.4 us -> 21.9 us
    ppermute x8 -> x0, starting transfers between devices: 10.9 us -> none  [the longest x2 5.65 us: inwards(): return lax.ppermute(value, 'tensor', [(0, 1), (3, 2)])]
    ppermute x23 -> x27, waiting for transfers between devices: 17.6 us -> 21.9 us  [swap(): return lax.ppermute(value, axis, [(i, i ^ distance) for i in range(count)])]
    ppermute x23 -> x27, starting transfers between devices: 23.3 us -> 27.3 us  [swap(): return lax.ppermute(value, axis, [(i, i ^ distance) for i in range(count)])]
    ppermute x8 -> x0, waiting for transfers between devices: 2.86 us -> none  [the longest x2 2.11 us: outwards(): return lax.ppermute(value, 'tensor', [(1, 0), (2, 3)])]
    pallas_call x4 -> x2, Pallas kernels: 11.6 us -> 9.41 us  [prefetch(): pl.pallas_call(functools.partial(prefetch_kernel, parts=[part for _, part...]
    pallas_call x8 -> x7, Pallas kernels: 5.03 us -> 4.98 us  [the longest x4 4.1 us: down(): pl.pallas_call(functools.partial(down_kernel, part=part, waits=len(after)...]
  transfers between devices with their start and end apart: 31 -> 27, of which waited for: 13 -> 13; matrix products, arithmetic and copies ran while one was open for 0% -> 0% of each run, Pallas kernels for 25% -> 23%
where the time goes in v8:
time: 75.3 us; the launch traced here: 75.2 us
  starting transfers between devices  27.3 us (36%)
  Pallas kernels  24.2 us (32%)
  waiting for transfers between devices  21.9 us (29%)
  local copies, waits for them, and re-layouts  1.54 us (2%)
    ppermute x27, starting transfers between devices, swap(): return lax.ppermute(value, axis, [(i, i ^ distance) for i in range(count)])  27.3 us
    ppermute x27, waiting for transfers between devices, swap(): return lax.ppermute(value, axis, [(i, i ^ distance) for i in range(count)])  21.9 us
    pallas_call x2, Pallas kernels, prefetch(): pl.pallas_call(functools.partial(prefetch_kernel, parts=[part for _, part...  9.41 us
    pallas_call x3, Pallas kernels, gate_up(): pl.pallas_call(functools.partial(gate_up_kernel, experts=experts, slices=...  7.72 us
    pallas_call x4, Pallas kernels, down(): pl.pallas_call(functools.partial(down_kernel, part=part, waits=len(after)...  4.1 us
    pallas_call x4, Pallas kernels, combine(): pl.pallas_call(functools.partial(combine_kernel, experts=len(blocks), sum...  1.94 us
    unnamed x12, local copies, waits for them, and re-layouts  1.54 us
  transfers between devices with their start and end apart: 27, of which 13 were waited for; matrix products, arithmetic and copies ran while one was open for 0% of the time, Pallas kernels for 23%

profile of v8, /device:TPU:0, one launch (start us, length us, event | category | flops | bytes accessed | tf_op | source)
XLA Modules:
  0.0 75.2 jit_solution(9706080380418631707)
XLA Ops:
  0.0 4.0 %collective-permute-start = (bf16[128,768]{1,0:T(8,128)(2,1)}, bf16[128,768]{1,0:T(8,128)(2,1)S(1)}, u32[]{:S(2)}, u32[]{:S(2)}) collective-permute-start(bf16[128,768]{1,0:T(8,128)(2,1)} %refs_0_.4), channel_id=1, source_target_pairs={{0,8},{4,12},{8,0},{12,4},{1,9},{5,13},{9,1},{13,5},{2,10},{6,14},... | collective-permute-start | bytes 589832 | tf_op jit(solution)/shard_map/ppermute | solution.py:267
  4.0 1.6 %collective-permute-start.5 = (bf16[128,768]{1,0:T(8,128)(2,1)}, bf16[128,768]{1,0:T(8,128)(2,1)S(1)}, u32[]{:S(2)}, u32[]{:S(2)}) collective-permute-start(bf16[128,768]{1,0:T(8,128)(2,1)} %refs_0_.4), channel_id=1, source_target_pairs={{0,4},{4,0},{8,12},{12,8},{1,5},{5,1},{9,13},{13,9},{2,6},{6,2},{1... | collective-permute-start | bytes 589832 | tf_op jit(solution)/shard_map/ppermute | solution.py:267
  5.6 0.7 copy-done.1
  6.3 0.7 copy-done.2
  7.2 4.7 %prefetch.2 = (bf16[768,2048]{1,0:T(8,128)(2,1)S(1)}, bf16[768,2048]{1,0:T(8,128)(2,1)S(1)}, bf16[768,2048]{1,0:T(8,128)(2,1)S(1)}, bf16[768,2048]{1,0:T(8,128)(2,1)S(1)}) custom-call(s32[1]{0:T(128)} %bitcast.3.column_ref, bf16[256,128]{1,0:T(8,128)(2,1)S(1)} %get-tuple-element.50.placed_ref.after_ref, bf16[1,3072,2048]{2,1,0:T(8,128)(2,1)} %refs_2_.3, ...), custom_call_target="tpu_custom_call" | custom-call | bytes 12582912 | tf_op jit(solution)/shard_map/prefetch/pallas_call | solution.py:127
  11.9 1.6 %collective-permute-done.refs_0_ = bf16[128,768]{1,0:T(8,128)(2,1)S(1)} collective-permute-done((bf16[128,768]{1,0:T(8,128)(2,1)}, bf16[128,768]{1,0:T(8,128)(2,1)S(1)}, u32[]{:S(2)}, u32[]{:S(2)}) %collective-permute-start) | collective-permute-done | bytes 196640 | tf_op jit(solution)/shard_map/ppermute | solution.py:267
  13.5 0.7 collective-permute-start.1
  14.2 0.4 dispatch.4
  14.6 1.6 %collective-permute-start.10 = (bf16[64,1536]{1,0:T(8,128)(2,1)S(1)}, bf16[64,1536]{1,0:T(8,128)(2,1)S(1)}, u32[]{:S(2)}, u32[]{:S(2)}) collective-permute-start(bf16[64,1536]{1,0:T(8,128)(2,1)S(1)} %get-tuple-element.66), channel_id=1, source_target_pairs={{0,2},{1,3},{2,0},{3,1},{4,6},{5,7},{6,4},{7,5},{8,10},{9,11},{10,... | collective-permute-start | bytes 589832 | tf_op jit(solution)/shard_map/ppermute | solution.py:267
  16.1 0.6 collective-permute-start.9
  16.8 4.7 %prefetch.3 = (bf16[768,2048]{1,0:T(8,128)(2,1)S(1)}, bf16[768,2048]{1,0:T(8,128)(2,1)S(1)}, bf16[768,2048]{1,0:T(8,128)(2,1)S(1)}, bf16[768,2048]{1,0:T(8,128)(2,1)S(1)}) custom-call(s32[1]{0:T(128)} %bitcast.3.column_ref, bf16[64,1536]{1,0:T(8,128)(2,1)S(1)} %get-tuple-element.56.after_ref.refs_0_, bf16[1,3072,2048]{2,1,0:T(8,128)(2,1)} %refs_2_.3, ...), custom_call_target="tpu_custom_call" | custom-call | bytes 12582912 | tf_op jit(solution)/shard_map/prefetch/pallas_call | solution.py:127
  21.8 1.6 %collective-permute-start.7 = (bf16[64,768]{1,0:T(8,128)(2,1)S(1)}, bf16[64,768]{1,0:T(8,128)(2,1)S(1)}, u32[]{:S(2)}, u32[]{:S(2)}) collective-permute-start(bf16[64,768]{1,0:T(8,128)(2,1)S(1)} %get-tuple-element.61), channel_id=1, source_target_pairs={{0,2},{1,3},{2,0},{3,1},{4,6},{5,7},{6,4},{7,5},{8,10},{9,11},{10,... | collective-permute-start | bytes 294920 | tf_op jit(solution)/shard_map/ppermute | solution.py:267
  23.7 0.7 collective-permute-start.8
  24.4 0.4 collective-permute-start.2
  24.8 1.1 %collective-permute-start.3 = (bf16[64,768]{1,0:T(8,128)(2,1)S(1)}, bf16[64,768]{1,0:T(8,128)(2,1)S(1)}, u32[]{:S(2)}, u32[]{:S(2)}) collective-permute-start(bf16[64,768]{1,0:T(8,128)(2,1)S(1)} %get-tuple-element.53), channel_id=1, source_target_pairs={{0,2},{1,3},{2,0},{3,1},{4,6},{5,7},{6,4},{7,5},{8,10},{9,11},{10,... | collective-permute-start | bytes 294920 | tf_op jit(solution)/shard_map/ppermute | solution.py:267
  25.9 1.1 %collective-permute-start.4 = (bf16[64,768]{1,0:T(8,128)(2,1)S(1)}, bf16[64,768]{1,0:T(8,128)(2,1)S(1)}, u32[]{:S(2)}, u32[]{:S(2)}) collective-permute-start(bf16[64,768]{1,0:T(8,128)(2,1)S(1)} %get-tuple-element.54), channel_id=1, source_target_pairs={{0,3},{1,2},{2,1},{3,0},{4,7},{5,6},{6,5},{7,4},{8,11},{9,10},{10,... | collective-permute-start | bytes 294920 | tf_op jit(solution)/shard_map/ppermute | solution.py:267
  27.0 3.5 %gate_up.3 = (f32[256,2048]{1,0:T(8,128)S(1)}, f32[256,2048]{1,0:T(8,128)S(1)}) custom-call(bf16[64,1536]{1,0:T(8,128)(2,1)S(1)} %get-tuple-element.56.after_ref.refs_0_, bf16[64,1536]{1,0:T(8,128)(2,1)S(1)} %collective-permute-done.9.refs_1_, bf16[64,1536]{1,0:T(8,128)(2,1)S(1)} %collective-permute-done.10.refs_2_, ...), custom_call_target="tpu_custom_call" | custom-call | flops 3221225472 | bytes 12582912 | tf_op jit(solution)/shard_map/gate_up/pallas_call | solution.py:183
  30.5 2.1 %gate_up.4 = (f32[256,2048]{1,0:T(8,128)S(1)}, f32[256,2048]{1,0:T(8,128)S(1)}) custom-call(bf16[64,768]{1,0:T(8,128)(2,1)S(1)} %get-tuple-element.59.refs_0_, bf16[64,768]{1,0:T(8,128)(2,1)S(1)} %collective-permute-done.6.refs_8_.refs_1_, bf16[64,768]{1,0:T(8,128)(2,1)S(1)} %collective-permute-done.7.refs_2_, ...), custom_call_target="tpu_custom_call", output_to_operand_aliasing={{0}: (6, {}), {1}: (7, {})} | custom-call | flops 1610612736 | bytes 6291456 | tf_op jit(solution)/shard_map/gate_up/pallas_call | solution.py:183
  32.6 0.8 %collective-permute-done.4.refs_3_ = bf16[64,768]{1,0:T(8,128)(2,1)S(1)} collective-permute-done((bf16[64,768]{1,0:T(8,128)(2,1)S(1)}, bf16[64,768]{1,0:T(8,128)(2,1)S(1)}, u32[]{:S(2)}, u32[]{:S(2)}) %collective-permute-start.4) | collective-permute-done | bytes 98336 | tf_op jit(solution)/shard_map/ppermute | solution.py:267
  33.4 2.1 %gate_up.5.h_ref = bf16[256,2048]{1,0:T(8,128)(2,1)S(1)} custom-call(bf16[64,768]{1,0:T(8,128)(2,1)S(1)} %get-tuple-element.51.refs_0_, bf16[64,768]{1,0:T(8,128)(2,1)S(1)} %collective-permute-done.2.refs_1_, bf16[64,768]{1,0:T(8,128)(2,1)S(1)} %collective-permute-done.3.refs_2_, bf16[64,768]{1,0:T(8,128)(2,1)S(1)} %collective-permute-done.4.refs_3_, ...), custom_call_target="tpu_custom_call" | custom-call | flops 1610612736 | bytes 6291456 | tf_op jit(solution)/shard_map/gate_up/pallas_call | solution.py:183
  35.7 1.0 %down.5 = (bf16[64,768]{1,0:T(8,128)(2,1)S(1)}, bf16[64,768]{1,0:T(8,128)(2,1)S(1)}, bf16[64,768]{1,0:T(8,128)(2,1)S(1)}, bf16[64,768]{1,0:T(8,128)(2,1)S(1)}) custom-call(s32[1]{0:T(128)} %bitcast.3.column_ref, bf16[256,2048]{1,0:T(8,128)(2,1)S(1)} %gate_up.5.h_ref, bf16[1,2048,3072]{2,1,0:T(8,128)(2,1)S(1)} %bitcast.5), custom_call_target="tpu_custom_call" | custom-call | flops 805306368 | bytes 3538944 | tf_op jit(solution)/shard_map/down/pallas_call | solution.py:221
  36.8 1.0 %down.4 = (bf16[64,768]{1,0:T(8,128)(2,1)S(1)}, bf16[64,768]{1,0:T(8,128)(2,1)S(1)}, bf16[64,768]{1,0:T(8,128)(2,1)S(1)}, bf16[64,768]{1,0:T(8,128)(2,1)S(1)}) custom-call(s32[1]{0:T(128)} %bitcast.3.column_ref, bf16[256,2048]{1,0:T(8,128)(2,1)S(1)} %gate_up.5.h_ref, bf16[1,2048,3072]{2,1,0:T(8,128)(2,1)S(1)} %bitcast.5), custom_call_target="tpu_custom_call" | custom-call | flops 805306368 | bytes 3538944 | tf_op jit(solution)/shard_map/down/pallas_call | solution.py:221
  38.0 1.4 %collective-permute-start.16 = (bf16[64,768]{1,0:T(8,128)(2,1)S(1)}, bf16[64,768]{1,0:T(8,128)(2,1)S(1)}, u32[]{:S(2)}, u32[]{:S(2)}) collective-permute-start(bf16[64,768]{1,0:T(8,128)(2,1)S(1)} %get-tuple-element.81), channel_id=1, source_target_pairs={{0,2},{1,3},{2,0},{3,1},{4,6},{5,7},{6,4},{7,5},{8,10},{9,11},{10,... | collective-permute-start | bytes 294920 | tf_op jit(solution)/shard_map/ppermute | solution.py:267
  39.7 1.5 %collective-permute-start.13 = (bf16[64,768]{1,0:T(8,128)(2,1)S(1)}, bf16[64,768]{1,0:T(8,128)(2,1)S(1)}, u32[]{:S(2)}, u32[]{:S(2)}) collective-permute-start(bf16[64,768]{1,0:T(8,128)(2,1)S(1)} %get-tuple-element.77), channel_id=1, source_target_pairs={{0,2},{1,3},{2,0},{3,1},{4,6},{5,7},{6,4},{7,5},{8,10},{9,11},{10,... | collective-permute-start | bytes 294920 | tf_op jit(solution)/shard_map/ppermute | solution.py:267
  41.2 2.4 %collective-permute-done.16.refs_2_ = bf16[64,768]{1,0:T(8,128)(2,1)S(1)} collective-permute-done((bf16[64,768]{1,0:T(8,128)(2,1)S(1)}, bf16[64,768]{1,0:T(8,128)(2,1)S(1)}, u32[]{:S(2)}, u32[]{:S(2)}) %collective-permute-start.16) | collective-permute-done | bytes 98336 | tf_op jit(solution)/shard_map/ppermute | solution.py:267
  43.6 1.0 %collective-permute-done.17.refs_3_ = bf16[64,768]{1,0:T(8,128)(2,1)S(1)} collective-permute-done((bf16[64,768]{1,0:T(8,128)(2,1)S(1)}, bf16[64,768]{1,0:T(8,128)(2,1)S(1)}, u32[]{:S(2)}, u32[]{:S(2)}) %collective-permute-start.17) | collective-permute-done | bytes 98336 | tf_op jit(solution)/shard_map/ppermute | solution.py:267
  44.7 2.6 %collective-permute-done.13.refs_4_.refs_2_ = bf16[64,768]{1,0:T(8,128)(2,1)S(1)} collective-permute-done((bf16[64,768]{1,0:T(8,128)(2,1)S(1)}, bf16[64,768]{1,0:T(8,128)(2,1)S(1)}, u32[]{:S(2)}, u32[]{:S(2)}) %collective-permute-start.13) | collective-permute-done | bytes 98336 | tf_op jit(solution)/shard_map/ppermute | solution.py:267
  47.3 0.3 combine.4
  47.6 1.0 %collective-permute-start.18 = (bf16[128,768]{1,0:T(8,128)(2,1)S(1)}, bf16[128,768]{1,0:T(8,128)(2,1)S(1)}, u32[]{:S(2)}, u32[]{:S(2)}) collective-permute-start(bf16[128,768]{1,0:T(8,128)(2,1)S(1)} %combine.4), channel_id=1, source_target_pairs={{0,4},{4,0},{8,12},{12,8},{1,5},{5,1},{9,13},{13,9},{2,6},{6,2},{1... | collective-permute-start | bytes 589832 | tf_op jit(solution)/shard_map/ppermute | solution.py:267
  48.6 1.4 %collective-permute-start.14 = (bf16[64,768]{1,0:T(8,128)(2,1)S(1)}, bf16[64,768]{1,0:T(8,128)(2,1)S(1)}, u32[]{:S(2)}, u32[]{:S(2)}) collective-permute-start(bf16[64,768]{1,0:T(8,128)(2,1)S(1)} %get-tuple-element.78), channel_id=1, source_target_pairs={{0,3},{1,2},{2,1},{3,0},{4,7},{5,6},{6,5},{7,4},{8,11},{9,10},{10,... | collective-permute-start | bytes 294920 | tf_op jit(solution)/shard_map/ppermute | solution.py:267
  50.0 3.1 %collective-permute-done.14.refs_3_ = bf16[64,768]{1,0:T(8,128)(2,1)S(1)} collective-permute-done((bf16[64,768]{1,0:T(8,128)(2,1)S(1)}, bf16[64,768]{1,0:T(8,128)(2,1)S(1)}, u32[]{:S(2)}, u32[]{:S(2)}) %collective-permute-start.14) | collective-permute-done | bytes 98336 | tf_op jit(solution)/shard_map/ppermute | solution.py:267
  53.0 1.0 %collective-permute-done.18.refs_4_ = bf16[128,768]{1,0:T(8,128)(2,1)S(1)} collective-permute-done((bf16[128,768]{1,0:T(8,128)(2,1)S(1)}, bf16[128,768]{1,0:T(8,128)(2,1)S(1)}, u32[]{:S(2)}, u32[]{:S(2)}) %collective-permute-start.18) | collective-permute-done | bytes 196640 | tf_op jit(solution)/shard_map/ppermute | solution.py:267
  54.0 0.3 combine.5.refs_0_
  54.3 1.0 %down.7 = (bf16[64,768]{1,0:T(8,128)(2,1)S(1)}, bf16[64,768]{1,0:T(8,128)(2,1)S(1)}, bf16[64,768]{1,0:T(8,128)(2,1)S(1)}, bf16[64,768]{1,0:T(8,128)(2,1)S(1)}) custom-call(s32[1]{0:T(128)} %bitcast.3.column_ref, bf16[256,2048]{1,0:T(8,128)(2,1)S(1)} %gate_up.5.h_ref, bf16[1,2048,3072]{2,1,0:T(8,128)(2,1)S(1)} %bitcast.5, bf16[128,768]{1,0:T(8,128)(2,1)S(1)} %combine.5.refs_0_), custom_call_target="tpu_custom_call" | custom-call | flops 805306368 | bytes 3538944 | tf_op jit(solution)/shard_map/down/pallas_call | solution.py:221
  55.4 1.7 %collective-permute-start.23 = (bf16[64,768]{1,0:T(8,128)(2,1)S(1)}, bf16[64,768]{1,0:T(8,128)(2,1)S(1)}, u32[]{:S(2)}, u32[]{:S(2)}) collective-permute-start(bf16[64,768]{1,0:T(8,128)(2,1)S(1)} %get-tuple-element.89), channel_id=1, source_target_pairs={{0,2},{1,3},{2,0},{3,1},{4,6},{5,7},{6,4},{7,5},{8,10},{9,11},{10,... | collective-permute-start | bytes 294920 | tf_op jit(solution)/shard_map/ppermute | solution.py:267
  57.3 3.3 %collective-permute-start.26 = (bf16[128,768]{1,0:T(8,128)(2,1)S(1)}, bf16[128,768]{1,0:T(8,128)(2,1)S(1)}, u32[]{:S(2)}, u32[]{:S(2)}) collective-permute-start(bf16[128,768]{1,0:T(8,128)(2,1)S(1)} %combine.5.refs_0_), channel_id=1, source_target_pairs={{0,8},{4,12},{8,0},{12,4},{1,9},{5,13},{9,1},{13,5},{2,10},{6,14},... | collective-permute-start | bytes 589832 | tf_op jit(solution)/shard_map/ppermute | solution.py:267
  60.6 0.5 collective-permute-done.23.refs_2_
  61.1 1.2 %collective-permute-done.24.refs_3_ = bf16[64,768]{1,0:T(8,128)(2,1)S(1)} collective-permute-done((bf16[64,768]{1,0:T(8,128)(2,1)S(1)}, bf16[64,768]{1,0:T(8,128)(2,1)S(1)}, u32[]{:S(2)}, u32[]{:S(2)}) %collective-permute-start.24) | collective-permute-done | bytes 98336 | tf_op jit(solution)/shard_map/ppermute | solution.py:267
  62.3 0.3 combine.6
  62.6 1.0 %collective-permute-start.25 = (bf16[128,768]{1,0:T(8,128)(2,1)S(1)}, bf16[128,768]{1,0:T(8,128)(2,1)S(1)}, u32[]{:S(2)}, u32[]{:S(2)}) collective-permute-start(bf16[128,768]{1,0:T(8,128)(2,1)S(1)} %combine.6), channel_id=1, source_target_pairs={{0,4},{4,0},{8,12},{12,8},{1,5},{5,1},{9,13},{13,9},{2,6},{6,2},{1... | collective-permute-start | bytes 589832 | tf_op jit(solution)/shard_map/ppermute | solution.py:267
  63.6 1.0 %down.6 = (bf16[64,768]{1,0:T(8,128)(2,1)S(1)}, bf16[64,768]{1,0:T(8,128)(2,1)S(1)}, bf16[64,768]{1,0:T(8,128)(2,1)S(1)}, bf16[64,768]{1,0:T(8,128)(2,1)S(1)}) custom-call(s32[1]{0:T(128)} %bitcast.3.column_ref, bf16[256,2048]{1,0:T(8,128)(2,1)S(1)} %gate_up.5.h_ref, bf16[1,2048,3072]{2,1,0:T(8,128)(2,1)S(1)} %bitcast.5, bf16[128,768]{1,0:T(8,128)(2,1)S(1)} %combine.5.refs_0_), custom_call_target="tpu_custom_call" | custom-call | flops 805306368 | bytes 3538944 | tf_op jit(solution)/shard_map/down/pallas_call | solution.py:221
  64.6 0.4 collective-permute-start.19
  65.0 1.1 %collective-permute-start.20 = (bf16[64,768]{1,0:T(8,128)(2,1)S(1)}, bf16[64,768]{1,0:T(8,128)(2,1)S(1)}, u32[]{:S(2)}, u32[]{:S(2)}) collective-permute-start(bf16[64,768]{1,0:T(8,128)(2,1)S(1)} %get-tuple-element.85), channel_id=1, source_target_pairs={{0,2},{1,3},{2,0},{3,1},{4,6},{5,7},{6,4},{7,5},{8,10},{9,11},{10,... | collective-permute-start | bytes 294920 | tf_op jit(solution)/shard_map/ppermute | solution.py:267
  66.0 0.5 collective-permute-start.21
  66.5 4.1 %collective-permute-done.20.refs_2_ = bf16[64,768]{1,0:T(8,128)(2,1)S(1)} collective-permute-done((bf16[64,768]{1,0:T(8,128)(2,1)S(1)}, bf16[64,768]{1,0:T(8,128)(2,1)S(1)}, u32[]{:S(2)}, u32[]{:S(2)}) %collective-permute-start.20) | collective-permute-done | bytes 98336 | tf_op jit(solution)/shard_map/ppermute | solution.py:267
  70.6 0.7 collective-permute-done.21.refs_3_
  71.3 2.9 %collective-permute-done.25.refs_4_ = bf16[128,768]{1,0:T(8,128)(2,1)S(1)} collective-permute-done((bf16[128,768]{1,0:T(8,128)(2,1)S(1)}, bf16[128,768]{1,0:T(8,128)(2,1)S(1)}, u32[]{:S(2)}, u32[]{:S(2)}) %collective-permute-start.25) | collective-permute-done | bytes 196640 | tf_op jit(solution)/shard_map/ppermute | solution.py:267
  74.2 1.0 %combine.7 = bf16[128,768]{1,0:T(8,128)(2,1)} custom-call(bf16[256,256]{1,0:T(8,128)(2,1)S(1)} %get-tuple-element.48.pick_ref, f32[128,2]{1,0:T(8,128)S(1)} %get-tuple-element.49.mix_ref, bf16[64,768]{1,0:T(8,128)(2,1)S(1)} %get-tuple-element.83.refs_0_, bf16[64,768]{1,0:T(8,128)(2,1)S(1)} %collective-permute-done.19.refs_1_, ...), custom_call_target="tpu_custom_call" | custom-call | flops 100663296 | bytes 589824 | tf_op jit(solution)/shard_map/combine/pallas_call | solution.py:251
  (36 shorter events, 1.8 us)
Async XLA Ops:
  0.0 13.5 %collective-permute-start = (bf16[128,768]{1,0:T(8,128)(2,1)}, bf16[128,768]{1,0:T(8,128)(2,1)S(1)}, u32[]{:S(2)}, u32[]{:S(2)}) collective-permute-start(bf16[128,768]{1,0:T(8,128)(2,1)} %refs_0_.4), channel_id=1, source_target_pairs={{0,8},{4,12},{8,0},{12,4},{1,9},{5,13},{9,1},{13,5},{2,10},{6,14},... | collective-permute-start | bytes 589832 | tf_op jit(solution)/shard_map/ppermute | solution.py:267
  4.0 10.2 %collective-permute-start.5 = (bf16[128,768]{1,0:T(8,128)(2,1)}, bf16[128,768]{1,0:T(8,128)(2,1)S(1)}, u32[]{:S(2)}, u32[]{:S(2)}) collective-permute-start(bf16[128,768]{1,0:T(8,128)(2,1)} %refs_0_.4), channel_id=1, source_target_pairs={{0,4},{4,0},{8,12},{12,8},{1,5},{5,1},{9,13},{13,9},{2,6},{6,2},{1... | collective-permute-start | bytes 589832 | tf_op jit(solution)/shard_map/ppermute | solution.py:267
  5.6 0.7 copy-start.1
  6.3 0.7 copy-start.2
  7.1 7.0 %copy-start = (bf16[128,768]{1,0:T(8,128)(2,1)S(1)}, bf16[128,768]{1,0:T(8,128)(2,1)}, u32[]{:S(2)}) copy-start(bf16[128,768]{1,0:T(8,128)(2,1)} %refs_0_.4) | copy-start | bytes 589828
  13.5 8.3 %collective-permute-start.1 = (bf16[128,768]{1,0:T(8,128)(2,1)S(1)}, bf16[128,768]{1,0:T(8,128)(2,1)S(1)}, u32[]{:S(2)}, u32[]{:S(2)}) collective-permute-start(bf16[128,768]{1,0:T(8,128)(2,1)S(1)} %collective-permute-done.refs_0_), channel_id=1, source_target_pairs={{0,4},{4,0},{8,12},{12,8},{1,5},{5,1},{9,13},{13,9},{2,6},{6,2},{1... | collective-permute-start | bytes 589832 | tf_op jit(solution)/shard_map/ppermute | solution.py:267
  14.6 9.8 %collective-permute-start.10 = (bf16[64,1536]{1,0:T(8,128)(2,1)S(1)}, bf16[64,1536]{1,0:T(8,128)(2,1)S(1)}, u32[]{:S(2)}, u32[]{:S(2)}) collective-permute-start(bf16[64,1536]{1,0:T(8,128)(2,1)S(1)} %get-tuple-element.66), channel_id=1, source_target_pairs={{0,2},{1,3},{2,0},{3,1},{4,6},{5,7},{6,4},{7,5},{8,10},{9,11},{10,... | collective-permute-start | bytes 589832 | tf_op jit(solution)/shard_map/ppermute | solution.py:267
  16.1 8.7 %collective-permute-start.11 = (bf16[64,1536]{1,0:T(8,128)(2,1)S(1)}, bf16[64,1536]{1,0:T(8,128)(2,1)S(1)}, u32[]{:S(2)}, u32[]{:S(2)}) collective-permute-start(bf16[64,1536]{1,0:T(8,128)(2,1)S(1)} %get-tuple-element.67), channel_id=1, source_target_pairs={{0,3},{1,2},{2,1},{3,0},{4,7},{5,6},{6,5},{7,4},{8,11},{9,10},{10,... | collective-permute-start | bytes 589832 | tf_op jit(solution)/shard_map/ppermute | solution.py:267
  16.1 9.7 %collective-permute-start.9 = (bf16[64,1536]{1,0:T(8,128)(2,1)S(1)}, bf16[64,1536]{1,0:T(8,128)(2,1)S(1)}, u32[]{:S(2)}, u32[]{:S(2)}) collective-permute-start(bf16[64,1536]{1,0:T(8,128)(2,1)S(1)} %get-tuple-element.65), channel_id=1, source_target_pairs={{0,1},{1,0},{2,3},{3,2},{4,5},{5,4},{6,7},{7,6},{8,9},{9,8},{10,11... | collective-permute-start | bytes 589832 | tf_op jit(solution)/shard_map/ppermute | solution.py:267
  21.7 1.9 %collective-permute-start.6 = (bf16[64,768]{1,0:T(8,128)(2,1)S(1)}, bf16[64,768]{1,0:T(8,128)(2,1)S(1)}, u32[]{:S(2)}, u32[]{:S(2)}) collective-permute-start(bf16[64,768]{1,0:T(8,128)(2,1)S(1)} %get-tuple-element.60), channel_id=1, source_target_pairs={{0,1},{1,0},{2,3},{3,2},{4,5},{5,4},{6,7},{7,6},{8,9},{9,8},{10,11... | collective-permute-start | bytes 294920 | tf_op jit(solution)/shard_map/ppermute | solution.py:267
  21.8 8.6 %collective-permute-start.7 = (bf16[64,768]{1,0:T(8,128)(2,1)S(1)}, bf16[64,768]{1,0:T(8,128)(2,1)S(1)}, u32[]{:S(2)}, u32[]{:S(2)}) collective-permute-start(bf16[64,768]{1,0:T(8,128)(2,1)S(1)} %get-tuple-element.61), channel_id=1, source_target_pairs={{0,2},{1,3},{2,0},{3,1},{4,6},{5,7},{6,4},{7,5},{8,10},{9,11},{10,... | collective-permute-start | bytes 294920 | tf_op jit(solution)/shard_map/ppermute | solution.py:267
  23.7 6.8 %collective-permute-start.8 = (bf16[64,768]{1,0:T(8,128)(2,1)S(1)}, bf16[64,768]{1,0:T(8,128)(2,1)S(1)}, u32[]{:S(2)}, u32[]{:S(2)}) collective-permute-start(bf16[64,768]{1,0:T(8,128)(2,1)S(1)} %get-tuple-element.62), channel_id=1, source_target_pairs={{0,3},{1,2},{2,1},{3,0},{4,7},{5,6},{6,5},{7,4},{8,11},{9,10},{10,... | collective-permute-start | bytes 294920 | tf_op jit(solution)/shard_map/ppermute | solution.py:267
  24.4 8.3 %collective-permute-start.2 = (bf16[64,768]{1,0:T(8,128)(2,1)S(1)}, bf16[64,768]{1,0:T(8,128)(2,1)S(1)}, u32[]{:S(2)}, u32[]{:S(2)}) collective-permute-start(bf16[64,768]{1,0:T(8,128)(2,1)S(1)} %get-tuple-element.52), channel_id=1, source_target_pairs={{0,1},{1,0},{2,3},{3,2},{4,5},{5,4},{6,7},{7,6},{8,9},{9,8},{10,11... | collective-permute-start | bytes 294920 | tf_op jit(solution)/shard_map/ppermute | solution.py:267
  24.8 7.8 %collective-permute-start.3 = (bf16[64,768]{1,0:T(8,128)(2,1)S(1)}, bf16[64,768]{1,0:T(8,128)(2,1)S(1)}, u32[]{:S(2)}, u32[]{:S(2)}) collective-permute-start(bf16[64,768]{1,0:T(8,128)(2,1)S(1)} %get-tuple-element.53), channel_id=1, source_target_pairs={{0,2},{1,3},{2,0},{3,1},{4,6},{5,7},{6,4},{7,5},{8,10},{9,11},{10,... | collective-permute-start | bytes 294920 | tf_op jit(solution)/shard_map/ppermute | solution.py:267
  25.9 7.5 %collective-permute-start.4 = (bf16[64,768]{1,0:T(8,128)(2,1)S(1)}, bf16[64,768]{1,0:T(8,128)(2,1)S(1)}, u32[]{:S(2)}, u32[]{:S(2)}) collective-permute-start(bf16[64,768]{1,0:T(8,128)(2,1)S(1)} %get-tuple-element.54), channel_id=1, source_target_pairs={{0,3},{1,2},{2,1},{3,0},{4,7},{5,6},{6,5},{7,4},{8,11},{9,10},{10,... | collective-permute-start | bytes 294920 | tf_op jit(solution)/shard_map/ppermute | solution.py:267
  30.5 5.1 %slice-start = ((s8[12582912]{0:T(1024)(128)(4,1)}), s8[4194304]{0:T(1024)(128)(4,1)S(1)}, s32[]{:S(2)}) async-start(s8[12582912]{0:T(1024)(128)(4,1)} %bitcast.4), calls=%async_computation | async-start | bytes 8388608
  30.5 5.1 %slice-start.1 = ((s8[12582912]{0:T(1024)(128)(4,1)}), s8[4194304]{0:T(1024)(128)(4,1)S(1)}, s32[]{:S(2)}) async-start(s8[12582912]{0:T(1024)(128)(4,1)} %bitcast.4), calls=%async_computation.1 | async-start | bytes 8388608
  33.4 2.3 %slice-start.2 = ((s8[12582912]{0:T(1024)(128)(4,1)}), s8[4194304]{0:T(1024)(128)(4,1)S(1)}, s32[]{:S(2)}) async-start(s8[12582912]{0:T(1024)(128)(4,1)} %bitcast.4), calls=%async_computation.2 | async-start | bytes 8388608
  37.8 3.5 %collective-permute-start.15 = (bf16[64,768]{1,0:T(8,128)(2,1)S(1)}, bf16[64,768]{1,0:T(8,128)(2,1)S(1)}, u32[]{:S(2)}, u32[]{:S(2)}) collective-permute-start(bf16[64,768]{1,0:T(8,128)(2,1)S(1)} %get-tuple-element.80), channel_id=1, source_target_pairs={{0,1},{1,0},{2,3},{3,2},{4,5},{5,4},{6,7},{7,6},{8,9},{9,8},{10,11... | collective-permute-start | bytes 294920 | tf_op jit(solution)/shard_map/ppermute | solution.py:267
  38.0 5.6 %collective-permute-start.16 = (bf16[64,768]{1,0:T(8,128)(2,1)S(1)}, bf16[64,768]{1,0:T(8,128)(2,1)S(1)}, u32[]{:S(2)}, u32[]{:S(2)}) collective-permute-start(bf16[64,768]{1,0:T(8,128)(2,1)S(1)} %get-tuple-element.81), channel_id=1, source_target_pairs={{0,2},{1,3},{2,0},{3,1},{4,6},{5,7},{6,4},{7,5},{8,10},{9,11},{10,... | collective-permute-start | bytes 294920 | tf_op jit(solution)/shard_map/ppermute | solution.py:267
  39.4 5.2 %collective-permute-start.17 = (bf16[64,768]{1,0:T(8,128)(2,1)S(1)}, bf16[64,768]{1,0:T(8,128)(2,1)S(1)}, u32[]{:S(2)}, u32[]{:S(2)}) collective-permute-start(bf16[64,768]{1,0:T(8,128)(2,1)S(1)} %get-tuple-element.82), channel_id=1, source_target_pairs={{0,3},{1,2},{2,1},{3,0},{4,7},{5,6},{6,5},{7,4},{8,11},{9,10},{10,... | collective-permute-start | bytes 294920 | tf_op jit(solution)/shard_map/ppermute | solution.py:267
  39.7 7.6 %collective-permute-start.13 = (bf16[64,768]{1,0:T(8,128)(2,1)S(1)}, bf16[64,768]{1,0:T(8,128)(2,1)S(1)}, u32[]{:S(2)}, u32[]{:S(2)}) collective-permute-start(bf16[64,768]{1,0:T(8,128)(2,1)S(1)} %get-tuple-element.77), channel_id=1, source_target_pairs={{0,2},{1,3},{2,0},{3,1},{4,6},{5,7},{6,4},{7,5},{8,10},{9,11},{10,... | collective-permute-start | bytes 294920 | tf_op jit(solution)/shard_map/ppermute | solution.py:267
  47.6 6.4 %collective-permute-start.18 = (bf16[128,768]{1,0:T(8,128)(2,1)S(1)}, bf16[128,768]{1,0:T(8,128)(2,1)S(1)}, u32[]{:S(2)}, u32[]{:S(2)}) collective-permute-start(bf16[128,768]{1,0:T(8,128)(2,1)S(1)} %combine.4), channel_id=1, source_target_pairs={{0,4},{4,0},{8,12},{12,8},{1,5},{5,1},{9,13},{13,9},{2,6},{6,2},{1... | collective-permute-start | bytes 589832 | tf_op jit(solution)/shard_map/ppermute | solution.py:267
  48.6 1.4 %collective-permute-start.12 = (bf16[64,768]{1,0:T(8,128)(2,1)S(1)}, bf16[64,768]{1,0:T(8,128)(2,1)S(1)}, u32[]{:S(2)}, u32[]{:S(2)}) collective-permute-start(bf16[64,768]{1,0:T(8,128)(2,1)S(1)} %get-tuple-element.76), channel_id=1, source_target_pairs={{0,1},{1,0},{2,3},{3,2},{4,5},{5,4},{6,7},{7,6},{8,9},{9,8},{10,11... | collective-permute-start | bytes 294920 | tf_op jit(solution)/shard_map/ppermute | solution.py:267
  48.6 4.4 %collective-permute-start.14 = (bf16[64,768]{1,0:T(8,128)(2,1)S(1)}, bf16[64,768]{1,0:T(8,128)(2,1)S(1)}, u32[]{:S(2)}, u32[]{:S(2)}) collective-permute-start(bf16[64,768]{1,0:T(8,128)(2,1)S(1)} %get-tuple-element.78), channel_id=1, source_target_pairs={{0,3},{1,2},{2,1},{3,0},{4,7},{5,6},{6,5},{7,4},{8,11},{9,10},{10,... | collective-permute-start | bytes 294920 | tf_op jit(solution)/shard_map/ppermute | solution.py:267
  55.4 5.3 %collective-permute-start.22 = (bf16[64,768]{1,0:T(8,128)(2,1)S(1)}, bf16[64,768]{1,0:T(8,128)(2,1)S(1)}, u32[]{:S(2)}, u32[]{:S(2)}) collective-permute-start(bf16[64,768]{1,0:T(8,128)(2,1)S(1)} %get-tuple-element.88), channel_id=1, source_target_pairs={{0,1},{1,0},{2,3},{3,2},{4,5},{5,4},{6,7},{7,6},{8,9},{9,8},{10,11... | collective-permute-start | bytes 294920 | tf_op jit(solution)/shard_map/ppermute | solution.py:267
  55.4 5.7 %collective-permute-start.23 = (bf16[64,768]{1,0:T(8,128)(2,1)S(1)}, bf16[64,768]{1,0:T(8,128)(2,1)S(1)}, u32[]{:S(2)}, u32[]{:S(2)}) collective-permute-start(bf16[64,768]{1,0:T(8,128)(2,1)S(1)} %get-tuple-element.89), channel_id=1, source_target_pairs={{0,2},{1,3},{2,0},{3,1},{4,6},{5,7},{6,4},{7,5},{8,10},{9,11},{10,... | collective-permute-start | bytes 294920 | tf_op jit(solution)/shard_map/ppermute | solution.py:267
  57.1 5.2 %collective-permute-start.24 = (bf16[64,768]{1,0:T(8,128)(2,1)S(1)}, bf16[64,768]{1,0:T(8,128)(2,1)S(1)}, u32[]{:S(2)}, u32[]{:S(2)}) collective-permute-start(bf16[64,768]{1,0:T(8,128)(2,1)S(1)} %get-tuple-element.90), channel_id=1, source_target_pairs={{0,3},{1,2},{2,1},{3,0},{4,7},{5,6},{6,5},{7,4},{8,11},{9,10},{10,... | collective-permute-start | bytes 294920 | tf_op jit(solution)/shard_map/ppermute | solution.py:267
  57.3 14.0 %collective-permute-start.26 = (bf16[128,768]{1,0:T(8,128)(2,1)S(1)}, bf16[128,768]{1,0:T(8,128)(2,1)S(1)}, u32[]{:S(2)}, u32[]{:S(2)}) collective-permute-start(bf16[128,768]{1,0:T(8,128)(2,1)S(1)} %combine.5.refs_0_), channel_id=1, source_target_pairs={{0,8},{4,12},{8,0},{12,4},{1,9},{5,13},{9,1},{13,5},{2,10},{6,14},... | collective-permute-start | bytes 589832 | tf_op jit(solution)/shard_map/ppermute | solution.py:267
  62.6 11.6 %collective-permute-start.25 = (bf16[128,768]{1,0:T(8,128)(2,1)S(1)}, bf16[128,768]{1,0:T(8,128)(2,1)S(1)}, u32[]{:S(2)}, u32[]{:S(2)}) collective-permute-start(bf16[128,768]{1,0:T(8,128)(2,1)S(1)} %combine.6), channel_id=1, source_target_pairs={{0,4},{4,0},{8,12},{12,8},{1,5},{5,1},{9,13},{13,9},{2,6},{6,2},{1... | collective-permute-start | bytes 589832 | tf_op jit(solution)/shard_map/ppermute | solution.py:267
  64.6 1.9 %collective-permute-start.19 = (bf16[64,768]{1,0:T(8,128)(2,1)S(1)}, bf16[64,768]{1,0:T(8,128)(2,1)S(1)}, u32[]{:S(2)}, u32[]{:S(2)}) collective-permute-start(bf16[64,768]{1,0:T(8,128)(2,1)S(1)} %get-tuple-element.84), channel_id=1, source_target_pairs={{0,1},{1,0},{2,3},{3,2},{4,5},{5,4},{6,7},{7,6},{8,9},{9,8},{10,11... | collective-permute-start | bytes 294920 | tf_op jit(solution)/shard_map/ppermute | solution.py:267
  65.0 5.6 %collective-permute-start.20 = (bf16[64,768]{1,0:T(8,128)(2,1)S(1)}, bf16[64,768]{1,0:T(8,128)(2,1)S(1)}, u32[]{:S(2)}, u32[]{:S(2)}) collective-permute-start(bf16[64,768]{1,0:T(8,128)(2,1)S(1)} %get-tuple-element.85), channel_id=1, source_target_pairs={{0,2},{1,3},{2,0},{3,1},{4,6},{5,7},{6,4},{7,5},{8,10},{9,11},{10,... | collective-permute-start | bytes 294920 | tf_op jit(solution)/shard_map/ppermute | solution.py:267
  66.0 5.2 %collective-permute-start.21 = (bf16[64,768]{1,0:T(8,128)(2,1)S(1)}, bf16[64,768]{1,0:T(8,128)(2,1)S(1)}, u32[]{:S(2)}, u32[]{:S(2)}) collective-permute-start(bf16[64,768]{1,0:T(8,128)(2,1)S(1)} %get-tuple-element.86), channel_id=1, source_target_pairs={{0,3},{1,2},{2,1},{3,0},{4,7},{5,6},{6,5},{7,4},{8,11},{9,10},{10,... | collective-permute-start | bytes 294920 | tf_op jit(solution)/shard_map/ppermute | solution.py:267

commit v9 on v8

--- a/solution.py
+++ b/solution.py
@@ -231,8 +231,8 @@
     )(column.reshape(1), *pinned([hidden, down_w]), *after)
 
 
-def combine_kernel(pick_ref, mix_ref, *refs, experts, sums):
-    y_refs, added, out = refs[:experts], refs[experts : experts + sums], refs[-1]
+def combine_kernel(pick_ref, mix_ref, *refs, experts):
+    y_refs, added, out = refs[:experts], refs[experts:-1], refs[-1]
     rows = out.shape[0]
     y = jnp.concatenate([r[...] for r in y_refs], axis=0)
     picked = lax.dot_general(
@@ -244,20 +244,19 @@
     out[...] = mixed.astype(BF16)
 
 
-def combine(pick, mix, blocks, added, after=()):
+def combine(pick, mix, blocks, added):
     rows = mix.shape[0]
     width = blocks[0].shape[1]
     operands = 2 + len(blocks) + len(added)
     return pl.pallas_call(
-        functools.partial(combine_kernel, experts=len(blocks), sums=len(added)),
+        functools.partial(combine_kernel, experts=len(blocks)),
         out_shape=jax.ShapeDtypeStruct((rows, width), BF16),
-        in_specs=[pl.BlockSpec(memory_space=pltpu.VMEM)] * operands
-        + [pl.BlockSpec(memory_space=pl.ANY)] * len(after),
+        in_specs=[pl.BlockSpec(memory_space=pltpu.VMEM)] * operands,
         out_specs=pl.BlockSpec(memory_space=pltpu.VMEM),
         cost_estimate=cost(4 * rows * pick.shape[0] * width, 6 * rows * width),
         compiler_params=params(),
         name="combine",
-    )(pick, mix, *blocks, *added, *after)
+    )(pick, mix, *blocks, *added)
 
 
 def swap(value, axis, distance):
@@ -313,12 +312,12 @@
     if not doubling:
         mixed = combine(pick, mix, returned(everything), [])
         return lax.psum_scatter(mixed, "tensor", scatter_dimension=1, tiled=True)
-    blocks = [returned(across(3)), returned(across(2))]
-    passed = swap(combine(pick, mix, blocks[0], [], blocks[1][2:3]), "tensor", 1)
-    onwards = combine(pick, mix, blocks[1], [passed])
-    over = swap(onwards, "tensor", 2)
-    beside = swap(combine(pick, mix, returned(across(1), [onwards]), []), "tensor", 1)
-    return combine(pick, mix, returned(across(0), [onwards]), [beside, over])
+    sums, mixtures = [], []
+    for distance in (3, 2, 1):
+        blocks = returned(across(distance), mixtures[-2:-1])
+        mixtures.append(combine(pick, mix, blocks, []))
+        sums.append(swap(mixtures[-1], "tensor", distance))
+    return combine(pick, mix, returned(across(0), sums[:1]), sums[::-1])
 
 
 def solution(mesh):

time: 75.3 us -> 69.1 us (0.918); the launches traced: 75.2 us -> 67.8 us
  waiting for transfers between devices: 21.9 us -> 15.6 us
  starting transfers between devices: 27.3 us -> 26.2 us
    ppermute x27, waiting for transfers between devices: 21.9 us -> 15.6 us  [swap(): return lax.ppermute(value, axis, [(i, i ^ distance) for i in range(count)])]
    ppermute x27, starting transfers between devices: 27.3 us -> 26.2 us  [swap(): return lax.ppermute(value, axis, [(i, i ^ distance) for i in range(count)])]
  transfers between devices with their start and end apart: 27 -> 27, of which waited for: 13 -> 9; matrix products, arithmetic and copies ran while one was open for 0% -> 0% of each run, Pallas kernels for 23% -> 30%
where the time goes in v9:
time: 69.1 us; the launch traced here: 67.8 us
  starting transfers between devices  26.2 us (38%)
  Pallas kernels  24.2 us (35%)
  waiting for transfers between devices  15.6 us (23%)
  local copies, waits for them, and re-layouts  1.54 us (2%)
    ppermute x27, starting transfers between devices, swap(): return lax.ppermute(value, axis, [(i, i ^ distance) for i in range(count)])  26.2 us
    ppermute x27, waiting for transfers between devices, swap(): return lax.ppermute(value, axis, [(i, i ^ distance) for i in range(count)])  15.6 us
    pallas_call x2, Pallas kernels, prefetch(): pl.pallas_call(functools.partial(prefetch_kernel, parts=[part for _, part...  9.41 us
    pallas_call x3, Pallas kernels, gate_up(): pl.pallas_call(functools.partial(gate_up_kernel, experts=experts, slices=...  7.71 us
    pallas_call x4, Pallas kernels, down(): pl.pallas_call(functools.partial(down_kernel, part=part, waits=len(after)...  4.1 us
    pallas_call x4, Pallas kernels, combine(): pl.pallas_call(functools.partial(combine_kernel, experts=len(blocks)), ou...  1.95 us
    unnamed x12, local copies, waits for them, and re-layouts  1.54 us
  transfers between devices with their start and end apart: 27, of which 9 were waited for; matrix products, arithmetic and copies ran while one was open for 0% of the time, Pallas kernels for 30%

profile of v9, /device:TPU:0, one launch (start us, length us, event | category | flops | bytes accessed | tf_op | source)
XLA Modules:
  0.0 67.8 jit_solution(11131065895081986935)
XLA Ops:
  0.0 4.0 %collective-permute-start = (bf16[128,768]{1,0:T(8,128)(2,1)}, bf16[128,768]{1,0:T(8,128)(2,1)S(1)}, u32[]{:S(2)}, u32[]{:S(2)}) collective-permute-start(bf16[128,768]{1,0:T(8,128)(2,1)} %refs_0_.4), channel_id=1, source_target_pairs={{0,8},{4,12},{8,0},{12,4},{1,9},{5,13},{9,1},{13,5},{2,10},{6,14},... | collective-permute-start | bytes 589832 | tf_op jit(solution)/shard_map/ppermute | solution.py:266
  4.0 1.6 %collective-permute-start.5 = (bf16[128,768]{1,0:T(8,128)(2,1)}, bf16[128,768]{1,0:T(8,128)(2,1)S(1)}, u32[]{:S(2)}, u32[]{:S(2)}) collective-permute-start(bf16[128,768]{1,0:T(8,128)(2,1)} %refs_0_.4), channel_id=1, source_target_pairs={{0,4},{4,0},{8,12},{12,8},{1,5},{5,1},{9,13},{13,9},{2,6},{6,2},{1... | collective-permute-start | bytes 589832 | tf_op jit(solution)/shard_map/ppermute | solution.py:266
  5.6 0.7 copy-done.1
  6.3 0.7 copy-done.2
  7.2 4.7 %prefetch.2 = (bf16[768,2048]{1,0:T(8,128)(2,1)S(1)}, bf16[768,2048]{1,0:T(8,128)(2,1)S(1)}, bf16[768,2048]{1,0:T(8,128)(2,1)S(1)}, bf16[768,2048]{1,0:T(8,128)(2,1)S(1)}) custom-call(s32[1]{0:T(128)} %bitcast.3.column_ref, bf16[256,128]{1,0:T(8,128)(2,1)S(1)} %get-tuple-element.50.placed_ref.after_ref, bf16[1,3072,2048]{2,1,0:T(8,128)(2,1)} %refs_2_.3, ...), custom_call_target="tpu_custom_call" | custom-call | bytes 12582912 | tf_op jit(solution)/shard_map/prefetch/pallas_call | solution.py:127
  11.9 1.6 %collective-permute-done.refs_0_ = bf16[128,768]{1,0:T(8,128)(2,1)S(1)} collective-permute-done((bf16[128,768]{1,0:T(8,128)(2,1)}, bf16[128,768]{1,0:T(8,128)(2,1)S(1)}, u32[]{:S(2)}, u32[]{:S(2)}) %collective-permute-start) | collective-permute-done | bytes 196640 | tf_op jit(solution)/shard_map/ppermute | solution.py:266
  13.5 0.7 %collective-permute-start.1 = (bf16[128,768]{1,0:T(8,128)(2,1)S(1)}, bf16[128,768]{1,0:T(8,128)(2,1)S(1)}, u32[]{:S(2)}, u32[]{:S(2)}) collective-permute-start(bf16[128,768]{1,0:T(8,128)(2,1)S(1)} %collective-permute-done.refs_0_), channel_id=1, source_target_pairs={{0,4},{4,0},{8,12},{12,8},{1,5},{5,1},{9,13},{13,9},{2,6},{6,2},{1... | collective-permute-start | bytes 589832 | tf_op jit(solution)/shard_map/ppermute | solution.py:266
  14.2 0.4 dispatch.4
  14.6 1.6 %collective-permute-start.10 = (bf16[64,1536]{1,0:T(8,128)(2,1)S(1)}, bf16[64,1536]{1,0:T(8,128)(2,1)S(1)}, u32[]{:S(2)}, u32[]{:S(2)}) collective-permute-start(bf16[64,1536]{1,0:T(8,128)(2,1)S(1)} %get-tuple-element.66), channel_id=1, source_target_pairs={{0,2},{1,3},{2,0},{3,1},{4,6},{5,7},{6,4},{7,5},{8,10},{9,11},{10,... | collective-permute-start | bytes 589832 | tf_op jit(solution)/shard_map/ppermute | solution.py:266
  16.1 0.6 collective-permute-start.9
  16.8 4.7 %prefetch.3 = (bf16[768,2048]{1,0:T(8,128)(2,1)S(1)}, bf16[768,2048]{1,0:T(8,128)(2,1)S(1)}, bf16[768,2048]{1,0:T(8,128)(2,1)S(1)}, bf16[768,2048]{1,0:T(8,128)(2,1)S(1)}) custom-call(s32[1]{0:T(128)} %bitcast.3.column_ref, bf16[64,1536]{1,0:T(8,128)(2,1)S(1)} %get-tuple-element.56.after_ref.refs_0_, bf16[1,3072,2048]{2,1,0:T(8,128)(2,1)} %refs_2_.3, ...), custom_call_target="tpu_custom_call" | custom-call | bytes 12582912 | tf_op jit(solution)/shard_map/prefetch/pallas_call | solution.py:127
  21.5 0.3 dispatch.5
  21.8 1.6 %collective-permute-start.7 = (bf16[64,768]{1,0:T(8,128)(2,1)S(1)}, bf16[64,768]{1,0:T(8,128)(2,1)S(1)}, u32[]{:S(2)}, u32[]{:S(2)}) collective-permute-start(bf16[64,768]{1,0:T(8,128)(2,1)S(1)} %get-tuple-element.61), channel_id=1, source_target_pairs={{0,2},{1,3},{2,0},{3,1},{4,6},{5,7},{6,4},{7,5},{8,10},{9,11},{10,... | collective-permute-start | bytes 294920 | tf_op jit(solution)/shard_map/ppermute | solution.py:266
  23.4 0.3 dispatch.3
  23.7 0.7 %collective-permute-start.8 = (bf16[64,768]{1,0:T(8,128)(2,1)S(1)}, bf16[64,768]{1,0:T(8,128)(2,1)S(1)}, u32[]{:S(2)}, u32[]{:S(2)}) collective-permute-start(bf16[64,768]{1,0:T(8,128)(2,1)S(1)} %get-tuple-element.62), channel_id=1, source_target_pairs={{0,3},{1,2},{2,1},{3,0},{4,7},{5,6},{6,5},{7,4},{8,11},{9,10},{10,... | collective-permute-start | bytes 294920 | tf_op jit(solution)/shard_map/ppermute | solution.py:266
  24.4 0.4 collective-permute-start.2
  24.8 1.1 %collective-permute-start.3 = (bf16[64,768]{1,0:T(8,128)(2,1)S(1)}, bf16[64,768]{1,0:T(8,128)(2,1)S(1)}, u32[]{:S(2)}, u32[]{:S(2)}) collective-permute-start(bf16[64,768]{1,0:T(8,128)(2,1)S(1)} %get-tuple-element.53), channel_id=1, source_target_pairs={{0,2},{1,3},{2,0},{3,1},{4,6},{5,7},{6,4},{7,5},{8,10},{9,11},{10,... | collective-permute-start | bytes 294920 | tf_op jit(solution)/shard_map/ppermute | solution.py:266
  25.9 1.1 %collective-permute-start.4 = (bf16[64,768]{1,0:T(8,128)(2,1)S(1)}, bf16[64,768]{1,0:T(8,128)(2,1)S(1)}, u32[]{:S(2)}, u32[]{:S(2)}) collective-permute-start(bf16[64,768]{1,0:T(8,128)(2,1)S(1)} %get-tuple-element.54), channel_id=1, source_target_pairs={{0,3},{1,2},{2,1},{3,0},{4,7},{5,6},{6,5},{7,4},{8,11},{9,10},{10,... | collective-permute-start | bytes 294920 | tf_op jit(solution)/shard_map/ppermute | solution.py:266
  27.0 3.5 %gate_up.3 = (f32[256,2048]{1,0:T(8,128)S(1)}, f32[256,2048]{1,0:T(8,128)S(1)}) custom-call(bf16[64,1536]{1,0:T(8,128)(2,1)S(1)} %get-tuple-element.56.after_ref.refs_0_, bf16[64,1536]{1,0:T(8,128)(2,1)S(1)} %collective-permute-done.9.refs_1_, bf16[64,1536]{1,0:T(8,128)(2,1)S(1)} %collective-permute-done.10.refs_2_, ...), custom_call_target="tpu_custom_call" | custom-call | flops 3221225472 | bytes 12582912 | tf_op jit(solution)/shard_map/gate_up/pallas_call | solution.py:183
  30.5 2.1 %gate_up.4 = (f32[256,2048]{1,0:T(8,128)S(1)}, f32[256,2048]{1,0:T(8,128)S(1)}) custom-call(bf16[64,768]{1,0:T(8,128)(2,1)S(1)} %get-tuple-element.59.refs_0_, bf16[64,768]{1,0:T(8,128)(2,1)S(1)} %collective-permute-done.6.refs_8_.refs_1_, bf16[64,768]{1,0:T(8,128)(2,1)S(1)} %collective-permute-done.7.refs_2_, ...), custom_call_target="tpu_custom_call", output_to_operand_aliasing={{0}: (6, {}), {1}: (7, {})} | custom-call | flops 1610612736 | bytes 6291456 | tf_op jit(solution)/shard_map/gate_up/pallas_call | solution.py:183
  32.6 0.8 %collective-permute-done.4.refs_3_ = bf16[64,768]{1,0:T(8,128)(2,1)S(1)} collective-permute-done((bf16[64,768]{1,0:T(8,128)(2,1)S(1)}, bf16[64,768]{1,0:T(8,128)(2,1)S(1)}, u32[]{:S(2)}, u32[]{:S(2)}) %collective-permute-start.4) | collective-permute-done | bytes 98336 | tf_op jit(solution)/shard_map/ppermute | solution.py:266
  33.4 2.1 %gate_up.5.h_ref = bf16[256,2048]{1,0:T(8,128)(2,1)S(1)} custom-call(bf16[64,768]{1,0:T(8,128)(2,1)S(1)} %get-tuple-element.51.refs_0_, bf16[64,768]{1,0:T(8,128)(2,1)S(1)} %collective-permute-done.2.refs_1_, bf16[64,768]{1,0:T(8,128)(2,1)S(1)} %collective-permute-done.3.refs_2_, bf16[64,768]{1,0:T(8,128)(2,1)S(1)} %collective-permute-done.4.refs_3_, ...), custom_call_target="tpu_custom_call" | custom-call | flops 1610612736 | bytes 6291456 | tf_op jit(solution)/shard_map/gate_up/pallas_call | solution.py:183
  35.7 1.0 %down.4 = (bf16[64,768]{1,0:T(8,128)(2,1)S(1)}, bf16[64,768]{1,0:T(8,128)(2,1)S(1)}, bf16[64,768]{1,0:T(8,128)(2,1)S(1)}, bf16[64,768]{1,0:T(8,128)(2,1)S(1)}) custom-call(s32[1]{0:T(128)} %bitcast.3.column_ref, bf16[256,2048]{1,0:T(8,128)(2,1)S(1)} %gate_up.5.h_ref, bf16[1,2048,3072]{2,1,0:T(8,128)(2,1)S(1)} %bitcast.5), custom_call_target="tpu_custom_call" | custom-call | flops 805306368 | bytes 3538944 | tf_op jit(solution)/shard_map/down/pallas_call | solution.py:221
  36.8 0.2 collective-permute-start.12
  37.0 1.4 %collective-permute-start.13 = (bf16[64,768]{1,0:T(8,128)(2,1)S(1)}, bf16[64,768]{1,0:T(8,128)(2,1)S(1)}, u32[]{:S(2)}, u32[]{:S(2)}) collective-permute-start(bf16[64,768]{1,0:T(8,128)(2,1)S(1)} %get-tuple-element.77), channel_id=1, source_target_pairs={{0,2},{1,3},{2,0},{3,1},{4,6},{5,7},{6,4},{7,5},{8,10},{9,11},{10,... | collective-permute-start | bytes 294920 | tf_op jit(solution)/shard_map/ppermute | solution.py:266
  38.4 0.3 collective-permute-start.14
  38.7 1.0 %down.7 = (bf16[64,768]{1,0:T(8,128)(2,1)S(1)}, bf16[64,768]{1,0:T(8,128)(2,1)S(1)}, bf16[64,768]{1,0:T(8,128)(2,1)S(1)}, bf16[64,768]{1,0:T(8,128)(2,1)S(1)}) custom-call(s32[1]{0:T(128)} %bitcast.3.column_ref, bf16[256,2048]{1,0:T(8,128)(2,1)S(1)} %gate_up.5.h_ref, bf16[1,2048,3072]{2,1,0:T(8,128)(2,1)S(1)} %bitcast.5), custom_call_target="tpu_custom_call" | custom-call | flops 805306368 | bytes 3538944 | tf_op jit(solution)/shard_map/down/pallas_call | solution.py:221
  39.7 0.5 collective-permute-start.23
  40.2 1.4 %collective-permute-start.24 = (bf16[64,768]{1,0:T(8,128)(2,1)S(1)}, bf16[64,768]{1,0:T(8,128)(2,1)S(1)}, u32[]{:S(2)}, u32[]{:S(2)}) collective-permute-start(bf16[64,768]{1,0:T(8,128)(2,1)S(1)} %get-tuple-element.89), channel_id=1, source_target_pairs={{0,2},{1,3},{2,0},{3,1},{4,6},{5,7},{6,4},{7,5},{8,10},{9,11},{10,... | collective-permute-start | bytes 294920 | tf_op jit(solution)/shard_map/ppermute | solution.py:266
  41.7 0.9 %collective-permute-done.13.refs_2_ = bf16[64,768]{1,0:T(8,128)(2,1)S(1)} collective-permute-done((bf16[64,768]{1,0:T(8,128)(2,1)S(1)}, bf16[64,768]{1,0:T(8,128)(2,1)S(1)}, u32[]{:S(2)}, u32[]{:S(2)}) %collective-permute-start.13) | collective-permute-done | bytes 98336 | tf_op jit(solution)/shard_map/ppermute | solution.py:266
  42.6 1.0 %collective-permute-done.14.refs_3_ = bf16[64,768]{1,0:T(8,128)(2,1)S(1)} collective-permute-done((bf16[64,768]{1,0:T(8,128)(2,1)S(1)}, bf16[64,768]{1,0:T(8,128)(2,1)S(1)}, u32[]{:S(2)}, u32[]{:S(2)}) %collective-permute-start.14) | collective-permute-done | bytes 98336 | tf_op jit(solution)/shard_map/ppermute | solution.py:266
  43.6 0.3 combine.4.refs_0_
  44.0 3.1 %collective-permute-start.15 = (bf16[128,768]{1,0:T(8,128)(2,1)S(1)}, bf16[128,768]{1,0:T(8,128)(2,1)S(1)}, u32[]{:S(2)}, u32[]{:S(2)}) collective-permute-start(bf16[128,768]{1,0:T(8,128)(2,1)S(1)} %combine.4.refs_0_), channel_id=1, source_target_pairs={{0,12},{4,8},{8,4},{12,0},{1,13},{5,9},{9,5},{13,1},{2,14},{6,10},... | collective-permute-start | bytes 589832 | tf_op jit(solution)/shard_map/ppermute | solution.py:266
  47.1 1.0 %down.6 = (bf16[64,768]{1,0:T(8,128)(2,1)S(1)}, bf16[64,768]{1,0:T(8,128)(2,1)S(1)}, bf16[64,768]{1,0:T(8,128)(2,1)S(1)}, bf16[64,768]{1,0:T(8,128)(2,1)S(1)}) custom-call(s32[1]{0:T(128)} %bitcast.3.column_ref, bf16[256,2048]{1,0:T(8,128)(2,1)S(1)} %gate_up.5.h_ref, bf16[1,2048,3072]{2,1,0:T(8,128)(2,1)S(1)} %bitcast.5, bf16[128,768]{1,0:T(8,128)(2,1)S(1)} %combine.4.refs_0_), custom_call_target="tpu_custom_call" | custom-call | flops 805306368 | bytes 3538944 | tf_op jit(solution)/shard_map/down/pallas_call | solution.py:221
  48.1 0.6 collective-permute-start.19
  48.7 1.5 %collective-permute-start.20 = (bf16[64,768]{1,0:T(8,128)(2,1)S(1)}, bf16[64,768]{1,0:T(8,128)(2,1)S(1)}, u32[]{:S(2)}, u32[]{:S(2)}) collective-permute-start(bf16[64,768]{1,0:T(8,128)(2,1)S(1)} %get-tuple-element.85), channel_id=1, source_target_pairs={{0,2},{1,3},{2,0},{3,1},{4,6},{5,7},{6,4},{7,5},{8,10},{9,11},{10,... | collective-permute-start | bytes 294920 | tf_op jit(solution)/shard_map/ppermute | solution.py:266
  50.2 0.3 combine.6
  50.5 0.9 %collective-permute-start.26 = (bf16[128,768]{1,0:T(8,128)(2,1)S(1)}, bf16[128,768]{1,0:T(8,128)(2,1)S(1)}, u32[]{:S(2)}, u32[]{:S(2)}) collective-permute-start(bf16[128,768]{1,0:T(8,128)(2,1)S(1)} %combine.6), channel_id=1, source_target_pairs={{0,8},{4,12},{8,0},{12,4},{1,9},{5,13},{9,1},{13,5},{2,10},{6,14},... | collective-permute-start | bytes 589832 | tf_op jit(solution)/shard_map/ppermute | solution.py:266
  51.4 2.3 %collective-permute-done.20.refs_2_ = bf16[64,768]{1,0:T(8,128)(2,1)S(1)} collective-permute-done((bf16[64,768]{1,0:T(8,128)(2,1)S(1)}, bf16[64,768]{1,0:T(8,128)(2,1)S(1)}, u32[]{:S(2)}, u32[]{:S(2)}) %collective-permute-start.20) | collective-permute-done | bytes 98336 | tf_op jit(solution)/shard_map/ppermute | solution.py:266
  53.7 1.5 %collective-permute-done.21.refs_3_ = bf16[64,768]{1,0:T(8,128)(2,1)S(1)} collective-permute-done((bf16[64,768]{1,0:T(8,128)(2,1)S(1)}, bf16[64,768]{1,0:T(8,128)(2,1)S(1)}, u32[]{:S(2)}, u32[]{:S(2)}) %collective-permute-start.21) | collective-permute-done | bytes 98336 | tf_op jit(solution)/shard_map/ppermute | solution.py:266
  55.3 0.3 combine.5
  55.6 0.9 %collective-permute-start.22 = (bf16[128,768]{1,0:T(8,128)(2,1)S(1)}, bf16[128,768]{1,0:T(8,128)(2,1)S(1)}, u32[]{:S(2)}, u32[]{:S(2)}) collective-permute-start(bf16[128,768]{1,0:T(8,128)(2,1)S(1)} %combine.5), channel_id=1, source_target_pairs={{0,4},{4,0},{8,12},{12,8},{1,5},{5,1},{9,13},{13,9},{2,6},{6,2},{1... | collective-permute-start | bytes 589832 | tf_op jit(solution)/shard_map/ppermute | solution.py:266
  56.5 1.0 %down.5 = (bf16[64,768]{1,0:T(8,128)(2,1)S(1)}, bf16[64,768]{1,0:T(8,128)(2,1)S(1)}, bf16[64,768]{1,0:T(8,128)(2,1)S(1)}, bf16[64,768]{1,0:T(8,128)(2,1)S(1)}) custom-call(s32[1]{0:T(128)} %bitcast.3.column_ref, bf16[256,2048]{1,0:T(8,128)(2,1)S(1)} %gate_up.5.h_ref, bf16[1,2048,3072]{2,1,0:T(8,128)(2,1)S(1)} %bitcast.5, ...), custom_call_target="tpu_custom_call" | custom-call | flops 805306368 | bytes 3538944 | tf_op jit(solution)/shard_map/down/pallas_call | solution.py:221
  57.5 0.3 collective-permute-start.16
  57.8 1.4 %collective-permute-start.17 = (bf16[64,768]{1,0:T(8,128)(2,1)S(1)}, bf16[64,768]{1,0:T(8,128)(2,1)S(1)}, u32[]{:S(2)}, u32[]{:S(2)}) collective-permute-start(bf16[64,768]{1,0:T(8,128)(2,1)S(1)} %get-tuple-element.81), channel_id=1, source_target_pairs={{0,2},{1,3},{2,0},{3,1},{4,6},{5,7},{6,4},{7,5},{8,10},{9,11},{10,... | collective-permute-start | bytes 294920 | tf_op jit(solution)/shard_map/ppermute | solution.py:266
  59.4 6.2 %collective-permute-done.26.refs_5_ = bf16[128,768]{1,0:T(8,128)(2,1)S(1)} collective-permute-done((bf16[128,768]{1,0:T(8,128)(2,1)S(1)}, bf16[128,768]{1,0:T(8,128)(2,1)S(1)}, u32[]{:S(2)}, u32[]{:S(2)}) %collective-permute-start.26) | collective-permute-done | bytes 196640 | tf_op jit(solution)/shard_map/ppermute | solution.py:266
  65.6 1.2 %collective-permute-done.22.refs_4_ = bf16[128,768]{1,0:T(8,128)(2,1)S(1)} collective-permute-done((bf16[128,768]{1,0:T(8,128)(2,1)S(1)}, bf16[128,768]{1,0:T(8,128)(2,1)S(1)}, u32[]{:S(2)}, u32[]{:S(2)}) %collective-permute-start.22) | collective-permute-done | bytes 196640 | tf_op jit(solution)/shard_map/ppermute | solution.py:266
  66.8 1.0 %combine.7 = bf16[128,768]{1,0:T(8,128)(2,1)} custom-call(bf16[256,256]{1,0:T(8,128)(2,1)S(1)} %get-tuple-element.48.pick_ref, f32[128,2]{1,0:T(8,128)S(1)} %get-tuple-element.49.mix_ref, bf16[64,768]{1,0:T(8,128)(2,1)S(1)} %get-tuple-element.79.refs_0_, bf16[64,768]{1,0:T(8,128)(2,1)S(1)} %collective-permute-done.16.refs_1_, ...), custom_call_target="tpu_custom_call" | custom-call | flops 100663296 | bytes 589824 | tf_op jit(solution)/shard_map/combine/pallas_call | solution.py:251
  (36 shorter events, 0.8 us)
Async XLA Ops:
  0.0 13.5 %collective-permute-start = (bf16[128,768]{1,0:T(8,128)(2,1)}, bf16[128,768]{1,0:T(8,128)(2,1)S(1)}, u32[]{:S(2)}, u32[]{:S(2)}) collective-permute-start(bf16[128,768]{1,0:T(8,128)(2,1)} %refs_0_.4), channel_id=1, source_target_pairs={{0,8},{4,12},{8,0},{12,4},{1,9},{5,13},{9,1},{13,5},{2,10},{6,14},... | collective-permute-start | bytes 589832 | tf_op jit(solution)/shard_map/ppermute | solution.py:266
  4.0 10.2 %collective-permute-start.5 = (bf16[128,768]{1,0:T(8,128)(2,1)}, bf16[128,768]{1,0:T(8,128)(2,1)S(1)}, u32[]{:S(2)}, u32[]{:S(2)}) collective-permute-start(bf16[128,768]{1,0:T(8,128)(2,1)} %refs_0_.4), channel_id=1, source_target_pairs={{0,4},{4,0},{8,12},{12,8},{1,5},{5,1},{9,13},{13,9},{2,6},{6,2},{1... | collective-permute-start | bytes 589832 | tf_op jit(solution)/shard_map/ppermute | solution.py:266
  5.6 0.7 %copy-start.1 = (s32[128,2]{0,1:T(2,128)S(1)}, s32[128,2]{0,1:T(2,128)}, u32[]{:S(2)}) copy-start(s32[128,2]{0,1:T(2,128)} %param.7) | copy-start | bytes 3076
  6.3 0.7 %copy-start.2 = (f32[128,2]{0,1:T(2,128)S(1)}, f32[128,2]{0,1:T(2,128)}, u32[]{:S(2)}) copy-start(f32[128,2]{0,1:T(2,128)} %param.8) | copy-start | bytes 3076
  7.1 7.0 %copy-start = (bf16[128,768]{1,0:T(8,128)(2,1)S(1)}, bf16[128,768]{1,0:T(8,128)(2,1)}, u32[]{:S(2)}) copy-start(bf16[128,768]{1,0:T(8,128)(2,1)} %refs_0_.4) | copy-start | bytes 589828
  13.5 8.3 %collective-permute-start.1 = (bf16[128,768]{1,0:T(8,128)(2,1)S(1)}, bf16[128,768]{1,0:T(8,128)(2,1)S(1)}, u32[]{:S(2)}, u32[]{:S(2)}) collective-permute-start(bf16[128,768]{1,0:T(8,128)(2,1)S(1)} %collective-permute-done.refs_0_), channel_id=1, source_target_pairs={{0,4},{4,0},{8,12},{12,8},{1,5},{5,1},{9,13},{13,9},{2,6},{6,2},{1... | collective-permute-start | bytes 589832 | tf_op jit(solution)/shard_map/ppermute | solution.py:266
  14.6 9.8 %collective-permute-start.10 = (bf16[64,1536]{1,0:T(8,128)(2,1)S(1)}, bf16[64,1536]{1,0:T(8,128)(2,1)S(1)}, u32[]{:S(2)}, u32[]{:S(2)}) collective-permute-start(bf16[64,1536]{1,0:T(8,128)(2,1)S(1)} %get-tuple-element.66), channel_id=1, source_target_pairs={{0,2},{1,3},{2,0},{3,1},{4,6},{5,7},{6,4},{7,5},{8,10},{9,11},{10,... | collective-permute-start | bytes 589832 | tf_op jit(solution)/shard_map/ppermute | solution.py:266
  16.1 8.7 %collective-permute-start.11 = (bf16[64,1536]{1,0:T(8,128)(2,1)S(1)}, bf16[64,1536]{1,0:T(8,128)(2,1)S(1)}, u32[]{:S(2)}, u32[]{:S(2)}) collective-permute-start(bf16[64,1536]{1,0:T(8,128)(2,1)S(1)} %get-tuple-element.67), channel_id=1, source_target_pairs={{0,3},{1,2},{2,1},{3,0},{4,7},{5,6},{6,5},{7,4},{8,11},{9,10},{10,... | collective-permute-start | bytes 589832 | tf_op jit(solution)/shard_map/ppermute | solution.py:266
  16.1 9.7 %collective-permute-start.9 = (bf16[64,1536]{1,0:T(8,128)(2,1)S(1)}, bf16[64,1536]{1,0:T(8,128)(2,1)S(1)}, u32[]{:S(2)}, u32[]{:S(2)}) collective-permute-start(bf16[64,1536]{1,0:T(8,128)(2,1)S(1)} %get-tuple-element.65), channel_id=1, source_target_pairs={{0,1},{1,0},{2,3},{3,2},{4,5},{5,4},{6,7},{7,6},{8,9},{9,8},{10,11... | collective-permute-start | bytes 589832 | tf_op jit(solution)/shard_map/ppermute | solution.py:266
  21.7 1.9 %collective-permute-start.6 = (bf16[64,768]{1,0:T(8,128)(2,1)S(1)}, bf16[64,768]{1,0:T(8,128)(2,1)S(1)}, u32[]{:S(2)}, u32[]{:S(2)}) collective-permute-start(bf16[64,768]{1,0:T(8,128)(2,1)S(1)} %get-tuple-element.60), channel_id=1, source_target_pairs={{0,1},{1,0},{2,3},{3,2},{4,5},{5,4},{6,7},{7,6},{8,9},{9,8},{10,11... | collective-permute-start | bytes 294920 | tf_op jit(solution)/shard_map/ppermute | solution.py:266
  21.8 8.6 %collective-permute-start.7 = (bf16[64,768]{1,0:T(8,128)(2,1)S(1)}, bf16[64,768]{1,0:T(8,128)(2,1)S(1)}, u32[]{:S(2)}, u32[]{:S(2)}) collective-permute-start(bf16[64,768]{1,0:T(8,128)(2,1)S(1)} %get-tuple-element.61), channel_id=1, source_target_pairs={{0,2},{1,3},{2,0},{3,1},{4,6},{5,7},{6,4},{7,5},{8,10},{9,11},{10,... | collective-permute-start | bytes 294920 | tf_op jit(solution)/shard_map/ppermute | solution.py:266
  23.7 6.8 %collective-permute-start.8 = (bf16[64,768]{1,0:T(8,128)(2,1)S(1)}, bf16[64,768]{1,0:T(8,128)(2,1)S(1)}, u32[]{:S(2)}, u32[]{:S(2)}) collective-permute-start(bf16[64,768]{1,0:T(8,128)(2,1)S(1)} %get-tuple-element.62), channel_id=1, source_target_pairs={{0,3},{1,2},{2,1},{3,0},{4,7},{5,6},{6,5},{7,4},{8,11},{9,10},{10,... | collective-permute-start | bytes 294920 | tf_op jit(solution)/shard_map/ppermute | solution.py:266
  24.4 8.3 %collective-permute-start.2 = (bf16[64,768]{1,0:T(8,128)(2,1)S(1)}, bf16[64,768]{1,0:T(8,128)(2,1)S(1)}, u32[]{:S(2)}, u32[]{:S(2)}) collective-permute-start(bf16[64,768]{1,0:T(8,128)(2,1)S(1)} %get-tuple-element.52), channel_id=1, source_target_pairs={{0,1},{1,0},{2,3},{3,2},{4,5},{5,4},{6,7},{7,6},{8,9},{9,8},{10,11... | collective-permute-start | bytes 294920 | tf_op jit(solution)/shard_map/ppermute | solution.py:266
  24.8 7.8 %collective-permute-start.3 = (bf16[64,768]{1,0:T(8,128)(2,1)S(1)}, bf16[64,768]{1,0:T(8,128)(2,1)S(1)}, u32[]{:S(2)}, u32[]{:S(2)}) collective-permute-start(bf16[64,768]{1,0:T(8,128)(2,1)S(1)} %get-tuple-element.53), channel_id=1, source_target_pairs={{0,2},{1,3},{2,0},{3,1},{4,6},{5,7},{6,4},{7,5},{8,10},{9,11},{10,... | collective-permute-start | bytes 294920 | tf_op jit(solution)/shard_map/ppermute | solution.py:266
  25.9 7.5 %collective-permute-start.4 = (bf16[64,768]{1,0:T(8,128)(2,1)S(1)}, bf16[64,768]{1,0:T(8,128)(2,1)S(1)}, u32[]{:S(2)}, u32[]{:S(2)}) collective-permute-start(bf16[64,768]{1,0:T(8,128)(2,1)S(1)} %get-tuple-element.54), channel_id=1, source_target_pairs={{0,3},{1,2},{2,1},{3,0},{4,7},{5,6},{6,5},{7,4},{8,11},{9,10},{10,... | collective-permute-start | bytes 294920 | tf_op jit(solution)/shard_map/ppermute | solution.py:266
  30.5 5.1 %slice-start = ((s8[12582912]{0:T(1024)(128)(4,1)}), s8[4194304]{0:T(1024)(128)(4,1)S(1)}, s32[]{:S(2)}) async-start(s8[12582912]{0:T(1024)(128)(4,1)} %bitcast.4), calls=%async_computation | async-start | bytes 8388608
  30.5 5.1 %slice-start.1 = ((s8[12582912]{0:T(1024)(128)(4,1)}), s8[4194304]{0:T(1024)(128)(4,1)S(1)}, s32[]{:S(2)}) async-start(s8[12582912]{0:T(1024)(128)(4,1)} %bitcast.4), calls=%async_computation.1 | async-start | bytes 8388608
  33.4 2.3 %slice-start.2 = ((s8[12582912]{0:T(1024)(128)(4,1)}), s8[4194304]{0:T(1024)(128)(4,1)S(1)}, s32[]{:S(2)}) async-start(s8[12582912]{0:T(1024)(128)(4,1)} %bitcast.4), calls=%async_computation.2 | async-start | bytes 8388608
  36.8 4.9 %collective-permute-start.12 = (bf16[64,768]{1,0:T(8,128)(2,1)S(1)}, bf16[64,768]{1,0:T(8,128)(2,1)S(1)}, u32[]{:S(2)}, u32[]{:S(2)}) collective-permute-start(bf16[64,768]{1,0:T(8,128)(2,1)S(1)} %get-tuple-element.76), channel_id=1, source_target_pairs={{0,1},{1,0},{2,3},{3,2},{4,5},{5,4},{6,7},{7,6},{8,9},{9,8},{10,11... | collective-permute-start | bytes 294920 | tf_op jit(solution)/shard_map/ppermute | solution.py:266
  37.0 5.6 %collective-permute-start.13 = (bf16[64,768]{1,0:T(8,128)(2,1)S(1)}, bf16[64,768]{1,0:T(8,128)(2,1)S(1)}, u32[]{:S(2)}, u32[]{:S(2)}) collective-permute-start(bf16[64,768]{1,0:T(8,128)(2,1)S(1)} %get-tuple-element.77), channel_id=1, source_target_pairs={{0,2},{1,3},{2,0},{3,1},{4,6},{5,7},{6,4},{7,5},{8,10},{9,11},{10,... | collective-permute-start | bytes 294920 | tf_op jit(solution)/shard_map/ppermute | solution.py:266
  38.4 5.2 %collective-permute-start.14 = (bf16[64,768]{1,0:T(8,128)(2,1)S(1)}, bf16[64,768]{1,0:T(8,128)(2,1)S(1)}, u32[]{:S(2)}, u32[]{:S(2)}) collective-permute-start(bf16[64,768]{1,0:T(8,128)(2,1)S(1)} %get-tuple-element.78), channel_id=1, source_target_pairs={{0,3},{1,2},{2,1},{3,0},{4,7},{5,6},{6,5},{7,4},{8,11},{9,10},{10,... | collective-permute-start | bytes 294920 | tf_op jit(solution)/shard_map/ppermute | solution.py:266
  39.7 8.9 %collective-permute-start.23 = (bf16[64,768]{1,0:T(8,128)(2,1)S(1)}, bf16[64,768]{1,0:T(8,128)(2,1)S(1)}, u32[]{:S(2)}, u32[]{:S(2)}) collective-permute-start(bf16[64,768]{1,0:T(8,128)(2,1)S(1)} %get-tuple-element.88), channel_id=1, source_target_pairs={{0,1},{1,0},{2,3},{3,2},{4,5},{5,4},{6,7},{7,6},{8,9},{9,8},{10,11... | collective-permute-start | bytes 294920 | tf_op jit(solution)/shard_map/ppermute | solution.py:266
  40.2 10.0 %collective-permute-start.24 = (bf16[64,768]{1,0:T(8,128)(2,1)S(1)}, bf16[64,768]{1,0:T(8,128)(2,1)S(1)}, u32[]{:S(2)}, u32[]{:S(2)}) collective-permute-start(bf16[64,768]{1,0:T(8,128)(2,1)S(1)} %get-tuple-element.89), channel_id=1, source_target_pairs={{0,2},{1,3},{2,0},{3,1},{4,6},{5,7},{6,4},{7,5},{8,10},{9,11},{10,... | collective-permute-start | bytes 294920 | tf_op jit(solution)/shard_map/ppermute | solution.py:266
  41.6 8.5 %collective-permute-start.25 = (bf16[64,768]{1,0:T(8,128)(2,1)S(1)}, bf16[64,768]{1,0:T(8,128)(2,1)S(1)}, u32[]{:S(2)}, u32[]{:S(2)}) collective-permute-start(bf16[64,768]{1,0:T(8,128)(2,1)S(1)} %get-tuple-element.90), channel_id=1, source_target_pairs={{0,3},{1,2},{2,1},{3,0},{4,7},{5,6},{6,5},{7,4},{8,11},{9,10},{10,... | collective-permute-start | bytes 294920 | tf_op jit(solution)/shard_map/ppermute | solution.py:266
  44.0 12.5 %collective-permute-start.15 = (bf16[128,768]{1,0:T(8,128)(2,1)S(1)}, bf16[128,768]{1,0:T(8,128)(2,1)S(1)}, u32[]{:S(2)}, u32[]{:S(2)}) collective-permute-start(bf16[128,768]{1,0:T(8,128)(2,1)S(1)} %combine.4.refs_0_), channel_id=1, source_target_pairs={{0,12},{4,8},{8,4},{12,0},{1,13},{5,9},{9,5},{13,1},{2,14},{6,10},... | collective-permute-start | bytes 589832 | tf_op jit(solution)/shard_map/ppermute | solution.py:266
  48.1 3.4 %collective-permute-start.19 = (bf16[64,768]{1,0:T(8,128)(2,1)S(1)}, bf16[64,768]{1,0:T(8,128)(2,1)S(1)}, u32[]{:S(2)}, u32[]{:S(2)}) collective-permute-start(bf16[64,768]{1,0:T(8,128)(2,1)S(1)} %get-tuple-element.84), channel_id=1, source_target_pairs={{0,1},{1,0},{2,3},{3,2},{4,5},{5,4},{6,7},{7,6},{8,9},{9,8},{10,11... | collective-permute-start | bytes 294920 | tf_op jit(solution)/shard_map/ppermute | solution.py:266
  48.7 5.1 %collective-permute-start.20 = (bf16[64,768]{1,0:T(8,128)(2,1)S(1)}, bf16[64,768]{1,0:T(8,128)(2,1)S(1)}, u32[]{:S(2)}, u32[]{:S(2)}) collective-permute-start(bf16[64,768]{1,0:T(8,128)(2,1)S(1)} %get-tuple-element.85), channel_id=1, source_target_pairs={{0,2},{1,3},{2,0},{3,1},{4,6},{5,7},{6,4},{7,5},{8,10},{9,11},{10,... | collective-permute-start | bytes 294920 | tf_op jit(solution)/shard_map/ppermute | solution.py:266
  50.2 5.1 %collective-permute-start.21 = (bf16[64,768]{1,0:T(8,128)(2,1)S(1)}, bf16[64,768]{1,0:T(8,128)(2,1)S(1)}, u32[]{:S(2)}, u32[]{:S(2)}) collective-permute-start(bf16[64,768]{1,0:T(8,128)(2,1)S(1)} %get-tuple-element.86), channel_id=1, source_target_pairs={{0,3},{1,2},{2,1},{3,0},{4,7},{5,6},{6,5},{7,4},{8,11},{9,10},{10,... | collective-permute-start | bytes 294920 | tf_op jit(solution)/shard_map/ppermute | solution.py:266
  50.5 15.1 %collective-permute-start.26 = (bf16[128,768]{1,0:T(8,128)(2,1)S(1)}, bf16[128,768]{1,0:T(8,128)(2,1)S(1)}, u32[]{:S(2)}, u32[]{:S(2)}) collective-permute-start(bf16[128,768]{1,0:T(8,128)(2,1)S(1)} %combine.6), channel_id=1, source_target_pairs={{0,8},{4,12},{8,0},{12,4},{1,9},{5,13},{9,1},{13,5},{2,10},{6,14},... | collective-permute-start | bytes 589832 | tf_op jit(solution)/shard_map/ppermute | solution.py:266
  55.6 11.2 %collective-permute-start.22 = (bf16[128,768]{1,0:T(8,128)(2,1)S(1)}, bf16[128,768]{1,0:T(8,128)(2,1)S(1)}, u32[]{:S(2)}, u32[]{:S(2)}) collective-permute-start(bf16[128,768]{1,0:T(8,128)(2,1)S(1)} %combine.5), channel_id=1, source_target_pairs={{0,4},{4,0},{8,12},{12,8},{1,5},{5,1},{9,13},{13,9},{2,6},{6,2},{1... | collective-permute-start | bytes 589832 | tf_op jit(solution)/shard_map/ppermute | solution.py:266
  57.5 9.3 %collective-permute-start.16 = (bf16[64,768]{1,0:T(8,128)(2,1)S(1)}, bf16[64,768]{1,0:T(8,128)(2,1)S(1)}, u32[]{:S(2)}, u32[]{:S(2)}) collective-permute-start(bf16[64,768]{1,0:T(8,128)(2,1)S(1)} %get-tuple-element.80), channel_id=1, source_target_pairs={{0,1},{1,0},{2,3},{3,2},{4,5},{5,4},{6,7},{7,6},{8,9},{9,8},{10,11... | collective-permute-start | bytes 294920 | tf_op jit(solution)/shard_map/ppermute | solution.py:266
  57.8 9.0 %collective-permute-start.17 = (bf16[64,768]{1,0:T(8,128)(2,1)S(1)}, bf16[64,768]{1,0:T(8,128)(2,1)S(1)}, u32[]{:S(2)}, u32[]{:S(2)}) collective-permute-start(bf16[64,768]{1,0:T(8,128)(2,1)S(1)} %get-tuple-element.81), channel_id=1, source_target_pairs={{0,2},{1,3},{2,0},{3,1},{4,6},{5,7},{6,4},{7,5},{8,10},{9,11},{10,... | collective-permute-start | bytes 294920 | tf_op jit(solution)/shard_map/ppermute | solution.py:266
  59.2 7.6 %collective-permute-start.18 = (bf16[64,768]{1,0:T(8,128)(2,1)S(1)}, bf16[64,768]{1,0:T(8,128)(2,1)S(1)}, u32[]{:S(2)}, u32[]{:S(2)}) collective-permute-start(bf16[64,768]{1,0:T(8,128)(2,1)S(1)} %get-tuple-element.82), channel_id=1, source_target_pairs={{0,3},{1,2},{2,1},{3,0},{4,7},{5,6},{6,5},{7,4},{8,11},{9,10},{10,... | collective-permute-start | bytes 294920 | tf_op jit(solution)/shard_map/ppermute | solution.py:266

commit v10 on v8

--- a/solution.py
+++ b/solution.py
@@ -24,7 +24,9 @@
     return [pltpu.with_memory_space_constraint(array, pltpu.VMEM) for array in arrays]
 
 
-def routing_kernel(me_ref, ids_ref, logits_ref, placed_ref, pick_ref, mix_ref, *, experts):
+def routing_kernel(
+    me_ref, ids_ref, logits_ref, after_ref, placed_ref, pick_ref, mix_ref, *, experts
+):
     rows = ids_ref.shape[1]
     capacity = placed_ref.shape[0] // experts
     relative = lax.bitwise_xor(ids_ref[...], me_ref[0])
@@ -54,7 +56,7 @@
     mix_ref[:, 1:2] = 1.0 - share
 
 
-def place(me, expert_ids, route_logits, experts, capacity):
+def place(me, expert_ids, route_logits, experts, capacity, after):
     rows = expert_ids.shape[0]
     return pl.pallas_call(
         functools.partial(routing_kernel, experts=experts),
@@ -64,11 +66,12 @@
             jax.ShapeDtypeStruct((rows, 2), F32),
         ],
         in_specs=[pl.BlockSpec(memory_space=pltpu.SMEM)]
-        + [pl.BlockSpec(memory_space=pltpu.VMEM)] * 2,
+        + [pl.BlockSpec(memory_space=pltpu.VMEM)] * 2
+        + [pl.BlockSpec(memory_space=pl.ANY)],
         out_specs=[pl.BlockSpec(memory_space=pltpu.VMEM)] * 3,
         compiler_params=params(),
         name="routing",
-    )(me.reshape(1), expert_ids.T, route_logits.T)
+    )(me.reshape(1), expert_ids.T, route_logits.T, *pinned([after]))
 
 
 def dispatch_kernel(placed_ref, *refs, count, waits):
@@ -286,19 +289,19 @@
         slices = [lax.all_gather(tokens, "tensor", axis=1, tiled=True)]
         parts = [everything]
         groups = [[0]]
-    placed, pick, mix = place(me, expert_ids, route_logits, experts, capacity)
 
     def fetch(chosen, after):
         fetches = [(w, parts[i], width) for i in chosen for w in (gate_weight, up_weight)]
         return list(prefetch(column, fetches, after))
 
-    weights, arrived = fetch(groups[0], placed), []
+    weights, arrived = fetch(range(len(parts))[:3], tokens), []
+    placed, pick, mix = place(me, expert_ids, route_logits, experts, capacity, weights[0])
     for group in groups:
         after = weights[-1:] if len(arrived) < 2 else []
         outgoing = dispatch(placed, [slices[i] for i in group], experts, capacity, after)
         arrived.append([swap(block, "expert", e) for e, block in enumerate(outgoing)])
         if len(arrived) == 1 and len(groups) > 1:
-            weights += fetch([2, 3], outgoing[0])
+            weights += fetch([3], outgoing[0])
     sums = None
     for group, x_blocks in zip(groups, arrived):
         chosen = weights[2 * group[0] : 2 * group[-1] + 2]
@@ -313,12 +316,12 @@
     if not doubling:
         mixed = combine(pick, mix, returned(everything), [])
         return lax.psum_scatter(mixed, "tensor", scatter_dimension=1, tiled=True)
-    blocks = [returned(across(3)), returned(across(2))]
-    passed = swap(combine(pick, mix, blocks[0], [], blocks[1][2:3]), "tensor", 1)
-    onwards = combine(pick, mix, blocks[1], [passed])
-    over = swap(onwards, "tensor", 2)
-    beside = swap(combine(pick, mix, returned(across(1), [onwards]), []), "tensor", 1)
-    return combine(pick, mix, returned(across(0), [onwards]), [beside, over])
+    passed = swap(combine(pick, mix, returned(across(3)), []), "tensor", 1)
+    over = swap(combine(pick, mix, returned(across(2)), [passed]), "tensor", 2)
+    near = returned(across(1), [passed])
+    own = returned(across(0), [passed])
+    beside = swap(combine(pick, mix, near, [], own[1:2]), "tensor", 1)
+    return combine(pick, mix, own, [beside, over])
 
 
 def solution(mesh):

time: 75.3 us -> 73.1 us (0.971)
  starting transfers between devices: 27.3 us -> 25.6 us
    ppermute x27, starting transfers between devices: 27.3 us -> 25.6 us  [swap(): return lax.ppermute(value, axis, [(i, i ^ distance) for i in range(count)])]
  transfers between devices with their start and end apart: 27 -> 27, of which waited for: 13 -> 10; matrix products, arithmetic and copies ran while one was open for 0% -> 0% of each run, Pallas kernels for 23% -> 27%
where the time goes in v10:
time: 73.1 us; the launch traced here: 73 us
  starting transfers between devices  25.6 us (35%)
  Pallas kernels  24.2 us (33%)
  waiting for transfers between devices  21.4 us (29%)
  local copies, waits for them, and re-layouts  1.48 us (2%)
    ppermute x27, starting transfers between devices, swap(): return lax.ppermute(value, axis, [(i, i ^ distance) for i in range(count)])  25.6 us
    ppermute x27, waiting for transfers between devices, swap(): return lax.ppermute(value, axis, [(i, i ^ distance) for i in range(count)])  21.4 us
    pallas_call x2, Pallas kernels, prefetch(): pl.pallas_call(functools.partial(prefetch_kernel, parts=[part for _, part...  9.37 us
    pallas_call x3, Pallas kernels, gate_up(): pl.pallas_call(functools.partial(gate_up_kernel, experts=experts, slices=...  7.78 us
    pallas_call x4, Pallas kernels, down(): pl.pallas_call(functools.partial(down_kernel, part=part, waits=len(after)...  4.09 us
    pallas_call x4, Pallas kernels, combine(): pl.pallas_call(functools.partial(combine_kernel, experts=len(blocks), sum...  1.94 us
    unnamed x12, local copies, waits for them, and re-layouts  1.48 us
  transfers between devices with their start and end apart: 27, of which 10 were waited for; matrix products, arithmetic and copies ran while one was open for 0% of the time, Pallas kernels for 27%

profile of v10, /device:TPU:0, one launch (start us, length us, event | category | flops | bytes accessed | tf_op | source)
XLA Modules:
  0.0 73.0 jit_solution(13523897560825225836)
XLA Ops:
  0.0 4.0 %collective-permute-start = (bf16[128,768]{1,0:T(8,128)(2,1)}, bf16[128,768]{1,0:T(8,128)(2,1)S(1)}, u32[]{:S(2)}, u32[]{:S(2)}) collective-permute-start(bf16[128,768]{1,0:T(8,128)(2,1)} %refs_0_.4), channel_id=1, source_target_pairs={{0,8},{4,12},{8,0},{12,4},{1,9},{5,13},{9,1},{13,5},{2,10},{6,14},... | collective-permute-start | bytes 589832 | tf_op jit(solution)/shard_map/ppermute | solution.py:270
  4.0 1.6 %collective-permute-start.5 = (bf16[128,768]{1,0:T(8,128)(2,1)}, bf16[128,768]{1,0:T(8,128)(2,1)S(1)}, u32[]{:S(2)}, u32[]{:S(2)}) collective-permute-start(bf16[128,768]{1,0:T(8,128)(2,1)} %refs_0_.4), channel_id=1, source_target_pairs={{0,4},{4,0},{8,12},{12,8},{1,5},{5,1},{9,13},{13,9},{2,6},{6,2},{1... | collective-permute-start | bytes 589832 | tf_op jit(solution)/shard_map/ppermute | solution.py:270
  5.6 1.0 %copy-done = bf16[128,768]{1,0:T(8,128)(2,1)S(1)} copy-done((bf16[128,768]{1,0:T(8,128)(2,1)S(1)}, bf16[128,768]{1,0:T(8,128)(2,1)}, u32[]{:S(2)}) %copy-start) | copy-done | bytes 196632
  6.6 6.5 %prefetch.2 = (bf16[768,2048]{1,0:T(8,128)(2,1)S(1)}, bf16[768,2048]{1,0:T(8,128)(2,1)S(1)}, bf16[768,2048]{1,0:T(8,128)(2,1)S(1)}, bf16[768,2048]{1,0:T(8,128)(...) custom-call(s32[1]{0:T(128)} %bitcast.3.column_ref, bf16[128,768]{1,0:T(8,128)(2,1)S(1)} %copy-done, ...), custom_call_target="tpu_custom_call" | custom-call | bytes 18874368 | tf_op jit(solution)/shard_map/prefetch/pallas_call | solution.py:130
  13.5 0.7 collective-permute-start.1
  14.2 0.4 dispatch.4
  14.6 1.6 %collective-permute-start.10 = (bf16[64,1536]{1,0:T(8,128)(2,1)S(1)}, bf16[64,1536]{1,0:T(8,128)(2,1)S(1)}, u32[]{:S(2)}, u32[]{:S(2)}) collective-permute-start(bf16[64,1536]{1,0:T(8,128)(2,1)S(1)} %get-tuple-element.66), channel_id=1, source_target_pairs={{0,2},{1,3},{2,0},{3,1},{4,6},{5,7},{6,4},{7,5},{8,10},{9,11},{10,... | collective-permute-start | bytes 589832 | tf_op jit(solution)/shard_map/ppermute | solution.py:270
  16.1 0.6 collective-permute-start.9
  16.8 2.9 %prefetch.3 = (bf16[768,2048]{1,0:T(8,128)(2,1)S(1)}, bf16[768,2048]{1,0:T(8,128)(2,1)S(1)}) custom-call(s32[1]{0:T(128)} %bitcast.3.column_ref, bf16[64,1536]{1,0:T(8,128)(2,1)S(1)} %get-tuple-element.57.after_ref.refs_0_, bf16[1,3072,2048]{2,1,0:T(8,128)(2,1)} %refs_0_.5, bf16[1,3072,2048]{2,1,0:T(8,128)(2,1)} %refs_1_.3), custom_call_target="tpu_custom_call" | custom-call | bytes 6291456 | tf_op jit(solution)/shard_map/prefetch/pallas_call | solution.py:130
  19.6 0.3 dispatch.5
  20.0 1.6 %collective-permute-start.7 = (bf16[64,768]{1,0:T(8,128)(2,1)S(1)}, bf16[64,768]{1,0:T(8,128)(2,1)S(1)}, u32[]{:S(2)}, u32[]{:S(2)}) collective-permute-start(bf16[64,768]{1,0:T(8,128)(2,1)S(1)} %get-tuple-element.62), channel_id=1, source_target_pairs={{0,2},{1,3},{2,0},{3,1},{4,6},{5,7},{6,4},{7,5},{8,10},{9,11},{10,... | collective-permute-start | bytes 294920 | tf_op jit(solution)/shard_map/ppermute | solution.py:270
  21.6 0.3 dispatch.3
  21.8 0.7 collective-permute-start.8
  22.5 0.4 collective-permute-start.2
  22.9 2.8 %collective-permute-done.11.refs_3_ = bf16[64,1536]{1,0:T(8,128)(2,1)S(1)} collective-permute-done((bf16[64,1536]{1,0:T(8,128)(2,1)S(1)}, bf16[64,1536]{1,0:T(8,128)(2,1)S(1)}, u32[]{:S(2)}, u32[]{:S(2)}) %collective-permute-start.11) | collective-permute-done | bytes 196640 | tf_op jit(solution)/shard_map/ppermute | solution.py:270
  25.7 0.5 collective-permute-start.3
  26.2 1.9 %collective-permute-start.4 = (bf16[64,768]{1,0:T(8,128)(2,1)S(1)}, bf16[64,768]{1,0:T(8,128)(2,1)S(1)}, u32[]{:S(2)}, u32[]{:S(2)}) collective-permute-start(bf16[64,768]{1,0:T(8,128)(2,1)S(1)} %get-tuple-element.55), channel_id=1, source_target_pairs={{0,3},{1,2},{2,1},{3,0},{4,7},{5,6},{6,5},{7,4},{8,11},{9,10},{10,... | collective-permute-start | bytes 294920 | tf_op jit(solution)/shard_map/ppermute | solution.py:270
  28.1 3.5 %gate_up.3 = (f32[256,2048]{1,0:T(8,128)S(1)}, f32[256,2048]{1,0:T(8,128)S(1)}) custom-call(bf16[64,1536]{1,0:T(8,128)(2,1)S(1)} %get-tuple-element.57.after_ref.refs_0_, bf16[64,1536]{1,0:T(8,128)(2,1)S(1)} %collective-permute-done.9.refs_1_, bf16[64,1536]{1,0:T(8,128)(2,1)S(1)} %collective-permute-done.10.refs_2_, ...), custom_call_target="tpu_custom_call" | custom-call | flops 3221225472 | bytes 12582912 | tf_op jit(solution)/shard_map/gate_up/pallas_call | solution.py:186
  31.7 2.2 %gate_up.4 = (f32[256,2048]{1,0:T(8,128)S(1)}, f32[256,2048]{1,0:T(8,128)S(1)}) custom-call(bf16[64,768]{1,0:T(8,128)(2,1)S(1)} %get-tuple-element.60.refs_0_, bf16[64,768]{1,0:T(8,128)(2,1)S(1)} %collective-permute-done.6.refs_8_.refs_1_, bf16[64,768]{1,0:T(8,128)(2,1)S(1)} %collective-permute-done.7.refs_2_, ...), custom_call_target="tpu_custom_call", output_to_operand_aliasing={{0}: (6, {}), {1}: (7, {})} | custom-call | flops 1610612736 | bytes 6291456 | tf_op jit(solution)/shard_map/gate_up/pallas_call | solution.py:186
  33.9 2.1 %gate_up.5.h_ref = bf16[256,2048]{1,0:T(8,128)(2,1)S(1)} custom-call(bf16[64,768]{1,0:T(8,128)(2,1)S(1)} %get-tuple-element.52.refs_0_, bf16[64,768]{1,0:T(8,128)(2,1)S(1)} %collective-permute-done.2.refs_1_, bf16[64,768]{1,0:T(8,128)(2,1)S(1)} %collective-permute-done.3.refs_2_, bf16[64,768]{1,0:T(8,128)(2,1)S(1)} %collective-permute-done.4.refs_3_, ...), custom_call_target="tpu_custom_call" | custom-call | flops 1610612736 | bytes 6291456 | tf_op jit(solution)/shard_map/gate_up/pallas_call | solution.py:186
  36.0 0.5 slice-done.2
  36.5 1.0 %down.4 = (bf16[64,768]{1,0:T(8,128)(2,1)S(1)}, bf16[64,768]{1,0:T(8,128)(2,1)S(1)}, bf16[64,768]{1,0:T(8,128)(2,1)S(1)}, bf16[64,768]{1,0:T(8,128)(2,1)S(1)}) custom-call(s32[1]{0:T(128)} %bitcast.3.column_ref, bf16[256,2048]{1,0:T(8,128)(2,1)S(1)} %gate_up.5.h_ref, bf16[1,2048,3072]{2,1,0:T(8,128)(2,1)S(1)} %bitcast.5), custom_call_target="tpu_custom_call" | custom-call | flops 805306368 | bytes 3538944 | tf_op jit(solution)/shard_map/down/pallas_call | solution.py:224
  37.6 1.6 %collective-permute-start.13 = (bf16[64,768]{1,0:T(8,128)(2,1)S(1)}, bf16[64,768]{1,0:T(8,128)(2,1)S(1)}, u32[]{:S(2)}, u32[]{:S(2)}) collective-permute-start(bf16[64,768]{1,0:T(8,128)(2,1)S(1)} %get-tuple-element.77), channel_id=1, source_target_pairs={{0,2},{1,3},{2,0},{3,1},{4,6},{5,7},{6,4},{7,5},{8,10},{9,11},{10,... | collective-permute-start | bytes 294920 | tf_op jit(solution)/shard_map/ppermute | solution.py:270
  39.2 0.3 collective-permute-start.14
  39.5 3.8 %collective-permute-done.13.refs_2_ = bf16[64,768]{1,0:T(8,128)(2,1)S(1)} collective-permute-done((bf16[64,768]{1,0:T(8,128)(2,1)S(1)}, bf16[64,768]{1,0:T(8,128)(2,1)S(1)}, u32[]{:S(2)}, u32[]{:S(2)}) %collective-permute-start.13) | collective-permute-done | bytes 98336 | tf_op jit(solution)/shard_map/ppermute | solution.py:270
  43.3 1.2 %collective-permute-done.14.refs_3_ = bf16[64,768]{1,0:T(8,128)(2,1)S(1)} collective-permute-done((bf16[64,768]{1,0:T(8,128)(2,1)S(1)}, bf16[64,768]{1,0:T(8,128)(2,1)S(1)}, u32[]{:S(2)}, u32[]{:S(2)}) %collective-permute-start.14) | collective-permute-done | bytes 98336 | tf_op jit(solution)/shard_map/ppermute | solution.py:270
  44.5 0.3 combine.4
  44.8 0.5 collective-permute-start.15
  45.3 1.0 %down.7 = (bf16[64,768]{1,0:T(8,128)(2,1)S(1)}, bf16[64,768]{1,0:T(8,128)(2,1)S(1)}, bf16[64,768]{1,0:T(8,128)(2,1)S(1)}, bf16[64,768]{1,0:T(8,128)(2,1)S(1)}) custom-call(s32[1]{0:T(128)} %bitcast.3.column_ref, bf16[256,2048]{1,0:T(8,128)(2,1)S(1)} %gate_up.5.h_ref, bf16[1,2048,3072]{2,1,0:T(8,128)(2,1)S(1)} %bitcast.5), custom_call_target="tpu_custom_call" | custom-call | flops 805306368 | bytes 3538944 | tf_op jit(solution)/shard_map/down/pallas_call | solution.py:224
  46.4 1.6 %collective-permute-start.24 = (bf16[64,768]{1,0:T(8,128)(2,1)S(1)}, bf16[64,768]{1,0:T(8,128)(2,1)S(1)}, u32[]{:S(2)}, u32[]{:S(2)}) collective-permute-start(bf16[64,768]{1,0:T(8,128)(2,1)S(1)} %get-tuple-element.89), channel_id=1, source_target_pairs={{0,2},{1,3},{2,0},{3,1},{4,6},{5,7},{6,4},{7,5},{8,10},{9,11},{10,... | collective-permute-start | bytes 294920 | tf_op jit(solution)/shard_map/ppermute | solution.py:270
  48.3 3.7 %collective-permute-done.15.refs_0_.refs_4_ = bf16[128,768]{1,0:T(8,128)(2,1)S(1)} collective-permute-done((bf16[128,768]{1,0:T(8,128)(2,1)S(1)}, bf16[128,768]{1,0:T(8,128)(2,1)S(1)}, u32[]{:S(2)}, u32[]{:S(2)}) %collective-permute-start.15) | collective-permute-done | bytes 196640 | tf_op jit(solution)/shard_map/ppermute | solution.py:270
  52.0 1.0 %down.6 = (bf16[64,768]{1,0:T(8,128)(2,1)S(1)}, bf16[64,768]{1,0:T(8,128)(2,1)S(1)}, bf16[64,768]{1,0:T(8,128)(2,1)S(1)}, bf16[64,768]{1,0:T(8,128)(2,1)S(1)}) custom-call(s32[1]{0:T(128)} %bitcast.3.column_ref, bf16[256,2048]{1,0:T(8,128)(2,1)S(1)} %gate_up.5.h_ref, bf16[1,2048,3072]{2,1,0:T(8,128)(2,1)S(1)} %bitcast.5, ...), custom_call_target="tpu_custom_call" | custom-call | flops 805306368 | bytes 3538944 | tf_op jit(solution)/shard_map/down/pallas_call | solution.py:224
  53.1 1.6 %collective-permute-start.20 = (bf16[64,768]{1,0:T(8,128)(2,1)S(1)}, bf16[64,768]{1,0:T(8,128)(2,1)S(1)}, u32[]{:S(2)}, u32[]{:S(2)}) collective-permute-start(bf16[64,768]{1,0:T(8,128)(2,1)S(1)} %get-tuple-element.85), channel_id=1, source_target_pairs={{0,2},{1,3},{2,0},{3,1},{4,6},{5,7},{6,4},{7,5},{8,10},{9,11},{10,... | collective-permute-start | bytes 294920 | tf_op jit(solution)/shard_map/ppermute | solution.py:270
  54.6 1.0 %down.5 = (bf16[64,768]{1,0:T(8,128)(2,1)S(1)}, bf16[64,768]{1,0:T(8,128)(2,1)S(1)}, bf16[64,768]{1,0:T(8,128)(2,1)S(1)}, bf16[64,768]{1,0:T(8,128)(2,1)S(1)}) custom-call(s32[1]{0:T(128)} %bitcast.3.column_ref, bf16[256,2048]{1,0:T(8,128)(2,1)S(1)} %gate_up.5.h_ref, bf16[1,2048,3072]{2,1,0:T(8,128)(2,1)S(1)} %bitcast.5, ...), custom_call_target="tpu_custom_call" | custom-call | flops 805306368 | bytes 3538944 | tf_op jit(solution)/shard_map/down/pallas_call | solution.py:224
  55.7 0.4 collective-permute-start.21
  56.0 0.3 collective-permute-start.16
  56.4 0.3 combine.6
  56.7 3.3 %collective-permute-start.26 = (bf16[128,768]{1,0:T(8,128)(2,1)S(1)}, bf16[128,768]{1,0:T(8,128)(2,1)S(1)}, u32[]{:S(2)}, u32[]{:S(2)}) collective-permute-start(bf16[128,768]{1,0:T(8,128)(2,1)S(1)} %combine.6), channel_id=1, source_target_pairs={{0,8},{4,12},{8,0},{12,4},{1,9},{5,13},{9,1},{13,5},{2,10},{6,14},... | collective-permute-start | bytes 589832 | tf_op jit(solution)/shard_map/ppermute | solution.py:270
  60.0 0.5 collective-permute-done.21.refs_3_
  60.5 0.3 combine.5
  60.8 0.7 collective-permute-start.22
  61.5 0.9 %collective-permute-start.17 = (bf16[64,768]{1,0:T(8,128)(2,1)S(1)}, bf16[64,768]{1,0:T(8,128)(2,1)S(1)}, u32[]{:S(2)}, u32[]{:S(2)}) collective-permute-start(bf16[64,768]{1,0:T(8,128)(2,1)S(1)} %get-tuple-element.81), channel_id=1, source_target_pairs={{0,2},{1,3},{2,0},{3,1},{4,6},{5,7},{6,4},{7,5},{8,10},{9,11},{10,... | collective-permute-start | bytes 294920 | tf_op jit(solution)/shard_map/ppermute | solution.py:270
  62.3 0.3 collective-permute-start.18
  62.7 4.2 %collective-permute-done.17.refs_2_ = bf16[64,768]{1,0:T(8,128)(2,1)S(1)} collective-permute-done((bf16[64,768]{1,0:T(8,128)(2,1)S(1)}, bf16[64,768]{1,0:T(8,128)(2,1)S(1)}, u32[]{:S(2)}, u32[]{:S(2)}) %collective-permute-start.17) | collective-permute-done | bytes 98336 | tf_op jit(solution)/shard_map/ppermute | solution.py:270
  66.9 0.6 collective-permute-done.18.refs_3_
  67.4 1.9 %collective-permute-done.26.refs_5_ = bf16[128,768]{1,0:T(8,128)(2,1)S(1)} collective-permute-done((bf16[128,768]{1,0:T(8,128)(2,1)S(1)}, bf16[128,768]{1,0:T(8,128)(2,1)S(1)}, u32[]{:S(2)}, u32[]{:S(2)}) %collective-permute-start.26) | collective-permute-done | bytes 196640 | tf_op jit(solution)/shard_map/ppermute | solution.py:270
  69.3 2.7 %collective-permute-done.22.refs_4_ = bf16[128,768]{1,0:T(8,128)(2,1)S(1)} collective-permute-done((bf16[128,768]{1,0:T(8,128)(2,1)S(1)}, bf16[128,768]{1,0:T(8,128)(2,1)S(1)}, u32[]{:S(2)}, u32[]{:S(2)}) %collective-permute-start.22) | collective-permute-done | bytes 196640 | tf_op jit(solution)/shard_map/ppermute | solution.py:270
  72.0 1.0 %combine.7 = bf16[128,768]{1,0:T(8,128)(2,1)} custom-call(bf16[256,256]{1,0:T(8,128)(2,1)S(1)} %get-tuple-element.49.pick_ref, f32[128,2]{1,0:T(8,128)S(1)} %get-tuple-element.50.mix_ref, bf16[64,768]{1,0:T(8,128)(2,1)S(1)} %get-tuple-element.79.refs_0_, bf16[64,768]{1,0:T(8,128)(2,1)S(1)} %collective-permute-done.16.refs_4_.refs_1_, ...), custom_call_target="tpu_custom_call" | custom-call | flops 100663296 | bytes 589824 | tf_op jit(solution)/shard_map/combine/pallas_call | solution.py:254
  (36 shorter events, 0.9 us)
Async XLA Ops:
  0.0 13.5 %collective-permute-start = (bf16[128,768]{1,0:T(8,128)(2,1)}, bf16[128,768]{1,0:T(8,128)(2,1)S(1)}, u32[]{:S(2)}, u32[]{:S(2)}) collective-permute-start(bf16[128,768]{1,0:T(8,128)(2,1)} %refs_0_.4), channel_id=1, source_target_pairs={{0,8},{4,12},{8,0},{12,4},{1,9},{5,13},{9,1},{13,5},{2,10},{6,14},... | collective-permute-start | bytes 589832 | tf_op jit(solution)/shard_map/ppermute | solution.py:270
  4.0 10.2 %collective-permute-start.5 = (bf16[128,768]{1,0:T(8,128)(2,1)}, bf16[128,768]{1,0:T(8,128)(2,1)S(1)}, u32[]{:S(2)}, u32[]{:S(2)}) collective-permute-start(bf16[128,768]{1,0:T(8,128)(2,1)} %refs_0_.4), channel_id=1, source_target_pairs={{0,4},{4,0},{8,12},{12,8},{1,5},{5,1},{9,13},{13,9},{2,6},{6,2},{1... | collective-permute-start | bytes 589832 | tf_op jit(solution)/shard_map/ppermute | solution.py:270
  5.6 1.0 %copy-start = (bf16[128,768]{1,0:T(8,128)(2,1)S(1)}, bf16[128,768]{1,0:T(8,128)(2,1)}, u32[]{:S(2)}) copy-start(bf16[128,768]{1,0:T(8,128)(2,1)} %refs_0_.4) | copy-start | bytes 589828
  6.6 6.5 %copy-start.1 = (s32[128,2]{0,1:T(2,128)S(1)}, s32[128,2]{0,1:T(2,128)}, u32[]{:S(2)}) copy-start(s32[128,2]{0,1:T(2,128)} %param.7) | copy-start | bytes 3076
  6.6 6.5 %copy-start.2 = (f32[128,2]{0,1:T(2,128)S(1)}, f32[128,2]{0,1:T(2,128)}, u32[]{:S(2)}) copy-start(f32[128,2]{0,1:T(2,128)} %param.8) | copy-start | bytes 3076
  13.5 6.5 %collective-permute-start.1 = (bf16[128,768]{1,0:T(8,128)(2,1)S(1)}, bf16[128,768]{1,0:T(8,128)(2,1)S(1)}, u32[]{:S(2)}, u32[]{:S(2)}) collective-permute-start(bf16[128,768]{1,0:T(8,128)(2,1)S(1)} %collective-permute-done.refs_0_), channel_id=1, source_target_pairs={{0,4},{4,0},{8,12},{12,8},{1,5},{5,1},{9,13},{13,9},{2,6},{6,2},{1... | collective-permute-start | bytes 589832 | tf_op jit(solution)/shard_map/ppermute | solution.py:270
  14.6 8.0 %collective-permute-start.10 = (bf16[64,1536]{1,0:T(8,128)(2,1)S(1)}, bf16[64,1536]{1,0:T(8,128)(2,1)S(1)}, u32[]{:S(2)}, u32[]{:S(2)}) collective-permute-start(bf16[64,1536]{1,0:T(8,128)(2,1)S(1)} %get-tuple-element.66), channel_id=1, source_target_pairs={{0,2},{1,3},{2,0},{3,1},{4,6},{5,7},{6,4},{7,5},{8,10},{9,11},{10,... | collective-permute-start | bytes 589832 | tf_op jit(solution)/shard_map/ppermute | solution.py:270
  16.1 9.5 %collective-permute-start.11 = (bf16[64,1536]{1,0:T(8,128)(2,1)S(1)}, bf16[64,1536]{1,0:T(8,128)(2,1)S(1)}, u32[]{:S(2)}, u32[]{:S(2)}) collective-permute-start(bf16[64,1536]{1,0:T(8,128)(2,1)S(1)} %get-tuple-element.67), channel_id=1, source_target_pairs={{0,3},{1,2},{2,1},{3,0},{4,7},{5,6},{6,5},{7,4},{8,11},{9,10},{10,... | collective-permute-start | bytes 589832 | tf_op jit(solution)/shard_map/ppermute | solution.py:270
  16.1 10.1 %collective-permute-start.9 = (bf16[64,1536]{1,0:T(8,128)(2,1)S(1)}, bf16[64,1536]{1,0:T(8,128)(2,1)S(1)}, u32[]{:S(2)}, u32[]{:S(2)}) collective-permute-start(bf16[64,1536]{1,0:T(8,128)(2,1)S(1)} %get-tuple-element.65), channel_id=1, source_target_pairs={{0,1},{1,0},{2,3},{3,2},{4,5},{5,4},{6,7},{7,6},{8,9},{9,8},{10,11... | collective-permute-start | bytes 589832 | tf_op jit(solution)/shard_map/ppermute | solution.py:270
  19.9 1.9 %collective-permute-start.6 = (bf16[64,768]{1,0:T(8,128)(2,1)S(1)}, bf16[64,768]{1,0:T(8,128)(2,1)S(1)}, u32[]{:S(2)}, u32[]{:S(2)}) collective-permute-start(bf16[64,768]{1,0:T(8,128)(2,1)S(1)} %get-tuple-element.61), channel_id=1, source_target_pairs={{0,1},{1,0},{2,3},{3,2},{4,5},{5,4},{6,7},{7,6},{8,9},{9,8},{10,11... | collective-permute-start | bytes 294920 | tf_op jit(solution)/shard_map/ppermute | solution.py:270
  20.0 11.6 %collective-permute-start.7 = (bf16[64,768]{1,0:T(8,128)(2,1)S(1)}, bf16[64,768]{1,0:T(8,128)(2,1)S(1)}, u32[]{:S(2)}, u32[]{:S(2)}) collective-permute-start(bf16[64,768]{1,0:T(8,128)(2,1)S(1)} %get-tuple-element.62), channel_id=1, source_target_pairs={{0,2},{1,3},{2,0},{3,1},{4,6},{5,7},{6,4},{7,5},{8,10},{9,11},{10,... | collective-permute-start | bytes 294920 | tf_op jit(solution)/shard_map/ppermute | solution.py:270
  21.8 9.8 %collective-permute-start.8 = (bf16[64,768]{1,0:T(8,128)(2,1)S(1)}, bf16[64,768]{1,0:T(8,128)(2,1)S(1)}, u32[]{:S(2)}, u32[]{:S(2)}) collective-permute-start(bf16[64,768]{1,0:T(8,128)(2,1)S(1)} %get-tuple-element.63), channel_id=1, source_target_pairs={{0,3},{1,2},{2,1},{3,0},{4,7},{5,6},{6,5},{7,4},{8,11},{9,10},{10,... | collective-permute-start | bytes 294920 | tf_op jit(solution)/shard_map/ppermute | solution.py:270
  22.5 11.3 %collective-permute-start.2 = (bf16[64,768]{1,0:T(8,128)(2,1)S(1)}, bf16[64,768]{1,0:T(8,128)(2,1)S(1)}, u32[]{:S(2)}, u32[]{:S(2)}) collective-permute-start(bf16[64,768]{1,0:T(8,128)(2,1)S(1)} %get-tuple-element.53), channel_id=1, source_target_pairs={{0,1},{1,0},{2,3},{3,2},{4,5},{5,4},{6,7},{7,6},{8,9},{9,8},{10,11... | collective-permute-start | bytes 294920 | tf_op jit(solution)/shard_map/ppermute | solution.py:270
  25.7 8.2 %collective-permute-start.3 = (bf16[64,768]{1,0:T(8,128)(2,1)S(1)}, bf16[64,768]{1,0:T(8,128)(2,1)S(1)}, u32[]{:S(2)}, u32[]{:S(2)}) collective-permute-start(bf16[64,768]{1,0:T(8,128)(2,1)S(1)} %get-tuple-element.54), channel_id=1, source_target_pairs={{0,2},{1,3},{2,0},{3,1},{4,6},{5,7},{6,4},{7,5},{8,10},{9,11},{10,... | collective-permute-start | bytes 294920 | tf_op jit(solution)/shard_map/ppermute | solution.py:270
  26.2 7.7 %collective-permute-start.4 = (bf16[64,768]{1,0:T(8,128)(2,1)S(1)}, bf16[64,768]{1,0:T(8,128)(2,1)S(1)}, u32[]{:S(2)}, u32[]{:S(2)}) collective-permute-start(bf16[64,768]{1,0:T(8,128)(2,1)S(1)} %get-tuple-element.55), channel_id=1, source_target_pairs={{0,3},{1,2},{2,1},{3,0},{4,7},{5,6},{6,5},{7,4},{8,11},{9,10},{10,... | collective-permute-start | bytes 294920 | tf_op jit(solution)/shard_map/ppermute | solution.py:270
  31.6 4.4 %slice-start = ((s8[12582912]{0:T(1024)(128)(4,1)}), s8[4194304]{0:T(1024)(128)(4,1)S(1)}, s32[]{:S(2)}) async-start(s8[12582912]{0:T(1024)(128)(4,1)} %bitcast.4), calls=%async_computation | async-start | bytes 8388608
  31.6 4.4 %slice-start.1 = ((s8[12582912]{0:T(1024)(128)(4,1)}), s8[4194304]{0:T(1024)(128)(4,1)S(1)}, s32[]{:S(2)}) async-start(s8[12582912]{0:T(1024)(128)(4,1)} %bitcast.4), calls=%async_computation.1 | async-start | bytes 8388608
  33.9 2.7 %slice-start.2 = ((s8[12582912]{0:T(1024)(128)(4,1)}), s8[4194304]{0:T(1024)(128)(4,1)S(1)}, s32[]{:S(2)}) async-start(s8[12582912]{0:T(1024)(128)(4,1)} %bitcast.4), calls=%async_computation.2 | async-start | bytes 8388608
  37.6 1.9 %collective-permute-start.12 = (bf16[64,768]{1,0:T(8,128)(2,1)S(1)}, bf16[64,768]{1,0:T(8,128)(2,1)S(1)}, u32[]{:S(2)}, u32[]{:S(2)}) collective-permute-start(bf16[64,768]{1,0:T(8,128)(2,1)S(1)} %get-tuple-element.76), channel_id=1, source_target_pairs={{0,1},{1,0},{2,3},{3,2},{4,5},{5,4},{6,7},{7,6},{8,9},{9,8},{10,11... | collective-permute-start | bytes 294920 | tf_op jit(solution)/shard_map/ppermute | solution.py:270
  37.6 5.7 %collective-permute-start.13 = (bf16[64,768]{1,0:T(8,128)(2,1)S(1)}, bf16[64,768]{1,0:T(8,128)(2,1)S(1)}, u32[]{:S(2)}, u32[]{:S(2)}) collective-permute-start(bf16[64,768]{1,0:T(8,128)(2,1)S(1)} %get-tuple-element.77), channel_id=1, source_target_pairs={{0,2},{1,3},{2,0},{3,1},{4,6},{5,7},{6,4},{7,5},{8,10},{9,11},{10,... | collective-permute-start | bytes 294920 | tf_op jit(solution)/shard_map/ppermute | solution.py:270
  39.2 5.3 %collective-permute-start.14 = (bf16[64,768]{1,0:T(8,128)(2,1)S(1)}, bf16[64,768]{1,0:T(8,128)(2,1)S(1)}, u32[]{:S(2)}, u32[]{:S(2)}) collective-permute-start(bf16[64,768]{1,0:T(8,128)(2,1)S(1)} %get-tuple-element.78), channel_id=1, source_target_pairs={{0,3},{1,2},{2,1},{3,0},{4,7},{5,6},{6,5},{7,4},{8,11},{9,10},{10,... | collective-permute-start | bytes 294920 | tf_op jit(solution)/shard_map/ppermute | solution.py:270
  44.8 7.1 %collective-permute-start.15 = (bf16[128,768]{1,0:T(8,128)(2,1)S(1)}, bf16[128,768]{1,0:T(8,128)(2,1)S(1)}, u32[]{:S(2)}, u32[]{:S(2)}) collective-permute-start(bf16[128,768]{1,0:T(8,128)(2,1)S(1)} %combine.4), channel_id=1, source_target_pairs={{0,4},{4,0},{8,12},{12,8},{1,5},{5,1},{9,13},{13,9},{2,6},{6,2},{1... | collective-permute-start | bytes 589832 | tf_op jit(solution)/shard_map/ppermute | solution.py:270
  46.3 9.3 %collective-permute-start.23 = (bf16[64,768]{1,0:T(8,128)(2,1)S(1)}, bf16[64,768]{1,0:T(8,128)(2,1)S(1)}, u32[]{:S(2)}, u32[]{:S(2)}) collective-permute-start(bf16[64,768]{1,0:T(8,128)(2,1)S(1)} %get-tuple-element.88), channel_id=1, source_target_pairs={{0,1},{1,0},{2,3},{3,2},{4,5},{5,4},{6,7},{7,6},{8,9},{9,8},{10,11... | collective-permute-start | bytes 294920 | tf_op jit(solution)/shard_map/ppermute | solution.py:270
  46.4 9.6 %collective-permute-start.24 = (bf16[64,768]{1,0:T(8,128)(2,1)S(1)}, bf16[64,768]{1,0:T(8,128)(2,1)S(1)}, u32[]{:S(2)}, u32[]{:S(2)}) collective-permute-start(bf16[64,768]{1,0:T(8,128)(2,1)S(1)} %get-tuple-element.89), channel_id=1, source_target_pairs={{0,2},{1,3},{2,0},{3,1},{4,6},{5,7},{6,4},{7,5},{8,10},{9,11},{10,... | collective-permute-start | bytes 294920 | tf_op jit(solution)/shard_map/ppermute | solution.py:270
  48.1 8.3 %collective-permute-start.25 = (bf16[64,768]{1,0:T(8,128)(2,1)S(1)}, bf16[64,768]{1,0:T(8,128)(2,1)S(1)}, u32[]{:S(2)}, u32[]{:S(2)}) collective-permute-start(bf16[64,768]{1,0:T(8,128)(2,1)S(1)} %get-tuple-element.90), channel_id=1, source_target_pairs={{0,3},{1,2},{2,1},{3,0},{4,7},{5,6},{6,5},{7,4},{8,11},{9,10},{10,... | collective-permute-start | bytes 294920 | tf_op jit(solution)/shard_map/ppermute | solution.py:270
  53.0 7.1 %collective-permute-start.19 = (bf16[64,768]{1,0:T(8,128)(2,1)S(1)}, bf16[64,768]{1,0:T(8,128)(2,1)S(1)}, u32[]{:S(2)}, u32[]{:S(2)}) collective-permute-start(bf16[64,768]{1,0:T(8,128)(2,1)S(1)} %get-tuple-element.84), channel_id=1, source_target_pairs={{0,1},{1,0},{2,3},{3,2},{4,5},{5,4},{6,7},{7,6},{8,9},{9,8},{10,11... | collective-permute-start | bytes 294920 | tf_op jit(solution)/shard_map/ppermute | solution.py:270
  53.1 7.0 %collective-permute-start.20 = (bf16[64,768]{1,0:T(8,128)(2,1)S(1)}, bf16[64,768]{1,0:T(8,128)(2,1)S(1)}, u32[]{:S(2)}, u32[]{:S(2)}) collective-permute-start(bf16[64,768]{1,0:T(8,128)(2,1)S(1)} %get-tuple-element.85), channel_id=1, source_target_pairs={{0,2},{1,3},{2,0},{3,1},{4,6},{5,7},{6,4},{7,5},{8,10},{9,11},{10,... | collective-permute-start | bytes 294920 | tf_op jit(solution)/shard_map/ppermute | solution.py:270
  55.7 4.8 %collective-permute-start.21 = (bf16[64,768]{1,0:T(8,128)(2,1)S(1)}, bf16[64,768]{1,0:T(8,128)(2,1)S(1)}, u32[]{:S(2)}, u32[]{:S(2)}) collective-permute-start(bf16[64,768]{1,0:T(8,128)(2,1)S(1)} %get-tuple-element.86), channel_id=1, source_target_pairs={{0,3},{1,2},{2,1},{3,0},{4,7},{5,6},{6,5},{7,4},{8,11},{9,10},{10,... | collective-permute-start | bytes 294920 | tf_op jit(solution)/shard_map/ppermute | solution.py:270
  56.0 4.5 %collective-permute-start.16 = (bf16[64,768]{1,0:T(8,128)(2,1)S(1)}, bf16[64,768]{1,0:T(8,128)(2,1)S(1)}, u32[]{:S(2)}, u32[]{:S(2)}) collective-permute-start(bf16[64,768]{1,0:T(8,128)(2,1)S(1)} %get-tuple-element.80), channel_id=1, source_target_pairs={{0,1},{1,0},{2,3},{3,2},{4,5},{5,4},{6,7},{7,6},{8,9},{9,8},{10,11... | collective-permute-start | bytes 294920 | tf_op jit(solution)/shard_map/ppermute | solution.py:270
  56.7 12.6 %collective-permute-start.26 = (bf16[128,768]{1,0:T(8,128)(2,1)S(1)}, bf16[128,768]{1,0:T(8,128)(2,1)S(1)}, u32[]{:S(2)}, u32[]{:S(2)}) collective-permute-start(bf16[128,768]{1,0:T(8,128)(2,1)S(1)} %combine.6), channel_id=1, source_target_pairs={{0,8},{4,12},{8,0},{12,4},{1,9},{5,13},{9,1},{13,5},{2,10},{6,14},... | collective-permute-start | bytes 589832 | tf_op jit(solution)/shard_map/ppermute | solution.py:270
  60.8 11.2 %collective-permute-start.22 = (bf16[128,768]{1,0:T(8,128)(2,1)S(1)}, bf16[128,768]{1,0:T(8,128)(2,1)S(1)}, u32[]{:S(2)}, u32[]{:S(2)}) collective-permute-start(bf16[128,768]{1,0:T(8,128)(2,1)S(1)} %combine.5), channel_id=1, source_target_pairs={{0,4},{4,0},{8,12},{12,8},{1,5},{5,1},{9,13},{13,9},{2,6},{6,2},{1... | collective-permute-start | bytes 589832 | tf_op jit(solution)/shard_map/ppermute | solution.py:270
  61.5 5.4 %collective-permute-start.17 = (bf16[64,768]{1,0:T(8,128)(2,1)S(1)}, bf16[64,768]{1,0:T(8,128)(2,1)S(1)}, u32[]{:S(2)}, u32[]{:S(2)}) collective-permute-start(bf16[64,768]{1,0:T(8,128)(2,1)S(1)} %get-tuple-element.81), channel_id=1, source_target_pairs={{0,2},{1,3},{2,0},{3,1},{4,6},{5,7},{6,4},{7,5},{8,10},{9,11},{10,... | collective-permute-start | bytes 294920 | tf_op jit(solution)/shard_map/ppermute | solution.py:270
  62.3 5.1 %collective-permute-start.18 = (bf16[64,768]{1,0:T(8,128)(2,1)S(1)}, bf16[64,768]{1,0:T(8,128)(2,1)S(1)}, u32[]{:S(2)}, u32[]{:S(2)}) collective-permute-start(bf16[64,768]{1,0:T(8,128)(2,1)S(1)} %get-tuple-element.82), channel_id=1, source_target_pairs={{0,3},{1,2},{2,1},{3,0},{4,7},{5,6},{6,5},{7,4},{8,11},{9,10},{10,... | collective-permute-start | bytes 294920 | tf_op jit(solution)/shard_map/ppermute | solution.py:270

commit v11 on v9

--- a/solution.py
+++ b/solution.py
@@ -231,32 +231,41 @@
     )(column.reshape(1), *pinned([hidden, down_w]), *after)
 
 
-def combine_kernel(pick_ref, mix_ref, *refs, experts):
-    y_refs, added, out = refs[:experts], refs[experts:-1], refs[-1]
-    rows = out.shape[0]
+def combine_kernel(pick_ref, mix_ref, *refs, experts, starts):
+    y_refs, added = refs[:experts], refs[experts : experts + len(starts)]
+    outs = refs[experts + len(starts) :]
+    width = y_refs[0].shape[1]
+    rows, part = outs[0].shape
     y = jnp.concatenate([r[...] for r in y_refs], axis=0)
     picked = lax.dot_general(
         pick_ref[...], y, (((0,), (0,)), ((), ())), preferred_element_type=F32
     )
     mixed = picked[:rows] * mix_ref[:, 0:1] + picked[rows:] * mix_ref[:, 1:2]
-    for other in added:
-        mixed = mixed + other[...].astype(F32)
-    out[...] = mixed.astype(BF16)
-
-
-def combine(pick, mix, blocks, added):
+    for other, start in zip(added, starts):
+        value = other[...].astype(F32)
+        stop = start + value.shape[1]
+        pieces = [mixed[:, :start]] * (start > 0) + [mixed[:, start:stop] + value]
+        pieces += [mixed[:, stop:]] * (stop < width)
+        mixed = jnp.concatenate(pieces, axis=1) if len(pieces) > 1 else pieces[0]
+    for i, out in enumerate(outs):
+        out[...] = mixed[:, i * part : (i + 1) * part].astype(BF16)
+
+
+def combine(pick, mix, blocks, added, cuts=1):
     rows = mix.shape[0]
     width = blocks[0].shape[1]
     operands = 2 + len(blocks) + len(added)
     return pl.pallas_call(
-        functools.partial(combine_kernel, experts=len(blocks)),
-        out_shape=jax.ShapeDtypeStruct((rows, width), BF16),
+        functools.partial(
+            combine_kernel, experts=len(blocks), starts=[start for _, start in added]
+        ),
+        out_shape=[jax.ShapeDtypeStruct((rows, width // cuts), BF16)] * cuts,
         in_specs=[pl.BlockSpec(memory_space=pltpu.VMEM)] * operands,
-        out_specs=pl.BlockSpec(memory_space=pltpu.VMEM),
+        out_specs=[pl.BlockSpec(memory_space=pltpu.VMEM)] * cuts,
         cost_estimate=cost(4 * rows * pick.shape[0] * width, 6 * rows * width),
         compiler_params=params(),
         name="combine",
-    )(pick, mix, *blocks, *added)
+    )(pick, mix, *blocks, *[array for array, _ in added])
 
 
 def swap(value, axis, distance):
@@ -310,14 +319,14 @@
         return [swap(block, "expert", e) for e, block in enumerate(terms)]
 
     if not doubling:
-        mixed = combine(pick, mix, returned(everything), [])
+        mixed = combine(pick, mix, returned(everything), [])[0]
         return lax.psum_scatter(mixed, "tensor", scatter_dimension=1, tiled=True)
-    sums, mixtures = [], []
-    for distance in (3, 2, 1):
-        blocks = returned(across(distance), mixtures[-2:-1])
-        mixtures.append(combine(pick, mix, blocks, []))
-        sums.append(swap(mixtures[-1], "tensor", distance))
-    return combine(pick, mix, returned(across(0), sums[:1]), sums[::-1])
+    low, high = combine(pick, mix, returned(across(3)), [], cuts=2)
+    passed = swap(low, "tensor", 1)
+    far = (swap(high, "tensor", 3), width // 2)
+    over = (swap(combine(pick, mix, returned(across(2)), [(passed, 0)])[0], "tensor", 2), 0)
+    beside = (swap(combine(pick, mix, returned(across(1), [low]), [])[0], "tensor", 1), 0)
+    return combine(pick, mix, returned(across(0), [far[0]]), [beside, over, far])[0]
 
 
 def solution(mesh):

time: 69.1 us -> 68.6 us (level)
  the two profiles are of different devices: /device:TPU:0 before, /device:TPU:19 now
where the time goes in v11:
time: 68.6 us; the launch traced here: 68.5 us
  starting transfers between devices  25.4 us (37%)
  Pallas kernels  24.2 us (35%)
  waiting for transfers between devices  17.2 us (25%)
  local copies, waits for them, and re-layouts  1.41 us (2%)
    ppermute x28, starting transfers between devices, swap(): return lax.ppermute(value, axis, [(i, i ^ distance) for i in range(count)])  25.4 us
    ppermute x28, waiting for transfers between devices, swap(): return lax.ppermute(value, axis, [(i, i ^ distance) for i in range(count)])  17.2 us
    pallas_call x2, Pallas kernels, prefetch(): pl.pallas_call(functools.partial(prefetch_kernel, parts=[part for _, part...  9.41 us
    pallas_call x3, Pallas kernels, gate_up(): pl.pallas_call(functools.partial(gate_up_kernel, experts=experts, slices=...  7.71 us
    pallas_call x4, Pallas kernels, down(): pl.pallas_call(functools.partial(down_kernel, part=part, waits=len(after)...  4.1 us
    pallas_call x4, Pallas kernels, combine(): pl.pallas_call(functools.partial(combine_kernel, experts=len(blocks), sta...  1.94 us
    unnamed x12, local copies, waits for them, and re-layouts  1.41 us
  transfers between devices with their start and end apart: 28, of which 11 were waited for; matrix products, arithmetic and copies ran while one was open for 0% of the time, Pallas kernels for 29%

profile of v11, /device:TPU:19, one launch (start us, length us, event | category | flops | bytes accessed | tf_op | source)
XLA Modules:
  0.0 68.5 jit_solution(17987647449514058845)
XLA Ops:
  0.1 1.3 %collective-permute-start.5 = (bf16[128,768]{1,0:T(8,128)(2,1)}, bf16[128,768]{1,0:T(8,128)(2,1)S(1)}, u32[]{:S(2)}, u32[]{:S(2)}) collective-permute-start(bf16[128,768]{1,0:T(8,128)(2,1)} %refs_0_.4), channel_id=1, source_target_pairs={{0,4},{4,0},{8,12},{12,8},{1,5},{5,1},{9,13},{13,9},{2,6},{6,2},{1... | collective-permute-start | bytes 589832 | tf_op jit(solution)/shard_map/ppermute | solution.py:275
  1.4 0.7 copy-done.1
  2.0 0.7 copy-done.2
  2.9 4.7 %prefetch.2 = (bf16[768,2048]{1,0:T(8,128)(2,1)S(1)}, bf16[768,2048]{1,0:T(8,128)(2,1)S(1)}, bf16[768,2048]{1,0:T(8,128)(2,1)S(1)}, bf16[768,2048]{1,0:T(8,128)(2,1)S(1)}) custom-call(s32[1]{0:T(128)} %bitcast.3.column_ref, bf16[256,128]{1,0:T(8,128)(2,1)S(1)} %get-tuple-element.52.placed_ref.after_ref, bf16[1,3072,2048]{2,1,0:T(8,128)(2,1)} %refs_2_.3, ...), custom_call_target="tpu_custom_call" | custom-call | bytes 12582912 | tf_op jit(solution)/shard_map/prefetch/pallas_call | solution.py:127
  7.6 0.5 collective-permute-done.refs_0_
  8.2 5.2 %collective-permute-start.1 = (bf16[128,768]{1,0:T(8,128)(2,1)S(1)}, bf16[128,768]{1,0:T(8,128)(2,1)S(1)}, u32[]{:S(2)}, u32[]{:S(2)}) collective-permute-start(bf16[128,768]{1,0:T(8,128)(2,1)S(1)} %collective-permute-done.refs_0_), channel_id=1, source_target_pairs={{0,4},{4,0},{8,12},{12,8},{1,5},{5,1},{9,13},{13,9},{2,6},{6,2},{1... | collective-permute-start | bytes 589832 | tf_op jit(solution)/shard_map/ppermute | solution.py:275
  13.3 0.4 dispatch.4
  13.7 0.3 collective-permute-start.10
  14.0 2.1 %collective-permute-start.11 = (bf16[64,1536]{1,0:T(8,128)(2,1)S(1)}, bf16[64,1536]{1,0:T(8,128)(2,1)S(1)}, u32[]{:S(2)}, u32[]{:S(2)}) collective-permute-start(bf16[64,1536]{1,0:T(8,128)(2,1)S(1)} %get-tuple-element.69), channel_id=1, source_target_pairs={{0,3},{1,2},{2,1},{3,0},{4,7},{5,6},{6,5},{7,4},{8,11},{9,10},{10,... | collective-permute-start | bytes 589832 | tf_op jit(solution)/shard_map/ppermute | solution.py:275
  16.2 4.7 %prefetch.3 = (bf16[768,2048]{1,0:T(8,128)(2,1)S(1)}, bf16[768,2048]{1,0:T(8,128)(2,1)S(1)}, bf16[768,2048]{1,0:T(8,128)(2,1)S(1)}, bf16[768,2048]{1,0:T(8,128)(2,1)S(1)}) custom-call(s32[1]{0:T(128)} %bitcast.3.column_ref, bf16[64,1536]{1,0:T(8,128)(2,1)S(1)} %get-tuple-element.58.after_ref.refs_0_, bf16[1,3072,2048]{2,1,0:T(8,128)(2,1)} %refs_2_.3, ...), custom_call_target="tpu_custom_call" | custom-call | bytes 12582912 | tf_op jit(solution)/shard_map/prefetch/pallas_call | solution.py:127
  20.9 0.3 dispatch.5
  21.1 0.6 collective-permute-start.6
  21.7 0.3 collective-permute-start.7
  22.0 0.3 dispatch.3
  22.2 0.4 collective-permute-done.6.refs_8_.refs_1_
  22.7 1.1 %collective-permute-start.8 = (bf16[64,768]{1,0:T(8,128)(2,1)S(1)}, bf16[64,768]{1,0:T(8,128)(2,1)S(1)}, u32[]{:S(2)}, u32[]{:S(2)}) collective-permute-start(bf16[64,768]{1,0:T(8,128)(2,1)S(1)} %get-tuple-element.64), channel_id=1, source_target_pairs={{0,3},{1,2},{2,1},{3,0},{4,7},{5,6},{6,5},{7,4},{8,11},{9,10},{10,... | collective-permute-start | bytes 294920 | tf_op jit(solution)/shard_map/ppermute | solution.py:275
  23.9 1.1 %collective-permute-done.11.refs_3_ = bf16[64,1536]{1,0:T(8,128)(2,1)S(1)} collective-permute-done((bf16[64,1536]{1,0:T(8,128)(2,1)S(1)}, bf16[64,1536]{1,0:T(8,128)(2,1)S(1)}, u32[]{:S(2)}, u32[]{:S(2)}) %collective-permute-start.11) | collective-permute-done | bytes 196640 | tf_op jit(solution)/shard_map/ppermute | solution.py:275
  25.0 0.3 collective-permute-start.3
  25.3 0.7 collective-permute-start.4
  25.9 3.5 %gate_up.3 = (f32[256,2048]{1,0:T(8,128)S(1)}, f32[256,2048]{1,0:T(8,128)S(1)}) custom-call(bf16[64,1536]{1,0:T(8,128)(2,1)S(1)} %get-tuple-element.58.after_ref.refs_0_, bf16[64,1536]{1,0:T(8,128)(2,1)S(1)} %collective-permute-done.9.refs_1_, bf16[64,1536]{1,0:T(8,128)(2,1)S(1)} %collective-permute-done.10.refs_2_, ...), custom_call_target="tpu_custom_call" | custom-call | flops 3221225472 | bytes 12582912 | tf_op jit(solution)/shard_map/gate_up/pallas_call | solution.py:183
  29.4 2.1 %gate_up.4 = (f32[256,2048]{1,0:T(8,128)S(1)}, f32[256,2048]{1,0:T(8,128)S(1)}) custom-call(bf16[64,768]{1,0:T(8,128)(2,1)S(1)} %get-tuple-element.61.refs_0_, bf16[64,768]{1,0:T(8,128)(2,1)S(1)} %collective-permute-done.6.refs_8_.refs_1_, bf16[64,768]{1,0:T(8,128)(2,1)S(1)} %collective-permute-done.7.refs_2_, ...), custom_call_target="tpu_custom_call", output_to_operand_aliasing={{0}: (6, {}), {1}: (7, {})} | custom-call | flops 1610612736 | bytes 6291456 | tf_op jit(solution)/shard_map/gate_up/pallas_call | solution.py:183
  31.6 1.4 %collective-permute-done.4.refs_3_ = bf16[64,768]{1,0:T(8,128)(2,1)S(1)} collective-permute-done((bf16[64,768]{1,0:T(8,128)(2,1)S(1)}, bf16[64,768]{1,0:T(8,128)(2,1)S(1)}, u32[]{:S(2)}, u32[]{:S(2)}) %collective-permute-start.4) | collective-permute-done | bytes 98336 | tf_op jit(solution)/shard_map/ppermute | solution.py:275
  33.0 2.1 %gate_up.5.h_ref = bf16[256,2048]{1,0:T(8,128)(2,1)S(1)} custom-call(bf16[64,768]{1,0:T(8,128)(2,1)S(1)} %get-tuple-element.53.refs_0_, bf16[64,768]{1,0:T(8,128)(2,1)S(1)} %collective-permute-done.2.refs_1_, bf16[64,768]{1,0:T(8,128)(2,1)S(1)} %collective-permute-done.3.refs_2_, bf16[64,768]{1,0:T(8,128)(2,1)S(1)} %collective-permute-done.4.refs_3_, ...), custom_call_target="tpu_custom_call" | custom-call | flops 1610612736 | bytes 6291456 | tf_op jit(solution)/shard_map/gate_up/pallas_call | solution.py:183
  35.2 1.0 %down.4 = (bf16[64,768]{1,0:T(8,128)(2,1)S(1)}, bf16[64,768]{1,0:T(8,128)(2,1)S(1)}, bf16[64,768]{1,0:T(8,128)(2,1)S(1)}, bf16[64,768]{1,0:T(8,128)(2,1)S(1)}) custom-call(s32[1]{0:T(128)} %bitcast.3.column_ref, bf16[256,2048]{1,0:T(8,128)(2,1)S(1)} %gate_up.5.h_ref, bf16[1,2048,3072]{2,1,0:T(8,128)(2,1)S(1)} %bitcast.5), custom_call_target="tpu_custom_call" | custom-call | flops 805306368 | bytes 3538944 | tf_op jit(solution)/shard_map/down/pallas_call | solution.py:221
  36.2 0.5 collective-permute-start.12
  36.7 0.3 collective-permute-start.13
  37.0 1.5 %collective-permute-start.14 = (bf16[64,768]{1,0:T(8,128)(2,1)S(1)}, bf16[64,768]{1,0:T(8,128)(2,1)S(1)}, u32[]{:S(2)}, u32[]{:S(2)}) collective-permute-start(bf16[64,768]{1,0:T(8,128)(2,1)S(1)} %get-tuple-element.80), channel_id=1, source_target_pairs={{0,3},{1,2},{2,1},{3,0},{4,7},{5,6},{6,5},{7,4},{8,11},{9,10},{10,... | collective-permute-start | bytes 294920 | tf_op jit(solution)/shard_map/ppermute | solution.py:275
  38.5 1.0 %down.7 = (bf16[64,768]{1,0:T(8,128)(2,1)S(1)}, bf16[64,768]{1,0:T(8,128)(2,1)S(1)}, bf16[64,768]{1,0:T(8,128)(2,1)S(1)}, bf16[64,768]{1,0:T(8,128)(2,1)S(1)}) custom-call(s32[1]{0:T(128)} %bitcast.3.column_ref, bf16[256,2048]{1,0:T(8,128)(2,1)S(1)} %gate_up.5.h_ref, bf16[1,2048,3072]{2,1,0:T(8,128)(2,1)S(1)} %bitcast.5), custom_call_target="tpu_custom_call" | custom-call | flops 805306368 | bytes 3538944 | tf_op jit(solution)/shard_map/down/pallas_call | solution.py:221
  40.0 1.7 %collective-permute-start.25 = (bf16[64,768]{1,0:T(8,128)(2,1)S(1)}, bf16[64,768]{1,0:T(8,128)(2,1)S(1)}, u32[]{:S(2)}, u32[]{:S(2)}) collective-permute-start(bf16[64,768]{1,0:T(8,128)(2,1)S(1)} %get-tuple-element.94), channel_id=1, source_target_pairs={{0,3},{1,2},{2,1},{3,0},{4,7},{5,6},{6,5},{7,4},{8,11},{9,10},{10,... | collective-permute-start | bytes 294920 | tf_op jit(solution)/shard_map/ppermute | solution.py:275
  41.7 2.1 %collective-permute-done.14.refs_3_ = bf16[64,768]{1,0:T(8,128)(2,1)S(1)} collective-permute-done((bf16[64,768]{1,0:T(8,128)(2,1)S(1)}, bf16[64,768]{1,0:T(8,128)(2,1)S(1)}, u32[]{:S(2)}, u32[]{:S(2)}) %collective-permute-start.14) | collective-permute-done | bytes 98336 | tf_op jit(solution)/shard_map/ppermute | solution.py:275
  43.8 0.3 combine.4
  44.3 1.0 %down.6 = (bf16[64,768]{1,0:T(8,128)(2,1)S(1)}, bf16[64,768]{1,0:T(8,128)(2,1)S(1)}, bf16[64,768]{1,0:T(8,128)(2,1)S(1)}, bf16[64,768]{1,0:T(8,128)(2,1)S(1)}) custom-call(s32[1]{0:T(128)} %bitcast.3.column_ref, bf16[256,2048]{1,0:T(8,128)(2,1)S(1)} %gate_up.5.h_ref, bf16[1,2048,3072]{2,1,0:T(8,128)(2,1)S(1)} %bitcast.5, ...), custom_call_target="tpu_custom_call" | custom-call | flops 805306368 | bytes 3538944 | tf_op jit(solution)/shard_map/down/pallas_call | solution.py:221
  45.4 0.4 collective-permute-start.20
  45.8 1.8 %collective-permute-start.21 = (bf16[64,768]{1,0:T(8,128)(2,1)S(1)}, bf16[64,768]{1,0:T(8,128)(2,1)S(1)}, u32[]{:S(2)}, u32[]{:S(2)}) collective-permute-start(bf16[64,768]{1,0:T(8,128)(2,1)S(1)} %get-tuple-element.90), channel_id=1, source_target_pairs={{0,3},{1,2},{2,1},{3,0},{4,7},{5,6},{6,5},{7,4},{8,11},{9,10},{10,... | collective-permute-start | bytes 294920 | tf_op jit(solution)/shard_map/ppermute | solution.py:275
  47.6 0.3 collective-permute-done.25.refs_3_
  47.9 1.0 %collective-permute-done.26.refs_4_ = bf16[128,384]{1,0:T(8,128)(2,1)S(1)} collective-permute-done((bf16[128,384]{1,0:T(8,128)(2,1)S(1)}, bf16[128,384]{1,0:T(8,128)(2,1)S(1)}, u32[]{:S(2)}, u32[]{:S(2)}) %collective-permute-start.26) | collective-permute-done | bytes 98336 | tf_op jit(solution)/shard_map/ppermute | solution.py:275
  48.8 0.3 combine.6
  49.1 2.3 %collective-permute-start.27 = (bf16[128,768]{1,0:T(8,128)(2,1)S(1)}, bf16[128,768]{1,0:T(8,128)(2,1)S(1)}, u32[]{:S(2)}, u32[]{:S(2)}) collective-permute-start(bf16[128,768]{1,0:T(8,128)(2,1)S(1)} %combine.6), channel_id=1, source_target_pairs={{0,8},{4,12},{8,0},{12,4},{1,9},{5,13},{9,1},{13,5},{2,10},{6,14},... | collective-permute-start | bytes 589832 | tf_op jit(solution)/shard_map/ppermute | solution.py:275
  51.4 1.0 %collective-permute-done.21.refs_3_ = bf16[64,768]{1,0:T(8,128)(2,1)S(1)} collective-permute-done((bf16[64,768]{1,0:T(8,128)(2,1)S(1)}, bf16[64,768]{1,0:T(8,128)(2,1)S(1)}, u32[]{:S(2)}, u32[]{:S(2)}) %collective-permute-start.21) | collective-permute-done | bytes 98336 | tf_op jit(solution)/shard_map/ppermute | solution.py:275
  52.4 0.3 combine.5
  52.7 1.5 %collective-permute-start.22 = (bf16[128,768]{1,0:T(8,128)(2,1)S(1)}, bf16[128,768]{1,0:T(8,128)(2,1)S(1)}, u32[]{:S(2)}, u32[]{:S(2)}) collective-permute-start(bf16[128,768]{1,0:T(8,128)(2,1)S(1)} %combine.5), channel_id=1, source_target_pairs={{0,4},{4,0},{8,12},{12,8},{1,5},{5,1},{9,13},{13,9},{2,6},{6,2},{1... | collective-permute-start | bytes 589832 | tf_op jit(solution)/shard_map/ppermute | solution.py:275
  54.2 4.4 %collective-permute-done.15.refs_0_.refs_6_ = bf16[128,384]{1,0:T(8,128)(2,1)S(1)} collective-permute-done((bf16[128,384]{1,0:T(8,128)(2,1)S(1)}, bf16[128,384]{1,0:T(8,128)(2,1)S(1)}, u32[]{:S(2)}, u32[]{:S(2)}) %collective-permute-start.15) | collective-permute-done | bytes 98336 | tf_op jit(solution)/shard_map/ppermute | solution.py:275
  58.6 1.0 %down.5 = (bf16[64,768]{1,0:T(8,128)(2,1)S(1)}, bf16[64,768]{1,0:T(8,128)(2,1)S(1)}, bf16[64,768]{1,0:T(8,128)(2,1)S(1)}, bf16[64,768]{1,0:T(8,128)(2,1)S(1)}) custom-call(s32[1]{0:T(128)} %bitcast.3.column_ref, bf16[256,2048]{1,0:T(8,128)(2,1)S(1)} %gate_up.5.h_ref, bf16[1,2048,3072]{2,1,0:T(8,128)(2,1)S(1)} %bitcast.5, ...), custom_call_target="tpu_custom_call" | custom-call | flops 805306368 | bytes 3538944 | tf_op jit(solution)/shard_map/down/pallas_call | solution.py:221
  59.6 1.2 %collective-permute-start.16 = (bf16[64,768]{1,0:T(8,128)(2,1)S(1)}, bf16[64,768]{1,0:T(8,128)(2,1)S(1)}, u32[]{:S(2)}, u32[]{:S(2)}) collective-permute-start(bf16[64,768]{1,0:T(8,128)(2,1)S(1)} %get-tuple-element.83), channel_id=1, source_target_pairs={{0,1},{1,0},{2,3},{3,2},{4,5},{5,4},{6,7},{7,6},{8,9},{9,8},{10,11... | collective-permute-start | bytes 294920 | tf_op jit(solution)/shard_map/ppermute | solution.py:275
  61.0 1.5 %collective-permute-start.18 = (bf16[64,768]{1,0:T(8,128)(2,1)S(1)}, bf16[64,768]{1,0:T(8,128)(2,1)S(1)}, u32[]{:S(2)}, u32[]{:S(2)}) collective-permute-start(bf16[64,768]{1,0:T(8,128)(2,1)S(1)} %get-tuple-element.85), channel_id=1, source_target_pairs={{0,3},{1,2},{2,1},{3,0},{4,7},{5,6},{6,5},{7,4},{8,11},{9,10},{10,... | collective-permute-start | bytes 294920 | tf_op jit(solution)/shard_map/ppermute | solution.py:275
  62.5 2.7 %collective-permute-done.17.refs_2_ = bf16[64,768]{1,0:T(8,128)(2,1)S(1)} collective-permute-done((bf16[64,768]{1,0:T(8,128)(2,1)S(1)}, bf16[64,768]{1,0:T(8,128)(2,1)S(1)}, u32[]{:S(2)}, u32[]{:S(2)}) %collective-permute-start.17) | collective-permute-done | bytes 98336 | tf_op jit(solution)/shard_map/ppermute | solution.py:275
  65.2 2.3 %collective-permute-done.18.refs_3_ = bf16[64,768]{1,0:T(8,128)(2,1)S(1)} collective-permute-done((bf16[64,768]{1,0:T(8,128)(2,1)S(1)}, bf16[64,768]{1,0:T(8,128)(2,1)S(1)}, u32[]{:S(2)}, u32[]{:S(2)}) %collective-permute-start.18) | collective-permute-done | bytes 98336 | tf_op jit(solution)/shard_map/ppermute | solution.py:275
  67.4 1.0 %combine.7 = bf16[128,768]{1,0:T(8,128)(2,1)} custom-call(bf16[256,256]{1,0:T(8,128)(2,1)S(1)} %get-tuple-element.50.pick_ref, f32[128,2]{1,0:T(8,128)S(1)} %get-tuple-element.51.mix_ref, bf16[64,768]{1,0:T(8,128)(2,1)S(1)} %get-tuple-element.82.refs_0_, bf16[64,768]{1,0:T(8,128)(2,1)S(1)} %collective-permute-done.16.refs_1_, ...), custom_call_target="tpu_custom_call" | custom-call | flops 100663296 | bytes 589824 | tf_op jit(solution)/shard_map/combine/pallas_call | solution.py:258
  (38 shorter events, 1.4 us)
Async XLA Ops:
  0.0 8.2 %collective-permute-start = (bf16[128,768]{1,0:T(8,128)(2,1)}, bf16[128,768]{1,0:T(8,128)(2,1)S(1)}, u32[]{:S(2)}, u32[]{:S(2)}) collective-permute-start(bf16[128,768]{1,0:T(8,128)(2,1)} %refs_0_.4), channel_id=1, source_target_pairs={{0,8},{4,12},{8,0},{12,4},{1,9},{5,13},{9,1},{13,5},{2,10},{6,14},... | collective-permute-start | bytes 589832 | tf_op jit(solution)/shard_map/ppermute | solution.py:275
  0.1 13.3 %collective-permute-start.5 = (bf16[128,768]{1,0:T(8,128)(2,1)}, bf16[128,768]{1,0:T(8,128)(2,1)S(1)}, u32[]{:S(2)}, u32[]{:S(2)}) collective-permute-start(bf16[128,768]{1,0:T(8,128)(2,1)} %refs_0_.4), channel_id=1, source_target_pairs={{0,4},{4,0},{8,12},{12,8},{1,5},{5,1},{9,13},{13,9},{2,6},{6,2},{1... | collective-permute-start | bytes 589832 | tf_op jit(solution)/shard_map/ppermute | solution.py:275
  1.4 0.7 copy-start.1
  2.0 0.7 copy-start.2
  2.9 10.4 %copy-start = (bf16[128,768]{1,0:T(8,128)(2,1)S(1)}, bf16[128,768]{1,0:T(8,128)(2,1)}, u32[]{:S(2)}) copy-start(bf16[128,768]{1,0:T(8,128)(2,1)} %refs_0_.4) | copy-start | bytes 589828
  8.2 13.5 %collective-permute-start.1 = (bf16[128,768]{1,0:T(8,128)(2,1)S(1)}, bf16[128,768]{1,0:T(8,128)(2,1)S(1)}, u32[]{:S(2)}, u32[]{:S(2)}) collective-permute-start(bf16[128,768]{1,0:T(8,128)(2,1)S(1)} %collective-permute-done.refs_0_), channel_id=1, source_target_pairs={{0,4},{4,0},{8,12},{12,8},{1,5},{5,1},{9,13},{13,9},{2,6},{6,2},{1... | collective-permute-start | bytes 589832 | tf_op jit(solution)/shard_map/ppermute | solution.py:275
  13.7 10.1 %collective-permute-start.10 = (bf16[64,1536]{1,0:T(8,128)(2,1)S(1)}, bf16[64,1536]{1,0:T(8,128)(2,1)S(1)}, u32[]{:S(2)}, u32[]{:S(2)}) collective-permute-start(bf16[64,1536]{1,0:T(8,128)(2,1)S(1)} %get-tuple-element.68), channel_id=1, source_target_pairs={{0,2},{1,3},{2,0},{3,1},{4,6},{5,7},{6,4},{7,5},{8,10},{9,11},{10,... | collective-permute-start | bytes 589832 | tf_op jit(solution)/shard_map/ppermute | solution.py:275
  14.0 11.0 %collective-permute-start.11 = (bf16[64,1536]{1,0:T(8,128)(2,1)S(1)}, bf16[64,1536]{1,0:T(8,128)(2,1)S(1)}, u32[]{:S(2)}, u32[]{:S(2)}) collective-permute-start(bf16[64,1536]{1,0:T(8,128)(2,1)S(1)} %get-tuple-element.69), channel_id=1, source_target_pairs={{0,3},{1,2},{2,1},{3,0},{4,7},{5,6},{6,5},{7,4},{8,11},{9,10},{10,... | collective-permute-start | bytes 589832 | tf_op jit(solution)/shard_map/ppermute | solution.py:275
  16.2 9.1 %collective-permute-start.9 = (bf16[64,1536]{1,0:T(8,128)(2,1)S(1)}, bf16[64,1536]{1,0:T(8,128)(2,1)S(1)}, u32[]{:S(2)}, u32[]{:S(2)}) collective-permute-start(bf16[64,1536]{1,0:T(8,128)(2,1)S(1)} %get-tuple-element.67), channel_id=1, source_target_pairs={{0,1},{1,0},{2,3},{3,2},{4,5},{5,4},{6,7},{7,6},{8,9},{9,8},{10,11... | collective-permute-start | bytes 589832 | tf_op jit(solution)/shard_map/ppermute | solution.py:275
  21.1 1.5 %collective-permute-start.6 = (bf16[64,768]{1,0:T(8,128)(2,1)S(1)}, bf16[64,768]{1,0:T(8,128)(2,1)S(1)}, u32[]{:S(2)}, u32[]{:S(2)}) collective-permute-start(bf16[64,768]{1,0:T(8,128)(2,1)S(1)} %get-tuple-element.62), channel_id=1, source_target_pairs={{0,1},{1,0},{2,3},{3,2},{4,5},{5,4},{6,7},{7,6},{8,9},{9,8},{10,11... | collective-permute-start | bytes 294920 | tf_op jit(solution)/shard_map/ppermute | solution.py:275
  21.7 7.7 %collective-permute-start.7 = (bf16[64,768]{1,0:T(8,128)(2,1)S(1)}, bf16[64,768]{1,0:T(8,128)(2,1)S(1)}, u32[]{:S(2)}, u32[]{:S(2)}) collective-permute-start(bf16[64,768]{1,0:T(8,128)(2,1)S(1)} %get-tuple-element.63), channel_id=1, source_target_pairs={{0,2},{1,3},{2,0},{3,1},{4,6},{5,7},{6,4},{7,5},{8,10},{9,11},{10,... | collective-permute-start | bytes 294920 | tf_op jit(solution)/shard_map/ppermute | solution.py:275
  22.7 6.8 %collective-permute-start.8 = (bf16[64,768]{1,0:T(8,128)(2,1)S(1)}, bf16[64,768]{1,0:T(8,128)(2,1)S(1)}, u32[]{:S(2)}, u32[]{:S(2)}) collective-permute-start(bf16[64,768]{1,0:T(8,128)(2,1)S(1)} %get-tuple-element.64), channel_id=1, source_target_pairs={{0,3},{1,2},{2,1},{3,0},{4,7},{5,6},{6,5},{7,4},{8,11},{9,10},{10,... | collective-permute-start | bytes 294920 | tf_op jit(solution)/shard_map/ppermute | solution.py:275
  23.8 7.8 %collective-permute-start.2 = (bf16[64,768]{1,0:T(8,128)(2,1)S(1)}, bf16[64,768]{1,0:T(8,128)(2,1)S(1)}, u32[]{:S(2)}, u32[]{:S(2)}) collective-permute-start(bf16[64,768]{1,0:T(8,128)(2,1)S(1)} %get-tuple-element.54), channel_id=1, source_target_pairs={{0,1},{1,0},{2,3},{3,2},{4,5},{5,4},{6,7},{7,6},{8,9},{9,8},{10,11... | collective-permute-start | bytes 294920 | tf_op jit(solution)/shard_map/ppermute | solution.py:275
  25.0 6.6 %collective-permute-start.3 = (bf16[64,768]{1,0:T(8,128)(2,1)S(1)}, bf16[64,768]{1,0:T(8,128)(2,1)S(1)}, u32[]{:S(2)}, u32[]{:S(2)}) collective-permute-start(bf16[64,768]{1,0:T(8,128)(2,1)S(1)} %get-tuple-element.55), channel_id=1, source_target_pairs={{0,2},{1,3},{2,0},{3,1},{4,6},{5,7},{6,4},{7,5},{8,10},{9,11},{10,... | collective-permute-start | bytes 294920 | tf_op jit(solution)/shard_map/ppermute | solution.py:275
  25.3 7.8 %collective-permute-start.4 = (bf16[64,768]{1,0:T(8,128)(2,1)S(1)}, bf16[64,768]{1,0:T(8,128)(2,1)S(1)}, u32[]{:S(2)}, u32[]{:S(2)}) collective-permute-start(bf16[64,768]{1,0:T(8,128)(2,1)S(1)} %get-tuple-element.56), channel_id=1, source_target_pairs={{0,3},{1,2},{2,1},{3,0},{4,7},{5,6},{6,5},{7,4},{8,11},{9,10},{10,... | collective-permute-start | bytes 294920 | tf_op jit(solution)/shard_map/ppermute | solution.py:275
  29.4 5.8 %slice-start = ((s8[12582912]{0:T(1024)(128)(4,1)}), s8[4194304]{0:T(1024)(128)(4,1)S(1)}, s32[]{:S(2)}) async-start(s8[12582912]{0:T(1024)(128)(4,1)} %bitcast.4), calls=%async_computation | async-start | bytes 8388608
  29.4 5.8 %slice-start.1 = ((s8[12582912]{0:T(1024)(128)(4,1)}), s8[4194304]{0:T(1024)(128)(4,1)S(1)}, s32[]{:S(2)}) async-start(s8[12582912]{0:T(1024)(128)(4,1)} %bitcast.4), calls=%async_computation.1 | async-start | bytes 8388608
  33.0 2.2 %slice-start.2 = ((s8[12582912]{0:T(1024)(128)(4,1)}), s8[4194304]{0:T(1024)(128)(4,1)S(1)}, s32[]{:S(2)}) async-start(s8[12582912]{0:T(1024)(128)(4,1)} %bitcast.4), calls=%async_computation.2 | async-start | bytes 8388608
  36.2 3.7 %collective-permute-start.12 = (bf16[64,768]{1,0:T(8,128)(2,1)S(1)}, bf16[64,768]{1,0:T(8,128)(2,1)S(1)}, u32[]{:S(2)}, u32[]{:S(2)}) collective-permute-start(bf16[64,768]{1,0:T(8,128)(2,1)S(1)} %get-tuple-element.78), channel_id=1, source_target_pairs={{0,1},{1,0},{2,3},{3,2},{4,5},{5,4},{6,7},{7,6},{8,9},{9,8},{10,11... | collective-permute-start | bytes 294920 | tf_op jit(solution)/shard_map/ppermute | solution.py:275
  36.7 5.0 %collective-permute-start.13 = (bf16[64,768]{1,0:T(8,128)(2,1)S(1)}, bf16[64,768]{1,0:T(8,128)(2,1)S(1)}, u32[]{:S(2)}, u32[]{:S(2)}) collective-permute-start(bf16[64,768]{1,0:T(8,128)(2,1)S(1)} %get-tuple-element.79), channel_id=1, source_target_pairs={{0,2},{1,3},{2,0},{3,1},{4,6},{5,7},{6,4},{7,5},{8,10},{9,11},{10,... | collective-permute-start | bytes 294920 | tf_op jit(solution)/shard_map/ppermute | solution.py:275
  37.0 6.9 %collective-permute-start.14 = (bf16[64,768]{1,0:T(8,128)(2,1)S(1)}, bf16[64,768]{1,0:T(8,128)(2,1)S(1)}, u32[]{:S(2)}, u32[]{:S(2)}) collective-permute-start(bf16[64,768]{1,0:T(8,128)(2,1)S(1)} %get-tuple-element.80), channel_id=1, source_target_pairs={{0,3},{1,2},{2,1},{3,0},{4,7},{5,6},{6,5},{7,4},{8,11},{9,10},{10,... | collective-permute-start | bytes 294920 | tf_op jit(solution)/shard_map/ppermute | solution.py:275
  39.5 5.9 %collective-permute-start.23 = (bf16[64,768]{1,0:T(8,128)(2,1)S(1)}, bf16[64,768]{1,0:T(8,128)(2,1)S(1)}, u32[]{:S(2)}, u32[]{:S(2)}) collective-permute-start(bf16[64,768]{1,0:T(8,128)(2,1)S(1)} %get-tuple-element.92), channel_id=1, source_target_pairs={{0,1},{1,0},{2,3},{3,2},{4,5},{5,4},{6,7},{7,6},{8,9},{9,8},{10,11... | collective-permute-start | bytes 294920 | tf_op jit(solution)/shard_map/ppermute | solution.py:275
  39.7 6.0 %collective-permute-start.24 = (bf16[64,768]{1,0:T(8,128)(2,1)S(1)}, bf16[64,768]{1,0:T(8,128)(2,1)S(1)}, u32[]{:S(2)}, u32[]{:S(2)}) collective-permute-start(bf16[64,768]{1,0:T(8,128)(2,1)S(1)} %get-tuple-element.93), channel_id=1, source_target_pairs={{0,2},{1,3},{2,0},{3,1},{4,6},{5,7},{6,4},{7,5},{8,10},{9,11},{10,... | collective-permute-start | bytes 294920 | tf_op jit(solution)/shard_map/ppermute | solution.py:275
  40.0 7.9 %collective-permute-start.25 = (bf16[64,768]{1,0:T(8,128)(2,1)S(1)}, bf16[64,768]{1,0:T(8,128)(2,1)S(1)}, u32[]{:S(2)}, u32[]{:S(2)}) collective-permute-start(bf16[64,768]{1,0:T(8,128)(2,1)S(1)} %get-tuple-element.94), channel_id=1, source_target_pairs={{0,3},{1,2},{2,1},{3,0},{4,7},{5,6},{6,5},{7,4},{8,11},{9,10},{10,... | collective-permute-start | bytes 294920 | tf_op jit(solution)/shard_map/ppermute | solution.py:275
  44.2 4.7 %collective-permute-start.26 = (bf16[128,384]{1,0:T(8,128)(2,1)S(1)}, bf16[128,384]{1,0:T(8,128)(2,1)S(1)}, u32[]{:S(2)}, u32[]{:S(2)}) collective-permute-start(bf16[128,384]{1,0:T(8,128)(2,1)S(1)} %get-tuple-element.86.refs_0_), channel_id=1, source_target_pairs={{0,4},{4,0},{8,12},{12,8},{1,5},{5,1},{9,13},{13,9},{2,6},{6,2},{1... | collective-permute-start | bytes 294920 | tf_op jit(solution)/shard_map/ppermute | solution.py:275
  45.3 6.1 %collective-permute-start.19 = (bf16[64,768]{1,0:T(8,128)(2,1)S(1)}, bf16[64,768]{1,0:T(8,128)(2,1)S(1)}, u32[]{:S(2)}, u32[]{:S(2)}) collective-permute-start(bf16[64,768]{1,0:T(8,128)(2,1)S(1)} %get-tuple-element.88), channel_id=1, source_target_pairs={{0,1},{1,0},{2,3},{3,2},{4,5},{5,4},{6,7},{7,6},{8,9},{9,8},{10,11... | collective-permute-start | bytes 294920 | tf_op jit(solution)/shard_map/ppermute | solution.py:275
  45.4 6.0 %collective-permute-start.20 = (bf16[64,768]{1,0:T(8,128)(2,1)S(1)}, bf16[64,768]{1,0:T(8,128)(2,1)S(1)}, u32[]{:S(2)}, u32[]{:S(2)}) collective-permute-start(bf16[64,768]{1,0:T(8,128)(2,1)S(1)} %get-tuple-element.89), channel_id=1, source_target_pairs={{0,2},{1,3},{2,0},{3,1},{4,6},{5,7},{6,4},{7,5},{8,10},{9,11},{10,... | collective-permute-start | bytes 294920 | tf_op jit(solution)/shard_map/ppermute | solution.py:275
  45.8 6.6 %collective-permute-start.21 = (bf16[64,768]{1,0:T(8,128)(2,1)S(1)}, bf16[64,768]{1,0:T(8,128)(2,1)S(1)}, u32[]{:S(2)}, u32[]{:S(2)}) collective-permute-start(bf16[64,768]{1,0:T(8,128)(2,1)S(1)} %get-tuple-element.90), channel_id=1, source_target_pairs={{0,3},{1,2},{2,1},{3,0},{4,7},{5,6},{6,5},{7,4},{8,11},{9,10},{10,... | collective-permute-start | bytes 294920 | tf_op jit(solution)/shard_map/ppermute | solution.py:275
  47.9 10.7 %collective-permute-start.15 = (bf16[128,384]{1,0:T(8,128)(2,1)S(1)}, bf16[128,384]{1,0:T(8,128)(2,1)S(1)}, u32[]{:S(2)}, u32[]{:S(2)}) collective-permute-start(bf16[128,384]{1,0:T(8,128)(2,1)S(1)} %get-tuple-element.81), channel_id=1, source_target_pairs={{0,12},{4,8},{8,4},{12,0},{1,13},{5,9},{9,5},{13,1},{2,14},{6,10},... | collective-permute-start | bytes 294920 | tf_op jit(solution)/shard_map/ppermute | solution.py:275
  49.1 18.3 %collective-permute-start.27 = (bf16[128,768]{1,0:T(8,128)(2,1)S(1)}, bf16[128,768]{1,0:T(8,128)(2,1)S(1)}, u32[]{:S(2)}, u32[]{:S(2)}) collective-permute-start(bf16[128,768]{1,0:T(8,128)(2,1)S(1)} %combine.6), channel_id=1, source_target_pairs={{0,8},{4,12},{8,0},{12,4},{1,9},{5,13},{9,1},{13,5},{2,10},{6,14},... | collective-permute-start | bytes 589832 | tf_op jit(solution)/shard_map/ppermute | solution.py:275
  52.7 14.7 %collective-permute-start.22 = (bf16[128,768]{1,0:T(8,128)(2,1)S(1)}, bf16[128,768]{1,0:T(8,128)(2,1)S(1)}, u32[]{:S(2)}, u32[]{:S(2)}) collective-permute-start(bf16[128,768]{1,0:T(8,128)(2,1)S(1)} %combine.5), channel_id=1, source_target_pairs={{0,4},{4,0},{8,12},{12,8},{1,5},{5,1},{9,13},{13,9},{2,6},{6,2},{1... | collective-permute-start | bytes 589832 | tf_op jit(solution)/shard_map/ppermute | solution.py:275
  59.6 2.9 %collective-permute-start.16 = (bf16[64,768]{1,0:T(8,128)(2,1)S(1)}, bf16[64,768]{1,0:T(8,128)(2,1)S(1)}, u32[]{:S(2)}, u32[]{:S(2)}) collective-permute-start(bf16[64,768]{1,0:T(8,128)(2,1)S(1)} %get-tuple-element.83), channel_id=1, source_target_pairs={{0,1},{1,0},{2,3},{3,2},{4,5},{5,4},{6,7},{7,6},{8,9},{9,8},{10,11... | collective-permute-start | bytes 294920 | tf_op jit(solution)/shard_map/ppermute | solution.py:275
  60.8 4.4 %collective-permute-start.17 = (bf16[64,768]{1,0:T(8,128)(2,1)S(1)}, bf16[64,768]{1,0:T(8,128)(2,1)S(1)}, u32[]{:S(2)}, u32[]{:S(2)}) collective-permute-start(bf16[64,768]{1,0:T(8,128)(2,1)S(1)} %get-tuple-element.84), channel_id=1, source_target_pairs={{0,2},{1,3},{2,0},{3,1},{4,6},{5,7},{6,4},{7,5},{8,10},{9,11},{10,... | collective-permute-start | bytes 294920 | tf_op jit(solution)/shard_map/ppermute | solution.py:275
  61.0 6.4 %collective-permute-start.18 = (bf16[64,768]{1,0:T(8,128)(2,1)S(1)}, bf16[64,768]{1,0:T(8,128)(2,1)S(1)}, u32[]{:S(2)}, u32[]{:S(2)}) collective-permute-start(bf16[64,768]{1,0:T(8,128)(2,1)S(1)} %get-tuple-element.85), channel_id=1, source_target_pairs={{0,3},{1,2},{2,1},{3,0},{4,7},{5,6},{6,5},{7,4},{8,11},{9,10},{10,... | collective-permute-start | bytes 294920 | tf_op jit(solution)/shard_map/ppermute | solution.py:275

commit v12 on v11

--- a/solution.py
+++ b/solution.py
@@ -324,9 +324,11 @@
     low, high = combine(pick, mix, returned(across(3)), [], cuts=2)
     passed = swap(low, "tensor", 1)
     far = (swap(high, "tensor", 3), width // 2)
-    over = (swap(combine(pick, mix, returned(across(2)), [(passed, 0)])[0], "tensor", 2), 0)
-    beside = (swap(combine(pick, mix, returned(across(1), [low]), [])[0], "tensor", 1), 0)
-    return combine(pick, mix, returned(across(0), [far[0]]), [beside, over, far])[0]
+    onwards = combine(pick, mix, returned(across(2)), [(passed, 0)])[0]
+    over = (swap(onwards, "tensor", 2), 0)
+    near = combine(pick, mix, returned(across(1), [low]), [])[0]
+    beside = (swap(near, "tensor", 1), 0)
+    return combine(pick, mix, returned(across(0), [passed]), [beside, over, far])[0]
 
 
 def solution(mesh):

time: 68.6 us -> 66.4 us (0.968)
  the two profiles are of different devices: /device:TPU:19 before, /device:TPU:0 now
where the time goes in v12:
time: 66.4 us; the launch traced here: 66.3 us
  starting transfers between devices  28.2 us (42%)
  Pallas kernels  24.2 us (36%)
  waiting for transfers between devices  12.1 us (18%)
  local copies, waits for them, and re-layouts  1.54 us (2%)
    ppermute x28, starting transfers between devices, swap(): return lax.ppermute(value, axis, [(i, i ^ distance) for i in range(count)])  28.2 us
    ppermute x28, waiting for transfers between devices, swap(): return lax.ppermute(value, axis, [(i, i ^ distance) for i in range(count)])  12.1 us
    pallas_call x2, Pallas kernels, prefetch(): pl.pallas_call(functools.partial(prefetch_kernel, parts=[part for _, part...  9.41 us
    pallas_call x3, Pallas kernels, gate_up(): pl.pallas_call(functools.partial(gate_up_kernel, experts=experts, slices=...  7.71 us
    pallas_call x4, Pallas kernels, down(): pl.pallas_call(functools.partial(down_kernel, part=part, waits=len(after)...  4.1 us
    pallas_call x4, Pallas kernels, combine(): pl.pallas_call(functools.partial(combine_kernel, experts=len(blocks), sta...  1.94 us
    unnamed x12, local copies, waits for them, and re-layouts  1.54 us
  transfers between devices with their start and end apart: 28, of which 8 were waited for; matrix products, arithmetic and copies ran while one was open for 0% of the time, Pallas kernels for 30%

profile of v12, /device:TPU:0, one launch (start us, length us, event | category | flops | bytes accessed | tf_op | source)
XLA Modules:
  0.0 66.3 jit_solution(7385285167904701995)
XLA Ops:
  0.0 4.0 %collective-permute-start = (bf16[128,768]{1,0:T(8,128)(2,1)}, bf16[128,768]{1,0:T(8,128)(2,1)S(1)}, u32[]{:S(2)}, u32[]{:S(2)}) collective-permute-start(bf16[128,768]{1,0:T(8,128)(2,1)} %refs_0_.4), channel_id=1, source_target_pairs={{0,8},{4,12},{8,0},{12,4},{1,9},{5,13},{9,1},{13,5},{2,10},{6,14},... | collective-permute-start | bytes 589832 | tf_op jit(solution)/shard_map/ppermute | solution.py:275
  4.0 1.6 %collective-permute-start.5 = (bf16[128,768]{1,0:T(8,128)(2,1)}, bf16[128,768]{1,0:T(8,128)(2,1)S(1)}, u32[]{:S(2)}, u32[]{:S(2)}) collective-permute-start(bf16[128,768]{1,0:T(8,128)(2,1)} %refs_0_.4), channel_id=1, source_target_pairs={{0,4},{4,0},{8,12},{12,8},{1,5},{5,1},{9,13},{13,9},{2,6},{6,2},{1... | collective-permute-start | bytes 589832 | tf_op jit(solution)/shard_map/ppermute | solution.py:275
  5.6 0.7 %copy-done.1 = s32[128,2]{0,1:T(2,128)S(1)} copy-done((s32[128,2]{0,1:T(2,128)S(1)}, s32[128,2]{0,1:T(2,128)}, u32[]{:S(2)}) %copy-start.1) | copy-done | bytes 1048
  6.3 0.7 %copy-done.2 = f32[128,2]{0,1:T(2,128)S(1)} copy-done((f32[128,2]{0,1:T(2,128)S(1)}, f32[128,2]{0,1:T(2,128)}, u32[]{:S(2)}) %copy-start.2) | copy-done | bytes 1048
  7.2 4.7 %prefetch.2 = (bf16[768,2048]{1,0:T(8,128)(2,1)S(1)}, bf16[768,2048]{1,0:T(8,128)(2,1)S(1)}, bf16[768,2048]{1,0:T(8,128)(2,1)S(1)}, bf16[768,2048]{1,0:T(8,128)(2,1)S(1)}) custom-call(s32[1]{0:T(128)} %bitcast.3.column_ref, bf16[256,128]{1,0:T(8,128)(2,1)S(1)} %get-tuple-element.52.placed_ref.after_ref, bf16[1,3072,2048]{2,1,0:T(8,128)(2,1)} %refs_2_.3, ...), custom_call_target="tpu_custom_call" | custom-call | bytes 12582912 | tf_op jit(solution)/shard_map/prefetch/pallas_call | solution.py:127
  11.9 1.6 %collective-permute-done.refs_0_ = bf16[128,768]{1,0:T(8,128)(2,1)S(1)} collective-permute-done((bf16[128,768]{1,0:T(8,128)(2,1)}, bf16[128,768]{1,0:T(8,128)(2,1)S(1)}, u32[]{:S(2)}, u32[]{:S(2)}) %collective-permute-start) | collective-permute-done | bytes 196640 | tf_op jit(solution)/shard_map/ppermute | solution.py:275
  13.5 0.7 %collective-permute-start.1 = (bf16[128,768]{1,0:T(8,128)(2,1)S(1)}, bf16[128,768]{1,0:T(8,128)(2,1)S(1)}, u32[]{:S(2)}, u32[]{:S(2)}) collective-permute-start(bf16[128,768]{1,0:T(8,128)(2,1)S(1)} %collective-permute-done.refs_0_), channel_id=1, source_target_pairs={{0,4},{4,0},{8,12},{12,8},{1,5},{5,1},{9,13},{13,9},{2,6},{6,2},{1... | collective-permute-start | bytes 589832 | tf_op jit(solution)/shard_map/ppermute | solution.py:275
  14.2 0.4 dispatch.4
  14.6 1.6 %collective-permute-start.10 = (bf16[64,1536]{1,0:T(8,128)(2,1)S(1)}, bf16[64,1536]{1,0:T(8,128)(2,1)S(1)}, u32[]{:S(2)}, u32[]{:S(2)}) collective-permute-start(bf16[64,1536]{1,0:T(8,128)(2,1)S(1)} %get-tuple-element.68), channel_id=1, source_target_pairs={{0,2},{1,3},{2,0},{3,1},{4,6},{5,7},{6,4},{7,5},{8,10},{9,11},{10,... | collective-permute-start | bytes 589832 | tf_op jit(solution)/shard_map/ppermute | solution.py:275
  16.1 0.6 collective-permute-start.9
  16.8 4.7 %prefetch.3 = (bf16[768,2048]{1,0:T(8,128)(2,1)S(1)}, bf16[768,2048]{1,0:T(8,128)(2,1)S(1)}, bf16[768,2048]{1,0:T(8,128)(2,1)S(1)}, bf16[768,2048]{1,0:T(8,128)(2,1)S(1)}) custom-call(s32[1]{0:T(128)} %bitcast.3.column_ref, bf16[64,1536]{1,0:T(8,128)(2,1)S(1)} %get-tuple-element.58.after_ref.refs_0_, bf16[1,3072,2048]{2,1,0:T(8,128)(2,1)} %refs_2_.3, ...), custom_call_target="tpu_custom_call" | custom-call | bytes 12582912 | tf_op jit(solution)/shard_map/prefetch/pallas_call | solution.py:127
  21.5 0.3 dispatch.5
  21.8 1.6 %collective-permute-start.7 = (bf16[64,768]{1,0:T(8,128)(2,1)S(1)}, bf16[64,768]{1,0:T(8,128)(2,1)S(1)}, u32[]{:S(2)}, u32[]{:S(2)}) collective-permute-start(bf16[64,768]{1,0:T(8,128)(2,1)S(1)} %get-tuple-element.63), channel_id=1, source_target_pairs={{0,2},{1,3},{2,0},{3,1},{4,6},{5,7},{6,4},{7,5},{8,10},{9,11},{10,... | collective-permute-start | bytes 294920 | tf_op jit(solution)/shard_map/ppermute | solution.py:275
  23.4 0.3 dispatch.3
  23.7 0.7 %collective-permute-start.8 = (bf16[64,768]{1,0:T(8,128)(2,1)S(1)}, bf16[64,768]{1,0:T(8,128)(2,1)S(1)}, u32[]{:S(2)}, u32[]{:S(2)}) collective-permute-start(bf16[64,768]{1,0:T(8,128)(2,1)S(1)} %get-tuple-element.64), channel_id=1, source_target_pairs={{0,3},{1,2},{2,1},{3,0},{4,7},{5,6},{6,5},{7,4},{8,11},{9,10},{10,... | collective-permute-start | bytes 294920 | tf_op jit(solution)/shard_map/ppermute | solution.py:275
  24.4 0.4 collective-permute-start.2
  24.8 1.1 %collective-permute-start.3 = (bf16[64,768]{1,0:T(8,128)(2,1)S(1)}, bf16[64,768]{1,0:T(8,128)(2,1)S(1)}, u32[]{:S(2)}, u32[]{:S(2)}) collective-permute-start(bf16[64,768]{1,0:T(8,128)(2,1)S(1)} %get-tuple-element.55), channel_id=1, source_target_pairs={{0,2},{1,3},{2,0},{3,1},{4,6},{5,7},{6,4},{7,5},{8,10},{9,11},{10,... | collective-permute-start | bytes 294920 | tf_op jit(solution)/shard_map/ppermute | solution.py:275
  25.9 1.1 %collective-permute-start.4 = (bf16[64,768]{1,0:T(8,128)(2,1)S(1)}, bf16[64,768]{1,0:T(8,128)(2,1)S(1)}, u32[]{:S(2)}, u32[]{:S(2)}) collective-permute-start(bf16[64,768]{1,0:T(8,128)(2,1)S(1)} %get-tuple-element.56), channel_id=1, source_target_pairs={{0,3},{1,2},{2,1},{3,0},{4,7},{5,6},{6,5},{7,4},{8,11},{9,10},{10,... | collective-permute-start | bytes 294920 | tf_op jit(solution)/shard_map/ppermute | solution.py:275
  27.0 3.5 %gate_up.3 = (f32[256,2048]{1,0:T(8,128)S(1)}, f32[256,2048]{1,0:T(8,128)S(1)}) custom-call(bf16[64,1536]{1,0:T(8,128)(2,1)S(1)} %get-tuple-element.58.after_ref.refs_0_, bf16[64,1536]{1,0:T(8,128)(2,1)S(1)} %collective-permute-done.9.refs_1_, bf16[64,1536]{1,0:T(8,128)(2,1)S(1)} %collective-permute-done.10.refs_2_, ...), custom_call_target="tpu_custom_call" | custom-call | flops 3221225472 | bytes 12582912 | tf_op jit(solution)/shard_map/gate_up/pallas_call | solution.py:183
  30.5 2.1 %gate_up.4 = (f32[256,2048]{1,0:T(8,128)S(1)}, f32[256,2048]{1,0:T(8,128)S(1)}) custom-call(bf16[64,768]{1,0:T(8,128)(2,1)S(1)} %get-tuple-element.61.refs_0_, bf16[64,768]{1,0:T(8,128)(2,1)S(1)} %collective-permute-done.6.refs_8_.refs_1_, bf16[64,768]{1,0:T(8,128)(2,1)S(1)} %collective-permute-done.7.refs_2_, ...), custom_call_target="tpu_custom_call", output_to_operand_aliasing={{0}: (6, {}), {1}: (7, {})} | custom-call | flops 1610612736 | bytes 6291456 | tf_op jit(solution)/shard_map/gate_up/pallas_call | solution.py:183
  32.6 0.8 %collective-permute-done.4.refs_3_ = bf16[64,768]{1,0:T(8,128)(2,1)S(1)} collective-permute-done((bf16[64,768]{1,0:T(8,128)(2,1)S(1)}, bf16[64,768]{1,0:T(8,128)(2,1)S(1)}, u32[]{:S(2)}, u32[]{:S(2)}) %collective-permute-start.4) | collective-permute-done | bytes 98336 | tf_op jit(solution)/shard_map/ppermute | solution.py:275
  33.4 2.1 %gate_up.5.h_ref = bf16[256,2048]{1,0:T(8,128)(2,1)S(1)} custom-call(bf16[64,768]{1,0:T(8,128)(2,1)S(1)} %get-tuple-element.53.refs_0_, bf16[64,768]{1,0:T(8,128)(2,1)S(1)} %collective-permute-done.2.refs_1_, bf16[64,768]{1,0:T(8,128)(2,1)S(1)} %collective-permute-done.3.refs_2_, bf16[64,768]{1,0:T(8,128)(2,1)S(1)} %collective-permute-done.4.refs_3_, ...), custom_call_target="tpu_custom_call" | custom-call | flops 1610612736 | bytes 6291456 | tf_op jit(solution)/shard_map/gate_up/pallas_call | solution.py:183
  35.7 1.0 %down.4 = (bf16[64,768]{1,0:T(8,128)(2,1)S(1)}, bf16[64,768]{1,0:T(8,128)(2,1)S(1)}, bf16[64,768]{1,0:T(8,128)(2,1)S(1)}, bf16[64,768]{1,0:T(8,128)(2,1)S(1)}) custom-call(s32[1]{0:T(128)} %bitcast.3.column_ref, bf16[256,2048]{1,0:T(8,128)(2,1)S(1)} %gate_up.5.h_ref, bf16[1,2048,3072]{2,1,0:T(8,128)(2,1)S(1)} %bitcast.5), custom_call_target="tpu_custom_call" | custom-call | flops 805306368 | bytes 3538944 | tf_op jit(solution)/shard_map/down/pallas_call | solution.py:221
  36.8 0.2 collective-permute-start.12
  37.0 1.4 %collective-permute-start.13 = (bf16[64,768]{1,0:T(8,128)(2,1)S(1)}, bf16[64,768]{1,0:T(8,128)(2,1)S(1)}, u32[]{:S(2)}, u32[]{:S(2)}) collective-permute-start(bf16[64,768]{1,0:T(8,128)(2,1)S(1)} %get-tuple-element.79), channel_id=1, source_target_pairs={{0,2},{1,3},{2,0},{3,1},{4,6},{5,7},{6,4},{7,5},{8,10},{9,11},{10,... | collective-permute-start | bytes 294920 | tf_op jit(solution)/shard_map/ppermute | solution.py:275
  38.4 0.3 collective-permute-start.14
  38.7 1.0 %down.7 = (bf16[64,768]{1,0:T(8,128)(2,1)S(1)}, bf16[64,768]{1,0:T(8,128)(2,1)S(1)}, bf16[64,768]{1,0:T(8,128)(2,1)S(1)}, bf16[64,768]{1,0:T(8,128)(2,1)S(1)}) custom-call(s32[1]{0:T(128)} %bitcast.3.column_ref, bf16[256,2048]{1,0:T(8,128)(2,1)S(1)} %gate_up.5.h_ref, bf16[1,2048,3072]{2,1,0:T(8,128)(2,1)S(1)} %bitcast.5), custom_call_target="tpu_custom_call" | custom-call | flops 805306368 | bytes 3538944 | tf_op jit(solution)/shard_map/down/pallas_call | solution.py:221
  39.7 0.5 collective-permute-start.23
  40.2 1.4 %collective-permute-start.24 = (bf16[64,768]{1,0:T(8,128)(2,1)S(1)}, bf16[64,768]{1,0:T(8,128)(2,1)S(1)}, u32[]{:S(2)}, u32[]{:S(2)}) collective-permute-start(bf16[64,768]{1,0:T(8,128)(2,1)S(1)} %get-tuple-element.92), channel_id=1, source_target_pairs={{0,2},{1,3},{2,0},{3,1},{4,6},{5,7},{6,4},{7,5},{8,10},{9,11},{10,... | collective-permute-start | bytes 294920 | tf_op jit(solution)/shard_map/ppermute | solution.py:275
  41.7 0.9 %collective-permute-done.13.refs_2_ = bf16[64,768]{1,0:T(8,128)(2,1)S(1)} collective-permute-done((bf16[64,768]{1,0:T(8,128)(2,1)S(1)}, bf16[64,768]{1,0:T(8,128)(2,1)S(1)}, u32[]{:S(2)}, u32[]{:S(2)}) %collective-permute-start.13) | collective-permute-done | bytes 98336 | tf_op jit(solution)/shard_map/ppermute | solution.py:275
  42.6 1.0 %collective-permute-done.14.refs_3_ = bf16[64,768]{1,0:T(8,128)(2,1)S(1)} collective-permute-done((bf16[64,768]{1,0:T(8,128)(2,1)S(1)}, bf16[64,768]{1,0:T(8,128)(2,1)S(1)}, u32[]{:S(2)}, u32[]{:S(2)}) %collective-permute-start.14) | collective-permute-done | bytes 98336 | tf_op jit(solution)/shard_map/ppermute | solution.py:275
  43.6 0.3 combine.4
  44.0 1.0 %collective-permute-start.15 = (bf16[128,384]{1,0:T(8,128)(2,1)S(1)}, bf16[128,384]{1,0:T(8,128)(2,1)S(1)}, u32[]{:S(2)}, u32[]{:S(2)}) collective-permute-start(bf16[128,384]{1,0:T(8,128)(2,1)S(1)} %get-tuple-element.81.refs_0_), channel_id=1, source_target_pairs={{0,4},{4,0},{8,12},{12,8},{1,5},{5,1},{9,13},{13,9},{2,6},{6,2},{1... | collective-permute-start | bytes 294920 | tf_op jit(solution)/shard_map/ppermute | solution.py:275
  45.0 1.0 %down.6 = (bf16[64,768]{1,0:T(8,128)(2,1)S(1)}, bf16[64,768]{1,0:T(8,128)(2,1)S(1)}, bf16[64,768]{1,0:T(8,128)(2,1)S(1)}, bf16[64,768]{1,0:T(8,128)(2,1)S(1)}) custom-call(s32[1]{0:T(128)} %bitcast.3.column_ref, bf16[256,2048]{1,0:T(8,128)(2,1)S(1)} %gate_up.5.h_ref, bf16[1,2048,3072]{2,1,0:T(8,128)(2,1)S(1)} %bitcast.5, ...), custom_call_target="tpu_custom_call" | custom-call | flops 805306368 | bytes 3538944 | tf_op jit(solution)/shard_map/down/pallas_call | solution.py:221
  46.0 0.6 collective-permute-start.19
  46.6 1.5 %collective-permute-start.20 = (bf16[64,768]{1,0:T(8,128)(2,1)S(1)}, bf16[64,768]{1,0:T(8,128)(2,1)S(1)}, u32[]{:S(2)}, u32[]{:S(2)}) collective-permute-start(bf16[64,768]{1,0:T(8,128)(2,1)S(1)} %get-tuple-element.88), channel_id=1, source_target_pairs={{0,2},{1,3},{2,0},{3,1},{4,6},{5,7},{6,4},{7,5},{8,10},{9,11},{10,... | collective-permute-start | bytes 294920 | tf_op jit(solution)/shard_map/ppermute | solution.py:275
  48.1 3.8 %collective-permute-start.27 = (bf16[128,384]{1,0:T(8,128)(2,1)S(1)}, bf16[128,384]{1,0:T(8,128)(2,1)S(1)}, u32[]{:S(2)}, u32[]{:S(2)}) collective-permute-start(bf16[128,384]{1,0:T(8,128)(2,1)S(1)} %get-tuple-element.94), channel_id=1, source_target_pairs={{0,12},{4,8},{8,4},{12,0},{1,13},{5,9},{9,5},{13,1},{2,14},{6,10},... | collective-permute-start | bytes 294920 | tf_op jit(solution)/shard_map/ppermute | solution.py:275
  51.9 0.3 combine.6
  52.2 1.0 %collective-permute-start.26 = (bf16[128,768]{1,0:T(8,128)(2,1)S(1)}, bf16[128,768]{1,0:T(8,128)(2,1)S(1)}, u32[]{:S(2)}, u32[]{:S(2)}) collective-permute-start(bf16[128,768]{1,0:T(8,128)(2,1)S(1)} %combine.6), channel_id=1, source_target_pairs={{0,8},{4,12},{8,0},{12,4},{1,9},{5,13},{9,1},{13,5},{2,10},{6,14},... | collective-permute-start | bytes 589832 | tf_op jit(solution)/shard_map/ppermute | solution.py:275
  53.3 0.3 combine.5
  53.6 1.1 %collective-permute-start.22 = (bf16[128,768]{1,0:T(8,128)(2,1)S(1)}, bf16[128,768]{1,0:T(8,128)(2,1)S(1)}, u32[]{:S(2)}, u32[]{:S(2)}) collective-permute-start(bf16[128,768]{1,0:T(8,128)(2,1)S(1)} %combine.5), channel_id=1, source_target_pairs={{0,4},{4,0},{8,12},{12,8},{1,5},{5,1},{9,13},{13,9},{2,6},{6,2},{1... | collective-permute-start | bytes 589832 | tf_op jit(solution)/shard_map/ppermute | solution.py:275
  54.6 1.0 %down.5 = (bf16[64,768]{1,0:T(8,128)(2,1)S(1)}, bf16[64,768]{1,0:T(8,128)(2,1)S(1)}, bf16[64,768]{1,0:T(8,128)(2,1)S(1)}, bf16[64,768]{1,0:T(8,128)(2,1)S(1)}) custom-call(s32[1]{0:T(128)} %bitcast.3.column_ref, bf16[256,2048]{1,0:T(8,128)(2,1)S(1)} %gate_up.5.h_ref, bf16[1,2048,3072]{2,1,0:T(8,128)(2,1)S(1)} %bitcast.5, ...), custom_call_target="tpu_custom_call" | custom-call | flops 805306368 | bytes 3538944 | tf_op jit(solution)/shard_map/down/pallas_call | solution.py:221
  55.7 0.3 collective-permute-start.16
  56.0 1.4 %collective-permute-start.17 = (bf16[64,768]{1,0:T(8,128)(2,1)S(1)}, bf16[64,768]{1,0:T(8,128)(2,1)S(1)}, u32[]{:S(2)}, u32[]{:S(2)}) collective-permute-start(bf16[64,768]{1,0:T(8,128)(2,1)S(1)} %get-tuple-element.84), channel_id=1, source_target_pairs={{0,2},{1,3},{2,0},{3,1},{4,6},{5,7},{6,4},{7,5},{8,10},{9,11},{10,... | collective-permute-start | bytes 294920 | tf_op jit(solution)/shard_map/ppermute | solution.py:275
  57.6 3.9 %collective-permute-done.17.refs_2_ = bf16[64,768]{1,0:T(8,128)(2,1)S(1)} collective-permute-done((bf16[64,768]{1,0:T(8,128)(2,1)S(1)}, bf16[64,768]{1,0:T(8,128)(2,1)S(1)}, u32[]{:S(2)}, u32[]{:S(2)}) %collective-permute-start.17) | collective-permute-done | bytes 98336 | tf_op jit(solution)/shard_map/ppermute | solution.py:275
  61.5 0.9 %collective-permute-done.18.refs_3_ = bf16[64,768]{1,0:T(8,128)(2,1)S(1)} collective-permute-done((bf16[64,768]{1,0:T(8,128)(2,1)S(1)}, bf16[64,768]{1,0:T(8,128)(2,1)S(1)}, u32[]{:S(2)}, u32[]{:S(2)}) %collective-permute-start.18) | collective-permute-done | bytes 98336 | tf_op jit(solution)/shard_map/ppermute | solution.py:275
  62.5 2.7 %collective-permute-done.26.refs_5_ = bf16[128,768]{1,0:T(8,128)(2,1)S(1)} collective-permute-done((bf16[128,768]{1,0:T(8,128)(2,1)S(1)}, bf16[128,768]{1,0:T(8,128)(2,1)S(1)}, u32[]{:S(2)}, u32[]{:S(2)}) %collective-permute-start.26) | collective-permute-done | bytes 196640 | tf_op jit(solution)/shard_map/ppermute | solution.py:275
  65.2 1.0 %combine.7 = bf16[128,768]{1,0:T(8,128)(2,1)} custom-call(bf16[256,256]{1,0:T(8,128)(2,1)S(1)} %get-tuple-element.50.pick_ref, f32[128,2]{1,0:T(8,128)S(1)} %get-tuple-element.51.mix_ref, bf16[64,768]{1,0:T(8,128)(2,1)S(1)} %get-tuple-element.82.refs_0_, bf16[64,768]{1,0:T(8,128)(2,1)S(1)} %collective-permute-done.16.refs_1_, ...), custom_call_target="tpu_custom_call" | custom-call | flops 100663296 | bytes 589824 | tf_op jit(solution)/shard_map/combine/pallas_call | solution.py:258
  (38 shorter events, 0.8 us)
Async XLA Ops:
  0.0 13.5 %collective-permute-start = (bf16[128,768]{1,0:T(8,128)(2,1)}, bf16[128,768]{1,0:T(8,128)(2,1)S(1)}, u32[]{:S(2)}, u32[]{:S(2)}) collective-permute-start(bf16[128,768]{1,0:T(8,128)(2,1)} %refs_0_.4), channel_id=1, source_target_pairs={{0,8},{4,12},{8,0},{12,4},{1,9},{5,13},{9,1},{13,5},{2,10},{6,14},... | collective-permute-start | bytes 589832 | tf_op jit(solution)/shard_map/ppermute | solution.py:275
  4.0 10.2 %collective-permute-start.5 = (bf16[128,768]{1,0:T(8,128)(2,1)}, bf16[128,768]{1,0:T(8,128)(2,1)S(1)}, u32[]{:S(2)}, u32[]{:S(2)}) collective-permute-start(bf16[128,768]{1,0:T(8,128)(2,1)} %refs_0_.4), channel_id=1, source_target_pairs={{0,4},{4,0},{8,12},{12,8},{1,5},{5,1},{9,13},{13,9},{2,6},{6,2},{1... | collective-permute-start | bytes 589832 | tf_op jit(solution)/shard_map/ppermute | solution.py:275
  5.6 0.7 %copy-start.1 = (s32[128,2]{0,1:T(2,128)S(1)}, s32[128,2]{0,1:T(2,128)}, u32[]{:S(2)}) copy-start(s32[128,2]{0,1:T(2,128)} %param.7) | copy-start | bytes 3076
  6.3 0.7 %copy-start.2 = (f32[128,2]{0,1:T(2,128)S(1)}, f32[128,2]{0,1:T(2,128)}, u32[]{:S(2)}) copy-start(f32[128,2]{0,1:T(2,128)} %param.8) | copy-start | bytes 3076
  7.1 7.0 %copy-start = (bf16[128,768]{1,0:T(8,128)(2,1)S(1)}, bf16[128,768]{1,0:T(8,128)(2,1)}, u32[]{:S(2)}) copy-start(bf16[128,768]{1,0:T(8,128)(2,1)} %refs_0_.4) | copy-start | bytes 589828
  13.5 8.3 %collective-permute-start.1 = (bf16[128,768]{1,0:T(8,128)(2,1)S(1)}, bf16[128,768]{1,0:T(8,128)(2,1)S(1)}, u32[]{:S(2)}, u32[]{:S(2)}) collective-permute-start(bf16[128,768]{1,0:T(8,128)(2,1)S(1)} %collective-permute-done.refs_0_), channel_id=1, source_target_pairs={{0,4},{4,0},{8,12},{12,8},{1,5},{5,1},{9,13},{13,9},{2,6},{6,2},{1... | collective-permute-start | bytes 589832 | tf_op jit(solution)/shard_map/ppermute | solution.py:275
  14.6 9.8 %collective-permute-start.10 = (bf16[64,1536]{1,0:T(8,128)(2,1)S(1)}, bf16[64,1536]{1,0:T(8,128)(2,1)S(1)}, u32[]{:S(2)}, u32[]{:S(2)}) collective-permute-start(bf16[64,1536]{1,0:T(8,128)(2,1)S(1)} %get-tuple-element.68), channel_id=1, source_target_pairs={{0,2},{1,3},{2,0},{3,1},{4,6},{5,7},{6,4},{7,5},{8,10},{9,11},{10,... | collective-permute-start | bytes 589832 | tf_op jit(solution)/shard_map/ppermute | solution.py:275
  16.1 8.7 %collective-permute-start.11 = (bf16[64,1536]{1,0:T(8,128)(2,1)S(1)}, bf16[64,1536]{1,0:T(8,128)(2,1)S(1)}, u32[]{:S(2)}, u32[]{:S(2)}) collective-permute-start(bf16[64,1536]{1,0:T(8,128)(2,1)S(1)} %get-tuple-element.69), channel_id=1, source_target_pairs={{0,3},{1,2},{2,1},{3,0},{4,7},{5,6},{6,5},{7,4},{8,11},{9,10},{10,... | collective-permute-start | bytes 589832 | tf_op jit(solution)/shard_map/ppermute | solution.py:275
  16.1 9.7 %collective-permute-start.9 = (bf16[64,1536]{1,0:T(8,128)(2,1)S(1)}, bf16[64,1536]{1,0:T(8,128)(2,1)S(1)}, u32[]{:S(2)}, u32[]{:S(2)}) collective-permute-start(bf16[64,1536]{1,0:T(8,128)(2,1)S(1)} %get-tuple-element.67), channel_id=1, source_target_pairs={{0,1},{1,0},{2,3},{3,2},{4,5},{5,4},{6,7},{7,6},{8,9},{9,8},{10,11... | collective-permute-start | bytes 589832 | tf_op jit(solution)/shard_map/ppermute | solution.py:275
  21.7 1.9 %collective-permute-start.6 = (bf16[64,768]{1,0:T(8,128)(2,1)S(1)}, bf16[64,768]{1,0:T(8,128)(2,1)S(1)}, u32[]{:S(2)}, u32[]{:S(2)}) collective-permute-start(bf16[64,768]{1,0:T(8,128)(2,1)S(1)} %get-tuple-element.62), channel_id=1, source_target_pairs={{0,1},{1,0},{2,3},{3,2},{4,5},{5,4},{6,7},{7,6},{8,9},{9,8},{10,11... | collective-permute-start | bytes 294920 | tf_op jit(solution)/shard_map/ppermute | solution.py:275
  21.8 8.6 %collective-permute-start.7 = (bf16[64,768]{1,0:T(8,128)(2,1)S(1)}, bf16[64,768]{1,0:T(8,128)(2,1)S(1)}, u32[]{:S(2)}, u32[]{:S(2)}) collective-permute-start(bf16[64,768]{1,0:T(8,128)(2,1)S(1)} %get-tuple-element.63), channel_id=1, source_target_pairs={{0,2},{1,3},{2,0},{3,1},{4,6},{5,7},{6,4},{7,5},{8,10},{9,11},{10,... | collective-permute-start | bytes 294920 | tf_op jit(solution)/shard_map/ppermute | solution.py:275
  23.7 6.8 %collective-permute-start.8 = (bf16[64,768]{1,0:T(8,128)(2,1)S(1)}, bf16[64,768]{1,0:T(8,128)(2,1)S(1)}, u32[]{:S(2)}, u32[]{:S(2)}) collective-permute-start(bf16[64,768]{1,0:T(8,128)(2,1)S(1)} %get-tuple-element.64), channel_id=1, source_target_pairs={{0,3},{1,2},{2,1},{3,0},{4,7},{5,6},{6,5},{7,4},{8,11},{9,10},{10,... | collective-permute-start | bytes 294920 | tf_op jit(solution)/shard_map/ppermute | solution.py:275
  24.4 8.3 %collective-permute-start.2 = (bf16[64,768]{1,0:T(8,128)(2,1)S(1)}, bf16[64,768]{1,0:T(8,128)(2,1)S(1)}, u32[]{:S(2)}, u32[]{:S(2)}) collective-permute-start(bf16[64,768]{1,0:T(8,128)(2,1)S(1)} %get-tuple-element.54), channel_id=1, source_target_pairs={{0,1},{1,0},{2,3},{3,2},{4,5},{5,4},{6,7},{7,6},{8,9},{9,8},{10,11... | collective-permute-start | bytes 294920 | tf_op jit(solution)/shard_map/ppermute | solution.py:275
  24.8 7.8 %collective-permute-start.3 = (bf16[64,768]{1,0:T(8,128)(2,1)S(1)}, bf16[64,768]{1,0:T(8,128)(2,1)S(1)}, u32[]{:S(2)}, u32[]{:S(2)}) collective-permute-start(bf16[64,768]{1,0:T(8,128)(2,1)S(1)} %get-tuple-element.55), channel_id=1, source_target_pairs={{0,2},{1,3},{2,0},{3,1},{4,6},{5,7},{6,4},{7,5},{8,10},{9,11},{10,... | collective-permute-start | bytes 294920 | tf_op jit(solution)/shard_map/ppermute | solution.py:275
  25.9 7.5 %collective-permute-start.4 = (bf16[64,768]{1,0:T(8,128)(2,1)S(1)}, bf16[64,768]{1,0:T(8,128)(2,1)S(1)}, u32[]{:S(2)}, u32[]{:S(2)}) collective-permute-start(bf16[64,768]{1,0:T(8,128)(2,1)S(1)} %get-tuple-element.56), channel_id=1, source_target_pairs={{0,3},{1,2},{2,1},{3,0},{4,7},{5,6},{6,5},{7,4},{8,11},{9,10},{10,... | collective-permute-start | bytes 294920 | tf_op jit(solution)/shard_map/ppermute | solution.py:275
  30.5 5.1 %slice-start = ((s8[12582912]{0:T(1024)(128)(4,1)}), s8[4194304]{0:T(1024)(128)(4,1)S(1)}, s32[]{:S(2)}) async-start(s8[12582912]{0:T(1024)(128)(4,1)} %bitcast.4), calls=%async_computation | async-start | bytes 8388608
  30.5 5.1 %slice-start.1 = ((s8[12582912]{0:T(1024)(128)(4,1)}), s8[4194304]{0:T(1024)(128)(4,1)S(1)}, s32[]{:S(2)}) async-start(s8[12582912]{0:T(1024)(128)(4,1)} %bitcast.4), calls=%async_computation.1 | async-start | bytes 8388608
  33.4 2.3 %slice-start.2 = ((s8[12582912]{0:T(1024)(128)(4,1)}), s8[4194304]{0:T(1024)(128)(4,1)S(1)}, s32[]{:S(2)}) async-start(s8[12582912]{0:T(1024)(128)(4,1)} %bitcast.4), calls=%async_computation.2 | async-start | bytes 8388608
  36.8 4.9 %collective-permute-start.12 = (bf16[64,768]{1,0:T(8,128)(2,1)S(1)}, bf16[64,768]{1,0:T(8,128)(2,1)S(1)}, u32[]{:S(2)}, u32[]{:S(2)}) collective-permute-start(bf16[64,768]{1,0:T(8,128)(2,1)S(1)} %get-tuple-element.78), channel_id=1, source_target_pairs={{0,1},{1,0},{2,3},{3,2},{4,5},{5,4},{6,7},{7,6},{8,9},{9,8},{10,11... | collective-permute-start | bytes 294920 | tf_op jit(solution)/shard_map/ppermute | solution.py:275
  37.0 5.6 %collective-permute-start.13 = (bf16[64,768]{1,0:T(8,128)(2,1)S(1)}, bf16[64,768]{1,0:T(8,128)(2,1)S(1)}, u32[]{:S(2)}, u32[]{:S(2)}) collective-permute-start(bf16[64,768]{1,0:T(8,128)(2,1)S(1)} %get-tuple-element.79), channel_id=1, source_target_pairs={{0,2},{1,3},{2,0},{3,1},{4,6},{5,7},{6,4},{7,5},{8,10},{9,11},{10,... | collective-permute-start | bytes 294920 | tf_op jit(solution)/shard_map/ppermute | solution.py:275
  38.4 5.2 %collective-permute-start.14 = (bf16[64,768]{1,0:T(8,128)(2,1)S(1)}, bf16[64,768]{1,0:T(8,128)(2,1)S(1)}, u32[]{:S(2)}, u32[]{:S(2)}) collective-permute-start(bf16[64,768]{1,0:T(8,128)(2,1)S(1)} %get-tuple-element.80), channel_id=1, source_target_pairs={{0,3},{1,2},{2,1},{3,0},{4,7},{5,6},{6,5},{7,4},{8,11},{9,10},{10,... | collective-permute-start | bytes 294920 | tf_op jit(solution)/shard_map/ppermute | solution.py:275
  39.7 6.9 %collective-permute-start.23 = (bf16[64,768]{1,0:T(8,128)(2,1)S(1)}, bf16[64,768]{1,0:T(8,128)(2,1)S(1)}, u32[]{:S(2)}, u32[]{:S(2)}) collective-permute-start(bf16[64,768]{1,0:T(8,128)(2,1)S(1)} %get-tuple-element.91), channel_id=1, source_target_pairs={{0,1},{1,0},{2,3},{3,2},{4,5},{5,4},{6,7},{7,6},{8,9},{9,8},{10,11... | collective-permute-start | bytes 294920 | tf_op jit(solution)/shard_map/ppermute | solution.py:275
  40.2 7.9 %collective-permute-start.24 = (bf16[64,768]{1,0:T(8,128)(2,1)S(1)}, bf16[64,768]{1,0:T(8,128)(2,1)S(1)}, u32[]{:S(2)}, u32[]{:S(2)}) collective-permute-start(bf16[64,768]{1,0:T(8,128)(2,1)S(1)} %get-tuple-element.92), channel_id=1, source_target_pairs={{0,2},{1,3},{2,0},{3,1},{4,6},{5,7},{6,4},{7,5},{8,10},{9,11},{10,... | collective-permute-start | bytes 294920 | tf_op jit(solution)/shard_map/ppermute | solution.py:275
  41.6 6.5 %collective-permute-start.25 = (bf16[64,768]{1,0:T(8,128)(2,1)S(1)}, bf16[64,768]{1,0:T(8,128)(2,1)S(1)}, u32[]{:S(2)}, u32[]{:S(2)}) collective-permute-start(bf16[64,768]{1,0:T(8,128)(2,1)S(1)} %get-tuple-element.93), channel_id=1, source_target_pairs={{0,3},{1,2},{2,1},{3,0},{4,7},{5,6},{6,5},{7,4},{8,11},{9,10},{10,... | collective-permute-start | bytes 294920 | tf_op jit(solution)/shard_map/ppermute | solution.py:275
  44.0 8.0 %collective-permute-start.15 = (bf16[128,384]{1,0:T(8,128)(2,1)S(1)}, bf16[128,384]{1,0:T(8,128)(2,1)S(1)}, u32[]{:S(2)}, u32[]{:S(2)}) collective-permute-start(bf16[128,384]{1,0:T(8,128)(2,1)S(1)} %get-tuple-element.81.refs_0_), channel_id=1, source_target_pairs={{0,4},{4,0},{8,12},{12,8},{1,5},{5,1},{9,13},{13,9},{2,6},{6,2},{1... | collective-permute-start | bytes 294920 | tf_op jit(solution)/shard_map/ppermute | solution.py:275
  46.0 7.2 %collective-permute-start.19 = (bf16[64,768]{1,0:T(8,128)(2,1)S(1)}, bf16[64,768]{1,0:T(8,128)(2,1)S(1)}, u32[]{:S(2)}, u32[]{:S(2)}) collective-permute-start(bf16[64,768]{1,0:T(8,128)(2,1)S(1)} %get-tuple-element.87), channel_id=1, source_target_pairs={{0,1},{1,0},{2,3},{3,2},{4,5},{5,4},{6,7},{7,6},{8,9},{9,8},{10,11... | collective-permute-start | bytes 294920 | tf_op jit(solution)/shard_map/ppermute | solution.py:275
  46.6 6.6 %collective-permute-start.20 = (bf16[64,768]{1,0:T(8,128)(2,1)S(1)}, bf16[64,768]{1,0:T(8,128)(2,1)S(1)}, u32[]{:S(2)}, u32[]{:S(2)}) collective-permute-start(bf16[64,768]{1,0:T(8,128)(2,1)S(1)} %get-tuple-element.88), channel_id=1, source_target_pairs={{0,2},{1,3},{2,0},{3,1},{4,6},{5,7},{6,4},{7,5},{8,10},{9,11},{10,... | collective-permute-start | bytes 294920 | tf_op jit(solution)/shard_map/ppermute | solution.py:275
  48.1 5.1 %collective-permute-start.21 = (bf16[64,768]{1,0:T(8,128)(2,1)S(1)}, bf16[64,768]{1,0:T(8,128)(2,1)S(1)}, u32[]{:S(2)}, u32[]{:S(2)}) collective-permute-start(bf16[64,768]{1,0:T(8,128)(2,1)S(1)} %get-tuple-element.89), channel_id=1, source_target_pairs={{0,3},{1,2},{2,1},{3,0},{4,7},{5,6},{6,5},{7,4},{8,11},{9,10},{10,... | collective-permute-start | bytes 294920 | tf_op jit(solution)/shard_map/ppermute | solution.py:275
  48.1 9.3 %collective-permute-start.27 = (bf16[128,384]{1,0:T(8,128)(2,1)S(1)}, bf16[128,384]{1,0:T(8,128)(2,1)S(1)}, u32[]{:S(2)}, u32[]{:S(2)}) collective-permute-start(bf16[128,384]{1,0:T(8,128)(2,1)S(1)} %get-tuple-element.94), channel_id=1, source_target_pairs={{0,12},{4,8},{8,4},{12,0},{1,13},{5,9},{9,5},{13,1},{2,14},{6,10},... | collective-permute-start | bytes 294920 | tf_op jit(solution)/shard_map/ppermute | solution.py:275
  52.2 13.0 %collective-permute-start.26 = (bf16[128,768]{1,0:T(8,128)(2,1)S(1)}, bf16[128,768]{1,0:T(8,128)(2,1)S(1)}, u32[]{:S(2)}, u32[]{:S(2)}) collective-permute-start(bf16[128,768]{1,0:T(8,128)(2,1)S(1)} %combine.6), channel_id=1, source_target_pairs={{0,8},{4,12},{8,0},{12,4},{1,9},{5,13},{9,1},{13,5},{2,10},{6,14},... | collective-permute-start | bytes 589832 | tf_op jit(solution)/shard_map/ppermute | solution.py:275
  53.6 11.7 %collective-permute-start.22 = (bf16[128,768]{1,0:T(8,128)(2,1)S(1)}, bf16[128,768]{1,0:T(8,128)(2,1)S(1)}, u32[]{:S(2)}, u32[]{:S(2)}) collective-permute-start(bf16[128,768]{1,0:T(8,128)(2,1)S(1)} %combine.5), channel_id=1, source_target_pairs={{0,4},{4,0},{8,12},{12,8},{1,5},{5,1},{9,13},{13,9},{2,6},{6,2},{1... | collective-permute-start | bytes 589832 | tf_op jit(solution)/shard_map/ppermute | solution.py:275
  55.7 1.9 %collective-permute-start.16 = (bf16[64,768]{1,0:T(8,128)(2,1)S(1)}, bf16[64,768]{1,0:T(8,128)(2,1)S(1)}, u32[]{:S(2)}, u32[]{:S(2)}) collective-permute-start(bf16[64,768]{1,0:T(8,128)(2,1)S(1)} %get-tuple-element.83), channel_id=1, source_target_pairs={{0,1},{1,0},{2,3},{3,2},{4,5},{5,4},{6,7},{7,6},{8,9},{9,8},{10,11... | collective-permute-start | bytes 294920 | tf_op jit(solution)/shard_map/ppermute | solution.py:275
  56.0 5.5 %collective-permute-start.17 = (bf16[64,768]{1,0:T(8,128)(2,1)S(1)}, bf16[64,768]{1,0:T(8,128)(2,1)S(1)}, u32[]{:S(2)}, u32[]{:S(2)}) collective-permute-start(bf16[64,768]{1,0:T(8,128)(2,1)S(1)} %get-tuple-element.84), channel_id=1, source_target_pairs={{0,2},{1,3},{2,0},{3,1},{4,6},{5,7},{6,4},{7,5},{8,10},{9,11},{10,... | collective-permute-start | bytes 294920 | tf_op jit(solution)/shard_map/ppermute | solution.py:275
  57.4 5.1 %collective-permute-start.18 = (bf16[64,768]{1,0:T(8,128)(2,1)S(1)}, bf16[64,768]{1,0:T(8,128)(2,1)S(1)}, u32[]{:S(2)}, u32[]{:S(2)}) collective-permute-start(bf16[64,768]{1,0:T(8,128)(2,1)S(1)} %get-tuple-element.85), channel_id=1, source_target_pairs={{0,3},{1,2},{2,1},{3,0},{4,7},{5,6},{6,5},{7,4},{8,11},{9,10},{10,... | collective-permute-start | bytes 294920 | tf_op jit(solution)/shard_map/ppermute | solution.py:275

commit v13 on v12

--- a/solution.py
+++ b/solution.py
@@ -268,6 +268,22 @@
     )(pick, mix, *blocks, *[array for array, _ in added])
 
 
+def hold_kernel(array_ref, after_ref, out_ref):
+    out_ref[...] = array_ref[...]
+
+
+def hold(array, after):
+    return pl.pallas_call(
+        hold_kernel,
+        out_shape=jax.ShapeDtypeStruct(array.shape, array.dtype),
+        in_specs=[pl.BlockSpec(memory_space=pltpu.VMEM), pl.BlockSpec(memory_space=pl.ANY)],
+        out_specs=pl.BlockSpec(memory_space=pltpu.VMEM),
+        cost_estimate=cost(0, 4 * array.size),
+        compiler_params=params(),
+        name="hold",
+    )(array, after)
+
+
 def swap(value, axis, distance):
     if not distance:
         return value
@@ -323,9 +339,9 @@
         return lax.psum_scatter(mixed, "tensor", scatter_dimension=1, tiled=True)
     low, high = combine(pick, mix, returned(across(3)), [], cuts=2)
     passed = swap(low, "tensor", 1)
-    far = (swap(high, "tensor", 3), width // 2)
     onwards = combine(pick, mix, returned(across(2)), [(passed, 0)])[0]
     over = (swap(onwards, "tensor", 2), 0)
+    far = (swap(hold(high, onwards), "tensor", 3), width // 2)
     near = combine(pick, mix, returned(across(1), [low]), [])[0]
     beside = (swap(near, "tensor", 1), 0)
     return combine(pick, mix, returned(across(0), [passed]), [beside, over, far])[0]

time: 66.4 us -> 70.8 us (1.066)
  the two profiles are of different devices: /device:TPU:0 before, /device:TPU:21 now
where the time goes in v13:
time: 70.8 us; the launch traced here: 70.6 us
  starting transfers between devices  27.2 us (38%)
  Pallas kernels  24.2 us (34%)
  waiting for transfers between devices  17.4 us (25%)
  local copies, waits for them, and re-layouts  1.48 us (2%)
    ppermute x28, starting transfers between devices, swap(): return lax.ppermute(value, axis, [(i, i ^ distance) for i in range(count)])  27.2 us
    ppermute x28, waiting for transfers between devices, swap(): return lax.ppermute(value, axis, [(i, i ^ distance) for i in range(count)])  17.4 us
    pallas_call x2, Pallas kernels, prefetch(): pl.pallas_call(functools.partial(prefetch_kernel, parts=[part for _, part...  9.41 us
    pallas_call x3, Pallas kernels, gate_up(): pl.pallas_call(functools.partial(gate_up_kernel, experts=experts, slices=...  7.71 us
    pallas_call x4, Pallas kernels, down(): pl.pallas_call(functools.partial(down_kernel, part=part, waits=len(after)...  4.1 us
    pallas_call x4, Pallas kernels, combine(): pl.pallas_call(functools.partial(combine_kernel, experts=len(blocks), sta...  1.93 us
    unnamed x12, local copies, waits for them, and re-layouts  1.48 us
  transfers between devices with their start and end apart: 28, of which 9 were waited for; matrix products, arithmetic and copies ran while one was open for 0% of the time, Pallas kernels for 28%

profile of v13, /device:TPU:21, one launch (start us, length us, event | category | flops | bytes accessed | tf_op | source)
XLA Modules:
  0.0 70.6 jit_solution(18240898136753136286)
XLA Ops:
  0.1 1.3 %collective-permute-start.5 = (bf16[128,768]{1,0:T(8,128)(2,1)}, bf16[128,768]{1,0:T(8,128)(2,1)S(1)}, u32[]{:S(2)}, u32[]{:S(2)}) collective-permute-start(bf16[128,768]{1,0:T(8,128)(2,1)} %refs_0_.4), channel_id=1, source_target_pairs={{0,4},{4,0},{8,12},{12,8},{1,5},{5,1},{9,13},{13,9},{2,6},{6,2},{1... | collective-permute-start | bytes 589832 | tf_op jit(solution)/shard_map/ppermute | solution.py:291
  1.4 0.7 copy-done.1
  2.0 0.7 copy-done.2
  2.7 0.2 routing.1
  2.9 4.7 %prefetch.2 = (bf16[768,2048]{1,0:T(8,128)(2,1)S(1)}, bf16[768,2048]{1,0:T(8,128)(2,1)S(1)}, bf16[768,2048]{1,0:T(8,128)(2,1)S(1)}, bf16[768,2048]{1,0:T(8,128)(2,1)S(1)}) custom-call(s32[1]{0:T(128)} %bitcast.3.column_ref, bf16[256,128]{1,0:T(8,128)(2,1)S(1)} %get-tuple-element.52.placed_ref.after_ref, bf16[1,3072,2048]{2,1,0:T(8,128)(2,1)} %refs_2_.3, ...), custom_call_target="tpu_custom_call" | custom-call | bytes 12582912 | tf_op jit(solution)/shard_map/prefetch/pallas_call | solution.py:127
  7.6 0.5 collective-permute-done.refs_0_
  8.2 5.2 %collective-permute-start.1 = (bf16[128,768]{1,0:T(8,128)(2,1)S(1)}, bf16[128,768]{1,0:T(8,128)(2,1)S(1)}, u32[]{:S(2)}, u32[]{:S(2)}) collective-permute-start(bf16[128,768]{1,0:T(8,128)(2,1)S(1)} %collective-permute-done.refs_0_), channel_id=1, source_target_pairs={{0,4},{4,0},{8,12},{12,8},{1,5},{5,1},{9,13},{13,9},{2,6},{6,2},{1... | collective-permute-start | bytes 589832 | tf_op jit(solution)/shard_map/ppermute | solution.py:291
  13.3 0.4 dispatch.4
  13.7 1.3 %collective-permute-start.10 = (bf16[64,1536]{1,0:T(8,128)(2,1)S(1)}, bf16[64,1536]{1,0:T(8,128)(2,1)S(1)}, u32[]{:S(2)}, u32[]{:S(2)}) collective-permute-start(bf16[64,1536]{1,0:T(8,128)(2,1)S(1)} %get-tuple-element.68), channel_id=1, source_target_pairs={{0,2},{1,3},{2,0},{3,1},{4,6},{5,7},{6,4},{7,5},{8,10},{9,11},{10,... | collective-permute-start | bytes 589832 | tf_op jit(solution)/shard_map/ppermute | solution.py:291
  15.0 1.2 %collective-permute-start.11 = (bf16[64,1536]{1,0:T(8,128)(2,1)S(1)}, bf16[64,1536]{1,0:T(8,128)(2,1)S(1)}, u32[]{:S(2)}, u32[]{:S(2)}) collective-permute-start(bf16[64,1536]{1,0:T(8,128)(2,1)S(1)} %get-tuple-element.69), channel_id=1, source_target_pairs={{0,3},{1,2},{2,1},{3,0},{4,7},{5,6},{6,5},{7,4},{8,11},{9,10},{10,... | collective-permute-start | bytes 589832 | tf_op jit(solution)/shard_map/ppermute | solution.py:291
  16.2 4.7 %prefetch.3 = (bf16[768,2048]{1,0:T(8,128)(2,1)S(1)}, bf16[768,2048]{1,0:T(8,128)(2,1)S(1)}, bf16[768,2048]{1,0:T(8,128)(2,1)S(1)}, bf16[768,2048]{1,0:T(8,128)(2,1)S(1)}) custom-call(s32[1]{0:T(128)} %bitcast.3.column_ref, bf16[64,1536]{1,0:T(8,128)(2,1)S(1)} %get-tuple-element.58.after_ref.refs_0_, bf16[1,3072,2048]{2,1,0:T(8,128)(2,1)} %refs_2_.3, ...), custom_call_target="tpu_custom_call" | custom-call | bytes 12582912 | tf_op jit(solution)/shard_map/prefetch/pallas_call | solution.py:127
  20.9 0.3 dispatch.5
  21.1 0.6 collective-permute-start.6
  21.7 1.2 %collective-permute-start.7 = (bf16[64,768]{1,0:T(8,128)(2,1)S(1)}, bf16[64,768]{1,0:T(8,128)(2,1)S(1)}, u32[]{:S(2)}, u32[]{:S(2)}) collective-permute-start(bf16[64,768]{1,0:T(8,128)(2,1)S(1)} %get-tuple-element.63), channel_id=1, source_target_pairs={{0,2},{1,3},{2,0},{3,1},{4,6},{5,7},{6,4},{7,5},{8,10},{9,11},{10,... | collective-permute-start | bytes 294920 | tf_op jit(solution)/shard_map/ppermute | solution.py:291
  22.9 0.3 dispatch.3
  23.2 0.9 %collective-permute-start.8 = (bf16[64,768]{1,0:T(8,128)(2,1)S(1)}, bf16[64,768]{1,0:T(8,128)(2,1)S(1)}, u32[]{:S(2)}, u32[]{:S(2)}) collective-permute-start(bf16[64,768]{1,0:T(8,128)(2,1)S(1)} %get-tuple-element.64), channel_id=1, source_target_pairs={{0,3},{1,2},{2,1},{3,0},{4,7},{5,6},{6,5},{7,4},{8,11},{9,10},{10,... | collective-permute-start | bytes 294920 | tf_op jit(solution)/shard_map/ppermute | solution.py:291
  24.1 0.2 collective-permute-start.2
  24.3 0.7 %collective-permute-done.11.refs_3_ = bf16[64,1536]{1,0:T(8,128)(2,1)S(1)} collective-permute-done((bf16[64,1536]{1,0:T(8,128)(2,1)S(1)}, bf16[64,1536]{1,0:T(8,128)(2,1)S(1)}, u32[]{:S(2)}, u32[]{:S(2)}) %collective-permute-start.11) | collective-permute-done | bytes 196640 | tf_op jit(solution)/shard_map/ppermute | solution.py:291
  25.0 1.2 %collective-permute-start.3 = (bf16[64,768]{1,0:T(8,128)(2,1)S(1)}, bf16[64,768]{1,0:T(8,128)(2,1)S(1)}, u32[]{:S(2)}, u32[]{:S(2)}) collective-permute-start(bf16[64,768]{1,0:T(8,128)(2,1)S(1)} %get-tuple-element.55), channel_id=1, source_target_pairs={{0,2},{1,3},{2,0},{3,1},{4,6},{5,7},{6,4},{7,5},{8,10},{9,11},{10,... | collective-permute-start | bytes 294920 | tf_op jit(solution)/shard_map/ppermute | solution.py:291
  26.3 3.5 %gate_up.3 = (f32[256,2048]{1,0:T(8,128)S(1)}, f32[256,2048]{1,0:T(8,128)S(1)}) custom-call(bf16[64,1536]{1,0:T(8,128)(2,1)S(1)} %get-tuple-element.58.after_ref.refs_0_, bf16[64,1536]{1,0:T(8,128)(2,1)S(1)} %collective-permute-done.9.refs_1_, bf16[64,1536]{1,0:T(8,128)(2,1)S(1)} %collective-permute-done.10.refs_2_, ...), custom_call_target="tpu_custom_call" | custom-call | flops 3221225472 | bytes 12582912 | tf_op jit(solution)/shard_map/gate_up/pallas_call | solution.py:183
  29.9 2.1 %gate_up.4 = (f32[256,2048]{1,0:T(8,128)S(1)}, f32[256,2048]{1,0:T(8,128)S(1)}) custom-call(bf16[64,768]{1,0:T(8,128)(2,1)S(1)} %get-tuple-element.61.refs_0_, bf16[64,768]{1,0:T(8,128)(2,1)S(1)} %collective-permute-done.6.refs_8_.refs_1_, bf16[64,768]{1,0:T(8,128)(2,1)S(1)} %collective-permute-done.7.refs_2_, ...), custom_call_target="tpu_custom_call", output_to_operand_aliasing={{0}: (6, {}), {1}: (7, {})} | custom-call | flops 1610612736 | bytes 6291456 | tf_op jit(solution)/shard_map/gate_up/pallas_call | solution.py:183
  32.0 1.0 %collective-permute-done.4.refs_3_ = bf16[64,768]{1,0:T(8,128)(2,1)S(1)} collective-permute-done((bf16[64,768]{1,0:T(8,128)(2,1)S(1)}, bf16[64,768]{1,0:T(8,128)(2,1)S(1)}, u32[]{:S(2)}, u32[]{:S(2)}) %collective-permute-start.4) | collective-permute-done | bytes 98336 | tf_op jit(solution)/shard_map/ppermute | solution.py:291
  33.0 2.1 %gate_up.5.h_ref = bf16[256,2048]{1,0:T(8,128)(2,1)S(1)} custom-call(bf16[64,768]{1,0:T(8,128)(2,1)S(1)} %get-tuple-element.53.refs_0_, bf16[64,768]{1,0:T(8,128)(2,1)S(1)} %collective-permute-done.2.refs_1_, bf16[64,768]{1,0:T(8,128)(2,1)S(1)} %collective-permute-done.3.refs_2_, bf16[64,768]{1,0:T(8,128)(2,1)S(1)} %collective-permute-done.4.refs_3_, ...), custom_call_target="tpu_custom_call" | custom-call | flops 1610612736 | bytes 6291456 | tf_op jit(solution)/shard_map/gate_up/pallas_call | solution.py:183
  35.3 1.0 %down.4 = (bf16[64,768]{1,0:T(8,128)(2,1)S(1)}, bf16[64,768]{1,0:T(8,128)(2,1)S(1)}, bf16[64,768]{1,0:T(8,128)(2,1)S(1)}, bf16[64,768]{1,0:T(8,128)(2,1)S(1)}) custom-call(s32[1]{0:T(128)} %bitcast.3.column_ref, bf16[256,2048]{1,0:T(8,128)(2,1)S(1)} %gate_up.5.h_ref, bf16[1,2048,3072]{2,1,0:T(8,128)(2,1)S(1)} %bitcast.5), custom_call_target="tpu_custom_call" | custom-call | flops 805306368 | bytes 3538944 | tf_op jit(solution)/shard_map/down/pallas_call | solution.py:221
  36.3 0.4 collective-permute-start.12
  36.7 1.2 %collective-permute-start.13 = (bf16[64,768]{1,0:T(8,128)(2,1)S(1)}, bf16[64,768]{1,0:T(8,128)(2,1)S(1)}, u32[]{:S(2)}, u32[]{:S(2)}) collective-permute-start(bf16[64,768]{1,0:T(8,128)(2,1)S(1)} %get-tuple-element.79), channel_id=1, source_target_pairs={{0,2},{1,3},{2,0},{3,1},{4,6},{5,7},{6,4},{7,5},{8,10},{9,11},{10,... | collective-permute-start | bytes 294920 | tf_op jit(solution)/shard_map/ppermute | solution.py:291
  38.0 0.6 collective-permute-start.14
  38.5 1.0 %down.7 = (bf16[64,768]{1,0:T(8,128)(2,1)S(1)}, bf16[64,768]{1,0:T(8,128)(2,1)S(1)}, bf16[64,768]{1,0:T(8,128)(2,1)S(1)}, bf16[64,768]{1,0:T(8,128)(2,1)S(1)}) custom-call(s32[1]{0:T(128)} %bitcast.3.column_ref, bf16[256,2048]{1,0:T(8,128)(2,1)S(1)} %gate_up.5.h_ref, bf16[1,2048,3072]{2,1,0:T(8,128)(2,1)S(1)} %bitcast.5), custom_call_target="tpu_custom_call" | custom-call | flops 805306368 | bytes 3538944 | tf_op jit(solution)/shard_map/down/pallas_call | solution.py:221
  39.7 1.2 %collective-permute-start.24 = (bf16[64,768]{1,0:T(8,128)(2,1)S(1)}, bf16[64,768]{1,0:T(8,128)(2,1)S(1)}, u32[]{:S(2)}, u32[]{:S(2)}) collective-permute-start(bf16[64,768]{1,0:T(8,128)(2,1)S(1)} %get-tuple-element.92), channel_id=1, source_target_pairs={{0,2},{1,3},{2,0},{3,1},{4,6},{5,7},{6,4},{7,5},{8,10},{9,11},{10,... | collective-permute-start | bytes 294920 | tf_op jit(solution)/shard_map/ppermute | solution.py:291
  40.9 0.8 %collective-permute-start.25 = (bf16[64,768]{1,0:T(8,128)(2,1)S(1)}, bf16[64,768]{1,0:T(8,128)(2,1)S(1)}, u32[]{:S(2)}, u32[]{:S(2)}) collective-permute-start(bf16[64,768]{1,0:T(8,128)(2,1)S(1)} %get-tuple-element.93), channel_id=1, source_target_pairs={{0,3},{1,2},{2,1},{3,0},{4,7},{5,6},{6,5},{7,4},{8,11},{9,10},{10,... | collective-permute-start | bytes 294920 | tf_op jit(solution)/shard_map/ppermute | solution.py:291
  41.8 2.1 %collective-permute-done.14.refs_3_ = bf16[64,768]{1,0:T(8,128)(2,1)S(1)} collective-permute-done((bf16[64,768]{1,0:T(8,128)(2,1)S(1)}, bf16[64,768]{1,0:T(8,128)(2,1)S(1)}, u32[]{:S(2)}, u32[]{:S(2)}) %collective-permute-start.14) | collective-permute-done | bytes 98336 | tf_op jit(solution)/shard_map/ppermute | solution.py:291
  43.9 0.3 combine.4
  44.3 1.0 %down.6 = (bf16[64,768]{1,0:T(8,128)(2,1)S(1)}, bf16[64,768]{1,0:T(8,128)(2,1)S(1)}, bf16[64,768]{1,0:T(8,128)(2,1)S(1)}, bf16[64,768]{1,0:T(8,128)(2,1)S(1)}) custom-call(s32[1]{0:T(128)} %bitcast.3.column_ref, bf16[256,2048]{1,0:T(8,128)(2,1)S(1)} %gate_up.5.h_ref, bf16[1,2048,3072]{2,1,0:T(8,128)(2,1)S(1)} %bitcast.5, ...), custom_call_target="tpu_custom_call" | custom-call | flops 805306368 | bytes 3538944 | tf_op jit(solution)/shard_map/down/pallas_call | solution.py:221
  45.4 1.2 %collective-permute-start.20 = (bf16[64,768]{1,0:T(8,128)(2,1)S(1)}, bf16[64,768]{1,0:T(8,128)(2,1)S(1)}, u32[]{:S(2)}, u32[]{:S(2)}) collective-permute-start(bf16[64,768]{1,0:T(8,128)(2,1)S(1)} %get-tuple-element.88), channel_id=1, source_target_pairs={{0,2},{1,3},{2,0},{3,1},{4,6},{5,7},{6,4},{7,5},{8,10},{9,11},{10,... | collective-permute-start | bytes 294920 | tf_op jit(solution)/shard_map/ppermute | solution.py:291
  46.7 1.1 %collective-permute-start.21 = (bf16[64,768]{1,0:T(8,128)(2,1)S(1)}, bf16[64,768]{1,0:T(8,128)(2,1)S(1)}, u32[]{:S(2)}, u32[]{:S(2)}) collective-permute-start(bf16[64,768]{1,0:T(8,128)(2,1)S(1)} %get-tuple-element.89), channel_id=1, source_target_pairs={{0,3},{1,2},{2,1},{3,0},{4,7},{5,6},{6,5},{7,4},{8,11},{9,10},{10,... | collective-permute-start | bytes 294920 | tf_op jit(solution)/shard_map/ppermute | solution.py:291
  47.9 1.2 %collective-permute-done.15.refs_0_.refs_4_ = bf16[128,384]{1,0:T(8,128)(2,1)S(1)} collective-permute-done((bf16[128,384]{1,0:T(8,128)(2,1)S(1)}, bf16[128,384]{1,0:T(8,128)(2,1)S(1)}, u32[]{:S(2)}, u32[]{:S(2)}) %collective-permute-start.15) | collective-permute-done | bytes 98336 | tf_op jit(solution)/shard_map/ppermute | solution.py:291
  49.0 0.3 combine.6.after_ref
  49.4 1.2 %collective-permute-start.27 = (bf16[128,384]{1,0:T(8,128)(2,1)S(1)}, bf16[128,384]{1,0:T(8,128)(2,1)S(1)}, u32[]{:S(2)}, u32[]{:S(2)}) collective-permute-start(bf16[128,384]{1,0:T(8,128)(2,1)S(1)} %hold.1), channel_id=1, source_target_pairs={{0,12},{4,8},{8,4},{12,0},{1,13},{5,9},{9,5},{13,1},{2,14},{6,10},... | collective-permute-start | bytes 294920 | tf_op jit(solution)/shard_map/ppermute | solution.py:291
  50.6 1.5 %collective-permute-done.21.refs_3_ = bf16[64,768]{1,0:T(8,128)(2,1)S(1)} collective-permute-done((bf16[64,768]{1,0:T(8,128)(2,1)S(1)}, bf16[64,768]{1,0:T(8,128)(2,1)S(1)}, u32[]{:S(2)}, u32[]{:S(2)}) %collective-permute-start.21) | collective-permute-done | bytes 98336 | tf_op jit(solution)/shard_map/ppermute | solution.py:291
  52.1 0.3 combine.5
  52.5 1.5 %collective-permute-start.22 = (bf16[128,768]{1,0:T(8,128)(2,1)S(1)}, bf16[128,768]{1,0:T(8,128)(2,1)S(1)}, u32[]{:S(2)}, u32[]{:S(2)}) collective-permute-start(bf16[128,768]{1,0:T(8,128)(2,1)S(1)} %combine.5), channel_id=1, source_target_pairs={{0,4},{4,0},{8,12},{12,8},{1,5},{5,1},{9,13},{13,9},{2,6},{6,2},{1... | collective-permute-start | bytes 589832 | tf_op jit(solution)/shard_map/ppermute | solution.py:291
  53.9 1.0 %down.5 = (bf16[64,768]{1,0:T(8,128)(2,1)S(1)}, bf16[64,768]{1,0:T(8,128)(2,1)S(1)}, bf16[64,768]{1,0:T(8,128)(2,1)S(1)}, bf16[64,768]{1,0:T(8,128)(2,1)S(1)}) custom-call(s32[1]{0:T(128)} %bitcast.3.column_ref, bf16[256,2048]{1,0:T(8,128)(2,1)S(1)} %gate_up.5.h_ref, bf16[1,2048,3072]{2,1,0:T(8,128)(2,1)S(1)} %bitcast.5, ...), custom_call_target="tpu_custom_call" | custom-call | flops 805306368 | bytes 3538944 | tf_op jit(solution)/shard_map/down/pallas_call | solution.py:221
  55.0 0.9 %collective-permute-start.16 = (bf16[64,768]{1,0:T(8,128)(2,1)S(1)}, bf16[64,768]{1,0:T(8,128)(2,1)S(1)}, u32[]{:S(2)}, u32[]{:S(2)}) collective-permute-start(bf16[64,768]{1,0:T(8,128)(2,1)S(1)} %get-tuple-element.83), channel_id=1, source_target_pairs={{0,1},{1,0},{2,3},{3,2},{4,5},{5,4},{6,7},{7,6},{8,9},{9,8},{10,11... | collective-permute-start | bytes 294920 | tf_op jit(solution)/shard_map/ppermute | solution.py:291
  55.8 1.1 %collective-permute-start.17 = (bf16[64,768]{1,0:T(8,128)(2,1)S(1)}, bf16[64,768]{1,0:T(8,128)(2,1)S(1)}, u32[]{:S(2)}, u32[]{:S(2)}) collective-permute-start(bf16[64,768]{1,0:T(8,128)(2,1)S(1)} %get-tuple-element.84), channel_id=1, source_target_pairs={{0,2},{1,3},{2,0},{3,1},{4,6},{5,7},{6,4},{7,5},{8,10},{9,11},{10,... | collective-permute-start | bytes 294920 | tf_op jit(solution)/shard_map/ppermute | solution.py:291
  57.0 6.5 %collective-permute-done.27.refs_6_ = bf16[128,384]{1,0:T(8,128)(2,1)S(1)} collective-permute-done((bf16[128,384]{1,0:T(8,128)(2,1)S(1)}, bf16[128,384]{1,0:T(8,128)(2,1)S(1)}, u32[]{:S(2)}, u32[]{:S(2)}) %collective-permute-start.27) | collective-permute-done | bytes 98336 | tf_op jit(solution)/shard_map/ppermute | solution.py:291
  63.5 2.4 %collective-permute-start.18 = (bf16[64,768]{1,0:T(8,128)(2,1)S(1)}, bf16[64,768]{1,0:T(8,128)(2,1)S(1)}, u32[]{:S(2)}, u32[]{:S(2)}) collective-permute-start(bf16[64,768]{1,0:T(8,128)(2,1)S(1)} %get-tuple-element.85), channel_id=1, source_target_pairs={{0,3},{1,2},{2,1},{3,0},{4,7},{5,6},{6,5},{7,4},{8,11},{9,10},{10,... | collective-permute-start | bytes 294920 | tf_op jit(solution)/shard_map/ppermute | solution.py:291
  66.0 3.6 %collective-permute-done.18.refs_3_ = bf16[64,768]{1,0:T(8,128)(2,1)S(1)} collective-permute-done((bf16[64,768]{1,0:T(8,128)(2,1)S(1)}, bf16[64,768]{1,0:T(8,128)(2,1)S(1)}, u32[]{:S(2)}, u32[]{:S(2)}) %collective-permute-start.18) | collective-permute-done | bytes 98336 | tf_op jit(solution)/shard_map/ppermute | solution.py:291
  69.6 1.0 %combine.7 = bf16[128,768]{1,0:T(8,128)(2,1)} custom-call(bf16[256,256]{1,0:T(8,128)(2,1)S(1)} %get-tuple-element.50.pick_ref, f32[128,2]{1,0:T(8,128)S(1)} %get-tuple-element.51.mix_ref, bf16[64,768]{1,0:T(8,128)(2,1)S(1)} %get-tuple-element.82.refs_0_, bf16[64,768]{1,0:T(8,128)(2,1)S(1)} %collective-permute-done.16.refs_1_, ...), custom_call_target="tpu_custom_call" | custom-call | flops 100663296 | bytes 589824 | tf_op jit(solution)/shard_map/combine/pallas_call | solution.py:258
  (39 shorter events, 0.8 us)
Async XLA Ops:
  0.0 8.2 %collective-permute-start = (bf16[128,768]{1,0:T(8,128)(2,1)}, bf16[128,768]{1,0:T(8,128)(2,1)S(1)}, u32[]{:S(2)}, u32[]{:S(2)}) collective-permute-start(bf16[128,768]{1,0:T(8,128)(2,1)} %refs_0_.4), channel_id=1, source_target_pairs={{0,8},{4,12},{8,0},{12,4},{1,9},{5,13},{9,1},{13,5},{2,10},{6,14},... | collective-permute-start | bytes 589832 | tf_op jit(solution)/shard_map/ppermute | solution.py:291
  0.1 13.3 %collective-permute-start.5 = (bf16[128,768]{1,0:T(8,128)(2,1)}, bf16[128,768]{1,0:T(8,128)(2,1)S(1)}, u32[]{:S(2)}, u32[]{:S(2)}) collective-permute-start(bf16[128,768]{1,0:T(8,128)(2,1)} %refs_0_.4), channel_id=1, source_target_pairs={{0,4},{4,0},{8,12},{12,8},{1,5},{5,1},{9,13},{13,9},{2,6},{6,2},{1... | collective-permute-start | bytes 589832 | tf_op jit(solution)/shard_map/ppermute | solution.py:291
  1.4 0.7 copy-start.1
  2.0 0.7 copy-start.2
  2.9 10.4 %copy-start = (bf16[128,768]{1,0:T(8,128)(2,1)S(1)}, bf16[128,768]{1,0:T(8,128)(2,1)}, u32[]{:S(2)}) copy-start(bf16[128,768]{1,0:T(8,128)(2,1)} %refs_0_.4) | copy-start | bytes 589828
  8.2 13.5 %collective-permute-start.1 = (bf16[128,768]{1,0:T(8,128)(2,1)S(1)}, bf16[128,768]{1,0:T(8,128)(2,1)S(1)}, u32[]{:S(2)}, u32[]{:S(2)}) collective-permute-start(bf16[128,768]{1,0:T(8,128)(2,1)S(1)} %collective-permute-done.refs_0_), channel_id=1, source_target_pairs={{0,4},{4,0},{8,12},{12,8},{1,5},{5,1},{9,13},{13,9},{2,6},{6,2},{1... | collective-permute-start | bytes 589832 | tf_op jit(solution)/shard_map/ppermute | solution.py:291
  13.7 10.4 %collective-permute-start.10 = (bf16[64,1536]{1,0:T(8,128)(2,1)S(1)}, bf16[64,1536]{1,0:T(8,128)(2,1)S(1)}, u32[]{:S(2)}, u32[]{:S(2)}) collective-permute-start(bf16[64,1536]{1,0:T(8,128)(2,1)S(1)} %get-tuple-element.68), channel_id=1, source_target_pairs={{0,2},{1,3},{2,0},{3,1},{4,6},{5,7},{6,4},{7,5},{8,10},{9,11},{10,... | collective-permute-start | bytes 589832 | tf_op jit(solution)/shard_map/ppermute | solution.py:291
  15.0 10.0 %collective-permute-start.11 = (bf16[64,1536]{1,0:T(8,128)(2,1)S(1)}, bf16[64,1536]{1,0:T(8,128)(2,1)S(1)}, u32[]{:S(2)}, u32[]{:S(2)}) collective-permute-start(bf16[64,1536]{1,0:T(8,128)(2,1)S(1)} %get-tuple-element.69), channel_id=1, source_target_pairs={{0,3},{1,2},{2,1},{3,0},{4,7},{5,6},{6,5},{7,4},{8,11},{9,10},{10,... | collective-permute-start | bytes 589832 | tf_op jit(solution)/shard_map/ppermute | solution.py:291
  16.2 10.0 %collective-permute-start.9 = (bf16[64,1536]{1,0:T(8,128)(2,1)S(1)}, bf16[64,1536]{1,0:T(8,128)(2,1)S(1)}, u32[]{:S(2)}, u32[]{:S(2)}) collective-permute-start(bf16[64,1536]{1,0:T(8,128)(2,1)S(1)} %get-tuple-element.67), channel_id=1, source_target_pairs={{0,1},{1,0},{2,3},{3,2},{4,5},{5,4},{6,7},{7,6},{8,9},{9,8},{10,11... | collective-permute-start | bytes 589832 | tf_op jit(solution)/shard_map/ppermute | solution.py:291
  21.1 2.1 %collective-permute-start.6 = (bf16[64,768]{1,0:T(8,128)(2,1)S(1)}, bf16[64,768]{1,0:T(8,128)(2,1)S(1)}, u32[]{:S(2)}, u32[]{:S(2)}) collective-permute-start(bf16[64,768]{1,0:T(8,128)(2,1)S(1)} %get-tuple-element.62), channel_id=1, source_target_pairs={{0,1},{1,0},{2,3},{3,2},{4,5},{5,4},{6,7},{7,6},{8,9},{9,8},{10,11... | collective-permute-start | bytes 294920 | tf_op jit(solution)/shard_map/ppermute | solution.py:291
  21.7 8.1 %collective-permute-start.7 = (bf16[64,768]{1,0:T(8,128)(2,1)S(1)}, bf16[64,768]{1,0:T(8,128)(2,1)S(1)}, u32[]{:S(2)}, u32[]{:S(2)}) collective-permute-start(bf16[64,768]{1,0:T(8,128)(2,1)S(1)} %get-tuple-element.63), channel_id=1, source_target_pairs={{0,2},{1,3},{2,0},{3,1},{4,6},{5,7},{6,4},{7,5},{8,10},{9,11},{10,... | collective-permute-start | bytes 294920 | tf_op jit(solution)/shard_map/ppermute | solution.py:291
  23.2 6.6 %collective-permute-start.8 = (bf16[64,768]{1,0:T(8,128)(2,1)S(1)}, bf16[64,768]{1,0:T(8,128)(2,1)S(1)}, u32[]{:S(2)}, u32[]{:S(2)}) collective-permute-start(bf16[64,768]{1,0:T(8,128)(2,1)S(1)} %get-tuple-element.64), channel_id=1, source_target_pairs={{0,3},{1,2},{2,1},{3,0},{4,7},{5,6},{6,5},{7,4},{8,11},{9,10},{10,... | collective-permute-start | bytes 294920 | tf_op jit(solution)/shard_map/ppermute | solution.py:291
  24.1 7.9 %collective-permute-start.2 = (bf16[64,768]{1,0:T(8,128)(2,1)S(1)}, bf16[64,768]{1,0:T(8,128)(2,1)S(1)}, u32[]{:S(2)}, u32[]{:S(2)}) collective-permute-start(bf16[64,768]{1,0:T(8,128)(2,1)S(1)} %get-tuple-element.54), channel_id=1, source_target_pairs={{0,1},{1,0},{2,3},{3,2},{4,5},{5,4},{6,7},{7,6},{8,9},{9,8},{10,11... | collective-permute-start | bytes 294920 | tf_op jit(solution)/shard_map/ppermute | solution.py:291
  25.0 7.0 %collective-permute-start.3 = (bf16[64,768]{1,0:T(8,128)(2,1)S(1)}, bf16[64,768]{1,0:T(8,128)(2,1)S(1)}, u32[]{:S(2)}, u32[]{:S(2)}) collective-permute-start(bf16[64,768]{1,0:T(8,128)(2,1)S(1)} %get-tuple-element.55), channel_id=1, source_target_pairs={{0,2},{1,3},{2,0},{3,1},{4,6},{5,7},{6,4},{7,5},{8,10},{9,11},{10,... | collective-permute-start | bytes 294920 | tf_op jit(solution)/shard_map/ppermute | solution.py:291
  26.2 6.8 %collective-permute-start.4 = (bf16[64,768]{1,0:T(8,128)(2,1)S(1)}, bf16[64,768]{1,0:T(8,128)(2,1)S(1)}, u32[]{:S(2)}, u32[]{:S(2)}) collective-permute-start(bf16[64,768]{1,0:T(8,128)(2,1)S(1)} %get-tuple-element.56), channel_id=1, source_target_pairs={{0,3},{1,2},{2,1},{3,0},{4,7},{5,6},{6,5},{7,4},{8,11},{9,10},{10,... | collective-permute-start | bytes 294920 | tf_op jit(solution)/shard_map/ppermute | solution.py:291
  29.8 5.3 %slice-start = ((s8[12582912]{0:T(1024)(128)(4,1)}), s8[4194304]{0:T(1024)(128)(4,1)S(1)}, s32[]{:S(2)}) async-start(s8[12582912]{0:T(1024)(128)(4,1)} %bitcast.4), calls=%async_computation | async-start | bytes 8388608
  29.9 5.3 %slice-start.1 = ((s8[12582912]{0:T(1024)(128)(4,1)}), s8[4194304]{0:T(1024)(128)(4,1)S(1)}, s32[]{:S(2)}) async-start(s8[12582912]{0:T(1024)(128)(4,1)} %bitcast.4), calls=%async_computation.1 | async-start | bytes 8388608
  33.0 2.3 %slice-start.2 = ((s8[12582912]{0:T(1024)(128)(4,1)}), s8[4194304]{0:T(1024)(128)(4,1)S(1)}, s32[]{:S(2)}) async-start(s8[12582912]{0:T(1024)(128)(4,1)} %bitcast.4), calls=%async_computation.2 | async-start | bytes 8388608
  36.3 4.6 %collective-permute-start.12 = (bf16[64,768]{1,0:T(8,128)(2,1)S(1)}, bf16[64,768]{1,0:T(8,128)(2,1)S(1)}, u32[]{:S(2)}, u32[]{:S(2)}) collective-permute-start(bf16[64,768]{1,0:T(8,128)(2,1)S(1)} %get-tuple-element.78), channel_id=1, source_target_pairs={{0,1},{1,0},{2,3},{3,2},{4,5},{5,4},{6,7},{7,6},{8,9},{9,8},{10,11... | collective-permute-start | bytes 294920 | tf_op jit(solution)/shard_map/ppermute | solution.py:291
  36.7 5.1 %collective-permute-start.13 = (bf16[64,768]{1,0:T(8,128)(2,1)S(1)}, bf16[64,768]{1,0:T(8,128)(2,1)S(1)}, u32[]{:S(2)}, u32[]{:S(2)}) collective-permute-start(bf16[64,768]{1,0:T(8,128)(2,1)S(1)} %get-tuple-element.79), channel_id=1, source_target_pairs={{0,2},{1,3},{2,0},{3,1},{4,6},{5,7},{6,4},{7,5},{8,10},{9,11},{10,... | collective-permute-start | bytes 294920 | tf_op jit(solution)/shard_map/ppermute | solution.py:291
  38.0 6.0 %collective-permute-start.14 = (bf16[64,768]{1,0:T(8,128)(2,1)S(1)}, bf16[64,768]{1,0:T(8,128)(2,1)S(1)}, u32[]{:S(2)}, u32[]{:S(2)}) collective-permute-start(bf16[64,768]{1,0:T(8,128)(2,1)S(1)} %get-tuple-element.80), channel_id=1, source_target_pairs={{0,3},{1,2},{2,1},{3,0},{4,7},{5,6},{6,5},{7,4},{8,11},{9,10},{10,... | collective-permute-start | bytes 294920 | tf_op jit(solution)/shard_map/ppermute | solution.py:291
  39.6 5.9 %collective-permute-start.23 = (bf16[64,768]{1,0:T(8,128)(2,1)S(1)}, bf16[64,768]{1,0:T(8,128)(2,1)S(1)}, u32[]{:S(2)}, u32[]{:S(2)}) collective-permute-start(bf16[64,768]{1,0:T(8,128)(2,1)S(1)} %get-tuple-element.91), channel_id=1, source_target_pairs={{0,1},{1,0},{2,3},{3,2},{4,5},{5,4},{6,7},{7,6},{8,9},{9,8},{10,11... | collective-permute-start | bytes 294920 | tf_op jit(solution)/shard_map/ppermute | solution.py:291
  39.7 7.0 %collective-permute-start.24 = (bf16[64,768]{1,0:T(8,128)(2,1)S(1)}, bf16[64,768]{1,0:T(8,128)(2,1)S(1)}, u32[]{:S(2)}, u32[]{:S(2)}) collective-permute-start(bf16[64,768]{1,0:T(8,128)(2,1)S(1)} %get-tuple-element.92), channel_id=1, source_target_pairs={{0,2},{1,3},{2,0},{3,1},{4,6},{5,7},{6,4},{7,5},{8,10},{9,11},{10,... | collective-permute-start | bytes 294920 | tf_op jit(solution)/shard_map/ppermute | solution.py:291
  40.9 6.9 %collective-permute-start.25 = (bf16[64,768]{1,0:T(8,128)(2,1)S(1)}, bf16[64,768]{1,0:T(8,128)(2,1)S(1)}, u32[]{:S(2)}, u32[]{:S(2)}) collective-permute-start(bf16[64,768]{1,0:T(8,128)(2,1)S(1)} %get-tuple-element.93), channel_id=1, source_target_pairs={{0,3},{1,2},{2,1},{3,0},{4,7},{5,6},{6,5},{7,4},{8,11},{9,10},{10,... | collective-permute-start | bytes 294920 | tf_op jit(solution)/shard_map/ppermute | solution.py:291
  44.2 4.8 %collective-permute-start.15 = (bf16[128,384]{1,0:T(8,128)(2,1)S(1)}, bf16[128,384]{1,0:T(8,128)(2,1)S(1)}, u32[]{:S(2)}, u32[]{:S(2)}) collective-permute-start(bf16[128,384]{1,0:T(8,128)(2,1)S(1)} %get-tuple-element.81.refs_0_), channel_id=1, source_target_pairs={{0,4},{4,0},{8,12},{12,8},{1,5},{5,1},{9,13},{13,9},{2,6},{6,2},{1... | collective-permute-start | bytes 294920 | tf_op jit(solution)/shard_map/ppermute | solution.py:291
  45.4 5.3 %collective-permute-start.19 = (bf16[64,768]{1,0:T(8,128)(2,1)S(1)}, bf16[64,768]{1,0:T(8,128)(2,1)S(1)}, u32[]{:S(2)}, u32[]{:S(2)}) collective-permute-start(bf16[64,768]{1,0:T(8,128)(2,1)S(1)} %get-tuple-element.87), channel_id=1, source_target_pairs={{0,1},{1,0},{2,3},{3,2},{4,5},{5,4},{6,7},{7,6},{8,9},{9,8},{10,11... | collective-permute-start | bytes 294920 | tf_op jit(solution)/shard_map/ppermute | solution.py:291
  45.4 5.2 %collective-permute-start.20 = (bf16[64,768]{1,0:T(8,128)(2,1)S(1)}, bf16[64,768]{1,0:T(8,128)(2,1)S(1)}, u32[]{:S(2)}, u32[]{:S(2)}) collective-permute-start(bf16[64,768]{1,0:T(8,128)(2,1)S(1)} %get-tuple-element.88), channel_id=1, source_target_pairs={{0,2},{1,3},{2,0},{3,1},{4,6},{5,7},{6,4},{7,5},{8,10},{9,11},{10,... | collective-permute-start | bytes 294920 | tf_op jit(solution)/shard_map/ppermute | solution.py:291
  46.7 5.5 %collective-permute-start.21 = (bf16[64,768]{1,0:T(8,128)(2,1)S(1)}, bf16[64,768]{1,0:T(8,128)(2,1)S(1)}, u32[]{:S(2)}, u32[]{:S(2)}) collective-permute-start(bf16[64,768]{1,0:T(8,128)(2,1)S(1)} %get-tuple-element.89), channel_id=1, source_target_pairs={{0,3},{1,2},{2,1},{3,0},{4,7},{5,6},{6,5},{7,4},{8,11},{9,10},{10,... | collective-permute-start | bytes 294920 | tf_op jit(solution)/shard_map/ppermute | solution.py:291
  49.3 20.2 %collective-permute-start.26 = (bf16[128,768]{1,0:T(8,128)(2,1)S(1)}, bf16[128,768]{1,0:T(8,128)(2,1)S(1)}, u32[]{:S(2)}, u32[]{:S(2)}) collective-permute-start(bf16[128,768]{1,0:T(8,128)(2,1)S(1)} %combine.6.after_ref), channel_id=1, source_target_pairs={{0,8},{4,12},{8,0},{12,4},{1,9},{5,13},{9,1},{13,5},{2,10},{6,14},... | collective-permute-start | bytes 589832 | tf_op jit(solution)/shard_map/ppermute | solution.py:291
  49.4 14.1 %collective-permute-start.27 = (bf16[128,384]{1,0:T(8,128)(2,1)S(1)}, bf16[128,384]{1,0:T(8,128)(2,1)S(1)}, u32[]{:S(2)}, u32[]{:S(2)}) collective-permute-start(bf16[128,384]{1,0:T(8,128)(2,1)S(1)} %hold.1), channel_id=1, source_target_pairs={{0,12},{4,8},{8,4},{12,0},{1,13},{5,9},{9,5},{13,1},{2,14},{6,10},... | collective-permute-start | bytes 294920 | tf_op jit(solution)/shard_map/ppermute | solution.py:291
  52.5 17.1 %collective-permute-start.22 = (bf16[128,768]{1,0:T(8,128)(2,1)S(1)}, bf16[128,768]{1,0:T(8,128)(2,1)S(1)}, u32[]{:S(2)}, u32[]{:S(2)}) collective-permute-start(bf16[128,768]{1,0:T(8,128)(2,1)S(1)} %combine.5), channel_id=1, source_target_pairs={{0,4},{4,0},{8,12},{12,8},{1,5},{5,1},{9,13},{13,9},{2,6},{6,2},{1... | collective-permute-start | bytes 589832 | tf_op jit(solution)/shard_map/ppermute | solution.py:291
  55.0 11.0 %collective-permute-start.16 = (bf16[64,768]{1,0:T(8,128)(2,1)S(1)}, bf16[64,768]{1,0:T(8,128)(2,1)S(1)}, u32[]{:S(2)}, u32[]{:S(2)}) collective-permute-start(bf16[64,768]{1,0:T(8,128)(2,1)S(1)} %get-tuple-element.83), channel_id=1, source_target_pairs={{0,1},{1,0},{2,3},{3,2},{4,5},{5,4},{6,7},{7,6},{8,9},{9,8},{10,11... | collective-permute-start | bytes 294920 | tf_op jit(solution)/shard_map/ppermute | solution.py:291
  55.8 10.1 %collective-permute-start.17 = (bf16[64,768]{1,0:T(8,128)(2,1)S(1)}, bf16[64,768]{1,0:T(8,128)(2,1)S(1)}, u32[]{:S(2)}, u32[]{:S(2)}) collective-permute-start(bf16[64,768]{1,0:T(8,128)(2,1)S(1)} %get-tuple-element.84), channel_id=1, source_target_pairs={{0,2},{1,3},{2,0},{3,1},{4,6},{5,7},{6,4},{7,5},{8,10},{9,11},{10,... | collective-permute-start | bytes 294920 | tf_op jit(solution)/shard_map/ppermute | solution.py:291
  63.5 6.0 %collective-permute-start.18 = (bf16[64,768]{1,0:T(8,128)(2,1)S(1)}, bf16[64,768]{1,0:T(8,128)(2,1)S(1)}, u32[]{:S(2)}, u32[]{:S(2)}) collective-permute-start(bf16[64,768]{1,0:T(8,128)(2,1)S(1)} %get-tuple-element.85), channel_id=1, source_target_pairs={{0,3},{1,2},{2,1},{3,0},{4,7},{5,6},{6,5},{7,4},{8,11},{9,10},{10,... | collective-permute-start | bytes 294920 | tf_op jit(solution)/shard_map/ppermute | solution.py:291

commit v14 on v12

--- a/solution.py
+++ b/solution.py
@@ -203,40 +203,44 @@
     )(*x_blocks, *pinned(weights), *old, *after)
 
 
-def down_kernel(column_ref, h_ref, w_ref, *refs, part, waits):
+def down_kernel(column_ref, h_ref, w_ref, *refs, parts, waits):
     out_refs = refs[waits:]
-    capacity, width = out_refs[0].shape
+    capacity, wide = out_refs[0].shape
+    width = wide // len(parts)
     tile = min(256, width)
-    for n in range(width // tile):
-        start = pl.multiple_of(part(column_ref[0]) * width + n * tile, tile)
-        y = jnp.dot(h_ref[...], w_ref[0, :, pl.ds(start, tile)], preferred_element_type=F32)
-        columns = slice(n * tile, (n + 1) * tile)
-        for d, out in enumerate(out_refs):
-            out[:, columns] = y[d * capacity : (d + 1) * capacity].astype(BF16)
-
-
-def down(column, part, hidden, down_w, width, experts, after):
+    for i, part in enumerate(parts):
+        for n in range(width // tile):
+            start = pl.multiple_of(part(column_ref[0]) * width + n * tile, tile)
+            y = jnp.dot(h_ref[...], w_ref[0, :, pl.ds(start, tile)], preferred_element_type=F32)
+            columns = slice(i * width + n * tile, i * width + (n + 1) * tile)
+            for d, out in enumerate(out_refs):
+                out[:, columns] = y[d * capacity : (d + 1) * capacity].astype(BF16)
+
+
+def down(column, parts, hidden, down_w, width, experts, after):
     rows, depth = hidden.shape
     capacity = rows // experts
-    return pl.pallas_call(
-        functools.partial(down_kernel, part=part, waits=len(after)),
-        out_shape=[jax.ShapeDtypeStruct((capacity, width), BF16)] * experts,
+    wide = width * len(parts)
+    return pl.pallas_call(
+        functools.partial(down_kernel, parts=parts, waits=len(after)),
+        out_shape=[jax.ShapeDtypeStruct((capacity, wide), BF16)] * experts,
         in_specs=[pl.BlockSpec(memory_space=pltpu.SMEM)]
         + [pl.BlockSpec(memory_space=pltpu.VMEM)] * 2
         + [pl.BlockSpec(memory_space=pl.ANY)] * len(after),
         out_specs=[pl.BlockSpec(memory_space=pltpu.VMEM)] * experts,
-        cost_estimate=cost(2 * rows * depth * width, 2 * depth * width + 2 * rows * width),
+        cost_estimate=cost(2 * rows * depth * wide, 2 * depth * wide + 2 * rows * wide),
         compiler_params=params(),
         name="down",
     )(column.reshape(1), *pinned([hidden, down_w]), *after)
 
 
-def combine_kernel(pick_ref, mix_ref, *refs, experts, starts):
+def combine_kernel(pick_ref, mix_ref, *refs, experts, starts, index):
     y_refs, added = refs[:experts], refs[experts : experts + len(starts)]
     outs = refs[experts + len(starts) :]
-    width = y_refs[0].shape[1]
     rows, part = outs[0].shape
-    y = jnp.concatenate([r[...] for r in y_refs], axis=0)
+    width = part * len(outs)
+    columns = slice(index * width, (index + 1) * width)
+    y = jnp.concatenate([r[:, columns] for r in y_refs], axis=0)
     picked = lax.dot_general(
         pick_ref[...], y, (((0,), (0,)), ((), ())), preferred_element_type=F32
     )
@@ -251,13 +255,16 @@
         out[...] = mixed[:, i * part : (i + 1) * part].astype(BF16)
 
 
-def combine(pick, mix, blocks, added, cuts=1):
+def combine(pick, mix, blocks, added, cuts=1, slices=1, index=0):
     rows = mix.shape[0]
-    width = blocks[0].shape[1]
+    width = blocks[0].shape[1] // slices
     operands = 2 + len(blocks) + len(added)
     return pl.pallas_call(
         functools.partial(
-            combine_kernel, experts=len(blocks), starts=[start for _, start in added]
+            combine_kernel,
+            experts=len(blocks),
+            starts=[start for _, start in added],
+            index=index,
         ),
         out_shape=[jax.ShapeDtypeStruct((rows, width // cuts), BF16)] * cuts,
         in_specs=[pl.BlockSpec(memory_space=pltpu.VMEM)] * operands,
@@ -314,21 +321,21 @@
         sums = gate_up(x_blocks, chosen, sums, group is groups[-1], after)
     hidden = sums[0]
 
-    def returned(part, after=()):
-        terms = down(column, part, hidden, down_weight, width, experts, after)
+    def returned(parts, after=()):
+        terms = down(column, parts, hidden, down_weight, width, experts, after)
         return [swap(block, "expert", e) for e, block in enumerate(terms)]
 
     if not doubling:
-        mixed = combine(pick, mix, returned(everything), [])[0]
+        mixed = combine(pick, mix, returned([everything]), [])[0]
         return lax.psum_scatter(mixed, "tensor", scatter_dimension=1, tiled=True)
-    low, high = combine(pick, mix, returned(across(3)), [], cuts=2)
+    low, high = combine(pick, mix, returned([across(3)]), [], cuts=2)
     passed = swap(low, "tensor", 1)
     far = (swap(high, "tensor", 3), width // 2)
-    onwards = combine(pick, mix, returned(across(2)), [(passed, 0)])[0]
+    pair = returned([across(2), across(1)])
+    onwards = combine(pick, mix, pair, [(passed, 0)], slices=2)[0]
     over = (swap(onwards, "tensor", 2), 0)
-    near = combine(pick, mix, returned(across(1), [low]), [])[0]
-    beside = (swap(near, "tensor", 1), 0)
-    return combine(pick, mix, returned(across(0), [passed]), [beside, over, far])[0]
+    beside = (swap(combine(pick, mix, pair, [], slices=2, index=1)[0], "tensor", 1), 0)
+    return combine(pick, mix, returned([across(0)], [passed]), [beside, over, far])[0]
 
 
 def solution(mesh):

time: 66.4 us -> 68.2 us (1.027)
  waiting for transfers between devices: 12.1 us -> 14.8 us
  starting transfers between devices: 28.2 us -> 27.4 us
    ppermute x28 -> x25, waiting for transfers between devices: 12.1 us -> 14.8 us  [swap(): return lax.ppermute(value, axis, [(i, i ^ distance) for i in range(count)])]
    ppermute x28 -> x25, starting transfers between devices: 28.2 us -> 27.4 us  [swap(): return lax.ppermute(value, axis, [(i, i ^ distance) for i in range(count)])]
    pallas_call x4 -> x3, Pallas kernels: 4.1 us -> 3.92 us  [down(): pl.pallas_call(functools.partial(down_kernel, parts=parts, waits=len(afte...]
  transfers between devices with their start and end apart: 28 -> 25, of which waited for: 8 -> 11; matrix products, arithmetic and copies ran while one was open for 0% -> 0% of each run, Pallas kernels for 30% -> 29%
where the time goes in v14:
time: 68.2 us; the launch traced here: 68.1 us
  starting transfers between devices  27.4 us (40%)
  Pallas kernels  24 us (35%)
  waiting for transfers between devices  14.8 us (22%)
  local copies, waits for them, and re-layouts  1.54 us (2%)
    ppermute x25, starting transfers between devices, swap(): return lax.ppermute(value, axis, [(i, i ^ distance) for i in range(count)])  27.4 us
    ppermute x25, waiting for transfers between devices, swap(): return lax.ppermute(value, axis, [(i, i ^ distance) for i in range(count)])  14.8 us
    pallas_call x2, Pallas kernels, prefetch(): pl.pallas_call(functools.partial(prefetch_kernel, parts=[part for _, part...  9.41 us
    pallas_call x3, Pallas kernels, gate_up(): pl.pallas_call(functools.partial(gate_up_kernel, experts=experts, slices=...  7.71 us
    pallas_call x3, Pallas kernels, down(): pl.pallas_call(functools.partial(down_kernel, parts=parts, waits=len(afte...  3.92 us
    pallas_call x4, Pallas kernels, combine(): pl.pallas_call(functools.partial(combine_kernel, experts=len(blocks), sta...  1.93 us
    unnamed x12, local copies, waits for them, and re-layouts  1.54 us
  transfers between devices with their start and end apart: 25, of which 11 were waited for; matrix products, arithmetic and copies ran while one was open for 0% of the time, Pallas kernels for 29%

profile of v14, /device:TPU:0, one launch (start us, length us, event | category | flops | bytes accessed | tf_op | source)
XLA Modules:
  0.0 68.1 jit_solution(405892524234641411)
XLA Ops:
  0.0 4.0 %collective-permute-start = (bf16[128,768]{1,0:T(8,128)(2,1)}, bf16[128,768]{1,0:T(8,128)(2,1)S(1)}, u32[]{:S(2)}, u32[]{:S(2)}) collective-permute-start(bf16[128,768]{1,0:T(8,128)(2,1)} %refs_0_.4), channel_id=1, source_target_pairs={{0,8},{4,12},{8,0},{12,4},{1,9},{5,13},{9,1},{13,5},{2,10},{6,14},... | collective-permute-start | bytes 589832 | tf_op jit(solution)/shard_map/ppermute | solution.py:282
  4.0 1.6 %collective-permute-start.5 = (bf16[128,768]{1,0:T(8,128)(2,1)}, bf16[128,768]{1,0:T(8,128)(2,1)S(1)}, u32[]{:S(2)}, u32[]{:S(2)}) collective-permute-start(bf16[128,768]{1,0:T(8,128)(2,1)} %refs_0_.4), channel_id=1, source_target_pairs={{0,4},{4,0},{8,12},{12,8},{1,5},{5,1},{9,13},{13,9},{2,6},{6,2},{1... | collective-permute-start | bytes 589832 | tf_op jit(solution)/shard_map/ppermute | solution.py:282
  5.6 0.7 copy-done.1
  6.3 0.7 copy-done.2
  7.0 0.2 routing.1
  7.2 4.7 %prefetch.2 = (bf16[768,2048]{1,0:T(8,128)(2,1)S(1)}, bf16[768,2048]{1,0:T(8,128)(2,1)S(1)}, bf16[768,2048]{1,0:T(8,128)(2,1)S(1)}, bf16[768,2048]{1,0:T(8,128)(2,1)S(1)}) custom-call(s32[1]{0:T(128)} %bitcast.3.column_ref, bf16[256,128]{1,0:T(8,128)(2,1)S(1)} %get-tuple-element.48.placed_ref.after_ref, bf16[1,3072,2048]{2,1,0:T(8,128)(2,1)} %refs_2_.3, ...), custom_call_target="tpu_custom_call" | custom-call | bytes 12582912 | tf_op jit(solution)/shard_map/prefetch/pallas_call | solution.py:127
  11.9 1.6 %collective-permute-done.refs_0_ = bf16[128,768]{1,0:T(8,128)(2,1)S(1)} collective-permute-done((bf16[128,768]{1,0:T(8,128)(2,1)}, bf16[128,768]{1,0:T(8,128)(2,1)S(1)}, u32[]{:S(2)}, u32[]{:S(2)}) %collective-permute-start) | collective-permute-done | bytes 196640 | tf_op jit(solution)/shard_map/ppermute | solution.py:282
  13.5 0.7 %collective-permute-start.1 = (bf16[128,768]{1,0:T(8,128)(2,1)S(1)}, bf16[128,768]{1,0:T(8,128)(2,1)S(1)}, u32[]{:S(2)}, u32[]{:S(2)}) collective-permute-start(bf16[128,768]{1,0:T(8,128)(2,1)S(1)} %collective-permute-done.refs_0_), channel_id=1, source_target_pairs={{0,4},{4,0},{8,12},{12,8},{1,5},{5,1},{9,13},{13,9},{2,6},{6,2},{1... | collective-permute-start | bytes 589832 | tf_op jit(solution)/shard_map/ppermute | solution.py:282
  14.2 0.4 dispatch.4
  14.6 1.6 %collective-permute-start.10 = (bf16[64,1536]{1,0:T(8,128)(2,1)S(1)}, bf16[64,1536]{1,0:T(8,128)(2,1)S(1)}, u32[]{:S(2)}, u32[]{:S(2)}) collective-permute-start(bf16[64,1536]{1,0:T(8,128)(2,1)S(1)} %get-tuple-element.64), channel_id=1, source_target_pairs={{0,2},{1,3},{2,0},{3,1},{4,6},{5,7},{6,4},{7,5},{8,10},{9,11},{10,... | collective-permute-start | bytes 589832 | tf_op jit(solution)/shard_map/ppermute | solution.py:282
  16.1 0.6 collective-permute-start.9
  16.8 4.7 %prefetch.3 = (bf16[768,2048]{1,0:T(8,128)(2,1)S(1)}, bf16[768,2048]{1,0:T(8,128)(2,1)S(1)}, bf16[768,2048]{1,0:T(8,128)(2,1)S(1)}, bf16[768,2048]{1,0:T(8,128)(2,1)S(1)}) custom-call(s32[1]{0:T(128)} %bitcast.3.column_ref, bf16[64,1536]{1,0:T(8,128)(2,1)S(1)} %get-tuple-element.54.after_ref.refs_0_, bf16[1,3072,2048]{2,1,0:T(8,128)(2,1)} %refs_2_.3, ...), custom_call_target="tpu_custom_call" | custom-call | bytes 12582912 | tf_op jit(solution)/shard_map/prefetch/pallas_call | solution.py:127
  21.5 0.3 dispatch.5
  21.8 1.6 %collective-permute-start.7 = (bf16[64,768]{1,0:T(8,128)(2,1)S(1)}, bf16[64,768]{1,0:T(8,128)(2,1)S(1)}, u32[]{:S(2)}, u32[]{:S(2)}) collective-permute-start(bf16[64,768]{1,0:T(8,128)(2,1)S(1)} %get-tuple-element.59), channel_id=1, source_target_pairs={{0,2},{1,3},{2,0},{3,1},{4,6},{5,7},{6,4},{7,5},{8,10},{9,11},{10,... | collective-permute-start | bytes 294920 | tf_op jit(solution)/shard_map/ppermute | solution.py:282
  23.4 0.3 dispatch.3
  23.7 0.7 %collective-permute-start.8 = (bf16[64,768]{1,0:T(8,128)(2,1)S(1)}, bf16[64,768]{1,0:T(8,128)(2,1)S(1)}, u32[]{:S(2)}, u32[]{:S(2)}) collective-permute-start(bf16[64,768]{1,0:T(8,128)(2,1)S(1)} %get-tuple-element.60), channel_id=1, source_target_pairs={{0,3},{1,2},{2,1},{3,0},{4,7},{5,6},{6,5},{7,4},{8,11},{9,10},{10,... | collective-permute-start | bytes 294920 | tf_op jit(solution)/shard_map/ppermute | solution.py:282
  24.4 0.4 collective-permute-start.2
  24.8 1.1 %collective-permute-start.3 = (bf16[64,768]{1,0:T(8,128)(2,1)S(1)}, bf16[64,768]{1,0:T(8,128)(2,1)S(1)}, u32[]{:S(2)}, u32[]{:S(2)}) collective-permute-start(bf16[64,768]{1,0:T(8,128)(2,1)S(1)} %get-tuple-element.51), channel_id=1, source_target_pairs={{0,2},{1,3},{2,0},{3,1},{4,6},{5,7},{6,4},{7,5},{8,10},{9,11},{10,... | collective-permute-start | bytes 294920 | tf_op jit(solution)/shard_map/ppermute | solution.py:282
  25.9 1.1 %collective-permute-start.4 = (bf16[64,768]{1,0:T(8,128)(2,1)S(1)}, bf16[64,768]{1,0:T(8,128)(2,1)S(1)}, u32[]{:S(2)}, u32[]{:S(2)}) collective-permute-start(bf16[64,768]{1,0:T(8,128)(2,1)S(1)} %get-tuple-element.52), channel_id=1, source_target_pairs={{0,3},{1,2},{2,1},{3,0},{4,7},{5,6},{6,5},{7,4},{8,11},{9,10},{10,... | collective-permute-start | bytes 294920 | tf_op jit(solution)/shard_map/ppermute | solution.py:282
  27.0 3.5 %gate_up.3 = (f32[256,2048]{1,0:T(8,128)S(1)}, f32[256,2048]{1,0:T(8,128)S(1)}) custom-call(bf16[64,1536]{1,0:T(8,128)(2,1)S(1)} %get-tuple-element.54.after_ref.refs_0_, bf16[64,1536]{1,0:T(8,128)(2,1)S(1)} %collective-permute-done.9.refs_1_, bf16[64,1536]{1,0:T(8,128)(2,1)S(1)} %collective-permute-done.10.refs_2_, ...), custom_call_target="tpu_custom_call" | custom-call | flops 3221225472 | bytes 12582912 | tf_op jit(solution)/shard_map/gate_up/pallas_call | solution.py:183
  30.5 2.1 %gate_up.4 = (f32[256,2048]{1,0:T(8,128)S(1)}, f32[256,2048]{1,0:T(8,128)S(1)}) custom-call(bf16[64,768]{1,0:T(8,128)(2,1)S(1)} %get-tuple-element.57.refs_0_, bf16[64,768]{1,0:T(8,128)(2,1)S(1)} %collective-permute-done.6.refs_8_.refs_1_, bf16[64,768]{1,0:T(8,128)(2,1)S(1)} %collective-permute-done.7.refs_2_, ...), custom_call_target="tpu_custom_call", output_to_operand_aliasing={{0}: (6, {}), {1}: (7, {})} | custom-call | flops 1610612736 | bytes 6291456 | tf_op jit(solution)/shard_map/gate_up/pallas_call | solution.py:183
  32.6 0.8 %collective-permute-done.4.refs_3_ = bf16[64,768]{1,0:T(8,128)(2,1)S(1)} collective-permute-done((bf16[64,768]{1,0:T(8,128)(2,1)S(1)}, bf16[64,768]{1,0:T(8,128)(2,1)S(1)}, u32[]{:S(2)}, u32[]{:S(2)}) %collective-permute-start.4) | collective-permute-done | bytes 98336 | tf_op jit(solution)/shard_map/ppermute | solution.py:282
  33.4 2.1 %gate_up.5.h_ref = bf16[256,2048]{1,0:T(8,128)(2,1)S(1)} custom-call(bf16[64,768]{1,0:T(8,128)(2,1)S(1)} %get-tuple-element.49.refs_0_, bf16[64,768]{1,0:T(8,128)(2,1)S(1)} %collective-permute-done.2.refs_1_, bf16[64,768]{1,0:T(8,128)(2,1)S(1)} %collective-permute-done.3.refs_2_, bf16[64,768]{1,0:T(8,128)(2,1)S(1)} %collective-permute-done.4.refs_3_, ...), custom_call_target="tpu_custom_call" | custom-call | flops 1610612736 | bytes 6291456 | tf_op jit(solution)/shard_map/gate_up/pallas_call | solution.py:183
  35.7 1.0 %down.3 = (bf16[64,768]{1,0:T(8,128)(2,1)S(1)}, bf16[64,768]{1,0:T(8,128)(2,1)S(1)}, bf16[64,768]{1,0:T(8,128)(2,1)S(1)}, bf16[64,768]{1,0:T(8,128)(2,1)S(1)}) custom-call(s32[1]{0:T(128)} %bitcast.3.column_ref, bf16[256,2048]{1,0:T(8,128)(2,1)S(1)} %gate_up.5.h_ref, bf16[1,2048,3072]{2,1,0:T(8,128)(2,1)S(1)} %bitcast.5), custom_call_target="tpu_custom_call" | custom-call | flops 805306368 | bytes 3538944 | tf_op jit(solution)/shard_map/down/pallas_call | solution.py:224
  36.8 0.2 collective-permute-start.12
  37.0 1.4 %collective-permute-start.13 = (bf16[64,768]{1,0:T(8,128)(2,1)S(1)}, bf16[64,768]{1,0:T(8,128)(2,1)S(1)}, u32[]{:S(2)}, u32[]{:S(2)}) collective-permute-start(bf16[64,768]{1,0:T(8,128)(2,1)S(1)} %get-tuple-element.75), channel_id=1, source_target_pairs={{0,2},{1,3},{2,0},{3,1},{4,6},{5,7},{6,4},{7,5},{8,10},{9,11},{10,... | collective-permute-start | bytes 294920 | tf_op jit(solution)/shard_map/ppermute | solution.py:282
  38.4 0.3 collective-permute-start.14
  38.7 1.8 %down.5 = (bf16[64,1536]{1,0:T(8,128)(2,1)S(1)}, bf16[64,1536]{1,0:T(8,128)(2,1)S(1)}, bf16[64,1536]{1,0:T(8,128)(2,1)S(1)}, bf16[64,1536]{1,0:T(8,128)(2,1)S(1)}) custom-call(s32[1]{0:T(128)} %bitcast.3.column_ref, bf16[256,2048]{1,0:T(8,128)(2,1)S(1)} %gate_up.5.h_ref, bf16[1,2048,3072]{2,1,0:T(8,128)(2,1)S(1)} %bitcast.5), custom_call_target="tpu_custom_call" | custom-call | flops 1610612736 | bytes 7077888 | tf_op jit(solution)/shard_map/down/pallas_call | solution.py:224
  40.5 0.5 collective-permute-start.19
  41.1 1.4 %collective-permute-start.20 = (bf16[64,1536]{1,0:T(8,128)(2,1)S(1)}, bf16[64,1536]{1,0:T(8,128)(2,1)S(1)}, u32[]{:S(2)}, u32[]{:S(2)}) collective-permute-start(bf16[64,1536]{1,0:T(8,128)(2,1)S(1)} %get-tuple-element.84), channel_id=1, source_target_pairs={{0,2},{1,3},{2,0},{3,1},{4,6},{5,7},{6,4},{7,5},{8,10},{9,11},{10,... | collective-permute-start | bytes 589832 | tf_op jit(solution)/shard_map/ppermute | solution.py:282
  42.6 1.0 %collective-permute-done.14.refs_3_ = bf16[64,768]{1,0:T(8,128)(2,1)S(1)} collective-permute-done((bf16[64,768]{1,0:T(8,128)(2,1)S(1)}, bf16[64,768]{1,0:T(8,128)(2,1)S(1)}, u32[]{:S(2)}, u32[]{:S(2)}) %collective-permute-start.14) | collective-permute-done | bytes 98336 | tf_op jit(solution)/shard_map/ppermute | solution.py:282
  43.6 0.3 combine.4
  43.9 0.9 %collective-permute-start.15 = (bf16[128,384]{1,0:T(8,128)(2,1)S(1)}, bf16[128,384]{1,0:T(8,128)(2,1)S(1)}, u32[]{:S(2)}, u32[]{:S(2)}) collective-permute-start(bf16[128,384]{1,0:T(8,128)(2,1)S(1)} %get-tuple-element.77), channel_id=1, source_target_pairs={{0,4},{4,0},{8,12},{12,8},{1,5},{5,1},{9,13},{13,9},{2,6},{6,2},{1... | collective-permute-start | bytes 294920 | tf_op jit(solution)/shard_map/ppermute | solution.py:282
  44.8 3.9 %collective-permute-start.24 = (bf16[128,384]{1,0:T(8,128)(2,1)S(1)}, bf16[128,384]{1,0:T(8,128)(2,1)S(1)}, u32[]{:S(2)}, u32[]{:S(2)}) collective-permute-start(bf16[128,384]{1,0:T(8,128)(2,1)S(1)} %get-tuple-element.86), channel_id=1, source_target_pairs={{0,12},{4,8},{8,4},{12,0},{1,13},{5,9},{9,5},{13,1},{2,14},{6,10},... | collective-permute-start | bytes 294920 | tf_op jit(solution)/shard_map/ppermute | solution.py:282
  48.7 0.7 %collective-permute-done.15.refs_0_.refs_4_ = bf16[128,384]{1,0:T(8,128)(2,1)S(1)} collective-permute-done((bf16[128,384]{1,0:T(8,128)(2,1)S(1)}, bf16[128,384]{1,0:T(8,128)(2,1)S(1)}, u32[]{:S(2)}, u32[]{:S(2)}) %collective-permute-start.15) | collective-permute-done | bytes 98336 | tf_op jit(solution)/shard_map/ppermute | solution.py:282
  49.4 2.7 %collective-permute-done.21.refs_3_ = bf16[64,1536]{1,0:T(8,128)(2,1)S(1)} collective-permute-done((bf16[64,1536]{1,0:T(8,128)(2,1)S(1)}, bf16[64,1536]{1,0:T(8,128)(2,1)S(1)}, u32[]{:S(2)}, u32[]{:S(2)}) %collective-permute-start.21) | collective-permute-done | bytes 196640 | tf_op jit(solution)/shard_map/ppermute | solution.py:282
  52.1 0.3 combine.6
  52.4 3.3 %collective-permute-start.23 = (bf16[128,768]{1,0:T(8,128)(2,1)S(1)}, bf16[128,768]{1,0:T(8,128)(2,1)S(1)}, u32[]{:S(2)}, u32[]{:S(2)}) collective-permute-start(bf16[128,768]{1,0:T(8,128)(2,1)S(1)} %combine.6), channel_id=1, source_target_pairs={{0,8},{4,12},{8,0},{12,4},{1,9},{5,13},{9,1},{13,5},{2,10},{6,14},... | collective-permute-start | bytes 589832 | tf_op jit(solution)/shard_map/ppermute | solution.py:282
  55.7 0.3 combine.5
  56.2 1.0 %down.4 = (bf16[64,768]{1,0:T(8,128)(2,1)S(1)}, bf16[64,768]{1,0:T(8,128)(2,1)S(1)}, bf16[64,768]{1,0:T(8,128)(2,1)S(1)}, bf16[64,768]{1,0:T(8,128)(2,1)S(1)}) custom-call(s32[1]{0:T(128)} %bitcast.3.column_ref, bf16[256,2048]{1,0:T(8,128)(2,1)S(1)} %gate_up.5.h_ref, bf16[1,2048,3072]{2,1,0:T(8,128)(2,1)S(1)} %bitcast.5, ...), custom_call_target="tpu_custom_call" | custom-call | flops 805306368 | bytes 3538944 | tf_op jit(solution)/shard_map/down/pallas_call | solution.py:224
  57.2 0.2 collective-permute-start.16
  57.5 1.5 %collective-permute-start.17 = (bf16[64,768]{1,0:T(8,128)(2,1)S(1)}, bf16[64,768]{1,0:T(8,128)(2,1)S(1)}, u32[]{:S(2)}, u32[]{:S(2)}) collective-permute-start(bf16[64,768]{1,0:T(8,128)(2,1)S(1)} %get-tuple-element.80), channel_id=1, source_target_pairs={{0,2},{1,3},{2,0},{3,1},{4,6},{5,7},{6,4},{7,5},{8,10},{9,11},{10,... | collective-permute-start | bytes 294920 | tf_op jit(solution)/shard_map/ppermute | solution.py:282
  59.0 0.2 collective-permute-start.18
  59.2 3.9 %collective-permute-done.17.refs_2_ = bf16[64,768]{1,0:T(8,128)(2,1)S(1)} collective-permute-done((bf16[64,768]{1,0:T(8,128)(2,1)S(1)}, bf16[64,768]{1,0:T(8,128)(2,1)S(1)}, u32[]{:S(2)}, u32[]{:S(2)}) %collective-permute-start.17) | collective-permute-done | bytes 98336 | tf_op jit(solution)/shard_map/ppermute | solution.py:282
  63.1 1.0 %collective-permute-done.18.refs_3_ = bf16[64,768]{1,0:T(8,128)(2,1)S(1)} collective-permute-done((bf16[64,768]{1,0:T(8,128)(2,1)S(1)}, bf16[64,768]{1,0:T(8,128)(2,1)S(1)}, u32[]{:S(2)}, u32[]{:S(2)}) %collective-permute-start.18) | collective-permute-done | bytes 98336 | tf_op jit(solution)/shard_map/ppermute | solution.py:282
  64.1 1.3 %collective-permute-done.23.refs_5_ = bf16[128,768]{1,0:T(8,128)(2,1)S(1)} collective-permute-done((bf16[128,768]{1,0:T(8,128)(2,1)S(1)}, bf16[128,768]{1,0:T(8,128)(2,1)S(1)}, u32[]{:S(2)}, u32[]{:S(2)}) %collective-permute-start.23) | collective-permute-done | bytes 196640 | tf_op jit(solution)/shard_map/ppermute | solution.py:282
  65.4 1.7 %collective-permute-done.22.refs_4_ = bf16[128,768]{1,0:T(8,128)(2,1)S(1)} collective-permute-done((bf16[128,768]{1,0:T(8,128)(2,1)S(1)}, bf16[128,768]{1,0:T(8,128)(2,1)S(1)}, u32[]{:S(2)}, u32[]{:S(2)}) %collective-permute-start.22) | collective-permute-done | bytes 196640 | tf_op jit(solution)/shard_map/ppermute | solution.py:282
  67.0 1.0 %combine.7 = bf16[128,768]{1,0:T(8,128)(2,1)} custom-call(bf16[256,256]{1,0:T(8,128)(2,1)S(1)} %get-tuple-element.46.pick_ref, f32[128,2]{1,0:T(8,128)S(1)} %get-tuple-element.47.mix_ref, bf16[64,768]{1,0:T(8,128)(2,1)S(1)} %get-tuple-element.78.refs_0_, bf16[64,768]{1,0:T(8,128)(2,1)S(1)} %collective-permute-done.16.refs_1_, ...), custom_call_target="tpu_custom_call" | custom-call | flops 100663296 | bytes 589824 | tf_op jit(solution)/shard_map/combine/pallas_call | solution.py:262
  (31 shorter events, 0.6 us)
Async XLA Ops:
  0.0 13.5 %collective-permute-start = (bf16[128,768]{1,0:T(8,128)(2,1)}, bf16[128,768]{1,0:T(8,128)(2,1)S(1)}, u32[]{:S(2)}, u32[]{:S(2)}) collective-permute-start(bf16[128,768]{1,0:T(8,128)(2,1)} %refs_0_.4), channel_id=1, source_target_pairs={{0,8},{4,12},{8,0},{12,4},{1,9},{5,13},{9,1},{13,5},{2,10},{6,14},... | collective-permute-start | bytes 589832 | tf_op jit(solution)/shard_map/ppermute | solution.py:282
  4.0 10.2 %collective-permute-start.5 = (bf16[128,768]{1,0:T(8,128)(2,1)}, bf16[128,768]{1,0:T(8,128)(2,1)S(1)}, u32[]{:S(2)}, u32[]{:S(2)}) collective-permute-start(bf16[128,768]{1,0:T(8,128)(2,1)} %refs_0_.4), channel_id=1, source_target_pairs={{0,4},{4,0},{8,12},{12,8},{1,5},{5,1},{9,13},{13,9},{2,6},{6,2},{1... | collective-permute-start | bytes 589832 | tf_op jit(solution)/shard_map/ppermute | solution.py:282
  5.6 0.7 copy-start.1
  6.3 0.7 copy-start.2
  7.1 7.0 %copy-start = (bf16[128,768]{1,0:T(8,128)(2,1)S(1)}, bf16[128,768]{1,0:T(8,128)(2,1)}, u32[]{:S(2)}) copy-start(bf16[128,768]{1,0:T(8,128)(2,1)} %refs_0_.4) | copy-start | bytes 589828
  13.5 8.3 %collective-permute-start.1 = (bf16[128,768]{1,0:T(8,128)(2,1)S(1)}, bf16[128,768]{1,0:T(8,128)(2,1)S(1)}, u32[]{:S(2)}, u32[]{:S(2)}) collective-permute-start(bf16[128,768]{1,0:T(8,128)(2,1)S(1)} %collective-permute-done.refs_0_), channel_id=1, source_target_pairs={{0,4},{4,0},{8,12},{12,8},{1,5},{5,1},{9,13},{13,9},{2,6},{6,2},{1... | collective-permute-start | bytes 589832 | tf_op jit(solution)/shard_map/ppermute | solution.py:282
  14.6 9.8 %collective-permute-start.10 = (bf16[64,1536]{1,0:T(8,128)(2,1)S(1)}, bf16[64,1536]{1,0:T(8,128)(2,1)S(1)}, u32[]{:S(2)}, u32[]{:S(2)}) collective-permute-start(bf16[64,1536]{1,0:T(8,128)(2,1)S(1)} %get-tuple-element.64), channel_id=1, source_target_pairs={{0,2},{1,3},{2,0},{3,1},{4,6},{5,7},{6,4},{7,5},{8,10},{9,11},{10,... | collective-permute-start | bytes 589832 | tf_op jit(solution)/shard_map/ppermute | solution.py:282
  16.1 8.7 %collective-permute-start.11 = (bf16[64,1536]{1,0:T(8,128)(2,1)S(1)}, bf16[64,1536]{1,0:T(8,128)(2,1)S(1)}, u32[]{:S(2)}, u32[]{:S(2)}) collective-permute-start(bf16[64,1536]{1,0:T(8,128)(2,1)S(1)} %get-tuple-element.65), channel_id=1, source_target_pairs={{0,3},{1,2},{2,1},{3,0},{4,7},{5,6},{6,5},{7,4},{8,11},{9,10},{10,... | collective-permute-start | bytes 589832 | tf_op jit(solution)/shard_map/ppermute | solution.py:282
  16.1 9.7 %collective-permute-start.9 = (bf16[64,1536]{1,0:T(8,128)(2,1)S(1)}, bf16[64,1536]{1,0:T(8,128)(2,1)S(1)}, u32[]{:S(2)}, u32[]{:S(2)}) collective-permute-start(bf16[64,1536]{1,0:T(8,128)(2,1)S(1)} %get-tuple-element.63), channel_id=1, source_target_pairs={{0,1},{1,0},{2,3},{3,2},{4,5},{5,4},{6,7},{7,6},{8,9},{9,8},{10,11... | collective-permute-start | bytes 589832 | tf_op jit(solution)/shard_map/ppermute | solution.py:282
  21.7 1.9 %collective-permute-start.6 = (bf16[64,768]{1,0:T(8,128)(2,1)S(1)}, bf16[64,768]{1,0:T(8,128)(2,1)S(1)}, u32[]{:S(2)}, u32[]{:S(2)}) collective-permute-start(bf16[64,768]{1,0:T(8,128)(2,1)S(1)} %get-tuple-element.58), channel_id=1, source_target_pairs={{0,1},{1,0},{2,3},{3,2},{4,5},{5,4},{6,7},{7,6},{8,9},{9,8},{10,11... | collective-permute-start | bytes 294920 | tf_op jit(solution)/shard_map/ppermute | solution.py:282
  21.8 8.6 %collective-permute-start.7 = (bf16[64,768]{1,0:T(8,128)(2,1)S(1)}, bf16[64,768]{1,0:T(8,128)(2,1)S(1)}, u32[]{:S(2)}, u32[]{:S(2)}) collective-permute-start(bf16[64,768]{1,0:T(8,128)(2,1)S(1)} %get-tuple-element.59), channel_id=1, source_target_pairs={{0,2},{1,3},{2,0},{3,1},{4,6},{5,7},{6,4},{7,5},{8,10},{9,11},{10,... | collective-permute-start | bytes 294920 | tf_op jit(solution)/shard_map/ppermute | solution.py:282
  23.7 6.8 %collective-permute-start.8 = (bf16[64,768]{1,0:T(8,128)(2,1)S(1)}, bf16[64,768]{1,0:T(8,128)(2,1)S(1)}, u32[]{:S(2)}, u32[]{:S(2)}) collective-permute-start(bf16[64,768]{1,0:T(8,128)(2,1)S(1)} %get-tuple-element.60), channel_id=1, source_target_pairs={{0,3},{1,2},{2,1},{3,0},{4,7},{5,6},{6,5},{7,4},{8,11},{9,10},{10,... | collective-permute-start | bytes 294920 | tf_op jit(solution)/shard_map/ppermute | solution.py:282
  24.4 8.3 %collective-permute-start.2 = (bf16[64,768]{1,0:T(8,128)(2,1)S(1)}, bf16[64,768]{1,0:T(8,128)(2,1)S(1)}, u32[]{:S(2)}, u32[]{:S(2)}) collective-permute-start(bf16[64,768]{1,0:T(8,128)(2,1)S(1)} %get-tuple-element.50), channel_id=1, source_target_pairs={{0,1},{1,0},{2,3},{3,2},{4,5},{5,4},{6,7},{7,6},{8,9},{9,8},{10,11... | collective-permute-start | bytes 294920 | tf_op jit(solution)/shard_map/ppermute | solution.py:282
  24.8 7.8 %collective-permute-start.3 = (bf16[64,768]{1,0:T(8,128)(2,1)S(1)}, bf16[64,768]{1,0:T(8,128)(2,1)S(1)}, u32[]{:S(2)}, u32[]{:S(2)}) collective-permute-start(bf16[64,768]{1,0:T(8,128)(2,1)S(1)} %get-tuple-element.51), channel_id=1, source_target_pairs={{0,2},{1,3},{2,0},{3,1},{4,6},{5,7},{6,4},{7,5},{8,10},{9,11},{10,... | collective-permute-start | bytes 294920 | tf_op jit(solution)/shard_map/ppermute | solution.py:282
  25.9 7.5 %collective-permute-start.4 = (bf16[64,768]{1,0:T(8,128)(2,1)S(1)}, bf16[64,768]{1,0:T(8,128)(2,1)S(1)}, u32[]{:S(2)}, u32[]{:S(2)}) collective-permute-start(bf16[64,768]{1,0:T(8,128)(2,1)S(1)} %get-tuple-element.52), channel_id=1, source_target_pairs={{0,3},{1,2},{2,1},{3,0},{4,7},{5,6},{6,5},{7,4},{8,11},{9,10},{10,... | collective-permute-start | bytes 294920 | tf_op jit(solution)/shard_map/ppermute | solution.py:282
  30.5 5.1 %slice-start = ((s8[12582912]{0:T(1024)(128)(4,1)}), s8[4194304]{0:T(1024)(128)(4,1)S(1)}, s32[]{:S(2)}) async-start(s8[12582912]{0:T(1024)(128)(4,1)} %bitcast.4), calls=%async_computation | async-start | bytes 8388608
  30.5 5.1 %slice-start.1 = ((s8[12582912]{0:T(1024)(128)(4,1)}), s8[4194304]{0:T(1024)(128)(4,1)S(1)}, s32[]{:S(2)}) async-start(s8[12582912]{0:T(1024)(128)(4,1)} %bitcast.4), calls=%async_computation.1 | async-start | bytes 8388608
  33.4 2.3 %slice-start.2 = ((s8[12582912]{0:T(1024)(128)(4,1)}), s8[4194304]{0:T(1024)(128)(4,1)S(1)}, s32[]{:S(2)}) async-start(s8[12582912]{0:T(1024)(128)(4,1)} %bitcast.4), calls=%async_computation.2 | async-start | bytes 8388608
  36.8 5.7 %collective-permute-start.12 = (bf16[64,768]{1,0:T(8,128)(2,1)S(1)}, bf16[64,768]{1,0:T(8,128)(2,1)S(1)}, u32[]{:S(2)}, u32[]{:S(2)}) collective-permute-start(bf16[64,768]{1,0:T(8,128)(2,1)S(1)} %get-tuple-element.74), channel_id=1, source_target_pairs={{0,1},{1,0},{2,3},{3,2},{4,5},{5,4},{6,7},{7,6},{8,9},{9,8},{10,11... | collective-permute-start | bytes 294920 | tf_op jit(solution)/shard_map/ppermute | solution.py:282
  37.0 5.6 %collective-permute-start.13 = (bf16[64,768]{1,0:T(8,128)(2,1)S(1)}, bf16[64,768]{1,0:T(8,128)(2,1)S(1)}, u32[]{:S(2)}, u32[]{:S(2)}) collective-permute-start(bf16[64,768]{1,0:T(8,128)(2,1)S(1)} %get-tuple-element.75), channel_id=1, source_target_pairs={{0,2},{1,3},{2,0},{3,1},{4,6},{5,7},{6,4},{7,5},{8,10},{9,11},{10,... | collective-permute-start | bytes 294920 | tf_op jit(solution)/shard_map/ppermute | solution.py:282
  38.4 5.2 %collective-permute-start.14 = (bf16[64,768]{1,0:T(8,128)(2,1)S(1)}, bf16[64,768]{1,0:T(8,128)(2,1)S(1)}, u32[]{:S(2)}, u32[]{:S(2)}) collective-permute-start(bf16[64,768]{1,0:T(8,128)(2,1)S(1)} %get-tuple-element.76), channel_id=1, source_target_pairs={{0,3},{1,2},{2,1},{3,0},{4,7},{5,6},{6,5},{7,4},{8,11},{9,10},{10,... | collective-permute-start | bytes 294920 | tf_op jit(solution)/shard_map/ppermute | solution.py:282
  40.5 8.9 %collective-permute-start.19 = (bf16[64,1536]{1,0:T(8,128)(2,1)S(1)}, bf16[64,1536]{1,0:T(8,128)(2,1)S(1)}, u32[]{:S(2)}, u32[]{:S(2)}) collective-permute-start(bf16[64,1536]{1,0:T(8,128)(2,1)S(1)} %get-tuple-element.83), channel_id=1, source_target_pairs={{0,1},{1,0},{2,3},{3,2},{4,5},{5,4},{6,7},{7,6},{8,9},{9,8},{10,11... | collective-permute-start | bytes 589832 | tf_op jit(solution)/shard_map/ppermute | solution.py:282
  41.1 8.3 %collective-permute-start.20 = (bf16[64,1536]{1,0:T(8,128)(2,1)S(1)}, bf16[64,1536]{1,0:T(8,128)(2,1)S(1)}, u32[]{:S(2)}, u32[]{:S(2)}) collective-permute-start(bf16[64,1536]{1,0:T(8,128)(2,1)S(1)} %get-tuple-element.84), channel_id=1, source_target_pairs={{0,2},{1,3},{2,0},{3,1},{4,6},{5,7},{6,4},{7,5},{8,10},{9,11},{10,... | collective-permute-start | bytes 589832 | tf_op jit(solution)/shard_map/ppermute | solution.py:282
  42.5 9.6 %collective-permute-start.21 = (bf16[64,1536]{1,0:T(8,128)(2,1)S(1)}, bf16[64,1536]{1,0:T(8,128)(2,1)S(1)}, u32[]{:S(2)}, u32[]{:S(2)}) collective-permute-start(bf16[64,1536]{1,0:T(8,128)(2,1)S(1)} %get-tuple-element.85), channel_id=1, source_target_pairs={{0,3},{1,2},{2,1},{3,0},{4,7},{5,6},{6,5},{7,4},{8,11},{9,10},{10,... | collective-permute-start | bytes 589832 | tf_op jit(solution)/shard_map/ppermute | solution.py:282
  43.9 5.5 %collective-permute-start.15 = (bf16[128,384]{1,0:T(8,128)(2,1)S(1)}, bf16[128,384]{1,0:T(8,128)(2,1)S(1)}, u32[]{:S(2)}, u32[]{:S(2)}) collective-permute-start(bf16[128,384]{1,0:T(8,128)(2,1)S(1)} %get-tuple-element.77), channel_id=1, source_target_pairs={{0,4},{4,0},{8,12},{12,8},{1,5},{5,1},{9,13},{13,9},{2,6},{6,2},{1... | collective-permute-start | bytes 294920 | tf_op jit(solution)/shard_map/ppermute | solution.py:282
  44.8 14.2 %collective-permute-start.24 = (bf16[128,384]{1,0:T(8,128)(2,1)S(1)}, bf16[128,384]{1,0:T(8,128)(2,1)S(1)}, u32[]{:S(2)}, u32[]{:S(2)}) collective-permute-start(bf16[128,384]{1,0:T(8,128)(2,1)S(1)} %get-tuple-element.86), channel_id=1, source_target_pairs={{0,12},{4,8},{8,4},{12,0},{1,13},{5,9},{9,5},{13,1},{2,14},{6,10},... | collective-permute-start | bytes 294920 | tf_op jit(solution)/shard_map/ppermute | solution.py:282
  52.4 12.9 %collective-permute-start.23 = (bf16[128,768]{1,0:T(8,128)(2,1)S(1)}, bf16[128,768]{1,0:T(8,128)(2,1)S(1)}, u32[]{:S(2)}, u32[]{:S(2)}) collective-permute-start(bf16[128,768]{1,0:T(8,128)(2,1)S(1)} %combine.6), channel_id=1, source_target_pairs={{0,8},{4,12},{8,0},{12,4},{1,9},{5,13},{9,1},{13,5},{2,10},{6,14},... | collective-permute-start | bytes 589832 | tf_op jit(solution)/shard_map/ppermute | solution.py:282
  56.1 11.0 %collective-permute-start.22 = (bf16[128,768]{1,0:T(8,128)(2,1)S(1)}, bf16[128,768]{1,0:T(8,128)(2,1)S(1)}, u32[]{:S(2)}, u32[]{:S(2)}) collective-permute-start(bf16[128,768]{1,0:T(8,128)(2,1)S(1)} %combine.5), channel_id=1, source_target_pairs={{0,4},{4,0},{8,12},{12,8},{1,5},{5,1},{9,13},{13,9},{2,6},{6,2},{1... | collective-permute-start | bytes 589832 | tf_op jit(solution)/shard_map/ppermute | solution.py:282
  57.2 1.9 %collective-permute-start.16 = (bf16[64,768]{1,0:T(8,128)(2,1)S(1)}, bf16[64,768]{1,0:T(8,128)(2,1)S(1)}, u32[]{:S(2)}, u32[]{:S(2)}) collective-permute-start(bf16[64,768]{1,0:T(8,128)(2,1)S(1)} %get-tuple-element.79), channel_id=1, source_target_pairs={{0,1},{1,0},{2,3},{3,2},{4,5},{5,4},{6,7},{7,6},{8,9},{9,8},{10,11... | collective-permute-start | bytes 294920 | tf_op jit(solution)/shard_map/ppermute | solution.py:282
  57.5 5.6 %collective-permute-start.17 = (bf16[64,768]{1,0:T(8,128)(2,1)S(1)}, bf16[64,768]{1,0:T(8,128)(2,1)S(1)}, u32[]{:S(2)}, u32[]{:S(2)}) collective-permute-start(bf16[64,768]{1,0:T(8,128)(2,1)S(1)} %get-tuple-element.80), channel_id=1, source_target_pairs={{0,2},{1,3},{2,0},{3,1},{4,6},{5,7},{6,4},{7,5},{8,10},{9,11},{10,... | collective-permute-start | bytes 294920 | tf_op jit(solution)/shard_map/ppermute | solution.py:282
  59.0 5.1 %collective-permute-start.18 = (bf16[64,768]{1,0:T(8,128)(2,1)S(1)}, bf16[64,768]{1,0:T(8,128)(2,1)S(1)}, u32[]{:S(2)}, u32[]{:S(2)}) collective-permute-start(bf16[64,768]{1,0:T(8,128)(2,1)S(1)} %get-tuple-element.81), channel_id=1, source_target_pairs={{0,3},{1,2},{2,1},{3,0},{4,7},{5,6},{6,5},{7,4},{8,11},{9,10},{10,... | collective-permute-start | bytes 294920 | tf_op jit(solution)/shard_map/ppermute | solution.py:282

commit v15 on v12

--- a/solution.py
+++ b/solution.py
@@ -71,8 +71,11 @@
     )(me.reshape(1), expert_ids.T, route_logits.T)
 
 
-def dispatch_kernel(placed_ref, *refs, count, waits):
+def dispatch_kernel(placed_ref, *refs, count, waits, echo):
     inputs, outputs = refs[:count], refs[count + waits :]
+    if echo:
+        outputs[-1][...] = inputs[0][...]
+        outputs = outputs[:-1]
     capacity, wide = outputs[0].shape
     width = wide // count
     for i, block in enumerate(inputs):
@@ -84,19 +87,22 @@
             ).astype(BF16)
 
 
-def dispatch(placed, slices, experts, capacity, after):
+def dispatch(placed, slices, experts, capacity, after, echo=False):
     rows, width = slices[0].shape
     wide = width * len(slices)
     return pl.pallas_call(
-        functools.partial(dispatch_kernel, count=len(slices), waits=len(after)),
-        out_shape=[jax.ShapeDtypeStruct((capacity, wide), BF16)] * experts,
+        functools.partial(
+            dispatch_kernel, count=len(slices), waits=len(after), echo=echo
+        ),
+        out_shape=[jax.ShapeDtypeStruct((capacity, wide), BF16)] * experts
+        + [jax.ShapeDtypeStruct((rows, width), BF16)] * echo,
         in_specs=[pl.BlockSpec(memory_space=pltpu.VMEM)] * (1 + len(slices))
         + [pl.BlockSpec(memory_space=pl.ANY)] * len(after),
-        out_specs=[pl.BlockSpec(memory_space=pltpu.VMEM)] * experts,
+        out_specs=[pl.BlockSpec(memory_space=pltpu.VMEM)] * (experts + echo),
         cost_estimate=cost(2 * experts * capacity * rows * wide, 6 * rows * wide),
         compiler_params=params(),
         name="dispatch",
-    )(placed, *slices, *pinned(after))
+    )(placed, *slices, *after)
 
 
 def across(distance):
@@ -137,62 +143,91 @@
     )(column.reshape(1), after, *sources)
 
 
-def gate_up_kernel(*refs, experts, slices, first, last, waits):
-    x_refs = refs[:experts]
-    weights = refs[experts : experts + 2 * slices]
-    rest = refs[experts + 2 * slices :]
+def gate_up_kernel(column_ref, *refs, experts, slices, first, last, waits, parts):
+    x_refs = refs[: experts * slices]
+    weights = refs[experts * slices : (experts + 2) * slices]
+    rest = refs[(experts + 2) * slices :]
     if not first:
         old_gate, old_up = rest[:2]
         rest = rest[2:]
     rest = rest[waits:]
-    x = jnp.concatenate([r[...] for r in x_refs], axis=0)
-    width, hidden = weights[0].shape
+    sources, outs = rest[: len(parts)], rest[len(parts) :]
+    copies = []
+    for i, part in enumerate(parts):
+        target = outs[len(outs) - 1 - len(parts) + i]
+        count = target.shape[0]
+        start = pl.multiple_of(part(column_ref[0]) * count, count)
+        source = sources[i].at[0, pl.ds(start, count)]
+        copies.append(pltpu.make_async_copy(source, target, outs[-1].at[i]))
+    for copy in copies:
+        copy.start()
+    x = [
+        jnp.concatenate([r[...] for r in x_refs[i * experts : (i + 1) * experts]], axis=0)
+        for i in range(slices)
+    ]
+    hidden = weights[0].shape[1]
     tile = min(512, hidden)
-    for n in range(hidden // tile):
-        columns = slice(n * tile, (n + 1) * tile)
+
+    def step(columns):
         sums = []
         for kind in range(2):
             total = None if first else (old_gate, old_up)[kind][:, columns]
             for i in range(slices):
                 term = jnp.dot(
-                    x[:, i * width : (i + 1) * width],
-                    weights[2 * i + kind][:, columns],
-                    preferred_element_type=F32,
+                    x[i], weights[2 * i + kind][:, columns], preferred_element_type=F32
                 )
                 total = term if total is None else total + term
             sums.append(total)
         gate, up = sums
         if last:
-            rest[0][:, columns] = (gate / (1.0 + jnp.exp(-gate)) * up).astype(BF16)
+            outs[0][:, columns] = (gate / (1.0 + jnp.exp(-gate)) * up).astype(BF16)
         else:
-            rest[0][:, columns] = gate
-            rest[1][:, columns] = up
-
-
-def gate_up(x_blocks, weights, sums, last, after):
-    experts = len(x_blocks)
+            outs[0][:, columns] = gate
+            outs[1][:, columns] = up
+
+    if copies:
+
+        @pl.loop(0, hidden // tile)
+        def _(n):
+            step(pl.ds(pl.multiple_of(n * tile, tile), tile))
+
+    else:
+        for n in range(hidden // tile):
+            step(slice(n * tile, (n + 1) * tile))
+    for copy in copies:
+        copy.wait()
+
+
+def gate_up(column, x_slices, weights, sums, last, after, fetches):
+    experts = len(x_slices[0])
+    x_blocks = [block for blocks in x_slices for block in blocks]
     rows = experts * x_blocks[0].shape[0]
     hidden = weights[0].shape[1]
     first = sums is None
     old = [] if first else pinned(sums)
-    before = experts + len(weights)
+    before = 1 + len(x_blocks) + len(weights)
+    sources = [pltpu.with_memory_space_constraint(w, pltpu.HBM) for w, _, _ in fetches]
     if last:
         out_shape = [pltpu.VMEM((rows, hidden), BF16)]
     else:
         out_shape = [pltpu.VMEM((rows, hidden), F32)] * 2
-    return pl.pallas_call(
+    shapes = out_shape + [pltpu.VMEM((count, w.shape[2]), w.dtype) for w, _, count in fetches]
+    results = pl.pallas_call(
         functools.partial(
             gate_up_kernel,
             experts=experts,
-            slices=len(weights) // 2,
+            slices=len(x_slices),
             first=first,
             last=last,
             waits=len(after),
+            parts=[part for _, part, _ in fetches],
         ),
-        out_shape=out_shape,
-        in_specs=[pl.BlockSpec(memory_space=pltpu.VMEM)] * (before + len(old))
-        + [pl.BlockSpec(memory_space=pl.ANY)] * len(after),
-        out_specs=[pl.BlockSpec(memory_space=pltpu.VMEM)] * len(out_shape),
+        out_shape=shapes,
+        in_specs=[pl.BlockSpec(memory_space=pltpu.SMEM)]
+        + [pl.BlockSpec(memory_space=pltpu.VMEM)] * (before - 1 + len(old))
+        + [pl.BlockSpec(memory_space=pl.ANY)] * (len(after) + len(sources)),
+        out_specs=[pl.BlockSpec(memory_space=pltpu.VMEM)] * len(shapes),
+        scratch_shapes=[pltpu.SemaphoreType.DMA((len(fetches),))] if fetches else [],
         input_output_aliases={} if first or last else {before: 0, before + 1: 1},
         cost_estimate=cost(
             2 * rows * hidden * sum(w.shape[0] for w in weights),
@@ -200,7 +235,8 @@
         ),
         compiler_params=params(),
         name="gate_up",
-    )(*x_blocks, *pinned(weights), *old, *after)
+    )(column.reshape(1), *x_blocks, *pinned(weights), *old, *after, *sources)
+    return results[: len(out_shape)], list(results[len(out_shape) :])
 
 
 def down_kernel(column_ref, h_ref, w_ref, *refs, part, waits):
@@ -286,32 +322,34 @@
     width = own_width if doubling else own_width * shards
 
     if doubling:
-        across_two = swap(tokens, "tensor", 2)
-        slices = [tokens, swap(tokens, "tensor", 1), across_two, swap(across_two, "tensor", 1)]
+        slices = [tokens, swap(tokens, "tensor", 1), swap(tokens, "tensor", 2)]
         parts = [across(distance) for distance in range(4)]
-        groups = [[0, 1], [2], [3]]
     else:
         slices = [lax.all_gather(tokens, "tensor", axis=1, tiled=True)]
         parts = [everything]
-        groups = [[0]]
     placed, pick, mix = place(me, expert_ids, route_logits, experts, capacity)
 
-    def fetch(chosen, after):
-        fetches = [(w, parts[i], width) for i in chosen for w in (gate_weight, up_weight)]
-        return list(prefetch(column, fetches, after))
-
-    weights, arrived = fetch(groups[0], placed), []
-    for group in groups:
-        after = weights[-1:] if len(arrived) < 2 else []
-        outgoing = dispatch(placed, [slices[i] for i in group], experts, capacity, after)
-        arrived.append([swap(block, "expert", e) for e, block in enumerate(outgoing)])
-        if len(arrived) == 1 and len(groups) > 1:
-            weights += fetch([2, 3], outgoing[0])
+    fetches = [(w, part, width) for part in parts for w in (gate_weight, up_weight)]
+    arrived, weights = [], []
+    for i in range(len(parts)):
+        echo = i == 2
+        after = pinned(weights[:1]) + (arrived[0][2:] if echo else [])
+        outgoing = dispatch(placed, [slices[i]], experts, capacity, after, echo)
+        blocks = outgoing[:experts]
+        arrived.append([swap(block, "expert", e) for e, block in enumerate(blocks)])
+        if echo:
+            slices.append(swap(outgoing[-1], "tensor", 1))
+        if not weights:
+            weights = list(prefetch(column, fetches[:4], outgoing[0]))
     sums = None
-    for group, x_blocks in zip(groups, arrived):
-        chosen = weights[2 * group[0] : 2 * group[-1] + 2]
-        after = arrived[1][1:2] if sums is None and len(groups) > 1 else []
-        sums = gate_up(x_blocks, chosen, sums, group is groups[-1], after)
+    for group in [slice(0, 2), slice(2, 3), slice(3, 4)][: max(1, len(parts) - 1)]:
+        first = sums is None
+        last = group.stop >= len(parts)
+        after = arrived[2][1:2] + arrived[3][1:2] if first and not last else []
+        chosen = weights[2 * group.start : 2 * group.stop]
+        later = fetches[4:] if first else []
+        sums, brought = gate_up(column, arrived[group], chosen, sums, last, after, later)
+        weights += brought
     hidden = sums[0]
 
     def returned(part, after=()):

time: 66.4 us -> 67.3 us (1.014)
  waiting for transfers between devices: 12.1 us -> 15.6 us
  Pallas kernels: 24.2 us -> 20.8 us
  local copies, waits for them, and re-layouts: 1.54 us -> 2.65 us
    pallas_call x2 -> x1, Pallas kernels: 9.41 us -> 4.68 us  [prefetch(): pl.pallas_call(functools.partial(prefetch_kernel, parts=[part for _, part...]
    ppermute x28 -> x31, waiting for transfers between devices: 12.1 us -> 15.6 us  [swap(): return lax.ppermute(value, axis, [(i, i ^ distance) for i in range(count)])]
    pallas_call x3, Pallas kernels: 7.71 us -> 8.9 us  [gate_up(): pl.pallas_call(functools.partial(gate_up_kernel, experts=experts, slices=...]
    unnamed x12, local copies, waits for them, and re-layouts: 1.54 us -> 2.65 us
    ppermute x28 -> x31, starting transfers between devices: 28.2 us -> 27.7 us  [swap(): return lax.ppermute(value, axis, [(i, i ^ distance) for i in range(count)])]
  transfers between devices with their start and end apart: 28 -> 31, of which waited for: 8 -> 11; matrix products, arithmetic and copies ran while one was open for 0% -> 0% of each run, Pallas kernels for 30% -> 25%
where the time goes in v15:
time: 67.3 us; the launch traced here: 67.1 us
  starting transfers between devices  27.7 us (41%)
  Pallas kernels  20.8 us (31%)
  waiting for transfers between devices  15.6 us (23%)
  local copies, waits for them, and re-layouts  2.65 us (4%)
    ppermute x31, starting transfers between devices, swap(): return lax.ppermute(value, axis, [(i, i ^ distance) for i in range(count)])  27.7 us
    ppermute x31, waiting for transfers between devices, swap(): return lax.ppermute(value, axis, [(i, i ^ distance) for i in range(count)])  15.6 us
    pallas_call x3, Pallas kernels, gate_up(): pl.pallas_call(functools.partial(gate_up_kernel, experts=experts, slices=...  8.9 us
    pallas_call x1, Pallas kernels, prefetch(): pl.pallas_call(functools.partial(prefetch_kernel, parts=[part for _, part...  4.68 us
    pallas_call x4, Pallas kernels, down(): pl.pallas_call(functools.partial(down_kernel, part=part, waits=len(after)...  4.1 us
    unnamed x12, local copies, waits for them, and re-layouts  2.65 us
    pallas_call x4, Pallas kernels, combine(): pl.pallas_call(functools.partial(combine_kernel, experts=len(blocks), sta...  1.94 us
  transfers between devices with their start and end apart: 31, of which 11 were waited for; matrix products, arithmetic and copies ran while one was open for 0% of the time, Pallas kernels for 25%

profile of v15, /device:TPU:0, one launch (start us, length us, event | category | flops | bytes accessed | tf_op | source)
XLA Modules:
  0.0 67.1 jit_solution(3494826884904227710)
XLA Ops:
  0.0 4.0 %collective-permute-start = (bf16[128,768]{1,0:T(8,128)(2,1)}, bf16[128,768]{1,0:T(8,128)(2,1)S(1)}, u32[]{:S(2)}, u32[]{:S(2)}) collective-permute-start(bf16[128,768]{1,0:T(8,128)(2,1)} %refs_0_.2), channel_id=1, source_target_pairs={{0,8},{4,12},{8,0},{12,4},{1,9},{5,13},{9,1},{13,5},{2,10},{6,14},... | collective-permute-start | bytes 589832 | tf_op jit(solution)/shard_map/ppermute | solution.py:311
  4.0 0.7 %copy-done.1 = s32[128,2]{0,1:T(2,128)S(1)} copy-done((s32[128,2]{0,1:T(2,128)S(1)}, s32[128,2]{0,1:T(2,128)}, u32[]{:S(2)}) %copy-start.1) | copy-done | bytes 1048
  4.7 0.7 %copy-done.2 = f32[128,2]{0,1:T(2,128)S(1)} copy-done((f32[128,2]{0,1:T(2,128)S(1)}, f32[128,2]{0,1:T(2,128)}, u32[]{:S(2)}) %copy-start.2) | copy-done | bytes 1048
  5.6 0.9 %copy-done = bf16[128,768]{1,0:T(8,128)(2,1)S(1)} copy-done((bf16[128,768]{1,0:T(8,128)(2,1)S(1)}, bf16[128,768]{1,0:T(8,128)(2,1)}, u32[]{:S(2)}) %copy-start) | copy-done | bytes 196632
  6.5 0.3 dispatch.4
  6.8 1.6 %collective-permute-start.1 = (bf16[64,768]{1,0:T(8,128)(2,1)S(1)}, bf16[64,768]{1,0:T(8,128)(2,1)S(1)}, u32[]{:S(2)}, u32[]{:S(2)}) collective-permute-start(bf16[64,768]{1,0:T(8,128)(2,1)S(1)} %get-tuple-element.60), channel_id=1, source_target_pairs={{0,2},{1,3},{2,0},{3,1},{4,6},{5,7},{6,4},{7,5},{8,10},{9,11},{10,... | collective-permute-start | bytes 294920 | tf_op jit(solution)/shard_map/ppermute | solution.py:311
  8.3 1.6 %collective-permute-start.8 = (bf16[128,768]{1,0:T(8,128)(2,1)}, bf16[128,768]{1,0:T(8,128)(2,1)S(1)}, u32[]{:S(2)}, u32[]{:S(2)}) collective-permute-start(bf16[128,768]{1,0:T(8,128)(2,1)} %refs_0_.2), channel_id=1, source_target_pairs={{0,4},{4,0},{8,12},{12,8},{1,5},{5,1},{9,13},{13,9},{2,6},{6,2},{1... | collective-permute-start | bytes 589832 | tf_op jit(solution)/shard_map/ppermute | solution.py:311
  9.9 4.7 %prefetch.1 = (bf16[768,2048]{1,0:T(8,128)(2,1)S(1)}, bf16[768,2048]{1,0:T(8,128)(2,1)S(1)}, bf16[768,2048]{1,0:T(8,128)(2,1)S(1)}, bf16[768,2048]{1,0:T(8,128)(2,1)S(1)}) custom-call(s32[1]{0:T(128)} %bitcast.3.column_ref, bf16[64,768]{1,0:T(8,128)(2,1)S(1)} %get-tuple-element.58.after_ref.refs_0_, bf16[1,3072,2048]{2,1,0:T(8,128)(2,1)} %refs_16_.1, ...), custom_call_target="tpu_custom_call" | custom-call | bytes 12582912 | tf_op jit(solution)/shard_map/prefetch/pallas_call | solution.py:133
  14.9 0.5 collective-permute-start.3
  15.5 2.1 %collective-permute-done.8.refs_0_ = bf16[128,768]{1,0:T(8,128)(2,1)S(1)} collective-permute-done((bf16[128,768]{1,0:T(8,128)(2,1)}, bf16[128,768]{1,0:T(8,128)(2,1)S(1)}, u32[]{:S(2)}, u32[]{:S(2)}) %collective-permute-start.8) | collective-permute-done | bytes 196640 | tf_op jit(solution)/shard_map/ppermute | solution.py:311
  17.6 0.3 dispatch.7
  18.0 1.6 %collective-permute-start.10 = (bf16[64,768]{1,0:T(8,128)(2,1)S(1)}, bf16[64,768]{1,0:T(8,128)(2,1)S(1)}, u32[]{:S(2)}, u32[]{:S(2)}) collective-permute-start(bf16[64,768]{1,0:T(8,128)(2,1)S(1)} %get-tuple-element.70), channel_id=1, source_target_pairs={{0,2},{1,3},{2,0},{3,1},{4,6},{5,7},{6,4},{7,5},{8,10},{9,11},{10,... | collective-permute-start | bytes 294920 | tf_op jit(solution)/shard_map/ppermute | solution.py:311
  19.8 2.4 %collective-permute-done.3.refs_0_ = bf16[128,768]{1,0:T(8,128)(2,1)S(1)} collective-permute-done((bf16[128,768]{1,0:T(8,128)(2,1)S(1)}, bf16[128,768]{1,0:T(8,128)(2,1)S(1)}, u32[]{:S(2)}, u32[]{:S(2)}) %collective-permute-start.3) | collective-permute-done | bytes 196640 | tf_op jit(solution)/shard_map/ppermute | solution.py:311
  22.4 0.6 collective-permute-start.4
  23.0 1.5 %collective-permute-start.13 = (bf16[64,768]{1,0:T(8,128)(2,1)S(1)}, bf16[64,768]{1,0:T(8,128)(2,1)S(1)}, u32[]{:S(2)}, u32[]{:S(2)}) collective-permute-start(bf16[64,768]{1,0:T(8,128)(2,1)S(1)} %get-tuple-element.79), channel_id=1, source_target_pairs={{0,2},{1,3},{2,0},{3,1},{4,6},{5,7},{6,4},{7,5},{8,10},{9,11},{10,... | collective-permute-start | bytes 294920 | tf_op jit(solution)/shard_map/ppermute | solution.py:311
  24.5 0.3 collective-permute-done.11.refs_7_
  24.8 1.4 %collective-permute-start.5 = (bf16[64,768]{1,0:T(8,128)(2,1)S(1)}, bf16[64,768]{1,0:T(8,128)(2,1)S(1)}, u32[]{:S(2)}, u32[]{:S(2)}) collective-permute-start(bf16[64,768]{1,0:T(8,128)(2,1)S(1)} %get-tuple-element.65), channel_id=1, source_target_pairs={{0,2},{1,3},{2,0},{3,1},{4,6},{5,7},{6,4},{7,5},{8,10},{9,11},{10,... | collective-permute-start | bytes 294920 | tf_op jit(solution)/shard_map/ppermute | solution.py:311
  26.2 0.5 collective-permute-start.6
  26.7 4.7 %gate_up.3 = (f32[256,2048]{1,0:T(8,128)S(1)}, f32[256,2048]{1,0:T(8,128)S(1)}, bf16[768,2048]{1,0:T(8,128)(2,1)S(1)}, bf16[768,2048]{1,0:T(8,128)(2,1)S(1)}, bf...) custom-call(s32[1]{0:T(128)} %bitcast.3.column_ref, bf16[64,768]{1,0:T(8,128)(2,1)S(1)} %get-tuple-element.58.after_ref.refs_0_, ...), custom_call_target="tpu_custom_call" | custom-call | flops 3221225472 | bytes 12582912 | tf_op jit(solution)/shard_map/gate_up/pallas_call | solution.py:215
  31.4 2.1 %gate_up.4 = (f32[256,2048]{1,0:T(8,128)S(1)}, f32[256,2048]{1,0:T(8,128)S(1)}) custom-call(s32[1]{0:T(128)} %bitcast.3.column_ref, bf16[64,768]{1,0:T(8,128)(2,1)S(1)} %get-tuple-element.78.refs_0_, bf16[64,768]{1,0:T(8,128)(2,1)S(1)} %collective-permute-done.12.refs_12_.refs_1_, ...), custom_call_target="tpu_custom_call", output_to_operand_aliasing={{0}: (7, {}), {1}: (8, {})} | custom-call | flops 1610612736 | bytes 6291456 | tf_op jit(solution)/shard_map/gate_up/pallas_call | solution.py:215
  33.5 0.3 collective-permute-done.6.refs_3_
  33.8 2.1 %gate_up.5.h_ref = bf16[256,2048]{1,0:T(8,128)(2,1)S(1)} custom-call(s32[1]{0:T(128)} %bitcast.3.column_ref, bf16[64,768]{1,0:T(8,128)(2,1)S(1)} %get-tuple-element.63.refs_0_, bf16[64,768]{1,0:T(8,128)(2,1)S(1)} %collective-permute-done.4.refs_13_.refs_1_, bf16[64,768]{1,0:T(8,128)(2,1)S(1)} %collective-permute-done.5.refs_2_, ...), custom_call_target="tpu_custom_call" | custom-call | flops 1610612736 | bytes 6291456 | tf_op jit(solution)/shard_map/gate_up/pallas_call | solution.py:215
  35.9 0.4 slice-done.2
  36.3 1.0 %down.4 = (bf16[64,768]{1,0:T(8,128)(2,1)S(1)}, bf16[64,768]{1,0:T(8,128)(2,1)S(1)}, bf16[64,768]{1,0:T(8,128)(2,1)S(1)}, bf16[64,768]{1,0:T(8,128)(2,1)S(1)}) custom-call(s32[1]{0:T(128)} %bitcast.3.column_ref, bf16[256,2048]{1,0:T(8,128)(2,1)S(1)} %gate_up.5.h_ref, bf16[1,2048,3072]{2,1,0:T(8,128)(2,1)S(1)} %bitcast.5), custom_call_target="tpu_custom_call" | custom-call | flops 805306368 | bytes 3538944 | tf_op jit(solution)/shard_map/down/pallas_call | solution.py:257
  37.3 0.3 collective-permute-start.15
  37.6 1.4 %collective-permute-start.16 = (bf16[64,768]{1,0:T(8,128)(2,1)S(1)}, bf16[64,768]{1,0:T(8,128)(2,1)S(1)}, u32[]{:S(2)}, u32[]{:S(2)}) collective-permute-start(bf16[64,768]{1,0:T(8,128)(2,1)S(1)} %get-tuple-element.89), channel_id=1, source_target_pairs={{0,2},{1,3},{2,0},{3,1},{4,6},{5,7},{6,4},{7,5},{8,10},{9,11},{10,... | collective-permute-start | bytes 294920 | tf_op jit(solution)/shard_map/ppermute | solution.py:311
  39.3 1.0 %down.7 = (bf16[64,768]{1,0:T(8,128)(2,1)S(1)}, bf16[64,768]{1,0:T(8,128)(2,1)S(1)}, bf16[64,768]{1,0:T(8,128)(2,1)S(1)}, bf16[64,768]{1,0:T(8,128)(2,1)S(1)}) custom-call(s32[1]{0:T(128)} %bitcast.3.column_ref, bf16[256,2048]{1,0:T(8,128)(2,1)S(1)} %gate_up.5.h_ref, bf16[1,2048,3072]{2,1,0:T(8,128)(2,1)S(1)} %bitcast.5), custom_call_target="tpu_custom_call" | custom-call | flops 805306368 | bytes 3538944 | tf_op jit(solution)/shard_map/down/pallas_call | solution.py:257
  40.3 0.6 collective-permute-start.26
  40.9 1.4 %collective-permute-start.27 = (bf16[64,768]{1,0:T(8,128)(2,1)S(1)}, bf16[64,768]{1,0:T(8,128)(2,1)S(1)}, u32[]{:S(2)}, u32[]{:S(2)}) collective-permute-start(bf16[64,768]{1,0:T(8,128)(2,1)S(1)} %get-tuple-element.102), channel_id=1, source_target_pairs={{0,2},{1,3},{2,0},{3,1},{4,6},{5,7},{6,4},{7,5},{8,10},{9,11},{10,... | collective-permute-start | bytes 294920 | tf_op jit(solution)/shard_map/ppermute | solution.py:311
  42.3 0.8 %collective-permute-done.16.refs_2_ = bf16[64,768]{1,0:T(8,128)(2,1)S(1)} collective-permute-done((bf16[64,768]{1,0:T(8,128)(2,1)S(1)}, bf16[64,768]{1,0:T(8,128)(2,1)S(1)}, u32[]{:S(2)}, u32[]{:S(2)}) %collective-permute-start.16) | collective-permute-done | bytes 98336 | tf_op jit(solution)/shard_map/ppermute | solution.py:311
  43.2 1.2 %collective-permute-done.17.refs_3_ = bf16[64,768]{1,0:T(8,128)(2,1)S(1)} collective-permute-done((bf16[64,768]{1,0:T(8,128)(2,1)S(1)}, bf16[64,768]{1,0:T(8,128)(2,1)S(1)}, u32[]{:S(2)}, u32[]{:S(2)}) %collective-permute-start.17) | collective-permute-done | bytes 98336 | tf_op jit(solution)/shard_map/ppermute | solution.py:311
  44.3 0.3 combine.4
  44.6 0.4 collective-permute-start.18
  45.0 1.0 %down.6 = (bf16[64,768]{1,0:T(8,128)(2,1)S(1)}, bf16[64,768]{1,0:T(8,128)(2,1)S(1)}, bf16[64,768]{1,0:T(8,128)(2,1)S(1)}, bf16[64,768]{1,0:T(8,128)(2,1)S(1)}) custom-call(s32[1]{0:T(128)} %bitcast.3.column_ref, bf16[256,2048]{1,0:T(8,128)(2,1)S(1)} %gate_up.5.h_ref, bf16[1,2048,3072]{2,1,0:T(8,128)(2,1)S(1)} %bitcast.5, ...), custom_call_target="tpu_custom_call" | custom-call | flops 805306368 | bytes 3538944 | tf_op jit(solution)/shard_map/down/pallas_call | solution.py:257
  46.0 0.6 collective-permute-start.22
  46.6 1.5 %collective-permute-start.23 = (bf16[64,768]{1,0:T(8,128)(2,1)S(1)}, bf16[64,768]{1,0:T(8,128)(2,1)S(1)}, u32[]{:S(2)}, u32[]{:S(2)}) collective-permute-start(bf16[64,768]{1,0:T(8,128)(2,1)S(1)} %get-tuple-element.98), channel_id=1, source_target_pairs={{0,2},{1,3},{2,0},{3,1},{4,6},{5,7},{6,4},{7,5},{8,10},{9,11},{10,... | collective-permute-start | bytes 294920 | tf_op jit(solution)/shard_map/ppermute | solution.py:311
  48.4 3.4 %collective-permute-start.30 = (bf16[128,384]{1,0:T(8,128)(2,1)S(1)}, bf16[128,384]{1,0:T(8,128)(2,1)S(1)}, u32[]{:S(2)}, u32[]{:S(2)}) collective-permute-start(bf16[128,384]{1,0:T(8,128)(2,1)S(1)} %get-tuple-element.104), channel_id=1, source_target_pairs={{0,12},{4,8},{8,4},{12,0},{1,13},{5,9},{9,5},{13,1},{2,14},{6,10},... | collective-permute-start | bytes 294920 | tf_op jit(solution)/shard_map/ppermute | solution.py:311
  51.8 0.3 combine.6
  52.1 0.5 collective-permute-start.29
  52.5 0.7 collective-permute-done.24.refs_3_
  53.2 0.3 combine.5
  53.5 1.8 %collective-permute-start.25 = (bf16[128,768]{1,0:T(8,128)(2,1)S(1)}, bf16[128,768]{1,0:T(8,128)(2,1)S(1)}, u32[]{:S(2)}, u32[]{:S(2)}) collective-permute-start(bf16[128,768]{1,0:T(8,128)(2,1)S(1)} %combine.5), channel_id=1, source_target_pairs={{0,4},{4,0},{8,12},{12,8},{1,5},{5,1},{9,13},{13,9},{2,6},{6,2},{1... | collective-permute-start | bytes 589832 | tf_op jit(solution)/shard_map/ppermute | solution.py:311
  55.3 1.0 %down.5 = (bf16[64,768]{1,0:T(8,128)(2,1)S(1)}, bf16[64,768]{1,0:T(8,128)(2,1)S(1)}, bf16[64,768]{1,0:T(8,128)(2,1)S(1)}, bf16[64,768]{1,0:T(8,128)(2,1)S(1)}) custom-call(s32[1]{0:T(128)} %bitcast.3.column_ref, bf16[256,2048]{1,0:T(8,128)(2,1)S(1)} %gate_up.5.h_ref, bf16[1,2048,3072]{2,1,0:T(8,128)(2,1)S(1)} %bitcast.5, ...), custom_call_target="tpu_custom_call" | custom-call | flops 805306368 | bytes 3538944 | tf_op jit(solution)/shard_map/down/pallas_call | solution.py:257
  56.5 1.5 %collective-permute-start.20 = (bf16[64,768]{1,0:T(8,128)(2,1)S(1)}, bf16[64,768]{1,0:T(8,128)(2,1)S(1)}, u32[]{:S(2)}, u32[]{:S(2)}) collective-permute-start(bf16[64,768]{1,0:T(8,128)(2,1)S(1)} %get-tuple-element.94), channel_id=1, source_target_pairs={{0,2},{1,3},{2,0},{3,1},{4,6},{5,7},{6,4},{7,5},{8,10},{9,11},{10,... | collective-permute-start | bytes 294920 | tf_op jit(solution)/shard_map/ppermute | solution.py:311
  58.3 3.8 %collective-permute-done.20.refs_2_ = bf16[64,768]{1,0:T(8,128)(2,1)S(1)} collective-permute-done((bf16[64,768]{1,0:T(8,128)(2,1)S(1)}, bf16[64,768]{1,0:T(8,128)(2,1)S(1)}, u32[]{:S(2)}, u32[]{:S(2)}) %collective-permute-start.20) | collective-permute-done | bytes 98336 | tf_op jit(solution)/shard_map/ppermute | solution.py:311
  62.1 1.2 %collective-permute-done.21.refs_3_ = bf16[64,768]{1,0:T(8,128)(2,1)S(1)} collective-permute-done((bf16[64,768]{1,0:T(8,128)(2,1)S(1)}, bf16[64,768]{1,0:T(8,128)(2,1)S(1)}, u32[]{:S(2)}, u32[]{:S(2)}) %collective-permute-start.21) | collective-permute-done | bytes 98336 | tf_op jit(solution)/shard_map/ppermute | solution.py:311
  63.3 2.7 %collective-permute-done.29.refs_5_ = bf16[128,768]{1,0:T(8,128)(2,1)S(1)} collective-permute-done((bf16[128,768]{1,0:T(8,128)(2,1)S(1)}, bf16[128,768]{1,0:T(8,128)(2,1)S(1)}, u32[]{:S(2)}, u32[]{:S(2)}) %collective-permute-start.29) | collective-permute-done | bytes 196640 | tf_op jit(solution)/shard_map/ppermute | solution.py:311
  66.0 1.0 %combine.7 = bf16[128,768]{1,0:T(8,128)(2,1)} custom-call(bf16[256,256]{1,0:T(8,128)(2,1)S(1)} %get-tuple-element.55.pick_ref, f32[128,2]{1,0:T(8,128)S(1)} %get-tuple-element.56.mix_ref, bf16[64,768]{1,0:T(8,128)(2,1)S(1)} %get-tuple-element.92.refs_0_, bf16[64,768]{1,0:T(8,128)(2,1)S(1)} %collective-permute-done.19.refs_1_, ...), custom_call_target="tpu_custom_call" | custom-call | flops 100663296 | bytes 589824 | tf_op jit(solution)/shard_map/combine/pallas_call | solution.py:294
  (44 shorter events, 2.0 us)
Async XLA Ops:
  0.0 14.6 %collective-permute-start = (bf16[128,768]{1,0:T(8,128)(2,1)}, bf16[128,768]{1,0:T(8,128)(2,1)S(1)}, u32[]{:S(2)}, u32[]{:S(2)}) collective-permute-start(bf16[128,768]{1,0:T(8,128)(2,1)} %refs_0_.2), channel_id=1, source_target_pairs={{0,8},{4,12},{8,0},{12,4},{1,9},{5,13},{9,1},{13,5},{2,10},{6,14},... | collective-permute-start | bytes 589832 | tf_op jit(solution)/shard_map/ppermute | solution.py:311
  4.0 0.7 %copy-start.1 = (s32[128,2]{0,1:T(2,128)S(1)}, s32[128,2]{0,1:T(2,128)}, u32[]{:S(2)}) copy-start(s32[128,2]{0,1:T(2,128)} %param.7) | copy-start | bytes 3076
  4.7 0.7 %copy-start.2 = (f32[128,2]{0,1:T(2,128)S(1)}, f32[128,2]{0,1:T(2,128)}, u32[]{:S(2)}) copy-start(f32[128,2]{0,1:T(2,128)} %param.8) | copy-start | bytes 3076
  5.6 0.9 %copy-start = (bf16[128,768]{1,0:T(8,128)(2,1)S(1)}, bf16[128,768]{1,0:T(8,128)(2,1)}, u32[]{:S(2)}) copy-start(bf16[128,768]{1,0:T(8,128)(2,1)} %refs_0_.2) | copy-start | bytes 589828
  6.8 7.8 %collective-permute-start.1 = (bf16[64,768]{1,0:T(8,128)(2,1)S(1)}, bf16[64,768]{1,0:T(8,128)(2,1)S(1)}, u32[]{:S(2)}, u32[]{:S(2)}) collective-permute-start(bf16[64,768]{1,0:T(8,128)(2,1)S(1)} %get-tuple-element.60), channel_id=1, source_target_pairs={{0,2},{1,3},{2,0},{3,1},{4,6},{5,7},{6,4},{7,5},{8,10},{9,11},{10,... | collective-permute-start | bytes 294920 | tf_op jit(solution)/shard_map/ppermute | solution.py:311
  8.3 6.3 %collective-permute-start.2 = (bf16[64,768]{1,0:T(8,128)(2,1)S(1)}, bf16[64,768]{1,0:T(8,128)(2,1)S(1)}, u32[]{:S(2)}, u32[]{:S(2)}) collective-permute-start(bf16[64,768]{1,0:T(8,128)(2,1)S(1)} %get-tuple-element.61), channel_id=1, source_target_pairs={{0,3},{1,2},{2,1},{3,0},{4,7},{5,6},{6,5},{7,4},{8,11},{9,10},{10,... | collective-permute-start | bytes 294920 | tf_op jit(solution)/shard_map/ppermute | solution.py:311
  8.3 9.2 %collective-permute-start.8 = (bf16[128,768]{1,0:T(8,128)(2,1)}, bf16[128,768]{1,0:T(8,128)(2,1)S(1)}, u32[]{:S(2)}, u32[]{:S(2)}) collective-permute-start(bf16[128,768]{1,0:T(8,128)(2,1)} %refs_0_.2), channel_id=1, source_target_pairs={{0,4},{4,0},{8,12},{12,8},{1,5},{5,1},{9,13},{13,9},{2,6},{6,2},{1... | collective-permute-start | bytes 589832 | tf_op jit(solution)/shard_map/ppermute | solution.py:311
  14.9 7.2 %collective-permute-start.3 = (bf16[128,768]{1,0:T(8,128)(2,1)S(1)}, bf16[128,768]{1,0:T(8,128)(2,1)S(1)}, u32[]{:S(2)}, u32[]{:S(2)}) collective-permute-start(bf16[128,768]{1,0:T(8,128)(2,1)S(1)} %get-tuple-element.62), channel_id=1, source_target_pairs={{0,4},{4,0},{8,12},{12,8},{1,5},{5,1},{9,13},{13,9},{2,6},{6,2},{1... | collective-permute-start | bytes 589832 | tf_op jit(solution)/shard_map/ppermute | solution.py:311
  15.4 7.0 %collective-permute-start.7 = (bf16[64,768]{1,0:T(8,128)(2,1)S(1)}, bf16[64,768]{1,0:T(8,128)(2,1)S(1)}, u32[]{:S(2)}, u32[]{:S(2)}) collective-permute-start(bf16[64,768]{1,0:T(8,128)(2,1)S(1)} %get-tuple-element.67), channel_id=1, source_target_pairs={{0,1},{1,0},{2,3},{3,2},{4,5},{5,4},{6,7},{7,6},{8,9},{9,8},{10,11... | collective-permute-start | bytes 294920 | tf_op jit(solution)/shard_map/ppermute | solution.py:311
  17.8 5.2 %collective-permute-start.9 = (bf16[64,768]{1,0:T(8,128)(2,1)S(1)}, bf16[64,768]{1,0:T(8,128)(2,1)S(1)}, u32[]{:S(2)}, u32[]{:S(2)}) collective-permute-start(bf16[64,768]{1,0:T(8,128)(2,1)S(1)} %get-tuple-element.69), channel_id=1, source_target_pairs={{0,1},{1,0},{2,3},{3,2},{4,5},{5,4},{6,7},{7,6},{8,9},{9,8},{10,11... | collective-permute-start | bytes 294920 | tf_op jit(solution)/shard_map/ppermute | solution.py:311
  18.0 6.5 %collective-permute-start.10 = (bf16[64,768]{1,0:T(8,128)(2,1)S(1)}, bf16[64,768]{1,0:T(8,128)(2,1)S(1)}, u32[]{:S(2)}, u32[]{:S(2)}) collective-permute-start(bf16[64,768]{1,0:T(8,128)(2,1)S(1)} %get-tuple-element.70), channel_id=1, source_target_pairs={{0,2},{1,3},{2,0},{3,1},{4,6},{5,7},{6,4},{7,5},{8,10},{9,11},{10,... | collective-permute-start | bytes 294920 | tf_op jit(solution)/shard_map/ppermute | solution.py:311
  19.6 5.2 %collective-permute-start.11 = (bf16[64,768]{1,0:T(8,128)(2,1)S(1)}, bf16[64,768]{1,0:T(8,128)(2,1)S(1)}, u32[]{:S(2)}, u32[]{:S(2)}) collective-permute-start(bf16[64,768]{1,0:T(8,128)(2,1)S(1)} %get-tuple-element.71), channel_id=1, source_target_pairs={{0,3},{1,2},{2,1},{3,0},{4,7},{5,6},{6,5},{7,4},{8,11},{9,10},{10,... | collective-permute-start | bytes 294920 | tf_op jit(solution)/shard_map/ppermute | solution.py:311
  22.1 4.1 %collective-permute-start.12 = (bf16[64,768]{1,0:T(8,128)(2,1)S(1)}, bf16[64,768]{1,0:T(8,128)(2,1)S(1)}, u32[]{:S(2)}, u32[]{:S(2)}) collective-permute-start(bf16[64,768]{1,0:T(8,128)(2,1)S(1)} %get-tuple-element.75), channel_id=1, source_target_pairs={{0,1},{1,0},{2,3},{3,2},{4,5},{5,4},{6,7},{7,6},{8,9},{9,8},{10,11... | collective-permute-start | bytes 294920 | tf_op jit(solution)/shard_map/ppermute | solution.py:311
  22.4 4.3 %collective-permute-start.4 = (bf16[64,768]{1,0:T(8,128)(2,1)S(1)}, bf16[64,768]{1,0:T(8,128)(2,1)S(1)}, u32[]{:S(2)}, u32[]{:S(2)}) collective-permute-start(bf16[64,768]{1,0:T(8,128)(2,1)S(1)} %get-tuple-element.64), channel_id=1, source_target_pairs={{0,1},{1,0},{2,3},{3,2},{4,5},{5,4},{6,7},{7,6},{8,9},{9,8},{10,11... | collective-permute-start | bytes 294920 | tf_op jit(solution)/shard_map/ppermute | solution.py:311
  23.0 8.4 %collective-permute-start.13 = (bf16[64,768]{1,0:T(8,128)(2,1)S(1)}, bf16[64,768]{1,0:T(8,128)(2,1)S(1)}, u32[]{:S(2)}, u32[]{:S(2)}) collective-permute-start(bf16[64,768]{1,0:T(8,128)(2,1)S(1)} %get-tuple-element.79), channel_id=1, source_target_pairs={{0,2},{1,3},{2,0},{3,1},{4,6},{5,7},{6,4},{7,5},{8,10},{9,11},{10,... | collective-permute-start | bytes 294920 | tf_op jit(solution)/shard_map/ppermute | solution.py:311
  24.5 6.9 %collective-permute-start.14 = (bf16[64,768]{1,0:T(8,128)(2,1)S(1)}, bf16[64,768]{1,0:T(8,128)(2,1)S(1)}, u32[]{:S(2)}, u32[]{:S(2)}) collective-permute-start(bf16[64,768]{1,0:T(8,128)(2,1)S(1)} %get-tuple-element.80), channel_id=1, source_target_pairs={{0,3},{1,2},{2,1},{3,0},{4,7},{5,6},{6,5},{7,4},{8,11},{9,10},{10,... | collective-permute-start | bytes 294920 | tf_op jit(solution)/shard_map/ppermute | solution.py:311
  24.8 8.7 %collective-permute-start.5 = (bf16[64,768]{1,0:T(8,128)(2,1)S(1)}, bf16[64,768]{1,0:T(8,128)(2,1)S(1)}, u32[]{:S(2)}, u32[]{:S(2)}) collective-permute-start(bf16[64,768]{1,0:T(8,128)(2,1)S(1)} %get-tuple-element.65), channel_id=1, source_target_pairs={{0,2},{1,3},{2,0},{3,1},{4,6},{5,7},{6,4},{7,5},{8,10},{9,11},{10,... | collective-permute-start | bytes 294920 | tf_op jit(solution)/shard_map/ppermute | solution.py:311
  26.2 7.6 %collective-permute-start.6 = (bf16[64,768]{1,0:T(8,128)(2,1)S(1)}, bf16[64,768]{1,0:T(8,128)(2,1)S(1)}, u32[]{:S(2)}, u32[]{:S(2)}) collective-permute-start(bf16[64,768]{1,0:T(8,128)(2,1)S(1)} %get-tuple-element.66), channel_id=1, source_target_pairs={{0,3},{1,2},{2,1},{3,0},{4,7},{5,6},{6,5},{7,4},{8,11},{9,10},{10,... | collective-permute-start | bytes 294920 | tf_op jit(solution)/shard_map/ppermute | solution.py:311
  31.4 4.5 %slice-start = ((s8[12582912]{0:T(1024)(128)(4,1)}), s8[4194304]{0:T(1024)(128)(4,1)S(1)}, s32[]{:S(2)}) async-start(s8[12582912]{0:T(1024)(128)(4,1)} %bitcast.4), calls=%async_computation | async-start | bytes 8388608
  31.4 4.5 %slice-start.1 = ((s8[12582912]{0:T(1024)(128)(4,1)}), s8[4194304]{0:T(1024)(128)(4,1)S(1)}, s32[]{:S(2)}) async-start(s8[12582912]{0:T(1024)(128)(4,1)} %bitcast.4), calls=%async_computation.1 | async-start | bytes 8388608
  33.8 2.5 %slice-start.2 = ((s8[12582912]{0:T(1024)(128)(4,1)}), s8[4194304]{0:T(1024)(128)(4,1)S(1)}, s32[]{:S(2)}) async-start(s8[12582912]{0:T(1024)(128)(4,1)} %bitcast.4), calls=%async_computation.2 | async-start | bytes 8388608
  37.3 5.0 %collective-permute-start.15 = (bf16[64,768]{1,0:T(8,128)(2,1)S(1)}, bf16[64,768]{1,0:T(8,128)(2,1)S(1)}, u32[]{:S(2)}, u32[]{:S(2)}) collective-permute-start(bf16[64,768]{1,0:T(8,128)(2,1)S(1)} %get-tuple-element.88), channel_id=1, source_target_pairs={{0,1},{1,0},{2,3},{3,2},{4,5},{5,4},{6,7},{7,6},{8,9},{9,8},{10,11... | collective-permute-start | bytes 294920 | tf_op jit(solution)/shard_map/ppermute | solution.py:311
  37.6 5.5 %collective-permute-start.16 = (bf16[64,768]{1,0:T(8,128)(2,1)S(1)}, bf16[64,768]{1,0:T(8,128)(2,1)S(1)}, u32[]{:S(2)}, u32[]{:S(2)}) collective-permute-start(bf16[64,768]{1,0:T(8,128)(2,1)S(1)} %get-tuple-element.89), channel_id=1, source_target_pairs={{0,2},{1,3},{2,0},{3,1},{4,6},{5,7},{6,4},{7,5},{8,10},{9,11},{10,... | collective-permute-start | bytes 294920 | tf_op jit(solution)/shard_map/ppermute | solution.py:311
  39.1 5.3 %collective-permute-start.17 = (bf16[64,768]{1,0:T(8,128)(2,1)S(1)}, bf16[64,768]{1,0:T(8,128)(2,1)S(1)}, u32[]{:S(2)}, u32[]{:S(2)}) collective-permute-start(bf16[64,768]{1,0:T(8,128)(2,1)S(1)} %get-tuple-element.90), channel_id=1, source_target_pairs={{0,3},{1,2},{2,1},{3,0},{4,7},{5,6},{6,5},{7,4},{8,11},{9,10},{10,... | collective-permute-start | bytes 294920 | tf_op jit(solution)/shard_map/ppermute | solution.py:311
  40.3 6.3 %collective-permute-start.26 = (bf16[64,768]{1,0:T(8,128)(2,1)S(1)}, bf16[64,768]{1,0:T(8,128)(2,1)S(1)}, u32[]{:S(2)}, u32[]{:S(2)}) collective-permute-start(bf16[64,768]{1,0:T(8,128)(2,1)S(1)} %get-tuple-element.101), channel_id=1, source_target_pairs={{0,1},{1,0},{2,3},{3,2},{4,5},{5,4},{6,7},{7,6},{8,9},{9,8},{10,11... | collective-permute-start | bytes 294920 | tf_op jit(solution)/shard_map/ppermute | solution.py:311
  40.9 7.2 %collective-permute-start.27 = (bf16[64,768]{1,0:T(8,128)(2,1)S(1)}, bf16[64,768]{1,0:T(8,128)(2,1)S(1)}, u32[]{:S(2)}, u32[]{:S(2)}) collective-permute-start(bf16[64,768]{1,0:T(8,128)(2,1)S(1)} %get-tuple-element.102), channel_id=1, source_target_pairs={{0,2},{1,3},{2,0},{3,1},{4,6},{5,7},{6,4},{7,5},{8,10},{9,11},{10,... | collective-permute-start | bytes 294920 | tf_op jit(solution)/shard_map/ppermute | solution.py:311
  42.3 6.0 %collective-permute-start.28 = (bf16[64,768]{1,0:T(8,128)(2,1)S(1)}, bf16[64,768]{1,0:T(8,128)(2,1)S(1)}, u32[]{:S(2)}, u32[]{:S(2)}) collective-permute-start(bf16[64,768]{1,0:T(8,128)(2,1)S(1)} %get-tuple-element.103), channel_id=1, source_target_pairs={{0,3},{1,2},{2,1},{3,0},{4,7},{5,6},{6,5},{7,4},{8,11},{9,10},{10,... | collective-permute-start | bytes 294920 | tf_op jit(solution)/shard_map/ppermute | solution.py:311
  44.6 7.1 %collective-permute-start.18 = (bf16[128,384]{1,0:T(8,128)(2,1)S(1)}, bf16[128,384]{1,0:T(8,128)(2,1)S(1)}, u32[]{:S(2)}, u32[]{:S(2)}) collective-permute-start(bf16[128,384]{1,0:T(8,128)(2,1)S(1)} %get-tuple-element.91.refs_0_), channel_id=1, source_target_pairs={{0,4},{4,0},{8,12},{12,8},{1,5},{5,1},{9,13},{13,9},{2,6},{6,2},{1... | collective-permute-start | bytes 294920 | tf_op jit(solution)/shard_map/ppermute | solution.py:311
  46.0 6.5 %collective-permute-start.22 = (bf16[64,768]{1,0:T(8,128)(2,1)S(1)}, bf16[64,768]{1,0:T(8,128)(2,1)S(1)}, u32[]{:S(2)}, u32[]{:S(2)}) collective-permute-start(bf16[64,768]{1,0:T(8,128)(2,1)S(1)} %get-tuple-element.97), channel_id=1, source_target_pairs={{0,1},{1,0},{2,3},{3,2},{4,5},{5,4},{6,7},{7,6},{8,9},{9,8},{10,11... | collective-permute-start | bytes 294920 | tf_op jit(solution)/shard_map/ppermute | solution.py:311
  46.6 5.9 %collective-permute-start.23 = (bf16[64,768]{1,0:T(8,128)(2,1)S(1)}, bf16[64,768]{1,0:T(8,128)(2,1)S(1)}, u32[]{:S(2)}, u32[]{:S(2)}) collective-permute-start(bf16[64,768]{1,0:T(8,128)(2,1)S(1)} %get-tuple-element.98), channel_id=1, source_target_pairs={{0,2},{1,3},{2,0},{3,1},{4,6},{5,7},{6,4},{7,5},{8,10},{9,11},{10,... | collective-permute-start | bytes 294920 | tf_op jit(solution)/shard_map/ppermute | solution.py:311
  48.1 5.1 %collective-permute-start.24 = (bf16[64,768]{1,0:T(8,128)(2,1)S(1)}, bf16[64,768]{1,0:T(8,128)(2,1)S(1)}, u32[]{:S(2)}, u32[]{:S(2)}) collective-permute-start(bf16[64,768]{1,0:T(8,128)(2,1)S(1)} %get-tuple-element.99), channel_id=1, source_target_pairs={{0,3},{1,2},{2,1},{3,0},{4,7},{5,6},{6,5},{7,4},{8,11},{9,10},{10,... | collective-permute-start | bytes 294920 | tf_op jit(solution)/shard_map/ppermute | solution.py:311
  48.4 9.7 %collective-permute-start.30 = (bf16[128,384]{1,0:T(8,128)(2,1)S(1)}, bf16[128,384]{1,0:T(8,128)(2,1)S(1)}, u32[]{:S(2)}, u32[]{:S(2)}) collective-permute-start(bf16[128,384]{1,0:T(8,128)(2,1)S(1)} %get-tuple-element.104), channel_id=1, source_target_pairs={{0,12},{4,8},{8,4},{12,0},{1,13},{5,9},{9,5},{13,1},{2,14},{6,10},... | collective-permute-start | bytes 294920 | tf_op jit(solution)/shard_map/ppermute | solution.py:311
  52.1 14.0 %collective-permute-start.29 = (bf16[128,768]{1,0:T(8,128)(2,1)S(1)}, bf16[128,768]{1,0:T(8,128)(2,1)S(1)}, u32[]{:S(2)}, u32[]{:S(2)}) collective-permute-start(bf16[128,768]{1,0:T(8,128)(2,1)S(1)} %combine.6), channel_id=1, source_target_pairs={{0,8},{4,12},{8,0},{12,4},{1,9},{5,13},{9,1},{13,5},{2,10},{6,14},... | collective-permute-start | bytes 589832 | tf_op jit(solution)/shard_map/ppermute | solution.py:311
  53.5 12.5 %collective-permute-start.25 = (bf16[128,768]{1,0:T(8,128)(2,1)S(1)}, bf16[128,768]{1,0:T(8,128)(2,1)S(1)}, u32[]{:S(2)}, u32[]{:S(2)}) collective-permute-start(bf16[128,768]{1,0:T(8,128)(2,1)S(1)} %combine.5), channel_id=1, source_target_pairs={{0,4},{4,0},{8,12},{12,8},{1,5},{5,1},{9,13},{13,9},{2,6},{6,2},{1... | collective-permute-start | bytes 589832 | tf_op jit(solution)/shard_map/ppermute | solution.py:311
  56.4 1.9 %collective-permute-start.19 = (bf16[64,768]{1,0:T(8,128)(2,1)S(1)}, bf16[64,768]{1,0:T(8,128)(2,1)S(1)}, u32[]{:S(2)}, u32[]{:S(2)}) collective-permute-start(bf16[64,768]{1,0:T(8,128)(2,1)S(1)} %get-tuple-element.93), channel_id=1, source_target_pairs={{0,1},{1,0},{2,3},{3,2},{4,5},{5,4},{6,7},{7,6},{8,9},{9,8},{10,11... | collective-permute-start | bytes 294920 | tf_op jit(solution)/shard_map/ppermute | solution.py:311
  56.5 5.6 %collective-permute-start.20 = (bf16[64,768]{1,0:T(8,128)(2,1)S(1)}, bf16[64,768]{1,0:T(8,128)(2,1)S(1)}, u32[]{:S(2)}, u32[]{:S(2)}) collective-permute-start(bf16[64,768]{1,0:T(8,128)(2,1)S(1)} %get-tuple-element.94), channel_id=1, source_target_pairs={{0,2},{1,3},{2,0},{3,1},{4,6},{5,7},{6,4},{7,5},{8,10},{9,11},{10,... | collective-permute-start | bytes 294920 | tf_op jit(solution)/shard_map/ppermute | solution.py:311
  58.1 5.3 %collective-permute-start.21 = (bf16[64,768]{1,0:T(8,128)(2,1)S(1)}, bf16[64,768]{1,0:T(8,128)(2,1)S(1)}, u32[]{:S(2)}, u32[]{:S(2)}) collective-permute-start(bf16[64,768]{1,0:T(8,128)(2,1)S(1)} %get-tuple-element.95), channel_id=1, source_target_pairs={{0,3},{1,2},{2,1},{3,0},{4,7},{5,6},{6,5},{7,4},{8,11},{9,10},{10,... | collective-permute-start | bytes 294920 | tf_op jit(solution)/shard_map/ppermute | solution.py:311

commit v16 on v15

--- a/solution.py
+++ b/solution.py
@@ -322,8 +322,8 @@
     width = own_width if doubling else own_width * shards
 
     if doubling:
-        slices = [tokens, swap(tokens, "tensor", 1), swap(tokens, "tensor", 2)]
-        parts = [across(distance) for distance in range(4)]
+        slices = [tokens, swap(tokens, "tensor", 2), swap(tokens, "tensor", 1)]
+        parts = [across(distance) for distance in (0, 2, 1, 3)]
     else:
         slices = [lax.all_gather(tokens, "tensor", axis=1, tiled=True)]
         parts = [everything]
@@ -332,8 +332,14 @@
     fetches = [(w, part, width) for part in parts for w in (gate_weight, up_weight)]
     arrived, weights = [], []
     for i in range(len(parts)):
-        echo = i == 2
-        after = pinned(weights[:1]) + (arrived[0][2:] if echo else [])
+        echo = i == 1
+        after = pinned(weights[:1])
+        if echo:
+            after += arrived[0][2:]
+        elif i == 2:
+            after += arrived[1][1:2]
+        elif i == 3:
+            after += arrived[2][2:]
         outgoing = dispatch(placed, [slices[i]], experts, capacity, after, echo)
         blocks = outgoing[:experts]
         arrived.append([swap(block, "expert", e) for e, block in enumerate(blocks)])
@@ -345,7 +351,7 @@
     for group in [slice(0, 2), slice(2, 3), slice(3, 4)][: max(1, len(parts) - 1)]:
         first = sums is None
         last = group.stop >= len(parts)
-        after = arrived[2][1:2] + arrived[3][1:2] if first and not last else []
+        after = arrived[2][1:2] if first and not last else []
         chosen = weights[2 * group.start : 2 * group.stop]
         later = fetches[4:] if first else []
         sums, brought = gate_up(column, arrived[group], chosen, sums, last, after, later)

time: 67.3 us -> 69.5 us (1.033)
  starting transfers between devices: 27.7 us -> 30.2 us
    ppermute x31, starting transfers between devices: 27.7 us -> 30.2 us  [swap(): return lax.ppermute(value, axis, [(i, i ^ distance) for i in range(count)])]
  transfers between devices with their start and end apart: 31 -> 31, of which waited for: 11 -> 10; matrix products, arithmetic and copies ran while one was open for 0% -> 0% of each run, Pallas kernels for 25% -> 24%
where the time goes in v16:
time: 69.5 us; the launch traced here: 69.3 us
  starting transfers between devices  30.2 us (43%)
  Pallas kernels  20.9 us (30%)
  waiting for transfers between devices  15.1 us (22%)
  local copies, waits for them, and re-layouts  2.86 us (4%)
    ppermute x31, starting transfers between devices, swap(): return lax.ppermute(value, axis, [(i, i ^ distance) for i in range(count)])  30.2 us
    ppermute x31, waiting for transfers between devices, swap(): return lax.ppermute(value, axis, [(i, i ^ distance) for i in range(count)])  15.1 us
    pallas_call x3, Pallas kernels, gate_up(): pl.pallas_call(functools.partial(gate_up_kernel, experts=experts, slices=...  8.9 us
    pallas_call x1, Pallas kernels, prefetch(): pl.pallas_call(functools.partial(prefetch_kernel, parts=[part for _, part...  4.72 us
    pallas_call x4, Pallas kernels, down(): pl.pallas_call(functools.partial(down_kernel, part=part, waits=len(after)...  4.1 us
    unnamed x12, local copies, waits for them, and re-layouts  2.86 us
    pallas_call x4, Pallas kernels, combine(): pl.pallas_call(functools.partial(combine_kernel, experts=len(blocks), sta...  1.94 us
  transfers between devices with their start and end apart: 31, of which 10 were waited for; matrix products, arithmetic and copies ran while one was open for 0% of the time, Pallas kernels for 24%

profile of v16, /device:TPU:0, one launch (start us, length us, event | category | flops | bytes accessed | tf_op | source)
XLA Modules:
  0.0 69.3 jit_solution(15076610731966927018)
XLA Ops:
  0.0 4.0 %collective-permute-start = (bf16[128,768]{1,0:T(8,128)(2,1)}, bf16[128,768]{1,0:T(8,128)(2,1)S(1)}, u32[]{:S(2)}, u32[]{:S(2)}) collective-permute-start(bf16[128,768]{1,0:T(8,128)(2,1)} %refs_0_.2), channel_id=1, source_target_pairs={{0,8},{4,12},{8,0},{12,4},{1,9},{5,13},{9,1},{13,5},{2,10},{6,14},... | collective-permute-start | bytes 589832 | tf_op jit(solution)/shard_map/ppermute | solution.py:311
  4.0 0.7 copy-done.1
  4.7 0.7 copy-done.2
  5.6 0.9 %copy-done = bf16[128,768]{1,0:T(8,128)(2,1)S(1)} copy-done((bf16[128,768]{1,0:T(8,128)(2,1)S(1)}, bf16[128,768]{1,0:T(8,128)(2,1)}, u32[]{:S(2)}) %copy-start) | copy-done | bytes 196632
  6.8 1.6 %collective-permute-start.1 = (bf16[64,768]{1,0:T(8,128)(2,1)S(1)}, bf16[64,768]{1,0:T(8,128)(2,1)S(1)}, u32[]{:S(2)}, u32[]{:S(2)}) collective-permute-start(bf16[64,768]{1,0:T(8,128)(2,1)S(1)} %get-tuple-element.60), channel_id=1, source_target_pairs={{0,2},{1,3},{2,0},{3,1},{4,6},{5,7},{6,4},{7,5},{8,10},{9,11},{10,... | collective-permute-start | bytes 294920 | tf_op jit(solution)/shard_map/ppermute | solution.py:311
  8.3 1.6 %collective-permute-start.4 = (bf16[128,768]{1,0:T(8,128)(2,1)}, bf16[128,768]{1,0:T(8,128)(2,1)S(1)}, u32[]{:S(2)}, u32[]{:S(2)}) collective-permute-start(bf16[128,768]{1,0:T(8,128)(2,1)} %refs_0_.2), channel_id=1, source_target_pairs={{0,4},{4,0},{8,12},{12,8},{1,5},{5,1},{9,13},{13,9},{2,6},{6,2},{1... | collective-permute-start | bytes 589832 | tf_op jit(solution)/shard_map/ppermute | solution.py:311
  9.9 4.7 %prefetch.1 = (bf16[768,2048]{1,0:T(8,128)(2,1)S(1)}, bf16[768,2048]{1,0:T(8,128)(2,1)S(1)}, bf16[768,2048]{1,0:T(8,128)(2,1)S(1)}, bf16[768,2048]{1,0:T(8,128)(2,1)S(1)}) custom-call(s32[1]{0:T(128)} %bitcast.3.column_ref, bf16[64,768]{1,0:T(8,128)(2,1)S(1)} %get-tuple-element.58.after_ref.refs_0_, bf16[1,3072,2048]{2,1,0:T(8,128)(2,1)} %refs_15_.1, ...), custom_call_target="tpu_custom_call" | custom-call | bytes 12582912 | tf_op jit(solution)/shard_map/prefetch/pallas_call | solution.py:133
  14.9 0.4 collective-permute-start.5
  15.4 0.4 collective-permute-start.3
  15.8 1.8 %collective-permute-done.4.refs_0_ = bf16[128,768]{1,0:T(8,128)(2,1)S(1)} collective-permute-done((bf16[128,768]{1,0:T(8,128)(2,1)}, bf16[128,768]{1,0:T(8,128)(2,1)S(1)}, u32[]{:S(2)}, u32[]{:S(2)}) %collective-permute-start.4) | collective-permute-done | bytes 196640 | tf_op jit(solution)/shard_map/ppermute | solution.py:311
  17.8 1.6 %collective-permute-start.6 = (bf16[64,768]{1,0:T(8,128)(2,1)S(1)}, bf16[64,768]{1,0:T(8,128)(2,1)S(1)}, u32[]{:S(2)}, u32[]{:S(2)}) collective-permute-start(bf16[64,768]{1,0:T(8,128)(2,1)S(1)} %get-tuple-element.64), channel_id=1, source_target_pairs={{0,2},{1,3},{2,0},{3,1},{4,6},{5,7},{6,4},{7,5},{8,10},{9,11},{10,... | collective-permute-start | bytes 294920 | tf_op jit(solution)/shard_map/ppermute | solution.py:311
  19.4 0.6 collective-permute-start.11
  20.1 1.5 %collective-permute-start.12 = (bf16[64,768]{1,0:T(8,128)(2,1)S(1)}, bf16[64,768]{1,0:T(8,128)(2,1)S(1)}, u32[]{:S(2)}, u32[]{:S(2)}) collective-permute-start(bf16[64,768]{1,0:T(8,128)(2,1)S(1)} %get-tuple-element.72), channel_id=1, source_target_pairs={{0,2},{1,3},{2,0},{3,1},{4,6},{5,7},{6,4},{7,5},{8,10},{9,11},{10,... | collective-permute-start | bytes 294920 | tf_op jit(solution)/shard_map/ppermute | solution.py:311
  21.6 1.4 %collective-permute-done.6.refs_2_ = bf16[64,768]{1,0:T(8,128)(2,1)S(1)} collective-permute-done((bf16[64,768]{1,0:T(8,128)(2,1)S(1)}, bf16[64,768]{1,0:T(8,128)(2,1)S(1)}, u32[]{:S(2)}, u32[]{:S(2)}) %collective-permute-start.6) | collective-permute-done | bytes 98336 | tf_op jit(solution)/shard_map/ppermute | solution.py:311
  23.1 1.6 %collective-permute-done.7.refs_3_ = bf16[64,768]{1,0:T(8,128)(2,1)S(1)} collective-permute-done((bf16[64,768]{1,0:T(8,128)(2,1)S(1)}, bf16[64,768]{1,0:T(8,128)(2,1)S(1)}, u32[]{:S(2)}, u32[]{:S(2)}) %collective-permute-start.7) | collective-permute-done | bytes 98336 | tf_op jit(solution)/shard_map/ppermute | solution.py:311
  24.7 0.5 collective-permute-start.14
  25.5 1.5 %collective-permute-start.10 = (bf16[64,768]{1,0:T(8,128)(2,1)S(1)}, bf16[64,768]{1,0:T(8,128)(2,1)S(1)}, u32[]{:S(2)}, u32[]{:S(2)}) collective-permute-start(bf16[64,768]{1,0:T(8,128)(2,1)S(1)} %get-tuple-element.69), channel_id=1, source_target_pairs={{0,3},{1,2},{2,1},{3,0},{4,7},{5,6},{6,5},{7,4},{8,11},{9,10},{10,... | collective-permute-start | bytes 294920 | tf_op jit(solution)/shard_map/ppermute | solution.py:311
  27.0 0.5 collective-permute-start.8
  27.5 1.3 %collective-permute-start.9 = (bf16[64,768]{1,0:T(8,128)(2,1)S(1)}, bf16[64,768]{1,0:T(8,128)(2,1)S(1)}, u32[]{:S(2)}, u32[]{:S(2)}) collective-permute-start(bf16[64,768]{1,0:T(8,128)(2,1)S(1)} %get-tuple-element.68), channel_id=1, source_target_pairs={{0,2},{1,3},{2,0},{3,1},{4,6},{5,7},{6,4},{7,5},{8,10},{9,11},{10,... | collective-permute-start | bytes 294920 | tf_op jit(solution)/shard_map/ppermute | solution.py:311
  28.8 4.7 %gate_up.3 = (f32[256,2048]{1,0:T(8,128)S(1)}, f32[256,2048]{1,0:T(8,128)S(1)}, bf16[768,2048]{1,0:T(8,128)(2,1)S(1)}, bf16[768,2048]{1,0:T(8,128)(2,1)S(1)}, bf...) custom-call(s32[1]{0:T(128)} %bitcast.3.column_ref, bf16[64,768]{1,0:T(8,128)(2,1)S(1)} %get-tuple-element.58.after_ref.refs_0_, ...), custom_call_target="tpu_custom_call" | custom-call | flops 3221225472 | bytes 12582912 | tf_op jit(solution)/shard_map/gate_up/pallas_call | solution.py:215
  33.5 2.1 %gate_up.4 = (f32[256,2048]{1,0:T(8,128)S(1)}, f32[256,2048]{1,0:T(8,128)S(1)}) custom-call(s32[1]{0:T(128)} %bitcast.3.column_ref, bf16[64,768]{1,0:T(8,128)(2,1)S(1)} %get-tuple-element.80.refs_0_, bf16[64,768]{1,0:T(8,128)(2,1)S(1)} %collective-permute-done.14.refs_12_.refs_1_, ...), custom_call_target="tpu_custom_call", output_to_operand_aliasing={{0}: (7, {}), {1}: (8, {})} | custom-call | flops 1610612736 | bytes 6291456 | tf_op jit(solution)/shard_map/gate_up/pallas_call | solution.py:215
  35.7 2.1 %gate_up.5.h_ref = bf16[256,2048]{1,0:T(8,128)(2,1)S(1)} custom-call(s32[1]{0:T(128)} %bitcast.3.column_ref, bf16[64,768]{1,0:T(8,128)(2,1)S(1)} %get-tuple-element.66.refs_0_, bf16[64,768]{1,0:T(8,128)(2,1)S(1)} %collective-permute-done.8.refs_1_, bf16[64,768]{1,0:T(8,128)(2,1)S(1)} %collective-permute-done.9.refs_2_, ...), custom_call_target="tpu_custom_call" | custom-call | flops 1610612736 | bytes 6291456 | tf_op jit(solution)/shard_map/gate_up/pallas_call | solution.py:215
  37.8 0.6 slice-done.2
  38.4 1.0 %down.4 = (bf16[64,768]{1,0:T(8,128)(2,1)S(1)}, bf16[64,768]{1,0:T(8,128)(2,1)S(1)}, bf16[64,768]{1,0:T(8,128)(2,1)S(1)}, bf16[64,768]{1,0:T(8,128)(2,1)S(1)}) custom-call(s32[1]{0:T(128)} %bitcast.3.column_ref, bf16[256,2048]{1,0:T(8,128)(2,1)S(1)} %gate_up.5.h_ref, bf16[1,2048,3072]{2,1,0:T(8,128)(2,1)S(1)} %bitcast.5), custom_call_target="tpu_custom_call" | custom-call | flops 805306368 | bytes 3538944 | tf_op jit(solution)/shard_map/down/pallas_call | solution.py:257
  39.4 0.7 collective-permute-start.15
  40.1 1.5 %collective-permute-start.16 = (bf16[64,768]{1,0:T(8,128)(2,1)S(1)}, bf16[64,768]{1,0:T(8,128)(2,1)S(1)}, u32[]{:S(2)}, u32[]{:S(2)}) collective-permute-start(bf16[64,768]{1,0:T(8,128)(2,1)S(1)} %get-tuple-element.89), channel_id=1, source_target_pairs={{0,2},{1,3},{2,0},{3,1},{4,6},{5,7},{6,4},{7,5},{8,10},{9,11},{10,... | collective-permute-start | bytes 294920 | tf_op jit(solution)/shard_map/ppermute | solution.py:311
  41.6 1.0 %down.7 = (bf16[64,768]{1,0:T(8,128)(2,1)S(1)}, bf16[64,768]{1,0:T(8,128)(2,1)S(1)}, bf16[64,768]{1,0:T(8,128)(2,1)S(1)}, bf16[64,768]{1,0:T(8,128)(2,1)S(1)}) custom-call(s32[1]{0:T(128)} %bitcast.3.column_ref, bf16[256,2048]{1,0:T(8,128)(2,1)S(1)} %gate_up.5.h_ref, bf16[1,2048,3072]{2,1,0:T(8,128)(2,1)S(1)} %bitcast.5), custom_call_target="tpu_custom_call" | custom-call | flops 805306368 | bytes 3538944 | tf_op jit(solution)/shard_map/down/pallas_call | solution.py:257
  42.6 0.7 %collective-permute-start.26 = (bf16[64,768]{1,0:T(8,128)(2,1)S(1)}, bf16[64,768]{1,0:T(8,128)(2,1)S(1)}, u32[]{:S(2)}, u32[]{:S(2)}) collective-permute-start(bf16[64,768]{1,0:T(8,128)(2,1)S(1)} %get-tuple-element.101), channel_id=1, source_target_pairs={{0,1},{1,0},{2,3},{3,2},{4,5},{5,4},{6,7},{7,6},{8,9},{9,8},{10,11... | collective-permute-start | bytes 294920 | tf_op jit(solution)/shard_map/ppermute | solution.py:311
  43.4 1.5 %collective-permute-start.27 = (bf16[64,768]{1,0:T(8,128)(2,1)S(1)}, bf16[64,768]{1,0:T(8,128)(2,1)S(1)}, u32[]{:S(2)}, u32[]{:S(2)}) collective-permute-start(bf16[64,768]{1,0:T(8,128)(2,1)S(1)} %get-tuple-element.102), channel_id=1, source_target_pairs={{0,2},{1,3},{2,0},{3,1},{4,6},{5,7},{6,4},{7,5},{8,10},{9,11},{10,... | collective-permute-start | bytes 294920 | tf_op jit(solution)/shard_map/ppermute | solution.py:311
  44.8 0.4 collective-permute-done.16.refs_2_
  45.2 1.6 %collective-permute-done.17.refs_3_ = bf16[64,768]{1,0:T(8,128)(2,1)S(1)} collective-permute-done((bf16[64,768]{1,0:T(8,128)(2,1)S(1)}, bf16[64,768]{1,0:T(8,128)(2,1)S(1)}, u32[]{:S(2)}, u32[]{:S(2)}) %collective-permute-start.17) | collective-permute-done | bytes 98336 | tf_op jit(solution)/shard_map/ppermute | solution.py:311
  46.9 0.3 combine.4
  47.2 1.0 %down.6 = (bf16[64,768]{1,0:T(8,128)(2,1)S(1)}, bf16[64,768]{1,0:T(8,128)(2,1)S(1)}, bf16[64,768]{1,0:T(8,128)(2,1)S(1)}, bf16[64,768]{1,0:T(8,128)(2,1)S(1)}) custom-call(s32[1]{0:T(128)} %bitcast.3.column_ref, bf16[256,2048]{1,0:T(8,128)(2,1)S(1)} %gate_up.5.h_ref, bf16[1,2048,3072]{2,1,0:T(8,128)(2,1)S(1)} %bitcast.5, ...), custom_call_target="tpu_custom_call" | custom-call | flops 805306368 | bytes 3538944 | tf_op jit(solution)/shard_map/down/pallas_call | solution.py:257
  48.3 0.4 collective-permute-start.22
  48.6 2.0 %collective-permute-start.23 = (bf16[64,768]{1,0:T(8,128)(2,1)S(1)}, bf16[64,768]{1,0:T(8,128)(2,1)S(1)}, u32[]{:S(2)}, u32[]{:S(2)}) collective-permute-start(bf16[64,768]{1,0:T(8,128)(2,1)S(1)} %get-tuple-element.98), channel_id=1, source_target_pairs={{0,2},{1,3},{2,0},{3,1},{4,6},{5,7},{6,4},{7,5},{8,10},{9,11},{10,... | collective-permute-start | bytes 294920 | tf_op jit(solution)/shard_map/ppermute | solution.py:311
  50.9 3.5 %collective-permute-start.30 = (bf16[128,384]{1,0:T(8,128)(2,1)S(1)}, bf16[128,384]{1,0:T(8,128)(2,1)S(1)}, u32[]{:S(2)}, u32[]{:S(2)}) collective-permute-start(bf16[128,384]{1,0:T(8,128)(2,1)S(1)} %get-tuple-element.104), channel_id=1, source_target_pairs={{0,12},{4,8},{8,4},{12,0},{1,13},{5,9},{9,5},{13,1},{2,14},{6,10},... | collective-permute-start | bytes 294920 | tf_op jit(solution)/shard_map/ppermute | solution.py:311
  54.4 0.3 combine.6
  54.7 0.4 collective-permute-start.29
  55.1 0.7 collective-permute-done.24.refs_3_
  55.8 0.3 combine.5
  56.1 1.8 %collective-permute-start.25 = (bf16[128,768]{1,0:T(8,128)(2,1)S(1)}, bf16[128,768]{1,0:T(8,128)(2,1)S(1)}, u32[]{:S(2)}, u32[]{:S(2)}) collective-permute-start(bf16[128,768]{1,0:T(8,128)(2,1)S(1)} %combine.5), channel_id=1, source_target_pairs={{0,4},{4,0},{8,12},{12,8},{1,5},{5,1},{9,13},{13,9},{2,6},{6,2},{1... | collective-permute-start | bytes 589832 | tf_op jit(solution)/shard_map/ppermute | solution.py:311
  57.9 1.0 %down.5 = (bf16[64,768]{1,0:T(8,128)(2,1)S(1)}, bf16[64,768]{1,0:T(8,128)(2,1)S(1)}, bf16[64,768]{1,0:T(8,128)(2,1)S(1)}, bf16[64,768]{1,0:T(8,128)(2,1)S(1)}) custom-call(s32[1]{0:T(128)} %bitcast.3.column_ref, bf16[256,2048]{1,0:T(8,128)(2,1)S(1)} %gate_up.5.h_ref, bf16[1,2048,3072]{2,1,0:T(8,128)(2,1)S(1)} %bitcast.5, ...), custom_call_target="tpu_custom_call" | custom-call | flops 805306368 | bytes 3538944 | tf_op jit(solution)/shard_map/down/pallas_call | solution.py:257
  59.0 1.6 %collective-permute-start.20 = (bf16[64,768]{1,0:T(8,128)(2,1)S(1)}, bf16[64,768]{1,0:T(8,128)(2,1)S(1)}, u32[]{:S(2)}, u32[]{:S(2)}) collective-permute-start(bf16[64,768]{1,0:T(8,128)(2,1)S(1)} %get-tuple-element.94), channel_id=1, source_target_pairs={{0,2},{1,3},{2,0},{3,1},{4,6},{5,7},{6,4},{7,5},{8,10},{9,11},{10,... | collective-permute-start | bytes 294920 | tf_op jit(solution)/shard_map/ppermute | solution.py:311
  60.6 0.3 collective-permute-start.21
  60.9 3.8 %collective-permute-done.20.refs_2_ = bf16[64,768]{1,0:T(8,128)(2,1)S(1)} collective-permute-done((bf16[64,768]{1,0:T(8,128)(2,1)S(1)}, bf16[64,768]{1,0:T(8,128)(2,1)S(1)}, u32[]{:S(2)}, u32[]{:S(2)}) %collective-permute-start.20) | collective-permute-done | bytes 98336 | tf_op jit(solution)/shard_map/ppermute | solution.py:311
  64.7 1.2 %collective-permute-done.21.refs_3_ = bf16[64,768]{1,0:T(8,128)(2,1)S(1)} collective-permute-done((bf16[64,768]{1,0:T(8,128)(2,1)S(1)}, bf16[64,768]{1,0:T(8,128)(2,1)S(1)}, u32[]{:S(2)}, u32[]{:S(2)}) %collective-permute-start.21) | collective-permute-done | bytes 98336 | tf_op jit(solution)/shard_map/ppermute | solution.py:311
  65.9 2.4 %collective-permute-done.29.refs_5_ = bf16[128,768]{1,0:T(8,128)(2,1)S(1)} collective-permute-done((bf16[128,768]{1,0:T(8,128)(2,1)S(1)}, bf16[128,768]{1,0:T(8,128)(2,1)S(1)}, u32[]{:S(2)}, u32[]{:S(2)}) %collective-permute-start.29) | collective-permute-done | bytes 196640 | tf_op jit(solution)/shard_map/ppermute | solution.py:311
  68.3 1.0 %combine.7 = bf16[128,768]{1,0:T(8,128)(2,1)} custom-call(bf16[256,256]{1,0:T(8,128)(2,1)S(1)} %get-tuple-element.55.pick_ref, f32[128,2]{1,0:T(8,128)S(1)} %get-tuple-element.56.mix_ref, bf16[64,768]{1,0:T(8,128)(2,1)S(1)} %get-tuple-element.92.refs_0_, bf16[64,768]{1,0:T(8,128)(2,1)S(1)} %collective-permute-done.19.refs_1_, ...), custom_call_target="tpu_custom_call" | custom-call | flops 100663296 | bytes 589824 | tf_op jit(solution)/shard_map/combine/pallas_call | solution.py:294
  (44 shorter events, 1.8 us)
Async XLA Ops:
  0.0 14.7 %collective-permute-start = (bf16[128,768]{1,0:T(8,128)(2,1)}, bf16[128,768]{1,0:T(8,128)(2,1)S(1)}, u32[]{:S(2)}, u32[]{:S(2)}) collective-permute-start(bf16[128,768]{1,0:T(8,128)(2,1)} %refs_0_.2), channel_id=1, source_target_pairs={{0,8},{4,12},{8,0},{12,4},{1,9},{5,13},{9,1},{13,5},{2,10},{6,14},... | collective-permute-start | bytes 589832 | tf_op jit(solution)/shard_map/ppermute | solution.py:311
  4.0 0.7 copy-start.1
  4.7 0.7 copy-start.2
  5.6 0.9 %copy-start = (bf16[128,768]{1,0:T(8,128)(2,1)S(1)}, bf16[128,768]{1,0:T(8,128)(2,1)}, u32[]{:S(2)}) copy-start(bf16[128,768]{1,0:T(8,128)(2,1)} %refs_0_.2) | copy-start | bytes 589828
  6.8 7.9 %collective-permute-start.1 = (bf16[64,768]{1,0:T(8,128)(2,1)S(1)}, bf16[64,768]{1,0:T(8,128)(2,1)S(1)}, u32[]{:S(2)}, u32[]{:S(2)}) collective-permute-start(bf16[64,768]{1,0:T(8,128)(2,1)S(1)} %get-tuple-element.60), channel_id=1, source_target_pairs={{0,2},{1,3},{2,0},{3,1},{4,6},{5,7},{6,4},{7,5},{8,10},{9,11},{10,... | collective-permute-start | bytes 294920 | tf_op jit(solution)/shard_map/ppermute | solution.py:311
  8.3 6.3 %collective-permute-start.2 = (bf16[64,768]{1,0:T(8,128)(2,1)S(1)}, bf16[64,768]{1,0:T(8,128)(2,1)S(1)}, u32[]{:S(2)}, u32[]{:S(2)}) collective-permute-start(bf16[64,768]{1,0:T(8,128)(2,1)S(1)} %get-tuple-element.61), channel_id=1, source_target_pairs={{0,3},{1,2},{2,1},{3,0},{4,7},{5,6},{6,5},{7,4},{8,11},{9,10},{10,... | collective-permute-start | bytes 294920 | tf_op jit(solution)/shard_map/ppermute | solution.py:311
  8.3 9.2 %collective-permute-start.4 = (bf16[128,768]{1,0:T(8,128)(2,1)}, bf16[128,768]{1,0:T(8,128)(2,1)S(1)}, u32[]{:S(2)}, u32[]{:S(2)}) collective-permute-start(bf16[128,768]{1,0:T(8,128)(2,1)} %refs_0_.2), channel_id=1, source_target_pairs={{0,4},{4,0},{8,12},{12,8},{1,5},{5,1},{9,13},{13,9},{2,6},{6,2},{1... | collective-permute-start | bytes 589832 | tf_op jit(solution)/shard_map/ppermute | solution.py:311
  14.9 2.6 %collective-permute-start.5 = (bf16[64,768]{1,0:T(8,128)(2,1)S(1)}, bf16[64,768]{1,0:T(8,128)(2,1)S(1)}, u32[]{:S(2)}, u32[]{:S(2)}) collective-permute-start(bf16[64,768]{1,0:T(8,128)(2,1)S(1)} %get-tuple-element.63), channel_id=1, source_target_pairs={{0,1},{1,0},{2,3},{3,2},{4,5},{5,4},{6,7},{7,6},{8,9},{9,8},{10,11... | collective-permute-start | bytes 294920 | tf_op jit(solution)/shard_map/ppermute | solution.py:311
  15.4 9.8 %collective-permute-start.3 = (bf16[128,768]{1,0:T(8,128)(2,1)S(1)}, bf16[128,768]{1,0:T(8,128)(2,1)S(1)}, u32[]{:S(2)}, u32[]{:S(2)}) collective-permute-start(bf16[128,768]{1,0:T(8,128)(2,1)S(1)} %get-tuple-element.62), channel_id=1, source_target_pairs={{0,4},{4,0},{8,12},{12,8},{1,5},{5,1},{9,13},{13,9},{2,6},{6,2},{1... | collective-permute-start | bytes 589832 | tf_op jit(solution)/shard_map/ppermute | solution.py:311
  17.8 5.1 %collective-permute-start.6 = (bf16[64,768]{1,0:T(8,128)(2,1)S(1)}, bf16[64,768]{1,0:T(8,128)(2,1)S(1)}, u32[]{:S(2)}, u32[]{:S(2)}) collective-permute-start(bf16[64,768]{1,0:T(8,128)(2,1)S(1)} %get-tuple-element.64), channel_id=1, source_target_pairs={{0,2},{1,3},{2,0},{3,1},{4,6},{5,7},{6,4},{7,5},{8,10},{9,11},{10,... | collective-permute-start | bytes 294920 | tf_op jit(solution)/shard_map/ppermute | solution.py:311
  19.4 5.3 %collective-permute-start.7 = (bf16[64,768]{1,0:T(8,128)(2,1)S(1)}, bf16[64,768]{1,0:T(8,128)(2,1)S(1)}, u32[]{:S(2)}, u32[]{:S(2)}) collective-permute-start(bf16[64,768]{1,0:T(8,128)(2,1)S(1)} %get-tuple-element.65), channel_id=1, source_target_pairs={{0,3},{1,2},{2,1},{3,0},{4,7},{5,6},{6,5},{7,4},{8,11},{9,10},{10,... | collective-permute-start | bytes 294920 | tf_op jit(solution)/shard_map/ppermute | solution.py:311
  19.4 7.5 %collective-permute-start.11 = (bf16[64,768]{1,0:T(8,128)(2,1)S(1)}, bf16[64,768]{1,0:T(8,128)(2,1)S(1)}, u32[]{:S(2)}, u32[]{:S(2)}) collective-permute-start(bf16[64,768]{1,0:T(8,128)(2,1)S(1)} %get-tuple-element.70), channel_id=1, source_target_pairs={{0,1},{1,0},{2,3},{3,2},{4,5},{5,4},{6,7},{7,6},{8,9},{9,8},{10,11... | collective-permute-start | bytes 294920 | tf_op jit(solution)/shard_map/ppermute | solution.py:311
  20.1 7.4 %collective-permute-start.12 = (bf16[64,768]{1,0:T(8,128)(2,1)S(1)}, bf16[64,768]{1,0:T(8,128)(2,1)S(1)}, u32[]{:S(2)}, u32[]{:S(2)}) collective-permute-start(bf16[64,768]{1,0:T(8,128)(2,1)S(1)} %get-tuple-element.72), channel_id=1, source_target_pairs={{0,2},{1,3},{2,0},{3,1},{4,6},{5,7},{6,4},{7,5},{8,10},{9,11},{10,... | collective-permute-start | bytes 294920 | tf_op jit(solution)/shard_map/ppermute | solution.py:311
  23.0 5.8 %collective-permute-start.13 = (bf16[64,768]{1,0:T(8,128)(2,1)S(1)}, bf16[64,768]{1,0:T(8,128)(2,1)S(1)}, u32[]{:S(2)}, u32[]{:S(2)}) collective-permute-start(bf16[64,768]{1,0:T(8,128)(2,1)S(1)} %get-tuple-element.73), channel_id=1, source_target_pairs={{0,3},{1,2},{2,1},{3,0},{4,7},{5,6},{6,5},{7,4},{8,11},{9,10},{10,... | collective-permute-start | bytes 294920 | tf_op jit(solution)/shard_map/ppermute | solution.py:311
  24.7 4.1 %collective-permute-start.14 = (bf16[64,768]{1,0:T(8,128)(2,1)S(1)}, bf16[64,768]{1,0:T(8,128)(2,1)S(1)}, u32[]{:S(2)}, u32[]{:S(2)}) collective-permute-start(bf16[64,768]{1,0:T(8,128)(2,1)S(1)} %get-tuple-element.77), channel_id=1, source_target_pairs={{0,1},{1,0},{2,3},{3,2},{4,5},{5,4},{6,7},{7,6},{8,9},{9,8},{10,11... | collective-permute-start | bytes 294920 | tf_op jit(solution)/shard_map/ppermute | solution.py:311
  25.5 10.2 %collective-permute-start.10 = (bf16[64,768]{1,0:T(8,128)(2,1)S(1)}, bf16[64,768]{1,0:T(8,128)(2,1)S(1)}, u32[]{:S(2)}, u32[]{:S(2)}) collective-permute-start(bf16[64,768]{1,0:T(8,128)(2,1)S(1)} %get-tuple-element.69), channel_id=1, source_target_pairs={{0,3},{1,2},{2,1},{3,0},{4,7},{5,6},{6,5},{7,4},{8,11},{9,10},{10,... | collective-permute-start | bytes 294920 | tf_op jit(solution)/shard_map/ppermute | solution.py:311
  27.0 8.7 %collective-permute-start.8 = (bf16[64,768]{1,0:T(8,128)(2,1)S(1)}, bf16[64,768]{1,0:T(8,128)(2,1)S(1)}, u32[]{:S(2)}, u32[]{:S(2)}) collective-permute-start(bf16[64,768]{1,0:T(8,128)(2,1)S(1)} %get-tuple-element.67), channel_id=1, source_target_pairs={{0,1},{1,0},{2,3},{3,2},{4,5},{5,4},{6,7},{7,6},{8,9},{9,8},{10,11... | collective-permute-start | bytes 294920 | tf_op jit(solution)/shard_map/ppermute | solution.py:311
  27.5 8.2 %collective-permute-start.9 = (bf16[64,768]{1,0:T(8,128)(2,1)S(1)}, bf16[64,768]{1,0:T(8,128)(2,1)S(1)}, u32[]{:S(2)}, u32[]{:S(2)}) collective-permute-start(bf16[64,768]{1,0:T(8,128)(2,1)S(1)} %get-tuple-element.68), channel_id=1, source_target_pairs={{0,2},{1,3},{2,0},{3,1},{4,6},{5,7},{6,4},{7,5},{8,10},{9,11},{10,... | collective-permute-start | bytes 294920 | tf_op jit(solution)/shard_map/ppermute | solution.py:311
  33.5 4.3 %slice-start = ((s8[12582912]{0:T(1024)(128)(4,1)}), s8[4194304]{0:T(1024)(128)(4,1)S(1)}, s32[]{:S(2)}) async-start(s8[12582912]{0:T(1024)(128)(4,1)} %bitcast.4), calls=%async_computation | async-start | bytes 8388608
  33.5 4.3 %slice-start.1 = ((s8[12582912]{0:T(1024)(128)(4,1)}), s8[4194304]{0:T(1024)(128)(4,1)S(1)}, s32[]{:S(2)}) async-start(s8[12582912]{0:T(1024)(128)(4,1)} %bitcast.4), calls=%async_computation.1 | async-start | bytes 8388608
  35.7 2.7 %slice-start.2 = ((s8[12582912]{0:T(1024)(128)(4,1)}), s8[4194304]{0:T(1024)(128)(4,1)S(1)}, s32[]{:S(2)}) async-start(s8[12582912]{0:T(1024)(128)(4,1)} %bitcast.4), calls=%async_computation.2 | async-start | bytes 8388608
  39.4 5.4 %collective-permute-start.15 = (bf16[64,768]{1,0:T(8,128)(2,1)S(1)}, bf16[64,768]{1,0:T(8,128)(2,1)S(1)}, u32[]{:S(2)}, u32[]{:S(2)}) collective-permute-start(bf16[64,768]{1,0:T(8,128)(2,1)S(1)} %get-tuple-element.88), channel_id=1, source_target_pairs={{0,1},{1,0},{2,3},{3,2},{4,5},{5,4},{6,7},{7,6},{8,9},{9,8},{10,11... | collective-permute-start | bytes 294920 | tf_op jit(solution)/shard_map/ppermute | solution.py:311
  40.1 5.1 %collective-permute-start.16 = (bf16[64,768]{1,0:T(8,128)(2,1)S(1)}, bf16[64,768]{1,0:T(8,128)(2,1)S(1)}, u32[]{:S(2)}, u32[]{:S(2)}) collective-permute-start(bf16[64,768]{1,0:T(8,128)(2,1)S(1)} %get-tuple-element.89), channel_id=1, source_target_pairs={{0,2},{1,3},{2,0},{3,1},{4,6},{5,7},{6,4},{7,5},{8,10},{9,11},{10,... | collective-permute-start | bytes 294920 | tf_op jit(solution)/shard_map/ppermute | solution.py:311
  41.6 5.3 %collective-permute-start.17 = (bf16[64,768]{1,0:T(8,128)(2,1)S(1)}, bf16[64,768]{1,0:T(8,128)(2,1)S(1)}, u32[]{:S(2)}, u32[]{:S(2)}) collective-permute-start(bf16[64,768]{1,0:T(8,128)(2,1)S(1)} %get-tuple-element.90), channel_id=1, source_target_pairs={{0,3},{1,2},{2,1},{3,0},{4,7},{5,6},{6,5},{7,4},{8,11},{9,10},{10,... | collective-permute-start | bytes 294920 | tf_op jit(solution)/shard_map/ppermute | solution.py:311
  42.6 6.0 %collective-permute-start.26 = (bf16[64,768]{1,0:T(8,128)(2,1)S(1)}, bf16[64,768]{1,0:T(8,128)(2,1)S(1)}, u32[]{:S(2)}, u32[]{:S(2)}) collective-permute-start(bf16[64,768]{1,0:T(8,128)(2,1)S(1)} %get-tuple-element.101), channel_id=1, source_target_pairs={{0,1},{1,0},{2,3},{3,2},{4,5},{5,4},{6,7},{7,6},{8,9},{9,8},{10,11... | collective-permute-start | bytes 294920 | tf_op jit(solution)/shard_map/ppermute | solution.py:311
  43.4 7.3 %collective-permute-start.27 = (bf16[64,768]{1,0:T(8,128)(2,1)S(1)}, bf16[64,768]{1,0:T(8,128)(2,1)S(1)}, u32[]{:S(2)}, u32[]{:S(2)}) collective-permute-start(bf16[64,768]{1,0:T(8,128)(2,1)S(1)} %get-tuple-element.102), channel_id=1, source_target_pairs={{0,2},{1,3},{2,0},{3,1},{4,6},{5,7},{6,4},{7,5},{8,10},{9,11},{10,... | collective-permute-start | bytes 294920 | tf_op jit(solution)/shard_map/ppermute | solution.py:311
  44.8 6.0 %collective-permute-start.28 = (bf16[64,768]{1,0:T(8,128)(2,1)S(1)}, bf16[64,768]{1,0:T(8,128)(2,1)S(1)}, u32[]{:S(2)}, u32[]{:S(2)}) collective-permute-start(bf16[64,768]{1,0:T(8,128)(2,1)S(1)} %get-tuple-element.103), channel_id=1, source_target_pairs={{0,3},{1,2},{2,1},{3,0},{4,7},{5,6},{6,5},{7,4},{8,11},{9,10},{10,... | collective-permute-start | bytes 294920 | tf_op jit(solution)/shard_map/ppermute | solution.py:311
  47.2 7.2 %collective-permute-start.18 = (bf16[128,384]{1,0:T(8,128)(2,1)S(1)}, bf16[128,384]{1,0:T(8,128)(2,1)S(1)}, u32[]{:S(2)}, u32[]{:S(2)}) collective-permute-start(bf16[128,384]{1,0:T(8,128)(2,1)S(1)} %get-tuple-element.91.refs_0_), channel_id=1, source_target_pairs={{0,4},{4,0},{8,12},{12,8},{1,5},{5,1},{9,13},{13,9},{2,6},{6,2},{1... | collective-permute-start | bytes 294920 | tf_op jit(solution)/shard_map/ppermute | solution.py:311
  48.3 6.8 %collective-permute-start.22 = (bf16[64,768]{1,0:T(8,128)(2,1)S(1)}, bf16[64,768]{1,0:T(8,128)(2,1)S(1)}, u32[]{:S(2)}, u32[]{:S(2)}) collective-permute-start(bf16[64,768]{1,0:T(8,128)(2,1)S(1)} %get-tuple-element.97), channel_id=1, source_target_pairs={{0,1},{1,0},{2,3},{3,2},{4,5},{5,4},{6,7},{7,6},{8,9},{9,8},{10,11... | collective-permute-start | bytes 294920 | tf_op jit(solution)/shard_map/ppermute | solution.py:311
  48.6 6.5 %collective-permute-start.23 = (bf16[64,768]{1,0:T(8,128)(2,1)S(1)}, bf16[64,768]{1,0:T(8,128)(2,1)S(1)}, u32[]{:S(2)}, u32[]{:S(2)}) collective-permute-start(bf16[64,768]{1,0:T(8,128)(2,1)S(1)} %get-tuple-element.98), channel_id=1, source_target_pairs={{0,2},{1,3},{2,0},{3,1},{4,6},{5,7},{6,4},{7,5},{8,10},{9,11},{10,... | collective-permute-start | bytes 294920 | tf_op jit(solution)/shard_map/ppermute | solution.py:311
  50.6 5.1 %collective-permute-start.24 = (bf16[64,768]{1,0:T(8,128)(2,1)S(1)}, bf16[64,768]{1,0:T(8,128)(2,1)S(1)}, u32[]{:S(2)}, u32[]{:S(2)}) collective-permute-start(bf16[64,768]{1,0:T(8,128)(2,1)S(1)} %get-tuple-element.99), channel_id=1, source_target_pairs={{0,3},{1,2},{2,1},{3,0},{4,7},{5,6},{6,5},{7,4},{8,11},{9,10},{10,... | collective-permute-start | bytes 294920 | tf_op jit(solution)/shard_map/ppermute | solution.py:311
  50.9 9.7 %collective-permute-start.30 = (bf16[128,384]{1,0:T(8,128)(2,1)S(1)}, bf16[128,384]{1,0:T(8,128)(2,1)S(1)}, u32[]{:S(2)}, u32[]{:S(2)}) collective-permute-start(bf16[128,384]{1,0:T(8,128)(2,1)S(1)} %get-tuple-element.104), channel_id=1, source_target_pairs={{0,12},{4,8},{8,4},{12,0},{1,13},{5,9},{9,5},{13,1},{2,14},{6,10},... | collective-permute-start | bytes 294920 | tf_op jit(solution)/shard_map/ppermute | solution.py:311
  54.7 13.6 %collective-permute-start.29 = (bf16[128,768]{1,0:T(8,128)(2,1)S(1)}, bf16[128,768]{1,0:T(8,128)(2,1)S(1)}, u32[]{:S(2)}, u32[]{:S(2)}) collective-permute-start(bf16[128,768]{1,0:T(8,128)(2,1)S(1)} %combine.6), channel_id=1, source_target_pairs={{0,8},{4,12},{8,0},{12,4},{1,9},{5,13},{9,1},{13,5},{2,10},{6,14},... | collective-permute-start | bytes 589832 | tf_op jit(solution)/shard_map/ppermute | solution.py:311
  56.1 12.2 %collective-permute-start.25 = (bf16[128,768]{1,0:T(8,128)(2,1)S(1)}, bf16[128,768]{1,0:T(8,128)(2,1)S(1)}, u32[]{:S(2)}, u32[]{:S(2)}) collective-permute-start(bf16[128,768]{1,0:T(8,128)(2,1)S(1)} %combine.5), channel_id=1, source_target_pairs={{0,4},{4,0},{8,12},{12,8},{1,5},{5,1},{9,13},{13,9},{2,6},{6,2},{1... | collective-permute-start | bytes 589832 | tf_op jit(solution)/shard_map/ppermute | solution.py:311
  58.9 1.9 %collective-permute-start.19 = (bf16[64,768]{1,0:T(8,128)(2,1)S(1)}, bf16[64,768]{1,0:T(8,128)(2,1)S(1)}, u32[]{:S(2)}, u32[]{:S(2)}) collective-permute-start(bf16[64,768]{1,0:T(8,128)(2,1)S(1)} %get-tuple-element.93), channel_id=1, source_target_pairs={{0,1},{1,0},{2,3},{3,2},{4,5},{5,4},{6,7},{7,6},{8,9},{9,8},{10,11... | collective-permute-start | bytes 294920 | tf_op jit(solution)/shard_map/ppermute | solution.py:311
  59.0 5.7 %collective-permute-start.20 = (bf16[64,768]{1,0:T(8,128)(2,1)S(1)}, bf16[64,768]{1,0:T(8,128)(2,1)S(1)}, u32[]{:S(2)}, u32[]{:S(2)}) collective-permute-start(bf16[64,768]{1,0:T(8,128)(2,1)S(1)} %get-tuple-element.94), channel_id=1, source_target_pairs={{0,2},{1,3},{2,0},{3,1},{4,6},{5,7},{6,4},{7,5},{8,10},{9,11},{10,... | collective-permute-start | bytes 294920 | tf_op jit(solution)/shard_map/ppermute | solution.py:311
  60.6 5.3 %collective-permute-start.21 = (bf16[64,768]{1,0:T(8,128)(2,1)S(1)}, bf16[64,768]{1,0:T(8,128)(2,1)S(1)}, u32[]{:S(2)}, u32[]{:S(2)}) collective-permute-start(bf16[64,768]{1,0:T(8,128)(2,1)S(1)} %get-tuple-element.95), channel_id=1, source_target_pairs={{0,3},{1,2},{2,1},{3,0},{4,7},{5,6},{6,5},{7,4},{8,11},{9,10},{10,... | collective-permute-start | bytes 294920 | tf_op jit(solution)/shard_map/ppermute | solution.py:311

commit v17 on v12

--- a/solution.py
+++ b/solution.py
@@ -321,12 +321,13 @@
     if not doubling:
         mixed = combine(pick, mix, returned(everything), [])[0]
         return lax.psum_scatter(mixed, "tensor", scatter_dimension=1, tiled=True)
-    low, high = combine(pick, mix, returned(across(3)), [], cuts=2)
+    first, second = returned(across(3)), returned(across(2))
+    low, high = combine(pick, mix, first, [], cuts=2)
     passed = swap(low, "tensor", 1)
     far = (swap(high, "tensor", 3), width // 2)
-    onwards = combine(pick, mix, returned(across(2)), [(passed, 0)])[0]
+    onwards = combine(pick, mix, second, [(passed, 0)])[0]
     over = (swap(onwards, "tensor", 2), 0)
-    near = combine(pick, mix, returned(across(1), [low]), [])[0]
+    near = combine(pick, mix, returned(across(1), second[1:2]), [])[0]
     beside = (swap(near, "tensor", 1), 0)
     return combine(pick, mix, returned(across(0), [passed]), [beside, over, far])[0]
 

time: 66.4 us -> 66.4 us (level)
  no operation moved by 1% of the time
where the time goes in v17:
time: 66.4 us; the launch traced here: 66.3 us
  starting transfers between devices  28.2 us (42%)
  Pallas kernels  24.2 us (36%)
  waiting for transfers between devices  12.1 us (18%)
  local copies, waits for them, and re-layouts  1.54 us (2%)
    ppermute x28, starting transfers between devices, swap(): return lax.ppermute(value, axis, [(i, i ^ distance) for i in range(count)])  28.2 us
    ppermute x28, waiting for transfers between devices, swap(): return lax.ppermute(value, axis, [(i, i ^ distance) for i in range(count)])  12.1 us
    pallas_call x2, Pallas kernels, prefetch(): pl.pallas_call(functools.partial(prefetch_kernel, parts=[part for _, part...  9.41 us
    pallas_call x3, Pallas kernels, gate_up(): pl.pallas_call(functools.partial(gate_up_kernel, experts=experts, slices=...  7.71 us
    pallas_call x4, Pallas kernels, down(): pl.pallas_call(functools.partial(down_kernel, part=part, waits=len(after)...  4.11 us
    pallas_call x4, Pallas kernels, combine(): pl.pallas_call(functools.partial(combine_kernel, experts=len(blocks), sta...  1.94 us
    unnamed x12, local copies, waits for them, and re-layouts  1.54 us
  transfers between devices with their start and end apart: 28, of which 8 were waited for; matrix products, arithmetic and copies ran while one was open for 0% of the time, Pallas kernels for 30%

profile of v17, /device:TPU:0, one launch (start us, length us, event | category | flops | bytes accessed | tf_op | source)
XLA Modules:
  0.0 66.3 jit_solution(13305679507607223170)
XLA Ops:
  0.0 4.0 %collective-permute-start = (bf16[128,768]{1,0:T(8,128)(2,1)}, bf16[128,768]{1,0:T(8,128)(2,1)S(1)}, u32[]{:S(2)}, u32[]{:S(2)}) collective-permute-start(bf16[128,768]{1,0:T(8,128)(2,1)} %refs_0_.4), channel_id=1, source_target_pairs={{0,8},{4,12},{8,0},{12,4},{1,9},{5,13},{9,1},{13,5},{2,10},{6,14},... | collective-permute-start | bytes 589832 | tf_op jit(solution)/shard_map/ppermute | solution.py:275
  4.0 1.6 %collective-permute-start.5 = (bf16[128,768]{1,0:T(8,128)(2,1)}, bf16[128,768]{1,0:T(8,128)(2,1)S(1)}, u32[]{:S(2)}, u32[]{:S(2)}) collective-permute-start(bf16[128,768]{1,0:T(8,128)(2,1)} %refs_0_.4), channel_id=1, source_target_pairs={{0,4},{4,0},{8,12},{12,8},{1,5},{5,1},{9,13},{13,9},{2,6},{6,2},{1... | collective-permute-start | bytes 589832 | tf_op jit(solution)/shard_map/ppermute | solution.py:275
  5.6 0.7 %copy-done.1 = s32[128,2]{0,1:T(2,128)S(1)} copy-done((s32[128,2]{0,1:T(2,128)S(1)}, s32[128,2]{0,1:T(2,128)}, u32[]{:S(2)}) %copy-start.1) | copy-done | bytes 1048
  6.3 0.7 %copy-done.2 = f32[128,2]{0,1:T(2,128)S(1)} copy-done((f32[128,2]{0,1:T(2,128)S(1)}, f32[128,2]{0,1:T(2,128)}, u32[]{:S(2)}) %copy-start.2) | copy-done | bytes 1048
  7.2 4.7 %prefetch.2 = (bf16[768,2048]{1,0:T(8,128)(2,1)S(1)}, bf16[768,2048]{1,0:T(8,128)(2,1)S(1)}, bf16[768,2048]{1,0:T(8,128)(2,1)S(1)}, bf16[768,2048]{1,0:T(8,128)(2,1)S(1)}) custom-call(s32[1]{0:T(128)} %bitcast.3.column_ref, bf16[256,128]{1,0:T(8,128)(2,1)S(1)} %get-tuple-element.52.placed_ref.after_ref, bf16[1,3072,2048]{2,1,0:T(8,128)(2,1)} %refs_2_.3, ...), custom_call_target="tpu_custom_call" | custom-call | bytes 12582912 | tf_op jit(solution)/shard_map/prefetch/pallas_call | solution.py:127
  11.9 1.6 %collective-permute-done.refs_0_ = bf16[128,768]{1,0:T(8,128)(2,1)S(1)} collective-permute-done((bf16[128,768]{1,0:T(8,128)(2,1)}, bf16[128,768]{1,0:T(8,128)(2,1)S(1)}, u32[]{:S(2)}, u32[]{:S(2)}) %collective-permute-start) | collective-permute-done | bytes 196640 | tf_op jit(solution)/shard_map/ppermute | solution.py:275
  13.5 0.7 %collective-permute-start.1 = (bf16[128,768]{1,0:T(8,128)(2,1)S(1)}, bf16[128,768]{1,0:T(8,128)(2,1)S(1)}, u32[]{:S(2)}, u32[]{:S(2)}) collective-permute-start(bf16[128,768]{1,0:T(8,128)(2,1)S(1)} %collective-permute-done.refs_0_), channel_id=1, source_target_pairs={{0,4},{4,0},{8,12},{12,8},{1,5},{5,1},{9,13},{13,9},{2,6},{6,2},{1... | collective-permute-start | bytes 589832 | tf_op jit(solution)/shard_map/ppermute | solution.py:275
  14.2 0.4 dispatch.4
  14.6 1.6 %collective-permute-start.10 = (bf16[64,1536]{1,0:T(8,128)(2,1)S(1)}, bf16[64,1536]{1,0:T(8,128)(2,1)S(1)}, u32[]{:S(2)}, u32[]{:S(2)}) collective-permute-start(bf16[64,1536]{1,0:T(8,128)(2,1)S(1)} %get-tuple-element.68), channel_id=1, source_target_pairs={{0,2},{1,3},{2,0},{3,1},{4,6},{5,7},{6,4},{7,5},{8,10},{9,11},{10,... | collective-permute-start | bytes 589832 | tf_op jit(solution)/shard_map/ppermute | solution.py:275
  16.1 0.6 collective-permute-start.9
  16.8 4.7 %prefetch.3 = (bf16[768,2048]{1,0:T(8,128)(2,1)S(1)}, bf16[768,2048]{1,0:T(8,128)(2,1)S(1)}, bf16[768,2048]{1,0:T(8,128)(2,1)S(1)}, bf16[768,2048]{1,0:T(8,128)(2,1)S(1)}) custom-call(s32[1]{0:T(128)} %bitcast.3.column_ref, bf16[64,1536]{1,0:T(8,128)(2,1)S(1)} %get-tuple-element.58.after_ref.refs_0_, bf16[1,3072,2048]{2,1,0:T(8,128)(2,1)} %refs_2_.3, ...), custom_call_target="tpu_custom_call" | custom-call | bytes 12582912 | tf_op jit(solution)/shard_map/prefetch/pallas_call | solution.py:127
  21.5 0.3 dispatch.5
  21.8 1.6 %collective-permute-start.7 = (bf16[64,768]{1,0:T(8,128)(2,1)S(1)}, bf16[64,768]{1,0:T(8,128)(2,1)S(1)}, u32[]{:S(2)}, u32[]{:S(2)}) collective-permute-start(bf16[64,768]{1,0:T(8,128)(2,1)S(1)} %get-tuple-element.63), channel_id=1, source_target_pairs={{0,2},{1,3},{2,0},{3,1},{4,6},{5,7},{6,4},{7,5},{8,10},{9,11},{10,... | collective-permute-start | bytes 294920 | tf_op jit(solution)/shard_map/ppermute | solution.py:275
  23.4 0.3 dispatch.3
  23.7 0.7 %collective-permute-start.8 = (bf16[64,768]{1,0:T(8,128)(2,1)S(1)}, bf16[64,768]{1,0:T(8,128)(2,1)S(1)}, u32[]{:S(2)}, u32[]{:S(2)}) collective-permute-start(bf16[64,768]{1,0:T(8,128)(2,1)S(1)} %get-tuple-element.64), channel_id=1, source_target_pairs={{0,3},{1,2},{2,1},{3,0},{4,7},{5,6},{6,5},{7,4},{8,11},{9,10},{10,... | collective-permute-start | bytes 294920 | tf_op jit(solution)/shard_map/ppermute | solution.py:275
  24.4 0.4 collective-permute-start.2
  24.8 1.1 %collective-permute-start.3 = (bf16[64,768]{1,0:T(8,128)(2,1)S(1)}, bf16[64,768]{1,0:T(8,128)(2,1)S(1)}, u32[]{:S(2)}, u32[]{:S(2)}) collective-permute-start(bf16[64,768]{1,0:T(8,128)(2,1)S(1)} %get-tuple-element.55), channel_id=1, source_target_pairs={{0,2},{1,3},{2,0},{3,1},{4,6},{5,7},{6,4},{7,5},{8,10},{9,11},{10,... | collective-permute-start | bytes 294920 | tf_op jit(solution)/shard_map/ppermute | solution.py:275
  25.9 1.1 %collective-permute-start.4 = (bf16[64,768]{1,0:T(8,128)(2,1)S(1)}, bf16[64,768]{1,0:T(8,128)(2,1)S(1)}, u32[]{:S(2)}, u32[]{:S(2)}) collective-permute-start(bf16[64,768]{1,0:T(8,128)(2,1)S(1)} %get-tuple-element.56), channel_id=1, source_target_pairs={{0,3},{1,2},{2,1},{3,0},{4,7},{5,6},{6,5},{7,4},{8,11},{9,10},{10,... | collective-permute-start | bytes 294920 | tf_op jit(solution)/shard_map/ppermute | solution.py:275
  27.0 3.5 %gate_up.3 = (f32[256,2048]{1,0:T(8,128)S(1)}, f32[256,2048]{1,0:T(8,128)S(1)}) custom-call(bf16[64,1536]{1,0:T(8,128)(2,1)S(1)} %get-tuple-element.58.after_ref.refs_0_, bf16[64,1536]{1,0:T(8,128)(2,1)S(1)} %collective-permute-done.9.refs_1_, bf16[64,1536]{1,0:T(8,128)(2,1)S(1)} %collective-permute-done.10.refs_2_, ...), custom_call_target="tpu_custom_call" | custom-call | flops 3221225472 | bytes 12582912 | tf_op jit(solution)/shard_map/gate_up/pallas_call | solution.py:183
  30.5 2.1 %gate_up.4 = (f32[256,2048]{1,0:T(8,128)S(1)}, f32[256,2048]{1,0:T(8,128)S(1)}) custom-call(bf16[64,768]{1,0:T(8,128)(2,1)S(1)} %get-tuple-element.61.refs_0_, bf16[64,768]{1,0:T(8,128)(2,1)S(1)} %collective-permute-done.6.refs_8_.refs_1_, bf16[64,768]{1,0:T(8,128)(2,1)S(1)} %collective-permute-done.7.refs_2_, ...), custom_call_target="tpu_custom_call", output_to_operand_aliasing={{0}: (6, {}), {1}: (7, {})} | custom-call | flops 1610612736 | bytes 6291456 | tf_op jit(solution)/shard_map/gate_up/pallas_call | solution.py:183
  32.6 0.8 %collective-permute-done.4.refs_3_ = bf16[64,768]{1,0:T(8,128)(2,1)S(1)} collective-permute-done((bf16[64,768]{1,0:T(8,128)(2,1)S(1)}, bf16[64,768]{1,0:T(8,128)(2,1)S(1)}, u32[]{:S(2)}, u32[]{:S(2)}) %collective-permute-start.4) | collective-permute-done | bytes 98336 | tf_op jit(solution)/shard_map/ppermute | solution.py:275
  33.4 2.1 %gate_up.5.h_ref = bf16[256,2048]{1,0:T(8,128)(2,1)S(1)} custom-call(bf16[64,768]{1,0:T(8,128)(2,1)S(1)} %get-tuple-element.53.refs_0_, bf16[64,768]{1,0:T(8,128)(2,1)S(1)} %collective-permute-done.2.refs_1_, bf16[64,768]{1,0:T(8,128)(2,1)S(1)} %collective-permute-done.3.refs_2_, bf16[64,768]{1,0:T(8,128)(2,1)S(1)} %collective-permute-done.4.refs_3_, ...), custom_call_target="tpu_custom_call" | custom-call | flops 1610612736 | bytes 6291456 | tf_op jit(solution)/shard_map/gate_up/pallas_call | solution.py:183
  35.7 1.0 %down.4 = (bf16[64,768]{1,0:T(8,128)(2,1)S(1)}, bf16[64,768]{1,0:T(8,128)(2,1)S(1)}, bf16[64,768]{1,0:T(8,128)(2,1)S(1)}, bf16[64,768]{1,0:T(8,128)(2,1)S(1)}) custom-call(s32[1]{0:T(128)} %bitcast.3.column_ref, bf16[256,2048]{1,0:T(8,128)(2,1)S(1)} %gate_up.5.h_ref, bf16[1,2048,3072]{2,1,0:T(8,128)(2,1)S(1)} %bitcast.5), custom_call_target="tpu_custom_call" | custom-call | flops 805306368 | bytes 3538944 | tf_op jit(solution)/shard_map/down/pallas_call | solution.py:221
  36.8 0.2 collective-permute-start.12
  37.0 1.4 %collective-permute-start.13 = (bf16[64,768]{1,0:T(8,128)(2,1)S(1)}, bf16[64,768]{1,0:T(8,128)(2,1)S(1)}, u32[]{:S(2)}, u32[]{:S(2)}) collective-permute-start(bf16[64,768]{1,0:T(8,128)(2,1)S(1)} %get-tuple-element.79), channel_id=1, source_target_pairs={{0,2},{1,3},{2,0},{3,1},{4,6},{5,7},{6,4},{7,5},{8,10},{9,11},{10,... | collective-permute-start | bytes 294920 | tf_op jit(solution)/shard_map/ppermute | solution.py:275
  38.4 0.3 collective-permute-start.14
  38.7 1.0 %down.6 = (bf16[64,768]{1,0:T(8,128)(2,1)S(1)}, bf16[64,768]{1,0:T(8,128)(2,1)S(1)}, bf16[64,768]{1,0:T(8,128)(2,1)S(1)}, bf16[64,768]{1,0:T(8,128)(2,1)S(1)}) custom-call(s32[1]{0:T(128)} %bitcast.3.column_ref, bf16[256,2048]{1,0:T(8,128)(2,1)S(1)} %gate_up.5.h_ref, bf16[1,2048,3072]{2,1,0:T(8,128)(2,1)S(1)} %bitcast.5), custom_call_target="tpu_custom_call" | custom-call | flops 805306368 | bytes 3538944 | tf_op jit(solution)/shard_map/down/pallas_call | solution.py:221
  39.7 0.5 collective-permute-start.19
  40.2 1.4 %collective-permute-start.24 = (bf16[64,768]{1,0:T(8,128)(2,1)S(1)}, bf16[64,768]{1,0:T(8,128)(2,1)S(1)}, u32[]{:S(2)}, u32[]{:S(2)}) collective-permute-start(bf16[64,768]{1,0:T(8,128)(2,1)S(1)} %get-tuple-element.92), channel_id=1, source_target_pairs={{0,2},{1,3},{2,0},{3,1},{4,6},{5,7},{6,4},{7,5},{8,10},{9,11},{10,... | collective-permute-start | bytes 294920 | tf_op jit(solution)/shard_map/ppermute | solution.py:275
  41.7 0.9 %collective-permute-done.13.refs_2_ = bf16[64,768]{1,0:T(8,128)(2,1)S(1)} collective-permute-done((bf16[64,768]{1,0:T(8,128)(2,1)S(1)}, bf16[64,768]{1,0:T(8,128)(2,1)S(1)}, u32[]{:S(2)}, u32[]{:S(2)}) %collective-permute-start.13) | collective-permute-done | bytes 98336 | tf_op jit(solution)/shard_map/ppermute | solution.py:275
  42.6 1.0 %collective-permute-done.14.refs_3_ = bf16[64,768]{1,0:T(8,128)(2,1)S(1)} collective-permute-done((bf16[64,768]{1,0:T(8,128)(2,1)S(1)}, bf16[64,768]{1,0:T(8,128)(2,1)S(1)}, u32[]{:S(2)}, u32[]{:S(2)}) %collective-permute-start.14) | collective-permute-done | bytes 98336 | tf_op jit(solution)/shard_map/ppermute | solution.py:275
  43.6 0.3 combine.4
  44.0 1.0 %collective-permute-start.15 = (bf16[128,384]{1,0:T(8,128)(2,1)S(1)}, bf16[128,384]{1,0:T(8,128)(2,1)S(1)}, u32[]{:S(2)}, u32[]{:S(2)}) collective-permute-start(bf16[128,384]{1,0:T(8,128)(2,1)S(1)} %get-tuple-element.81), channel_id=1, source_target_pairs={{0,4},{4,0},{8,12},{12,8},{1,5},{5,1},{9,13},{13,9},{2,6},{6,2},{1... | collective-permute-start | bytes 294920 | tf_op jit(solution)/shard_map/ppermute | solution.py:275
  45.0 1.0 %down.7 = (bf16[64,768]{1,0:T(8,128)(2,1)S(1)}, bf16[64,768]{1,0:T(8,128)(2,1)S(1)}, bf16[64,768]{1,0:T(8,128)(2,1)S(1)}, bf16[64,768]{1,0:T(8,128)(2,1)S(1)}) custom-call(s32[1]{0:T(128)} %bitcast.3.column_ref, bf16[256,2048]{1,0:T(8,128)(2,1)S(1)} %gate_up.5.h_ref, bf16[1,2048,3072]{2,1,0:T(8,128)(2,1)S(1)} %bitcast.5, ...), custom_call_target="tpu_custom_call" | custom-call | flops 805306368 | bytes 3538944 | tf_op jit(solution)/shard_map/down/pallas_call | solution.py:221
  46.0 0.6 collective-permute-start.20
  46.7 1.5 %collective-permute-start.21 = (bf16[64,768]{1,0:T(8,128)(2,1)S(1)}, bf16[64,768]{1,0:T(8,128)(2,1)S(1)}, u32[]{:S(2)}, u32[]{:S(2)}) collective-permute-start(bf16[64,768]{1,0:T(8,128)(2,1)S(1)} %get-tuple-element.89), channel_id=1, source_target_pairs={{0,2},{1,3},{2,0},{3,1},{4,6},{5,7},{6,4},{7,5},{8,10},{9,11},{10,... | collective-permute-start | bytes 294920 | tf_op jit(solution)/shard_map/ppermute | solution.py:275
  48.1 3.8 %collective-permute-start.27 = (bf16[128,384]{1,0:T(8,128)(2,1)S(1)}, bf16[128,384]{1,0:T(8,128)(2,1)S(1)}, u32[]{:S(2)}, u32[]{:S(2)}) collective-permute-start(bf16[128,384]{1,0:T(8,128)(2,1)S(1)} %get-tuple-element.94), channel_id=1, source_target_pairs={{0,12},{4,8},{8,4},{12,0},{1,13},{5,9},{9,5},{13,1},{2,14},{6,10},... | collective-permute-start | bytes 294920 | tf_op jit(solution)/shard_map/ppermute | solution.py:275
  51.9 0.3 combine.6
  52.2 1.0 %collective-permute-start.26 = (bf16[128,768]{1,0:T(8,128)(2,1)S(1)}, bf16[128,768]{1,0:T(8,128)(2,1)S(1)}, u32[]{:S(2)}, u32[]{:S(2)}) collective-permute-start(bf16[128,768]{1,0:T(8,128)(2,1)S(1)} %combine.6), channel_id=1, source_target_pairs={{0,8},{4,12},{8,0},{12,4},{1,9},{5,13},{9,1},{13,5},{2,10},{6,14},... | collective-permute-start | bytes 589832 | tf_op jit(solution)/shard_map/ppermute | solution.py:275
  53.3 0.3 combine.5
  53.6 1.1 %collective-permute-start.23 = (bf16[128,768]{1,0:T(8,128)(2,1)S(1)}, bf16[128,768]{1,0:T(8,128)(2,1)S(1)}, u32[]{:S(2)}, u32[]{:S(2)}) collective-permute-start(bf16[128,768]{1,0:T(8,128)(2,1)S(1)} %combine.5), channel_id=1, source_target_pairs={{0,4},{4,0},{8,12},{12,8},{1,5},{5,1},{9,13},{13,9},{2,6},{6,2},{1... | collective-permute-start | bytes 589832 | tf_op jit(solution)/shard_map/ppermute | solution.py:275
  54.6 1.0 %down.5 = (bf16[64,768]{1,0:T(8,128)(2,1)S(1)}, bf16[64,768]{1,0:T(8,128)(2,1)S(1)}, bf16[64,768]{1,0:T(8,128)(2,1)S(1)}, bf16[64,768]{1,0:T(8,128)(2,1)S(1)}) custom-call(s32[1]{0:T(128)} %bitcast.3.column_ref, bf16[256,2048]{1,0:T(8,128)(2,1)S(1)} %gate_up.5.h_ref, bf16[1,2048,3072]{2,1,0:T(8,128)(2,1)S(1)} %bitcast.5, ...), custom_call_target="tpu_custom_call" | custom-call | flops 805306368 | bytes 3538944 | tf_op jit(solution)/shard_map/down/pallas_call | solution.py:221
  55.7 0.3 collective-permute-start.16
  56.0 1.4 %collective-permute-start.17 = (bf16[64,768]{1,0:T(8,128)(2,1)S(1)}, bf16[64,768]{1,0:T(8,128)(2,1)S(1)}, u32[]{:S(2)}, u32[]{:S(2)}) collective-permute-start(bf16[64,768]{1,0:T(8,128)(2,1)S(1)} %get-tuple-element.84), channel_id=1, source_target_pairs={{0,2},{1,3},{2,0},{3,1},{4,6},{5,7},{6,4},{7,5},{8,10},{9,11},{10,... | collective-permute-start | bytes 294920 | tf_op jit(solution)/shard_map/ppermute | solution.py:275
  57.6 3.9 %collective-permute-done.17.refs_2_ = bf16[64,768]{1,0:T(8,128)(2,1)S(1)} collective-permute-done((bf16[64,768]{1,0:T(8,128)(2,1)S(1)}, bf16[64,768]{1,0:T(8,128)(2,1)S(1)}, u32[]{:S(2)}, u32[]{:S(2)}) %collective-permute-start.17) | collective-permute-done | bytes 98336 | tf_op jit(solution)/shard_map/ppermute | solution.py:275
  61.6 0.9 %collective-permute-done.18.refs_3_ = bf16[64,768]{1,0:T(8,128)(2,1)S(1)} collective-permute-done((bf16[64,768]{1,0:T(8,128)(2,1)S(1)}, bf16[64,768]{1,0:T(8,128)(2,1)S(1)}, u32[]{:S(2)}, u32[]{:S(2)}) %collective-permute-start.18) | collective-permute-done | bytes 98336 | tf_op jit(solution)/shard_map/ppermute | solution.py:275
  62.5 2.8 %collective-permute-done.26.refs_5_ = bf16[128,768]{1,0:T(8,128)(2,1)S(1)} collective-permute-done((bf16[128,768]{1,0:T(8,128)(2,1)S(1)}, bf16[128,768]{1,0:T(8,128)(2,1)S(1)}, u32[]{:S(2)}, u32[]{:S(2)}) %collective-permute-start.26) | collective-permute-done | bytes 196640 | tf_op jit(solution)/shard_map/ppermute | solution.py:275
  65.2 1.0 %combine.7 = bf16[128,768]{1,0:T(8,128)(2,1)} custom-call(bf16[256,256]{1,0:T(8,128)(2,1)S(1)} %get-tuple-element.50.pick_ref, f32[128,2]{1,0:T(8,128)S(1)} %get-tuple-element.51.mix_ref, bf16[64,768]{1,0:T(8,128)(2,1)S(1)} %get-tuple-element.82.refs_0_, bf16[64,768]{1,0:T(8,128)(2,1)S(1)} %collective-permute-done.16.refs_1_, ...), custom_call_target="tpu_custom_call" | custom-call | flops 100663296 | bytes 589824 | tf_op jit(solution)/shard_map/combine/pallas_call | solution.py:258
  (38 shorter events, 0.8 us)
Async XLA Ops:
  0.0 13.5 %collective-permute-start = (bf16[128,768]{1,0:T(8,128)(2,1)}, bf16[128,768]{1,0:T(8,128)(2,1)S(1)}, u32[]{:S(2)}, u32[]{:S(2)}) collective-permute-start(bf16[128,768]{1,0:T(8,128)(2,1)} %refs_0_.4), channel_id=1, source_target_pairs={{0,8},{4,12},{8,0},{12,4},{1,9},{5,13},{9,1},{13,5},{2,10},{6,14},... | collective-permute-start | bytes 589832 | tf_op jit(solution)/shard_map/ppermute | solution.py:275
  4.0 10.2 %collective-permute-start.5 = (bf16[128,768]{1,0:T(8,128)(2,1)}, bf16[128,768]{1,0:T(8,128)(2,1)S(1)}, u32[]{:S(2)}, u32[]{:S(2)}) collective-permute-start(bf16[128,768]{1,0:T(8,128)(2,1)} %refs_0_.4), channel_id=1, source_target_pairs={{0,4},{4,0},{8,12},{12,8},{1,5},{5,1},{9,13},{13,9},{2,6},{6,2},{1... | collective-permute-start | bytes 589832 | tf_op jit(solution)/shard_map/ppermute | solution.py:275
  5.6 0.7 %copy-start.1 = (s32[128,2]{0,1:T(2,128)S(1)}, s32[128,2]{0,1:T(2,128)}, u32[]{:S(2)}) copy-start(s32[128,2]{0,1:T(2,128)} %param.7) | copy-start | bytes 3076
  6.3 0.7 %copy-start.2 = (f32[128,2]{0,1:T(2,128)S(1)}, f32[128,2]{0,1:T(2,128)}, u32[]{:S(2)}) copy-start(f32[128,2]{0,1:T(2,128)} %param.8) | copy-start | bytes 3076
  7.1 7.0 %copy-start = (bf16[128,768]{1,0:T(8,128)(2,1)S(1)}, bf16[128,768]{1,0:T(8,128)(2,1)}, u32[]{:S(2)}) copy-start(bf16[128,768]{1,0:T(8,128)(2,1)} %refs_0_.4) | copy-start | bytes 589828
  13.5 8.3 %collective-permute-start.1 = (bf16[128,768]{1,0:T(8,128)(2,1)S(1)}, bf16[128,768]{1,0:T(8,128)(2,1)S(1)}, u32[]{:S(2)}, u32[]{:S(2)}) collective-permute-start(bf16[128,768]{1,0:T(8,128)(2,1)S(1)} %collective-permute-done.refs_0_), channel_id=1, source_target_pairs={{0,4},{4,0},{8,12},{12,8},{1,5},{5,1},{9,13},{13,9},{2,6},{6,2},{1... | collective-permute-start | bytes 589832 | tf_op jit(solution)/shard_map/ppermute | solution.py:275
  14.6 9.8 %collective-permute-start.10 = (bf16[64,1536]{1,0:T(8,128)(2,1)S(1)}, bf16[64,1536]{1,0:T(8,128)(2,1)S(1)}, u32[]{:S(2)}, u32[]{:S(2)}) collective-permute-start(bf16[64,1536]{1,0:T(8,128)(2,1)S(1)} %get-tuple-element.68), channel_id=1, source_target_pairs={{0,2},{1,3},{2,0},{3,1},{4,6},{5,7},{6,4},{7,5},{8,10},{9,11},{10,... | collective-permute-start | bytes 589832 | tf_op jit(solution)/shard_map/ppermute | solution.py:275
  16.1 8.7 %collective-permute-start.11 = (bf16[64,1536]{1,0:T(8,128)(2,1)S(1)}, bf16[64,1536]{1,0:T(8,128)(2,1)S(1)}, u32[]{:S(2)}, u32[]{:S(2)}) collective-permute-start(bf16[64,1536]{1,0:T(8,128)(2,1)S(1)} %get-tuple-element.69), channel_id=1, source_target_pairs={{0,3},{1,2},{2,1},{3,0},{4,7},{5,6},{6,5},{7,4},{8,11},{9,10},{10,... | collective-permute-start | bytes 589832 | tf_op jit(solution)/shard_map/ppermute | solution.py:275
  16.1 9.7 %collective-permute-start.9 = (bf16[64,1536]{1,0:T(8,128)(2,1)S(1)}, bf16[64,1536]{1,0:T(8,128)(2,1)S(1)}, u32[]{:S(2)}, u32[]{:S(2)}) collective-permute-start(bf16[64,1536]{1,0:T(8,128)(2,1)S(1)} %get-tuple-element.67), channel_id=1, source_target_pairs={{0,1},{1,0},{2,3},{3,2},{4,5},{5,4},{6,7},{7,6},{8,9},{9,8},{10,11... | collective-permute-start | bytes 589832 | tf_op jit(solution)/shard_map/ppermute | solution.py:275
  21.7 1.9 %collective-permute-start.6 = (bf16[64,768]{1,0:T(8,128)(2,1)S(1)}, bf16[64,768]{1,0:T(8,128)(2,1)S(1)}, u32[]{:S(2)}, u32[]{:S(2)}) collective-permute-start(bf16[64,768]{1,0:T(8,128)(2,1)S(1)} %get-tuple-element.62), channel_id=1, source_target_pairs={{0,1},{1,0},{2,3},{3,2},{4,5},{5,4},{6,7},{7,6},{8,9},{9,8},{10,11... | collective-permute-start | bytes 294920 | tf_op jit(solution)/shard_map/ppermute | solution.py:275
  21.8 8.6 %collective-permute-start.7 = (bf16[64,768]{1,0:T(8,128)(2,1)S(1)}, bf16[64,768]{1,0:T(8,128)(2,1)S(1)}, u32[]{:S(2)}, u32[]{:S(2)}) collective-permute-start(bf16[64,768]{1,0:T(8,128)(2,1)S(1)} %get-tuple-element.63), channel_id=1, source_target_pairs={{0,2},{1,3},{2,0},{3,1},{4,6},{5,7},{6,4},{7,5},{8,10},{9,11},{10,... | collective-permute-start | bytes 294920 | tf_op jit(solution)/shard_map/ppermute | solution.py:275
  23.7 6.8 %collective-permute-start.8 = (bf16[64,768]{1,0:T(8,128)(2,1)S(1)}, bf16[64,768]{1,0:T(8,128)(2,1)S(1)}, u32[]{:S(2)}, u32[]{:S(2)}) collective-permute-start(bf16[64,768]{1,0:T(8,128)(2,1)S(1)} %get-tuple-element.64), channel_id=1, source_target_pairs={{0,3},{1,2},{2,1},{3,0},{4,7},{5,6},{6,5},{7,4},{8,11},{9,10},{10,... | collective-permute-start | bytes 294920 | tf_op jit(solution)/shard_map/ppermute | solution.py:275
  24.4 8.3 %collective-permute-start.2 = (bf16[64,768]{1,0:T(8,128)(2,1)S(1)}, bf16[64,768]{1,0:T(8,128)(2,1)S(1)}, u32[]{:S(2)}, u32[]{:S(2)}) collective-permute-start(bf16[64,768]{1,0:T(8,128)(2,1)S(1)} %get-tuple-element.54), channel_id=1, source_target_pairs={{0,1},{1,0},{2,3},{3,2},{4,5},{5,4},{6,7},{7,6},{8,9},{9,8},{10,11... | collective-permute-start | bytes 294920 | tf_op jit(solution)/shard_map/ppermute | solution.py:275
  24.8 7.8 %collective-permute-start.3 = (bf16[64,768]{1,0:T(8,128)(2,1)S(1)}, bf16[64,768]{1,0:T(8,128)(2,1)S(1)}, u32[]{:S(2)}, u32[]{:S(2)}) collective-permute-start(bf16[64,768]{1,0:T(8,128)(2,1)S(1)} %get-tuple-element.55), channel_id=1, source_target_pairs={{0,2},{1,3},{2,0},{3,1},{4,6},{5,7},{6,4},{7,5},{8,10},{9,11},{10,... | collective-permute-start | bytes 294920 | tf_op jit(solution)/shard_map/ppermute | solution.py:275
  25.9 7.5 %collective-permute-start.4 = (bf16[64,768]{1,0:T(8,128)(2,1)S(1)}, bf16[64,768]{1,0:T(8,128)(2,1)S(1)}, u32[]{:S(2)}, u32[]{:S(2)}) collective-permute-start(bf16[64,768]{1,0:T(8,128)(2,1)S(1)} %get-tuple-element.56), channel_id=1, source_target_pairs={{0,3},{1,2},{2,1},{3,0},{4,7},{5,6},{6,5},{7,4},{8,11},{9,10},{10,... | collective-permute-start | bytes 294920 | tf_op jit(solution)/shard_map/ppermute | solution.py:275
  30.5 5.1 %slice-start = ((s8[12582912]{0:T(1024)(128)(4,1)}), s8[4194304]{0:T(1024)(128)(4,1)S(1)}, s32[]{:S(2)}) async-start(s8[12582912]{0:T(1024)(128)(4,1)} %bitcast.4), calls=%async_computation | async-start | bytes 8388608
  30.5 5.1 %slice-start.1 = ((s8[12582912]{0:T(1024)(128)(4,1)}), s8[4194304]{0:T(1024)(128)(4,1)S(1)}, s32[]{:S(2)}) async-start(s8[12582912]{0:T(1024)(128)(4,1)} %bitcast.4), calls=%async_computation.1 | async-start | bytes 8388608
  33.4 2.3 %slice-start.2 = ((s8[12582912]{0:T(1024)(128)(4,1)}), s8[4194304]{0:T(1024)(128)(4,1)S(1)}, s32[]{:S(2)}) async-start(s8[12582912]{0:T(1024)(128)(4,1)} %bitcast.4), calls=%async_computation.2 | async-start | bytes 8388608
  36.8 4.9 %collective-permute-start.12 = (bf16[64,768]{1,0:T(8,128)(2,1)S(1)}, bf16[64,768]{1,0:T(8,128)(2,1)S(1)}, u32[]{:S(2)}, u32[]{:S(2)}) collective-permute-start(bf16[64,768]{1,0:T(8,128)(2,1)S(1)} %get-tuple-element.78), channel_id=1, source_target_pairs={{0,1},{1,0},{2,3},{3,2},{4,5},{5,4},{6,7},{7,6},{8,9},{9,8},{10,11... | collective-permute-start | bytes 294920 | tf_op jit(solution)/shard_map/ppermute | solution.py:275
  37.0 5.6 %collective-permute-start.13 = (bf16[64,768]{1,0:T(8,128)(2,1)S(1)}, bf16[64,768]{1,0:T(8,128)(2,1)S(1)}, u32[]{:S(2)}, u32[]{:S(2)}) collective-permute-start(bf16[64,768]{1,0:T(8,128)(2,1)S(1)} %get-tuple-element.79), channel_id=1, source_target_pairs={{0,2},{1,3},{2,0},{3,1},{4,6},{5,7},{6,4},{7,5},{8,10},{9,11},{10,... | collective-permute-start | bytes 294920 | tf_op jit(solution)/shard_map/ppermute | solution.py:275
  38.4 5.2 %collective-permute-start.14 = (bf16[64,768]{1,0:T(8,128)(2,1)S(1)}, bf16[64,768]{1,0:T(8,128)(2,1)S(1)}, u32[]{:S(2)}, u32[]{:S(2)}) collective-permute-start(bf16[64,768]{1,0:T(8,128)(2,1)S(1)} %get-tuple-element.80), channel_id=1, source_target_pairs={{0,3},{1,2},{2,1},{3,0},{4,7},{5,6},{6,5},{7,4},{8,11},{9,10},{10,... | collective-permute-start | bytes 294920 | tf_op jit(solution)/shard_map/ppermute | solution.py:275
  39.7 5.3 %collective-permute-start.19 = (bf16[64,768]{1,0:T(8,128)(2,1)S(1)}, bf16[64,768]{1,0:T(8,128)(2,1)S(1)}, u32[]{:S(2)}, u32[]{:S(2)}) collective-permute-start(bf16[64,768]{1,0:T(8,128)(2,1)S(1)} %get-tuple-element.86), channel_id=1, source_target_pairs={{0,1},{1,0},{2,3},{3,2},{4,5},{5,4},{6,7},{7,6},{8,9},{9,8},{10,11... | collective-permute-start | bytes 294920 | tf_op jit(solution)/shard_map/ppermute | solution.py:275
  40.2 7.9 %collective-permute-start.24 = (bf16[64,768]{1,0:T(8,128)(2,1)S(1)}, bf16[64,768]{1,0:T(8,128)(2,1)S(1)}, u32[]{:S(2)}, u32[]{:S(2)}) collective-permute-start(bf16[64,768]{1,0:T(8,128)(2,1)S(1)} %get-tuple-element.92), channel_id=1, source_target_pairs={{0,2},{1,3},{2,0},{3,1},{4,6},{5,7},{6,4},{7,5},{8,10},{9,11},{10,... | collective-permute-start | bytes 294920 | tf_op jit(solution)/shard_map/ppermute | solution.py:275
  41.6 6.5 %collective-permute-start.25 = (bf16[64,768]{1,0:T(8,128)(2,1)S(1)}, bf16[64,768]{1,0:T(8,128)(2,1)S(1)}, u32[]{:S(2)}, u32[]{:S(2)}) collective-permute-start(bf16[64,768]{1,0:T(8,128)(2,1)S(1)} %get-tuple-element.93), channel_id=1, source_target_pairs={{0,3},{1,2},{2,1},{3,0},{4,7},{5,6},{6,5},{7,4},{8,11},{9,10},{10,... | collective-permute-start | bytes 294920 | tf_op jit(solution)/shard_map/ppermute | solution.py:275
  44.0 8.0 %collective-permute-start.15 = (bf16[128,384]{1,0:T(8,128)(2,1)S(1)}, bf16[128,384]{1,0:T(8,128)(2,1)S(1)}, u32[]{:S(2)}, u32[]{:S(2)}) collective-permute-start(bf16[128,384]{1,0:T(8,128)(2,1)S(1)} %get-tuple-element.81), channel_id=1, source_target_pairs={{0,4},{4,0},{8,12},{12,8},{1,5},{5,1},{9,13},{13,9},{2,6},{6,2},{1... | collective-permute-start | bytes 294920 | tf_op jit(solution)/shard_map/ppermute | solution.py:275
  46.0 7.2 %collective-permute-start.20 = (bf16[64,768]{1,0:T(8,128)(2,1)S(1)}, bf16[64,768]{1,0:T(8,128)(2,1)S(1)}, u32[]{:S(2)}, u32[]{:S(2)}) collective-permute-start(bf16[64,768]{1,0:T(8,128)(2,1)S(1)} %get-tuple-element.88), channel_id=1, source_target_pairs={{0,1},{1,0},{2,3},{3,2},{4,5},{5,4},{6,7},{7,6},{8,9},{9,8},{10,11... | collective-permute-start | bytes 294920 | tf_op jit(solution)/shard_map/ppermute | solution.py:275
  46.7 6.6 %collective-permute-start.21 = (bf16[64,768]{1,0:T(8,128)(2,1)S(1)}, bf16[64,768]{1,0:T(8,128)(2,1)S(1)}, u32[]{:S(2)}, u32[]{:S(2)}) collective-permute-start(bf16[64,768]{1,0:T(8,128)(2,1)S(1)} %get-tuple-element.89), channel_id=1, source_target_pairs={{0,2},{1,3},{2,0},{3,1},{4,6},{5,7},{6,4},{7,5},{8,10},{9,11},{10,... | collective-permute-start | bytes 294920 | tf_op jit(solution)/shard_map/ppermute | solution.py:275
  48.1 5.1 %collective-permute-start.22 = (bf16[64,768]{1,0:T(8,128)(2,1)S(1)}, bf16[64,768]{1,0:T(8,128)(2,1)S(1)}, u32[]{:S(2)}, u32[]{:S(2)}) collective-permute-start(bf16[64,768]{1,0:T(8,128)(2,1)S(1)} %get-tuple-element.90), channel_id=1, source_target_pairs={{0,3},{1,2},{2,1},{3,0},{4,7},{5,6},{6,5},{7,4},{8,11},{9,10},{10,... | collective-permute-start | bytes 294920 | tf_op jit(solution)/shard_map/ppermute | solution.py:275
  48.1 9.3 %collective-permute-start.27 = (bf16[128,384]{1,0:T(8,128)(2,1)S(1)}, bf16[128,384]{1,0:T(8,128)(2,1)S(1)}, u32[]{:S(2)}, u32[]{:S(2)}) collective-permute-start(bf16[128,384]{1,0:T(8,128)(2,1)S(1)} %get-tuple-element.94), channel_id=1, source_target_pairs={{0,12},{4,8},{8,4},{12,0},{1,13},{5,9},{9,5},{13,1},{2,14},{6,10},... | collective-permute-start | bytes 294920 | tf_op jit(solution)/shard_map/ppermute | solution.py:275
  52.2 13.0 %collective-permute-start.26 = (bf16[128,768]{1,0:T(8,128)(2,1)S(1)}, bf16[128,768]{1,0:T(8,128)(2,1)S(1)}, u32[]{:S(2)}, u32[]{:S(2)}) collective-permute-start(bf16[128,768]{1,0:T(8,128)(2,1)S(1)} %combine.6), channel_id=1, source_target_pairs={{0,8},{4,12},{8,0},{12,4},{1,9},{5,13},{9,1},{13,5},{2,10},{6,14},... | collective-permute-start | bytes 589832 | tf_op jit(solution)/shard_map/ppermute | solution.py:275
  53.6 11.7 %collective-permute-start.23 = (bf16[128,768]{1,0:T(8,128)(2,1)S(1)}, bf16[128,768]{1,0:T(8,128)(2,1)S(1)}, u32[]{:S(2)}, u32[]{:S(2)}) collective-permute-start(bf16[128,768]{1,0:T(8,128)(2,1)S(1)} %combine.5), channel_id=1, source_target_pairs={{0,4},{4,0},{8,12},{12,8},{1,5},{5,1},{9,13},{13,9},{2,6},{6,2},{1... | collective-permute-start | bytes 589832 | tf_op jit(solution)/shard_map/ppermute | solution.py:275
  55.7 1.9 %collective-permute-start.16 = (bf16[64,768]{1,0:T(8,128)(2,1)S(1)}, bf16[64,768]{1,0:T(8,128)(2,1)S(1)}, u32[]{:S(2)}, u32[]{:S(2)}) collective-permute-start(bf16[64,768]{1,0:T(8,128)(2,1)S(1)} %get-tuple-element.83), channel_id=1, source_target_pairs={{0,1},{1,0},{2,3},{3,2},{4,5},{5,4},{6,7},{7,6},{8,9},{9,8},{10,11... | collective-permute-start | bytes 294920 | tf_op jit(solution)/shard_map/ppermute | solution.py:275
  56.0 5.6 %collective-permute-start.17 = (bf16[64,768]{1,0:T(8,128)(2,1)S(1)}, bf16[64,768]{1,0:T(8,128)(2,1)S(1)}, u32[]{:S(2)}, u32[]{:S(2)}) collective-permute-start(bf16[64,768]{1,0:T(8,128)(2,1)S(1)} %get-tuple-element.84), channel_id=1, source_target_pairs={{0,2},{1,3},{2,0},{3,1},{4,6},{5,7},{6,4},{7,5},{8,10},{9,11},{10,... | collective-permute-start | bytes 294920 | tf_op jit(solution)/shard_map/ppermute | solution.py:275
  57.4 5.1 %collective-permute-start.18 = (bf16[64,768]{1,0:T(8,128)(2,1)S(1)}, bf16[64,768]{1,0:T(8,128)(2,1)S(1)}, u32[]{:S(2)}, u32[]{:S(2)}) collective-permute-start(bf16[64,768]{1,0:T(8,128)(2,1)S(1)} %get-tuple-element.85), channel_id=1, source_target_pairs={{0,3},{1,2},{2,1},{3,0},{4,7},{5,6},{6,5},{7,4},{8,11},{9,10},{10,... | collective-permute-start | bytes 294920 | tf_op jit(solution)/shard_map/ppermute | solution.py:275
